TPU v7x, 32 devices: a whole 2x2x4 slice. The times are simulated.
32 devices in a mesh: segment: 4 (over y, x), dom: 8 (over z, core).
Axes of the slice: x: 2, y: 2, z: 4, core: 2. Of those that a mesh axis runs over, the one named last changes fastest.
Arguments:
- grid_state: bfloat16 [4, 1024, 227], P(None, 'dom'), may hold values from -6 to 6
- w_embed: bfloat16 [227, 512], replicated, may hold values from -0.375 to 0.375
- w_project: bfloat16 [4, 512, 1024], P('segment'), may hold values from -0.25 to 0.25
- w_message: bfloat16 [4, 512, 512], P('segment'), may hold values from -0.25 to 0.25
- w_update: bfloat16 [4, 1024, 512], P('segment'), may hold values from -0.1875 to 0.1875
- w_decode: bfloat16 [1024, 512], replicated, may hold values from -0.1875 to 0.1875
- w_output: bfloat16 [512, 227], replicated, may hold values from -0.25 to 0.25
- grid_mesh: int32 [1024], P('dom'), may hold values from 0 to 63
- mesh_grid: int32 [1024], P('dom'), may hold values from 0 to 63
- neighbors: int32 [512, 8], P('dom'), may hold values from 0 to 319
- send_rows: int32 [4, 512], P(None, 'dom'), may hold values from 0 to 63
- halo_count: int32 [4, 8], P(None, 'dom'), may hold values from 16 to 64, as said below
Outputs:
- prediction: bfloat16 [4, 1024, 227], P('segment', 'dom')
Inputs may be any that keep to these rules, and one draw needn't show every extreme that they name: `halo_count`: at least 16; some list of some partition is full in every draw. `neighbors`: rows 0 to 63 are the node's own partition, then four blocks of 64 rows from the partitions -1, +1, -2, +2 away.
All inputs are finite; a program needn't handle non-finite values.
Results may differ from a plain program's by a relative error of at most 0.018.
Values may be sent and summed in bfloat16 or wider, within the bound.
No kernel may reach another device: no remote copies, remote signals or barrier semaphores. Data moves between devices by JAX's collectives and lax.ppermute only.
A program may use at most 64 MiB of HBM per device.

v0:
```python
import jax
import jax.numpy as jnp
from jax import lax
from jax.sharding import PartitionSpec as P

epsilon = 1e-05


def from_behind(value, axis, steps):
    count = lax.axis_size(axis)
    pairs = [(source, (source + steps) % count) for source in range(count)]
    return lax.ppermute(value, axis, pairs)


def from_behind_2(block, axis, distance):
    devices = range(lax.axis_size(axis))
    route = [(i - distance, i) for i in devices if i - distance in devices]
    return lax.ppermute(block, axis, route)


def from_root(value, axis, source):
    kept = jnp.where(lax.axis_index(axis) == source, value, 0).astype(value.dtype)
    return lax.psum(kept, axis)


def rms_scale(values):
    return values * lax.rsqrt(jnp.mean(values * values, axis=-1, keepdims=True) + epsilon)


def body(
    grid_state,
    w_embed,
    w_project,
    w_message,
    w_update,
    w_decode,
    w_output,
    grid_mesh,
    mesh_grid,
    neighbors,
    send_rows,
    halo_count,
):
    segment_index = lax.axis_index("segment")
    segment_count = lax.axis_size("segment")
    final_segment = segment_count - 1
    samples, grid_rows, channels = grid_state.shape
    width = w_embed.shape[1]
    mesh_rows = neighbors.shape[0]
    fanout = neighbors.shape[1]
    halo_rows = send_rows.shape[1]
    share = samples // segment_count
    pool_table = (grid_mesh[None, :] == jnp.arange(mesh_rows, dtype=jnp.int32)[:, None]).astype(
        jnp.bfloat16
    )
    read_table = (mesh_grid[:, None] == jnp.arange(mesh_rows, dtype=jnp.int32)[None, :]).astype(
        jnp.bfloat16
    )
    valid_rows = jnp.arange(halo_rows, dtype=jnp.int32)[None, :] < halo_count[:, 0][:, None]
    source_rows = neighbors.reshape(mesh_rows * fanout)

    def embed_grid(snapshot):
        return jax.nn.silu(jnp.dot(snapshot, w_embed, preferred_element_type=jnp.float32)).astype(
            jnp.bfloat16
        )

    def encode(snapshot):
        latent = embed_grid(snapshot)
        pooled = jnp.dot(pool_table, latent, preferred_element_type=jnp.float32)
        return (rms_scale(pooled).astype(jnp.bfloat16), latent)

    def project(state, weights):
        projected = jnp.dot(state, weights[0], preferred_element_type=jnp.float32)
        return (projected[:, :width], projected[:, width:].astype(jnp.bfloat16))

    def renew(state, receiver, extended, weights):
        fetched = extended[source_rows].reshape(mesh_rows, fanout, width)
        edges = jax.nn.silu(receiver[:, None, :] + fetched.astype(jnp.float32)).astype(jnp.bfloat16)
        messages = jnp.dot(
            edges.reshape(mesh_rows * fanout, width), weights[1], preferred_element_type=jnp.float32
        )
        aggregate = (jnp.sum(messages.reshape(mesh_rows, fanout, width), axis=1) / fanout).astype(
            jnp.bfloat16
        )
        update = jax.nn.silu(
            jnp.dot(state, weights[2][:width], preferred_element_type=jnp.float32)
            + jnp.dot(aggregate, weights[2][width:], preferred_element_type=jnp.float32)
        )
        return (state.astype(jnp.float32) + rms_scale(update)).astype(jnp.bfloat16)

    def decode(state, latent):
        readout = jnp.dot(read_table, state, preferred_element_type=jnp.float32).astype(
            jnp.bfloat16
        )
        hidden = jax.nn.silu(
            jnp.dot(latent, w_decode[:width], preferred_element_type=jnp.float32)
            + jnp.dot(readout, w_decode[width:], preferred_element_type=jnp.float32)
        ).astype(jnp.bfloat16)
        return jnp.dot(hidden, w_output, preferred_element_type=jnp.float32).astype(jnp.bfloat16)

    own_weights = (w_project[0], w_message[0], w_update[0])
    empty_mesh = jnp.zeros((mesh_rows, width), jnp.bfloat16)
    empty_receiver = jnp.zeros((mesh_rows, width), jnp.float32)
    empty_grid = jnp.zeros((grid_rows, width), jnp.bfloat16)
    empty_output = jnp.zeros((grid_rows, channels), jnp.bfloat16)
    received = empty_mesh
    carried = {}
    results = [empty_output for sample in range(samples)]
    for moment in range(samples + final_segment):
        current = received
        if moment < samples:
            snapshot = grid_state[moment]
            started, latent = lax.cond(
                segment_index == 0, lambda: encode(snapshot), lambda: (empty_mesh, empty_grid)
            )
            current = jnp.where(segment_index == 0, started, received)
            carried[moment] = from_behind_2(latent, "segment", final_segment)
        active = (moment - segment_index >= 0) & (moment - segment_index < samples)
        receiver, outgoing = lax.cond(
            active, lambda: project(current, own_weights), lambda: (empty_receiver, empty_mesh)
        )
        picked = jnp.where(valid_rows[:, :, None], outgoing[send_rows], jnp.zeros((), jnp.bfloat16))
        arrived = [outgoing]
        for list_index, offset in enumerate((1, -1, 2, -2)):
            arrived.append(from_behind(picked[list_index], "dom", offset))
        extended = jnp.concatenate(arrived, axis=0)
        renewed = lax.cond(
            active, lambda: renew(current, receiver, extended, own_weights), lambda: empty_mesh
        )
        if moment >= final_segment:
            finished = moment - final_segment
            skipped = carried[finished]
            results[finished] = lax.cond(
                segment_index == final_segment,
                lambda: decode(renewed, skipped),
                lambda: empty_output,
            )
        if moment < samples + final_segment - 1:
            received = from_behind_2(renewed, "segment", 1)
    everything = from_root(jnp.stack(results), "segment", final_segment)
    return lax.dynamic_slice_in_dim(everything, segment_index * share, share, 0)


def solution(mesh):
    return jax.shard_map(
        body,
        mesh=mesh,
        in_specs=(
            P(None, "dom", None),
            P(),
            P("segment", None, None),
            P("segment", None, None),
            P("segment", None, None),
            P(),
            P(),
            P("dom"),
            P("dom"),
            P("dom", None),
            P(None, "dom"),
            P(None, "dom"),
        ),
        out_specs=P("segment", "dom", None),
        check_vma=False,
    )
```

profile of v0, /device:TPU:3, one launch (start us, length us, event | category | flops | bytes accessed | tf_op | source)
XLA Modules:
  0.0 239.2 jit_solution(13285142229495336324)
XLA Ops:
  10.8 1.9 collective-permute-start.1
  14.0 2.0 collective-permute-start.4
  16.2 2.1 collective-permute-done.2
  19.5 3.1 %collective-permute-start.5 = (bf16[64,512]{1,0:T(8,128)(2,1)}, bf16[64,512]{1,0:T(8,128)(2,1)S(1)}, u32[]{:S(2)}, u32[]{:S(2)}) collective-permute-start(bf16[64,512]{1,0:T(8,128)(2,1)} %get-tuple-element.548), channel_id=1, source_target_pairs={{0,8},{8,16},{16,24},{1,9},{9,17},{17,25},{2,10},{10,18},{18,26},{... | collective-permute-start | bytes 196616 | tf_op jit(solution)/shard_map/ppermute | solution.py:18
  23.3 7.3 %collective-permute-done.5 = bf16[64,512]{1,0:T(8,128)(2,1)S(1)} collective-permute-done((bf16[64,512]{1,0:T(8,128)(2,1)}, bf16[64,512]{1,0:T(8,128)(2,1)S(1)}, u32[]{:S(2)}, u32[]{:S(2)}) %collective-permute-start.5) | collective-permute-done | bytes 65568 | tf_op jit(solution)/shard_map/ppermute | solution.py:18
  32.3 3.7 %collective-permute-start.6 = (bf16[64,512]{1,0:T(8,128)(2,1)S(1)}, bf16[64,512]{1,0:T(8,128)(2,1)S(1)}, u32[]{:S(2)}, u32[]{:S(2)}) collective-permute-start(bf16[64,512]{1,0:T(8,128)(2,1)S(1)} %get-tuple-element.499), channel_id=1, source_target_pairs={{0,1},{1,2},{2,3},{3,4},{4,5},{5,6},{6,7},{7,0},{8,9},{9,10},{10,1... | collective-permute-start | bytes 196616 | tf_op jit(solution)/shard_map/ppermute | solution.py:12
  36.7 2.5 %collective-permute-start.9 = (bf16[64,512]{1,0:T(8,128)(2,1)S(1)}, bf16[64,512]{1,0:T(8,128)(2,1)S(1)}, u32[]{:S(2)}, u32[]{:S(2)}) collective-permute-start(bf16[64,512]{1,0:T(8,128)(2,1)S(1)} %get-tuple-element.496), channel_id=1, source_target_pairs={{0,6},{1,7},{2,0},{3,1},{4,2},{5,3},{6,4},{7,5},{8,14},{9,15},{10,... | collective-permute-start | bytes 196616 | tf_op jit(solution)/shard_map/ppermute | solution.py:12
  39.9 1.4 collective-permute-done.8
  42.0 4.9 %conditional.29 = (bf16[64,512]{1,0:T(8,128)(2,1)}) conditional(s32[]{:T(128)} %convert_element_type.287, () %tuple.174, (bf16[64,512]{1,0:T(8,128)(2,1)S(1)}, bf16[1024,512]{1,0:T(8,128)(2,1)S(1)}, f32[64,512]{1,0:T(8,128)S(1)}, s32[512]{0:T(512)S(1)}, bf16[320,512]{1,0:T(8,128)(2,1)S(1)}, /*index=5*/bf16[512,512]{1,0:T(8,128)(2,1)}) %tuple.337), branch_computations={%region_20.21_spmd, %region_21.24_spmd} | conditional | flops 338037312 | bytes 4273160 | solution.py:127
  42.2 2.0 gather_fusion.1
  44.2 1.6 convolution_reduce_fusion.1
  46.9 1.9 collective-permute-start.10
  49.5 2.6 %collective-permute-done.10 = bf16[64,512]{1,0:T(8,128)(2,1)S(1)} collective-permute-done((bf16[64,512]{1,0:T(8,128)(2,1)}, bf16[64,512]{1,0:T(8,128)(2,1)S(1)}, u32[]{:S(2)}, u32[]{:S(2)}) %collective-permute-start.10) | collective-permute-done | bytes 65568 | tf_op jit(solution)/shard_map/ppermute | solution.py:18
  53.8 3.6 %collective-permute-start.11 = (bf16[64,512]{1,0:T(8,128)(2,1)S(1)}, bf16[64,512]{1,0:T(8,128)(2,1)S(1)}, u32[]{:S(2)}, u32[]{:S(2)}) collective-permute-start(bf16[64,512]{1,0:T(8,128)(2,1)S(1)} %get-tuple-element.495), channel_id=1, source_target_pairs={{0,1},{1,2},{2,3},{3,4},{4,5},{5,6},{6,7},{7,0},{8,9},{9,10},{10,1... | collective-permute-start | bytes 196616 | tf_op jit(solution)/shard_map/ppermute | solution.py:12
  59.5 2.4 %collective-permute-start.14 = (bf16[64,512]{1,0:T(8,128)(2,1)S(1)}, bf16[64,512]{1,0:T(8,128)(2,1)S(1)}, u32[]{:S(2)}, u32[]{:S(2)}) collective-permute-start(bf16[64,512]{1,0:T(8,128)(2,1)S(1)} %get-tuple-element.492), channel_id=1, source_target_pairs={{0,6},{1,7},{2,0},{3,1},{4,2},{5,3},{6,4},{7,5},{8,14},{9,15},{10,... | collective-permute-start | bytes 196616 | tf_op jit(solution)/shard_map/ppermute | solution.py:12
  62.0 2.0 collective-permute-done.13
  64.6 4.9 %conditional.31 = (bf16[64,512]{1,0:T(8,128)(2,1)}) conditional(s32[]{:T(128)} %convert_element_type.286, () %tuple.172, (bf16[64,512]{1,0:T(8,128)(2,1)S(1)}, bf16[1024,512]{1,0:T(8,128)(2,1)S(1)}, f32[64,512]{1,0:T(8,128)S(1)}, s32[512]{0:T(512)S(1)}, bf16[320,512]{1,0:T(8,128)(2,1)S(1)}, /*index=5*/bf16[512,512]{1,0:T(8,128)(2,1)}) %tuple.338), branch_computations={%region_26.27_spmd, %region_27.30_spmd} | conditional | flops 338037312 | bytes 4273160 | solution.py:127
  64.9 2.0 gather_fusion.2
  66.9 1.6 convolution_reduce_fusion.2
  69.6 2.5 %collective-permute-start.15 = (bf16[64,512]{1,0:T(8,128)(2,1)}, bf16[64,512]{1,0:T(8,128)(2,1)S(1)}, u32[]{:S(2)}, u32[]{:S(2)}) collective-permute-start(bf16[64,512]{1,0:T(8,128)(2,1)} %get-tuple-element.550), channel_id=1, source_target_pairs={{0,8},{8,16},{16,24},{1,9},{9,17},{17,25},{2,10},{10,18},{18,26},{... | collective-permute-start | bytes 196616 | tf_op jit(solution)/shard_map/ppermute | solution.py:18
  72.8 2.0 collective-permute-done.15
  76.4 3.6 %collective-permute-start.16 = (bf16[64,512]{1,0:T(8,128)(2,1)S(1)}, bf16[64,512]{1,0:T(8,128)(2,1)S(1)}, u32[]{:S(2)}, u32[]{:S(2)}) collective-permute-start(bf16[64,512]{1,0:T(8,128)(2,1)S(1)} %get-tuple-element.491), channel_id=1, source_target_pairs={{0,1},{1,2},{2,3},{3,4},{4,5},{5,6},{6,7},{7,0},{8,9},{9,10},{10,1... | collective-permute-start | bytes 196616 | tf_op jit(solution)/shard_map/ppermute | solution.py:12
  82.1 2.4 %collective-permute-start.19 = (bf16[64,512]{1,0:T(8,128)(2,1)S(1)}, bf16[64,512]{1,0:T(8,128)(2,1)S(1)}, u32[]{:S(2)}, u32[]{:S(2)}) collective-permute-start(bf16[64,512]{1,0:T(8,128)(2,1)S(1)} %get-tuple-element.488), channel_id=1, source_target_pairs={{0,6},{1,7},{2,0},{3,1},{4,2},{5,3},{6,4},{7,5},{8,14},{9,15},{10,... | collective-permute-start | bytes 196616 | tf_op jit(solution)/shard_map/ppermute | solution.py:12
  84.6 2.0 collective-permute-done.18
  87.3 4.3 %conditional.33 = (bf16[64,512]{1,0:T(8,128)(2,1)S(1)}) conditional(s32[]{:T(128)} %convert_element_type.285, () %tuple.170, (bf16[64,512]{1,0:T(8,128)(2,1)S(1)}, bf16[1024,512]{1,0:T(8,128)(2,1)S(1)}, f32[64,512]{1,0:T(8,128)S(1)}, s32[512]{0:T(512)S(1)}, bf16[320,512]{1,0:T(8,128)(2,1)S(1)}, /*index=5*/bf16[512,512]{1,0:T(8,128)(2,1)}) %tuple.339), branch_computations={%region_32.33_spmd, %region_33.36_spmd} | conditional | flops 338037312 | bytes 4273160 | solution.py:127
  87.5 2.0 gather_fusion.3
  89.5 1.6 convolution_reduce_fusion.3
  91.6 3.4 %collective-permute-start.21 = (bf16[64,512]{1,0:T(8,128)(2,1)S(1)}, bf16[64,512]{1,0:T(8,128)(2,1)S(1)}, u32[]{:S(2)}, u32[]{:S(2)}) collective-permute-start(bf16[64,512]{1,0:T(8,128)(2,1)S(1)} %get-tuple-element.551), channel_id=1, source_target_pairs={{0,8},{8,16},{16,24},{1,9},{9,17},{17,25},{2,10},{10,18},{18,26},{... | collective-permute-start | bytes 196616 | tf_op jit(solution)/shard_map/ppermute | solution.py:18
  95.0 1.6 collective-permute-done.21
  98.2 3.6 %collective-permute-start.22 = (bf16[64,512]{1,0:T(8,128)(2,1)S(1)}, bf16[64,512]{1,0:T(8,128)(2,1)S(1)}, u32[]{:S(2)}, u32[]{:S(2)}) collective-permute-start(bf16[64,512]{1,0:T(8,128)(2,1)S(1)} %get-tuple-element.487), channel_id=1, source_target_pairs={{0,1},{1,2},{2,3},{3,4},{4,5},{5,6},{6,7},{7,0},{8,9},{9,10},{10,1... | collective-permute-start | bytes 196616 | tf_op jit(solution)/shard_map/ppermute | solution.py:12
  103.9 2.5 %collective-permute-start.25 = (bf16[64,512]{1,0:T(8,128)(2,1)S(1)}, bf16[64,512]{1,0:T(8,128)(2,1)S(1)}, u32[]{:S(2)}, u32[]{:S(2)}) collective-permute-start(bf16[64,512]{1,0:T(8,128)(2,1)S(1)} %get-tuple-element.484), channel_id=1, source_target_pairs={{0,6},{1,7},{2,0},{3,1},{4,2},{5,3},{6,4},{7,5},{8,14},{9,15},{10,... | collective-permute-start | bytes 196616 | tf_op jit(solution)/shard_map/ppermute | solution.py:12
  106.4 2.0 collective-permute-done.24
  109.1 4.3 %conditional.36 = (bf16[64,512]{1,0:T(8,128)(2,1)S(1)}) conditional(s32[]{:T(128)} %convert_element_type.289, () %tuple.191, (bf16[64,512]{1,0:T(8,128)(2,1)S(1)}, bf16[1024,512]{1,0:T(8,128)(2,1)S(1)}, f32[64,512]{1,0:T(8,128)S(1)}, s32[512]{0:T(512)S(1)}, bf16[320,512]{1,0:T(8,128)(2,1)S(1)}, /*index=5*/bf16[512,512]{1,0:T(8,128)(2,1)}) %tuple.340), branch_computations={%region_40.41_spmd, %region_41.44_spmd} | conditional | flops 338037312 | bytes 4273160 | solution.py:127
  109.3 2.0 gather_fusion.4
  111.3 1.6 convolution_reduce_fusion.4
  113.4 4.3 %collective-permute-start.27 = (bf16[64,512]{1,0:T(8,128)(2,1)S(1)}, bf16[64,512]{1,0:T(8,128)(2,1)S(1)}, u32[]{:S(2)}, u32[]{:S(2)}) collective-permute-start(bf16[64,512]{1,0:T(8,128)(2,1)S(1)} %get-tuple-element.553), channel_id=1, source_target_pairs={{0,8},{8,16},{16,24},{1,9},{9,17},{17,25},{2,10},{10,18},{18,26},{... | collective-permute-start | bytes 196616 | tf_op jit(solution)/shard_map/ppermute | solution.py:18
  124.3 2.8 %collective-permute-start.28 = (bf16[64,512]{1,0:T(8,128)(2,1)S(1)}, bf16[64,512]{1,0:T(8,128)(2,1)S(1)}, u32[]{:S(2)}, u32[]{:S(2)}) collective-permute-start(bf16[64,512]{1,0:T(8,128)(2,1)S(1)} %get-tuple-element.483), channel_id=1, source_target_pairs={{0,1},{1,2},{2,3},{3,4},{4,5},{5,6},{6,7},{7,0},{8,9},{9,10},{10,1... | collective-permute-start | bytes 196616 | tf_op jit(solution)/shard_map/ppermute | solution.py:12
  127.1 1.6 collective-permute-done.28
  128.8 4.8 %collective-permute-start.29 = (bf16[64,512]{1,0:T(8,128)(2,1)S(1)}, bf16[64,512]{1,0:T(8,128)(2,1)S(1)}, u32[]{:S(2)}, u32[]{:S(2)}) collective-permute-start(bf16[64,512]{1,0:T(8,128)(2,1)S(1)} %get-tuple-element.482), channel_id=1, source_target_pairs={{0,7},{1,0},{2,1},{3,2},{4,3},{5,4},{6,5},{7,6},{8,15},{9,8},{10,9... | collective-permute-start | bytes 196616 | tf_op jit(solution)/shard_map/ppermute | solution.py:12
  134.8 6.2 %collective-permute-done.30 = bf16[64,512]{1,0:T(8,128)(2,1)S(1)} collective-permute-done((bf16[64,512]{1,0:T(8,128)(2,1)S(1)}, bf16[64,512]{1,0:T(8,128)(2,1)S(1)}, u32[]{:S(2)}, u32[]{:S(2)}) %collective-permute-start.30) | collective-permute-done | bytes 65568 | tf_op jit(solution)/shard_map/ppermute | solution.py:12
  141.9 2.2 collective-permute-done.31
  144.7 7.9 %collective-permute-start.33 = (bf16[64,512]{1,0:T(8,128)(2,1)}, bf16[64,512]{1,0:T(8,128)(2,1)S(1)}, u32[]{:S(2)}, u32[]{:S(2)}) collective-permute-start(bf16[64,512]{1,0:T(8,128)(2,1)} %get-tuple-element.555), channel_id=1, source_target_pairs={{0,8},{8,16},{16,24},{1,9},{9,17},{17,25},{2,10},{10,18},{18,26},{... | collective-permute-start | bytes 196616 | tf_op jit(solution)/shard_map/ppermute | solution.py:18
  156.0 1.9 collective-permute-start.34
  158.8 3.3 %collective-permute-start.37 = (bf16[64,512]{1,0:T(8,128)(2,1)S(1)}, bf16[64,512]{1,0:T(8,128)(2,1)S(1)}, u32[]{:S(2)}, u32[]{:S(2)}) collective-permute-start(bf16[64,512]{1,0:T(8,128)(2,1)S(1)} %get-tuple-element.476), channel_id=1, source_target_pairs={{0,6},{1,7},{2,0},{3,1},{4,2},{5,3},{6,4},{7,5},{8,14},{9,15},{10,... | collective-permute-start | bytes 196616 | tf_op jit(solution)/shard_map/ppermute | solution.py:12
  162.1 2.6 %collective-permute-done.36 = bf16[64,512]{1,0:T(8,128)(2,1)S(1)} collective-permute-done((bf16[64,512]{1,0:T(8,128)(2,1)S(1)}, bf16[64,512]{1,0:T(8,128)(2,1)S(1)}, u32[]{:S(2)}, u32[]{:S(2)}) %collective-permute-start.36) | collective-permute-done | bytes 65568 | tf_op jit(solution)/shard_map/ppermute | solution.py:12
  165.7 1.6 maximum_select_fusion
  167.3 63.5 %all-reduce.2.cloned.1.call-done = bf16[4,128,227]{1,2,0:T(8,128)(2,1)} async-done(((bf16[4,128,227]{1,2,0:T(8,128)(2,1)}), bf16[4,128,227]{1,2,0:T(8,128)(2,1)}) %all-reduce.2.cloned.1.call-update) | async-done | bytes 232464 | tf_op jit(solution)/shard_map/psum | solution.py:23
  230.9 1.5 constant_dynamic-slice_fusion
  (216 shorter events, 50.5 us)
Async XLA Ops:
  6.5 224.3 %all-reduce.2.cloned.1.call-start = ((), (), s32[]{:S(2)}) async-start(), calls=%async_computation | async-start | bytes 475136 | tf_op jit(solution)/shard_map/psum | solution.py:23
  7.2 2.2 copy-start
  10.6 8.2 %copy-start.1 = (bf16[1,1024,512]{2,1,0:T(8,128)(2,1)S(1)}, bf16[1,1024,512]{2,1,0:T(8,128)(2,1)}, u32[]{:S(2)}) copy-start(bf16[1,1024,512]{2,1,0:T(8,128)(2,1)} %param.60) | copy-start | bytes 3145732
  10.8 5.2 %copy-start.14 = (s32[64,8]{0,1:T(8,128)S(1)}, s32[64,8]{0,1:T(8,128)}, u32[]{:S(2)}) copy-start(s32[64,8]{0,1:T(8,128)} %param.65) | copy-start | bytes 6148
  10.8 5.4 %collective-permute-start.1 = (bf16[64,512]{1,0:T(8,128)(2,1)S(1)}, bf16[64,512]{1,0:T(8,128)(2,1)S(1)}, u32[]{:S(2)}, u32[]{:S(2)}) collective-permute-start(bf16[64,512]{1,0:T(8,128)(2,1)S(1)} %get-tuple-element.503), channel_id=1, source_target_pairs={{0,1},{1,2},{2,3},{3,4},{4,5},{5,6},{6,7},{7,0},{8,9},{9,10},{10,1... | collective-permute-start | bytes 196616 | tf_op jit(solution)/shard_map/ppermute | solution.py:12
  12.7 5.6 %collective-permute-start.2 = (bf16[64,512]{1,0:T(8,128)(2,1)S(1)}, bf16[64,512]{1,0:T(8,128)(2,1)S(1)}, u32[]{:S(2)}, u32[]{:S(2)}) collective-permute-start(bf16[64,512]{1,0:T(8,128)(2,1)S(1)} %get-tuple-element.502), channel_id=1, source_target_pairs={{0,7},{1,0},{2,1},{3,2},{4,3},{5,4},{6,5},{7,6},{8,15},{9,8},{10,9... | collective-permute-start | bytes 196616 | tf_op jit(solution)/shard_map/ppermute | solution.py:12
  12.7 5.6 %collective-permute-start.3 = (bf16[64,512]{1,0:T(8,128)(2,1)S(1)}, bf16[64,512]{1,0:T(8,128)(2,1)S(1)}, u32[]{:S(2)}, u32[]{:S(2)}) collective-permute-start(bf16[64,512]{1,0:T(8,128)(2,1)S(1)} %get-tuple-element.501), channel_id=1, source_target_pairs={{0,2},{1,3},{2,4},{3,5},{4,6},{5,7},{6,0},{7,1},{8,10},{9,11},{10,... | collective-permute-start | bytes 196616 | tf_op jit(solution)/shard_map/ppermute | solution.py:12
  14.0 4.8 %collective-permute-start.4 = (bf16[64,512]{1,0:T(8,128)(2,1)S(1)}, bf16[64,512]{1,0:T(8,128)(2,1)S(1)}, u32[]{:S(2)}, u32[]{:S(2)}) collective-permute-start(bf16[64,512]{1,0:T(8,128)(2,1)S(1)} %get-tuple-element.500), channel_id=1, source_target_pairs={{0,6},{1,7},{2,0},{3,1},{4,2},{5,3},{6,4},{7,5},{8,14},{9,15},{10,... | collective-permute-start | bytes 196616 | tf_op jit(solution)/shard_map/ppermute | solution.py:12
  18.8 3.8 %copy-start.7 = (bf16[4,128,227]{1,0,2:T(4,128)(2,1)S(1)}, bf16[4,128,227]{1,0,2:T(4,128)(2,1)}, u32[]{:S(2)}) copy-start(bf16[4,128,227]{1,0,2:T(4,128)(2,1)} %param.56) | copy-start | bytes 697348
  19.5 11.1 %collective-permute-start.5 = (bf16[64,512]{1,0:T(8,128)(2,1)}, bf16[64,512]{1,0:T(8,128)(2,1)S(1)}, u32[]{:S(2)}, u32[]{:S(2)}) collective-permute-start(bf16[64,512]{1,0:T(8,128)(2,1)} %get-tuple-element.548), channel_id=1, source_target_pairs={{0,8},{8,16},{16,24},{1,9},{9,17},{17,25},{2,10},{10,18},{18,26},{... | collective-permute-start | bytes 196616 | tf_op jit(solution)/shard_map/ppermute | solution.py:18
  32.3 6.9 %collective-permute-start.6 = (bf16[64,512]{1,0:T(8,128)(2,1)S(1)}, bf16[64,512]{1,0:T(8,128)(2,1)S(1)}, u32[]{:S(2)}, u32[]{:S(2)}) collective-permute-start(bf16[64,512]{1,0:T(8,128)(2,1)S(1)} %get-tuple-element.499), channel_id=1, source_target_pairs={{0,1},{1,2},{2,3},{3,4},{4,5},{5,6},{6,7},{7,0},{8,9},{9,10},{10,1... | collective-permute-start | bytes 196616 | tf_op jit(solution)/shard_map/ppermute | solution.py:12
  36.0 4.0 %collective-permute-start.7 = (bf16[64,512]{1,0:T(8,128)(2,1)S(1)}, bf16[64,512]{1,0:T(8,128)(2,1)S(1)}, u32[]{:S(2)}, u32[]{:S(2)}) collective-permute-start(bf16[64,512]{1,0:T(8,128)(2,1)S(1)} %get-tuple-element.498), channel_id=1, source_target_pairs={{0,7},{1,0},{2,1},{3,2},{4,3},{5,4},{6,5},{7,6},{8,15},{9,8},{10,9... | collective-permute-start | bytes 196616 | tf_op jit(solution)/shard_map/ppermute | solution.py:12
  36.0 5.4 %collective-permute-start.8 = (bf16[64,512]{1,0:T(8,128)(2,1)S(1)}, bf16[64,512]{1,0:T(8,128)(2,1)S(1)}, u32[]{:S(2)}, u32[]{:S(2)}) collective-permute-start(bf16[64,512]{1,0:T(8,128)(2,1)S(1)} %get-tuple-element.497), channel_id=1, source_target_pairs={{0,2},{1,3},{2,4},{3,5},{4,6},{5,7},{6,0},{7,1},{8,10},{9,11},{10,... | collective-permute-start | bytes 196616 | tf_op jit(solution)/shard_map/ppermute | solution.py:12
  36.7 5.3 %collective-permute-start.9 = (bf16[64,512]{1,0:T(8,128)(2,1)S(1)}, bf16[64,512]{1,0:T(8,128)(2,1)S(1)}, u32[]{:S(2)}, u32[]{:S(2)}) collective-permute-start(bf16[64,512]{1,0:T(8,128)(2,1)S(1)} %get-tuple-element.496), channel_id=1, source_target_pairs={{0,6},{1,7},{2,0},{3,1},{4,2},{5,3},{6,4},{7,5},{8,14},{9,15},{10,... | collective-permute-start | bytes 196616 | tf_op jit(solution)/shard_map/ppermute | solution.py:12
  46.9 5.2 %collective-permute-start.10 = (bf16[64,512]{1,0:T(8,128)(2,1)}, bf16[64,512]{1,0:T(8,128)(2,1)S(1)}, u32[]{:S(2)}, u32[]{:S(2)}) collective-permute-start(bf16[64,512]{1,0:T(8,128)(2,1)} %get-tuple-element.549), channel_id=1, source_target_pairs={{0,8},{8,16},{16,24},{1,9},{9,17},{17,25},{2,10},{10,18},{18,26},{... | collective-permute-start | bytes 196616 | tf_op jit(solution)/shard_map/ppermute | solution.py:18
  53.8 8.1 %collective-permute-start.11 = (bf16[64,512]{1,0:T(8,128)(2,1)S(1)}, bf16[64,512]{1,0:T(8,128)(2,1)S(1)}, u32[]{:S(2)}, u32[]{:S(2)}) collective-permute-start(bf16[64,512]{1,0:T(8,128)(2,1)S(1)} %get-tuple-element.495), channel_id=1, source_target_pairs={{0,1},{1,2},{2,3},{3,4},{4,5},{5,6},{6,7},{7,0},{8,9},{9,10},{10,1... | collective-permute-start | bytes 196616 | tf_op jit(solution)/shard_map/ppermute | solution.py:12
  57.4 4.6 %collective-permute-start.12 = (bf16[64,512]{1,0:T(8,128)(2,1)S(1)}, bf16[64,512]{1,0:T(8,128)(2,1)S(1)}, u32[]{:S(2)}, u32[]{:S(2)}) collective-permute-start(bf16[64,512]{1,0:T(8,128)(2,1)S(1)} %get-tuple-element.494), channel_id=1, source_target_pairs={{0,7},{1,0},{2,1},{3,2},{4,3},{5,4},{6,5},{7,6},{8,15},{9,8},{10,9... | collective-permute-start | bytes 196616 | tf_op jit(solution)/shard_map/ppermute | solution.py:12
  58.4 5.6 %collective-permute-start.13 = (bf16[64,512]{1,0:T(8,128)(2,1)S(1)}, bf16[64,512]{1,0:T(8,128)(2,1)S(1)}, u32[]{:S(2)}, u32[]{:S(2)}) collective-permute-start(bf16[64,512]{1,0:T(8,128)(2,1)S(1)} %get-tuple-element.493), channel_id=1, source_target_pairs={{0,2},{1,3},{2,4},{3,5},{4,6},{5,7},{6,0},{7,1},{8,10},{9,11},{10,... | collective-permute-start | bytes 196616 | tf_op jit(solution)/shard_map/ppermute | solution.py:12
  59.5 5.2 %collective-permute-start.14 = (bf16[64,512]{1,0:T(8,128)(2,1)S(1)}, bf16[64,512]{1,0:T(8,128)(2,1)S(1)}, u32[]{:S(2)}, u32[]{:S(2)}) collective-permute-start(bf16[64,512]{1,0:T(8,128)(2,1)S(1)} %get-tuple-element.492), channel_id=1, source_target_pairs={{0,6},{1,7},{2,0},{3,1},{4,2},{5,3},{6,4},{7,5},{8,14},{9,15},{10,... | collective-permute-start | bytes 196616 | tf_op jit(solution)/shard_map/ppermute | solution.py:12
  69.6 5.2 %collective-permute-start.15 = (bf16[64,512]{1,0:T(8,128)(2,1)}, bf16[64,512]{1,0:T(8,128)(2,1)S(1)}, u32[]{:S(2)}, u32[]{:S(2)}) collective-permute-start(bf16[64,512]{1,0:T(8,128)(2,1)} %get-tuple-element.550), channel_id=1, source_target_pairs={{0,8},{8,16},{16,24},{1,9},{9,17},{17,25},{2,10},{10,18},{18,26},{... | collective-permute-start | bytes 196616 | tf_op jit(solution)/shard_map/ppermute | solution.py:18
  76.4 8.1 %collective-permute-start.16 = (bf16[64,512]{1,0:T(8,128)(2,1)S(1)}, bf16[64,512]{1,0:T(8,128)(2,1)S(1)}, u32[]{:S(2)}, u32[]{:S(2)}) collective-permute-start(bf16[64,512]{1,0:T(8,128)(2,1)S(1)} %get-tuple-element.491), channel_id=1, source_target_pairs={{0,1},{1,2},{2,3},{3,4},{4,5},{5,6},{6,7},{7,0},{8,9},{9,10},{10,1... | collective-permute-start | bytes 196616 | tf_op jit(solution)/shard_map/ppermute | solution.py:12
  80.1 4.5 %collective-permute-start.17 = (bf16[64,512]{1,0:T(8,128)(2,1)S(1)}, bf16[64,512]{1,0:T(8,128)(2,1)S(1)}, u32[]{:S(2)}, u32[]{:S(2)}) collective-permute-start(bf16[64,512]{1,0:T(8,128)(2,1)S(1)} %get-tuple-element.490), channel_id=1, source_target_pairs={{0,7},{1,0},{2,1},{3,2},{4,3},{5,4},{6,5},{7,6},{8,15},{9,8},{10,9... | collective-permute-start | bytes 196616 | tf_op jit(solution)/shard_map/ppermute | solution.py:12
  81.0 5.6 %collective-permute-start.18 = (bf16[64,512]{1,0:T(8,128)(2,1)S(1)}, bf16[64,512]{1,0:T(8,128)(2,1)S(1)}, u32[]{:S(2)}, u32[]{:S(2)}) collective-permute-start(bf16[64,512]{1,0:T(8,128)(2,1)S(1)} %get-tuple-element.489), channel_id=1, source_target_pairs={{0,2},{1,3},{2,4},{3,5},{4,6},{5,7},{6,0},{7,1},{8,10},{9,11},{10,... | collective-permute-start | bytes 196616 | tf_op jit(solution)/shard_map/ppermute | solution.py:12
  82.1 5.2 %collective-permute-start.19 = (bf16[64,512]{1,0:T(8,128)(2,1)S(1)}, bf16[64,512]{1,0:T(8,128)(2,1)S(1)}, u32[]{:S(2)}, u32[]{:S(2)}) collective-permute-start(bf16[64,512]{1,0:T(8,128)(2,1)S(1)} %get-tuple-element.488), channel_id=1, source_target_pairs={{0,6},{1,7},{2,0},{3,1},{4,2},{5,3},{6,4},{7,5},{8,14},{9,15},{10,... | collective-permute-start | bytes 196616 | tf_op jit(solution)/shard_map/ppermute | solution.py:12
  91.6 5.0 %copy-start.10 = (bf16[64,512]{1,0:T(8,128)(2,1)}, bf16[64,512]{1,0:T(8,128)(2,1)S(1)}, u32[]{:S(2)}) copy-start(bf16[64,512]{1,0:T(8,128)(2,1)S(1)} %get-tuple-element.551) | copy-start | bytes 196612
  91.6 5.0 %collective-permute-start.21 = (bf16[64,512]{1,0:T(8,128)(2,1)S(1)}, bf16[64,512]{1,0:T(8,128)(2,1)S(1)}, u32[]{:S(2)}, u32[]{:S(2)}) collective-permute-start(bf16[64,512]{1,0:T(8,128)(2,1)S(1)} %get-tuple-element.551), channel_id=1, source_target_pairs={{0,8},{8,16},{16,24},{1,9},{9,17},{17,25},{2,10},{10,18},{18,26},{... | collective-permute-start | bytes 196616 | tf_op jit(solution)/shard_map/ppermute | solution.py:18
  98.2 8.1 %collective-permute-start.22 = (bf16[64,512]{1,0:T(8,128)(2,1)S(1)}, bf16[64,512]{1,0:T(8,128)(2,1)S(1)}, u32[]{:S(2)}, u32[]{:S(2)}) collective-permute-start(bf16[64,512]{1,0:T(8,128)(2,1)S(1)} %get-tuple-element.487), channel_id=1, source_target_pairs={{0,1},{1,2},{2,3},{3,4},{4,5},{5,6},{6,7},{7,0},{8,9},{9,10},{10,1... | collective-permute-start | bytes 196616 | tf_op jit(solution)/shard_map/ppermute | solution.py:12
  101.8 4.5 %collective-permute-start.23 = (bf16[64,512]{1,0:T(8,128)(2,1)S(1)}, bf16[64,512]{1,0:T(8,128)(2,1)S(1)}, u32[]{:S(2)}, u32[]{:S(2)}) collective-permute-start(bf16[64,512]{1,0:T(8,128)(2,1)S(1)} %get-tuple-element.486), channel_id=1, source_target_pairs={{0,7},{1,0},{2,1},{3,2},{4,3},{5,4},{6,5},{7,6},{8,15},{9,8},{10,9... | collective-permute-start | bytes 196616 | tf_op jit(solution)/shard_map/ppermute | solution.py:12
  102.8 5.6 %collective-permute-start.24 = (bf16[64,512]{1,0:T(8,128)(2,1)S(1)}, bf16[64,512]{1,0:T(8,128)(2,1)S(1)}, u32[]{:S(2)}, u32[]{:S(2)}) collective-permute-start(bf16[64,512]{1,0:T(8,128)(2,1)S(1)} %get-tuple-element.485), channel_id=1, source_target_pairs={{0,2},{1,3},{2,4},{3,5},{4,6},{5,7},{6,0},{7,1},{8,10},{9,11},{10,... | collective-permute-start | bytes 196616 | tf_op jit(solution)/shard_map/ppermute | solution.py:12
  103.9 5.2 %collective-permute-start.25 = (bf16[64,512]{1,0:T(8,128)(2,1)S(1)}, bf16[64,512]{1,0:T(8,128)(2,1)S(1)}, u32[]{:S(2)}, u32[]{:S(2)}) collective-permute-start(bf16[64,512]{1,0:T(8,128)(2,1)S(1)} %get-tuple-element.484), channel_id=1, source_target_pairs={{0,6},{1,7},{2,0},{3,1},{4,2},{5,3},{6,4},{7,5},{8,14},{9,15},{10,... | collective-permute-start | bytes 196616 | tf_op jit(solution)/shard_map/ppermute | solution.py:12
  113.3 9.6 %copy-start.12 = (bf16[64,512]{1,0:T(8,128)(2,1)}, bf16[64,512]{1,0:T(8,128)(2,1)S(1)}, u32[]{:S(2)}) copy-start(bf16[64,512]{1,0:T(8,128)(2,1)S(1)} %get-tuple-element.553) | copy-start | bytes 196612
  113.4 9.6 %collective-permute-start.27 = (bf16[64,512]{1,0:T(8,128)(2,1)S(1)}, bf16[64,512]{1,0:T(8,128)(2,1)S(1)}, u32[]{:S(2)}, u32[]{:S(2)}) collective-permute-start(bf16[64,512]{1,0:T(8,128)(2,1)S(1)} %get-tuple-element.553), channel_id=1, source_target_pairs={{0,8},{8,16},{16,24},{1,9},{9,17},{17,25},{2,10},{10,18},{18,26},{... | collective-permute-start | bytes 196616 | tf_op jit(solution)/shard_map/ppermute | solution.py:18
  117.7 47.1 %collective-permute-start.32 = (bf16[128,512]{1,0:T(8,128)(2,1)}, bf16[128,512]{1,0:T(8,128)(2,1)}, u32[]{:S(2)}, u32[]{:S(2)}) collective-permute-start(bf16[128,512]{1,0:T(8,128)(2,1)} %get-tuple-element.355), channel_id=1, source_target_pairs={{0,24},{1,25},{2,26},{3,27},{4,28},{5,29},{6,30},{7,31}} | collective-permute-start | bytes 393224 | tf_op jit(solution)/shard_map/ppermute | solution.py:18
  119.0 35.0 %collective-permute-start.26 = (bf16[128,512]{1,0:T(8,128)(2,1)}, bf16[128,512]{1,0:T(8,128)(2,1)}, u32[]{:S(2)}, u32[]{:S(2)}) collective-permute-start(bf16[128,512]{1,0:T(8,128)(2,1)} %get-tuple-element.352), channel_id=1, source_target_pairs={{0,24},{1,25},{2,26},{3,27},{4,28},{5,29},{6,30},{7,31}} | collective-permute-start | bytes 393224 | tf_op jit(solution)/shard_map/ppermute | solution.py:18
  120.3 33.1 %collective-permute-start.20 = (bf16[128,512]{1,0:T(8,128)(2,1)}, bf16[128,512]{1,0:T(8,128)(2,1)}, u32[]{:S(2)}, u32[]{:S(2)}) collective-permute-start(bf16[128,512]{1,0:T(8,128)(2,1)} %get-tuple-element.349), channel_id=1, source_target_pairs={{0,24},{1,25},{2,26},{3,27},{4,28},{5,29},{6,30},{7,31}} | collective-permute-start | bytes 393224 | tf_op jit(solution)/shard_map/ppermute | solution.py:18
  121.7 31.7 %collective-permute-start = (bf16[128,512]{1,0:T(8,128)(2,1)}, bf16[128,512]{1,0:T(8,128)(2,1)}, u32[]{:S(2)}, u32[]{:S(2)}) collective-permute-start(bf16[128,512]{1,0:T(8,128)(2,1)} %get-tuple-element.336), channel_id=1, source_target_pairs={{0,24},{1,25},{2,26},{3,27},{4,28},{5,29},{6,30},{7,31}} | collective-permute-start | bytes 393224 | tf_op jit(solution)/shard_map/ppermute | solution.py:18
  123.0 1.2 copy-start.8
  124.3 4.4 %collective-permute-start.28 = (bf16[64,512]{1,0:T(8,128)(2,1)S(1)}, bf16[64,512]{1,0:T(8,128)(2,1)S(1)}, u32[]{:S(2)}, u32[]{:S(2)}) collective-permute-start(bf16[64,512]{1,0:T(8,128)(2,1)S(1)} %get-tuple-element.483), channel_id=1, source_target_pairs={{0,1},{1,2},{2,3},{3,4},{4,5},{5,6},{6,7},{7,0},{8,9},{9,10},{10,1... | collective-permute-start | bytes 196616 | tf_op jit(solution)/shard_map/ppermute | solution.py:12
  128.8 5.7 %collective-permute-start.29 = (bf16[64,512]{1,0:T(8,128)(2,1)S(1)}, bf16[64,512]{1,0:T(8,128)(2,1)S(1)}, u32[]{:S(2)}, u32[]{:S(2)}) collective-permute-start(bf16[64,512]{1,0:T(8,128)(2,1)S(1)} %get-tuple-element.482), channel_id=1, source_target_pairs={{0,7},{1,0},{2,1},{3,2},{4,3},{5,4},{6,5},{7,6},{8,15},{9,8},{10,9... | collective-permute-start | bytes 196616 | tf_op jit(solution)/shard_map/ppermute | solution.py:12
  134.5 6.5 %collective-permute-start.30 = (bf16[64,512]{1,0:T(8,128)(2,1)S(1)}, bf16[64,512]{1,0:T(8,128)(2,1)S(1)}, u32[]{:S(2)}, u32[]{:S(2)}) collective-permute-start(bf16[64,512]{1,0:T(8,128)(2,1)S(1)} %get-tuple-element.481), channel_id=1, source_target_pairs={{0,2},{1,3},{2,4},{3,5},{4,6},{5,7},{6,0},{7,1},{8,10},{9,11},{10,... | collective-permute-start | bytes 196616 | tf_op jit(solution)/shard_map/ppermute | solution.py:12
  141.0 3.1 %collective-permute-start.31 = (bf16[64,512]{1,0:T(8,128)(2,1)S(1)}, bf16[64,512]{1,0:T(8,128)(2,1)S(1)}, u32[]{:S(2)}, u32[]{:S(2)}) collective-permute-start(bf16[64,512]{1,0:T(8,128)(2,1)S(1)} %get-tuple-element.480), channel_id=1, source_target_pairs={{0,6},{1,7},{2,0},{3,1},{4,2},{5,3},{6,4},{7,5},{8,14},{9,15},{10,... | collective-permute-start | bytes 196616 | tf_op jit(solution)/shard_map/ppermute | solution.py:12
  144.1 9.3 %copy-start.2 = (bf16[1024,512]{1,0:T(8,128)(2,1)S(1)}, bf16[1024,512]{1,0:T(8,128)(2,1)}, u32[]{:S(2)}) copy-start(bf16[1024,512]{1,0:T(8,128)(2,1)} %param.61) | copy-start | bytes 3145732
  144.7 7.9 %copy-start.16 = (s32[128]{0:T(128)S(1)}, s32[128]{0:T(128)}, u32[]{:S(2)}) copy-start(s32[128]{0:T(128)} %param.64) | copy-start | bytes 1540
  144.7 10.0 %collective-permute-start.33 = (bf16[64,512]{1,0:T(8,128)(2,1)}, bf16[64,512]{1,0:T(8,128)(2,1)S(1)}, u32[]{:S(2)}, u32[]{:S(2)}) collective-permute-start(bf16[64,512]{1,0:T(8,128)(2,1)} %get-tuple-element.555), channel_id=1, source_target_pairs={{0,8},{8,16},{16,24},{1,9},{9,17},{17,25},{2,10},{10,18},{18,26},{... | collective-permute-start | bytes 196616 | tf_op jit(solution)/shard_map/ppermute | solution.py:18
  156.0 6.0 %collective-permute-start.34 = (bf16[64,512]{1,0:T(8,128)(2,1)S(1)}, bf16[64,512]{1,0:T(8,128)(2,1)S(1)}, u32[]{:S(2)}, u32[]{:S(2)}) collective-permute-start(bf16[64,512]{1,0:T(8,128)(2,1)S(1)} %get-tuple-element.479), channel_id=1, source_target_pairs={{0,1},{1,2},{2,3},{3,4},{4,5},{5,6},{6,7},{7,0},{8,9},{9,10},{10,1... | collective-permute-start | bytes 196616 | tf_op jit(solution)/shard_map/ppermute | solution.py:12
  158.0 4.1 %collective-permute-start.35 = (bf16[64,512]{1,0:T(8,128)(2,1)S(1)}, bf16[64,512]{1,0:T(8,128)(2,1)S(1)}, u32[]{:S(2)}, u32[]{:S(2)}) collective-permute-start(bf16[64,512]{1,0:T(8,128)(2,1)S(1)} %get-tuple-element.478), channel_id=1, source_target_pairs={{0,7},{1,0},{2,1},{3,2},{4,3},{5,4},{6,5},{7,6},{8,15},{9,8},{10,9... | collective-permute-start | bytes 196616 | tf_op jit(solution)/shard_map/ppermute | solution.py:12
  158.8 6.0 %collective-permute-start.36 = (bf16[64,512]{1,0:T(8,128)(2,1)S(1)}, bf16[64,512]{1,0:T(8,128)(2,1)S(1)}, u32[]{:S(2)}, u32[]{:S(2)}) collective-permute-start(bf16[64,512]{1,0:T(8,128)(2,1)S(1)} %get-tuple-element.477), channel_id=1, source_target_pairs={{0,2},{1,3},{2,4},{3,5},{4,6},{5,7},{6,0},{7,1},{8,10},{9,11},{10,... | collective-permute-start | bytes 196616 | tf_op jit(solution)/shard_map/ppermute | solution.py:12
  158.8 6.0 %collective-permute-start.37 = (bf16[64,512]{1,0:T(8,128)(2,1)S(1)}, bf16[64,512]{1,0:T(8,128)(2,1)S(1)}, u32[]{:S(2)}, u32[]{:S(2)}) collective-permute-start(bf16[64,512]{1,0:T(8,128)(2,1)S(1)} %get-tuple-element.476), channel_id=1, source_target_pairs={{0,6},{1,7},{2,0},{3,1},{4,2},{5,3},{6,4},{7,5},{8,14},{9,15},{10,... | collective-permute-start | bytes 196616 | tf_op jit(solution)/shard_map/ppermute | solution.py:12
  (5 other events, 3.9 us)
Sparse Core Ops, SparseCore 0:
  167.5 63.3 all-reduce.1
where the time goes:
time: 242 us; the launch traced here: 239 us
  waiting for transfers between devices  104 us (43%)
  starting transfers between devices  79.7 us (33%)
  local copies, waits for them, and re-layouts  26.3 us (11%)
  between operations  14 us (6%)
  matrix products  9.83 us (4%)
  other arithmetic  4.82 us (2%)
    psum x1, waiting for transfers between devices, from_root(): return lax.psum(kept, axis)  63.5 us
    ppermute x28, starting transfers between devices, from_behind(): return lax.ppermute(value, axis, pairs)  51.2 us
    ppermute x10, starting transfers between devices, from_behind_2(): return lax.ppermute(block, axis, route)  28.5 us
    ppermute x28, waiting for transfers between devices, from_behind(): return lax.ppermute(value, axis, pairs)  27 us
    ppermute x10, waiting for transfers between devices, from_behind_2(): return lax.ppermute(block, axis, route)  13.5 us
    gather x7, local copies, waits for them, and re-layouts, body(): outgoing[send_rows]  8.07 us
    gather x4, local copies, waits for them, and re-layouts, renew(): fetched = extended[source_rows].reshape(mesh_rows, fanout, width)  7.89 us
    dot_general x4, matrix products, renew(): jnp.dot(edges.reshape(mesh_rows * fanout, width), weights[1], preferred_e...  6.48 us
  transfers between devices with their start and end apart: 39, of which 21 were waited for; matrix products, arithmetic and copies ran while one was open for 3% of the time, Pallas kernels for 0%

commit v1 on v0

--- a/solution.py
+++ b/solution.py
@@ -1,9 +1,15 @@
+import functools
+
 import jax
 import jax.numpy as jnp
 from jax import lax
+from jax.experimental import pallas as pl
+from jax.experimental.pallas import tpu as pltpu
 from jax.sharding import PartitionSpec as P
 
 epsilon = 1e-05
+VMEM = pl.BlockSpec(memory_space=pltpu.VMEM)
+SMEM = pl.BlockSpec(memory_space=pltpu.SMEM)
 
 
 def from_behind(value, axis, steps):
@@ -27,7 +33,7 @@
     return values * lax.rsqrt(jnp.mean(values * values, axis=-1, keepdims=True) + epsilon)
 
 
-def body(
+def streamed(
     grid_state,
     w_embed,
     w_project,
@@ -141,9 +147,247 @@
     return lax.dynamic_slice_in_dim(everything, segment_index * share, share, 0)
 
 
+def silu_by_tanh(values):
+    half = 0.5 * values
+    return half + half * jnp.tanh(half)
+
+
+def matmul(left, right):
+    return jnp.dot(left, right, preferred_element_type=jnp.float32)
+
+
+def matmul_nt(left, right):
+    return lax.dot_general(left, right, (((1,), (1,)), ((), ())), preferred_element_type=jnp.float32)
+
+
+def matmul_tn(left, right):
+    return lax.dot_general(left, right, (((0,), (0,)), ((), ())), preferred_element_type=jnp.float32)
+
+
+def encode_kernel(counts, snapshot, w_embed, grid_mesh, neighbors, send_rows, payload, latent_out):
+    mesh_rows = neighbors.shape[1]
+    fanout = neighbors.shape[0]
+    grid_rows = snapshot.shape[1]
+    lists, halo_rows = send_rows.shape
+    width = w_embed.shape[1]
+    latent = silu_by_tanh(matmul_tn(snapshot[...], w_embed[...])).astype(jnp.bfloat16)
+    latent_out[...] = latent
+    table = lax.broadcasted_iota(jnp.int32, (mesh_rows, grid_rows), 0) == grid_mesh[...]
+    pooled = matmul(jnp.where(table, 1.0, 0.0).astype(jnp.bfloat16), latent)
+    payload[:mesh_rows, :] = rms_scale(pooled).astype(jnp.bfloat16)
+    near = neighbors[...]
+    block = near // mesh_rows
+    row = near - block * mesh_rows
+    position = lax.broadcasted_iota(jnp.int32, (1, halo_rows), 1)
+    rows = []
+    for list_index in range(lists):
+        kept = position < counts[list_index]
+        rows.append(jnp.where(kept, send_rows[list_index : list_index + 1, :], mesh_rows))
+    rows.append(jnp.zeros((fanout - lists, halo_rows), jnp.int32))
+    filler = jnp.zeros((fanout, 128 - mesh_rows), jnp.int32)
+    pieces = [block, filler, row, filler, jnp.concatenate(rows, axis=0), filler]
+    coded = jnp.concatenate(pieces + [jnp.zeros((fanout, width - 384), jnp.int32)], axis=1)
+    coded = jnp.concatenate([coded, jnp.zeros_like(coded)], axis=0)
+    payload[mesh_rows:, :] = coded.astype(jnp.float32).astype(jnp.bfloat16)
+
+
+def index_kernel(parts, mesh_rows, active, *refs):
+    payloads, (index_out, state_out) = refs[:parts], refs[parts:]
+    fanout = index_out.shape[0]
+
+    @pl.when(active[0] == 1)
+    def _():
+        tables = []
+        for part in range(parts):
+            state_out[part * mesh_rows : (part + 1) * mesh_rows, :] = payloads[part][:mesh_rows, :]
+            coded = payloads[part][mesh_rows:, :384].astype(jnp.float32).astype(jnp.int32)
+            tables.append(coded[:fanout])
+        for part in range(parts):
+            block = tables[part][:, :128]
+            row = tables[part][:, 128:256]
+            found = part * mesh_rows + row
+            for list_index, offset in enumerate((-1, 1, -2, 2)):
+                source = (part + offset) % parts
+                lists = tables[source][list_index : list_index + 1, 256:384]
+                lists = jnp.broadcast_to(lists, (fanout, 128))
+                picked = jnp.take_along_axis(lists, row, axis=1)
+                picked = jnp.where(picked == mesh_rows, parts * mesh_rows, source * mesh_rows + picked)
+                found = jnp.where(block == list_index + 1, picked, found)
+            index_out[:, part * mesh_rows : (part + 1) * mesh_rows] = found[:, :mesh_rows]
+
+
+def layer_kernel(active, index, state_in, w_project, w_message, w_update, state_out):
+    nodes, width = state_in.shape
+    fanout = index.shape[0]
+    chunk = min(256, nodes)
+
+    @pl.when(active[0] == 1)
+    def _():
+        state = state_in[...]
+        sender = matmul(state, w_project[0, :, width:]).astype(jnp.bfloat16)
+        columns = jnp.concatenate([index[...], jnp.zeros((128 - fanout, nodes), jnp.int32)], axis=0)
+        columns = jnp.transpose(columns.astype(jnp.float32))
+        names = lax.broadcasted_iota(jnp.int32, (chunk, nodes), 1).astype(jnp.float32)
+        for start in range(0, nodes, chunk):
+            own = state_in[start : start + chunk, :]
+            receiver = matmul(own, w_project[0, :, :width])
+            total = jnp.zeros((chunk, width), jnp.float32)
+            for k in range(fanout):
+                hit = columns[start : start + chunk, k : k + 1] == names
+                fetched = matmul(jnp.where(hit, 1.0, 0.0).astype(jnp.bfloat16), sender)
+                edge = silu_by_tanh(receiver + fetched).astype(jnp.bfloat16)
+                total = total + edge.astype(jnp.float32)
+            gathered = (total * (1.0 / fanout)).astype(jnp.bfloat16)
+            aggregate = matmul(gathered, w_message[0]).astype(jnp.bfloat16)
+            update = silu_by_tanh(
+                matmul(own, w_update[0, :width, :]) + matmul(aggregate, w_update[0, width:, :])
+            )
+            renewed = own.astype(jnp.float32) + rms_scale(update)
+            state_out[start : start + chunk, :] = renewed.astype(jnp.bfloat16)
+
+
+def prepare_kernel(latent, w_decode, ready):
+    ready[...] = matmul(latent[...], w_decode[: latent.shape[1], :])
+
+
+def decode_kernel(parts, ready, mesh_grid, w_decode, w_output, *refs):
+    blocks, out = refs[:parts], refs[parts]
+    width = ready.shape[1]
+    state = blocks[0][...]
+    for other in blocks[1:]:
+        state = state + other[...]
+    mesh_rows = state.shape[0]
+    grid_rows = ready.shape[0]
+    table = lax.broadcasted_iota(jnp.int32, (mesh_rows, grid_rows), 0) == mesh_grid[...]
+    readout = matmul_tn(jnp.where(table, 1.0, 0.0).astype(jnp.bfloat16), state).astype(jnp.bfloat16)
+    hidden = silu_by_tanh(ready[...] + matmul(readout, w_decode[width:, :])).astype(jnp.bfloat16)
+    out[...] = matmul_nt(w_output[...], hidden).astype(jnp.bfloat16)
+
+
+def call(kernel, name, shapes, inputs, scalars=1, flops=0, moved=0):
+    return pl.pallas_call(
+        kernel,
+        out_shape=shapes,
+        in_specs=[SMEM] * scalars + [VMEM] * (len(inputs) - scalars),
+        out_specs=[VMEM] * len(shapes),
+        name=name,
+        compiler_params=pltpu.CompilerParams(vmem_limit_bytes=40 * 1024 * 1024),
+        cost_estimate=pl.CostEstimate(flops=flops, bytes_accessed=moved, transcendentals=0),
+    )(*inputs)
+
+
+def resident(
+    grid_state,
+    w_embed,
+    w_project,
+    w_message,
+    w_update,
+    w_decode,
+    w_output,
+    grid_mesh,
+    mesh_grid,
+    neighbors,
+    send_rows,
+    halo_count,
+):
+    segment = lax.axis_index("segment")
+    place = lax.axis_index("dom")
+    segments = lax.axis_size("segment")
+    parts = lax.axis_size("dom")
+    samples, grid_rows, channels = grid_state.shape
+    width = w_embed.shape[1]
+    mesh_rows, fanout = neighbors.shape
+    nodes = parts * mesh_rows
+    group = parts // samples
+    bf16 = jnp.bfloat16
+
+    def device(at_segment, at_dom):
+        return at_segment * parts + at_dom
+
+    snapshot = lax.dynamic_index_in_dim(jnp.transpose(grid_state, (2, 0, 1)), segment, 1, keepdims=False)
+    payload, latent = call(
+        encode_kernel,
+        "encode",
+        [
+            jax.ShapeDtypeStruct((mesh_rows + 2 * fanout, width), bf16),
+            jax.ShapeDtypeStruct((grid_rows, width), bf16),
+        ],
+        [
+            halo_count.reshape(-1),
+            snapshot,
+            w_embed,
+            grid_mesh.reshape(1, grid_rows),
+            neighbors.T,
+            send_rows,
+        ],
+    )
+    payloads = []
+    for turn in range(parts):
+        pairs = [
+            (device(m, (m * group + turn) % parts), device(0, m * group)) for m in range(samples)
+        ]
+        payloads.append(lax.ppermute(payload, ("segment", "dom"), pairs))
+    is_owner = place % group == 0
+
+    def active(at_segment):
+        return ((segment == at_segment) & is_owner).astype(jnp.int32).reshape(1)
+
+    index, state = call(
+        functools.partial(index_kernel, parts, mesh_rows),
+        "index",
+        [jax.ShapeDtypeStruct((fanout, nodes), jnp.int32), jax.ShapeDtypeStruct((nodes, width), bf16)],
+        [active(0)] + payloads,
+    )
+    indices = [index]
+    for at_segment in range(1, segments):
+        pairs = [(device(0, m * group), device(at_segment, m * group)) for m in range(samples)]
+        indices.append(lax.ppermute(index, ("segment", "dom"), pairs))
+    for at_segment in range(segments):
+        (state,) = call(
+            layer_kernel,
+            "layer",
+            [jax.ShapeDtypeStruct((nodes, width), bf16)],
+            [active(at_segment), indices[at_segment], state, w_project, w_message, w_update],
+        )
+        if at_segment + 1 < segments:
+            pairs = [
+                (device(at_segment, m * group), device(at_segment + 1, m * group)) for m in range(samples)
+            ]
+            state = lax.ppermute(state, ("segment", "dom"), pairs)
+        if at_segment == 0:
+            (ready,) = call(
+                prepare_kernel,
+                "prepare",
+                [jax.ShapeDtypeStruct((grid_rows, width), jnp.float32)],
+                [latent, w_decode],
+                scalars=0,
+            )
+    blocks = []
+    for turn in range(parts):
+        pairs = [
+            (device(segments - 1, m * group), device(m, (m * group + turn) % parts))
+            for m in range(samples)
+        ]
+        block = state[turn * mesh_rows : (turn + 1) * mesh_rows]
+        blocks.append(lax.ppermute(block, ("segment", "dom"), pairs))
+    (prediction,) = call(
+        functools.partial(decode_kernel, parts),
+        "decode",
+        [jax.ShapeDtypeStruct((channels, grid_rows), bf16)],
+        [ready, mesh_grid.reshape(1, grid_rows), w_decode, w_output.T] + blocks,
+        scalars=0,
+    )
+    return prediction.T.reshape(1, grid_rows, channels)
+
+
+def fits(mesh):
+    segments, parts = mesh.shape["segment"], mesh.shape["dom"]
+    return parts % segments == 0 and parts <= 16
+
+
 def solution(mesh):
     return jax.shard_map(
-        body,
+        resident if fits(mesh) else streamed,
         mesh=mesh,
         in_specs=(
             P(None, "dom", None),

time: 242 us -> 97.9 us (0.40)
  the two profiles are of different devices: /device:TPU:3 before, /device:TPU:25 now
where the time goes in v1:
time: 97.9 us; the launch traced here: 97.2 us
  waiting for transfers between devices  61.1 us (62%)
  starting transfers between devices  23.3 us (24%)
  local copies, waits for them, and re-layouts  6.71 us (7%)
  Pallas kernels  5.59 us (6%)
    ppermute x8, waiting for transfers between devices, resident(): blocks.append(lax.ppermute(block, ('segment', 'dom'), pairs))  59.4 us
    ppermute x8, starting transfers between devices, resident(): payloads.append(lax.ppermute(payload, ('segment', 'dom'), pairs))  10.8 us
    unnamed x29, local copies, waits for them, and re-layouts  6.55 us
    ppermute x8, starting transfers between devices, resident(): blocks.append(lax.ppermute(block, ('segment', 'dom'), pairs))  6.08 us
    pallas_call x8, Pallas kernels, call(): pl.pallas_call(kernel, out_shape=shapes, in_specs=[SMEM] * scalars + [VME...  5.59 us
    ppermute x3, starting transfers between devices, resident(): state = lax.ppermute(state, ('segment', 'dom'), pairs)  4.49 us
  transfers between devices with their start and end apart: 22, of which 2 were waited for; matrix products, arithmetic and copies ran while one was open for 0% of the time, Pallas kernels for 0%

profile of v1, /device:TPU:25, one launch (start us, length us, event | category | flops | bytes accessed | tf_op | source)
XLA Modules:
  0.0 97.2 jit_solution(17862077658454118689)
XLA Ops:
  0.0 0.9 copy-done
  0.9 0.1 constant_dynamic-slice_fusion
  1.1 0.0 copy-start.9
  1.1 0.7 copy-done.9
  1.8 0.7 copy-done.10
  2.5 0.7 copy-done.11
  3.1 0.7 copy-done.12
  3.8 1.0 %encode.1 = (bf16[80,512]{1,0:T(8,128)(2,1)S(1)}, bf16[128,512]{1,0:T(8,128)(2,1)S(1)}) custom-call(s32[4]{0:T(128)S(1)} %bitcast.20, bf16[227,128]{1,0:T(8,128)(2,1)S(1)} %bitcast.17, bf16[227,512]{1,0:T(8,128)(2,1)S(1)} %copy-done.7, s32[1,128]{1,0:T(1,128)S(1)} %bitcast.21, s32[8,64]{1,0:T(8,128)S(1)} %bitcast.19, s32[4,64]{1,0:T(4,128)S(1)} %copy-done.10), custom_call_target="tpu_custom_call" | custom-call | tf_op jit(solution)/shard_map/encode/pallas_call | solution.py:268
  4.8 0.7 collective-permute-start
  5.5 0.7 collective-permute-start.1
  6.1 0.7 collective-permute-start.2
  6.8 0.7 collective-permute-start.3
  7.5 0.7 collective-permute-start.4
  8.2 0.7 collective-permute-start.5
  8.8 0.0 collective-permute-done.1.refs_1_
  8.8 0.7 collective-permute-start.6
  9.5 6.1 %collective-permute-start.7 = (bf16[80,512]{1,0:T(8,128)(2,1)S(1)}, bf16[80,512]{1,0:T(8,128)(2,1)S(1)}, u32[]{:S(2)}, u32[]{:S(2)}) collective-permute-start(bf16[80,512]{1,0:T(8,128)(2,1)S(1)} %get-tuple-element.10), channel_id=1, source_target_pairs={{7,0},{9,2},{19,4},{29,6}} | collective-permute-start | bytes 245768 | tf_op jit(solution)/shard_map/ppermute | solution.py:329
  15.7 0.0 collective-permute-done.4.refs_4_
  15.7 0.0 collective-permute-done.5.refs_5_
  15.8 1.6 %collective-permute-done.7.refs_7_ = bf16[80,512]{1,0:T(8,128)(2,1)S(1)} collective-permute-done((bf16[80,512]{1,0:T(8,128)(2,1)S(1)}, bf16[80,512]{1,0:T(8,128)(2,1)S(1)}, u32[]{:S(2)}, u32[]{:S(2)}) %collective-permute-start.7) | collective-permute-done | bytes 81952 | tf_op jit(solution)/shard_map/ppermute | solution.py:329
  17.4 1.2 %copy-done.2 = bf16[1,1024,512]{2,1,0:T(8,128)(2,1)S(1)} copy-done((bf16[1,1024,512]{2,1,0:T(8,128)(2,1)S(1)}, bf16[1,1024,512]{2,1,0:T(8,128)(2,1)}, u32[]{:S(2)}) %copy-start.2) | copy-done | bytes 1048600
  18.6 1.0 %copy-done.4 = bf16[1,512,512]{2,1,0:T(8,128)(2,1)S(1)} copy-done((bf16[1,512,512]{2,1,0:T(8,128)(2,1)S(1)}, bf16[1,512,512]{2,1,0:T(8,128)(2,1)}, u32[]{:S(2)}) %copy-start.4) | copy-done | bytes 524312
  19.7 1.6 %collective-permute-start.11 = (bf16[512,512]{1,0:T(8,128)(2,1)S(1)}, bf16[512,512]{1,0:T(8,128)(2,1)}, u32[]{:S(2)}, u32[]{:S(2)}) collective-permute-start(bf16[512,512]{1,0:T(8,128)(2,1)S(1)} %layer.4), channel_id=1, source_target_pairs={{0,8},{2,10},{4,12},{6,14}} | collective-permute-start | bytes 1572872 | tf_op jit(solution)/shard_map/ppermute | solution.py:356
  21.2 0.7 collective-permute-start.10
  21.9 0.0 collective-permute-done.10.index
  21.9 0.0 collective-permute-done.11.state_in
  22.0 1.0 %layer.5 = bf16[512,512]{1,0:T(8,128)(2,1)S(1)} custom-call(s32[1]{0:T(128)} %bitcast.10.active, s32[8,512]{1,0:T(8,128)S(1)} %collective-permute-done.10.index, bf16[512,512]{1,0:T(8,128)(2,1)} %collective-permute-done.11.state_in, bf16[1,512,1024]{2,1,0:T(8,128)(2,1)S(1)} %copy-done.1, bf16[1,512,512]{2,1,0:T(8,128)(2,1)S(1)} %copy-done.5, ...), custom_call_target="tpu_custom_call" | custom-call | tf_op jit(solution)/shard_map/layer/pallas_call | solution.py:268
  23.0 1.5 %collective-permute-start.12 = (bf16[512,512]{1,0:T(8,128)(2,1)S(1)}, bf16[512,512]{1,0:T(8,128)(2,1)}, u32[]{:S(2)}, u32[]{:S(2)}) collective-permute-start(bf16[512,512]{1,0:T(8,128)(2,1)S(1)} %layer.5), channel_id=1, source_target_pairs={{8,16},{10,18},{12,20},{14,22}} | collective-permute-start | bytes 1572872 | tf_op jit(solution)/shard_map/ppermute | solution.py:356
  24.5 0.7 collective-permute-start.9
  25.1 0.0 collective-permute-done.9.index
  25.1 1.0 %layer.6 = bf16[512,512]{1,0:T(8,128)(2,1)S(1)} custom-call(s32[1]{0:T(128)} %bitcast.9.active, s32[8,512]{1,0:T(8,128)S(1)} %collective-permute-done.9.index, bf16[512,512]{1,0:T(8,128)(2,1)} %collective-permute-done.12.state_in, bf16[1,512,1024]{2,1,0:T(8,128)(2,1)S(1)} %copy-done.1, bf16[1,512,512]{2,1,0:T(8,128)(2,1)S(1)} %copy-done.5, ...), custom_call_target="tpu_custom_call" | custom-call | tf_op jit(solution)/shard_map/layer/pallas_call | solution.py:268
  26.2 1.5 %collective-permute-start.13 = (bf16[512,512]{1,0:T(8,128)(2,1)S(1)}, bf16[512,512]{1,0:T(8,128)(2,1)}, u32[]{:S(2)}, u32[]{:S(2)}) collective-permute-start(bf16[512,512]{1,0:T(8,128)(2,1)S(1)} %layer.6), channel_id=1, source_target_pairs={{16,24},{18,26},{20,28},{22,30}} | collective-permute-start | bytes 1572872 | tf_op jit(solution)/shard_map/ppermute | solution.py:356
  27.6 0.7 collective-permute-start.8
  28.3 0.0 collective-permute-done.8.index
  28.3 1.0 %layer.7 = bf16[512,512]{1,0:T(8,128)(2,1)S(1)} custom-call(s32[1]{0:T(128)} %bitcast.7.active, s32[8,512]{1,0:T(8,128)S(1)} %collective-permute-done.8.index, bf16[512,512]{1,0:T(8,128)(2,1)} %collective-permute-done.13.state_in, bf16[1,512,1024]{2,1,0:T(8,128)(2,1)S(1)} %copy-done.1, bf16[1,512,512]{2,1,0:T(8,128)(2,1)S(1)} %copy-done.5, ...), custom_call_target="tpu_custom_call" | custom-call | tf_op jit(solution)/shard_map/layer/pallas_call | solution.py:268
  29.4 0.8 collective-permute-start.14
  30.2 0.7 collective-permute-start.15
  30.9 0.7 collective-permute-start.16
  31.6 0.7 collective-permute-start.17
  32.2 0.7 collective-permute-start.18
  32.9 0.7 collective-permute-start.19
  33.6 0.7 collective-permute-start.20
  34.3 1.3 %collective-permute-start.21 = (bf16[64,512]{1,0:T(8,128)(2,1)S(1)}, bf16[64,512]{1,0:T(8,128)(2,1)S(1)}, u32[]{:S(2)}, u32[]{:S(2)}) collective-permute-start(bf16[64,512]{1,0:T(8,128)(2,1)S(1)} %get-tuple-element.13), channel_id=1, source_target_pairs={{24,7},{26,9},{28,19},{30,29}} | collective-permute-start | bytes 196616 | tf_op jit(solution)/shard_map/ppermute | solution.py:372
  35.6 0.0 copy-start.8
  35.6 0.2 prepare.1.ready
  35.9 59.4 %collective-permute-done.21.refs_7_ = bf16[64,512]{1,0:T(8,128)(2,1)S(1)} collective-permute-done((bf16[64,512]{1,0:T(8,128)(2,1)S(1)}, bf16[64,512]{1,0:T(8,128)(2,1)S(1)}, u32[]{:S(2)}, u32[]{:S(2)}) %collective-permute-start.21) | collective-permute-done | bytes 65568 | tf_op jit(solution)/shard_map/ppermute | solution.py:372
  95.3 0.7 copy-done.13
  95.9 1.2 %decode.1 = bf16[227,128]{1,0:T(8,128)(2,1)} custom-call(f32[128,512]{1,0:T(8,128)S(1)} %prepare.1.ready, s32[1,128]{1,0:T(1,128)S(1)} %bitcast.22, bf16[1024,512]{1,0:T(8,128)(2,1)S(1)} %copy-done.6, bf16[227,512]{1,0:T(8,128)(2,1)S(1)} %bitcast.18, bf16[64,512]{1,0:T(8,128)(2,1)S(1)} %collective-permute-done.14.refs_0_, ...), custom_call_target="tpu_custom_call" | custom-call | tf_op jit(solution)/shard_map/decode/pallas_call | solution.py:268
  (35 shorter events, 0.1 us)
Async XLA Ops:
  0.0 0.9 copy-start
  0.0 1.1 %copy-start.7 = (bf16[227,512]{1,0:T(8,128)(2,1)S(1)}, bf16[227,512]{1,0:T(8,128)(2,1)}, u32[]{:S(2)}) copy-start(bf16[227,512]{1,0:T(8,128)(2,1)} %w_embed.1) | copy-start | bytes 697348
  0.0 17.4 %copy-start.1 = (bf16[1,512,1024]{2,1,0:T(8,128)(2,1)S(1)}, bf16[1,512,1024]{2,1,0:T(8,128)(2,1)}, u32[]{:S(2)}) copy-start(bf16[1,512,1024]{2,1,0:T(8,128)(2,1)} %w_project.7) | copy-start | bytes 3145732
  1.1 0.7 copy-start.9
  1.8 0.7 copy-start.10
  2.5 0.7 copy-start.11
  3.1 0.7 copy-start.12
  4.8 3.4 %collective-permute-start = (bf16[80,512]{1,0:T(8,128)(2,1)S(1)}, bf16[80,512]{1,0:T(8,128)(2,1)S(1)}, u32[]{:S(2)}, u32[]{:S(2)}) collective-permute-start(bf16[80,512]{1,0:T(8,128)(2,1)S(1)} %get-tuple-element.10), channel_id=1, source_target_pairs={{0,0},{10,2},{20,4},{30,6}} | collective-permute-start | bytes 245768 | tf_op jit(solution)/shard_map/ppermute | solution.py:329
  5.5 3.4 %collective-permute-start.1 = (bf16[80,512]{1,0:T(8,128)(2,1)S(1)}, bf16[80,512]{1,0:T(8,128)(2,1)S(1)}, u32[]{:S(2)}, u32[]{:S(2)}) collective-permute-start(bf16[80,512]{1,0:T(8,128)(2,1)S(1)} %get-tuple-element.10), channel_id=1, source_target_pairs={{1,0},{11,2},{21,4},{31,6}} | collective-permute-start | bytes 245768 | tf_op jit(solution)/shard_map/ppermute | solution.py:329
  6.1 3.4 %collective-permute-start.2 = (bf16[80,512]{1,0:T(8,128)(2,1)S(1)}, bf16[80,512]{1,0:T(8,128)(2,1)S(1)}, u32[]{:S(2)}, u32[]{:S(2)}) collective-permute-start(bf16[80,512]{1,0:T(8,128)(2,1)S(1)} %get-tuple-element.10), channel_id=1, source_target_pairs={{2,0},{12,2},{22,4},{24,6}} | collective-permute-start | bytes 245768 | tf_op jit(solution)/shard_map/ppermute | solution.py:329
  6.8 8.9 %collective-permute-start.3 = (bf16[80,512]{1,0:T(8,128)(2,1)S(1)}, bf16[80,512]{1,0:T(8,128)(2,1)S(1)}, u32[]{:S(2)}, u32[]{:S(2)}) collective-permute-start(bf16[80,512]{1,0:T(8,128)(2,1)S(1)} %get-tuple-element.10), channel_id=1, source_target_pairs={{3,0},{13,2},{23,4},{25,6}} | collective-permute-start | bytes 245768 | tf_op jit(solution)/shard_map/ppermute | solution.py:329
  7.5 8.2 %collective-permute-start.4 = (bf16[80,512]{1,0:T(8,128)(2,1)S(1)}, bf16[80,512]{1,0:T(8,128)(2,1)S(1)}, u32[]{:S(2)}, u32[]{:S(2)}) collective-permute-start(bf16[80,512]{1,0:T(8,128)(2,1)S(1)} %get-tuple-element.10), channel_id=1, source_target_pairs={{4,0},{14,2},{16,4},{26,6}} | collective-permute-start | bytes 245768 | tf_op jit(solution)/shard_map/ppermute | solution.py:329
  8.2 7.6 %collective-permute-start.5 = (bf16[80,512]{1,0:T(8,128)(2,1)S(1)}, bf16[80,512]{1,0:T(8,128)(2,1)S(1)}, u32[]{:S(2)}, u32[]{:S(2)}) collective-permute-start(bf16[80,512]{1,0:T(8,128)(2,1)S(1)} %get-tuple-element.10), channel_id=1, source_target_pairs={{5,0},{15,2},{17,4},{27,6}} | collective-permute-start | bytes 245768 | tf_op jit(solution)/shard_map/ppermute | solution.py:329
  8.8 6.9 %collective-permute-start.6 = (bf16[80,512]{1,0:T(8,128)(2,1)S(1)}, bf16[80,512]{1,0:T(8,128)(2,1)S(1)}, u32[]{:S(2)}, u32[]{:S(2)}) collective-permute-start(bf16[80,512]{1,0:T(8,128)(2,1)S(1)} %get-tuple-element.10), channel_id=1, source_target_pairs={{6,0},{8,2},{18,4},{28,6}} | collective-permute-start | bytes 245768 | tf_op jit(solution)/shard_map/ppermute | solution.py:329
  9.5 7.9 %collective-permute-start.7 = (bf16[80,512]{1,0:T(8,128)(2,1)S(1)}, bf16[80,512]{1,0:T(8,128)(2,1)S(1)}, u32[]{:S(2)}, u32[]{:S(2)}) collective-permute-start(bf16[80,512]{1,0:T(8,128)(2,1)S(1)} %get-tuple-element.10), channel_id=1, source_target_pairs={{7,0},{9,2},{19,4},{29,6}} | collective-permute-start | bytes 245768 | tf_op jit(solution)/shard_map/ppermute | solution.py:329
  17.4 1.2 %copy-start.2 = (bf16[1,1024,512]{2,1,0:T(8,128)(2,1)S(1)}, bf16[1,1024,512]{2,1,0:T(8,128)(2,1)}, u32[]{:S(2)}) copy-start(bf16[1,1024,512]{2,1,0:T(8,128)(2,1)} %w_update.7) | copy-start | bytes 3145732
  18.6 1.0 %copy-start.4 = (bf16[1,512,512]{2,1,0:T(8,128)(2,1)S(1)}, bf16[1,512,512]{2,1,0:T(8,128)(2,1)}, u32[]{:S(2)}) copy-start(bf16[1,512,512]{2,1,0:T(8,128)(2,1)} %w_message.7) | copy-start | bytes 1572868
  19.7 2.3 %copy-start.3 = (bf16[1,1024,512]{2,1,0:T(8,128)(2,1)S(1)}, bf16[1,1024,512]{2,1,0:T(8,128)(2,1)}, u32[]{:S(2)}) copy-start(bf16[1,1024,512]{2,1,0:T(8,128)(2,1)} %w_update.7) | copy-start | bytes 3145732
  19.7 2.3 %copy-start.5 = (bf16[1,512,512]{2,1,0:T(8,128)(2,1)S(1)}, bf16[1,512,512]{2,1,0:T(8,128)(2,1)}, u32[]{:S(2)}) copy-start(bf16[1,512,512]{2,1,0:T(8,128)(2,1)} %w_message.7) | copy-start | bytes 1572868
  19.7 2.3 %collective-permute-start.11 = (bf16[512,512]{1,0:T(8,128)(2,1)S(1)}, bf16[512,512]{1,0:T(8,128)(2,1)}, u32[]{:S(2)}, u32[]{:S(2)}) collective-permute-start(bf16[512,512]{1,0:T(8,128)(2,1)S(1)} %layer.4), channel_id=1, source_target_pairs={{0,8},{2,10},{4,12},{6,14}} | collective-permute-start | bytes 1572872 | tf_op jit(solution)/shard_map/ppermute | solution.py:356
  21.2 0.7 collective-permute-start.10
  23.0 2.1 %collective-permute-start.12 = (bf16[512,512]{1,0:T(8,128)(2,1)S(1)}, bf16[512,512]{1,0:T(8,128)(2,1)}, u32[]{:S(2)}, u32[]{:S(2)}) collective-permute-start(bf16[512,512]{1,0:T(8,128)(2,1)S(1)} %layer.5), channel_id=1, source_target_pairs={{8,16},{10,18},{12,20},{14,22}} | collective-permute-start | bytes 1572872 | tf_op jit(solution)/shard_map/ppermute | solution.py:356
  24.5 0.7 collective-permute-start.9
  26.2 2.1 %collective-permute-start.13 = (bf16[512,512]{1,0:T(8,128)(2,1)S(1)}, bf16[512,512]{1,0:T(8,128)(2,1)}, u32[]{:S(2)}, u32[]{:S(2)}) collective-permute-start(bf16[512,512]{1,0:T(8,128)(2,1)S(1)} %layer.6), channel_id=1, source_target_pairs={{16,24},{18,26},{20,28},{22,30}} | collective-permute-start | bytes 1572872 | tf_op jit(solution)/shard_map/ppermute | solution.py:356
  27.6 0.7 collective-permute-start.8
  29.4 6.2 %copy-start.6 = (bf16[1024,512]{1,0:T(8,128)(2,1)S(1)}, bf16[1024,512]{1,0:T(8,128)(2,1)}, u32[]{:S(2)}) copy-start(bf16[1024,512]{1,0:T(8,128)(2,1)} %w_decode.3) | copy-start | bytes 3145732
  29.4 3.5 %collective-permute-start.14 = (bf16[64,512]{1,0:T(8,128)(2,1)S(1)}, bf16[64,512]{1,0:T(8,128)(2,1)S(1)}, u32[]{:S(2)}, u32[]{:S(2)}) collective-permute-start(bf16[64,512]{1,0:T(8,128)(2,1)S(1)} %get-tuple-element.20), channel_id=1, source_target_pairs={{24,0},{26,10},{28,20},{30,30}} | collective-permute-start | bytes 196616 | tf_op jit(solution)/shard_map/ppermute | solution.py:372
  30.2 3.4 %collective-permute-start.15 = (bf16[64,512]{1,0:T(8,128)(2,1)S(1)}, bf16[64,512]{1,0:T(8,128)(2,1)S(1)}, u32[]{:S(2)}, u32[]{:S(2)}) collective-permute-start(bf16[64,512]{1,0:T(8,128)(2,1)S(1)} %get-tuple-element.19), channel_id=1, source_target_pairs={{24,1},{26,11},{28,21},{30,31}} | collective-permute-start | bytes 196616 | tf_op jit(solution)/shard_map/ppermute | solution.py:372
  30.9 3.4 %collective-permute-start.16 = (bf16[64,512]{1,0:T(8,128)(2,1)S(1)}, bf16[64,512]{1,0:T(8,128)(2,1)S(1)}, u32[]{:S(2)}, u32[]{:S(2)}) collective-permute-start(bf16[64,512]{1,0:T(8,128)(2,1)S(1)} %get-tuple-element.18), channel_id=1, source_target_pairs={{24,2},{26,12},{28,22},{30,24}} | collective-permute-start | bytes 196616 | tf_op jit(solution)/shard_map/ppermute | solution.py:372
  31.6 4.3 %collective-permute-start.17 = (bf16[64,512]{1,0:T(8,128)(2,1)S(1)}, bf16[64,512]{1,0:T(8,128)(2,1)S(1)}, u32[]{:S(2)}, u32[]{:S(2)}) collective-permute-start(bf16[64,512]{1,0:T(8,128)(2,1)S(1)} %get-tuple-element.17), channel_id=1, source_target_pairs={{24,3},{26,13},{28,23},{30,25}} | collective-permute-start | bytes 196616 | tf_op jit(solution)/shard_map/ppermute | solution.py:372
  32.2 3.6 %collective-permute-start.18 = (bf16[64,512]{1,0:T(8,128)(2,1)S(1)}, bf16[64,512]{1,0:T(8,128)(2,1)S(1)}, u32[]{:S(2)}, u32[]{:S(2)}) collective-permute-start(bf16[64,512]{1,0:T(8,128)(2,1)S(1)} %get-tuple-element.16), channel_id=1, source_target_pairs={{24,4},{26,14},{28,16},{30,26}} | collective-permute-start | bytes 196616 | tf_op jit(solution)/shard_map/ppermute | solution.py:372
  32.9 2.9 %collective-permute-start.19 = (bf16[64,512]{1,0:T(8,128)(2,1)S(1)}, bf16[64,512]{1,0:T(8,128)(2,1)S(1)}, u32[]{:S(2)}, u32[]{:S(2)}) collective-permute-start(bf16[64,512]{1,0:T(8,128)(2,1)S(1)} %get-tuple-element.15), channel_id=1, source_target_pairs={{24,5},{26,15},{28,17},{30,27}} | collective-permute-start | bytes 196616 | tf_op jit(solution)/shard_map/ppermute | solution.py:372
  33.6 2.3 %collective-permute-start.20 = (bf16[64,512]{1,0:T(8,128)(2,1)S(1)}, bf16[64,512]{1,0:T(8,128)(2,1)S(1)}, u32[]{:S(2)}, u32[]{:S(2)}) collective-permute-start(bf16[64,512]{1,0:T(8,128)(2,1)S(1)} %get-tuple-element.14), channel_id=1, source_target_pairs={{24,6},{26,8},{28,18},{30,28}} | collective-permute-start | bytes 196616 | tf_op jit(solution)/shard_map/ppermute | solution.py:372
  34.3 61.0 %collective-permute-start.21 = (bf16[64,512]{1,0:T(8,128)(2,1)S(1)}, bf16[64,512]{1,0:T(8,128)(2,1)S(1)}, u32[]{:S(2)}, u32[]{:S(2)}) collective-permute-start(bf16[64,512]{1,0:T(8,128)(2,1)S(1)} %get-tuple-element.13), channel_id=1, source_target_pairs={{24,7},{26,9},{28,19},{30,29}} | collective-permute-start | bytes 196616 | tf_op jit(solution)/shard_map/ppermute | solution.py:372
  35.6 59.7 %copy-start.8 = (bf16[512,227]{0,1:T(8,128)(2,1)S(1)}, bf16[512,227]{0,1:T(8,128)(2,1)}, u32[]{:S(2)}) copy-start(bf16[512,227]{0,1:T(8,128)(2,1)} %param.18) | copy-start | bytes 697348
  95.3 0.7 copy-start.13

commit v2 on v1

--- a/solution.py
+++ b/solution.py
@@ -10,6 +10,7 @@
 epsilon = 1e-05
 VMEM = pl.BlockSpec(memory_space=pltpu.VMEM)
 SMEM = pl.BlockSpec(memory_space=pltpu.SMEM)
+ANY = pl.BlockSpec(memory_space=pl.ANY)
 
 
 def from_behind(value, axis, steps):
@@ -164,7 +165,22 @@
     return lax.dot_general(left, right, (((0,), (0,)), ((), ())), preferred_element_type=jnp.float32)
 
 
-def encode_kernel(counts, snapshot, w_embed, grid_mesh, neighbors, send_rows, payload, latent_out):
+def fetch(sources, targets, semaphores):
+    copies = [
+        pltpu.make_async_copy(source, target, semaphores.at[place])
+        for place, (source, target) in enumerate(zip(sources, targets))
+    ]
+    for copy in copies:
+        copy.start()
+    return copies
+
+
+def encode_kernel(*refs):
+    inputs, (payload, latent_out), held, semaphores = refs[:6], refs[6:8], refs[8:14], refs[14]
+    copies = fetch(inputs, held, semaphores)
+    for copy in copies:
+        copy.wait()
+    snapshot, w_embed, grid_mesh, neighbors, send_rows, counts = held
     mesh_rows = neighbors.shape[1]
     fanout = neighbors.shape[0]
     grid_rows = snapshot.shape[1]
@@ -216,21 +232,24 @@
             index_out[:, part * mesh_rows : (part + 1) * mesh_rows] = found[:, :mesh_rows]
 
 
-def layer_kernel(active, index, state_in, w_project, w_message, w_update, state_out):
+def layer_kernel(active, index, state_in, *refs):
+    inputs, state_out, held, semaphores = refs[:3], refs[3], refs[4:7], refs[7]
     nodes, width = state_in.shape
     fanout = index.shape[0]
     chunk = min(256, nodes)
 
     @pl.when(active[0] == 1)
     def _():
-        state = state_in[...]
-        sender = matmul(state, w_project[0, :, width:]).astype(jnp.bfloat16)
+        copies = fetch([ref.at[0] for ref in inputs], held, semaphores)
+        w_project, w_message, w_update = held
         columns = jnp.concatenate([index[...], jnp.zeros((128 - fanout, nodes), jnp.int32)], axis=0)
         columns = jnp.transpose(columns.astype(jnp.float32))
         names = lax.broadcasted_iota(jnp.int32, (chunk, nodes), 1).astype(jnp.float32)
+        copies[0].wait()
+        sender = matmul(state_in[...], w_project[:, width:]).astype(jnp.bfloat16)
         for start in range(0, nodes, chunk):
             own = state_in[start : start + chunk, :]
-            receiver = matmul(own, w_project[0, :, :width])
+            receiver = matmul(own, w_project[:, :width])
             total = jnp.zeros((chunk, width), jnp.float32)
             for k in range(fanout):
                 hit = columns[start : start + chunk, k : k + 1] == names
@@ -238,9 +257,12 @@
                 edge = silu_by_tanh(receiver + fetched).astype(jnp.bfloat16)
                 total = total + edge.astype(jnp.float32)
             gathered = (total * (1.0 / fanout)).astype(jnp.bfloat16)
-            aggregate = matmul(gathered, w_message[0]).astype(jnp.bfloat16)
+            if start == 0:
+                copies[1].wait()
+                copies[2].wait()
+            aggregate = matmul(gathered, w_message[...]).astype(jnp.bfloat16)
             update = silu_by_tanh(
-                matmul(own, w_update[0, :width, :]) + matmul(aggregate, w_update[0, width:, :])
+                matmul(own, w_update[:width, :]) + matmul(aggregate, w_update[width:, :])
             )
             renewed = own.astype(jnp.float32) + rms_scale(update)
             state_out[start : start + chunk, :] = renewed.astype(jnp.bfloat16)
@@ -250,30 +272,51 @@
     ready[...] = matmul(latent[...], w_decode[: latent.shape[1], :])
 
 
-def decode_kernel(parts, ready, mesh_grid, w_decode, w_output, *refs):
-    blocks, out = refs[:parts], refs[parts]
+def decode_kernel(parts, turn, ready, mesh_grid, w_decode, w_output, *refs):
+    blocks, out, state = refs[:parts], refs[parts], refs[parts + 1]
     width = ready.shape[1]
-    state = blocks[0][...]
-    for other in blocks[1:]:
-        state = state + other[...]
+    for number, block in enumerate(blocks):
+
+        @pl.when(turn[0] == number)
+        def _():
+            state[...] = block[...]
+
     mesh_rows = state.shape[0]
     grid_rows = ready.shape[0]
     table = lax.broadcasted_iota(jnp.int32, (mesh_rows, grid_rows), 0) == mesh_grid[...]
-    readout = matmul_tn(jnp.where(table, 1.0, 0.0).astype(jnp.bfloat16), state).astype(jnp.bfloat16)
+    table = jnp.where(table, 1.0, 0.0).astype(jnp.bfloat16)
+    readout = matmul_tn(table, state[...]).astype(jnp.bfloat16)
     hidden = silu_by_tanh(ready[...] + matmul(readout, w_decode[width:, :])).astype(jnp.bfloat16)
     out[...] = matmul_nt(w_output[...], hidden).astype(jnp.bfloat16)
 
 
-def call(kernel, name, shapes, inputs, scalars=1, flops=0, moved=0):
+def call(kernel, name, shapes, inputs, places, scratch=(), flops=0, moved=0):
+    kinds = {"s": SMEM, "v": VMEM, "a": ANY}
     return pl.pallas_call(
         kernel,
         out_shape=shapes,
-        in_specs=[SMEM] * scalars + [VMEM] * (len(inputs) - scalars),
+        in_specs=[kinds[place] for place in places],
         out_specs=[VMEM] * len(shapes),
+        scratch_shapes=list(scratch),
         name=name,
-        compiler_params=pltpu.CompilerParams(vmem_limit_bytes=40 * 1024 * 1024),
+        compiler_params=pltpu.CompilerParams(vmem_limit_bytes=32 * 1024 * 1024),
         cost_estimate=pl.CostEstimate(flops=flops, bytes_accessed=moved, transcendentals=0),
     )(*inputs)
+
+
+def every_device(pairs, count):
+    onward = dict(pairs)
+    reached = set(onward.values())
+    for first in range(count):
+        if first in reached or first not in onward:
+            continue
+        last = first
+        while last in onward:
+            last = onward[last]
+        onward[last] = first
+    for other in range(count):
+        onward.setdefault(other, other)
+    return sorted(onward.items())
 
 
 def resident(
@@ -302,9 +345,23 @@
     bf16 = jnp.bfloat16
 
     def device(at_segment, at_dom):
-        return at_segment * parts + at_dom
+        return at_segment * parts + at_dom % parts
+
+    def send(value, pairs):
+        return lax.ppermute(value, ("segment", "dom"), every_device(pairs, segments * parts))
+
+    def active(at_segment):
+        return ((segment == at_segment) & (place % group == 0)).astype(jnp.int32).reshape(1)
 
     snapshot = lax.dynamic_index_in_dim(jnp.transpose(grid_state, (2, 0, 1)), segment, 1, keepdims=False)
+    inputs = [
+        snapshot,
+        w_embed,
+        grid_mesh.reshape(1, grid_rows),
+        neighbors.T,
+        send_rows,
+        halo_count.reshape(-1),
+    ]
     payload, latent = call(
         encode_kernel,
         "encode",
@@ -312,70 +369,69 @@
             jax.ShapeDtypeStruct((mesh_rows + 2 * fanout, width), bf16),
             jax.ShapeDtypeStruct((grid_rows, width), bf16),
         ],
-        [
-            halo_count.reshape(-1),
-            snapshot,
-            w_embed,
-            grid_mesh.reshape(1, grid_rows),
-            neighbors.T,
-            send_rows,
-        ],
+        inputs,
+        "aaaaaa",
+        [pltpu.VMEM(value.shape, value.dtype) for value in inputs[:-1]]
+        + [pltpu.SMEM(inputs[-1].shape, jnp.int32), pltpu.SemaphoreType.DMA((6,))],
     )
     payloads = []
     for turn in range(parts):
-        pairs = [
-            (device(m, (m * group + turn) % parts), device(0, m * group)) for m in range(samples)
-        ]
-        payloads.append(lax.ppermute(payload, ("segment", "dom"), pairs))
-    is_owner = place % group == 0
-
-    def active(at_segment):
-        return ((segment == at_segment) & is_owner).astype(jnp.int32).reshape(1)
-
+        pairs = [(device(m, m * group + turn), device(0, m * group)) for m in range(samples)]
+        payloads.append(send(payload, pairs))
     index, state = call(
         functools.partial(index_kernel, parts, mesh_rows),
         "index",
         [jax.ShapeDtypeStruct((fanout, nodes), jnp.int32), jax.ShapeDtypeStruct((nodes, width), bf16)],
         [active(0)] + payloads,
+        "s" + "v" * parts,
     )
     indices = [index]
     for at_segment in range(1, segments):
         pairs = [(device(0, m * group), device(at_segment, m * group)) for m in range(samples)]
-        indices.append(lax.ppermute(index, ("segment", "dom"), pairs))
+        indices.append(send(index, pairs))
+    weights = [w_project, w_message, w_update]
     for at_segment in range(segments):
         (state,) = call(
             layer_kernel,
             "layer",
             [jax.ShapeDtypeStruct((nodes, width), bf16)],
-            [active(at_segment), indices[at_segment], state, w_project, w_message, w_update],
+            [active(at_segment), indices[at_segment], state] + weights,
+            "svvaaa",
+            [pltpu.VMEM(weight.shape[1:], bf16) for weight in weights] + [pltpu.SemaphoreType.DMA((3,))],
         )
         if at_segment + 1 < segments:
             pairs = [
                 (device(at_segment, m * group), device(at_segment + 1, m * group)) for m in range(samples)
             ]
-            state = lax.ppermute(state, ("segment", "dom"), pairs)
+            state = send(state, pairs)
         if at_segment == 0:
             (ready,) = call(
                 prepare_kernel,
                 "prepare",
                 [jax.ShapeDtypeStruct((grid_rows, width), jnp.float32)],
                 [latent, w_decode],
-                scalars=0,
+                "vv",
             )
     blocks = []
     for turn in range(parts):
         pairs = [
-            (device(segments - 1, m * group), device(m, (m * group + turn) % parts))
-            for m in range(samples)
+            (device(segments - 1, m * group), device(m, m * group + turn)) for m in range(samples)
         ]
-        block = state[turn * mesh_rows : (turn + 1) * mesh_rows]
-        blocks.append(lax.ppermute(block, ("segment", "dom"), pairs))
+        blocks.append(send(state[turn * mesh_rows : (turn + 1) * mesh_rows], pairs))
     (prediction,) = call(
         functools.partial(decode_kernel, parts),
         "decode",
         [jax.ShapeDtypeStruct((channels, grid_rows), bf16)],
-        [ready, mesh_grid.reshape(1, grid_rows), w_decode, w_output.T] + blocks,
-        scalars=0,
+        [
+            ((place - segment * group) % parts).reshape(1),
+            ready,
+            mesh_grid.reshape(1, grid_rows),
+            w_decode,
+            w_output.T,
+        ]
+        + blocks,
+        "s" + "v" * (4 + parts),
+        [pltpu.VMEM((mesh_rows, width), bf16)],
     )
     return prediction.T.reshape(1, grid_rows, channels)
 

time: 97.9 us -> 114 us (1.16)
  the two profiles are of different devices: /device:TPU:25 before, /device:TPU:6 now
where the time goes in v2:
time: 114 us; the launch traced here: 113 us
  starting transfers between devices  81.3 us (71%)
  waiting for transfers between devices  12.3 us (11%)
  Pallas kernels  12.2 us (11%)
  local copies, waits for them, and re-layouts  6.71 us (6%)
    ppermute x22, starting transfers between devices, send(): lax.ppermute(value, ('segment', 'dom'), every_device(pairs, segments * pa...  81.3 us
    ppermute x22, waiting for transfers between devices, send(): lax.ppermute(value, ('segment', 'dom'), every_device(pairs, segments * pa...  12.3 us
    pallas_call x8, Pallas kernels, call(): pl.pallas_call(kernel, out_shape=shapes, in_specs=[kinds[place] for place...  12.2 us
    unnamed x29, local copies, waits for them, and re-layouts  6.55 us
  transfers between devices with their start and end apart: 22, of which 6 were waited for; matrix products, arithmetic and copies ran while one was open for 0% of the time, Pallas kernels for 0%

profile of v2, /device:TPU:6, one launch (start us, length us, event | category | flops | bytes accessed | tf_op | source)
XLA Modules:
  0.0 113.0 jit_solution(191681789817780403)
XLA Ops:
  0.0 0.9 copy-done
  0.9 0.1 constant_dynamic-slice_fusion
  1.1 0.0 copy-start.9
  1.1 0.7 copy-done.9
  1.8 0.7 copy-done.10
  2.5 0.7 copy-done.11
  3.1 0.7 copy-done.12
  3.8 1.4 %encode.1 = (bf16[80,512]{1,0:T(8,128)(2,1)S(1)}, bf16[128,512]{1,0:T(8,128)(2,1)S(1)}) custom-call(bf16[227,128]{1,0:T(8,128)(2,1)S(1)} %bitcast.18, bf16[227,512]{1,0:T(8,128)(2,1)S(1)} %copy-done.7, s32[1,128]{1,0:T(1,128)S(1)} %bitcast.21, s32[8,64]{1,0:T(8,128)S(1)} %bitcast.20, s32[4,64]{1,0:T(4,128)S(1)} %copy-done.10, s32[4]{0:T(128)S(1)} %bitcast.22), custom_call_target="tpu_custom_call" | custom-call | tf_op jit(solution)/shard_map/encode/pallas_call | solution.py:295
  5.2 0.7 collective-permute-start
  5.9 0.7 collective-permute-start.1
  6.5 10.4 %collective-permute-start.2 = (bf16[80,512]{1,0:T(8,128)(2,1)S(1)}, bf16[80,512]{1,0:T(8,128)(2,1)S(1)}, u32[]{:S(2)}, u32[]{:S(2)}) collective-permute-start(bf16[80,512]{1,0:T(8,128)(2,1)S(1)} %get-tuple-element.10), channel_id=1, source_target_pairs={{0,12},{1,1},{2,0},{3,3},{4,22},{5,5},{6,24},{7,7},{8,8},{9,9},{10... | collective-permute-start | bytes 245768 | tf_op jit(solution)/shard_map/ppermute | solution.py:351
  16.9 0.7 collective-permute-start.3
  17.6 0.7 collective-permute-start.4
  18.3 0.7 collective-permute-start.5
  18.9 0.0 collective-permute-done.1.refs_1_
  19.0 0.7 collective-permute-start.6
  19.6 0.7 collective-permute-start.7
  20.4 0.0 copy-start.2
  20.4 1.2 %copy-done.2 = bf16[1,1024,512]{2,1,0:T(8,128)(2,1)S(1)} copy-done((bf16[1,1024,512]{2,1,0:T(8,128)(2,1)S(1)}, bf16[1,1024,512]{2,1,0:T(8,128)(2,1)}, u32[]{:S(2)}) %copy-start.2) | copy-done | bytes 1048600
  21.6 1.0 copy-done.4
  22.7 1.6 %collective-permute-start.11 = (bf16[512,512]{1,0:T(8,128)(2,1)S(1)}, bf16[512,512]{1,0:T(8,128)(2,1)}, u32[]{:S(2)}, u32[]{:S(2)}) collective-permute-start(bf16[512,512]{1,0:T(8,128)(2,1)S(1)} %layer.4), channel_id=1, source_target_pairs={{0,8},{1,1},{2,10},{3,3},{4,12},{5,5},{6,14},{7,7},{8,0},{9,9},{10... | collective-permute-start | bytes 1572872 | tf_op jit(solution)/shard_map/ppermute | solution.py:351
  24.3 0.7 collective-permute-start.10
  25.0 1.1 layer.5
  26.1 1.5 %collective-permute-start.12 = (bf16[512,512]{1,0:T(8,128)(2,1)S(1)}, bf16[512,512]{1,0:T(8,128)(2,1)}, u32[]{:S(2)}, u32[]{:S(2)}) collective-permute-start(bf16[512,512]{1,0:T(8,128)(2,1)S(1)} %layer.5), channel_id=1, source_target_pairs={{0,0},{1,1},{2,2},{3,3},{4,4},{5,5},{6,6},{7,7},{8,16},{9,9},{10,1... | collective-permute-start | bytes 1572872 | tf_op jit(solution)/shard_map/ppermute | solution.py:351
  27.6 0.7 collective-permute-start.9
  28.2 1.1 layer.6
  29.3 44.5 %collective-permute-start.13 = (bf16[512,512]{1,0:T(8,128)(2,1)S(1)}, bf16[512,512]{1,0:T(8,128)(2,1)}, u32[]{:S(2)}, u32[]{:S(2)}) collective-permute-start(bf16[512,512]{1,0:T(8,128)(2,1)S(1)} %layer.6), channel_id=1, source_target_pairs={{0,0},{1,1},{2,2},{3,3},{4,4},{5,5},{6,6},{7,7},{8,8},{9,9},{10,10... | collective-permute-start | bytes 1572872 | tf_op jit(solution)/shard_map/ppermute | solution.py:351
  73.8 1.9 %collective-permute-start.8 = (s32[8,512]{1,0:T(8,128)S(1)}, s32[8,512]{1,0:T(8,128)S(1)}, u32[]{:S(2)}, u32[]{:S(2)}) collective-permute-start(s32[8,512]{1,0:T(8,128)S(1)} %get-tuple-element.11.index), channel_id=1, source_target_pairs={{0,24},{1,1},{2,26},{3,3},{4,28},{5,5},{6,30},{7,7},{8,8},{9,9},{1... | collective-permute-start | bytes 49160 | tf_op jit(solution)/shard_map/ppermute | solution.py:351
  75.8 4.9 %collective-permute-done.8.index = s32[8,512]{1,0:T(8,128)S(1)} collective-permute-done((s32[8,512]{1,0:T(8,128)S(1)}, s32[8,512]{1,0:T(8,128)S(1)}, u32[]{:S(2)}, u32[]{:S(2)}) %collective-permute-start.8) | collective-permute-done | bytes 16416 | tf_op jit(solution)/shard_map/ppermute | solution.py:351
  80.7 0.4 collective-permute-done.13.state_in
  81.1 7.1 %layer.7 = bf16[512,512]{1,0:T(8,128)(2,1)S(1)} custom-call(s32[1]{0:T(128)} %bitcast.8.active, s32[8,512]{1,0:T(8,128)S(1)} %collective-permute-done.8.index, bf16[512,512]{1,0:T(8,128)(2,1)} %collective-permute-done.13.state_in, bf16[1,512,1024]{2,1,0:T(8,128)(2,1)S(1)} %copy-done.1, bf16[1,512,512]{2,1,0:T(8,128)(2,1)S(1)} %copy-done.5, ...), custom_call_target="tpu_custom_call" | custom-call | tf_op jit(solution)/shard_map/layer/pallas_call | solution.py:295
  88.2 0.0 copy-start.6
  88.3 2.1 %collective-permute-start.14 = (bf16[64,512]{1,0:T(8,128)(2,1)S(1)}, bf16[64,512]{1,0:T(8,128)(2,1)S(1)}, u32[]{:S(2)}, u32[]{:S(2)}) collective-permute-start(bf16[64,512]{1,0:T(8,128)(2,1)S(1)} %get-tuple-element.20), channel_id=1, source_target_pairs={{0,24},{1,1},{2,2},{3,3},{4,4},{5,5},{6,6},{7,7},{8,8},{9,9},{10,2... | collective-permute-start | bytes 196616 | tf_op jit(solution)/shard_map/ppermute | solution.py:351
  90.3 1.9 %collective-permute-start.15 = (bf16[64,512]{1,0:T(8,128)(2,1)S(1)}, bf16[64,512]{1,0:T(8,128)(2,1)S(1)}, u32[]{:S(2)}, u32[]{:S(2)}) collective-permute-start(bf16[64,512]{1,0:T(8,128)(2,1)S(1)} %get-tuple-element.19), channel_id=1, source_target_pairs={{0,0},{1,24},{2,2},{3,3},{4,4},{5,5},{6,6},{7,7},{8,8},{9,9},{10,1... | collective-permute-start | bytes 196616 | tf_op jit(solution)/shard_map/ppermute | solution.py:351
  92.3 1.9 %collective-permute-start.16 = (bf16[64,512]{1,0:T(8,128)(2,1)S(1)}, bf16[64,512]{1,0:T(8,128)(2,1)S(1)}, u32[]{:S(2)}, u32[]{:S(2)}) collective-permute-start(bf16[64,512]{1,0:T(8,128)(2,1)S(1)} %get-tuple-element.18), channel_id=1, source_target_pairs={{0,0},{1,1},{2,30},{3,3},{4,4},{5,5},{6,6},{7,7},{8,8},{9,9},{10,1... | collective-permute-start | bytes 196616 | tf_op jit(solution)/shard_map/ppermute | solution.py:351
  94.2 1.9 %collective-permute-start.17 = (bf16[64,512]{1,0:T(8,128)(2,1)S(1)}, bf16[64,512]{1,0:T(8,128)(2,1)S(1)}, u32[]{:S(2)}, u32[]{:S(2)}) collective-permute-start(bf16[64,512]{1,0:T(8,128)(2,1)S(1)} %get-tuple-element.17), channel_id=1, source_target_pairs={{0,0},{1,1},{2,2},{3,24},{4,4},{5,5},{6,6},{7,7},{8,8},{9,9},{10,1... | collective-permute-start | bytes 196616 | tf_op jit(solution)/shard_map/ppermute | solution.py:351
  96.1 1.9 %collective-permute-start.18 = (bf16[64,512]{1,0:T(8,128)(2,1)S(1)}, bf16[64,512]{1,0:T(8,128)(2,1)S(1)}, u32[]{:S(2)}, u32[]{:S(2)}) collective-permute-start(bf16[64,512]{1,0:T(8,128)(2,1)S(1)} %get-tuple-element.16), channel_id=1, source_target_pairs={{0,0},{1,1},{2,2},{3,3},{4,24},{5,5},{6,6},{7,7},{8,8},{9,9},{10,1... | collective-permute-start | bytes 196616 | tf_op jit(solution)/shard_map/ppermute | solution.py:351
  98.1 1.9 %collective-permute-start.19 = (bf16[64,512]{1,0:T(8,128)(2,1)S(1)}, bf16[64,512]{1,0:T(8,128)(2,1)S(1)}, u32[]{:S(2)}, u32[]{:S(2)}) collective-permute-start(bf16[64,512]{1,0:T(8,128)(2,1)S(1)} %get-tuple-element.15), channel_id=1, source_target_pairs={{0,0},{1,1},{2,2},{3,3},{4,4},{5,24},{6,6},{7,7},{8,8},{9,9},{10,1... | collective-permute-start | bytes 196616 | tf_op jit(solution)/shard_map/ppermute | solution.py:351
  100.0 1.9 %collective-permute-start.20 = (bf16[64,512]{1,0:T(8,128)(2,1)S(1)}, bf16[64,512]{1,0:T(8,128)(2,1)S(1)}, u32[]{:S(2)}, u32[]{:S(2)}) collective-permute-start(bf16[64,512]{1,0:T(8,128)(2,1)S(1)} %get-tuple-element.14), channel_id=1, source_target_pairs={{0,0},{1,1},{2,2},{3,3},{4,4},{5,5},{6,24},{7,7},{8,26},{9,9},{10,... | collective-permute-start | bytes 196616 | tf_op jit(solution)/shard_map/ppermute | solution.py:351
  101.9 1.9 %collective-permute-start.21 = (bf16[64,512]{1,0:T(8,128)(2,1)S(1)}, bf16[64,512]{1,0:T(8,128)(2,1)S(1)}, u32[]{:S(2)}, u32[]{:S(2)}) collective-permute-start(bf16[64,512]{1,0:T(8,128)(2,1)S(1)} %get-tuple-element.13), channel_id=1, source_target_pairs={{0,0},{1,1},{2,2},{3,3},{4,4},{5,5},{6,6},{7,24},{8,8},{9,26},{10,... | collective-permute-start | bytes 196616 | tf_op jit(solution)/shard_map/ppermute | solution.py:351
  103.9 0.0 copy-start.8
  103.9 0.2 prepare.1.ready
  104.1 0.8 collective-permute-done.18.refs_4_
  105.0 1.4 %collective-permute-done.19.refs_5_ = bf16[64,512]{1,0:T(8,128)(2,1)S(1)} collective-permute-done((bf16[64,512]{1,0:T(8,128)(2,1)S(1)}, bf16[64,512]{1,0:T(8,128)(2,1)S(1)}, u32[]{:S(2)}, u32[]{:S(2)}) %collective-permute-start.19) | collective-permute-done | bytes 65568 | tf_op jit(solution)/shard_map/ppermute | solution.py:351
  106.3 3.4 %collective-permute-done.20.refs_6_ = bf16[64,512]{1,0:T(8,128)(2,1)S(1)} collective-permute-done((bf16[64,512]{1,0:T(8,128)(2,1)S(1)}, bf16[64,512]{1,0:T(8,128)(2,1)S(1)}, u32[]{:S(2)}, u32[]{:S(2)}) %collective-permute-start.20) | collective-permute-done | bytes 65568 | tf_op jit(solution)/shard_map/ppermute | solution.py:351
  109.7 1.4 %collective-permute-done.21.refs_7_ = bf16[64,512]{1,0:T(8,128)(2,1)S(1)} collective-permute-done((bf16[64,512]{1,0:T(8,128)(2,1)S(1)}, bf16[64,512]{1,0:T(8,128)(2,1)S(1)}, u32[]{:S(2)}, u32[]{:S(2)}) %collective-permute-start.21) | collective-permute-done | bytes 65568 | tf_op jit(solution)/shard_map/ppermute | solution.py:351
  111.1 0.7 copy-done.13
  111.8 1.2 %decode.1 = bf16[227,128]{1,0:T(8,128)(2,1)} custom-call(s32[1]{0:T(128)} %bitcast.turn, f32[128,512]{1,0:T(8,128)S(1)} %prepare.1.ready, s32[1,128]{1,0:T(1,128)S(1)} %bitcast.23, bf16[1024,512]{1,0:T(8,128)(2,1)S(1)} %copy-done.6, bf16[227,512]{1,0:T(8,128)(2,1)S(1)} %bitcast.19, bf16[64,512]{1,0:T(8,128)(2,1)S(1)} %collective-permute-done.14.refs_0_, ...), custom_call_target="tpu_custom_call" | custom-call | tf_op jit(solution)/shard_map/decode/pallas_call | solution.py:295
  (35 shorter events, 0.2 us)
Async XLA Ops:
  0.0 0.9 copy-start
  0.0 1.1 copy-start.7
  0.0 20.4 %copy-start.1 = (bf16[1,512,1024]{2,1,0:T(8,128)(2,1)S(1)}, bf16[1,512,1024]{2,1,0:T(8,128)(2,1)}, u32[]{:S(2)}) copy-start(bf16[1,512,1024]{2,1,0:T(8,128)(2,1)} %refs_0_.7) | copy-start | bytes 3145732
  1.1 0.7 copy-start.9
  1.8 0.7 copy-start.10
  2.5 0.7 copy-start.11
  3.1 0.7 copy-start.12
  5.2 13.1 %collective-permute-start = (bf16[80,512]{1,0:T(8,128)(2,1)S(1)}, bf16[80,512]{1,0:T(8,128)(2,1)S(1)}, u32[]{:S(2)}, u32[]{:S(2)}) collective-permute-start(bf16[80,512]{1,0:T(8,128)(2,1)S(1)} %get-tuple-element.10), channel_id=1, source_target_pairs={{0,0},{1,1},{2,10},{3,3},{4,20},{5,5},{6,30},{7,7},{8,8},{9,9},{10... | collective-permute-start | bytes 245768 | tf_op jit(solution)/shard_map/ppermute | solution.py:351
  5.9 13.1 %collective-permute-start.1 = (bf16[80,512]{1,0:T(8,128)(2,1)S(1)}, bf16[80,512]{1,0:T(8,128)(2,1)S(1)}, u32[]{:S(2)}, u32[]{:S(2)}) collective-permute-start(bf16[80,512]{1,0:T(8,128)(2,1)S(1)} %get-tuple-element.10), channel_id=1, source_target_pairs={{0,1},{1,0},{2,11},{3,3},{4,21},{5,5},{6,31},{7,7},{8,8},{9,9},{10... | collective-permute-start | bytes 245768 | tf_op jit(solution)/shard_map/ppermute | solution.py:351
  6.5 13.1 %collective-permute-start.2 = (bf16[80,512]{1,0:T(8,128)(2,1)S(1)}, bf16[80,512]{1,0:T(8,128)(2,1)S(1)}, u32[]{:S(2)}, u32[]{:S(2)}) collective-permute-start(bf16[80,512]{1,0:T(8,128)(2,1)S(1)} %get-tuple-element.10), channel_id=1, source_target_pairs={{0,12},{1,1},{2,0},{3,3},{4,22},{5,5},{6,24},{7,7},{8,8},{9,9},{10... | collective-permute-start | bytes 245768 | tf_op jit(solution)/shard_map/ppermute | solution.py:351
  16.9 3.4 %collective-permute-start.3 = (bf16[80,512]{1,0:T(8,128)(2,1)S(1)}, bf16[80,512]{1,0:T(8,128)(2,1)S(1)}, u32[]{:S(2)}, u32[]{:S(2)}) collective-permute-start(bf16[80,512]{1,0:T(8,128)(2,1)S(1)} %get-tuple-element.10), channel_id=1, source_target_pairs={{0,3},{1,1},{2,13},{3,0},{4,23},{5,5},{6,25},{7,7},{8,8},{9,9},{10... | collective-permute-start | bytes 245768 | tf_op jit(solution)/shard_map/ppermute | solution.py:351
  17.6 2.8 %collective-permute-start.4 = (bf16[80,512]{1,0:T(8,128)(2,1)S(1)}, bf16[80,512]{1,0:T(8,128)(2,1)S(1)}, u32[]{:S(2)}, u32[]{:S(2)}) collective-permute-start(bf16[80,512]{1,0:T(8,128)(2,1)S(1)} %get-tuple-element.10), channel_id=1, source_target_pairs={{0,16},{1,1},{2,14},{3,3},{4,0},{5,5},{6,26},{7,7},{8,8},{9,9},{10... | collective-permute-start | bytes 245768 | tf_op jit(solution)/shard_map/ppermute | solution.py:351
  18.3 2.1 %collective-permute-start.5 = (bf16[80,512]{1,0:T(8,128)(2,1)S(1)}, bf16[80,512]{1,0:T(8,128)(2,1)S(1)}, u32[]{:S(2)}, u32[]{:S(2)}) collective-permute-start(bf16[80,512]{1,0:T(8,128)(2,1)S(1)} %get-tuple-element.10), channel_id=1, source_target_pairs={{0,5},{1,1},{2,15},{3,3},{4,17},{5,0},{6,27},{7,7},{8,8},{9,9},{10... | collective-permute-start | bytes 245768 | tf_op jit(solution)/shard_map/ppermute | solution.py:351
  19.0 1.4 %collective-permute-start.6 = (bf16[80,512]{1,0:T(8,128)(2,1)S(1)}, bf16[80,512]{1,0:T(8,128)(2,1)S(1)}, u32[]{:S(2)}, u32[]{:S(2)}) collective-permute-start(bf16[80,512]{1,0:T(8,128)(2,1)S(1)} %get-tuple-element.10), channel_id=1, source_target_pairs={{0,28},{1,1},{2,8},{3,3},{4,18},{5,5},{6,0},{7,7},{8,2},{9,9},{10,... | collective-permute-start | bytes 245768 | tf_op jit(solution)/shard_map/ppermute | solution.py:351
  19.6 0.7 collective-permute-start.7
  20.4 1.2 %copy-start.2 = (bf16[1,1024,512]{2,1,0:T(8,128)(2,1)S(1)}, bf16[1,1024,512]{2,1,0:T(8,128)(2,1)}, u32[]{:S(2)}) copy-start(bf16[1,1024,512]{2,1,0:T(8,128)(2,1)} %refs_2_.7) | copy-start | bytes 3145732
  21.6 1.0 copy-start.4
  22.7 2.3 %copy-start.3 = (bf16[1,1024,512]{2,1,0:T(8,128)(2,1)S(1)}, bf16[1,1024,512]{2,1,0:T(8,128)(2,1)}, u32[]{:S(2)}) copy-start(bf16[1,1024,512]{2,1,0:T(8,128)(2,1)} %refs_2_.7) | copy-start | bytes 3145732
  22.7 2.3 %copy-start.5 = (bf16[1,512,512]{2,1,0:T(8,128)(2,1)S(1)}, bf16[1,512,512]{2,1,0:T(8,128)(2,1)}, u32[]{:S(2)}) copy-start(bf16[1,512,512]{2,1,0:T(8,128)(2,1)} %refs_1_.9) | copy-start | bytes 1572868
  22.7 2.3 %collective-permute-start.11 = (bf16[512,512]{1,0:T(8,128)(2,1)S(1)}, bf16[512,512]{1,0:T(8,128)(2,1)}, u32[]{:S(2)}, u32[]{:S(2)}) collective-permute-start(bf16[512,512]{1,0:T(8,128)(2,1)S(1)} %layer.4), channel_id=1, source_target_pairs={{0,8},{1,1},{2,10},{3,3},{4,12},{5,5},{6,14},{7,7},{8,0},{9,9},{10... | collective-permute-start | bytes 1572872 | tf_op jit(solution)/shard_map/ppermute | solution.py:351
  24.3 0.7 collective-permute-start.10
  26.1 2.1 %collective-permute-start.12 = (bf16[512,512]{1,0:T(8,128)(2,1)S(1)}, bf16[512,512]{1,0:T(8,128)(2,1)}, u32[]{:S(2)}, u32[]{:S(2)}) collective-permute-start(bf16[512,512]{1,0:T(8,128)(2,1)S(1)} %layer.5), channel_id=1, source_target_pairs={{0,0},{1,1},{2,2},{3,3},{4,4},{5,5},{6,6},{7,7},{8,16},{9,9},{10,1... | collective-permute-start | bytes 1572872 | tf_op jit(solution)/shard_map/ppermute | solution.py:351
  27.6 0.7 collective-permute-start.9
  29.3 51.8 %collective-permute-start.13 = (bf16[512,512]{1,0:T(8,128)(2,1)S(1)}, bf16[512,512]{1,0:T(8,128)(2,1)}, u32[]{:S(2)}, u32[]{:S(2)}) collective-permute-start(bf16[512,512]{1,0:T(8,128)(2,1)S(1)} %layer.6), channel_id=1, source_target_pairs={{0,0},{1,1},{2,2},{3,3},{4,4},{5,5},{6,6},{7,7},{8,8},{9,9},{10,10... | collective-permute-start | bytes 1572872 | tf_op jit(solution)/shard_map/ppermute | solution.py:351
  73.8 6.9 %collective-permute-start.8 = (s32[8,512]{1,0:T(8,128)S(1)}, s32[8,512]{1,0:T(8,128)S(1)}, u32[]{:S(2)}, u32[]{:S(2)}) collective-permute-start(s32[8,512]{1,0:T(8,128)S(1)} %get-tuple-element.11.index), channel_id=1, source_target_pairs={{0,24},{1,1},{2,26},{3,3},{4,28},{5,5},{6,30},{7,7},{8,8},{9,9},{1... | collective-permute-start | bytes 49160 | tf_op jit(solution)/shard_map/ppermute | solution.py:351
  88.2 15.7 %copy-start.6 = (bf16[1024,512]{1,0:T(8,128)(2,1)S(1)}, bf16[1024,512]{1,0:T(8,128)(2,1)}, u32[]{:S(2)}) copy-start(bf16[1024,512]{1,0:T(8,128)(2,1)} %w_decode.3) | copy-start | bytes 3145732
  88.3 9.8 %collective-permute-start.14 = (bf16[64,512]{1,0:T(8,128)(2,1)S(1)}, bf16[64,512]{1,0:T(8,128)(2,1)S(1)}, u32[]{:S(2)}, u32[]{:S(2)}) collective-permute-start(bf16[64,512]{1,0:T(8,128)(2,1)S(1)} %get-tuple-element.20), channel_id=1, source_target_pairs={{0,24},{1,1},{2,2},{3,3},{4,4},{5,5},{6,6},{7,7},{8,8},{9,9},{10,2... | collective-permute-start | bytes 196616 | tf_op jit(solution)/shard_map/ppermute | solution.py:351
  90.3 9.7 %collective-permute-start.15 = (bf16[64,512]{1,0:T(8,128)(2,1)S(1)}, bf16[64,512]{1,0:T(8,128)(2,1)S(1)}, u32[]{:S(2)}, u32[]{:S(2)}) collective-permute-start(bf16[64,512]{1,0:T(8,128)(2,1)S(1)} %get-tuple-element.19), channel_id=1, source_target_pairs={{0,0},{1,24},{2,2},{3,3},{4,4},{5,5},{6,6},{7,7},{8,8},{9,9},{10,1... | collective-permute-start | bytes 196616 | tf_op jit(solution)/shard_map/ppermute | solution.py:351
  92.3 9.7 %collective-permute-start.16 = (bf16[64,512]{1,0:T(8,128)(2,1)S(1)}, bf16[64,512]{1,0:T(8,128)(2,1)S(1)}, u32[]{:S(2)}, u32[]{:S(2)}) collective-permute-start(bf16[64,512]{1,0:T(8,128)(2,1)S(1)} %get-tuple-element.18), channel_id=1, source_target_pairs={{0,0},{1,1},{2,30},{3,3},{4,4},{5,5},{6,6},{7,7},{8,8},{9,9},{10,1... | collective-permute-start | bytes 196616 | tf_op jit(solution)/shard_map/ppermute | solution.py:351
  94.2 10.0 %collective-permute-start.17 = (bf16[64,512]{1,0:T(8,128)(2,1)S(1)}, bf16[64,512]{1,0:T(8,128)(2,1)S(1)}, u32[]{:S(2)}, u32[]{:S(2)}) collective-permute-start(bf16[64,512]{1,0:T(8,128)(2,1)S(1)} %get-tuple-element.17), channel_id=1, source_target_pairs={{0,0},{1,1},{2,2},{3,24},{4,4},{5,5},{6,6},{7,7},{8,8},{9,9},{10,1... | collective-permute-start | bytes 196616 | tf_op jit(solution)/shard_map/ppermute | solution.py:351
  96.1 8.9 %collective-permute-start.18 = (bf16[64,512]{1,0:T(8,128)(2,1)S(1)}, bf16[64,512]{1,0:T(8,128)(2,1)S(1)}, u32[]{:S(2)}, u32[]{:S(2)}) collective-permute-start(bf16[64,512]{1,0:T(8,128)(2,1)S(1)} %get-tuple-element.16), channel_id=1, source_target_pairs={{0,0},{1,1},{2,2},{3,3},{4,24},{5,5},{6,6},{7,7},{8,8},{9,9},{10,1... | collective-permute-start | bytes 196616 | tf_op jit(solution)/shard_map/ppermute | solution.py:351
  98.1 8.3 %collective-permute-start.19 = (bf16[64,512]{1,0:T(8,128)(2,1)S(1)}, bf16[64,512]{1,0:T(8,128)(2,1)S(1)}, u32[]{:S(2)}, u32[]{:S(2)}) collective-permute-start(bf16[64,512]{1,0:T(8,128)(2,1)S(1)} %get-tuple-element.15), channel_id=1, source_target_pairs={{0,0},{1,1},{2,2},{3,3},{4,4},{5,24},{6,6},{7,7},{8,8},{9,9},{10,1... | collective-permute-start | bytes 196616 | tf_op jit(solution)/shard_map/ppermute | solution.py:351
  100.0 9.8 %collective-permute-start.20 = (bf16[64,512]{1,0:T(8,128)(2,1)S(1)}, bf16[64,512]{1,0:T(8,128)(2,1)S(1)}, u32[]{:S(2)}, u32[]{:S(2)}) collective-permute-start(bf16[64,512]{1,0:T(8,128)(2,1)S(1)} %get-tuple-element.14), channel_id=1, source_target_pairs={{0,0},{1,1},{2,2},{3,3},{4,4},{5,5},{6,24},{7,7},{8,26},{9,9},{10,... | collective-permute-start | bytes 196616 | tf_op jit(solution)/shard_map/ppermute | solution.py:351
  101.9 9.2 %collective-permute-start.21 = (bf16[64,512]{1,0:T(8,128)(2,1)S(1)}, bf16[64,512]{1,0:T(8,128)(2,1)S(1)}, u32[]{:S(2)}, u32[]{:S(2)}) collective-permute-start(bf16[64,512]{1,0:T(8,128)(2,1)S(1)} %get-tuple-element.13), channel_id=1, source_target_pairs={{0,0},{1,1},{2,2},{3,3},{4,4},{5,5},{6,6},{7,24},{8,8},{9,26},{10,... | collective-permute-start | bytes 196616 | tf_op jit(solution)/shard_map/ppermute | solution.py:351
  103.9 7.2 %copy-start.8 = (bf16[512,227]{0,1:T(8,128)(2,1)S(1)}, bf16[512,227]{0,1:T(8,128)(2,1)}, u32[]{:S(2)}) copy-start(bf16[512,227]{0,1:T(8,128)(2,1)} %param.18) | copy-start | bytes 697348
  111.1 0.7 copy-start.13

commit v3 on v2

--- a/solution.py
+++ b/solution.py
@@ -10,7 +10,7 @@
 epsilon = 1e-05
 VMEM = pl.BlockSpec(memory_space=pltpu.VMEM)
 SMEM = pl.BlockSpec(memory_space=pltpu.SMEM)
-ANY = pl.BlockSpec(memory_space=pl.ANY)
+HBM = pl.BlockSpec(memory_space=pltpu.HBM)
 
 
 def from_behind(value, axis, steps):
@@ -232,24 +232,20 @@
             index_out[:, part * mesh_rows : (part + 1) * mesh_rows] = found[:, :mesh_rows]
 
 
-def layer_kernel(active, index, state_in, *refs):
-    inputs, state_out, held, semaphores = refs[:3], refs[3], refs[4:7], refs[7]
+def layer_kernel(active, index, state_in, w_project, w_message, w_update, state_out):
     nodes, width = state_in.shape
     fanout = index.shape[0]
     chunk = min(256, nodes)
 
     @pl.when(active[0] == 1)
     def _():
-        copies = fetch([ref.at[0] for ref in inputs], held, semaphores)
-        w_project, w_message, w_update = held
         columns = jnp.concatenate([index[...], jnp.zeros((128 - fanout, nodes), jnp.int32)], axis=0)
         columns = jnp.transpose(columns.astype(jnp.float32))
         names = lax.broadcasted_iota(jnp.int32, (chunk, nodes), 1).astype(jnp.float32)
-        copies[0].wait()
-        sender = matmul(state_in[...], w_project[:, width:]).astype(jnp.bfloat16)
+        sender = matmul(state_in[...], w_project[0, :, width:]).astype(jnp.bfloat16)
         for start in range(0, nodes, chunk):
             own = state_in[start : start + chunk, :]
-            receiver = matmul(own, w_project[:, :width])
+            receiver = matmul(own, w_project[0, :, :width])
             total = jnp.zeros((chunk, width), jnp.float32)
             for k in range(fanout):
                 hit = columns[start : start + chunk, k : k + 1] == names
@@ -257,12 +253,9 @@
                 edge = silu_by_tanh(receiver + fetched).astype(jnp.bfloat16)
                 total = total + edge.astype(jnp.float32)
             gathered = (total * (1.0 / fanout)).astype(jnp.bfloat16)
-            if start == 0:
-                copies[1].wait()
-                copies[2].wait()
-            aggregate = matmul(gathered, w_message[...]).astype(jnp.bfloat16)
+            aggregate = matmul(gathered, w_message[0]).astype(jnp.bfloat16)
             update = silu_by_tanh(
-                matmul(own, w_update[:width, :]) + matmul(aggregate, w_update[width:, :])
+                matmul(own, w_update[0, :width, :]) + matmul(aggregate, w_update[0, width:, :])
             )
             renewed = own.astype(jnp.float32) + rms_scale(update)
             state_out[start : start + chunk, :] = renewed.astype(jnp.bfloat16)
@@ -290,8 +283,8 @@
     out[...] = matmul_nt(w_output[...], hidden).astype(jnp.bfloat16)
 
 
-def call(kernel, name, shapes, inputs, places, scratch=(), flops=0, moved=0):
-    kinds = {"s": SMEM, "v": VMEM, "a": ANY}
+def call(kernel, name, shapes, inputs, places, scratch=(), room=16):
+    kinds = {"s": SMEM, "v": VMEM, "h": HBM}
     return pl.pallas_call(
         kernel,
         out_shape=shapes,
@@ -299,8 +292,7 @@
         out_specs=[VMEM] * len(shapes),
         scratch_shapes=list(scratch),
         name=name,
-        compiler_params=pltpu.CompilerParams(vmem_limit_bytes=32 * 1024 * 1024),
-        cost_estimate=pl.CostEstimate(flops=flops, bytes_accessed=moved, transcendentals=0),
+        compiler_params=pltpu.CompilerParams(vmem_limit_bytes=room * 1024 * 1024),
     )(*inputs)
 
 
@@ -314,8 +306,9 @@
         while last in onward:
             last = onward[last]
         onward[last] = first
-    for other in range(count):
-        onward.setdefault(other, other)
+    rest = [other for other in range(count) if other not in onward]
+    for place, other in enumerate(rest):
+        onward[other] = rest[place ^ 1] if place | 1 < len(rest) else other
     return sorted(onward.items())
 
 
@@ -370,9 +363,10 @@
             jax.ShapeDtypeStruct((grid_rows, width), bf16),
         ],
         inputs,
-        "aaaaaa",
+        "hhhhhh",
         [pltpu.VMEM(value.shape, value.dtype) for value in inputs[:-1]]
         + [pltpu.SMEM(inputs[-1].shape, jnp.int32), pltpu.SemaphoreType.DMA((6,))],
+        room=60,
     )
     payloads = []
     for turn in range(parts):
@@ -396,8 +390,7 @@
             "layer",
             [jax.ShapeDtypeStruct((nodes, width), bf16)],
             [active(at_segment), indices[at_segment], state] + weights,
-            "svvaaa",
-            [pltpu.VMEM(weight.shape[1:], bf16) for weight in weights] + [pltpu.SemaphoreType.DMA((3,))],
+            "svvvvv",
         )
         if at_segment + 1 < segments:
             pairs = [

time: 114 us -> 109 us (0.956)
  the two profiles are of different devices: /device:TPU:6 before, /device:TPU:7 now
where the time goes in v3:
time: 109 us
  starting transfers between devices  77.6 us (71%)
  waiting for transfers between devices  19.3 us (18%)
  Pallas kernels  6.75 us (6%)
  local copies, waits for them, and re-layouts  4.67 us (4%)
    ppermute x22, starting transfers between devices, send(): lax.ppermute(value, ('segment', 'dom'), every_device(pairs, segments * pa...  77.6 us
    ppermute x22, waiting for transfers between devices, send(): lax.ppermute(value, ('segment', 'dom'), every_device(pairs, segments * pa...  19.3 us
    pallas_call x8, Pallas kernels, call(): pl.pallas_call(kernel, out_shape=shapes, in_specs=[kinds[place] for place...  6.75 us
    unnamed x21, local copies, waits for them, and re-layouts  4.51 us
  transfers between devices with their start and end apart: 22, of which 10 were waited for; matrix products, arithmetic and copies ran while one was open for 0% of the time, Pallas kernels for 0%

profile of v3, /device:TPU:7, one launch (start us, length us, event | category | flops | bytes accessed | tf_op | source)
XLA Modules:
  0.0 108.6 jit_solution(12502066621740690758)
XLA Ops:
  0.0 0.9 copy-done
  0.9 0.1 constant_dynamic-slice_fusion
  1.1 0.6 copy.16
  1.7 2.1 %encode.1 = (bf16[80,512]{1,0:T(8,128)(2,1)}, bf16[128,512]{1,0:T(8,128)(2,1)}) custom-call(bf16[227,128]{1,0:T(8,128)(2,1)} %bitcast.20, bf16[227,512]{1,0:T(8,128)(2,1)} %refs_1_.1, s32[1,128]{1,0:T(1,128)} %bitcast.22, s32[8,64]{1,0:T(8,128)} %bitcast.21, s32[4,64]{1,0:T(4,128)} %refs_4_.1, s32[4]{0:T(128)} %bitcast.23), custom_call_target="tpu_custom_call" | custom-call | tf_op jit(solution)/shard_map/encode/pallas_call | solution.py:288
  3.8 2.6 %collective-permute-start = (bf16[80,512]{1,0:T(8,128)(2,1)}, bf16[80,512]{1,0:T(8,128)(2,1)S(1)}, u32[]{:S(2)}, u32[]{:S(2)}) collective-permute-start(bf16[80,512]{1,0:T(8,128)(2,1)} %get-tuple-element.10), channel_id=1, source_target_pairs={{0,0},{1,3},{2,10},{3,1},{4,20},{5,7},{6,30},{7,5},{8,9},{9,8},{10... | collective-permute-start | bytes 245768 | tf_op jit(solution)/shard_map/ppermute | solution.py:344
  6.4 1.3 %collective-permute-start.1 = (bf16[80,512]{1,0:T(8,128)(2,1)}, bf16[80,512]{1,0:T(8,128)(2,1)S(1)}, u32[]{:S(2)}, u32[]{:S(2)}) collective-permute-start(bf16[80,512]{1,0:T(8,128)(2,1)} %get-tuple-element.10), channel_id=1, source_target_pairs={{0,1},{1,0},{2,11},{3,5},{4,21},{5,3},{6,31},{7,8},{8,7},{9,10},{1... | collective-permute-start | bytes 245768 | tf_op jit(solution)/shard_map/ppermute | solution.py:344
  7.7 2.4 %collective-permute-start.2 = (bf16[80,512]{1,0:T(8,128)(2,1)}, bf16[80,512]{1,0:T(8,128)(2,1)S(1)}, u32[]{:S(2)}, u32[]{:S(2)}) collective-permute-start(bf16[80,512]{1,0:T(8,128)(2,1)} %get-tuple-element.10), channel_id=1, source_target_pairs={{0,12},{1,3},{2,0},{3,1},{4,22},{5,7},{6,24},{7,5},{8,9},{9,8},{10... | collective-permute-start | bytes 245768 | tf_op jit(solution)/shard_map/ppermute | solution.py:344
  10.1 7.2 %collective-permute-start.3 = (bf16[80,512]{1,0:T(8,128)(2,1)}, bf16[80,512]{1,0:T(8,128)(2,1)S(1)}, u32[]{:S(2)}, u32[]{:S(2)}) collective-permute-start(bf16[80,512]{1,0:T(8,128)(2,1)} %get-tuple-element.10), channel_id=1, source_target_pairs={{0,3},{1,5},{2,13},{3,0},{4,23},{5,1},{6,25},{7,8},{8,7},{9,10},{1... | collective-permute-start | bytes 245768 | tf_op jit(solution)/shard_map/ppermute | solution.py:344
  17.4 1.9 %collective-permute-start.4 = (bf16[80,512]{1,0:T(8,128)(2,1)}, bf16[80,512]{1,0:T(8,128)(2,1)S(1)}, u32[]{:S(2)}, u32[]{:S(2)}) collective-permute-start(bf16[80,512]{1,0:T(8,128)(2,1)} %get-tuple-element.10), channel_id=1, source_target_pairs={{0,16},{1,3},{2,14},{3,1},{4,0},{5,7},{6,26},{7,5},{8,9},{9,8},{10... | collective-permute-start | bytes 245768 | tf_op jit(solution)/shard_map/ppermute | solution.py:344
  19.3 0.6 collective-permute-start.5
  19.9 0.0 collective-permute-done.1.refs_1_
  19.9 3.2 %collective-permute-start.6 = (bf16[80,512]{1,0:T(8,128)(2,1)}, bf16[80,512]{1,0:T(8,128)(2,1)S(1)}, u32[]{:S(2)}, u32[]{:S(2)}) collective-permute-start(bf16[80,512]{1,0:T(8,128)(2,1)} %get-tuple-element.10), channel_id=1, source_target_pairs={{0,28},{1,3},{2,8},{3,1},{4,18},{5,7},{6,0},{7,5},{8,2},{9,10},{10... | collective-permute-start | bytes 245768 | tf_op jit(solution)/shard_map/ppermute | solution.py:344
  23.2 0.0 collective-permute-done.2.refs_2_
  23.2 0.1 collective-permute-start.7
  23.3 0.1 collective-permute-done.5.refs_5_
  23.4 0.8 collective-permute-done.6.refs_6_
  24.3 3.0 %collective-permute-done.7.refs_7_ = bf16[80,512]{1,0:T(8,128)(2,1)S(1)} collective-permute-done((bf16[80,512]{1,0:T(8,128)(2,1)}, bf16[80,512]{1,0:T(8,128)(2,1)S(1)}, u32[]{:S(2)}, u32[]{:S(2)}) %collective-permute-start.7) | collective-permute-done | bytes 81952 | tf_op jit(solution)/shard_map/ppermute | solution.py:344
  27.3 1.2 %copy-done.2 = bf16[1,1024,512]{2,1,0:T(8,128)(2,1)S(1)} copy-done((bf16[1,1024,512]{2,1,0:T(8,128)(2,1)S(1)}, bf16[1,1024,512]{2,1,0:T(8,128)(2,1)}, u32[]{:S(2)}) %copy-start.2) | copy-done | bytes 1048600
  28.6 1.0 copy-done.4
  29.6 2.9 %collective-permute-start.11 = (bf16[512,512]{1,0:T(8,128)(2,1)S(1)}, bf16[512,512]{1,0:T(8,128)(2,1)}, u32[]{:S(2)}, u32[]{:S(2)}) collective-permute-start(bf16[512,512]{1,0:T(8,128)(2,1)S(1)} %layer.4), channel_id=1, source_target_pairs={{0,8},{1,3},{2,10},{3,1},{4,12},{5,7},{6,14},{7,5},{8,0},{9,11},{1... | collective-permute-start | bytes 1572872 | tf_op jit(solution)/shard_map/ppermute | solution.py:344
  32.5 0.1 collective-permute-start.10
  32.6 1.5 %collective-permute-done.10.index = s32[8,512]{1,0:T(8,128)S(1)} collective-permute-done((s32[8,512]{1,0:T(8,128)S(1)}, s32[8,512]{1,0:T(8,128)S(1)}, u32[]{:S(2)}, u32[]{:S(2)}) %collective-permute-start.10) | collective-permute-done | bytes 16416 | tf_op jit(solution)/shard_map/ppermute | solution.py:344
  34.1 0.1 collective-permute-done.11.state_in
  34.2 1.0 layer.5
  35.3 0.4 collective-permute-start.12
  35.7 0.1 collective-permute-start.9
  35.8 1.4 %collective-permute-done.9.index = s32[8,512]{1,0:T(8,128)S(1)} collective-permute-done((s32[8,512]{1,0:T(8,128)S(1)}, s32[8,512]{1,0:T(8,128)S(1)}, u32[]{:S(2)}, u32[]{:S(2)}) %collective-permute-start.9) | collective-permute-done | bytes 16416 | tf_op jit(solution)/shard_map/ppermute | solution.py:344
  37.2 0.1 collective-permute-done.12.state_in
  37.3 1.0 layer.6
  38.4 1.5 %collective-permute-start.8 = (s32[8,512]{1,0:T(8,128)S(1)}, s32[8,512]{1,0:T(8,128)S(1)}, u32[]{:S(2)}, u32[]{:S(2)}) collective-permute-start(s32[8,512]{1,0:T(8,128)S(1)} %get-tuple-element.11.index), channel_id=1, source_target_pairs={{0,24},{1,3},{2,26},{3,1},{4,28},{5,7},{6,30},{7,5},{8,9},{9,8},{1... | collective-permute-start | bytes 49160 | tf_op jit(solution)/shard_map/ppermute | solution.py:344
  39.8 6.7 %collective-permute-done.8.index = s32[8,512]{1,0:T(8,128)S(1)} collective-permute-done((s32[8,512]{1,0:T(8,128)S(1)}, s32[8,512]{1,0:T(8,128)S(1)}, u32[]{:S(2)}, u32[]{:S(2)}) %collective-permute-start.8) | collective-permute-done | bytes 16416 | tf_op jit(solution)/shard_map/ppermute | solution.py:344
  46.6 0.0 collective-permute-done.13.state_in
  46.6 1.1 layer.7
  47.7 24.2 %collective-permute-start.14 = (bf16[64,512]{1,0:T(8,128)(2,1)S(1)}, bf16[64,512]{1,0:T(8,128)(2,1)S(1)}, u32[]{:S(2)}, u32[]{:S(2)}) collective-permute-start(bf16[64,512]{1,0:T(8,128)(2,1)S(1)} %get-tuple-element.20), channel_id=1, source_target_pairs={{0,24},{1,2},{2,1},{3,4},{4,3},{5,6},{6,5},{7,8},{8,7},{9,11},{10,... | collective-permute-start | bytes 196616 | tf_op jit(solution)/shard_map/ppermute | solution.py:344
  71.9 0.1 collective-permute-start.15
  72.0 6.0 %collective-permute-start.16 = (bf16[64,512]{1,0:T(8,128)(2,1)S(1)}, bf16[64,512]{1,0:T(8,128)(2,1)S(1)}, u32[]{:S(2)}, u32[]{:S(2)}) collective-permute-start(bf16[64,512]{1,0:T(8,128)(2,1)S(1)} %get-tuple-element.18), channel_id=1, source_target_pairs={{0,1},{1,0},{2,30},{3,4},{4,3},{5,6},{6,5},{7,8},{8,7},{9,10},{10,... | collective-permute-start | bytes 196616 | tf_op jit(solution)/shard_map/ppermute | solution.py:344
  78.0 10.7 %collective-permute-start.17 = (bf16[64,512]{1,0:T(8,128)(2,1)S(1)}, bf16[64,512]{1,0:T(8,128)(2,1)S(1)}, u32[]{:S(2)}, u32[]{:S(2)}) collective-permute-start(bf16[64,512]{1,0:T(8,128)(2,1)S(1)} %get-tuple-element.17), channel_id=1, source_target_pairs={{0,1},{1,0},{2,4},{3,24},{4,2},{5,6},{6,5},{7,8},{8,7},{9,10},{10,... | collective-permute-start | bytes 196616 | tf_op jit(solution)/shard_map/ppermute | solution.py:344
  88.7 5.6 %collective-permute-start.18 = (bf16[64,512]{1,0:T(8,128)(2,1)S(1)}, bf16[64,512]{1,0:T(8,128)(2,1)S(1)}, u32[]{:S(2)}, u32[]{:S(2)}) collective-permute-start(bf16[64,512]{1,0:T(8,128)(2,1)S(1)} %get-tuple-element.16), channel_id=1, source_target_pairs={{0,1},{1,0},{2,3},{3,2},{4,24},{5,6},{6,5},{7,8},{8,7},{9,10},{10,... | collective-permute-start | bytes 196616 | tf_op jit(solution)/shard_map/ppermute | solution.py:344
  94.3 0.5 collective-permute-start.19
  94.9 0.0 collective-permute-done.15.refs_1_
  94.9 5.6 %collective-permute-start.20 = (bf16[64,512]{1,0:T(8,128)(2,1)S(1)}, bf16[64,512]{1,0:T(8,128)(2,1)S(1)}, u32[]{:S(2)}, u32[]{:S(2)}) collective-permute-start(bf16[64,512]{1,0:T(8,128)(2,1)S(1)} %get-tuple-element.14), channel_id=1, source_target_pairs={{0,1},{1,0},{2,3},{3,2},{4,5},{5,4},{6,24},{7,9},{8,26},{9,7},{10,... | collective-permute-start | bytes 196616 | tf_op jit(solution)/shard_map/ppermute | solution.py:344
  100.5 0.0 collective-permute-done.16.refs_2_
  100.5 0.5 collective-permute-start.21
  101.0 0.2 prepare.1.ready
  101.3 1.6 %collective-permute-done.20.refs_6_ = bf16[64,512]{1,0:T(8,128)(2,1)S(1)} collective-permute-done((bf16[64,512]{1,0:T(8,128)(2,1)S(1)}, bf16[64,512]{1,0:T(8,128)(2,1)S(1)}, u32[]{:S(2)}, u32[]{:S(2)}) %collective-permute-start.20) | collective-permute-done | bytes 65568 | tf_op jit(solution)/shard_map/ppermute | solution.py:344
  102.8 3.8 %collective-permute-done.21.refs_7_ = bf16[64,512]{1,0:T(8,128)(2,1)S(1)} collective-permute-done((bf16[64,512]{1,0:T(8,128)(2,1)S(1)}, bf16[64,512]{1,0:T(8,128)(2,1)S(1)}, u32[]{:S(2)}, u32[]{:S(2)}) %collective-permute-start.21) | collective-permute-done | bytes 65568 | tf_op jit(solution)/shard_map/ppermute | solution.py:344
  106.7 0.7 copy-done.9
  107.3 1.2 %decode.1 = bf16[227,128]{1,0:T(8,128)(2,1)} custom-call(s32[1]{0:T(128)} %bitcast.turn, f32[128,512]{1,0:T(8,128)S(1)} %prepare.1.ready, s32[1,128]{1,0:T(1,128)S(1)} %bitcast.19, bf16[1024,512]{1,0:T(8,128)(2,1)S(1)} %copy-done.6, bf16[227,512]{1,0:T(8,128)(2,1)S(1)} %bitcast.18, bf16[64,512]{1,0:T(8,128)(2,1)S(1)} %collective-permute-done.14.refs_0_, ...), custom_call_target="tpu_custom_call" | custom-call | tf_op jit(solution)/shard_map/decode/pallas_call | solution.py:288
  (27 shorter events, 0.1 us)
Async XLA Ops:
  0.0 0.9 copy-start
  0.0 27.3 %copy-start.1 = (bf16[1,512,1024]{2,1,0:T(8,128)(2,1)S(1)}, bf16[1,512,1024]{2,1,0:T(8,128)(2,1)}, u32[]{:S(2)}) copy-start(bf16[1,512,1024]{2,1,0:T(8,128)(2,1)} %w_project.7) | copy-start | bytes 3145732
  3.8 15.5 %collective-permute-start = (bf16[80,512]{1,0:T(8,128)(2,1)}, bf16[80,512]{1,0:T(8,128)(2,1)S(1)}, u32[]{:S(2)}, u32[]{:S(2)}) collective-permute-start(bf16[80,512]{1,0:T(8,128)(2,1)} %get-tuple-element.10), channel_id=1, source_target_pairs={{0,0},{1,3},{2,10},{3,1},{4,20},{5,7},{6,30},{7,5},{8,9},{9,8},{10... | collective-permute-start | bytes 245768 | tf_op jit(solution)/shard_map/ppermute | solution.py:344
  6.4 13.5 %collective-permute-start.1 = (bf16[80,512]{1,0:T(8,128)(2,1)}, bf16[80,512]{1,0:T(8,128)(2,1)S(1)}, u32[]{:S(2)}, u32[]{:S(2)}) collective-permute-start(bf16[80,512]{1,0:T(8,128)(2,1)} %get-tuple-element.10), channel_id=1, source_target_pairs={{0,1},{1,0},{2,11},{3,5},{4,21},{5,3},{6,31},{7,8},{8,7},{9,10},{1... | collective-permute-start | bytes 245768 | tf_op jit(solution)/shard_map/ppermute | solution.py:344
  7.7 15.5 %collective-permute-start.2 = (bf16[80,512]{1,0:T(8,128)(2,1)}, bf16[80,512]{1,0:T(8,128)(2,1)S(1)}, u32[]{:S(2)}, u32[]{:S(2)}) collective-permute-start(bf16[80,512]{1,0:T(8,128)(2,1)} %get-tuple-element.10), channel_id=1, source_target_pairs={{0,12},{1,3},{2,0},{3,1},{4,22},{5,7},{6,24},{7,5},{8,9},{9,8},{10... | collective-permute-start | bytes 245768 | tf_op jit(solution)/shard_map/ppermute | solution.py:344
  10.1 13.1 %collective-permute-start.3 = (bf16[80,512]{1,0:T(8,128)(2,1)}, bf16[80,512]{1,0:T(8,128)(2,1)S(1)}, u32[]{:S(2)}, u32[]{:S(2)}) collective-permute-start(bf16[80,512]{1,0:T(8,128)(2,1)} %get-tuple-element.10), channel_id=1, source_target_pairs={{0,3},{1,5},{2,13},{3,0},{4,23},{5,1},{6,25},{7,8},{8,7},{9,10},{1... | collective-permute-start | bytes 245768 | tf_op jit(solution)/shard_map/ppermute | solution.py:344
  17.4 5.9 %collective-permute-start.4 = (bf16[80,512]{1,0:T(8,128)(2,1)}, bf16[80,512]{1,0:T(8,128)(2,1)S(1)}, u32[]{:S(2)}, u32[]{:S(2)}) collective-permute-start(bf16[80,512]{1,0:T(8,128)(2,1)} %get-tuple-element.10), channel_id=1, source_target_pairs={{0,16},{1,3},{2,14},{3,1},{4,0},{5,7},{6,26},{7,5},{8,9},{9,8},{10... | collective-permute-start | bytes 245768 | tf_op jit(solution)/shard_map/ppermute | solution.py:344
  19.3 4.1 %collective-permute-start.5 = (bf16[80,512]{1,0:T(8,128)(2,1)}, bf16[80,512]{1,0:T(8,128)(2,1)S(1)}, u32[]{:S(2)}, u32[]{:S(2)}) collective-permute-start(bf16[80,512]{1,0:T(8,128)(2,1)} %get-tuple-element.10), channel_id=1, source_target_pairs={{0,5},{1,3},{2,15},{3,1},{4,17},{5,0},{6,27},{7,8},{8,7},{9,10},{1... | collective-permute-start | bytes 245768 | tf_op jit(solution)/shard_map/ppermute | solution.py:344
  19.9 4.3 %collective-permute-start.6 = (bf16[80,512]{1,0:T(8,128)(2,1)}, bf16[80,512]{1,0:T(8,128)(2,1)S(1)}, u32[]{:S(2)}, u32[]{:S(2)}) collective-permute-start(bf16[80,512]{1,0:T(8,128)(2,1)} %get-tuple-element.10), channel_id=1, source_target_pairs={{0,28},{1,3},{2,8},{3,1},{4,18},{5,7},{6,0},{7,5},{8,2},{9,10},{10... | collective-permute-start | bytes 245768 | tf_op jit(solution)/shard_map/ppermute | solution.py:344
  23.2 4.1 %collective-permute-start.7 = (bf16[80,512]{1,0:T(8,128)(2,1)}, bf16[80,512]{1,0:T(8,128)(2,1)S(1)}, u32[]{:S(2)}, u32[]{:S(2)}) collective-permute-start(bf16[80,512]{1,0:T(8,128)(2,1)} %get-tuple-element.10), channel_id=1, source_target_pairs={{0,7},{1,3},{2,9},{3,1},{4,19},{5,8},{6,29},{7,0},{8,5},{9,2},{10,... | collective-permute-start | bytes 245768 | tf_op jit(solution)/shard_map/ppermute | solution.py:344
  27.3 1.2 %copy-start.2 = (bf16[1,1024,512]{2,1,0:T(8,128)(2,1)S(1)}, bf16[1,1024,512]{2,1,0:T(8,128)(2,1)}, u32[]{:S(2)}) copy-start(bf16[1,1024,512]{2,1,0:T(8,128)(2,1)} %w_update.7) | copy-start | bytes 3145732
  28.6 1.0 copy-start.4
  29.6 4.6 %copy-start.3 = (bf16[1,1024,512]{2,1,0:T(8,128)(2,1)S(1)}, bf16[1,1024,512]{2,1,0:T(8,128)(2,1)}, u32[]{:S(2)}) copy-start(bf16[1,1024,512]{2,1,0:T(8,128)(2,1)} %w_update.7) | copy-start | bytes 3145732
  29.6 4.6 %copy-start.5 = (bf16[1,512,512]{2,1,0:T(8,128)(2,1)S(1)}, bf16[1,512,512]{2,1,0:T(8,128)(2,1)}, u32[]{:S(2)}) copy-start(bf16[1,512,512]{2,1,0:T(8,128)(2,1)} %w_message.7) | copy-start | bytes 1572868
  29.6 4.6 %collective-permute-start.11 = (bf16[512,512]{1,0:T(8,128)(2,1)S(1)}, bf16[512,512]{1,0:T(8,128)(2,1)}, u32[]{:S(2)}, u32[]{:S(2)}) collective-permute-start(bf16[512,512]{1,0:T(8,128)(2,1)S(1)} %layer.4), channel_id=1, source_target_pairs={{0,8},{1,3},{2,10},{3,1},{4,12},{5,7},{6,14},{7,5},{8,0},{9,11},{1... | collective-permute-start | bytes 1572872 | tf_op jit(solution)/shard_map/ppermute | solution.py:344
  32.5 1.5 %collective-permute-start.10 = (s32[8,512]{1,0:T(8,128)S(1)}, s32[8,512]{1,0:T(8,128)S(1)}, u32[]{:S(2)}, u32[]{:S(2)}) collective-permute-start(s32[8,512]{1,0:T(8,128)S(1)} %get-tuple-element.11.index), channel_id=1, source_target_pairs={{0,8},{1,3},{2,10},{3,1},{4,12},{5,7},{6,14},{7,5},{8,0},{9,11},{1... | collective-permute-start | bytes 49160 | tf_op jit(solution)/shard_map/ppermute | solution.py:344
  35.3 2.0 %collective-permute-start.12 = (bf16[512,512]{1,0:T(8,128)(2,1)S(1)}, bf16[512,512]{1,0:T(8,128)(2,1)}, u32[]{:S(2)}, u32[]{:S(2)}) collective-permute-start(bf16[512,512]{1,0:T(8,128)(2,1)S(1)} %layer.5), channel_id=1, source_target_pairs={{0,1},{1,0},{2,3},{3,2},{4,5},{5,4},{6,7},{7,6},{8,16},{9,11},{10,... | collective-permute-start | bytes 1572872 | tf_op jit(solution)/shard_map/ppermute | solution.py:344
  35.7 1.6 %collective-permute-start.9 = (s32[8,512]{1,0:T(8,128)S(1)}, s32[8,512]{1,0:T(8,128)S(1)}, u32[]{:S(2)}, u32[]{:S(2)}) collective-permute-start(s32[8,512]{1,0:T(8,128)S(1)} %get-tuple-element.11.index), channel_id=1, source_target_pairs={{0,16},{1,3},{2,18},{3,1},{4,20},{5,7},{6,22},{7,5},{8,9},{9,8},{1... | collective-permute-start | bytes 49160 | tf_op jit(solution)/shard_map/ppermute | solution.py:344
  38.4 8.2 %collective-permute-start.13 = (bf16[512,512]{1,0:T(8,128)(2,1)S(1)}, bf16[512,512]{1,0:T(8,128)(2,1)}, u32[]{:S(2)}, u32[]{:S(2)}) collective-permute-start(bf16[512,512]{1,0:T(8,128)(2,1)S(1)} %layer.6), channel_id=1, source_target_pairs={{0,1},{1,0},{2,3},{3,2},{4,5},{5,4},{6,7},{7,6},{8,9},{9,8},{10,11... | collective-permute-start | bytes 1572872 | tf_op jit(solution)/shard_map/ppermute | solution.py:344
  38.4 8.2 %collective-permute-start.8 = (s32[8,512]{1,0:T(8,128)S(1)}, s32[8,512]{1,0:T(8,128)S(1)}, u32[]{:S(2)}, u32[]{:S(2)}) collective-permute-start(s32[8,512]{1,0:T(8,128)S(1)} %get-tuple-element.11.index), channel_id=1, source_target_pairs={{0,24},{1,3},{2,26},{3,1},{4,28},{5,7},{6,30},{7,5},{8,9},{9,8},{1... | collective-permute-start | bytes 49160 | tf_op jit(solution)/shard_map/ppermute | solution.py:344
  46.6 54.4 %copy-start.8 = (bf16[128,512]{1,0:T(8,128)(2,1)S(1)}, bf16[128,512]{1,0:T(8,128)(2,1)}, u32[]{:S(2)}) copy-start(bf16[128,512]{1,0:T(8,128)(2,1)} %get-tuple-element.9.latent) | copy-start | bytes 393220
  47.7 53.3 %copy-start.6 = (bf16[1024,512]{1,0:T(8,128)(2,1)S(1)}, bf16[1024,512]{1,0:T(8,128)(2,1)}, u32[]{:S(2)}) copy-start(bf16[1024,512]{1,0:T(8,128)(2,1)} %w_decode.3) | copy-start | bytes 3145732
  47.7 46.6 %collective-permute-start.14 = (bf16[64,512]{1,0:T(8,128)(2,1)S(1)}, bf16[64,512]{1,0:T(8,128)(2,1)S(1)}, u32[]{:S(2)}, u32[]{:S(2)}) collective-permute-start(bf16[64,512]{1,0:T(8,128)(2,1)S(1)} %get-tuple-element.20), channel_id=1, source_target_pairs={{0,24},{1,2},{2,1},{3,4},{4,3},{5,6},{6,5},{7,8},{8,7},{9,11},{10,... | collective-permute-start | bytes 196616 | tf_op jit(solution)/shard_map/ppermute | solution.py:344
  71.9 23.0 %collective-permute-start.15 = (bf16[64,512]{1,0:T(8,128)(2,1)S(1)}, bf16[64,512]{1,0:T(8,128)(2,1)S(1)}, u32[]{:S(2)}, u32[]{:S(2)}) collective-permute-start(bf16[64,512]{1,0:T(8,128)(2,1)S(1)} %get-tuple-element.19), channel_id=1, source_target_pairs={{0,2},{1,24},{2,0},{3,4},{4,3},{5,6},{6,5},{7,8},{8,7},{9,10},{10,... | collective-permute-start | bytes 196616 | tf_op jit(solution)/shard_map/ppermute | solution.py:344
  72.0 28.5 %collective-permute-start.16 = (bf16[64,512]{1,0:T(8,128)(2,1)S(1)}, bf16[64,512]{1,0:T(8,128)(2,1)S(1)}, u32[]{:S(2)}, u32[]{:S(2)}) collective-permute-start(bf16[64,512]{1,0:T(8,128)(2,1)S(1)} %get-tuple-element.18), channel_id=1, source_target_pairs={{0,1},{1,0},{2,30},{3,4},{4,3},{5,6},{6,5},{7,8},{8,7},{9,10},{10,... | collective-permute-start | bytes 196616 | tf_op jit(solution)/shard_map/ppermute | solution.py:344
  78.0 23.2 %collective-permute-start.17 = (bf16[64,512]{1,0:T(8,128)(2,1)S(1)}, bf16[64,512]{1,0:T(8,128)(2,1)S(1)}, u32[]{:S(2)}, u32[]{:S(2)}) collective-permute-start(bf16[64,512]{1,0:T(8,128)(2,1)S(1)} %get-tuple-element.17), channel_id=1, source_target_pairs={{0,1},{1,0},{2,4},{3,24},{4,2},{5,6},{6,5},{7,8},{8,7},{9,10},{10,... | collective-permute-start | bytes 196616 | tf_op jit(solution)/shard_map/ppermute | solution.py:344
  88.7 12.5 %collective-permute-start.18 = (bf16[64,512]{1,0:T(8,128)(2,1)S(1)}, bf16[64,512]{1,0:T(8,128)(2,1)S(1)}, u32[]{:S(2)}, u32[]{:S(2)}) collective-permute-start(bf16[64,512]{1,0:T(8,128)(2,1)S(1)} %get-tuple-element.16), channel_id=1, source_target_pairs={{0,1},{1,0},{2,3},{3,2},{4,24},{5,6},{6,5},{7,8},{8,7},{9,10},{10,... | collective-permute-start | bytes 196616 | tf_op jit(solution)/shard_map/ppermute | solution.py:344
  94.3 6.9 %collective-permute-start.19 = (bf16[64,512]{1,0:T(8,128)(2,1)S(1)}, bf16[64,512]{1,0:T(8,128)(2,1)S(1)}, u32[]{:S(2)}, u32[]{:S(2)}) collective-permute-start(bf16[64,512]{1,0:T(8,128)(2,1)S(1)} %get-tuple-element.15), channel_id=1, source_target_pairs={{0,1},{1,0},{2,3},{3,2},{4,6},{5,24},{6,4},{7,8},{8,7},{9,10},{10,... | collective-permute-start | bytes 196616 | tf_op jit(solution)/shard_map/ppermute | solution.py:344
  94.9 8.0 %collective-permute-start.20 = (bf16[64,512]{1,0:T(8,128)(2,1)S(1)}, bf16[64,512]{1,0:T(8,128)(2,1)S(1)}, u32[]{:S(2)}, u32[]{:S(2)}) collective-permute-start(bf16[64,512]{1,0:T(8,128)(2,1)S(1)} %get-tuple-element.14), channel_id=1, source_target_pairs={{0,1},{1,0},{2,3},{3,2},{4,5},{5,4},{6,24},{7,9},{8,26},{9,7},{10,... | collective-permute-start | bytes 196616 | tf_op jit(solution)/shard_map/ppermute | solution.py:344
  100.5 6.2 %collective-permute-start.21 = (bf16[64,512]{1,0:T(8,128)(2,1)S(1)}, bf16[64,512]{1,0:T(8,128)(2,1)S(1)}, u32[]{:S(2)}, u32[]{:S(2)}) collective-permute-start(bf16[64,512]{1,0:T(8,128)(2,1)S(1)} %get-tuple-element.13), channel_id=1, source_target_pairs={{0,1},{1,0},{2,3},{3,2},{4,5},{5,4},{6,8},{7,24},{8,6},{9,26},{10,... | collective-permute-start | bytes 196616 | tf_op jit(solution)/shard_map/ppermute | solution.py:344
  101.0 5.7 %copy-start.7 = (bf16[512,227]{0,1:T(8,128)(2,1)S(1)}, bf16[512,227]{0,1:T(8,128)(2,1)}, u32[]{:S(2)}) copy-start(bf16[512,227]{0,1:T(8,128)(2,1)} %param.18) | copy-start | bytes 697348
  106.7 0.7 copy-start.9

commit v4 on v3

--- a/solution.py
+++ b/solution.py
@@ -175,22 +175,21 @@
     return copies
 
 
-def encode_kernel(*refs):
-    inputs, (payload, latent_out), held, semaphores = refs[:6], refs[6:8], refs[8:14], refs[14]
+def encode_kernel(samples, first, *refs):
+    inputs, payloads = refs[:6], refs[6 : 6 + samples]
+    held, latent, semaphores = refs[6 + samples : 12 + samples], refs[12 + samples], refs[13 + samples]
     copies = fetch(inputs, held, semaphores)
     for copy in copies:
         copy.wait()
-    snapshot, w_embed, grid_mesh, neighbors, send_rows, counts = held
+    snapshots, w_embed, grid_mesh, neighbors, send_rows, counts = held
     mesh_rows = neighbors.shape[1]
     fanout = neighbors.shape[0]
-    grid_rows = snapshot.shape[1]
+    grid_rows = snapshots.shape[1] // samples
     lists, halo_rows = send_rows.shape
     width = w_embed.shape[1]
-    latent = silu_by_tanh(matmul_tn(snapshot[...], w_embed[...])).astype(jnp.bfloat16)
-    latent_out[...] = latent
+    latent[...] = silu_by_tanh(matmul_tn(snapshots[...], w_embed[...])).astype(jnp.bfloat16)
     table = lax.broadcasted_iota(jnp.int32, (mesh_rows, grid_rows), 0) == grid_mesh[...]
-    pooled = matmul(jnp.where(table, 1.0, 0.0).astype(jnp.bfloat16), latent)
-    payload[:mesh_rows, :] = rms_scale(pooled).astype(jnp.bfloat16)
+    table = jnp.where(table, 1.0, 0.0).astype(jnp.bfloat16)
     near = neighbors[...]
     block = near // mesh_rows
     row = near - block * mesh_rows
@@ -204,19 +203,37 @@
     pieces = [block, filler, row, filler, jnp.concatenate(rows, axis=0), filler]
     coded = jnp.concatenate(pieces + [jnp.zeros((fanout, width - 384), jnp.int32)], axis=1)
     coded = jnp.concatenate([coded, jnp.zeros_like(coded)], axis=0)
-    payload[mesh_rows:, :] = coded.astype(jnp.float32).astype(jnp.bfloat16)
+    coded = coded.astype(jnp.float32).astype(jnp.bfloat16)
+    for turn, payload in enumerate(payloads):
+        sample = lax.rem(first[0] + turn, samples)
+        start = pl.multiple_of(sample * grid_rows, grid_rows)
+        pooled = matmul(table, latent[pl.ds(start, grid_rows), :])
+        payload[:mesh_rows, :] = rms_scale(pooled).astype(jnp.bfloat16)
+        payload[mesh_rows:, :] = coded
+
+
+def join_kernel(*refs):
+    payloads, joined = refs[:-1], refs[-1]
+    rows = payloads[0].shape[0]
+    for place, payload in enumerate(payloads):
+        joined[place * rows : (place + 1) * rows, :] = payload[...]
 
 
 def index_kernel(parts, mesh_rows, active, *refs):
-    payloads, (index_out, state_out) = refs[:parts], refs[parts:]
+    lanes, (index_out, state_out) = refs[:-2], refs[-2:]
     fanout = index_out.shape[0]
+    group = len(lanes)
+    owners = parts // group
+    rows = lanes[0].shape[0] // owners
 
     @pl.when(active[0] == 1)
     def _():
         tables = []
         for part in range(parts):
-            state_out[part * mesh_rows : (part + 1) * mesh_rows, :] = payloads[part][:mesh_rows, :]
-            coded = payloads[part][mesh_rows:, :384].astype(jnp.float32).astype(jnp.int32)
+            lane, turn = lanes[part % group], (-(part // group)) % owners
+            base = turn * rows
+            state_out[part * mesh_rows : (part + 1) * mesh_rows, :] = lane[base : base + mesh_rows, :]
+            coded = lane[base + mesh_rows : base + rows, :384].astype(jnp.float32).astype(jnp.int32)
             tables.append(coded[:fanout])
         for part in range(parts):
             block = tables[part][:, :128]
@@ -261,29 +278,29 @@
             state_out[start : start + chunk, :] = renewed.astype(jnp.bfloat16)
 
 
-def prepare_kernel(latent, w_decode, ready):
-    ready[...] = matmul(latent[...], w_decode[: latent.shape[1], :])
-
-
-def decode_kernel(parts, turn, ready, mesh_grid, w_decode, w_output, *refs):
-    blocks, out, state = refs[:parts], refs[parts], refs[parts + 1]
+def prepare_kernel(snapshot, w_embed, w_decode, mesh_grid, ready, table_out):
+    latent = silu_by_tanh(matmul_tn(snapshot[...], w_embed[...])).astype(jnp.bfloat16)
+    ready[...] = matmul(latent, w_decode[: latent.shape[1], :])
+    mesh_rows, grid_rows = table_out.shape
+    table = lax.broadcasted_iota(jnp.int32, (mesh_rows, grid_rows), 0) == mesh_grid[...]
+    table_out[...] = jnp.where(table, 1.0, 0.0).astype(jnp.bfloat16)
+
+
+def decode_kernel(turn, ready, table, w_decode, w_output, *refs):
+    blocks, out, state = refs[:-2], refs[-2], refs[-1]
     width = ready.shape[1]
     for number, block in enumerate(blocks):
 
         @pl.when(turn[0] == number)
         def _():
-            state[...] = block[...]
-
-    mesh_rows = state.shape[0]
-    grid_rows = ready.shape[0]
-    table = lax.broadcasted_iota(jnp.int32, (mesh_rows, grid_rows), 0) == mesh_grid[...]
-    table = jnp.where(table, 1.0, 0.0).astype(jnp.bfloat16)
-    readout = matmul_tn(table, state[...]).astype(jnp.bfloat16)
+            state[...] = block[: state.shape[0], :]
+
+    readout = matmul_tn(table[...], state[...]).astype(jnp.bfloat16)
     hidden = silu_by_tanh(ready[...] + matmul(readout, w_decode[width:, :])).astype(jnp.bfloat16)
     out[...] = matmul_nt(w_output[...], hidden).astype(jnp.bfloat16)
 
 
-def call(kernel, name, shapes, inputs, places, scratch=(), room=16):
+def call(kernel, name, shapes, inputs, places, scratch=(), room=16, flops=0):
     kinds = {"s": SMEM, "v": VMEM, "h": HBM}
     return pl.pallas_call(
         kernel,
@@ -293,10 +310,11 @@
         scratch_shapes=list(scratch),
         name=name,
         compiler_params=pltpu.CompilerParams(vmem_limit_bytes=room * 1024 * 1024),
+        cost_estimate=pl.CostEstimate(flops=flops, bytes_accessed=0, transcendentals=0),
     )(*inputs)
 
 
-def every_device(pairs, count):
+def every_device(pairs, count, kind):
     onward = dict(pairs)
     reached = set(onward.values())
     for first in range(count):
@@ -306,9 +324,16 @@
         while last in onward:
             last = onward[last]
         onward[last] = first
-    rest = [other for other in range(count) if other not in onward]
-    for place, other in enumerate(rest):
-        onward[other] = rest[place ^ 1] if place | 1 < len(rest) else other
+    rest = sorted((other for other in range(count) if other not in onward), key=lambda at: (kind(at), at))
+    if len(rest) % 2:
+        alone = rest.pop()
+        if rest:
+            one, two = rest.pop(), rest.pop()
+            onward.update({one: two, two: alone, alone: one})
+        else:
+            onward[alone] = alone
+    for one, two in zip(rest[::2], rest[1::2]):
+        onward.update({one: two, two: one})
     return sorted(onward.items())
 
 
@@ -340,90 +365,120 @@
     def device(at_segment, at_dom):
         return at_segment * parts + at_dom % parts
 
-    def send(value, pairs):
-        return lax.ppermute(value, ("segment", "dom"), every_device(pairs, segments * parts))
+    def send(value, pairs, kind=lambda at: 0):
+        return lax.ppermute(value, ("segment", "dom"), every_device(pairs, segments * parts, kind))
+
+    def rotate(value, steps):
+        return lax.ppermute(value, "dom", [(at, (at + steps) % parts) for at in range(parts)])
+
+    def change_lane(value, steps):
+        pairs = [(at, at - at % group + (at + steps) % group) for at in range(parts)]
+        return lax.ppermute(value, "dom", pairs)
+
+    is_owner = (place % group == 0).astype(jnp.int32).reshape(1)
 
     def active(at_segment):
         return ((segment == at_segment) & (place % group == 0)).astype(jnp.int32).reshape(1)
 
-    snapshot = lax.dynamic_index_in_dim(jnp.transpose(grid_state, (2, 0, 1)), segment, 1, keepdims=False)
+    by_channel = jnp.transpose(grid_state, (2, 0, 1))
     inputs = [
-        snapshot,
+        by_channel.reshape(channels, samples * grid_rows),
         w_embed,
         grid_mesh.reshape(1, grid_rows),
         neighbors.T,
         send_rows,
         halo_count.reshape(-1),
     ]
-    payload, latent = call(
-        encode_kernel,
+    payloads = call(
+        functools.partial(encode_kernel, samples),
         "encode",
-        [
-            jax.ShapeDtypeStruct((mesh_rows + 2 * fanout, width), bf16),
-            jax.ShapeDtypeStruct((grid_rows, width), bf16),
+        [jax.ShapeDtypeStruct((mesh_rows + 2 * fanout, width), bf16)] * samples,
+        [(place // group).reshape(1)] + inputs,
+        "shhhhhh",
+        [pltpu.VMEM(value.shape, value.dtype) for value in inputs[:-1]]
+        + [
+            pltpu.SMEM(inputs[-1].shape, jnp.int32),
+            pltpu.VMEM((samples * grid_rows, width), bf16),
+            pltpu.SemaphoreType.DMA((6,)),
         ],
-        inputs,
-        "hhhhhh",
-        [pltpu.VMEM(value.shape, value.dtype) for value in inputs[:-1]]
-        + [pltpu.SMEM(inputs[-1].shape, jnp.int32), pltpu.SemaphoreType.DMA((6,))],
         room=60,
     )
-    payloads = []
-    for turn in range(parts):
-        pairs = [(device(m, m * group + turn), device(0, m * group)) for m in range(samples)]
-        payloads.append(send(payload, pairs))
+    arrived = [payloads[0]] + [rotate(payloads[turn], turn * group) for turn in range(1, samples)]
+    (joined,) = call(
+        join_kernel,
+        "join",
+        [jax.ShapeDtypeStruct((samples * (mesh_rows + 2 * fanout), width), bf16)],
+        arrived,
+        "v" * samples,
+    )
+    lanes = [joined] + [change_lane(joined, -steps) for steps in range(1, group)]
     index, state = call(
         functools.partial(index_kernel, parts, mesh_rows),
         "index",
         [jax.ShapeDtypeStruct((fanout, nodes), jnp.int32), jax.ShapeDtypeStruct((nodes, width), bf16)],
-        [active(0)] + payloads,
-        "s" + "v" * parts,
-    )
-    indices = [index]
-    for at_segment in range(1, segments):
-        pairs = [(device(0, m * group), device(at_segment, m * group)) for m in range(samples)]
-        indices.append(send(index, pairs))
+        [is_owner] + lanes,
+        "s" + "v" * group,
+    )
     weights = [w_project, w_message, w_update]
     for at_segment in range(segments):
         (state,) = call(
             layer_kernel,
             "layer",
             [jax.ShapeDtypeStruct((nodes, width), bf16)],
-            [active(at_segment), indices[at_segment], state] + weights,
+            [active(at_segment), index, state] + weights,
             "svvvvv",
+            flops=10**10,
         )
         if at_segment + 1 < segments:
             pairs = [
                 (device(at_segment, m * group), device(at_segment + 1, m * group)) for m in range(samples)
             ]
-            state = send(state, pairs)
+            state = send(state, pairs, lambda at: at % group > 0)
         if at_segment == 0:
-            (ready,) = call(
+            snapshot = lax.dynamic_index_in_dim(by_channel, segment, 1, keepdims=False)
+            ready, table = call(
                 prepare_kernel,
                 "prepare",
-                [jax.ShapeDtypeStruct((grid_rows, width), jnp.float32)],
-                [latent, w_decode],
-                "vv",
+                [
+                    jax.ShapeDtypeStruct((grid_rows, width), jnp.float32),
+                    jax.ShapeDtypeStruct((mesh_rows, grid_rows), bf16),
+                ],
+                [snapshot, w_embed, w_decode, mesh_grid.reshape(1, grid_rows)],
+                "vvvv",
+                flops=10**9,
             )
+    own_turn = (place // group - segment) % samples
+    share = group * mesh_rows
     blocks = []
-    for turn in range(parts):
+    for turn in range(samples):
         pairs = [
-            (device(segments - 1, m * group), device(m, m * group + turn)) for m in range(samples)
+            (device(segments - 1, m * group), device(m, (m + turn) * group)) for m in range(samples)
         ]
-        blocks.append(send(state[turn * mesh_rows : (turn + 1) * mesh_rows], pairs))
+
+        def kind(at, turn=turn):
+            at_segment, at_dom = divmod(at, parts)
+            if at_dom % group:
+                return samples
+            own = (at_dom // group - at_segment) % samples
+            return 0 if own > turn else 1
+
+        pairs = [(source, target) for source, target in pairs if source != target]
+        block = state[turn * share : (turn + 1) * share]
+        blocks.append(send(block, pairs, kind))
+    last_owner = (segment == segments - 1) & (place == (samples - 1) * group)
+    blocks[0] = jnp.where(last_owner, state[:share], blocks[0])
+    block = blocks[0]
+    for turn in range(1, samples):
+        block = jnp.where(own_turn == turn, blocks[turn], block)
+    handed = [block]
+    for steps in range(1, group):
+        handed.append(change_lane(block[steps * mesh_rows : (steps + 1) * mesh_rows], steps))
     (prediction,) = call(
-        functools.partial(decode_kernel, parts),
+        decode_kernel,
         "decode",
         [jax.ShapeDtypeStruct((channels, grid_rows), bf16)],
-        [
-            ((place - segment * group) % parts).reshape(1),
-            ready,
-            mesh_grid.reshape(1, grid_rows),
-            w_decode,
-            w_output.T,
-        ]
-        + blocks,
-        "s" + "v" * (4 + parts),
+        [(place % group).reshape(1), ready, table, w_decode, w_output.T] + handed,
+        "svvvv" + "v" * group,
         [pltpu.VMEM((mesh_rows, width), bf16)],
     )
     return prediction.T.reshape(1, grid_rows, channels)

time: 109 us -> 90.2 us (0.83)
  the two profiles are of different devices: /device:TPU:7 before, /device:TPU:0 now
where the time goes in v4:
time: 90.2 us; the launch traced here: 89.9 us
  waiting for transfers between devices  43.5 us (48%)
  starting transfers between devices  28 us (31%)
  Pallas kernels  12.8 us (14%)
  local copies, waits for them, and re-layouts  5.32 us (6%)
    ppermute x7, waiting for transfers between devices, send(): lax.ppermute(value, ('segment', 'dom'), every_device(pairs, segments * pa...  37.3 us
    ppermute x7, starting transfers between devices, send(): lax.ppermute(value, ('segment', 'dom'), every_device(pairs, segments * pa...  19.7 us
    pallas_call x9, Pallas kernels, call(): pl.pallas_call(kernel, out_shape=shapes, in_specs=[kinds[place] for place...  12.8 us
    ppermute x3, starting transfers between devices, rotate(): lax.ppermute(value, 'dom', [(at, (at + steps) % parts) for at in range(pa...  7.02 us
    unnamed x23, local copies, waits for them, and re-layouts  5.16 us
    ppermute x3, waiting for transfers between devices, rotate(): lax.ppermute(value, 'dom', [(at, (at + steps) % parts) for at in range(pa...  4.57 us
  transfers between devices with their start and end apart: 12, of which 9 were waited for; matrix products, arithmetic and copies ran while one was open for 0% of the time, Pallas kernels for 0%

profile of v4, /device:TPU:0, one launch (start us, length us, event | category | flops | bytes accessed | tf_op | source)
XLA Modules:
  0.0 89.9 jit_solution(11465315470279944060)
XLA Ops:
  0.0 0.0 copy-start.4
  0.0 1.1 %pad = bf16[232,4,128]{2,1,0:T(4,128)(2,1)S(1)} pad(bf16[227,4,128]{2,1,0:T(4,128)(2,1)} %bitcast.29, bf16[]{:T(256)} %constant.67), padding=0_5x0_0x0_0 | pad | bytes 470018
  1.1 0.7 copy.15
  1.8 2.5 %encode.1 = (bf16[80,512]{1,0:T(8,128)(2,1)}, bf16[80,512]{1,0:T(8,128)(2,1)}, bf16[80,512]{1,0:T(8,128)(2,1)}, bf16[80,512]{1,0:T(8,128)(2,1)}) custom-call(s32[1]{0:T(128)} %bitcast.7.first, bf16[227,512]{1,0:T(8,128)(2,1)} %bitcast.27, bf16[227,512]{1,0:T(8,128)(2,1)} %refs_1_.1, s32[1,128]{1,0:T(1,128)} %bitcast.31, s32[8,64]{1,0:T(8,128)} %bitcast.30, ...), custom_call_target="tpu_custom_call" | custom-call | tf_op jit(solution)/shard_map/encode/pallas_call | solution.py:305
  4.3 3.1 %collective-permute-start = (bf16[80,512]{1,0:T(8,128)(2,1)}, bf16[80,512]{1,0:T(8,128)(2,1)S(1)}, u32[]{:S(2)}, u32[]{:S(2)}) collective-permute-start(bf16[80,512]{1,0:T(8,128)(2,1)} %get-tuple-element.16), channel_id=1, source_target_pairs={{0,2},{1,3},{2,4},{3,5},{4,6},{5,7},{6,0},{7,1},{8,10},{9,11},{10,... | collective-permute-start | bytes 245768 | tf_op jit(solution)/shard_map/ppermute | solution.py:372
  7.4 2.6 %collective-permute-start.1 = (bf16[80,512]{1,0:T(8,128)(2,1)}, bf16[80,512]{1,0:T(8,128)(2,1)S(1)}, u32[]{:S(2)}, u32[]{:S(2)}) collective-permute-start(bf16[80,512]{1,0:T(8,128)(2,1)} %get-tuple-element.17), channel_id=1, source_target_pairs={{0,4},{1,5},{2,6},{3,7},{4,0},{5,1},{6,2},{7,3},{8,12},{9,13},{10,... | collective-permute-start | bytes 245768 | tf_op jit(solution)/shard_map/ppermute | solution.py:372
  10.0 1.3 %collective-permute-start.2 = (bf16[80,512]{1,0:T(8,128)(2,1)}, bf16[80,512]{1,0:T(8,128)(2,1)S(1)}, u32[]{:S(2)}, u32[]{:S(2)}) collective-permute-start(bf16[80,512]{1,0:T(8,128)(2,1)} %get-tuple-element.18), channel_id=1, source_target_pairs={{0,6},{1,7},{2,0},{3,1},{4,2},{5,3},{6,4},{7,5},{8,14},{9,15},{10,... | collective-permute-start | bytes 245768 | tf_op jit(solution)/shard_map/ppermute | solution.py:372
  11.3 1.3 %collective-permute-done.refs_1_ = bf16[80,512]{1,0:T(8,128)(2,1)S(1)} collective-permute-done((bf16[80,512]{1,0:T(8,128)(2,1)}, bf16[80,512]{1,0:T(8,128)(2,1)S(1)}, u32[]{:S(2)}, u32[]{:S(2)}) %collective-permute-start) | collective-permute-done | bytes 81952 | tf_op jit(solution)/shard_map/ppermute | solution.py:372
  12.7 3.0 %collective-permute-done.1.refs_2_ = bf16[80,512]{1,0:T(8,128)(2,1)S(1)} collective-permute-done((bf16[80,512]{1,0:T(8,128)(2,1)}, bf16[80,512]{1,0:T(8,128)(2,1)S(1)}, u32[]{:S(2)}, u32[]{:S(2)}) %collective-permute-start.1) | collective-permute-done | bytes 81952 | tf_op jit(solution)/shard_map/ppermute | solution.py:372
  15.7 0.2 collective-permute-done.2.refs_3_
  15.9 0.0 copy-start.3
  15.9 0.9 copy-done.3
  16.8 0.1 collective-permute-start.3
  16.9 1.6 %collective-permute-done.3.refs_1_ = bf16[320,512]{1,0:T(8,128)(2,1)S(1)} collective-permute-done((bf16[320,512]{1,0:T(8,128)(2,1)S(1)}, bf16[320,512]{1,0:T(8,128)(2,1)S(1)}, u32[]{:S(2)}, u32[]{:S(2)}) %collective-permute-start.3) | collective-permute-done | bytes 327712 | tf_op jit(solution)/shard_map/ppermute | solution.py:376
  18.5 0.2 index.1
  18.7 0.0 copy-done.4
  18.7 0.0 copy-done.7
  18.7 1.2 %copy-done.5 = bf16[1,1024,512]{2,1,0:T(8,128)(2,1)S(1)} copy-done((bf16[1,1024,512]{2,1,0:T(8,128)(2,1)S(1)}, bf16[1,1024,512]{2,1,0:T(8,128)(2,1)}, u32[]{:S(2)}) %copy-start.5) | copy-done | bytes 1048600
  19.9 5.4 %layer.4 = bf16[512,512]{1,0:T(8,128)(2,1)S(1)} custom-call(s32[1]{0:T(128)} %bitcast.14.active, s32[8,512]{1,0:T(8,128)S(1)} %get-tuple-element.19.index, bf16[512,512]{1,0:T(8,128)(2,1)S(1)} %get-tuple-element.20.state_in, bf16[1,512,1024]{2,1,0:T(8,128)(2,1)S(1)} %copy-done.4, bf16[1,512,512]{2,1,0:T(8,128)(2,1)S(1)} %copy-done.7, ...), custom_call_target="tpu_custom_call" | custom-call | flops 10000000000 | tf_op jit(solution)/shard_map/layer/pallas_call | solution.py:305
  25.3 0.1 collective-permute-start.4
  25.4 9.3 %collective-permute-done.4.state_in = bf16[512,512]{1,0:T(8,128)(2,1)} collective-permute-done((bf16[512,512]{1,0:T(8,128)(2,1)S(1)}, bf16[512,512]{1,0:T(8,128)(2,1)}, u32[]{:S(2)}, u32[]{:S(2)}) %collective-permute-start.4) | collective-permute-done | bytes 524320 | tf_op jit(solution)/shard_map/ppermute | solution.py:369
  34.7 0.0 copy-done.6
  34.7 1.0 %layer.5 = bf16[512,512]{1,0:T(8,128)(2,1)S(1)} custom-call(s32[1]{0:T(128)} %bitcast.13.active, s32[8,512]{1,0:T(8,128)S(1)} %get-tuple-element.19.index, bf16[512,512]{1,0:T(8,128)(2,1)} %collective-permute-done.4.state_in, bf16[1,512,1024]{2,1,0:T(8,128)(2,1)S(1)} %copy-done.4, bf16[1,512,512]{2,1,0:T(8,128)(2,1)S(1)} %copy-done.7, ...), custom_call_target="tpu_custom_call" | custom-call | flops 10000000000 | tf_op jit(solution)/shard_map/layer/pallas_call | solution.py:305
  35.7 2.0 %collective-permute-start.5 = (bf16[512,512]{1,0:T(8,128)(2,1)S(1)}, bf16[512,512]{1,0:T(8,128)(2,1)}, u32[]{:S(2)}, u32[]{:S(2)}) collective-permute-start(bf16[512,512]{1,0:T(8,128)(2,1)S(1)} %layer.5), channel_id=1, source_target_pairs={{0,2},{1,3},{2,0},{3,1},{4,6},{5,7},{6,4},{7,5},{8,16},{9,11},{10,... | collective-permute-start | bytes 1572872 | tf_op jit(solution)/shard_map/ppermute | solution.py:369
  37.7 11.0 %collective-permute-done.5.state_in = bf16[512,512]{1,0:T(8,128)(2,1)} collective-permute-done((bf16[512,512]{1,0:T(8,128)(2,1)S(1)}, bf16[512,512]{1,0:T(8,128)(2,1)}, u32[]{:S(2)}, u32[]{:S(2)}) %collective-permute-start.5) | collective-permute-done | bytes 524320 | tf_op jit(solution)/shard_map/ppermute | solution.py:369
  48.7 1.0 %layer.6 = bf16[512,512]{1,0:T(8,128)(2,1)S(1)} custom-call(s32[1]{0:T(128)} %bitcast.12.active, s32[8,512]{1,0:T(8,128)S(1)} %get-tuple-element.19.index, bf16[512,512]{1,0:T(8,128)(2,1)} %collective-permute-done.5.state_in, bf16[1,512,1024]{2,1,0:T(8,128)(2,1)S(1)} %copy-done.4, bf16[1,512,512]{2,1,0:T(8,128)(2,1)S(1)} %copy-done.7, ...), custom_call_target="tpu_custom_call" | custom-call | flops 10000000000 | tf_op jit(solution)/shard_map/layer/pallas_call | solution.py:305
  49.7 2.3 %collective-permute-start.6 = (bf16[512,512]{1,0:T(8,128)(2,1)S(1)}, bf16[512,512]{1,0:T(8,128)(2,1)}, u32[]{:S(2)}, u32[]{:S(2)}) collective-permute-start(bf16[512,512]{1,0:T(8,128)(2,1)S(1)} %layer.6), channel_id=1, source_target_pairs={{0,2},{1,3},{2,0},{3,1},{4,6},{5,7},{6,4},{7,5},{8,10},{9,11},{10,... | collective-permute-start | bytes 1572872 | tf_op jit(solution)/shard_map/ppermute | solution.py:369
  52.0 10.7 %collective-permute-done.6.state_in = bf16[512,512]{1,0:T(8,128)(2,1)} collective-permute-done((bf16[512,512]{1,0:T(8,128)(2,1)S(1)}, bf16[512,512]{1,0:T(8,128)(2,1)}, u32[]{:S(2)}, u32[]{:S(2)}) %collective-permute-start.6) | collective-permute-done | bytes 524320 | tf_op jit(solution)/shard_map/ppermute | solution.py:369
  62.6 1.1 %layer.7 = bf16[512,512]{1,0:T(8,128)(2,1)S(1)} custom-call(s32[1]{0:T(128)} %bitcast.5.active, s32[8,512]{1,0:T(8,128)S(1)} %get-tuple-element.19.index, bf16[512,512]{1,0:T(8,128)(2,1)} %collective-permute-done.6.state_in, bf16[1,512,1024]{2,1,0:T(8,128)(2,1)S(1)} %copy-done.4, bf16[1,512,512]{2,1,0:T(8,128)(2,1)S(1)} %copy-done.7, ...), custom_call_target="tpu_custom_call" | custom-call | flops 10000000000 | tf_op jit(solution)/shard_map/layer/pallas_call | solution.py:305
  63.8 7.8 %collective-permute-start.10 = (bf16[128,512]{1,0:T(8,128)(2,1)S(1)}, bf16[128,512]{1,0:T(8,128)(2,1)S(1)}, u32[]{:S(2)}, u32[]{:S(2)}) collective-permute-start(bf16[128,512]{1,0:T(8,128)(2,1)S(1)} %get-tuple-element.21), channel_id=1, source_target_pairs={{0,24},{1,3},{2,4},{3,1},{4,2},{5,7},{6,8},{7,5},{8,6},{9,11},{10,... | collective-permute-start | bytes 393224 | tf_op jit(solution)/shard_map/ppermute | solution.py:369
  71.6 0.0 collective-permute-start.7
  71.6 7.6 %collective-permute-start.8 = (bf16[128,512]{1,0:T(8,128)(2,1)S(1)}, bf16[128,512]{1,0:T(8,128)(2,1)S(1)}, u32[]{:S(2)}, u32[]{:S(2)}) collective-permute-start(bf16[128,512]{1,0:T(8,128)(2,1)S(1)} %get-tuple-element.23), channel_id=1, source_target_pairs={{0,18},{1,22},{2,10},{3,5},{4,24},{5,3},{6,8},{7,9},{8,6},{9,7},{1... | collective-permute-start | bytes 393224 | tf_op jit(solution)/shard_map/ppermute | solution.py:369
  79.1 0.0 collective-permute-start.9
  79.1 0.0 copy-done.9
  79.1 0.1 constant_dynamic-slice_fusion
  79.3 0.0 copy-start.2
  79.3 0.0 collective-permute-done.10
  79.3 0.0 collective-permute-done.7
  79.3 4.1 %collective-permute-done.8 = bf16[128,512]{1,0:T(8,128)(2,1)S(1)} collective-permute-done((bf16[128,512]{1,0:T(8,128)(2,1)S(1)}, bf16[128,512]{1,0:T(8,128)(2,1)S(1)}, u32[]{:S(2)}, u32[]{:S(2)}) %collective-permute-start.8) | collective-permute-done | bytes 131104 | tf_op jit(solution)/shard_map/ppermute | solution.py:369
  83.4 2.4 %collective-permute-done.9 = bf16[128,512]{1,0:T(8,128)(2,1)S(1)} collective-permute-done((bf16[128,512]{1,0:T(8,128)(2,1)S(1)}, bf16[128,512]{1,0:T(8,128)(2,1)S(1)}, u32[]{:S(2)}, u32[]{:S(2)}) %collective-permute-start.9) | collective-permute-done | bytes 131104 | tf_op jit(solution)/shard_map/ppermute | solution.py:369
  85.8 1.2 %collective-permute-start.11 = (bf16[64,512]{1,0:T(8,128)(2,1)S(1)}, bf16[64,512]{1,0:T(8,128)(2,1)S(1)}, u32[]{:S(2)}, u32[]{:S(2)}) collective-permute-start(bf16[64,512]{1,0:T(8,128)(2,1)S(1)} %slice.25), channel_id=1, source_target_pairs={{0,1},{1,0},{2,3},{3,2},{4,5},{5,4},{6,7},{7,6},{8,9},{9,8},{10,11... | collective-permute-start | bytes 196616 | tf_op jit(solution)/shard_map/ppermute | solution.py:376
  87.0 0.0 copy-done
  87.0 0.0 copy-done.2
  87.0 0.6 copy-done.8
  87.7 0.4 prepare.1
  88.1 0.0 collective-permute-done.11.refs_1_
  88.1 0.5 copy-done.1
  88.6 1.2 %decode.1 = bf16[227,128]{1,0:T(8,128)(2,1)} custom-call(s32[1]{0:T(128)} %bitcast.turn, f32[128,512]{1,0:T(8,128)S(1)} %get-tuple-element.13.ready, bf16[64,128]{1,0:T(8,128)(2,1)S(1)} %get-tuple-element.14.table, bf16[1024,512]{1,0:T(8,128)(2,1)S(1)} %copy-done, bf16[227,512]{1,0:T(8,128)(2,1)S(1)} %bitcast.24, ...), custom_call_target="tpu_custom_call" | custom-call | tf_op jit(solution)/shard_map/decode/pallas_call | solution.py:305
  (12 shorter events, 0.1 us)
Async XLA Ops:
  0.0 18.7 %copy-start.4 = (bf16[1,512,1024]{2,1,0:T(8,128)(2,1)S(1)}, bf16[1,512,1024]{2,1,0:T(8,128)(2,1)}, u32[]{:S(2)}) copy-start(bf16[1,512,1024]{2,1,0:T(8,128)(2,1)} %w_project.7) | copy-start | bytes 3145732
  4.3 8.3 %collective-permute-start = (bf16[80,512]{1,0:T(8,128)(2,1)}, bf16[80,512]{1,0:T(8,128)(2,1)S(1)}, u32[]{:S(2)}, u32[]{:S(2)}) collective-permute-start(bf16[80,512]{1,0:T(8,128)(2,1)} %get-tuple-element.16), channel_id=1, source_target_pairs={{0,2},{1,3},{2,4},{3,5},{4,6},{5,7},{6,0},{7,1},{8,10},{9,11},{10,... | collective-permute-start | bytes 245768 | tf_op jit(solution)/shard_map/ppermute | solution.py:372
  7.4 8.3 %collective-permute-start.1 = (bf16[80,512]{1,0:T(8,128)(2,1)}, bf16[80,512]{1,0:T(8,128)(2,1)S(1)}, u32[]{:S(2)}, u32[]{:S(2)}) collective-permute-start(bf16[80,512]{1,0:T(8,128)(2,1)} %get-tuple-element.17), channel_id=1, source_target_pairs={{0,4},{1,5},{2,6},{3,7},{4,0},{5,1},{6,2},{7,3},{8,12},{9,13},{10,... | collective-permute-start | bytes 245768 | tf_op jit(solution)/shard_map/ppermute | solution.py:372
  10.0 5.9 %collective-permute-start.2 = (bf16[80,512]{1,0:T(8,128)(2,1)}, bf16[80,512]{1,0:T(8,128)(2,1)S(1)}, u32[]{:S(2)}, u32[]{:S(2)}) collective-permute-start(bf16[80,512]{1,0:T(8,128)(2,1)} %get-tuple-element.18), channel_id=1, source_target_pairs={{0,6},{1,7},{2,0},{3,1},{4,2},{5,3},{6,4},{7,5},{8,14},{9,15},{10,... | collective-permute-start | bytes 245768 | tf_op jit(solution)/shard_map/ppermute | solution.py:372
  15.9 0.9 copy-start.3
  16.8 1.9 %copy-start.7 = (bf16[1,512,512]{2,1,0:T(8,128)(2,1)S(1)}, bf16[1,512,512]{2,1,0:T(8,128)(2,1)}, u32[]{:S(2)}) copy-start(bf16[1,512,512]{2,1,0:T(8,128)(2,1)} %w_message.7) | copy-start | bytes 1572868
  16.8 1.7 %collective-permute-start.3 = (bf16[320,512]{1,0:T(8,128)(2,1)S(1)}, bf16[320,512]{1,0:T(8,128)(2,1)S(1)}, u32[]{:S(2)}, u32[]{:S(2)}) collective-permute-start(bf16[320,512]{1,0:T(8,128)(2,1)S(1)} %join.1.refs_0_), channel_id=1, source_target_pairs={{0,1},{1,0},{2,3},{3,2},{4,5},{5,4},{6,7},{7,6},{8,9},{9,8},{10,11... | collective-permute-start | bytes 983048 | tf_op jit(solution)/shard_map/ppermute | solution.py:376
  18.7 1.2 %copy-start.5 = (bf16[1,1024,512]{2,1,0:T(8,128)(2,1)S(1)}, bf16[1,1024,512]{2,1,0:T(8,128)(2,1)}, u32[]{:S(2)}) copy-start(bf16[1,1024,512]{2,1,0:T(8,128)(2,1)} %w_update.7) | copy-start | bytes 3145732
  19.9 14.7 %copy-start.6 = (bf16[1,1024,512]{2,1,0:T(8,128)(2,1)S(1)}, bf16[1,1024,512]{2,1,0:T(8,128)(2,1)}, u32[]{:S(2)}) copy-start(bf16[1,1024,512]{2,1,0:T(8,128)(2,1)} %w_update.7) | copy-start | bytes 3145732
  25.3 9.4 %collective-permute-start.4 = (bf16[512,512]{1,0:T(8,128)(2,1)S(1)}, bf16[512,512]{1,0:T(8,128)(2,1)}, u32[]{:S(2)}, u32[]{:S(2)}) collective-permute-start(bf16[512,512]{1,0:T(8,128)(2,1)S(1)} %layer.4), channel_id=1, source_target_pairs={{0,8},{1,3},{2,10},{3,1},{4,12},{5,7},{6,14},{7,5},{8,0},{9,11},{1... | collective-permute-start | bytes 1572872 | tf_op jit(solution)/shard_map/ppermute | solution.py:369
  35.7 13.0 %collective-permute-start.5 = (bf16[512,512]{1,0:T(8,128)(2,1)S(1)}, bf16[512,512]{1,0:T(8,128)(2,1)}, u32[]{:S(2)}, u32[]{:S(2)}) collective-permute-start(bf16[512,512]{1,0:T(8,128)(2,1)S(1)} %layer.5), channel_id=1, source_target_pairs={{0,2},{1,3},{2,0},{3,1},{4,6},{5,7},{6,4},{7,5},{8,16},{9,11},{10,... | collective-permute-start | bytes 1572872 | tf_op jit(solution)/shard_map/ppermute | solution.py:369
  49.7 12.9 %collective-permute-start.6 = (bf16[512,512]{1,0:T(8,128)(2,1)S(1)}, bf16[512,512]{1,0:T(8,128)(2,1)}, u32[]{:S(2)}, u32[]{:S(2)}) collective-permute-start(bf16[512,512]{1,0:T(8,128)(2,1)S(1)} %layer.6), channel_id=1, source_target_pairs={{0,2},{1,3},{2,0},{3,1},{4,6},{5,7},{6,4},{7,5},{8,10},{9,11},{10,... | collective-permute-start | bytes 1572872 | tf_op jit(solution)/shard_map/ppermute | solution.py:369
  62.6 16.5 %copy-start.9 = (bf16[4,128,227]{1,0,2:T(4,128)(2,1)S(1)}, bf16[4,128,227]{1,0,2:T(4,128)(2,1)}, u32[]{:S(2)}) copy-start(bf16[4,128,227]{1,0,2:T(4,128)(2,1)} %param.12) | copy-start | bytes 697348
  63.7 23.3 %copy-start = (bf16[1024,512]{1,0:T(8,128)(2,1)S(1)}, bf16[1024,512]{1,0:T(8,128)(2,1)}, u32[]{:S(2)}) copy-start(bf16[1024,512]{1,0:T(8,128)(2,1)} %w_decode.3) | copy-start | bytes 3145732
  63.8 15.5 %collective-permute-start.10 = (bf16[128,512]{1,0:T(8,128)(2,1)S(1)}, bf16[128,512]{1,0:T(8,128)(2,1)S(1)}, u32[]{:S(2)}, u32[]{:S(2)}) collective-permute-start(bf16[128,512]{1,0:T(8,128)(2,1)S(1)} %get-tuple-element.21), channel_id=1, source_target_pairs={{0,24},{1,3},{2,4},{3,1},{4,2},{5,7},{6,8},{7,5},{8,6},{9,11},{10,... | collective-permute-start | bytes 393224 | tf_op jit(solution)/shard_map/ppermute | solution.py:369
  71.6 7.7 %collective-permute-start.7 = (bf16[128,512]{1,0:T(8,128)(2,1)S(1)}, bf16[128,512]{1,0:T(8,128)(2,1)S(1)}, u32[]{:S(2)}, u32[]{:S(2)}) collective-permute-start(bf16[128,512]{1,0:T(8,128)(2,1)S(1)} %get-tuple-element.24), channel_id=1, source_target_pairs={{0,2},{1,22},{2,0},{3,5},{4,10},{5,3},{6,24},{7,9},{8,26},{9,7},{1... | collective-permute-start | bytes 393224 | tf_op jit(solution)/shard_map/ppermute | solution.py:369
  71.6 11.8 %collective-permute-start.8 = (bf16[128,512]{1,0:T(8,128)(2,1)S(1)}, bf16[128,512]{1,0:T(8,128)(2,1)S(1)}, u32[]{:S(2)}, u32[]{:S(2)}) collective-permute-start(bf16[128,512]{1,0:T(8,128)(2,1)S(1)} %get-tuple-element.23), channel_id=1, source_target_pairs={{0,18},{1,22},{2,10},{3,5},{4,24},{5,3},{6,8},{7,9},{8,6},{9,7},{1... | collective-permute-start | bytes 393224 | tf_op jit(solution)/shard_map/ppermute | solution.py:369
  79.1 6.6 %collective-permute-start.9 = (bf16[128,512]{1,0:T(8,128)(2,1)S(1)}, bf16[128,512]{1,0:T(8,128)(2,1)S(1)}, u32[]{:S(2)}, u32[]{:S(2)}) collective-permute-start(bf16[128,512]{1,0:T(8,128)(2,1)S(1)} %get-tuple-element.22), channel_id=1, source_target_pairs={{0,10},{1,20},{2,30},{3,5},{4,6},{5,3},{6,4},{7,9},{8,14},{9,7},{1... | collective-permute-start | bytes 393224 | tf_op jit(solution)/shard_map/ppermute | solution.py:369
  79.3 7.8 %copy-start.2 = (bf16[227,512]{1,0:T(8,128)(2,1)S(1)}, bf16[227,512]{1,0:T(8,128)(2,1)}, u32[]{:S(2)}) copy-start(bf16[227,512]{1,0:T(8,128)(2,1)} %refs_1_.1) | copy-start | bytes 697348
  85.8 2.3 %collective-permute-start.11 = (bf16[64,512]{1,0:T(8,128)(2,1)S(1)}, bf16[64,512]{1,0:T(8,128)(2,1)S(1)}, u32[]{:S(2)}, u32[]{:S(2)}) collective-permute-start(bf16[64,512]{1,0:T(8,128)(2,1)S(1)} %slice.25), channel_id=1, source_target_pairs={{0,1},{1,0},{2,3},{3,2},{4,5},{5,4},{6,7},{7,6},{8,9},{9,8},{10,11... | collective-permute-start | bytes 196616 | tf_op jit(solution)/shard_map/ppermute | solution.py:376
  87.0 0.7 copy-start.8
  87.7 0.9 %copy-start.1 = (bf16[512,227]{0,1:T(8,128)(2,1)S(1)}, bf16[512,227]{0,1:T(8,128)(2,1)}, u32[]{:S(2)}) copy-start(bf16[512,227]{0,1:T(8,128)(2,1)} %param.18) | copy-start | bytes 697348

commit v5 on v4

--- a/solution.py
+++ b/solution.py
@@ -175,16 +175,16 @@
     return copies
 
 
-def encode_kernel(samples, first, *refs):
-    inputs, payloads = refs[:6], refs[6 : 6 + samples]
-    held, latent, semaphores = refs[6 + samples : 12 + samples], refs[12 + samples], refs[13 + samples]
+def encode_kernel(turns, held_states, chosen, *refs):
+    inputs, payloads = refs[:6], refs[6 : 6 + turns]
+    held, latent, semaphores = refs[6 + turns : 12 + turns], refs[12 + turns], refs[13 + turns]
     copies = fetch(inputs, held, semaphores)
     for copy in copies:
         copy.wait()
     snapshots, w_embed, grid_mesh, neighbors, send_rows, counts = held
     mesh_rows = neighbors.shape[1]
     fanout = neighbors.shape[0]
-    grid_rows = snapshots.shape[1] // samples
+    grid_rows = snapshots.shape[1] // held_states
     lists, halo_rows = send_rows.shape
     width = w_embed.shape[1]
     latent[...] = silu_by_tanh(matmul_tn(snapshots[...], w_embed[...])).astype(jnp.bfloat16)
@@ -205,8 +205,7 @@
     coded = jnp.concatenate([coded, jnp.zeros_like(coded)], axis=0)
     coded = coded.astype(jnp.float32).astype(jnp.bfloat16)
     for turn, payload in enumerate(payloads):
-        sample = lax.rem(first[0] + turn, samples)
-        start = pl.multiple_of(sample * grid_rows, grid_rows)
+        start = pl.multiple_of(chosen[turn] * grid_rows, grid_rows)
         pooled = matmul(table, latent[pl.ds(start, grid_rows), :])
         payload[:mesh_rows, :] = rms_scale(pooled).astype(jnp.bfloat16)
         payload[mesh_rows:, :] = coded
@@ -219,21 +218,21 @@
         joined[place * rows : (place + 1) * rows, :] = payload[...]
 
 
-def index_kernel(parts, mesh_rows, active, *refs):
+def index_kernel(parts, mesh_rows, chip, *refs):
     lanes, (index_out, state_out) = refs[:-2], refs[-2:]
     fanout = index_out.shape[0]
     group = len(lanes)
-    owners = parts // group
-    rows = lanes[0].shape[0] // owners
-
-    @pl.when(active[0] == 1)
+    rows = lanes[0].shape[0] // (parts // group)
+
+    @pl.when(chip[1] == 1)
     def _():
         tables = []
         for part in range(parts):
-            lane, turn = lanes[part % group], (-(part // group)) % owners
-            base = turn * rows
-            state_out[part * mesh_rows : (part + 1) * mesh_rows, :] = lane[base : base + mesh_rows, :]
-            coded = lane[base + mesh_rows : base + rows, :384].astype(jnp.float32).astype(jnp.int32)
+            lane, turn = lanes[part % group], jnp.bitwise_xor(chip[0], part // group)
+            base = pl.multiple_of(turn * rows, 16)
+            state_out[part * mesh_rows : (part + 1) * mesh_rows, :] = lane[pl.ds(base, mesh_rows), :]
+            base = pl.multiple_of(turn * rows + mesh_rows, 16)
+            coded = lane[pl.ds(base, rows - mesh_rows), :384].astype(jnp.float32).astype(jnp.int32)
             tables.append(coded[:fanout])
         for part in range(parts):
             block = tables[part][:, :128]
@@ -249,33 +248,58 @@
             index_out[:, part * mesh_rows : (part + 1) * mesh_rows] = found[:, :mesh_rows]
 
 
-def layer_kernel(active, index, state_in, w_project, w_message, w_update, state_out):
+def run_layer(fanout, columns, state_in, weights, copies, state_out):
+    w_project, w_message, w_update = weights
     nodes, width = state_in.shape
+    chunk = min(256, nodes)
+    names = lax.broadcasted_iota(jnp.int32, (chunk, nodes), 1).astype(jnp.float32)
+    copies[0].wait()
+    sender = matmul(state_in[...], w_project[:, width:]).astype(jnp.bfloat16)
+    for start in range(0, nodes, chunk):
+        own = state_in[start : start + chunk, :]
+        receiver = matmul(own, w_project[:, :width])
+        total = jnp.zeros((chunk, width), jnp.float32)
+        for k in range(fanout):
+            hit = columns[start : start + chunk, k : k + 1] == names
+            fetched = matmul(jnp.where(hit, 1.0, 0.0).astype(jnp.bfloat16), sender)
+            edge = silu_by_tanh(receiver + fetched).astype(jnp.bfloat16)
+            total = total + edge.astype(jnp.float32)
+        gathered = (total * (1.0 / fanout)).astype(jnp.bfloat16)
+        if start == 0:
+            copies[1].wait()
+            copies[2].wait()
+        aggregate = matmul(gathered, w_message[...]).astype(jnp.bfloat16)
+        update = silu_by_tanh(
+            matmul(own, w_update[:width, :]) + matmul(aggregate, w_update[width:, :])
+        )
+        renewed = own.astype(jnp.float32) + rms_scale(update)
+        state_out[start : start + chunk, :] = renewed.astype(jnp.bfloat16)
+
+
+def stage_kernel(where, index, state_in, *refs):
+    own, other, state_out = refs[:3], refs[3:6], refs[6]
+    first, second, between, columns, semaphores = refs[7:10], refs[10:13], refs[13], refs[14], refs[15]
+    nodes = state_in.shape[0]
     fanout = index.shape[0]
-    chunk = min(256, nodes)
-
-    @pl.when(active[0] == 1)
+
+    @pl.when(where[0] == 1)
     def _():
-        columns = jnp.concatenate([index[...], jnp.zeros((128 - fanout, nodes), jnp.int32)], axis=0)
-        columns = jnp.transpose(columns.astype(jnp.float32))
-        names = lax.broadcasted_iota(jnp.int32, (chunk, nodes), 1).astype(jnp.float32)
-        sender = matmul(state_in[...], w_project[0, :, width:]).astype(jnp.bfloat16)
-        for start in range(0, nodes, chunk):
-            own = state_in[start : start + chunk, :]
-            receiver = matmul(own, w_project[0, :, :width])
-            total = jnp.zeros((chunk, width), jnp.float32)
-            for k in range(fanout):
-                hit = columns[start : start + chunk, k : k + 1] == names
-                fetched = matmul(jnp.where(hit, 1.0, 0.0).astype(jnp.bfloat16), sender)
-                edge = silu_by_tanh(receiver + fetched).astype(jnp.bfloat16)
-                total = total + edge.astype(jnp.float32)
-            gathered = (total * (1.0 / fanout)).astype(jnp.bfloat16)
-            aggregate = matmul(gathered, w_message[0]).astype(jnp.bfloat16)
-            update = silu_by_tanh(
-                matmul(own, w_update[0, :width, :]) + matmul(aggregate, w_update[0, width:, :])
-            )
-            renewed = own.astype(jnp.float32) + rms_scale(update)
-            state_out[start : start + chunk, :] = renewed.astype(jnp.bfloat16)
+        @pl.when(where[1] == 0)
+        def _():
+            fetch([ref.at[0] for ref in own + other], first + second, semaphores)
+
+        @pl.when(where[1] == 1)
+        def _():
+            fetch([ref.at[0] for ref in other + own], first + second, semaphores)
+
+        copies = [
+            pltpu.make_async_copy(source.at[0], target, semaphores.at[place])
+            for place, (source, target) in enumerate(zip(own + other, first + second))
+        ]
+        rows = jnp.concatenate([index[...], jnp.zeros((128 - fanout, nodes), jnp.int32)], axis=0)
+        columns[...] = jnp.transpose(rows.astype(jnp.float32))
+        run_layer(fanout, columns, state_in, first, copies[:3], between)
+        run_layer(fanout, columns, between, second, copies[3:], state_out)
 
 
 def prepare_kernel(snapshot, w_embed, w_decode, mesh_grid, ready, table_out):
@@ -368,42 +392,76 @@
     def send(value, pairs, kind=lambda at: 0):
         return lax.ppermute(value, ("segment", "dom"), every_device(pairs, segments * parts, kind))
 
-    def rotate(value, steps):
-        return lax.ppermute(value, "dom", [(at, (at + steps) % parts) for at in range(parts)])
+    def to_chip(value, steps):
+        pairs = [(at, (at // group ^ steps) * group + at % group) for at in range(parts)]
+        return lax.ppermute(value, "dom", pairs)
 
     def change_lane(value, steps):
         pairs = [(at, at - at % group + (at + steps) % group) for at in range(parts)]
         return lax.ppermute(value, "dom", pairs)
 
-    is_owner = (place % group == 0).astype(jnp.int32).reshape(1)
-
-    def active(at_segment):
-        return ((segment == at_segment) & (place % group == 0)).astype(jnp.int32).reshape(1)
+    def chip_of(m):
+        return samples // 2 - 1 + m // 2
+
+    def owner(m, stage):
+        return device(2 * stage + m % 2, chip_of(m) * group)
 
     by_channel = jnp.transpose(grid_state, (2, 0, 1))
+    weights = [w_project, w_message, w_update]
+    chip, lane, parity = place // group, place % group, segment % 2
+    held_states = samples // 2
+
+    def beside(skip):
+        across = segments // 2
+        return [
+            (device(at, dom), device((at + across) % segments, dom))
+            for at in range(segments)
+            for dom in range(parts)
+            if dom % group and dom // group not in skip
+        ]
+
+    chips = [chip_of(m) for m in range(0, samples, 2)]
+    ends = [0, samples - 1]
+    direct = [
+        (device(at, one * group), device(at ^ 1, one * group)) for at in range(segments) for one in chips
+    ] + beside(ends)
+    around = []
+    for at in range(segments):
+        for one, end in zip(chips, ends):
+            around.append((device(at ^ 1, end * group), device(at, one * group)))
+            around.append((device(at, one * group), device(at, end * group)))
+    around += beside([])
+    swapped = [send(w_project, direct), send(w_message, direct), send(w_update, around)]
     inputs = [
-        by_channel.reshape(channels, samples * grid_rows),
+        jnp.concatenate(
+            [
+                lax.dynamic_index_in_dim(by_channel, parity + 2 * one, 1, keepdims=False)
+                for one in range(held_states)
+            ],
+            axis=1,
+        ),
         w_embed,
         grid_mesh.reshape(1, grid_rows),
         neighbors.T,
         send_rows,
         halo_count.reshape(-1),
     ]
+    chosen = jnp.clip((chip ^ jnp.arange(samples, dtype=jnp.int32)) - chips[0], 0, held_states - 1)
     payloads = call(
-        functools.partial(encode_kernel, samples),
+        functools.partial(encode_kernel, samples, held_states),
         "encode",
         [jax.ShapeDtypeStruct((mesh_rows + 2 * fanout, width), bf16)] * samples,
-        [(place // group).reshape(1)] + inputs,
+        [chosen] + inputs,
         "shhhhhh",
         [pltpu.VMEM(value.shape, value.dtype) for value in inputs[:-1]]
         + [
             pltpu.SMEM(inputs[-1].shape, jnp.int32),
-            pltpu.VMEM((samples * grid_rows, width), bf16),
+            pltpu.VMEM((held_states * grid_rows, width), bf16),
             pltpu.SemaphoreType.DMA((6,)),
         ],
         room=60,
     )
-    arrived = [payloads[0]] + [rotate(payloads[turn], turn * group) for turn in range(1, samples)]
+    arrived = [payloads[0]] + [to_chip(payloads[turn], turn) for turn in range(1, samples)]
     (joined,) = call(
         join_kernel,
         "join",
@@ -412,29 +470,35 @@
         "v" * samples,
     )
     lanes = [joined] + [change_lane(joined, -steps) for steps in range(1, group)]
+    is_owner = (lane == 0) & (chip >= chips[0]) & (chip <= chips[-1])
     index, state = call(
         functools.partial(index_kernel, parts, mesh_rows),
         "index",
         [jax.ShapeDtypeStruct((fanout, nodes), jnp.int32), jax.ShapeDtypeStruct((nodes, width), bf16)],
-        [is_owner] + lanes,
+        [jnp.stack([chip, is_owner.astype(jnp.int32)])] + lanes,
         "s" + "v" * group,
     )
-    weights = [w_project, w_message, w_update]
-    for at_segment in range(segments):
+    for stage in range(segments // 2):
+        active = is_owner & (segment // 2 == stage)
         (state,) = call(
-            layer_kernel,
-            "layer",
+            stage_kernel,
+            "stage",
             [jax.ShapeDtypeStruct((nodes, width), bf16)],
-            [active(at_segment), index, state] + weights,
-            "svvvvv",
+            [jnp.stack([active.astype(jnp.int32), parity]), index, state] + weights + swapped,
+            "svv" + "h" * 6,
+            [pltpu.VMEM(weight.shape[1:], bf16) for weight in weights * 2]
+            + [
+                pltpu.VMEM((nodes, width), bf16),
+                pltpu.VMEM((nodes, 128), jnp.float32),
+                pltpu.SemaphoreType.DMA((6,)),
+            ],
+            room=24,
             flops=10**10,
         )
-        if at_segment + 1 < segments:
-            pairs = [
-                (device(at_segment, m * group), device(at_segment + 1, m * group)) for m in range(samples)
-            ]
-            state = send(state, pairs, lambda at: at % group > 0)
-        if at_segment == 0:
+        if 2 * stage + 2 < segments:
+            pairs = [(owner(m, stage), owner(m, stage + 1)) for m in range(samples)]
+            state = send(state, pairs)
+        if stage == 0:
             snapshot = lax.dynamic_index_in_dim(by_channel, segment, 1, keepdims=False)
             ready, table = call(
                 prepare_kernel,
@@ -447,29 +511,26 @@
                 "vvvv",
                 flops=10**9,
             )
-    own_turn = (place // group - segment) % samples
     share = group * mesh_rows
+    last = segments // 2 - 1
     blocks = []
     for turn in range(samples):
-        pairs = [
-            (device(segments - 1, m * group), device(m, (m + turn) * group)) for m in range(samples)
-        ]
 
         def kind(at, turn=turn):
-            at_segment, at_dom = divmod(at, parts)
-            if at_dom % group:
-                return samples
-            own = (at_dom // group - at_segment) % samples
-            return 0 if own > turn else 1
-
+            dom = at % parts
+            return 2 if dom % group else int(dom // group <= turn)
+
+        pairs = [(owner(m, last), device(m, turn * group)) for m in range(samples)]
+        kept = [source for source, target in pairs if source == target]
         pairs = [(source, target) for source, target in pairs if source != target]
         block = state[turn * share : (turn + 1) * share]
-        blocks.append(send(block, pairs, kind))
-    last_owner = (segment == segments - 1) & (place == (samples - 1) * group)
-    blocks[0] = jnp.where(last_owner, state[:share], blocks[0])
+        came = send(block, pairs, kind)
+        for at in kept:
+            came = jnp.where(segment * parts + place == at, block, came)
+        blocks.append(came)
     block = blocks[0]
     for turn in range(1, samples):
-        block = jnp.where(own_turn == turn, blocks[turn], block)
+        block = jnp.where(chip == turn, blocks[turn], block)
     handed = [block]
     for steps in range(1, group):
         handed.append(change_lane(block[steps * mesh_rows : (steps + 1) * mesh_rows], steps))
@@ -477,7 +538,7 @@
         decode_kernel,
         "decode",
         [jax.ShapeDtypeStruct((channels, grid_rows), bf16)],
-        [(place % group).reshape(1), ready, table, w_decode, w_output.T] + handed,
+        [lane.reshape(1), ready, table, w_decode, w_output.T] + handed,
         "svvvv" + "v" * group,
         [pltpu.VMEM((mesh_rows, width), bf16)],
     )
@@ -486,7 +547,7 @@
 
 def fits(mesh):
     segments, parts = mesh.shape["segment"], mesh.shape["dom"]
-    return parts % segments == 0 and parts <= 16
+    return segments == 4 and parts % segments == 0 and parts <= 16
 
 
 def solution(mesh):

time: 90.2 us -> 87.4 us (0.969)
  the two profiles are of different devices: /device:TPU:0 before, /device:TPU:3 now
where the time goes in v5:
time: 87.4 us; the launch traced here: 86.7 us
  starting transfers between devices  54.6 us (62%)
  waiting for transfers between devices  16.4 us (19%)
  Pallas kernels  7.88 us (9%)
  local copies, waits for them, and re-layouts  6.19 us (7%)
  other arithmetic  1.43 us (2%)
    ppermute x2, starting transfers between devices, change_lane(): return lax.ppermute(value, 'dom', pairs)  34.6 us
    ppermute x8, starting transfers between devices, send(): lax.ppermute(value, ('segment', 'dom'), every_device(pairs, segments * pa...  15.5 us
    ppermute x3, waiting for transfers between devices, to_chip(): return lax.ppermute(value, 'dom', pairs)  8.39 us
    pallas_call x7, Pallas kernels, call(): pl.pallas_call(kernel, out_shape=shapes, in_specs=[kinds[place] for place...  7.88 us
    ppermute x8, waiting for transfers between devices, send(): lax.ppermute(value, ('segment', 'dom'), every_device(pairs, segments * pa...  6.87 us
    ppermute x3, starting transfers between devices, to_chip(): return lax.ppermute(value, 'dom', pairs)  4.52 us
    unnamed x23, local copies, waits for them, and re-layouts  4.51 us
  transfers between devices with their start and end apart: 13, of which 8 were waited for; matrix products, arithmetic and copies ran while one was open for 4% of the time, Pallas kernels for 5%

profile of v5, /device:TPU:3, one launch (start us, length us, event | category | flops | bytes accessed | tf_op | source)
XLA Modules:
  0.0 86.7 jit_solution(11060929271069095537)
XLA Ops:
  0.0 0.7 collective-permute-start.4
  0.7 1.2 %collective-permute-start.6 = (bf16[1,1024,512]{2,1,0:T(8,128)(2,1)}, bf16[1,1024,512]{2,1,0:T(8,128)(2,1)}, u32[]{:S(2)}, u32[]{:S(2)}) collective-permute-start(bf16[1,1024,512]{2,1,0:T(8,128)(2,1)} %refs_2_.3), channel_id=1, source_target_pairs={{0,10},{1,17},{2,0},{3,19},{4,6},{5,21},{6,12},{7,23},{8,2},{9,25}... | collective-permute-start | bytes 3145736 | tf_op jit(solution)/shard_map/ppermute | solution.py:393
  1.9 1.8 %collective-permute-start.5 = (bf16[1,512,512]{2,1,0:T(8,128)(2,1)}, bf16[1,512,512]{2,1,0:T(8,128)(2,1)S(1)}, u32[]{:S(2)}, u32[]{:S(2)}) collective-permute-start(bf16[1,512,512]{2,1,0:T(8,128)(2,1)} %refs_1_.5), channel_id=1, source_target_pairs={{0,1},{1,0},{2,10},{3,19},{4,12},{5,21},{6,7},{7,6},{8,9},{9,8},{1... | collective-permute-start | bytes 1572872 | tf_op jit(solution)/shard_map/ppermute | solution.py:393
  3.7 1.6 %constant_dynamic-slice_fusion.1 = (bf16[1,128,227]{1,0,2:T(2,128)(2,1)S(1)}, bf16[1,128,227]{1,0,2:T(2,128)(2,1)S(1)}, bf16[1,128,227]{1,0,2:T(2,128)(2,1)S(1)}) fusion(bf16[4,128,227]{1,0,2:T(4,128)(2,1)} %param.12, s32[]{:T(128)S(6)} %select_n.67, s32[]{:T(128)S(6)} %select_n.62, s32[]{:T(128)S(6)} %select_n.68), kind=kLoop, calls=%fused_computation.8 | loop fusion | bytes 348684 | tf_op jit(solution)/shard_map/dynamic-slice.1
  5.4 0.7 pad_maximum_fusion.refs_0_
  6.0 0.5 add_clamp_fusion.chosen
  6.5 3.0 %encode.1 = (bf16[80,512]{1,0:T(8,128)(2,1)}, bf16[80,512]{1,0:T(8,128)(2,1)}, bf16[80,512]{1,0:T(8,128)(2,1)}, bf16[80,512]{1,0:T(8,128)(2,1)}) custom-call(s32[4]{0:T(128)} %add_clamp_fusion.chosen, bf16[227,256]{1,0:T(8,128)(2,1)} %pad_maximum_fusion.refs_0_, bf16[227,512]{1,0:T(8,128)(2,1)} %refs_1_.3, s32[1,128]{1,0:T(1,128)} %bitcast.31, ...), custom_call_target="tpu_custom_call" | custom-call | tf_op jit(solution)/shard_map/encode/pallas_call | solution.py:329
  9.5 0.4 collective-permute-start
  9.9 2.2 %collective-permute-start.1 = (bf16[80,512]{1,0:T(8,128)(2,1)}, bf16[80,512]{1,0:T(8,128)(2,1)S(1)}, u32[]{:S(2)}, u32[]{:S(2)}) collective-permute-start(bf16[80,512]{1,0:T(8,128)(2,1)} %get-tuple-element.17), channel_id=1, source_target_pairs={{0,4},{1,5},{2,6},{3,7},{4,0},{5,1},{6,2},{7,3},{8,12},{9,13},{10,... | collective-permute-start | bytes 245768 | tf_op jit(solution)/shard_map/ppermute | solution.py:397
  12.1 4.1 %collective-permute-done.refs_1_ = bf16[80,512]{1,0:T(8,128)(2,1)S(1)} collective-permute-done((bf16[80,512]{1,0:T(8,128)(2,1)}, bf16[80,512]{1,0:T(8,128)(2,1)S(1)}, u32[]{:S(2)}, u32[]{:S(2)}) %collective-permute-start) | collective-permute-done | bytes 81952 | tf_op jit(solution)/shard_map/ppermute | solution.py:397
  16.2 2.0 %collective-permute-start.2 = (bf16[80,512]{1,0:T(8,128)(2,1)}, bf16[80,512]{1,0:T(8,128)(2,1)S(1)}, u32[]{:S(2)}, u32[]{:S(2)}) collective-permute-start(bf16[80,512]{1,0:T(8,128)(2,1)} %get-tuple-element.18), channel_id=1, source_target_pairs={{0,6},{1,7},{2,4},{3,5},{4,2},{5,3},{6,0},{7,1},{8,14},{9,15},{10,... | collective-permute-start | bytes 245768 | tf_op jit(solution)/shard_map/ppermute | solution.py:397
  18.2 0.0 collective-permute-done.1.refs_2_
  18.2 4.3 %collective-permute-done.2.refs_3_ = bf16[80,512]{1,0:T(8,128)(2,1)S(1)} collective-permute-done((bf16[80,512]{1,0:T(8,128)(2,1)}, bf16[80,512]{1,0:T(8,128)(2,1)S(1)}, u32[]{:S(2)}, u32[]{:S(2)}) %collective-permute-start.2) | collective-permute-done | bytes 81952 | tf_op jit(solution)/shard_map/ppermute | solution.py:397
  22.4 0.9 %copy-done.3 = bf16[80,512]{1,0:T(8,128)(2,1)S(1)} copy-done((bf16[80,512]{1,0:T(8,128)(2,1)S(1)}, bf16[80,512]{1,0:T(8,128)(2,1)}, u32[]{:S(2)}) %copy-start.3) | copy-done | bytes 81944
  23.3 3.5 %collective-permute-start.3 = (bf16[320,512]{1,0:T(8,128)(2,1)S(1)}, bf16[320,512]{1,0:T(8,128)(2,1)S(1)}, u32[]{:S(2)}, u32[]{:S(2)}) collective-permute-start(bf16[320,512]{1,0:T(8,128)(2,1)S(1)} %join.1.refs_0_), channel_id=1, source_target_pairs={{0,1},{1,0},{2,3},{3,2},{4,5},{5,4},{6,7},{7,6},{8,9},{9,8},{10,11... | collective-permute-start | bytes 983048 | tf_op jit(solution)/shard_map/ppermute | solution.py:401
  26.8 0.1 pad_add_fusion.1.chip
  26.9 0.1 pad_add_fusion.2.where
  27.0 1.1 %collective-permute-done.3.refs_1_ = bf16[320,512]{1,0:T(8,128)(2,1)S(1)} collective-permute-done((bf16[320,512]{1,0:T(8,128)(2,1)S(1)}, bf16[320,512]{1,0:T(8,128)(2,1)S(1)}, u32[]{:S(2)}, u32[]{:S(2)}) %collective-permute-start.3) | collective-permute-done | bytes 327712 | tf_op jit(solution)/shard_map/ppermute | solution.py:401
  28.1 0.5 index.1
  28.6 0.0 collective-permute-done.5.refs_4_
  28.7 0.0 collective-permute-done.4.refs_3_
  28.7 0.0 collective-permute-done.6.refs_5_
  28.7 0.0 copy-start.5
  28.7 1.4 %copy-done.5 = bf16[1,1024,512]{2,1,0:T(8,128)(2,1)S(1)} copy-done((bf16[1,1024,512]{2,1,0:T(8,128)(2,1)S(1)}, bf16[1,1024,512]{2,1,0:T(8,128)(2,1)}, u32[]{:S(2)}) %copy-start.5) | copy-done | bytes 1048600
  30.1 1.6 %stage.2 = bf16[512,512]{1,0:T(8,128)(2,1)} custom-call(s32[2]{0:T(128)S(1)} %pad_add_fusion.2.where, s32[8,512]{1,0:T(8,128)S(1)} %get-tuple-element.19.index, bf16[512,512]{1,0:T(8,128)(2,1)S(1)} %get-tuple-element.20.state_in, bf16[1,512,1024]{2,1,0:T(8,128)(2,1)S(1)} %copy-done.4, bf16[1,512,512]{2,1,0:T(8,128)(2,1)S(1)} %copy-done.7, ...), custom_call_target="tpu_custom_call" | custom-call | flops 10000000000 | tf_op jit(solution)/shard_map/stage/pallas_call | solution.py:329
  31.7 0.0 copy-done.8
  31.7 0.4 collective-permute-start.7
  32.1 0.1 pad_add_fusion.where
  32.2 1.8 %collective-permute-done.7.state_in = bf16[512,512]{1,0:T(8,128)(2,1)} collective-permute-done((bf16[512,512]{1,0:T(8,128)(2,1)}, bf16[512,512]{1,0:T(8,128)(2,1)}, u32[]{:S(2)}, u32[]{:S(2)}) %collective-permute-start.7) | collective-permute-done | bytes 524320 | tf_op jit(solution)/shard_map/ppermute | solution.py:393
  34.0 1.0 %copy-done.9 = bf16[1,512,512]{2,1,0:T(8,128)(2,1)S(1)} copy-done((bf16[1,512,512]{2,1,0:T(8,128)(2,1)S(1)}, bf16[1,512,512]{2,1,0:T(8,128)(2,1)}, u32[]{:S(2)}) %copy-start.9) | copy-done | bytes 524312
  35.0 1.1 %stage.3 = bf16[512,512]{1,0:T(8,128)(2,1)S(1)} custom-call(s32[2]{0:T(128)S(1)} %pad_add_fusion.where, s32[8,512]{1,0:T(8,128)S(1)} %get-tuple-element.19.index, bf16[512,512]{1,0:T(8,128)(2,1)} %collective-permute-done.7.state_in, bf16[1,512,1024]{2,1,0:T(8,128)(2,1)S(1)} %copy-done.4, bf16[1,512,512]{2,1,0:T(8,128)(2,1)S(1)} %copy-done.7, ...), custom_call_target="tpu_custom_call" | custom-call | flops 10000000000 | tf_op jit(solution)/shard_map/stage/pallas_call | solution.py:329
  36.2 0.0 copy-start
  36.2 9.8 %collective-permute-start.10 = (bf16[128,512]{1,0:T(8,128)(2,1)S(1)}, bf16[128,512]{1,0:T(8,128)(2,1)S(1)}, u32[]{:S(2)}, u32[]{:S(2)}) collective-permute-start(bf16[128,512]{1,0:T(8,128)(2,1)S(1)} %get-tuple-element.22), channel_id=1, source_target_pairs={{0,8},{1,3},{2,20},{3,1},{4,6},{5,7},{6,4},{7,5},{8,0},{9,11},{10,... | collective-permute-start | bytes 393224 | tf_op jit(solution)/shard_map/ppermute | solution.py:393
  46.0 0.1 collective-permute-start.11
  46.1 1.4 %collective-permute-start.8 = (bf16[128,512]{1,0:T(8,128)(2,1)S(1)}, bf16[128,512]{1,0:T(8,128)(2,1)S(1)}, u32[]{:S(2)}, u32[]{:S(2)}) collective-permute-start(bf16[128,512]{1,0:T(8,128)(2,1)S(1)} %get-tuple-element.24), channel_id=1, source_target_pairs={{0,2},{1,3},{2,0},{3,1},{4,8},{5,7},{6,18},{7,5},{8,4},{9,11},{10,... | collective-permute-start | bytes 393224 | tf_op jit(solution)/shard_map/ppermute | solution.py:393
  47.5 0.1 collective-permute-start.9
  47.6 0.0 copy-start.2
  47.6 0.8 collective-permute-done.10
  48.4 1.5 %collective-permute-done.11 = bf16[128,512]{1,0:T(8,128)(2,1)S(1)} collective-permute-done((bf16[128,512]{1,0:T(8,128)(2,1)S(1)}, bf16[128,512]{1,0:T(8,128)(2,1)S(1)}, u32[]{:S(2)}, u32[]{:S(2)}) %collective-permute-start.11) | collective-permute-done | bytes 131104 | tf_op jit(solution)/shard_map/ppermute | solution.py:393
  49.8 1.4 %collective-permute-done.8 = bf16[128,512]{1,0:T(8,128)(2,1)S(1)} collective-permute-done((bf16[128,512]{1,0:T(8,128)(2,1)S(1)}, bf16[128,512]{1,0:T(8,128)(2,1)S(1)}, u32[]{:S(2)}, u32[]{:S(2)}) %collective-permute-start.8) | collective-permute-done | bytes 131104 | tf_op jit(solution)/shard_map/ppermute | solution.py:393
  51.3 1.4 %collective-permute-done.9 = bf16[128,512]{1,0:T(8,128)(2,1)S(1)} collective-permute-done((bf16[128,512]{1,0:T(8,128)(2,1)S(1)}, bf16[128,512]{1,0:T(8,128)(2,1)S(1)}, u32[]{:S(2)}, u32[]{:S(2)}) %collective-permute-start.9) | collective-permute-done | bytes 131104 | tf_op jit(solution)/shard_map/ppermute | solution.py:393
  52.7 31.1 %collective-permute-start.12 = (bf16[64,512]{1,0:T(8,128)(2,1)S(1)}, bf16[64,512]{1,0:T(8,128)(2,1)S(1)}, u32[]{:S(2)}, u32[]{:S(2)}) collective-permute-start(bf16[64,512]{1,0:T(8,128)(2,1)S(1)} %slice.24), channel_id=1, source_target_pairs={{0,1},{1,0},{2,3},{3,2},{4,5},{5,4},{6,7},{7,6},{8,9},{9,8},{10,11... | collective-permute-start | bytes 196616 | tf_op jit(solution)/shard_map/ppermute | solution.py:401
  83.8 0.0 copy-done
  83.9 0.6 copy-done.10
  84.5 0.4 prepare.1
  84.9 0.0 collective-permute-done.12.refs_1_
  84.9 0.5 copy-done.1
  85.4 1.2 %decode.1 = bf16[227,128]{1,0:T(8,128)(2,1)} custom-call(s32[1]{0:T(128)} %bitcast.turn, f32[128,512]{1,0:T(8,128)S(1)} %get-tuple-element.13.ready, bf16[64,128]{1,0:T(8,128)(2,1)S(1)} %get-tuple-element.14.table, bf16[1024,512]{1,0:T(8,128)(2,1)S(1)} %copy-done, bf16[227,512]{1,0:T(8,128)(2,1)S(1)} %bitcast.27, bf16[128,512]{1,0:T(8,128)(2,1)S(1)} %fusion.1.refs_0_, ...), custom_call_target="tpu_custom_call" | custom-call | tf_op jit(solution)/shard_map/decode/pallas_call | solution.py:329
  (18 shorter events, 0.1 us)
Async XLA Ops:
  0.0 28.7 %collective-permute-start.4 = (bf16[1,512,1024]{2,1,0:T(8,128)(2,1)}, bf16[1,512,1024]{2,1,0:T(8,128)(2,1)}, u32[]{:S(2)}, u32[]{:S(2)}) collective-permute-start(bf16[1,512,1024]{2,1,0:T(8,128)(2,1)} %refs_0_.3), channel_id=1, source_target_pairs={{0,1},{1,0},{2,10},{3,19},{4,12},{5,21},{6,7},{7,6},{8,9},{9,8},{1... | collective-permute-start | bytes 3145736 | tf_op jit(solution)/shard_map/ppermute | solution.py:393
  0.7 28.0 %collective-permute-start.6 = (bf16[1,1024,512]{2,1,0:T(8,128)(2,1)}, bf16[1,1024,512]{2,1,0:T(8,128)(2,1)}, u32[]{:S(2)}, u32[]{:S(2)}) collective-permute-start(bf16[1,1024,512]{2,1,0:T(8,128)(2,1)} %refs_2_.3), channel_id=1, source_target_pairs={{0,10},{1,17},{2,0},{3,19},{4,6},{5,21},{6,12},{7,23},{8,2},{9,25}... | collective-permute-start | bytes 3145736 | tf_op jit(solution)/shard_map/ppermute | solution.py:393
  1.9 26.7 %collective-permute-start.5 = (bf16[1,512,512]{2,1,0:T(8,128)(2,1)}, bf16[1,512,512]{2,1,0:T(8,128)(2,1)S(1)}, u32[]{:S(2)}, u32[]{:S(2)}) collective-permute-start(bf16[1,512,512]{2,1,0:T(8,128)(2,1)} %refs_1_.5), channel_id=1, source_target_pairs={{0,1},{1,0},{2,10},{3,19},{4,12},{5,21},{6,7},{7,6},{8,9},{9,8},{1... | collective-permute-start | bytes 1572872 | tf_op jit(solution)/shard_map/ppermute | solution.py:393
  3.7 25.0 %copy-start.4 = (bf16[1,512,1024]{2,1,0:T(8,128)(2,1)S(1)}, bf16[1,512,1024]{2,1,0:T(8,128)(2,1)}, u32[]{:S(2)}) copy-start(bf16[1,512,1024]{2,1,0:T(8,128)(2,1)} %refs_0_.3) | copy-start | bytes 3145732
  9.5 6.7 %collective-permute-start = (bf16[80,512]{1,0:T(8,128)(2,1)}, bf16[80,512]{1,0:T(8,128)(2,1)S(1)}, u32[]{:S(2)}, u32[]{:S(2)}) collective-permute-start(bf16[80,512]{1,0:T(8,128)(2,1)} %get-tuple-element.16), channel_id=1, source_target_pairs={{0,2},{1,3},{2,0},{3,1},{4,6},{5,7},{6,4},{7,5},{8,10},{9,11},{10,... | collective-permute-start | bytes 245768 | tf_op jit(solution)/shard_map/ppermute | solution.py:397
  9.9 8.3 %collective-permute-start.1 = (bf16[80,512]{1,0:T(8,128)(2,1)}, bf16[80,512]{1,0:T(8,128)(2,1)S(1)}, u32[]{:S(2)}, u32[]{:S(2)}) collective-permute-start(bf16[80,512]{1,0:T(8,128)(2,1)} %get-tuple-element.17), channel_id=1, source_target_pairs={{0,4},{1,5},{2,6},{3,7},{4,0},{5,1},{6,2},{7,3},{8,12},{9,13},{10,... | collective-permute-start | bytes 245768 | tf_op jit(solution)/shard_map/ppermute | solution.py:397
  16.2 6.2 %collective-permute-start.2 = (bf16[80,512]{1,0:T(8,128)(2,1)}, bf16[80,512]{1,0:T(8,128)(2,1)S(1)}, u32[]{:S(2)}, u32[]{:S(2)}) collective-permute-start(bf16[80,512]{1,0:T(8,128)(2,1)} %get-tuple-element.18), channel_id=1, source_target_pairs={{0,6},{1,7},{2,4},{3,5},{4,2},{5,3},{6,0},{7,1},{8,14},{9,15},{10,... | collective-permute-start | bytes 245768 | tf_op jit(solution)/shard_map/ppermute | solution.py:397
  22.4 0.9 %copy-start.3 = (bf16[80,512]{1,0:T(8,128)(2,1)S(1)}, bf16[80,512]{1,0:T(8,128)(2,1)}, u32[]{:S(2)}) copy-start(bf16[80,512]{1,0:T(8,128)(2,1)} %get-tuple-element.15.refs_0_) | copy-start | bytes 245764
  23.3 5.4 %copy-start.7 = (bf16[1,512,512]{2,1,0:T(8,128)(2,1)S(1)}, bf16[1,512,512]{2,1,0:T(8,128)(2,1)}, u32[]{:S(2)}) copy-start(bf16[1,512,512]{2,1,0:T(8,128)(2,1)} %refs_1_.5) | copy-start | bytes 1572868
  23.3 4.7 %collective-permute-start.3 = (bf16[320,512]{1,0:T(8,128)(2,1)S(1)}, bf16[320,512]{1,0:T(8,128)(2,1)S(1)}, u32[]{:S(2)}, u32[]{:S(2)}) collective-permute-start(bf16[320,512]{1,0:T(8,128)(2,1)S(1)} %join.1.refs_0_), channel_id=1, source_target_pairs={{0,1},{1,0},{2,3},{3,2},{4,5},{5,4},{6,7},{7,6},{8,9},{9,8},{10,11... | collective-permute-start | bytes 983048 | tf_op jit(solution)/shard_map/ppermute | solution.py:401
  28.6 3.0 %copy-start.8 = (bf16[1,512,512]{2,1,0:T(8,128)(2,1)}, bf16[1,512,512]{2,1,0:T(8,128)(2,1)S(1)}, u32[]{:S(2)}) copy-start(bf16[1,512,512]{2,1,0:T(8,128)(2,1)S(1)} %collective-permute-done.5.refs_4_) | copy-start | bytes 1572868
  28.7 1.4 %copy-start.5 = (bf16[1,1024,512]{2,1,0:T(8,128)(2,1)S(1)}, bf16[1,1024,512]{2,1,0:T(8,128)(2,1)}, u32[]{:S(2)}) copy-start(bf16[1,1024,512]{2,1,0:T(8,128)(2,1)} %refs_2_.3) | copy-start | bytes 3145732
  30.1 3.9 %copy-start.6 = (bf16[1,1024,512]{2,1,0:T(8,128)(2,1)S(1)}, bf16[1,1024,512]{2,1,0:T(8,128)(2,1)}, u32[]{:S(2)}) copy-start(bf16[1,1024,512]{2,1,0:T(8,128)(2,1)} %refs_2_.3) | copy-start | bytes 3145732
  31.7 2.3 %collective-permute-start.7 = (bf16[512,512]{1,0:T(8,128)(2,1)}, bf16[512,512]{1,0:T(8,128)(2,1)}, u32[]{:S(2)}, u32[]{:S(2)}) collective-permute-start(bf16[512,512]{1,0:T(8,128)(2,1)} %stage.2), channel_id=1, source_target_pairs={{0,1},{1,0},{2,18},{3,5},{4,20},{5,3},{6,7},{7,6},{8,9},{9,8},{10,... | collective-permute-start | bytes 1572872 | tf_op jit(solution)/shard_map/ppermute | solution.py:393
  34.0 1.0 %copy-start.9 = (bf16[1,512,512]{2,1,0:T(8,128)(2,1)S(1)}, bf16[1,512,512]{2,1,0:T(8,128)(2,1)}, u32[]{:S(2)}) copy-start(bf16[1,512,512]{2,1,0:T(8,128)(2,1)} %copy-done.8) | copy-start | bytes 1572868
  36.2 47.7 %copy-start = (bf16[1024,512]{1,0:T(8,128)(2,1)S(1)}, bf16[1024,512]{1,0:T(8,128)(2,1)}, u32[]{:S(2)}) copy-start(bf16[1024,512]{1,0:T(8,128)(2,1)} %w_decode.3) | copy-start | bytes 3145732
  36.2 12.2 %collective-permute-start.10 = (bf16[128,512]{1,0:T(8,128)(2,1)S(1)}, bf16[128,512]{1,0:T(8,128)(2,1)S(1)}, u32[]{:S(2)}, u32[]{:S(2)}) collective-permute-start(bf16[128,512]{1,0:T(8,128)(2,1)S(1)} %get-tuple-element.22), channel_id=1, source_target_pairs={{0,8},{1,3},{2,20},{3,1},{4,6},{5,7},{6,4},{7,5},{8,0},{9,11},{10,... | collective-permute-start | bytes 393224 | tf_op jit(solution)/shard_map/ppermute | solution.py:393
  46.0 3.8 %collective-permute-start.11 = (bf16[128,512]{1,0:T(8,128)(2,1)S(1)}, bf16[128,512]{1,0:T(8,128)(2,1)S(1)}, u32[]{:S(2)}, u32[]{:S(2)}) collective-permute-start(bf16[128,512]{1,0:T(8,128)(2,1)S(1)} %get-tuple-element.21), channel_id=1, source_target_pairs={{0,18},{1,3},{2,4},{3,1},{4,2},{5,7},{6,10},{7,5},{8,26},{9,11},{1... | collective-permute-start | bytes 393224 | tf_op jit(solution)/shard_map/ppermute | solution.py:393
  46.1 5.1 %collective-permute-start.8 = (bf16[128,512]{1,0:T(8,128)(2,1)S(1)}, bf16[128,512]{1,0:T(8,128)(2,1)S(1)}, u32[]{:S(2)}, u32[]{:S(2)}) collective-permute-start(bf16[128,512]{1,0:T(8,128)(2,1)S(1)} %get-tuple-element.24), channel_id=1, source_target_pairs={{0,2},{1,3},{2,0},{3,1},{4,8},{5,7},{6,18},{7,5},{8,4},{9,11},{10,... | collective-permute-start | bytes 393224 | tf_op jit(solution)/shard_map/ppermute | solution.py:393
  47.5 5.2 %collective-permute-start.9 = (bf16[128,512]{1,0:T(8,128)(2,1)S(1)}, bf16[128,512]{1,0:T(8,128)(2,1)S(1)}, u32[]{:S(2)}, u32[]{:S(2)}) collective-permute-start(bf16[128,512]{1,0:T(8,128)(2,1)S(1)} %get-tuple-element.23), channel_id=1, source_target_pairs={{0,2},{1,3},{2,0},{3,1},{4,18},{5,7},{6,14},{7,5},{8,10},{9,11},{1... | collective-permute-start | bytes 393224 | tf_op jit(solution)/shard_map/ppermute | solution.py:393
  47.6 36.3 %copy-start.2 = (bf16[227,512]{1,0:T(8,128)(2,1)S(1)}, bf16[227,512]{1,0:T(8,128)(2,1)}, u32[]{:S(2)}) copy-start(bf16[227,512]{1,0:T(8,128)(2,1)} %refs_1_.3) | copy-start | bytes 697348
  52.7 32.2 %collective-permute-start.12 = (bf16[64,512]{1,0:T(8,128)(2,1)S(1)}, bf16[64,512]{1,0:T(8,128)(2,1)S(1)}, u32[]{:S(2)}, u32[]{:S(2)}) collective-permute-start(bf16[64,512]{1,0:T(8,128)(2,1)S(1)} %slice.24), channel_id=1, source_target_pairs={{0,1},{1,0},{2,3},{3,2},{4,5},{5,4},{6,7},{7,6},{8,9},{9,8},{10,11... | collective-permute-start | bytes 196616 | tf_op jit(solution)/shard_map/ppermute | solution.py:401
  83.8 0.7 copy-start.10
  84.5 0.9 %copy-start.1 = (bf16[512,227]{0,1:T(8,128)(2,1)S(1)}, bf16[512,227]{0,1:T(8,128)(2,1)}, u32[]{:S(2)}) copy-start(bf16[512,227]{0,1:T(8,128)(2,1)} %param.18) | copy-start | bytes 697348

commit v6 on v4

--- a/solution.py
+++ b/solution.py
@@ -175,29 +175,27 @@
     return copies
 
 
-def encode_kernel(samples, first, *refs):
-    inputs, payloads = refs[:6], refs[6 : 6 + samples]
-    held, latent, semaphores = refs[6 + samples : 12 + samples], refs[12 + samples], refs[13 + samples]
-    copies = fetch(inputs, held, semaphores)
-    for copy in copies:
-        copy.wait()
-    snapshots, w_embed, grid_mesh, neighbors, send_rows, counts = held
-    mesh_rows = neighbors.shape[1]
-    fanout = neighbors.shape[0]
-    grid_rows = snapshots.shape[1] // samples
-    lists, halo_rows = send_rows.shape
+def encode_kernel(mesh_rows, fanout, lists, chip, snapshots, w_embed, packed, *refs):
+    payloads, latent = refs[:-1], refs[-1]
+    neighbors = packed[:fanout, :mesh_rows]
+    grid_rows = snapshots.shape[2]
+    grid_mesh = packed[fanout + lists : fanout + lists + 1, :grid_rows]
+    counts = packed[fanout + lists + 1 : fanout + lists + 2, :lists]
     width = w_embed.shape[1]
-    latent[...] = silu_by_tanh(matmul_tn(snapshots[...], w_embed[...])).astype(jnp.bfloat16)
-    table = lax.broadcasted_iota(jnp.int32, (mesh_rows, grid_rows), 0) == grid_mesh[...]
+    for place in range(snapshots.shape[0]):
+        found = silu_by_tanh(matmul_tn(snapshots[place], w_embed[...])).astype(jnp.bfloat16)
+        latent[place * grid_rows : (place + 1) * grid_rows, :] = found
+    table = lax.broadcasted_iota(jnp.int32, (mesh_rows, grid_rows), 0) == grid_mesh
     table = jnp.where(table, 1.0, 0.0).astype(jnp.bfloat16)
-    near = neighbors[...]
-    block = near // mesh_rows
-    row = near - block * mesh_rows
+    block = neighbors // mesh_rows
+    row = neighbors - block * mesh_rows
+    halo_rows = mesh_rows
     position = lax.broadcasted_iota(jnp.int32, (1, halo_rows), 1)
     rows = []
     for list_index in range(lists):
-        kept = position < counts[list_index]
-        rows.append(jnp.where(kept, send_rows[list_index : list_index + 1, :], mesh_rows))
+        kept = position < counts[:, list_index : list_index + 1]
+        listed = packed[fanout + list_index : fanout + list_index + 1, :halo_rows]
+        rows.append(jnp.where(kept, listed, mesh_rows))
     rows.append(jnp.zeros((fanout - lists, halo_rows), jnp.int32))
     filler = jnp.zeros((fanout, 128 - mesh_rows), jnp.int32)
     pieces = [block, filler, row, filler, jnp.concatenate(rows, axis=0), filler]
@@ -205,8 +203,7 @@
     coded = jnp.concatenate([coded, jnp.zeros_like(coded)], axis=0)
     coded = coded.astype(jnp.float32).astype(jnp.bfloat16)
     for turn, payload in enumerate(payloads):
-        sample = lax.rem(first[0] + turn, samples)
-        start = pl.multiple_of(sample * grid_rows, grid_rows)
+        start = pl.multiple_of(jnp.bitwise_xor(chip[0], turn) * grid_rows, grid_rows)
         pooled = matmul(table, latent[pl.ds(start, grid_rows), :])
         payload[:mesh_rows, :] = rms_scale(pooled).astype(jnp.bfloat16)
         payload[mesh_rows:, :] = coded
@@ -219,22 +216,25 @@
         joined[place * rows : (place + 1) * rows, :] = payload[...]
 
 
-def index_kernel(parts, mesh_rows, active, *refs):
-    lanes, (index_out, state_out) = refs[:-2], refs[-2:]
-    fanout = index_out.shape[0]
+def index_kernel(parts, mesh_rows, chip, active, *refs):
+    lanes, (columns_out, low, high), index_out = refs[:-4], refs[-4:-1], refs[-1]
+    nodes = columns_out.shape[0]
     group = len(lanes)
-    owners = parts // group
-    rows = lanes[0].shape[0] // owners
+    rows = lanes[0].shape[0] // (parts // group)
 
     @pl.when(active[0] == 1)
     def _():
         tables = []
         for part in range(parts):
-            lane, turn = lanes[part % group], (-(part // group)) % owners
-            base = turn * rows
-            state_out[part * mesh_rows : (part + 1) * mesh_rows, :] = lane[base : base + mesh_rows, :]
-            coded = lane[base + mesh_rows : base + rows, :384].astype(jnp.float32).astype(jnp.int32)
-            tables.append(coded[:fanout])
+            lane, turn = lanes[part % group], jnp.bitwise_xor(chip[0], part // group)
+            base = pl.multiple_of(turn * rows, 16)
+            half, spot = (low, part) if part < parts // 2 else (high, part - parts // 2)
+            half[spot * mesh_rows : (spot + 1) * mesh_rows, :] = lane[pl.ds(base, mesh_rows), :]
+            base = pl.multiple_of(turn * rows + mesh_rows, 16)
+            coded = lane[pl.ds(base, rows - mesh_rows), :384].astype(jnp.float32).astype(jnp.int32)
+            tables.append(coded[: coded.shape[0] // 2])
+        fanout = tables[0].shape[0]
+        index_out[fanout:, :] = jnp.zeros((index_out.shape[0] - fanout, nodes), jnp.int32)
         for part in range(parts):
             block = tables[part][:, :128]
             row = tables[part][:, 128:256]
@@ -246,36 +246,64 @@
                 picked = jnp.take_along_axis(lists, row, axis=1)
                 picked = jnp.where(picked == mesh_rows, parts * mesh_rows, source * mesh_rows + picked)
                 found = jnp.where(block == list_index + 1, picked, found)
-            index_out[:, part * mesh_rows : (part + 1) * mesh_rows] = found[:, :mesh_rows]
-
-
-def layer_kernel(active, index, state_in, w_project, w_message, w_update, state_out):
-    nodes, width = state_in.shape
-    fanout = index.shape[0]
-    chunk = min(256, nodes)
+            index_out[:fanout, part * mesh_rows : (part + 1) * mesh_rows] = found[:, :mesh_rows]
+        columns_out[...] = jnp.transpose(index_out[...].astype(jnp.float32))
+
+
+def hold_kernel(*refs):
+    half = len(refs) // 2
+    for copy in fetch(refs[:half], refs[half:-1], refs[-1]):
+        copy.wait()
+
+
+def renew(fanout, columns, sender, own, w_project, w_message, w_update):
+    chunk, width = own.shape
+    nodes = sender.shape[0]
+    names = lax.broadcasted_iota(jnp.int32, (chunk, nodes), 1).astype(jnp.float32)
+    receiver = matmul(own, w_project[0, :, :width])
+    total = jnp.zeros((chunk, width), jnp.float32)
+    for k in range(fanout):
+        hit = columns[:, k : k + 1] == names
+        fetched = matmul(jnp.where(hit, 1.0, 0.0).astype(jnp.bfloat16), sender)
+        edge = silu_by_tanh(receiver + fetched).astype(jnp.bfloat16)
+        total = total + edge.astype(jnp.float32)
+    gathered = (total * (1.0 / fanout)).astype(jnp.bfloat16)
+    aggregate = matmul(gathered, w_message[0]).astype(jnp.bfloat16)
+    update = silu_by_tanh(
+        matmul(own, w_update[0, :width, :]) + matmul(aggregate, w_update[0, width:, :])
+    )
+    return (own.astype(jnp.float32) + rms_scale(update)).astype(jnp.bfloat16)
+
+
+def sender_kernel(active, low, w_project, sender_low):
+    width = low.shape[1]
 
     @pl.when(active[0] == 1)
     def _():
-        columns = jnp.concatenate([index[...], jnp.zeros((128 - fanout, nodes), jnp.int32)], axis=0)
-        columns = jnp.transpose(columns.astype(jnp.float32))
-        names = lax.broadcasted_iota(jnp.int32, (chunk, nodes), 1).astype(jnp.float32)
-        sender = matmul(state_in[...], w_project[0, :, width:]).astype(jnp.bfloat16)
-        for start in range(0, nodes, chunk):
-            own = state_in[start : start + chunk, :]
-            receiver = matmul(own, w_project[0, :, :width])
-            total = jnp.zeros((chunk, width), jnp.float32)
-            for k in range(fanout):
-                hit = columns[start : start + chunk, k : k + 1] == names
-                fetched = matmul(jnp.where(hit, 1.0, 0.0).astype(jnp.bfloat16), sender)
-                edge = silu_by_tanh(receiver + fetched).astype(jnp.bfloat16)
-                total = total + edge.astype(jnp.float32)
-            gathered = (total * (1.0 / fanout)).astype(jnp.bfloat16)
-            aggregate = matmul(gathered, w_message[0]).astype(jnp.bfloat16)
-            update = silu_by_tanh(
-                matmul(own, w_update[0, :width, :]) + matmul(aggregate, w_update[0, width:, :])
-            )
-            renewed = own.astype(jnp.float32) + rms_scale(update)
-            state_out[start : start + chunk, :] = renewed.astype(jnp.bfloat16)
+        sender_low[...] = matmul(low[...], w_project[0, :, width:]).astype(jnp.bfloat16)
+
+
+def low_kernel(fanout, active, columns, sender_low, low, high, w_project, w_message, w_update, *outs):
+    sender, new_low = outs
+    half, width = low.shape
+
+    @pl.when(active[0] == 1)
+    def _():
+        sender[:half, :] = sender_low[...]
+        sender[half:, :] = matmul(high[...], w_project[0, :, width:]).astype(jnp.bfloat16)
+        new_low[...] = renew(
+            fanout, columns[:half, :], sender[...], low[...], w_project, w_message, w_update
+        )
+
+
+def high_kernel(fanout, active, columns, sender, high, w_project, w_message, w_update, new_high):
+    half = high.shape[0]
+
+    @pl.when(active[0] == 1)
+    def _():
+        new_high[...] = renew(
+            fanout, columns[half:, :], sender[...], high[...], w_project, w_message, w_update
+        )
 
 
 def prepare_kernel(snapshot, w_embed, w_decode, mesh_grid, ready, table_out):
@@ -314,26 +342,19 @@
     )(*inputs)
 
 
-def every_device(pairs, count, kind):
+def every_device(pairs, count, group):
     onward = dict(pairs)
     reached = set(onward.values())
-    for first in range(count):
-        if first in reached or first not in onward:
-            continue
+    for first in [source for source in onward if source not in reached]:
         last = first
         while last in onward:
             last = onward[last]
-        onward[last] = first
-    rest = sorted((other for other in range(count) if other not in onward), key=lambda at: (kind(at), at))
-    if len(rest) % 2:
-        alone = rest.pop()
-        if rest:
-            one, two = rest.pop(), rest.pop()
-            onward.update({one: two, two: alone, alone: one})
-        else:
-            onward[alone] = alone
-    for one, two in zip(rest[::2], rest[1::2]):
-        onward.update({one: two, two: one})
+        onward.update({last: last + group - 1, last + group - 1: first + group - 1, first + group - 1: first})
+    reached = set(onward.values())
+    for at in range(0, count, group):
+        givers = [lane for lane in range(at, at + group) if lane not in onward]
+        takers = [lane for lane in range(at, at + group) if lane not in reached]
+        onward.update(zip(givers, takers[1:] + takers[:1]))
     return sorted(onward.items())
 
 
@@ -365,45 +386,57 @@
     def device(at_segment, at_dom):
         return at_segment * parts + at_dom % parts
 
-    def send(value, pairs, kind=lambda at: 0):
-        return lax.ppermute(value, ("segment", "dom"), every_device(pairs, segments * parts, kind))
-
-    def rotate(value, steps):
-        return lax.ppermute(value, "dom", [(at, (at + steps) % parts) for at in range(parts)])
+    def send(value, pairs):
+        return lax.ppermute(value, ("segment", "dom"), every_device(pairs, segments * parts, group))
+
+    def to_chip(value, steps):
+        pairs = [(at, (at // group ^ steps) * group + at % group) for at in range(parts)]
+        return lax.ppermute(value, "dom", pairs)
 
     def change_lane(value, steps):
         pairs = [(at, at - at % group + (at + steps) % group) for at in range(parts)]
         return lax.ppermute(value, "dom", pairs)
 
-    is_owner = (place % group == 0).astype(jnp.int32).reshape(1)
-
-    def active(at_segment):
-        return ((segment == at_segment) & (place % group == 0)).astype(jnp.int32).reshape(1)
-
-    by_channel = jnp.transpose(grid_state, (2, 0, 1))
-    inputs = [
-        by_channel.reshape(channels, samples * grid_rows),
-        w_embed,
-        grid_mesh.reshape(1, grid_rows),
-        neighbors.T,
-        send_rows,
-        halo_count.reshape(-1),
-    ]
+    def owner(m, at_segment):
+        return device(at_segment, m * group)
+
+    chip, lane = place // group, place % group
+    weights = [w_project, w_message, w_update]
+    last = segments - 2
+    pairs = [(owner(m, last + 1), owner(m, last)) for m in range(samples)]
+    came_weights = [send(weight, pairs) for weight in weights]
+    snapshots = jnp.transpose(grid_state, (0, 2, 1))
+    lists = send_rows.shape[0]
+
+    def rows_of(value):
+        return jnp.pad(value, ((0, 0), (0, 128 - value.shape[1])))
+
+    packed = jnp.concatenate(
+        [
+            rows_of(neighbors.T),
+            rows_of(send_rows),
+            rows_of(grid_mesh.reshape(1, grid_rows)),
+            rows_of(halo_count.reshape(1, lists)),
+        ],
+        axis=0,
+    )
     payloads = call(
-        functools.partial(encode_kernel, samples),
+        functools.partial(encode_kernel, mesh_rows, fanout, lists),
         "encode",
         [jax.ShapeDtypeStruct((mesh_rows + 2 * fanout, width), bf16)] * samples,
-        [(place // group).reshape(1)] + inputs,
-        "shhhhhh",
-        [pltpu.VMEM(value.shape, value.dtype) for value in inputs[:-1]]
-        + [
-            pltpu.SMEM(inputs[-1].shape, jnp.int32),
-            pltpu.VMEM((samples * grid_rows, width), bf16),
-            pltpu.SemaphoreType.DMA((6,)),
-        ],
-        room=60,
-    )
-    arrived = [payloads[0]] + [rotate(payloads[turn], turn * group) for turn in range(1, samples)]
+        [chip.reshape(1), snapshots, w_embed, packed],
+        "svvv",
+        [pltpu.VMEM((samples * grid_rows, width), bf16)],
+    )
+    held = call(
+        hold_kernel,
+        "hold",
+        [jax.ShapeDtypeStruct(weight.shape, bf16) for weight in weights],
+        weights,
+        "hhh",
+        [pltpu.SemaphoreType.DMA((3,))],
+    )
+    arrived = [payloads[0]] + [to_chip(payloads[turn], turn) for turn in range(1, samples)]
     (joined,) = call(
         join_kernel,
         "join",
@@ -412,30 +445,50 @@
         "v" * samples,
     )
     lanes = [joined] + [change_lane(joined, -steps) for steps in range(1, group)]
-    index, state = call(
+    half = nodes // 2
+    columns, low, high = call(
         functools.partial(index_kernel, parts, mesh_rows),
         "index",
-        [jax.ShapeDtypeStruct((fanout, nodes), jnp.int32), jax.ShapeDtypeStruct((nodes, width), bf16)],
-        [is_owner] + lanes,
-        "s" + "v" * group,
-    )
-    weights = [w_project, w_message, w_update]
-    for at_segment in range(segments):
-        (state,) = call(
-            layer_kernel,
-            "layer",
-            [jax.ShapeDtypeStruct((nodes, width), bf16)],
-            [active(at_segment), index, state] + weights,
-            "svvvvv",
-            flops=10**10,
-        )
-        if at_segment + 1 < segments:
-            pairs = [
-                (device(at_segment, m * group), device(at_segment + 1, m * group)) for m in range(samples)
-            ]
-            state = send(state, pairs, lambda at: at % group > 0)
-        if at_segment == 0:
-            snapshot = lax.dynamic_index_in_dim(by_channel, segment, 1, keepdims=False)
+        [
+            jax.ShapeDtypeStruct((nodes, 128), jnp.float32),
+            jax.ShapeDtypeStruct((half, width), bf16),
+            jax.ShapeDtypeStruct((half, width), bf16),
+        ],
+        [chip.reshape(1), (lane == 0).astype(jnp.int32).reshape(1)] + lanes,
+        "ss" + "v" * group,
+        [pltpu.VMEM((128, nodes), jnp.int32)],
+    )
+    state_shape = jax.ShapeDtypeStruct((half, width), bf16)
+    for layer in range(segments):
+        at_segment = min(layer, last)
+        active = ((segment == at_segment) & (lane == 0)).astype(jnp.int32).reshape(1)
+        used = list(held) if layer <= last else came_weights
+        (sender_low,) = call(sender_kernel, "sender", [state_shape], [active, low, used[0]], "svv")
+        sender, new_low = call(
+            functools.partial(low_kernel, fanout),
+            "low",
+            [jax.ShapeDtypeStruct((nodes, width), bf16), state_shape],
+            [active, columns, sender_low, low, high] + used,
+            "svvvvvvv",
+        )
+        pairs = [(owner(m, layer), owner(m, layer + 1)) for m in range(samples)]
+        if layer < last:
+            low = send(new_low, pairs)
+        else:
+            low = new_low
+        (new_high,) = call(
+            functools.partial(high_kernel, fanout),
+            "high",
+            [state_shape],
+            [active, columns, sender, high] + used,
+            "svvvvvv",
+        )
+        if layer < last:
+            high = send(new_high, pairs)
+        else:
+            high = new_high
+        if layer == 0:
+            snapshot = lax.dynamic_index_in_dim(snapshots, segment, 0, keepdims=False)
             ready, table = call(
                 prepare_kernel,
                 "prepare",
@@ -445,31 +498,24 @@
                 ],
                 [snapshot, w_embed, w_decode, mesh_grid.reshape(1, grid_rows)],
                 "vvvv",
-                flops=10**9,
-            )
-    own_turn = (place // group - segment) % samples
+                    )
+            low, ready, table = lax.optimization_barrier((low, ready, table))
     share = group * mesh_rows
     blocks = []
     for turn in range(samples):
-        pairs = [
-            (device(segments - 1, m * group), device(m, (m + turn) * group)) for m in range(samples)
-        ]
-
-        def kind(at, turn=turn):
-            at_segment, at_dom = divmod(at, parts)
-            if at_dom % group:
-                return samples
-            own = (at_dom // group - at_segment) % samples
-            return 0 if own > turn else 1
-
+        pairs = [(owner(m, last), device(m, turn * group)) for m in range(samples)]
+        kept = [source for source, target in pairs if source == target]
         pairs = [(source, target) for source, target in pairs if source != target]
-        block = state[turn * share : (turn + 1) * share]
-        blocks.append(send(block, pairs, kind))
-    last_owner = (segment == segments - 1) & (place == (samples - 1) * group)
-    blocks[0] = jnp.where(last_owner, state[:share], blocks[0])
+        part = low if turn < samples // 2 else high
+        start = turn % (samples // 2) * share
+        block = part[start : start + share]
+        came = send(block, pairs)
+        for at in kept:
+            came = jnp.where(segment * parts + place == at, block, came)
+        blocks.append(came)
     block = blocks[0]
     for turn in range(1, samples):
-        block = jnp.where(own_turn == turn, blocks[turn], block)
+        block = jnp.where(chip == turn, blocks[turn], block)
     handed = [block]
     for steps in range(1, group):
         handed.append(change_lane(block[steps * mesh_rows : (steps + 1) * mesh_rows], steps))
@@ -477,7 +523,7 @@
         decode_kernel,
         "decode",
         [jax.ShapeDtypeStruct((channels, grid_rows), bf16)],
-        [(place % group).reshape(1), ready, table, w_decode, w_output.T] + handed,
+        [lane.reshape(1), ready, table, w_decode, w_output.T] + handed,
         "svvvv" + "v" * group,
         [pltpu.VMEM((mesh_rows, width), bf16)],
     )
@@ -486,7 +532,7 @@
 
 def fits(mesh):
     segments, parts = mesh.shape["segment"], mesh.shape["dom"]
-    return parts % segments == 0 and parts <= 16
+    return segments == 4 and parts % segments == 0 and parts <= 16
 
 
 def solution(mesh):

time: 90.2 us -> 82 us (0.909)
  the two profiles are of different devices: /device:TPU:0 before, /device:TPU:5 now
where the time goes in v6:
time: 82 us; the launch traced here: 81.3 us
  starting transfers between devices  42.7 us (52%)
  Pallas kernels  16.6 us (20%)
  waiting for transfers between devices  13.7 us (17%)
  local copies, waits for them, and re-layouts  7.93 us (10%)
    ppermute x11, starting transfers between devices, send(): lax.ppermute(value, ('segment', 'dom'), every_device(pairs, segments * pa...  32.7 us
    pallas_call x18, Pallas kernels, call(): pl.pallas_call(kernel, out_shape=shapes, in_specs=[kinds[place] for place...  16.6 us
    unnamed x31, local copies, waits for them, and re-layouts  7.06 us
    ppermute x11, waiting for transfers between devices, send(): lax.ppermute(value, ('segment', 'dom'), every_device(pairs, segments * pa...  7.05 us
    ppermute x2, starting transfers between devices, change_lane(): return lax.ppermute(value, 'dom', pairs)  6.38 us
    ppermute x3, waiting for transfers between devices, to_chip(): return lax.ppermute(value, 'dom', pairs)  5.75 us
    ppermute x3, starting transfers between devices, to_chip(): return lax.ppermute(value, 'dom', pairs)  3.71 us
  transfers between devices with their start and end apart: 16, of which 7 were waited for; matrix products, arithmetic and copies ran while one was open for 2% of the time, Pallas kernels for 15%

profile of v6, /device:TPU:5, one launch (start us, length us, event | category | flops | bytes accessed | tf_op | source)
XLA Modules:
  0.0 81.3 jit_solution(5668263983447217045)
XLA Ops:
  0.0 1.2 %collective-permute-start.8 = (bf16[1,512,1024]{2,1,0:T(8,128)(2,1)}, bf16[1,512,1024]{2,1,0:T(8,128)(2,1)}, u32[]{:S(2)}, u32[]{:S(2)}) collective-permute-start(bf16[1,512,1024]{2,1,0:T(8,128)(2,1)} %refs_0_.1), channel_id=1, source_target_pairs={{0,1},{1,0},{2,3},{3,2},{4,5},{5,4},{6,7},{7,6},{8,9},{9,8},{10,11... | collective-permute-start | bytes 3145736 | tf_op jit(solution)/shard_map/ppermute | solution.py:390
  1.2 0.7 collective-permute-start.10
  1.9 1.0 %copy.17 = bf16[4,128,227]{1,2,0:T(8,128)(2,1)S(1)} copy(bf16[4,128,227]{1,0,2:T(4,128)(2,1)} %param.12) | data formatting | bytes 464896 | tf_op args[0]
  2.9 0.0 copy-start.11
  2.9 0.0 copy-start.12
  3.0 0.7 copy-done.11
  3.7 0.0 copy-done.12
  3.7 0.7 encode.1
  4.5 1.4 %collective-permute-start = (bf16[80,512]{1,0:T(8,128)(2,1)S(1)}, bf16[80,512]{1,0:T(8,128)(2,1)S(1)}, u32[]{:S(2)}, u32[]{:S(2)}) collective-permute-start(bf16[80,512]{1,0:T(8,128)(2,1)S(1)} %get-tuple-element.29), channel_id=1, source_target_pairs={{0,2},{1,3},{2,0},{3,1},{4,6},{5,7},{6,4},{7,5},{8,10},{9,11},{10,... | collective-permute-start | bytes 245768 | tf_op jit(solution)/shard_map/ppermute | solution.py:394
  5.8 2.3 %collective-permute-start.1 = (bf16[80,512]{1,0:T(8,128)(2,1)S(1)}, bf16[80,512]{1,0:T(8,128)(2,1)S(1)}, u32[]{:S(2)}, u32[]{:S(2)}) collective-permute-start(bf16[80,512]{1,0:T(8,128)(2,1)S(1)} %get-tuple-element.30), channel_id=1, source_target_pairs={{0,4},{1,5},{2,6},{3,7},{4,0},{5,1},{6,2},{7,3},{8,12},{9,13},{10,... | collective-permute-start | bytes 245768 | tf_op jit(solution)/shard_map/ppermute | solution.py:394
  8.2 0.6 collective-permute-done.refs_1_
  8.8 2.0 %collective-permute-done.1.refs_2_ = bf16[80,512]{1,0:T(8,128)(2,1)S(1)} collective-permute-done((bf16[80,512]{1,0:T(8,128)(2,1)S(1)}, bf16[80,512]{1,0:T(8,128)(2,1)S(1)}, u32[]{:S(2)}, u32[]{:S(2)}) %collective-permute-start.1) | collective-permute-done | bytes 81952 | tf_op jit(solution)/shard_map/ppermute | solution.py:394
  10.8 3.2 %collective-permute-done.2.refs_3_ = bf16[80,512]{1,0:T(8,128)(2,1)S(1)} collective-permute-done((bf16[80,512]{1,0:T(8,128)(2,1)S(1)}, bf16[80,512]{1,0:T(8,128)(2,1)S(1)}, u32[]{:S(2)}, u32[]{:S(2)}) %collective-permute-start.2) | collective-permute-done | bytes 81952 | tf_op jit(solution)/shard_map/ppermute | solution.py:394
  14.0 1.8 %collective-permute-start.3 = (bf16[320,512]{1,0:T(8,128)(2,1)S(1)}, bf16[320,512]{1,0:T(8,128)(2,1)S(1)}, u32[]{:S(2)}, u32[]{:S(2)}) collective-permute-start(bf16[320,512]{1,0:T(8,128)(2,1)S(1)} %join.1.refs_0_), channel_id=1, source_target_pairs={{0,1},{1,0},{2,3},{3,2},{4,5},{5,4},{6,7},{7,6},{8,9},{9,8},{10,11... | collective-permute-start | bytes 983048 | tf_op jit(solution)/shard_map/ppermute | solution.py:398
  15.7 1.2 %copy-done.3 = bf16[1,512,1024]{2,1,0:T(8,128)(2,1)S(1)} copy-done((bf16[1,512,1024]{2,1,0:T(8,128)(2,1)S(1)}, bf16[1,512,1024]{2,1,0:T(8,128)(2,1)}, u32[]{:S(2)}) %copy-start.3) | copy-done | bytes 1048600
  17.0 1.2 %copy-done.4 = bf16[1,1024,512]{2,1,0:T(8,128)(2,1)S(1)} copy-done((bf16[1,1024,512]{2,1,0:T(8,128)(2,1)S(1)}, bf16[1,1024,512]{2,1,0:T(8,128)(2,1)}, u32[]{:S(2)}) %copy-start.4) | copy-done | bytes 1048600
  18.2 1.1 %hold.1 = (bf16[1,512,1024]{2,1,0:T(8,128)(2,1)S(1)}, bf16[1,512,512]{2,1,0:T(8,128)(2,1)S(1)}, bf16[1,1024,512]{2,1,0:T(8,128)(2,1)S(1)}) custom-call(bf16[1,512,1024]{2,1,0:T(8,128)(2,1)S(1)} %copy-done.3, bf16[1,512,512]{2,1,0:T(8,128)(2,1)} %refs_1_.1, bf16[1,1024,512]{2,1,0:T(8,128)(2,1)S(1)} %copy-done.4), custom_call_target="tpu_custom_call" | custom-call | tf_op jit(solution)/shard_map/hold/pallas_call | solution.py:333
  19.4 0.7 low.4
  20.1 0.4 collective-permute-start.4
  20.5 0.7 high.4
  21.2 0.1 collective-permute-start.5
  21.3 0.6 collective-permute-start.9
  21.9 0.8 %dynamic-slice_bitcast_fusion.snapshot = bf16[227,128]{1,0:T(8,128)(2,1)S(1)} fusion(bf16[4,128,227]{1,2,0:T(8,128)(2,1)} %copy-done.2, s32[]{:T(128)S(6)} %select_n.43), kind=kLoop, calls=%fused_computation.1 | loop fusion | bytes 116228 | tf_op jit(solution)/shard_map/jit(dynamic_index_in_dim)/squeeze | solution.py:491
  22.7 0.7 copy-done.10
  23.4 1.2 %copy-done = bf16[1024,512]{1,0:T(8,128)(2,1)S(1)} copy-done((bf16[1024,512]{1,0:T(8,128)(2,1)S(1)}, bf16[1024,512]{1,0:T(8,128)(2,1)}, u32[]{:S(2)}) %copy-start) | copy-done | bytes 1048600
  24.6 0.9 %copy-done.6 = bf16[227,512]{1,0:T(8,128)(2,1)S(1)} copy-done((bf16[227,512]{1,0:T(8,128)(2,1)S(1)}, bf16[227,512]{1,0:T(8,128)(2,1)}, u32[]{:S(2)}) %copy-start.6) | copy-done | bytes 232472
  25.5 0.4 prepare.1
  26.0 1.0 %sender.5.sender_low = bf16[256,512]{1,0:T(8,128)(2,1)S(1)} custom-call(s32[1]{0:T(128)} %bitcast.13.active, bf16[256,512]{1,0:T(8,128)(2,1)} %collective-permute-done.4.low, bf16[1,512,1024]{2,1,0:T(8,128)(2,1)S(1)} %get-tuple-element.34.w_project), custom_call_target="tpu_custom_call" | custom-call | tf_op jit(solution)/shard_map/sender/pallas_call | solution.py:333
  27.0 1.7 %low.5 = (bf16[512,512]{1,0:T(8,128)(2,1)S(1)}, bf16[256,512]{1,0:T(8,128)(2,1)}) custom-call(s32[1]{0:T(128)} %bitcast.13.active, f32[512,128]{1,0:T(8,128)S(1)} %get-tuple-element.32.columns, bf16[256,512]{1,0:T(8,128)(2,1)S(1)} %sender.5.sender_low, bf16[256,512]{1,0:T(8,128)(2,1)} %collective-permute-done.4.low, ...), custom_call_target="tpu_custom_call" | custom-call | tf_op jit(solution)/shard_map/low/pallas_call | solution.py:333
  28.8 3.1 %collective-permute-start.6 = (bf16[256,512]{1,0:T(8,128)(2,1)}, bf16[256,512]{1,0:T(8,128)(2,1)}, u32[]{:S(2)}, u32[]{:S(2)}) collective-permute-start(bf16[256,512]{1,0:T(8,128)(2,1)} %get-tuple-element.45), channel_id=1, source_target_pairs={{0,1},{1,0},{2,3},{3,2},{4,5},{5,4},{6,7},{7,6},{8,16},{9,8},{10,1... | collective-permute-start | bytes 786440 | tf_op jit(solution)/shard_map/ppermute | solution.py:390
  31.9 1.6 %high.5 = bf16[256,512]{1,0:T(8,128)(2,1)} custom-call(s32[1]{0:T(128)} %bitcast.13.active, f32[512,128]{1,0:T(8,128)S(1)} %get-tuple-element.32.columns, bf16[512,512]{1,0:T(8,128)(2,1)S(1)} %get-tuple-element.46.sender, bf16[256,512]{1,0:T(8,128)(2,1)} %collective-permute-done.5.high, bf16[1,512,1024]{2,1,0:T(8,128)(2,1)S(1)} %get-tuple-element.34.w_project, ...), custom_call_target="tpu_custom_call" | custom-call | tf_op jit(solution)/shard_map/high/pallas_call | solution.py:333
  33.5 5.6 %collective-permute-start.7 = (bf16[256,512]{1,0:T(8,128)(2,1)}, bf16[256,512]{1,0:T(8,128)(2,1)}, u32[]{:S(2)}, u32[]{:S(2)}) collective-permute-start(bf16[256,512]{1,0:T(8,128)(2,1)} %high.5), channel_id=1, source_target_pairs={{0,1},{1,0},{2,3},{3,2},{4,5},{5,4},{6,7},{7,6},{8,16},{9,8},{10,1... | collective-permute-start | bytes 786440 | tf_op jit(solution)/shard_map/ppermute | solution.py:390
  39.1 1.0 %sender.6.sender_low = bf16[256,512]{1,0:T(8,128)(2,1)S(1)} custom-call(s32[1]{0:T(128)} %bitcast.12.active, bf16[256,512]{1,0:T(8,128)(2,1)} %collective-permute-done.6.low, bf16[1,512,1024]{2,1,0:T(8,128)(2,1)S(1)} %get-tuple-element.34.w_project), custom_call_target="tpu_custom_call" | custom-call | tf_op jit(solution)/shard_map/sender/pallas_call | solution.py:333
  40.1 2.7 %collective-permute-done.7.high = bf16[256,512]{1,0:T(8,128)(2,1)} collective-permute-done((bf16[256,512]{1,0:T(8,128)(2,1)}, bf16[256,512]{1,0:T(8,128)(2,1)}, u32[]{:S(2)}, u32[]{:S(2)}) %collective-permute-start.7) | collective-permute-done | bytes 262176 | tf_op jit(solution)/shard_map/ppermute | solution.py:390
  42.8 1.0 %low.6 = (bf16[512,512]{1,0:T(8,128)(2,1)S(1)}, bf16[256,512]{1,0:T(8,128)(2,1)S(1)}) custom-call(s32[1]{0:T(128)} %bitcast.12.active, f32[512,128]{1,0:T(8,128)S(1)} %get-tuple-element.32.columns, bf16[256,512]{1,0:T(8,128)(2,1)S(1)} %sender.6.sender_low, bf16[256,512]{1,0:T(8,128)(2,1)} %collective-permute-done.6.low, ...), custom_call_target="tpu_custom_call" | custom-call | tf_op jit(solution)/shard_map/low/pallas_call | solution.py:333
  43.8 0.9 %high.6 = bf16[256,512]{1,0:T(8,128)(2,1)S(1)} custom-call(s32[1]{0:T(128)} %bitcast.12.active, f32[512,128]{1,0:T(8,128)S(1)} %get-tuple-element.32.columns, bf16[512,512]{1,0:T(8,128)(2,1)S(1)} %get-tuple-element.48.sender, bf16[256,512]{1,0:T(8,128)(2,1)} %collective-permute-done.7.high, bf16[1,512,1024]{2,1,0:T(8,128)(2,1)S(1)} %get-tuple-element.34.w_project, ...), custom_call_target="tpu_custom_call" | custom-call | tf_op jit(solution)/shard_map/high/pallas_call | solution.py:333
  44.7 1.2 %sender.7.sender_low = bf16[256,512]{1,0:T(8,128)(2,1)S(1)} custom-call(s32[1]{0:T(128)} %bitcast.12.active, bf16[256,512]{1,0:T(8,128)(2,1)S(1)} %get-tuple-element.47.low, bf16[1,512,1024]{2,1,0:T(8,128)(2,1)} %collective-permute-done.8.w_project), custom_call_target="tpu_custom_call" | custom-call | tf_op jit(solution)/shard_map/sender/pallas_call | solution.py:333
  46.0 1.5 %low.7 = (bf16[512,512]{1,0:T(8,128)(2,1)S(1)}, bf16[256,512]{1,0:T(8,128)(2,1)S(1)}) custom-call(s32[1]{0:T(128)} %bitcast.12.active, f32[512,128]{1,0:T(8,128)S(1)} %get-tuple-element.32.columns, bf16[256,512]{1,0:T(8,128)(2,1)S(1)} %sender.7.sender_low, bf16[256,512]{1,0:T(8,128)(2,1)S(1)} %get-tuple-element.47.low, bf16[256,512]{1,0:T(8,128)(2,1)S(1)} %high.6, ...), custom_call_target="tpu_custom_call" | custom-call | tf_op jit(solution)/shard_map/low/pallas_call | solution.py:333
  47.5 1.5 %high.7 = bf16[256,512]{1,0:T(8,128)(2,1)S(1)} custom-call(s32[1]{0:T(128)} %bitcast.12.active, f32[512,128]{1,0:T(8,128)S(1)} %get-tuple-element.32.columns, bf16[512,512]{1,0:T(8,128)(2,1)S(1)} %get-tuple-element.49.sender, bf16[256,512]{1,0:T(8,128)(2,1)S(1)} %high.6, bf16[1,512,1024]{2,1,0:T(8,128)(2,1)} %collective-permute-done.8.w_project, ...), custom_call_target="tpu_custom_call" | custom-call | tf_op jit(solution)/shard_map/high/pallas_call | solution.py:333
  49.1 18.3 %collective-permute-start.11 = (bf16[128,512]{1,0:T(8,128)(2,1)S(1)}, bf16[128,512]{1,0:T(8,128)(2,1)S(1)}, u32[]{:S(2)}, u32[]{:S(2)}) collective-permute-start(bf16[128,512]{1,0:T(8,128)(2,1)S(1)} %get-tuple-element.52), channel_id=1, source_target_pairs={{0,1},{1,0},{2,3},{3,2},{4,5},{5,4},{6,7},{7,17},{8,9},{9,8},{10,1... | collective-permute-start | bytes 393224 | tf_op jit(solution)/shard_map/ppermute | solution.py:390
  67.4 0.1 collective-permute-start.12
  67.5 1.9 %collective-permute-start.13 = (bf16[128,512]{1,0:T(8,128)(2,1)S(1)}, bf16[128,512]{1,0:T(8,128)(2,1)S(1)}, u32[]{:S(2)}, u32[]{:S(2)}) collective-permute-start(bf16[128,512]{1,0:T(8,128)(2,1)S(1)} %get-tuple-element.54), channel_id=1, source_target_pairs={{0,1},{1,0},{2,3},{3,17},{4,5},{5,4},{6,7},{7,6},{8,9},{9,8},{10,1... | collective-permute-start | bytes 393224 | tf_op jit(solution)/shard_map/ppermute | solution.py:390
  69.4 0.7 collective-permute-start.14
  70.1 3.0 %collective-permute-done.12 = bf16[128,512]{1,0:T(8,128)(2,1)S(1)} collective-permute-done((bf16[128,512]{1,0:T(8,128)(2,1)S(1)}, bf16[128,512]{1,0:T(8,128)(2,1)S(1)}, u32[]{:S(2)}, u32[]{:S(2)}) %collective-permute-start.12) | collective-permute-done | bytes 131104 | tf_op jit(solution)/shard_map/ppermute | solution.py:390
  73.1 1.4 %collective-permute-done.13 = bf16[128,512]{1,0:T(8,128)(2,1)S(1)} collective-permute-done((bf16[128,512]{1,0:T(8,128)(2,1)S(1)}, bf16[128,512]{1,0:T(8,128)(2,1)S(1)}, u32[]{:S(2)}, u32[]{:S(2)}) %collective-permute-start.13) | collective-permute-done | bytes 131104 | tf_op jit(solution)/shard_map/ppermute | solution.py:390
  74.5 4.6 %collective-permute-start.15 = (bf16[64,512]{1,0:T(8,128)(2,1)S(1)}, bf16[64,512]{1,0:T(8,128)(2,1)S(1)}, u32[]{:S(2)}, u32[]{:S(2)}) collective-permute-start(bf16[64,512]{1,0:T(8,128)(2,1)S(1)} %slice.22), channel_id=1, source_target_pairs={{0,1},{1,0},{2,3},{3,2},{4,5},{5,4},{6,7},{7,6},{8,9},{9,8},{10,11... | collective-permute-start | bytes 196616 | tf_op jit(solution)/shard_map/ppermute | solution.py:398
  79.1 0.9 %collective-permute-done.15.refs_1_ = bf16[64,512]{1,0:T(8,128)(2,1)S(1)} collective-permute-done((bf16[64,512]{1,0:T(8,128)(2,1)S(1)}, bf16[64,512]{1,0:T(8,128)(2,1)S(1)}, u32[]{:S(2)}, u32[]{:S(2)}) %collective-permute-start.15) | collective-permute-done | bytes 65568 | tf_op jit(solution)/shard_map/ppermute | solution.py:398
  80.0 1.2 %decode.1 = bf16[227,128]{1,0:T(8,128)(2,1)} custom-call(s32[1]{0:T(128)} %bitcast.turn, f32[128,512]{1,0:T(8,128)S(1)} %copy-done.8, bf16[64,128]{1,0:T(8,128)(2,1)S(1)} %get-tuple-element.42.table, bf16[1024,512]{1,0:T(8,128)(2,1)S(1)} %copy-done.1, bf16[227,512]{1,0:T(8,128)(2,1)S(1)} %bitcast.21, bf16[128,512]{1,0:T(8,128)(2,1)S(1)} %select_select_fusion.refs_0_, ...), custom_call_target="tpu_custom_call" | custom-call | tf_op jit(solution)/shard_map/decode/pallas_call | solution.py:333
  (39 shorter events, 0.2 us)
Async XLA Ops:
  0.0 44.7 %collective-permute-start.8 = (bf16[1,512,1024]{2,1,0:T(8,128)(2,1)}, bf16[1,512,1024]{2,1,0:T(8,128)(2,1)}, u32[]{:S(2)}, u32[]{:S(2)}) collective-permute-start(bf16[1,512,1024]{2,1,0:T(8,128)(2,1)} %refs_0_.1), channel_id=1, source_target_pairs={{0,1},{1,0},{2,3},{3,2},{4,5},{5,4},{6,7},{7,6},{8,9},{9,8},{10,11... | collective-permute-start | bytes 3145736 | tf_op jit(solution)/shard_map/ppermute | solution.py:390
  1.2 44.8 %collective-permute-start.10 = (bf16[1,1024,512]{2,1,0:T(8,128)(2,1)}, bf16[1,1024,512]{2,1,0:T(8,128)(2,1)}, u32[]{:S(2)}, u32[]{:S(2)}) collective-permute-start(bf16[1,1024,512]{2,1,0:T(8,128)(2,1)} %refs_2_.1), channel_id=1, source_target_pairs={{0,1},{1,0},{2,3},{3,2},{4,5},{5,4},{6,7},{7,6},{8,9},{9,8},{10,11... | collective-permute-start | bytes 3145736 | tf_op jit(solution)/shard_map/ppermute | solution.py:390
  1.9 1.8 %copy-start.5 = (bf16[227,512]{1,0:T(8,128)(2,1)S(1)}, bf16[227,512]{1,0:T(8,128)(2,1)}, u32[]{:S(2)}) copy-start(bf16[227,512]{1,0:T(8,128)(2,1)} %w_embed.3) | copy-start | bytes 697348
  2.9 1.6 %copy-start.2 = (bf16[4,128,227]{1,2,0:T(8,128)(2,1)}, bf16[4,128,227]{1,2,0:T(8,128)(2,1)S(1)}, u32[]{:S(2)}) copy-start(bf16[4,128,227]{1,2,0:T(8,128)(2,1)S(1)} %copy.17) | copy-start | bytes 697348
  2.9 0.7 copy-start.11
  2.9 0.8 copy-start.12
  3.0 0.8 copy-start.13
  3.0 0.8 copy-start.14
  4.5 4.3 %collective-permute-start = (bf16[80,512]{1,0:T(8,128)(2,1)S(1)}, bf16[80,512]{1,0:T(8,128)(2,1)S(1)}, u32[]{:S(2)}, u32[]{:S(2)}) collective-permute-start(bf16[80,512]{1,0:T(8,128)(2,1)S(1)} %get-tuple-element.29), channel_id=1, source_target_pairs={{0,2},{1,3},{2,0},{3,1},{4,6},{5,7},{6,4},{7,5},{8,10},{9,11},{10,... | collective-permute-start | bytes 245768 | tf_op jit(solution)/shard_map/ppermute | solution.py:394
  5.8 4.9 %collective-permute-start.1 = (bf16[80,512]{1,0:T(8,128)(2,1)S(1)}, bf16[80,512]{1,0:T(8,128)(2,1)S(1)}, u32[]{:S(2)}, u32[]{:S(2)}) collective-permute-start(bf16[80,512]{1,0:T(8,128)(2,1)S(1)} %get-tuple-element.30), channel_id=1, source_target_pairs={{0,4},{1,5},{2,6},{3,7},{4,0},{5,1},{6,2},{7,3},{8,12},{9,13},{10,... | collective-permute-start | bytes 245768 | tf_op jit(solution)/shard_map/ppermute | solution.py:394
  8.2 5.8 %collective-permute-start.2 = (bf16[80,512]{1,0:T(8,128)(2,1)S(1)}, bf16[80,512]{1,0:T(8,128)(2,1)S(1)}, u32[]{:S(2)}, u32[]{:S(2)}) collective-permute-start(bf16[80,512]{1,0:T(8,128)(2,1)S(1)} %get-tuple-element.31), channel_id=1, source_target_pairs={{0,6},{1,7},{2,4},{3,5},{4,2},{5,3},{6,0},{7,1},{8,14},{9,15},{10,... | collective-permute-start | bytes 245768 | tf_op jit(solution)/shard_map/ppermute | solution.py:394
  14.0 5.4 %collective-permute-start.3 = (bf16[320,512]{1,0:T(8,128)(2,1)S(1)}, bf16[320,512]{1,0:T(8,128)(2,1)S(1)}, u32[]{:S(2)}, u32[]{:S(2)}) collective-permute-start(bf16[320,512]{1,0:T(8,128)(2,1)S(1)} %join.1.refs_0_), channel_id=1, source_target_pairs={{0,1},{1,0},{2,3},{3,2},{4,5},{5,4},{6,7},{7,6},{8,9},{9,8},{10,11... | collective-permute-start | bytes 983048 | tf_op jit(solution)/shard_map/ppermute | solution.py:398
  15.7 1.2 %copy-start.3 = (bf16[1,512,1024]{2,1,0:T(8,128)(2,1)S(1)}, bf16[1,512,1024]{2,1,0:T(8,128)(2,1)}, u32[]{:S(2)}) copy-start(bf16[1,512,1024]{2,1,0:T(8,128)(2,1)} %refs_0_.1) | copy-start | bytes 3145732
  17.0 1.2 %copy-start.4 = (bf16[1,1024,512]{2,1,0:T(8,128)(2,1)S(1)}, bf16[1,1024,512]{2,1,0:T(8,128)(2,1)}, u32[]{:S(2)}) copy-start(bf16[1,1024,512]{2,1,0:T(8,128)(2,1)} %refs_2_.1) | copy-start | bytes 3145732
  20.1 5.8 %collective-permute-start.4 = (bf16[256,512]{1,0:T(8,128)(2,1)}, bf16[256,512]{1,0:T(8,128)(2,1)}, u32[]{:S(2)}, u32[]{:S(2)}) collective-permute-start(bf16[256,512]{1,0:T(8,128)(2,1)} %get-tuple-element.38), channel_id=1, source_target_pairs={{0,8},{1,0},{2,10},{3,2},{4,12},{5,4},{6,14},{7,6},{8,9},{9,1},{10... | collective-permute-start | bytes 786440 | tf_op jit(solution)/shard_map/ppermute | solution.py:390
  21.2 5.8 %collective-permute-start.5 = (bf16[256,512]{1,0:T(8,128)(2,1)}, bf16[256,512]{1,0:T(8,128)(2,1)}, u32[]{:S(2)}, u32[]{:S(2)}) collective-permute-start(bf16[256,512]{1,0:T(8,128)(2,1)} %high.4), channel_id=1, source_target_pairs={{0,8},{1,0},{2,10},{3,2},{4,12},{5,4},{6,14},{7,6},{8,9},{9,1},{10... | collective-permute-start | bytes 786440 | tf_op jit(solution)/shard_map/ppermute | solution.py:390
  21.3 24.7 %collective-permute-start.9 = (bf16[1,512,512]{2,1,0:T(8,128)(2,1)}, bf16[1,512,512]{2,1,0:T(8,128)(2,1)S(1)}, u32[]{:S(2)}, u32[]{:S(2)}) collective-permute-start(bf16[1,512,512]{2,1,0:T(8,128)(2,1)} %refs_1_.1), channel_id=1, source_target_pairs={{0,1},{1,0},{2,3},{3,2},{4,5},{5,4},{6,7},{7,6},{8,9},{9,8},{10,11... | collective-permute-start | bytes 1572872 | tf_op jit(solution)/shard_map/ppermute | solution.py:390
  22.7 0.7 copy-start.10
  23.4 1.2 %copy-start = (bf16[1024,512]{1,0:T(8,128)(2,1)S(1)}, bf16[1024,512]{1,0:T(8,128)(2,1)}, u32[]{:S(2)}) copy-start(bf16[1024,512]{1,0:T(8,128)(2,1)} %w_decode.3) | copy-start | bytes 3145732
  24.6 0.9 %copy-start.6 = (bf16[227,512]{1,0:T(8,128)(2,1)S(1)}, bf16[227,512]{1,0:T(8,128)(2,1)}, u32[]{:S(2)}) copy-start(bf16[227,512]{1,0:T(8,128)(2,1)} %w_embed.3) | copy-start | bytes 697348
  25.9 1.1 %copy-start.7 = (f32[128,512]{1,0:T(8,128)}, f32[128,512]{1,0:T(8,128)S(1)}, u32[]{:S(2)}) copy-start(f32[128,512]{1,0:T(8,128)S(1)} %get-tuple-element.41.ready) | copy-start | bytes 786436
  28.8 10.4 %collective-permute-start.6 = (bf16[256,512]{1,0:T(8,128)(2,1)}, bf16[256,512]{1,0:T(8,128)(2,1)}, u32[]{:S(2)}, u32[]{:S(2)}) collective-permute-start(bf16[256,512]{1,0:T(8,128)(2,1)} %get-tuple-element.45), channel_id=1, source_target_pairs={{0,1},{1,0},{2,3},{3,2},{4,5},{5,4},{6,7},{7,6},{8,16},{9,8},{10,1... | collective-permute-start | bytes 786440 | tf_op jit(solution)/shard_map/ppermute | solution.py:390
  33.5 9.2 %collective-permute-start.7 = (bf16[256,512]{1,0:T(8,128)(2,1)}, bf16[256,512]{1,0:T(8,128)(2,1)}, u32[]{:S(2)}, u32[]{:S(2)}) collective-permute-start(bf16[256,512]{1,0:T(8,128)(2,1)} %high.5), channel_id=1, source_target_pairs={{0,1},{1,0},{2,3},{3,2},{4,5},{5,4},{6,7},{7,6},{8,16},{9,8},{10,1... | collective-permute-start | bytes 786440 | tf_op jit(solution)/shard_map/ppermute | solution.py:390
  49.1 31.0 %copy-start.1 = (bf16[1024,512]{1,0:T(8,128)(2,1)S(1)}, bf16[1024,512]{1,0:T(8,128)(2,1)}, u32[]{:S(2)}) copy-start(bf16[1024,512]{1,0:T(8,128)(2,1)} %w_decode.3) | copy-start | bytes 3145732
  49.1 21.0 %collective-permute-start.11 = (bf16[128,512]{1,0:T(8,128)(2,1)S(1)}, bf16[128,512]{1,0:T(8,128)(2,1)S(1)}, u32[]{:S(2)}, u32[]{:S(2)}) collective-permute-start(bf16[128,512]{1,0:T(8,128)(2,1)S(1)} %get-tuple-element.52), channel_id=1, source_target_pairs={{0,1},{1,0},{2,3},{3,2},{4,5},{5,4},{6,7},{7,17},{8,9},{9,8},{10,1... | collective-permute-start | bytes 393224 | tf_op jit(solution)/shard_map/ppermute | solution.py:390
  67.4 5.7 %collective-permute-start.12 = (bf16[128,512]{1,0:T(8,128)(2,1)S(1)}, bf16[128,512]{1,0:T(8,128)(2,1)S(1)}, u32[]{:S(2)}, u32[]{:S(2)}) collective-permute-start(bf16[128,512]{1,0:T(8,128)(2,1)S(1)} %get-tuple-element.51), channel_id=1, source_target_pairs={{0,1},{1,0},{2,3},{3,2},{4,5},{5,17},{6,7},{7,6},{8,9},{9,8},{10,1... | collective-permute-start | bytes 393224 | tf_op jit(solution)/shard_map/ppermute | solution.py:390
  67.5 7.0 %collective-permute-start.13 = (bf16[128,512]{1,0:T(8,128)(2,1)S(1)}, bf16[128,512]{1,0:T(8,128)(2,1)S(1)}, u32[]{:S(2)}, u32[]{:S(2)}) collective-permute-start(bf16[128,512]{1,0:T(8,128)(2,1)S(1)} %get-tuple-element.54), channel_id=1, source_target_pairs={{0,1},{1,0},{2,3},{3,17},{4,5},{5,4},{6,7},{7,6},{8,9},{9,8},{10,1... | collective-permute-start | bytes 393224 | tf_op jit(solution)/shard_map/ppermute | solution.py:390
  69.4 5.1 %collective-permute-start.14 = (bf16[128,512]{1,0:T(8,128)(2,1)S(1)}, bf16[128,512]{1,0:T(8,128)(2,1)S(1)}, u32[]{:S(2)}, u32[]{:S(2)}) collective-permute-start(bf16[128,512]{1,0:T(8,128)(2,1)S(1)} %get-tuple-element.53), channel_id=1, source_target_pairs={{0,1},{1,21},{2,3},{3,2},{4,5},{5,4},{6,7},{7,6},{8,9},{9,19},{10,... | collective-permute-start | bytes 393224 | tf_op jit(solution)/shard_map/ppermute | solution.py:390
  74.5 5.6 %copy-start.8 = (f32[128,512]{1,0:T(8,128)S(1)}, f32[128,512]{1,0:T(8,128)}, u32[]{:S(2)}) copy-start(f32[128,512]{1,0:T(8,128)} %copy-done.7) | copy-start | bytes 786436
  74.5 5.6 %copy-start.9 = (bf16[512,227]{0,1:T(8,128)(2,1)S(1)}, bf16[512,227]{0,1:T(8,128)(2,1)}, u32[]{:S(2)}) copy-start(bf16[512,227]{0,1:T(8,128)(2,1)} %param.18) | copy-start | bytes 697348
  74.5 5.5 %collective-permute-start.15 = (bf16[64,512]{1,0:T(8,128)(2,1)S(1)}, bf16[64,512]{1,0:T(8,128)(2,1)S(1)}, u32[]{:S(2)}, u32[]{:S(2)}) collective-permute-start(bf16[64,512]{1,0:T(8,128)(2,1)S(1)} %slice.22), channel_id=1, source_target_pairs={{0,1},{1,0},{2,3},{3,2},{4,5},{5,4},{6,7},{7,6},{8,9},{9,8},{10,11... | collective-permute-start | bytes 196616 | tf_op jit(solution)/shard_map/ppermute | solution.py:398

commit v7 on v6

--- a/solution.py
+++ b/solution.py
@@ -275,6 +275,12 @@
     return (own.astype(jnp.float32) + rms_scale(update)).astype(jnp.bfloat16)
 
 
+def write_pieces(pieces, value):
+    rows = pieces[0].shape[0]
+    for place, piece in enumerate(pieces):
+        piece[...] = value[place * rows : (place + 1) * rows]
+
+
 def sender_kernel(active, low, w_project, sender_low):
     width = low.shape[1]
 
@@ -284,30 +290,33 @@
 
 
 def low_kernel(fanout, active, columns, sender_low, low, high, w_project, w_message, w_update, *outs):
-    sender, new_low = outs
+    sender, new_low = outs[0], outs[1:]
     half, width = low.shape
 
     @pl.when(active[0] == 1)
     def _():
         sender[:half, :] = sender_low[...]
         sender[half:, :] = matmul(high[...], w_project[0, :, width:]).astype(jnp.bfloat16)
-        new_low[...] = renew(
-            fanout, columns[:half, :], sender[...], low[...], w_project, w_message, w_update
-        )
-
-
-def high_kernel(fanout, active, columns, sender, high, w_project, w_message, w_update, new_high):
+        write_pieces(
+            new_low,
+            renew(fanout, columns[:half, :], sender[...], low[...], w_project, w_message, w_update),
+        )
+
+
+def high_kernel(fanout, active, columns, sender, high, w_project, w_message, w_update, *new_high):
     half = high.shape[0]
 
     @pl.when(active[0] == 1)
     def _():
-        new_high[...] = renew(
-            fanout, columns[half:, :], sender[...], high[...], w_project, w_message, w_update
-        )
-
-
-def prepare_kernel(snapshot, w_embed, w_decode, mesh_grid, ready, table_out):
-    latent = silu_by_tanh(matmul_tn(snapshot[...], w_embed[...])).astype(jnp.bfloat16)
+        write_pieces(
+            new_high,
+            renew(fanout, columns[half:, :], sender[...], high[...], w_project, w_message, w_update),
+        )
+
+
+def prepare_kernel(segment, snapshots, w_embed, w_decode, mesh_grid, ready, table_out):
+    snapshot = snapshots[segment[0]]
+    latent = silu_by_tanh(matmul_tn(snapshot, w_embed[...])).astype(jnp.bfloat16)
     ready[...] = matmul(latent, w_decode[: latent.shape[1], :])
     mesh_rows, grid_rows = table_out.shape
     table = lax.broadcasted_iota(jnp.int32, (mesh_rows, grid_rows), 0) == mesh_grid[...]
@@ -330,6 +339,7 @@
 
 def call(kernel, name, shapes, inputs, places, scratch=(), room=16, flops=0):
     kinds = {"s": SMEM, "v": VMEM, "h": HBM}
+    moved = sum(value.size * value.dtype.itemsize for value in list(inputs) + list(shapes))
     return pl.pallas_call(
         kernel,
         out_shape=shapes,
@@ -338,7 +348,7 @@
         scratch_shapes=list(scratch),
         name=name,
         compiler_params=pltpu.CompilerParams(vmem_limit_bytes=room * 1024 * 1024),
-        cost_estimate=pl.CostEstimate(flops=flops, bytes_accessed=0, transcendentals=0),
+        cost_estimate=pl.CostEstimate(flops=flops, bytes_accessed=moved, transcendentals=0),
     )(*inputs)
 
 
@@ -350,11 +360,18 @@
         while last in onward:
             last = onward[last]
         onward.update({last: last + group - 1, last + group - 1: first + group - 1, first + group - 1: first})
-    reached = set(onward.values())
+    alone = []
     for at in range(0, count, group):
-        givers = [lane for lane in range(at, at + group) if lane not in onward]
-        takers = [lane for lane in range(at, at + group) if lane not in reached]
-        onward.update(zip(givers, takers[1:] + takers[:1]))
+        rest = [lane for lane in range(at, at + group) if lane not in onward]
+        if len(rest) > 1:
+            onward.update(zip(rest, rest[1:] + rest[:1]))
+        else:
+            alone += rest
+    if len(alone) == 1:
+        before = next(at for at in onward if at % group and onward[at] % group == 0)
+        onward.update({before: alone[0], alone[0]: onward[before]})
+    else:
+        onward.update(zip(alone, alone[1:] + alone[:1]))
     return sorted(onward.items())
 
 
@@ -436,7 +453,8 @@
         "hhh",
         [pltpu.SemaphoreType.DMA((3,))],
     )
-    arrived = [payloads[0]] + [to_chip(payloads[turn], turn) for turn in range(1, samples)]
+    own_payload, *held = lax.optimization_barrier((payloads[0], *held))
+    arrived = [own_payload] + [to_chip(payloads[turn], turn) for turn in range(1, samples)]
     (joined,) = call(
         join_kernel,
         "join",
@@ -446,6 +464,7 @@
     )
     lanes = [joined] + [change_lane(joined, -steps) for steps in range(1, group)]
     half = nodes // 2
+    share = group * mesh_rows
     columns, low, high = call(
         functools.partial(index_kernel, parts, mesh_rows),
         "index",
@@ -464,31 +483,33 @@
         active = ((segment == at_segment) & (lane == 0)).astype(jnp.int32).reshape(1)
         used = list(held) if layer <= last else came_weights
         (sender_low,) = call(sender_kernel, "sender", [state_shape], [active, low, used[0]], "svv")
-        sender, new_low = call(
+        pieces = [state_shape]
+        if layer > last:
+            pieces = [jax.ShapeDtypeStruct((share, width), bf16)] * (half // share)
+        sender, *new_low = call(
             functools.partial(low_kernel, fanout),
             "low",
-            [jax.ShapeDtypeStruct((nodes, width), bf16), state_shape],
+            [jax.ShapeDtypeStruct((nodes, width), bf16)] + pieces,
             [active, columns, sender_low, low, high] + used,
             "svvvvvvv",
         )
         pairs = [(owner(m, layer), owner(m, layer + 1)) for m in range(samples)]
         if layer < last:
-            low = send(new_low, pairs)
+            low = send(new_low[0], pairs)
         else:
-            low = new_low
-        (new_high,) = call(
+            low = new_low[0]
+        new_high = call(
             functools.partial(high_kernel, fanout),
             "high",
-            [state_shape],
+            pieces,
             [active, columns, sender, high] + used,
             "svvvvvv",
         )
         if layer < last:
-            high = send(new_high, pairs)
+            high = send(new_high[0], pairs)
         else:
-            high = new_high
+            high = new_high[0]
         if layer == 0:
-            snapshot = lax.dynamic_index_in_dim(snapshots, segment, 0, keepdims=False)
             ready, table = call(
                 prepare_kernel,
                 "prepare",
@@ -496,19 +517,16 @@
                     jax.ShapeDtypeStruct((grid_rows, width), jnp.float32),
                     jax.ShapeDtypeStruct((mesh_rows, grid_rows), bf16),
                 ],
-                [snapshot, w_embed, w_decode, mesh_grid.reshape(1, grid_rows)],
-                "vvvv",
+                [segment.reshape(1), snapshots, w_embed, w_decode, mesh_grid.reshape(1, grid_rows)],
+                "svvvv",
                     )
             low, ready, table = lax.optimization_barrier((low, ready, table))
-    share = group * mesh_rows
     blocks = []
     for turn in range(samples):
         pairs = [(owner(m, last), device(m, turn * group)) for m in range(samples)]
         kept = [source for source, target in pairs if source == target]
         pairs = [(source, target) for source, target in pairs if source != target]
-        part = low if turn < samples // 2 else high
-        start = turn % (samples // 2) * share
-        block = part[start : start + share]
+        block = (list(new_low) + list(new_high))[turn]
         came = send(block, pairs)
         for at in kept:
             came = jnp.where(segment * parts + place == at, block, came)

time: 82 us -> 77 us (0.939)
  starting transfers between devices: 42.7 us -> 38 us
  waiting for transfers between devices: 13.7 us -> 15.3 us
  local copies, waits for them, and re-layouts: 7.93 us -> 6.98 us
    ppermute x11, waiting for transfers between devices: 7.05 us -> 10.9 us  [send(): lax.ppermute(value, ('segment', 'dom'), every_device(pairs, segments * pa...]
    ppermute x3, waiting for transfers between devices: 5.75 us -> 2.13 us  [to_chip(): return lax.ppermute(value, 'dom', pairs)]
    ppermute x2, starting transfers between devices: 6.38 us -> 4 us  [change_lane(): return lax.ppermute(value, 'dom', pairs)]
    ppermute x11, starting transfers between devices: 32.7 us -> 30.3 us  [send(): lax.ppermute(value, ('segment', 'dom'), every_device(pairs, segments * pa...]
    ppermute x2, waiting for transfers between devices: 0.9 us -> 2.29 us  [change_lane(): return lax.ppermute(value, 'dom', pairs)]
    squeeze x1 -> x0, local copies, waits for them, and re-layouts: 0.83 us -> none  [resident(): snapshot = lax.dynamic_index_in_dim(snapshots, segment, 0, keepdims=False)]
    unnamed x31 -> x29, local copies, waits for them, and re-layouts: 7.06 us -> 6.97 us
  transfers between devices with their start and end apart: 16 -> 16, of which waited for: 7 -> 6; matrix products, arithmetic and copies ran while one was open for 2% -> 1% of each run, Pallas kernels for 15% -> 15%
where the time goes in v7:
time: 77 us; the launch traced here: 76.4 us
  starting transfers between devices  38 us (49%)
  Pallas kernels  15.9 us (21%)
  waiting for transfers between devices  15.3 us (20%)
  local copies, waits for them, and re-layouts  6.98 us (9%)
    ppermute x11, starting transfers between devices, send(): lax.ppermute(value, ('segment', 'dom'), every_device(pairs, segments * pa...  30.3 us
    pallas_call x18, Pallas kernels, call(): pl.pallas_call(kernel, out_shape=shapes, in_specs=[kinds[place] for place...  15.9 us
    ppermute x11, waiting for transfers between devices, send(): lax.ppermute(value, ('segment', 'dom'), every_device(pairs, segments * pa...  10.9 us
    unnamed x29, local copies, waits for them, and re-layouts  6.97 us
    ppermute x2, starting transfers between devices, change_lane(): return lax.ppermute(value, 'dom', pairs)  4 us
    ppermute x3, starting transfers between devices, to_chip(): return lax.ppermute(value, 'dom', pairs)  3.67 us
    ppermute x2, waiting for transfers between devices, change_lane(): return lax.ppermute(value, 'dom', pairs)  2.29 us
    ppermute x3, waiting for transfers between devices, to_chip(): return lax.ppermute(value, 'dom', pairs)  2.13 us
  transfers between devices with their start and end apart: 16, of which 6 were waited for; matrix products, arithmetic and copies ran while one was open for 1% of the time, Pallas kernels for 15%

profile of v7, /device:TPU:5, one launch (start us, length us, event | category | flops | bytes accessed | tf_op | source)
XLA Modules:
  0.0 76.4 jit_solution(8656492481465870073)
XLA Ops:
  0.0 1.2 %collective-permute-start.8 = (bf16[1,512,1024]{2,1,0:T(8,128)(2,1)}, bf16[1,512,1024]{2,1,0:T(8,128)(2,1)}, u32[]{:S(2)}, u32[]{:S(2)}) collective-permute-start(bf16[1,512,1024]{2,1,0:T(8,128)(2,1)} %refs_0_.1), channel_id=1, source_target_pairs={{0,1},{1,0},{2,3},{3,2},{4,5},{5,4},{6,7},{7,6},{8,9},{9,8},{10,11... | collective-permute-start | bytes 3145736 | tf_op jit(solution)/shard_map/ppermute | solution.py:407
  1.2 0.7 collective-permute-start.10
  1.9 1.0 %copy.15 = bf16[4,128,227]{1,2,0:T(8,128)(2,1)S(1)} copy(bf16[4,128,227]{1,0,2:T(4,128)(2,1)} %param.12) | data formatting | bytes 464896 | tf_op args[0]
  2.9 0.0 copy-start.10
  2.9 0.0 copy-start.11
  2.9 0.0 copy-start.12
  3.0 0.0 copy-start.13
  3.0 0.6 copy-done.10
  3.6 0.0 copy-done.11
  3.6 0.7 encode.1
  4.4 1.4 %collective-permute-start = (bf16[80,512]{1,0:T(8,128)(2,1)S(1)}, bf16[80,512]{1,0:T(8,128)(2,1)S(1)}, u32[]{:S(2)}, u32[]{:S(2)}) collective-permute-start(bf16[80,512]{1,0:T(8,128)(2,1)S(1)} %get-tuple-element.40), channel_id=1, source_target_pairs={{0,2},{1,3},{2,0},{3,1},{4,6},{5,7},{6,4},{7,5},{8,10},{9,11},{10,... | collective-permute-start | bytes 245768 | tf_op jit(solution)/shard_map/ppermute | solution.py:411
  5.7 2.3 %collective-permute-start.1 = (bf16[80,512]{1,0:T(8,128)(2,1)S(1)}, bf16[80,512]{1,0:T(8,128)(2,1)S(1)}, u32[]{:S(2)}, u32[]{:S(2)}) collective-permute-start(bf16[80,512]{1,0:T(8,128)(2,1)S(1)} %get-tuple-element.41), channel_id=1, source_target_pairs={{0,4},{1,5},{2,6},{3,7},{4,0},{5,1},{6,2},{7,3},{8,12},{9,13},{10,... | collective-permute-start | bytes 245768 | tf_op jit(solution)/shard_map/ppermute | solution.py:411
  8.0 1.2 %copy-done.2 = bf16[1,512,1024]{2,1,0:T(8,128)(2,1)S(1)} copy-done((bf16[1,512,1024]{2,1,0:T(8,128)(2,1)S(1)}, bf16[1,512,1024]{2,1,0:T(8,128)(2,1)}, u32[]{:S(2)}) %copy-start.2) | copy-done | bytes 1048600
  9.3 1.2 %copy-done.3 = bf16[1,1024,512]{2,1,0:T(8,128)(2,1)S(1)} copy-done((bf16[1,1024,512]{2,1,0:T(8,128)(2,1)S(1)}, bf16[1,1024,512]{2,1,0:T(8,128)(2,1)}, u32[]{:S(2)}) %copy-start.3) | copy-done | bytes 1048600
  10.5 1.1 %hold.1 = (bf16[1,512,1024]{2,1,0:T(8,128)(2,1)S(1)}, bf16[1,512,512]{2,1,0:T(8,128)(2,1)S(1)}, bf16[1,1024,512]{2,1,0:T(8,128)(2,1)S(1)}) custom-call(bf16[1,512,1024]{2,1,0:T(8,128)(2,1)S(1)} %copy-done.2, bf16[1,512,512]{2,1,0:T(8,128)(2,1)} %refs_1_.1, bf16[1,1024,512]{2,1,0:T(8,128)(2,1)S(1)} %copy-done.3), custom_call_target="tpu_custom_call" | custom-call | bytes 5242880 | tf_op jit(solution)/shard_map/hold/pallas_call | solution.py:343
  11.7 2.1 %collective-permute-done.2.refs_3_ = bf16[80,512]{1,0:T(8,128)(2,1)S(1)} collective-permute-done((bf16[80,512]{1,0:T(8,128)(2,1)S(1)}, bf16[80,512]{1,0:T(8,128)(2,1)S(1)}, u32[]{:S(2)}, u32[]{:S(2)}) %collective-permute-start.2) | collective-permute-done | bytes 81952 | tf_op jit(solution)/shard_map/ppermute | solution.py:411
  13.8 1.8 %collective-permute-start.3 = (bf16[320,512]{1,0:T(8,128)(2,1)S(1)}, bf16[320,512]{1,0:T(8,128)(2,1)}, u32[]{:S(2)}, u32[]{:S(2)}) collective-permute-start(bf16[320,512]{1,0:T(8,128)(2,1)S(1)} %join.1.refs_0_), channel_id=1, source_target_pairs={{0,1},{1,0},{2,3},{3,2},{4,5},{5,4},{6,7},{7,6},{8,9},{9,8},{10,11... | collective-permute-start | bytes 983048 | tf_op jit(solution)/shard_map/ppermute | solution.py:415
  15.6 1.4 %collective-permute-done.3.refs_1_ = bf16[320,512]{1,0:T(8,128)(2,1)} collective-permute-done((bf16[320,512]{1,0:T(8,128)(2,1)S(1)}, bf16[320,512]{1,0:T(8,128)(2,1)}, u32[]{:S(2)}, u32[]{:S(2)}) %collective-permute-start.3) | collective-permute-done | bytes 327712 | tf_op jit(solution)/shard_map/ppermute | solution.py:415
  17.0 1.0 %index.1 = (f32[512,128]{1,0:T(8,128)S(1)}, bf16[256,512]{1,0:T(8,128)(2,1)S(1)}, bf16[256,512]{1,0:T(8,128)(2,1)S(1)}) custom-call(s32[1]{0:T(128)} %bitcast.2.chip, s32[1]{0:T(128)} %bitcast.3.active, bf16[320,512]{1,0:T(8,128)(2,1)S(1)} %join.1.refs_0_, bf16[320,512]{1,0:T(8,128)(2,1)} %collective-permute-done.3.refs_1_), custom_call_target="tpu_custom_call" | custom-call | bytes 1441800 | tf_op jit(solution)/shard_map/index/pallas_call | solution.py:343
  18.0 0.7 low.4
  18.7 0.7 collective-permute-start.4
  19.4 0.7 high.4
  20.1 0.0 collective-permute-start.5
  20.1 0.6 collective-permute-start.9
  20.7 0.7 copy-done.9
  21.4 1.2 %copy-done = bf16[1024,512]{1,0:T(8,128)(2,1)S(1)} copy-done((bf16[1024,512]{1,0:T(8,128)(2,1)S(1)}, bf16[1024,512]{1,0:T(8,128)(2,1)}, u32[]{:S(2)}) %copy-start) | copy-done | bytes 1048600
  22.6 0.9 %copy-done.5 = bf16[227,512]{1,0:T(8,128)(2,1)S(1)} copy-done((bf16[227,512]{1,0:T(8,128)(2,1)S(1)}, bf16[227,512]{1,0:T(8,128)(2,1)}, u32[]{:S(2)}) %copy-start.5) | copy-done | bytes 232472
  23.5 0.4 prepare.1
  24.0 1.0 %sender.5.sender_low = bf16[256,512]{1,0:T(8,128)(2,1)S(1)} custom-call(s32[1]{0:T(128)} %bitcast.12.active, bf16[256,512]{1,0:T(8,128)(2,1)} %collective-permute-done.4.low, bf16[1,512,1024]{2,1,0:T(8,128)(2,1)S(1)} %get-tuple-element.45.w_project), custom_call_target="tpu_custom_call" | custom-call | bytes 1572868 | tf_op jit(solution)/shard_map/sender/pallas_call | solution.py:343
  25.0 1.7 %low.5 = (bf16[512,512]{1,0:T(8,128)(2,1)S(1)}, bf16[256,512]{1,0:T(8,128)(2,1)}) custom-call(s32[1]{0:T(128)} %bitcast.12.active, f32[512,128]{1,0:T(8,128)S(1)} %get-tuple-element.43.columns, bf16[256,512]{1,0:T(8,128)(2,1)S(1)} %sender.5.sender_low, bf16[256,512]{1,0:T(8,128)(2,1)} %collective-permute-done.4.low, ...), custom_call_target="tpu_custom_call" | custom-call | bytes 4456452 | tf_op jit(solution)/shard_map/low/pallas_call | solution.py:343
  26.7 3.2 %collective-permute-start.6 = (bf16[256,512]{1,0:T(8,128)(2,1)}, bf16[256,512]{1,0:T(8,128)(2,1)}, u32[]{:S(2)}, u32[]{:S(2)}) collective-permute-start(bf16[256,512]{1,0:T(8,128)(2,1)} %get-tuple-element.56), channel_id=1, source_target_pairs={{0,1},{1,0},{2,3},{3,2},{4,5},{5,4},{6,7},{7,6},{8,16},{9,8},{10,1... | collective-permute-start | bytes 786440 | tf_op jit(solution)/shard_map/ppermute | solution.py:407
  29.9 0.7 high.5
  30.6 6.3 %collective-permute-start.7 = (bf16[256,512]{1,0:T(8,128)(2,1)}, bf16[256,512]{1,0:T(8,128)(2,1)S(1)}, u32[]{:S(2)}, u32[]{:S(2)}) collective-permute-start(bf16[256,512]{1,0:T(8,128)(2,1)} %high.5), channel_id=1, source_target_pairs={{0,1},{1,0},{2,3},{3,2},{4,5},{5,4},{6,7},{7,6},{8,16},{9,8},{10,1... | collective-permute-start | bytes 786440 | tf_op jit(solution)/shard_map/ppermute | solution.py:407
  36.9 1.0 %sender.6.sender_low = bf16[256,512]{1,0:T(8,128)(2,1)S(1)} custom-call(s32[1]{0:T(128)} %bitcast.11.active, bf16[256,512]{1,0:T(8,128)(2,1)} %collective-permute-done.6.low, bf16[1,512,1024]{2,1,0:T(8,128)(2,1)S(1)} %get-tuple-element.45.w_project), custom_call_target="tpu_custom_call" | custom-call | bytes 1572868 | tf_op jit(solution)/shard_map/sender/pallas_call | solution.py:343
  37.9 2.7 %collective-permute-done.7.high = bf16[256,512]{1,0:T(8,128)(2,1)S(1)} collective-permute-done((bf16[256,512]{1,0:T(8,128)(2,1)}, bf16[256,512]{1,0:T(8,128)(2,1)S(1)}, u32[]{:S(2)}, u32[]{:S(2)}) %collective-permute-start.7) | collective-permute-done | bytes 262176 | tf_op jit(solution)/shard_map/ppermute | solution.py:407
  40.6 0.9 %low.6 = (bf16[512,512]{1,0:T(8,128)(2,1)S(1)}, bf16[256,512]{1,0:T(8,128)(2,1)S(1)}) custom-call(s32[1]{0:T(128)} %bitcast.11.active, f32[512,128]{1,0:T(8,128)S(1)} %get-tuple-element.43.columns, bf16[256,512]{1,0:T(8,128)(2,1)S(1)} %sender.6.sender_low, bf16[256,512]{1,0:T(8,128)(2,1)} %collective-permute-done.6.low, ...), custom_call_target="tpu_custom_call" | custom-call | bytes 4456452 | tf_op jit(solution)/shard_map/low/pallas_call | solution.py:343
  41.5 1.2 %sender.7.sender_low = bf16[256,512]{1,0:T(8,128)(2,1)S(1)} custom-call(s32[1]{0:T(128)} %bitcast.11.active, bf16[256,512]{1,0:T(8,128)(2,1)S(1)} %get-tuple-element.58.low, bf16[1,512,1024]{2,1,0:T(8,128)(2,1)} %collective-permute-done.8.w_project), custom_call_target="tpu_custom_call" | custom-call | bytes 1572868 | tf_op jit(solution)/shard_map/sender/pallas_call | solution.py:343
  42.7 1.7 %low.7 = (bf16[512,512]{1,0:T(8,128)(2,1)S(1)}, bf16[128,512]{1,0:T(8,128)(2,1)S(1)}, bf16[128,512]{1,0:T(8,128)(2,1)S(1)}) custom-call(s32[1]{0:T(128)} %bitcast.11.active, f32[512,128]{1,0:T(8,128)S(1)} %get-tuple-element.43.columns, bf16[256,512]{1,0:T(8,128)(2,1)S(1)} %sender.7.sender_low, bf16[256,512]{1,0:T(8,128)(2,1)S(1)} %get-tuple-element.58.low, ...), custom_call_target="tpu_custom_call" | custom-call | bytes 4456452 | tf_op jit(solution)/shard_map/low/pallas_call | solution.py:343
  44.5 1.8 %high.7 = (bf16[128,512]{1,0:T(8,128)(2,1)S(1)}, bf16[128,512]{1,0:T(8,128)(2,1)S(1)}) custom-call(s32[1]{0:T(128)} %bitcast.11.active, f32[512,128]{1,0:T(8,128)S(1)} %get-tuple-element.43.columns, bf16[512,512]{1,0:T(8,128)(2,1)S(1)} %get-tuple-element.60.sender, bf16[256,512]{1,0:T(8,128)(2,1)S(1)} %high.6, ...), custom_call_target="tpu_custom_call" | custom-call | bytes 3932164 | tf_op jit(solution)/shard_map/high/pallas_call | solution.py:343
  46.2 2.2 %collective-permute-start.11 = (bf16[128,512]{1,0:T(8,128)(2,1)S(1)}, bf16[128,512]{1,0:T(8,128)(2,1)S(1)}, u32[]{:S(2)}, u32[]{:S(2)}) collective-permute-start(bf16[128,512]{1,0:T(8,128)(2,1)S(1)} %get-tuple-element.61), channel_id=1, source_target_pairs={{0,1},{1,0},{2,3},{3,2},{4,5},{5,4},{6,7},{7,17},{8,9},{9,8},{10,1... | collective-permute-start | bytes 393224 | tf_op jit(solution)/shard_map/ppermute | solution.py:407
  48.4 14.2 %collective-permute-start.12 = (bf16[128,512]{1,0:T(8,128)(2,1)S(1)}, bf16[128,512]{1,0:T(8,128)(2,1)S(1)}, u32[]{:S(2)}, u32[]{:S(2)}) collective-permute-start(bf16[128,512]{1,0:T(8,128)(2,1)S(1)} %get-tuple-element.62), channel_id=1, source_target_pairs={{0,1},{1,0},{2,3},{3,2},{4,5},{5,17},{6,7},{7,6},{8,9},{9,8},{10,1... | collective-permute-start | bytes 393224 | tf_op jit(solution)/shard_map/ppermute | solution.py:407
  62.6 1.2 %collective-permute-start.13 = (bf16[128,512]{1,0:T(8,128)(2,1)S(1)}, bf16[128,512]{1,0:T(8,128)(2,1)S(1)}, u32[]{:S(2)}, u32[]{:S(2)}) collective-permute-start(bf16[128,512]{1,0:T(8,128)(2,1)S(1)} %get-tuple-element.63), channel_id=1, source_target_pairs={{0,1},{1,0},{2,3},{3,17},{4,5},{5,4},{6,7},{7,6},{8,9},{9,8},{10,1... | collective-permute-start | bytes 393224 | tf_op jit(solution)/shard_map/ppermute | solution.py:407
  63.7 0.0 collective-permute-start.14
  63.8 3.8 %collective-permute-done.13 = bf16[128,512]{1,0:T(8,128)(2,1)S(1)} collective-permute-done((bf16[128,512]{1,0:T(8,128)(2,1)S(1)}, bf16[128,512]{1,0:T(8,128)(2,1)S(1)}, u32[]{:S(2)}, u32[]{:S(2)}) %collective-permute-start.13) | collective-permute-done | bytes 131104 | tf_op jit(solution)/shard_map/ppermute | solution.py:407
  67.6 4.4 %collective-permute-done.14 = bf16[128,512]{1,0:T(8,128)(2,1)S(1)} collective-permute-done((bf16[128,512]{1,0:T(8,128)(2,1)S(1)}, bf16[128,512]{1,0:T(8,128)(2,1)S(1)}, u32[]{:S(2)}, u32[]{:S(2)}) %collective-permute-start.14) | collective-permute-done | bytes 131104 | tf_op jit(solution)/shard_map/ppermute | solution.py:407
  72.0 2.2 %collective-permute-start.15 = (bf16[64,512]{1,0:T(8,128)(2,1)S(1)}, bf16[64,512]{1,0:T(8,128)(2,1)S(1)}, u32[]{:S(2)}, u32[]{:S(2)}) collective-permute-start(bf16[64,512]{1,0:T(8,128)(2,1)S(1)} %slice.4), channel_id=1, source_target_pairs={{0,1},{1,0},{2,3},{3,2},{4,5},{5,4},{6,7},{7,6},{8,9},{9,8},{10,11... | collective-permute-start | bytes 196616 | tf_op jit(solution)/shard_map/ppermute | solution.py:415
  74.2 0.9 %collective-permute-done.15.refs_1_ = bf16[64,512]{1,0:T(8,128)(2,1)S(1)} collective-permute-done((bf16[64,512]{1,0:T(8,128)(2,1)S(1)}, bf16[64,512]{1,0:T(8,128)(2,1)S(1)}, u32[]{:S(2)}, u32[]{:S(2)}) %collective-permute-start.15) | collective-permute-done | bytes 65568 | tf_op jit(solution)/shard_map/ppermute | solution.py:415
  75.1 1.2 %decode.1 = bf16[227,128]{1,0:T(8,128)(2,1)} custom-call(s32[1]{0:T(128)} %bitcast.turn, f32[128,512]{1,0:T(8,128)S(1)} %copy-done.7, bf16[64,128]{1,0:T(8,128)(2,1)S(1)} %get-tuple-element.53.table, bf16[1024,512]{1,0:T(8,128)(2,1)S(1)} %copy-done.1, bf16[227,512]{1,0:T(8,128)(2,1)S(1)} %bitcast.20, bf16[128,512]{1,0:T(8,128)(2,1)S(1)} %select_select_fusion.refs_0_, ...), custom_call_target="tpu_custom_call" | custom-call | bytes 1814276 | tf_op jit(solution)/shard_map/decode/pallas_call | solution.py:343
  (34 shorter events, 0.1 us)
Async XLA Ops:
  0.0 41.5 %collective-permute-start.8 = (bf16[1,512,1024]{2,1,0:T(8,128)(2,1)}, bf16[1,512,1024]{2,1,0:T(8,128)(2,1)}, u32[]{:S(2)}, u32[]{:S(2)}) collective-permute-start(bf16[1,512,1024]{2,1,0:T(8,128)(2,1)} %refs_0_.1), channel_id=1, source_target_pairs={{0,1},{1,0},{2,3},{3,2},{4,5},{5,4},{6,7},{7,6},{8,9},{9,8},{10,11... | collective-permute-start | bytes 3145736 | tf_op jit(solution)/shard_map/ppermute | solution.py:407
  1.2 41.5 %collective-permute-start.10 = (bf16[1,1024,512]{2,1,0:T(8,128)(2,1)}, bf16[1,1024,512]{2,1,0:T(8,128)(2,1)}, u32[]{:S(2)}, u32[]{:S(2)}) collective-permute-start(bf16[1,1024,512]{2,1,0:T(8,128)(2,1)} %refs_2_.1), channel_id=1, source_target_pairs={{0,1},{1,0},{2,3},{3,2},{4,5},{5,4},{6,7},{7,6},{8,9},{9,8},{10,11... | collective-permute-start | bytes 3145736 | tf_op jit(solution)/shard_map/ppermute | solution.py:407
  1.9 1.7 %copy-start.4 = (bf16[227,512]{1,0:T(8,128)(2,1)S(1)}, bf16[227,512]{1,0:T(8,128)(2,1)}, u32[]{:S(2)}) copy-start(bf16[227,512]{1,0:T(8,128)(2,1)} %w_embed.3) | copy-start | bytes 697348
  2.9 0.7 copy-start.10
  2.9 0.7 copy-start.11
  2.9 0.7 copy-start.12
  3.0 0.7 copy-start.13
  4.4 7.3 %collective-permute-start = (bf16[80,512]{1,0:T(8,128)(2,1)S(1)}, bf16[80,512]{1,0:T(8,128)(2,1)S(1)}, u32[]{:S(2)}, u32[]{:S(2)}) collective-permute-start(bf16[80,512]{1,0:T(8,128)(2,1)S(1)} %get-tuple-element.40), channel_id=1, source_target_pairs={{0,2},{1,3},{2,0},{3,1},{4,6},{5,7},{6,4},{7,5},{8,10},{9,11},{10,... | collective-permute-start | bytes 245768 | tf_op jit(solution)/shard_map/ppermute | solution.py:411
  5.7 5.9 %collective-permute-start.1 = (bf16[80,512]{1,0:T(8,128)(2,1)S(1)}, bf16[80,512]{1,0:T(8,128)(2,1)S(1)}, u32[]{:S(2)}, u32[]{:S(2)}) collective-permute-start(bf16[80,512]{1,0:T(8,128)(2,1)S(1)} %get-tuple-element.41), channel_id=1, source_target_pairs={{0,4},{1,5},{2,6},{3,7},{4,0},{5,1},{6,2},{7,3},{8,12},{9,13},{10,... | collective-permute-start | bytes 245768 | tf_op jit(solution)/shard_map/ppermute | solution.py:411
  8.0 5.7 %collective-permute-start.2 = (bf16[80,512]{1,0:T(8,128)(2,1)S(1)}, bf16[80,512]{1,0:T(8,128)(2,1)S(1)}, u32[]{:S(2)}, u32[]{:S(2)}) collective-permute-start(bf16[80,512]{1,0:T(8,128)(2,1)S(1)} %get-tuple-element.42), channel_id=1, source_target_pairs={{0,6},{1,7},{2,4},{3,5},{4,2},{5,3},{6,0},{7,1},{8,14},{9,15},{10,... | collective-permute-start | bytes 245768 | tf_op jit(solution)/shard_map/ppermute | solution.py:411
  8.0 1.2 %copy-start.2 = (bf16[1,512,1024]{2,1,0:T(8,128)(2,1)S(1)}, bf16[1,512,1024]{2,1,0:T(8,128)(2,1)}, u32[]{:S(2)}) copy-start(bf16[1,512,1024]{2,1,0:T(8,128)(2,1)} %refs_0_.1) | copy-start | bytes 3145732
  9.3 1.2 %copy-start.3 = (bf16[1,1024,512]{2,1,0:T(8,128)(2,1)S(1)}, bf16[1,1024,512]{2,1,0:T(8,128)(2,1)}, u32[]{:S(2)}) copy-start(bf16[1,1024,512]{2,1,0:T(8,128)(2,1)} %refs_2_.1) | copy-start | bytes 3145732
  13.8 3.2 %collective-permute-start.3 = (bf16[320,512]{1,0:T(8,128)(2,1)S(1)}, bf16[320,512]{1,0:T(8,128)(2,1)}, u32[]{:S(2)}, u32[]{:S(2)}) collective-permute-start(bf16[320,512]{1,0:T(8,128)(2,1)S(1)} %join.1.refs_0_), channel_id=1, source_target_pairs={{0,1},{1,0},{2,3},{3,2},{4,5},{5,4},{6,7},{7,6},{8,9},{9,8},{10,11... | collective-permute-start | bytes 983048 | tf_op jit(solution)/shard_map/ppermute | solution.py:415
  18.7 5.3 %collective-permute-start.4 = (bf16[256,512]{1,0:T(8,128)(2,1)}, bf16[256,512]{1,0:T(8,128)(2,1)}, u32[]{:S(2)}, u32[]{:S(2)}) collective-permute-start(bf16[256,512]{1,0:T(8,128)(2,1)} %get-tuple-element.49), channel_id=1, source_target_pairs={{0,8},{1,0},{2,10},{3,2},{4,12},{5,4},{6,14},{7,6},{8,9},{9,1},{10... | collective-permute-start | bytes 786440 | tf_op jit(solution)/shard_map/ppermute | solution.py:407
  20.1 4.9 %collective-permute-start.5 = (bf16[256,512]{1,0:T(8,128)(2,1)}, bf16[256,512]{1,0:T(8,128)(2,1)S(1)}, u32[]{:S(2)}, u32[]{:S(2)}) collective-permute-start(bf16[256,512]{1,0:T(8,128)(2,1)} %high.4), channel_id=1, source_target_pairs={{0,8},{1,0},{2,10},{3,2},{4,12},{5,4},{6,14},{7,6},{8,9},{9,1},{10... | collective-permute-start | bytes 786440 | tf_op jit(solution)/shard_map/ppermute | solution.py:407
  20.1 22.6 %collective-permute-start.9 = (bf16[1,512,512]{2,1,0:T(8,128)(2,1)}, bf16[1,512,512]{2,1,0:T(8,128)(2,1)}, u32[]{:S(2)}, u32[]{:S(2)}) collective-permute-start(bf16[1,512,512]{2,1,0:T(8,128)(2,1)} %refs_1_.1), channel_id=1, source_target_pairs={{0,1},{1,0},{2,3},{3,2},{4,5},{5,4},{6,7},{7,6},{8,9},{9,8},{10,11... | collective-permute-start | bytes 1572872 | tf_op jit(solution)/shard_map/ppermute | solution.py:407
  20.7 0.7 copy-start.9
  21.4 1.2 %copy-start = (bf16[1024,512]{1,0:T(8,128)(2,1)S(1)}, bf16[1024,512]{1,0:T(8,128)(2,1)}, u32[]{:S(2)}) copy-start(bf16[1024,512]{1,0:T(8,128)(2,1)} %w_decode.3) | copy-start | bytes 3145732
  22.6 0.9 %copy-start.5 = (bf16[227,512]{1,0:T(8,128)(2,1)S(1)}, bf16[227,512]{1,0:T(8,128)(2,1)}, u32[]{:S(2)}) copy-start(bf16[227,512]{1,0:T(8,128)(2,1)} %w_embed.3) | copy-start | bytes 697348
  23.9 1.1 %copy-start.6 = (f32[128,512]{1,0:T(8,128)}, f32[128,512]{1,0:T(8,128)S(1)}, u32[]{:S(2)}) copy-start(f32[128,512]{1,0:T(8,128)S(1)} %get-tuple-element.52.ready) | copy-start | bytes 786436
  26.7 10.3 %collective-permute-start.6 = (bf16[256,512]{1,0:T(8,128)(2,1)}, bf16[256,512]{1,0:T(8,128)(2,1)}, u32[]{:S(2)}, u32[]{:S(2)}) collective-permute-start(bf16[256,512]{1,0:T(8,128)(2,1)} %get-tuple-element.56), channel_id=1, source_target_pairs={{0,1},{1,0},{2,3},{3,2},{4,5},{5,4},{6,7},{7,6},{8,16},{9,8},{10,1... | collective-permute-start | bytes 786440 | tf_op jit(solution)/shard_map/ppermute | solution.py:407
  30.6 10.0 %collective-permute-start.7 = (bf16[256,512]{1,0:T(8,128)(2,1)}, bf16[256,512]{1,0:T(8,128)(2,1)S(1)}, u32[]{:S(2)}, u32[]{:S(2)}) collective-permute-start(bf16[256,512]{1,0:T(8,128)(2,1)} %high.5), channel_id=1, source_target_pairs={{0,1},{1,0},{2,3},{3,2},{4,5},{5,4},{6,7},{7,6},{8,16},{9,8},{10,1... | collective-permute-start | bytes 786440 | tf_op jit(solution)/shard_map/ppermute | solution.py:407
  44.5 30.7 %copy-start.1 = (bf16[1024,512]{1,0:T(8,128)(2,1)S(1)}, bf16[1024,512]{1,0:T(8,128)(2,1)}, u32[]{:S(2)}) copy-start(bf16[1024,512]{1,0:T(8,128)(2,1)} %w_decode.3) | copy-start | bytes 3145732
  46.2 17.5 %collective-permute-start.11 = (bf16[128,512]{1,0:T(8,128)(2,1)S(1)}, bf16[128,512]{1,0:T(8,128)(2,1)S(1)}, u32[]{:S(2)}, u32[]{:S(2)}) collective-permute-start(bf16[128,512]{1,0:T(8,128)(2,1)S(1)} %get-tuple-element.61), channel_id=1, source_target_pairs={{0,1},{1,0},{2,3},{3,2},{4,5},{5,4},{6,7},{7,17},{8,9},{9,8},{10,1... | collective-permute-start | bytes 393224 | tf_op jit(solution)/shard_map/ppermute | solution.py:407
  48.4 15.4 %collective-permute-start.12 = (bf16[128,512]{1,0:T(8,128)(2,1)S(1)}, bf16[128,512]{1,0:T(8,128)(2,1)S(1)}, u32[]{:S(2)}, u32[]{:S(2)}) collective-permute-start(bf16[128,512]{1,0:T(8,128)(2,1)S(1)} %get-tuple-element.62), channel_id=1, source_target_pairs={{0,1},{1,0},{2,3},{3,2},{4,5},{5,17},{6,7},{7,6},{8,9},{9,8},{10,1... | collective-permute-start | bytes 393224 | tf_op jit(solution)/shard_map/ppermute | solution.py:407
  62.6 5.0 %collective-permute-start.13 = (bf16[128,512]{1,0:T(8,128)(2,1)S(1)}, bf16[128,512]{1,0:T(8,128)(2,1)S(1)}, u32[]{:S(2)}, u32[]{:S(2)}) collective-permute-start(bf16[128,512]{1,0:T(8,128)(2,1)S(1)} %get-tuple-element.63), channel_id=1, source_target_pairs={{0,1},{1,0},{2,3},{3,17},{4,5},{5,4},{6,7},{7,6},{8,9},{9,8},{10,1... | collective-permute-start | bytes 393224 | tf_op jit(solution)/shard_map/ppermute | solution.py:407
  63.7 8.2 %collective-permute-start.14 = (bf16[128,512]{1,0:T(8,128)(2,1)S(1)}, bf16[128,512]{1,0:T(8,128)(2,1)S(1)}, u32[]{:S(2)}, u32[]{:S(2)}) collective-permute-start(bf16[128,512]{1,0:T(8,128)(2,1)S(1)} %get-tuple-element.64), channel_id=1, source_target_pairs={{0,1},{1,21},{2,3},{3,2},{4,5},{5,4},{6,7},{7,6},{8,9},{9,19},{10,... | collective-permute-start | bytes 393224 | tf_op jit(solution)/shard_map/ppermute | solution.py:407
  72.0 3.2 %copy-start.7 = (f32[128,512]{1,0:T(8,128)S(1)}, f32[128,512]{1,0:T(8,128)}, u32[]{:S(2)}) copy-start(f32[128,512]{1,0:T(8,128)} %copy-done.6) | copy-start | bytes 786436
  72.0 3.2 %copy-start.8 = (bf16[512,227]{0,1:T(8,128)(2,1)S(1)}, bf16[512,227]{0,1:T(8,128)(2,1)}, u32[]{:S(2)}) copy-start(bf16[512,227]{0,1:T(8,128)(2,1)} %param.18) | copy-start | bytes 697348
  72.0 3.1 %collective-permute-start.15 = (bf16[64,512]{1,0:T(8,128)(2,1)S(1)}, bf16[64,512]{1,0:T(8,128)(2,1)S(1)}, u32[]{:S(2)}, u32[]{:S(2)}) collective-permute-start(bf16[64,512]{1,0:T(8,128)(2,1)S(1)} %slice.4), channel_id=1, source_target_pairs={{0,1},{1,0},{2,3},{3,2},{4,5},{5,4},{6,7},{7,6},{8,9},{9,8},{10,11... | collective-permute-start | bytes 196616 | tf_op jit(solution)/shard_map/ppermute | solution.py:415

commit v8 on v7

--- a/solution.py
+++ b/solution.py
@@ -165,6 +165,14 @@
     return lax.dot_general(left, right, (((0,), (0,)), ((), ())), preferred_element_type=jnp.float32)
 
 
+def place_of(where, group):
+    return lax.div(where[1], group), lax.rem(where[1], group)
+
+
+def owns(where, group, at_segment):
+    return jnp.logical_and(where[0] == at_segment, lax.rem(where[1], group) == 0)
+
+
 def fetch(sources, targets, semaphores):
     copies = [
         pltpu.make_async_copy(source, target, semaphores.at[place])
@@ -175,8 +183,9 @@
     return copies
 
 
-def encode_kernel(mesh_rows, fanout, lists, chip, snapshots, w_embed, packed, *refs):
+def encode_kernel(group, mesh_rows, fanout, lists, where, snapshots, w_embed, packed, *refs):
     payloads, latent = refs[:-1], refs[-1]
+    chip, _ = place_of(where, group)
     neighbors = packed[:fanout, :mesh_rows]
     grid_rows = snapshots.shape[2]
     grid_mesh = packed[fanout + lists : fanout + lists + 1, :grid_rows]
@@ -203,7 +212,7 @@
     coded = jnp.concatenate([coded, jnp.zeros_like(coded)], axis=0)
     coded = coded.astype(jnp.float32).astype(jnp.bfloat16)
     for turn, payload in enumerate(payloads):
-        start = pl.multiple_of(jnp.bitwise_xor(chip[0], turn) * grid_rows, grid_rows)
+        start = pl.multiple_of(jnp.bitwise_xor(chip, turn) * grid_rows, grid_rows)
         pooled = matmul(table, latent[pl.ds(start, grid_rows), :])
         payload[:mesh_rows, :] = rms_scale(pooled).astype(jnp.bfloat16)
         payload[mesh_rows:, :] = coded
@@ -216,17 +225,18 @@
         joined[place * rows : (place + 1) * rows, :] = payload[...]
 
 
-def index_kernel(parts, mesh_rows, chip, active, *refs):
+def index_kernel(parts, mesh_rows, where, *refs):
     lanes, (columns_out, low, high), index_out = refs[:-4], refs[-4:-1], refs[-1]
     nodes = columns_out.shape[0]
     group = len(lanes)
     rows = lanes[0].shape[0] // (parts // group)
-
-    @pl.when(active[0] == 1)
+    chip, lane_place = place_of(where, group)
+
+    @pl.when(lane_place == 0)
     def _():
         tables = []
         for part in range(parts):
-            lane, turn = lanes[part % group], jnp.bitwise_xor(chip[0], part // group)
+            lane, turn = lanes[part % group], jnp.bitwise_xor(chip, part // group)
             base = pl.multiple_of(turn * rows, 16)
             half, spot = (low, part) if part < parts // 2 else (high, part - parts // 2)
             half[spot * mesh_rows : (spot + 1) * mesh_rows, :] = lane[pl.ds(base, mesh_rows), :]
@@ -281,41 +291,105 @@
         piece[...] = value[place * rows : (place + 1) * rows]
 
 
-def sender_kernel(active, low, w_project, sender_low):
+def sender_kernel(group, at_segment, where, low, w_project, sender_low):
     width = low.shape[1]
 
-    @pl.when(active[0] == 1)
+    @pl.when(owns(where, group, at_segment))
     def _():
         sender_low[...] = matmul(low[...], w_project[0, :, width:]).astype(jnp.bfloat16)
 
 
-def low_kernel(fanout, active, columns, sender_low, low, high, w_project, w_message, w_update, *outs):
-    sender, new_low = outs[0], outs[1:]
+def half_of(where, group, chips, far, low, high, own):
+    half = low.shape[0]
+    chip, _ = place_of(where, group)
+    upper = (chip < chips // 2) if far else (chip >= chips // 2)
+
+    @pl.when(upper)
+    def _():
+        own[...] = high[...]
+
+    @pl.when(jnp.logical_not(upper))
+    def _():
+        own[...] = low[...]
+
+    return pl.multiple_of(jnp.where(upper, half, 0), half)
+
+
+def first_kernel(
+    group, at_segment, chips, fanout, where, columns, sender_low, low, high, w_project, w_message, w_update, *outs
+):
+    sender, pieces, own = outs[0], outs[1:-1], outs[-1]
     half, width = low.shape
 
-    @pl.when(active[0] == 1)
+    @pl.when(owns(where, group, at_segment))
     def _():
         sender[:half, :] = sender_low[...]
         sender[half:, :] = matmul(high[...], w_project[0, :, width:]).astype(jnp.bfloat16)
-        write_pieces(
-            new_low,
-            renew(fanout, columns[:half, :], sender[...], low[...], w_project, w_message, w_update),
-        )
-
-
-def high_kernel(fanout, active, columns, sender, high, w_project, w_message, w_update, *new_high):
-    half = high.shape[0]
-
-    @pl.when(active[0] == 1)
+        start, state = 0, low
+        if chips:
+            start, state = half_of(where, group, chips, True, low, high, own), own
+        rows = columns[pl.ds(start, half), :]
+        write_pieces(pieces, renew(fanout, rows, sender[...], state[...], w_project, w_message, w_update))
+
+
+def second_kernel(
+    group, at_segment, chips, fanout, where, columns, sender, low, high, w_project, w_message, w_update, *outs
+):
+    pieces, own = outs[:-1], outs[-1]
+    half = low.shape[0]
+
+    @pl.when(owns(where, group, at_segment))
     def _():
-        write_pieces(
-            new_high,
-            renew(fanout, columns[half:, :], sender[...], high[...], w_project, w_message, w_update),
-        )
-
-
-def prepare_kernel(segment, snapshots, w_embed, w_decode, mesh_grid, ready, table_out):
-    snapshot = snapshots[segment[0]]
+        start, state = half, high
+        if chips:
+            start, state = half_of(where, group, chips, False, low, high, own), own
+        rows = columns[pl.ds(start, half), :]
+        write_pieces(pieces, renew(fanout, rows, sender[...], state[...], w_project, w_message, w_update))
+
+
+def arrival(where, group, chips, last):
+    each = chips // 2
+    segment = where[0]
+    chip, _ = place_of(where, group)
+    crosses = lax.div(chip, each) != lax.div(segment, each)
+    return crosses, jnp.logical_and(segment == last, chip == last), lax.rem(chip, each)
+
+
+def far_kernel(group, chips, last, where, *refs):
+    far, out = refs[:-1], refs[-1]
+    crosses, _, spot = arrival(where, group, chips, last)
+    for number, block in enumerate(far):
+
+        @pl.when(jnp.logical_and(crosses, spot == number))
+        def _(block=block):
+            out[...] = block[...]
+
+
+def near_kernel(group, chips, last, where, crossed, *refs):
+    each = chips // 2
+    near, kept, outs = refs[:each], refs[each : 2 * each], refs[2 * each :]
+    rows = outs[0].shape[0]
+    crosses, stays, spot = arrival(where, group, chips, last)
+    arrives = jnp.logical_not(jnp.logical_or(crosses, stays))
+
+    def give(block):
+        for place, out in enumerate(outs):
+            out[...] = block[place * rows : (place + 1) * rows, :]
+
+    @pl.when(crosses)
+    def _():
+        give(crossed)
+
+    for number in range(each):
+        for blocks, chosen in ((near, arrives), (kept, stays)):
+
+            @pl.when(jnp.logical_and(chosen, spot == number))
+            def _(block=blocks[number]):
+                give(block)
+
+
+def prepare_kernel(where, snapshots, w_embed, w_decode, mesh_grid, ready, table_out):
+    snapshot = snapshots[where[0]]
     latent = silu_by_tanh(matmul_tn(snapshot, w_embed[...])).astype(jnp.bfloat16)
     ready[...] = matmul(latent, w_decode[: latent.shape[1], :])
     mesh_rows, grid_rows = table_out.shape
@@ -323,14 +397,15 @@
     table_out[...] = jnp.where(table, 1.0, 0.0).astype(jnp.bfloat16)
 
 
-def decode_kernel(turn, ready, table, w_decode, w_output, *refs):
+def decode_kernel(where, ready, table, w_decode, w_output, *refs):
     blocks, out, state = refs[:-2], refs[-2], refs[-1]
     width = ready.shape[1]
+    _, lane = place_of(where, len(blocks))
     for number, block in enumerate(blocks):
 
-        @pl.when(turn[0] == number)
-        def _():
-            state[...] = block[: state.shape[0], :]
+        @pl.when(lane == number)
+        def _(block=block):
+            state[...] = block[...]
 
     readout = matmul_tn(table[...], state[...]).astype(jnp.bfloat16)
     hidden = silu_by_tanh(ready[...] + matmul(readout, w_decode[width:, :])).astype(jnp.bfloat16)
@@ -417,8 +492,9 @@
     def owner(m, at_segment):
         return device(at_segment, m * group)
 
-    chip, lane = place // group, place % group
-    weights = [w_project, w_message, w_update]
+    where, *weights = lax.optimization_barrier(
+        (jnp.stack([segment, place]).astype(jnp.int32), w_project, w_message, w_update)
+    )
     last = segments - 2
     pairs = [(owner(m, last + 1), owner(m, last)) for m in range(samples)]
     came_weights = [send(weight, pairs) for weight in weights]
@@ -438,10 +514,10 @@
         axis=0,
     )
     payloads = call(
-        functools.partial(encode_kernel, mesh_rows, fanout, lists),
+        functools.partial(encode_kernel, group, mesh_rows, fanout, lists),
         "encode",
         [jax.ShapeDtypeStruct((mesh_rows + 2 * fanout, width), bf16)] * samples,
-        [chip.reshape(1), snapshots, w_embed, packed],
+        [where, snapshots, w_embed, packed],
         "svvv",
         [pltpu.VMEM((samples * grid_rows, width), bf16)],
     )
@@ -473,42 +549,43 @@
             jax.ShapeDtypeStruct((half, width), bf16),
             jax.ShapeDtypeStruct((half, width), bf16),
         ],
-        [chip.reshape(1), (lane == 0).astype(jnp.int32).reshape(1)] + lanes,
-        "ss" + "v" * group,
+        [where] + lanes,
+        "s" + "v" * group,
         [pltpu.VMEM((128, nodes), jnp.int32)],
     )
     state_shape = jax.ShapeDtypeStruct((half, width), bf16)
     for layer in range(segments):
-        at_segment = min(layer, last)
-        active = ((segment == at_segment) & (lane == 0)).astype(jnp.int32).reshape(1)
+        at_segment, ends = min(layer, last), layer > last
         used = list(held) if layer <= last else came_weights
-        (sender_low,) = call(sender_kernel, "sender", [state_shape], [active, low, used[0]], "svv")
-        pieces = [state_shape]
-        if layer > last:
-            pieces = [jax.ShapeDtypeStruct((share, width), bf16)] * (half // share)
-        sender, *new_low = call(
-            functools.partial(low_kernel, fanout),
-            "low",
+        role = (group, at_segment, samples if ends else 0, fanout)
+        pieces = [jax.ShapeDtypeStruct((share, width), bf16)] * (half // share) if ends else [state_shape]
+        scratch = [pltpu.VMEM((half, width), bf16)]
+        (sender_low,) = call(
+            functools.partial(sender_kernel, group, at_segment),
+            "sender",
+            [state_shape],
+            [where, low, used[0]],
+            "svv",
+        )
+        sender, *first = call(
+            functools.partial(first_kernel, *role),
+            "first",
             [jax.ShapeDtypeStruct((nodes, width), bf16)] + pieces,
-            [active, columns, sender_low, low, high] + used,
+            [where, columns, sender_low, low, high] + used,
             "svvvvvvv",
+            scratch,
         )
         pairs = [(owner(m, layer), owner(m, layer + 1)) for m in range(samples)]
-        if layer < last:
-            low = send(new_low[0], pairs)
-        else:
-            low = new_low[0]
-        new_high = call(
-            functools.partial(high_kernel, fanout),
-            "high",
+        new_low = send(first[0], pairs) if layer < last else first[0]
+        second = call(
+            functools.partial(second_kernel, *role),
+            "second",
             pieces,
-            [active, columns, sender, high] + used,
-            "svvvvvv",
-        )
-        if layer < last:
-            high = send(new_high[0], pairs)
-        else:
-            high = new_high[0]
+            [where, columns, sender, low, high] + used,
+            "svvvvvvv",
+            scratch,
+        )
+        low, high = new_low, send(second[0], pairs) if layer < last else second[0]
         if layer == 0:
             ready, table = call(
                 prepare_kernel,
@@ -517,31 +594,40 @@
                     jax.ShapeDtypeStruct((grid_rows, width), jnp.float32),
                     jax.ShapeDtypeStruct((mesh_rows, grid_rows), bf16),
                 ],
-                [segment.reshape(1), snapshots, w_embed, w_decode, mesh_grid.reshape(1, grid_rows)],
+                [where, snapshots, w_embed, w_decode, mesh_grid.reshape(1, grid_rows)],
                 "svvvv",
                     )
             low, ready, table = lax.optimization_barrier((low, ready, table))
-    blocks = []
-    for turn in range(samples):
-        pairs = [(owner(m, last), device(m, turn * group)) for m in range(samples)]
-        kept = [source for source, target in pairs if source == target]
-        pairs = [(source, target) for source, target in pairs if source != target]
-        block = (list(new_low) + list(new_high))[turn]
-        came = send(block, pairs)
-        for at in kept:
-            came = jnp.where(segment * parts + place == at, block, came)
-        blocks.append(came)
-    block = blocks[0]
-    for turn in range(1, samples):
-        block = jnp.where(chip == turn, blocks[turn], block)
-    handed = [block]
+    each = samples // 2
+    arrived = []
+    for far, blocks in ((1, first), (0, second)):
+        for turn, block in enumerate(blocks):
+            pairs = [
+                (owner(m, last), device(m, ((m // each ^ far) * each + turn) * group)) for m in range(samples)
+            ]
+            arrived.append(send(block, [pair for pair in pairs if pair[0] != pair[1]]))
+    (crossed,) = call(
+        functools.partial(far_kernel, group, samples, last),
+        "far",
+        [jax.ShapeDtypeStruct((share, width), bf16)],
+        [where] + arrived[:each],
+        "s" + "v" * each,
+    )
+    parts_of_block = call(
+        functools.partial(near_kernel, group, samples, last),
+        "near",
+        [jax.ShapeDtypeStruct((mesh_rows, width), bf16)] * group,
+        [where, crossed] + arrived[each:] + list(second),
+        "s" + "v" * (1 + 2 * each),
+    )
+    handed = [parts_of_block[0]]
     for steps in range(1, group):
-        handed.append(change_lane(block[steps * mesh_rows : (steps + 1) * mesh_rows], steps))
+        handed.append(change_lane(parts_of_block[steps], steps))
     (prediction,) = call(
         decode_kernel,
         "decode",
         [jax.ShapeDtypeStruct((channels, grid_rows), bf16)],
-        [lane.reshape(1), ready, table, w_decode, w_output.T] + handed,
+        [where, ready, table, w_decode, w_output.T] + handed,
         "svvvv" + "v" * group,
         [pltpu.VMEM((mesh_rows, width), bf16)],
     )

time: 77 us -> 70.8 us (0.919)
  the two profiles are of different devices: /device:TPU:5 before, /device:TPU:3 now
where the time goes in v8:
time: 70.8 us; the launch traced here: 70.6 us
  starting transfers between devices  43.6 us (62%)
  Pallas kernels  12.7 us (18%)
  waiting for transfers between devices  10.4 us (15%)
  local copies, waits for them, and re-layouts  3.46 us (5%)
    ppermute x11, starting transfers between devices, send(): lax.ppermute(value, ('segment', 'dom'), every_device(pairs, segments * pa...  30.3 us
    pallas_call x20, Pallas kernels, call(): pl.pallas_call(kernel, out_shape=shapes, in_specs=[kinds[place] for place...  12.7 us
    ppermute x2, starting transfers between devices, change_lane(): return lax.ppermute(value, 'dom', pairs)  9.61 us
    ppermute x11, waiting for transfers between devices, send(): lax.ppermute(value, ('segment', 'dom'), every_device(pairs, segments * pa...  5.73 us
    ppermute x3, starting transfers between devices, to_chip(): return lax.ppermute(value, 'dom', pairs)  3.67 us
    unnamed x23, local copies, waits for them, and re-layouts  3.46 us
    ppermute x3, waiting for transfers between devices, to_chip(): return lax.ppermute(value, 'dom', pairs)  2.54 us
    ppermute x2, waiting for transfers between devices, change_lane(): return lax.ppermute(value, 'dom', pairs)  2.16 us
  transfers between devices with their start and end apart: 16, of which 6 were waited for; matrix products, arithmetic and copies ran while one was open for 1% of the time, Pallas kernels for 14%

profile of v8, /device:TPU:3, one launch (start us, length us, event | category | flops | bytes accessed | tf_op | source)
XLA Modules:
  0.0 70.6 jit_solution(14332880710712259588)
XLA Ops:
  0.0 0.1 pad_add_fusion.2.where
  0.1 0.7 collective-permute-start.8
  0.8 0.1 collective-permute-start.10
  0.9 1.0 %copy.15 = bf16[4,128,227]{1,2,0:T(8,128)(2,1)S(1)} copy(bf16[4,128,227]{1,0,2:T(4,128)(2,1)} %param.12) | data formatting | bytes 464896 | tf_op args[0]
  1.9 1.2 %encode.1 = (bf16[80,512]{1,0:T(8,128)(2,1)S(1)}, bf16[80,512]{1,0:T(8,128)(2,1)S(1)}, bf16[80,512]{1,0:T(8,128)(2,1)S(1)}, bf16[80,512]{1,0:T(8,128)(2,1)S(1)}) custom-call(s32[2]{0:T(128)S(1)} %pad_add_fusion.2.where, bf16[4,227,128]{2,1,0:T(8,128)(2,1)S(1)} %bitcast.13, bf16[227,512]{1,0:T(8,128)(2,1)S(1)} %copy-done.3, s32[14,128]{1,0:T(8,128)S(1)} %pad_add_fusion.packed), custom_call_target="tpu_custom_call" | custom-call | bytes 799752 | tf_op jit(solution)/shard_map/encode/pallas_call | solution.py:418
  3.2 1.4 %collective-permute-start = (bf16[80,512]{1,0:T(8,128)(2,1)S(1)}, bf16[80,512]{1,0:T(8,128)(2,1)S(1)}, u32[]{:S(2)}, u32[]{:S(2)}) collective-permute-start(bf16[80,512]{1,0:T(8,128)(2,1)S(1)} %get-tuple-element.50), channel_id=1, source_target_pairs={{0,2},{1,3},{2,0},{3,1},{4,6},{5,7},{6,4},{7,5},{8,10},{9,11},{10,... | collective-permute-start | bytes 245768 | tf_op jit(solution)/shard_map/ppermute | solution.py:486
  4.5 2.3 %collective-permute-start.1 = (bf16[80,512]{1,0:T(8,128)(2,1)S(1)}, bf16[80,512]{1,0:T(8,128)(2,1)S(1)}, u32[]{:S(2)}, u32[]{:S(2)}) collective-permute-start(bf16[80,512]{1,0:T(8,128)(2,1)S(1)} %get-tuple-element.51), channel_id=1, source_target_pairs={{0,4},{1,5},{2,6},{3,7},{4,0},{5,1},{6,2},{7,3},{8,12},{9,13},{10,... | collective-permute-start | bytes 245768 | tf_op jit(solution)/shard_map/ppermute | solution.py:486
  6.8 1.2 %copy-done.1 = bf16[1,512,1024]{2,1,0:T(8,128)(2,1)S(1)} copy-done((bf16[1,512,1024]{2,1,0:T(8,128)(2,1)S(1)}, bf16[1,512,1024]{2,1,0:T(8,128)(2,1)}, u32[]{:S(2)}) %copy-start.1) | copy-done | bytes 1048600
  8.1 1.2 %copy-done.2 = bf16[1,1024,512]{2,1,0:T(8,128)(2,1)S(1)} copy-done((bf16[1,1024,512]{2,1,0:T(8,128)(2,1)S(1)}, bf16[1,1024,512]{2,1,0:T(8,128)(2,1)}, u32[]{:S(2)}) %copy-start.2) | copy-done | bytes 1048600
  9.3 0.2 hold.1
  9.5 0.0 collective-permute-done.refs_1_
  9.5 0.0 collective-permute-done.1.refs_2_
  9.5 2.5 %collective-permute-done.2.refs_3_ = bf16[80,512]{1,0:T(8,128)(2,1)S(1)} collective-permute-done((bf16[80,512]{1,0:T(8,128)(2,1)S(1)}, bf16[80,512]{1,0:T(8,128)(2,1)S(1)}, u32[]{:S(2)}, u32[]{:S(2)}) %collective-permute-start.2) | collective-permute-done | bytes 81952 | tf_op jit(solution)/shard_map/ppermute | solution.py:486
  12.1 2.7 %collective-permute-start.3 = (bf16[320,512]{1,0:T(8,128)(2,1)S(1)}, bf16[320,512]{1,0:T(8,128)(2,1)S(1)}, u32[]{:S(2)}, u32[]{:S(2)}) collective-permute-start(bf16[320,512]{1,0:T(8,128)(2,1)S(1)} %join.1.refs_0_), channel_id=1, source_target_pairs={{0,1},{1,0},{2,3},{3,2},{4,5},{5,4},{6,7},{7,6},{8,9},{9,8},{10,11... | collective-permute-start | bytes 983048 | tf_op jit(solution)/shard_map/ppermute | solution.py:490
  14.8 1.3 %collective-permute-done.3.refs_1_ = bf16[320,512]{1,0:T(8,128)(2,1)S(1)} collective-permute-done((bf16[320,512]{1,0:T(8,128)(2,1)S(1)}, bf16[320,512]{1,0:T(8,128)(2,1)S(1)}, u32[]{:S(2)}, u32[]{:S(2)}) %collective-permute-start.3) | collective-permute-done | bytes 327712 | tf_op jit(solution)/shard_map/ppermute | solution.py:490
  16.0 0.6 index.1
  16.6 0.6 sender.4.sender_low
  17.1 0.6 first.4
  17.7 0.3 collective-permute-start.4
  18.0 0.6 second.4
  18.6 0.0 copy-start.6
  18.6 4.1 %collective-permute-start.5 = (bf16[256,512]{1,0:T(8,128)(2,1)S(1)}, bf16[256,512]{1,0:T(8,128)(2,1)S(1)}, u32[]{:S(2)}, u32[]{:S(2)}) collective-permute-start(bf16[256,512]{1,0:T(8,128)(2,1)S(1)} %second.4), channel_id=1, source_target_pairs={{0,8},{1,0},{2,10},{3,2},{4,12},{5,4},{6,14},{7,6},{8,9},{9,1},{10... | collective-permute-start | bytes 786440 | tf_op jit(solution)/shard_map/ppermute | solution.py:482
  22.7 0.0 collective-permute-start.9
  22.7 0.9 %prepare.1 = (f32[128,512]{1,0:T(8,128)S(1)}, bf16[64,128]{1,0:T(8,128)(2,1)S(1)}) custom-call(s32[2]{0:T(128)S(1)} %pad_add_fusion.2.where, bf16[4,227,128]{2,1,0:T(8,128)(2,1)S(1)} %bitcast.14, bf16[227,512]{1,0:T(8,128)(2,1)S(1)} %copy-done.3, bf16[1024,512]{1,0:T(8,128)(2,1)S(1)} %copy-done, s32[1,128]{1,0:T(1,128)S(1)} %bitcast.16), custom_call_target="tpu_custom_call" | custom-call | bytes 1792520 | tf_op jit(solution)/shard_map/prepare/pallas_call | solution.py:418
  23.6 0.6 sender.5.sender_low
  24.2 1.8 %collective-permute-done.5.high = bf16[256,512]{1,0:T(8,128)(2,1)S(1)} collective-permute-done((bf16[256,512]{1,0:T(8,128)(2,1)S(1)}, bf16[256,512]{1,0:T(8,128)(2,1)S(1)}, u32[]{:S(2)}, u32[]{:S(2)}) %collective-permute-start.5) | collective-permute-done | bytes 262176 | tf_op jit(solution)/shard_map/ppermute | solution.py:482
  26.0 0.6 first.5
  26.5 7.4 %collective-permute-start.6 = (bf16[256,512]{1,0:T(8,128)(2,1)S(1)}, bf16[256,512]{1,0:T(8,128)(2,1)S(1)}, u32[]{:S(2)}, u32[]{:S(2)}) collective-permute-start(bf16[256,512]{1,0:T(8,128)(2,1)S(1)} %get-tuple-element.66), channel_id=1, source_target_pairs={{0,1},{1,0},{2,3},{3,2},{4,5},{5,4},{6,7},{7,6},{8,16},{9,8},{10,1... | collective-permute-start | bytes 786440 | tf_op jit(solution)/shard_map/ppermute | solution.py:482
  33.9 0.7 %second.5 = bf16[256,512]{1,0:T(8,128)(2,1)S(1)} custom-call(s32[2]{0:T(128)S(1)} %pad_add_fusion.2.where, f32[512,128]{1,0:T(8,128)S(1)} %get-tuple-element.53.columns, bf16[512,512]{1,0:T(8,128)(2,1)S(1)} %get-tuple-element.67.sender, bf16[256,512]{1,0:T(8,128)(2,1)S(1)} %collective-permute-done.4.low, bf16[256,512]{1,0:T(8,128)(2,1)S(1)} %collective-permute-done.5.high, ...), custom_call_target="tpu_custom_call" | custom-call | bytes 4194312 | tf_op jit(solution)/shard_map/second/pallas_call | solution.py:418
  34.7 3.0 %collective-permute-start.7 = (bf16[256,512]{1,0:T(8,128)(2,1)S(1)}, bf16[256,512]{1,0:T(8,128)(2,1)S(1)}, u32[]{:S(2)}, u32[]{:S(2)}) collective-permute-start(bf16[256,512]{1,0:T(8,128)(2,1)S(1)} %second.5), channel_id=1, source_target_pairs={{0,1},{1,0},{2,3},{3,2},{4,5},{5,4},{6,7},{7,6},{8,16},{9,8},{10,1... | collective-permute-start | bytes 786440 | tf_op jit(solution)/shard_map/ppermute | solution.py:482
  37.7 0.0 collective-permute-done.6.low
  37.7 0.6 sender.6.sender_low
  38.3 2.6 %collective-permute-done.7.high = bf16[256,512]{1,0:T(8,128)(2,1)S(1)} collective-permute-done((bf16[256,512]{1,0:T(8,128)(2,1)S(1)}, bf16[256,512]{1,0:T(8,128)(2,1)S(1)}, u32[]{:S(2)}, u32[]{:S(2)}) %collective-permute-start.7) | collective-permute-done | bytes 262176 | tf_op jit(solution)/shard_map/ppermute | solution.py:482
  40.9 0.6 first.6
  41.4 0.6 second.6.high
  42.0 0.6 sender.7.sender_low
  42.6 0.6 first.7
  43.1 0.8 %collective-permute-start.11 = (bf16[128,512]{1,0:T(8,128)(2,1)S(1)}, bf16[128,512]{1,0:T(8,128)(2,1)S(1)}, u32[]{:S(2)}, u32[]{:S(2)}) collective-permute-start(bf16[128,512]{1,0:T(8,128)(2,1)S(1)} %get-tuple-element.70), channel_id=1, source_target_pairs={{0,1},{1,0},{2,3},{3,2},{4,5},{5,21},{6,7},{7,6},{8,9},{9,8},{10,1... | collective-permute-start | bytes 393224 | tf_op jit(solution)/shard_map/ppermute | solution.py:482
  43.9 0.1 collective-permute-start.12
  44.0 0.6 second.7
  44.6 13.8 %collective-permute-start.13 = (bf16[128,512]{1,0:T(8,128)(2,1)S(1)}, bf16[128,512]{1,0:T(8,128)(2,1)S(1)}, u32[]{:S(2)}, u32[]{:S(2)}) collective-permute-start(bf16[128,512]{1,0:T(8,128)(2,1)S(1)} %get-tuple-element.73.refs_2_), channel_id=1, source_target_pairs={{0,1},{1,17},{2,3},{3,2},{4,5},{5,4},{6,7},{7,6},{8,9},{9,19},{10,... | collective-permute-start | bytes 393224 | tf_op jit(solution)/shard_map/ppermute | solution.py:482
  58.4 0.6 far.1.crossed
  59.0 0.0 copy-start.5
  59.0 1.4 %collective-permute-done.13.refs_0_ = bf16[128,512]{1,0:T(8,128)(2,1)S(1)} collective-permute-done((bf16[128,512]{1,0:T(8,128)(2,1)S(1)}, bf16[128,512]{1,0:T(8,128)(2,1)S(1)}, u32[]{:S(2)}, u32[]{:S(2)}) %collective-permute-start.13) | collective-permute-done | bytes 131104 | tf_op jit(solution)/shard_map/ppermute | solution.py:482
  60.3 0.6 near.1
  60.9 6.9 %collective-permute-start.15 = (bf16[64,512]{1,0:T(8,128)(2,1)S(1)}, bf16[64,512]{1,0:T(8,128)(2,1)S(1)}, u32[]{:S(2)}, u32[]{:S(2)}) collective-permute-start(bf16[64,512]{1,0:T(8,128)(2,1)S(1)} %get-tuple-element.76), channel_id=1, source_target_pairs={{0,1},{1,0},{2,3},{3,2},{4,5},{5,4},{6,7},{7,6},{8,9},{9,8},{10,11... | collective-permute-start | bytes 196616 | tf_op jit(solution)/shard_map/ppermute | solution.py:490
  67.9 0.9 %collective-permute-done.15.refs_1_ = bf16[64,512]{1,0:T(8,128)(2,1)S(1)} collective-permute-done((bf16[64,512]{1,0:T(8,128)(2,1)S(1)}, bf16[64,512]{1,0:T(8,128)(2,1)S(1)}, u32[]{:S(2)}, u32[]{:S(2)}) %collective-permute-start.15) | collective-permute-done | bytes 65568 | tf_op jit(solution)/shard_map/ppermute | solution.py:490
  68.8 1.8 %decode.1 = bf16[227,128]{1,0:T(8,128)(2,1)} custom-call(s32[2]{0:T(128)S(1)} %pad_add_fusion.2.where, f32[128,512]{1,0:T(8,128)S(1)} %get-tuple-element.62.ready, bf16[64,128]{1,0:T(8,128)(2,1)S(1)} %get-tuple-element.63.table, bf16[1024,512]{1,0:T(8,128)(2,1)S(1)} %copy-done, bf16[227,512]{1,0:T(8,128)(2,1)S(1)} %bitcast.15, ...), custom_call_target="tpu_custom_call" | custom-call | bytes 1748744 | tf_op jit(solution)/shard_map/decode/pallas_call | solution.py:418
  (29 shorter events, 0.1 us)
Async XLA Ops:
  0.0 1.8 %copy-start.7 = (s32[64,8]{0,1:T(8,128)S(1)}, s32[64,8]{0,1:T(8,128)}, u32[]{:S(2)}) copy-start(s32[64,8]{0,1:T(8,128)} %param.21) | copy-start | bytes 6148
  0.0 1.8 %copy-start.8 = (s32[4,64]{1,0:T(4,128)S(1)}, s32[4,64]{1,0:T(4,128)}, u32[]{:S(2)}) copy-start(s32[4,64]{1,0:T(4,128)} %param.22) | copy-start | bytes 3076
  0.0 1.9 %copy-start.9 = (s32[4,1]{0,1:T(1,128)S(1)}, s32[4,1]{0,1:T(1,128)}, u32[]{:S(2)}) copy-start(s32[4,1]{0,1:T(1,128)} %param.23) | copy-start | bytes 52
  0.0 1.9 %copy-start.10 = (s32[128]{0:T(128)S(1)}, s32[128]{0:T(128)}, u32[]{:S(2)}) copy-start(s32[128]{0:T(128)} %param.19) | copy-start | bytes 1540
  0.1 1.8 %copy-start.3 = (bf16[227,512]{1,0:T(8,128)(2,1)S(1)}, bf16[227,512]{1,0:T(8,128)(2,1)}, u32[]{:S(2)}) copy-start(bf16[227,512]{1,0:T(8,128)(2,1)} %w_embed.3) | copy-start | bytes 697348
  0.1 6.7 %copy-start.4 = (bf16[1,512,512]{2,1,0:T(8,128)(2,1)S(1)}, bf16[1,512,512]{2,1,0:T(8,128)(2,1)}, u32[]{:S(2)}) copy-start(bf16[1,512,512]{2,1,0:T(8,128)(2,1)} %refs_1_) | copy-start | bytes 1572868
  0.1 41.9 %collective-permute-start.8 = (bf16[1,512,1024]{2,1,0:T(8,128)(2,1)}, bf16[1,512,1024]{2,1,0:T(8,128)(2,1)S(1)}, u32[]{:S(2)}, u32[]{:S(2)}) collective-permute-start(bf16[1,512,1024]{2,1,0:T(8,128)(2,1)} %refs_0_), channel_id=1, source_target_pairs={{0,1},{1,0},{2,3},{3,2},{4,5},{5,4},{6,7},{7,6},{8,9},{9,8},{10,11... | collective-permute-start | bytes 3145736 | tf_op jit(solution)/shard_map/ppermute | solution.py:482
  0.8 41.8 %collective-permute-start.10 = (bf16[1,1024,512]{2,1,0:T(8,128)(2,1)}, bf16[1,1024,512]{2,1,0:T(8,128)(2,1)S(1)}, u32[]{:S(2)}, u32[]{:S(2)}) collective-permute-start(bf16[1,1024,512]{2,1,0:T(8,128)(2,1)} %refs_2_), channel_id=1, source_target_pairs={{0,1},{1,0},{2,3},{3,2},{4,5},{5,4},{6,7},{7,6},{8,9},{9,8},{10,11... | collective-permute-start | bytes 3145736 | tf_op jit(solution)/shard_map/ppermute | solution.py:482
  3.2 6.3 %collective-permute-start = (bf16[80,512]{1,0:T(8,128)(2,1)S(1)}, bf16[80,512]{1,0:T(8,128)(2,1)S(1)}, u32[]{:S(2)}, u32[]{:S(2)}) collective-permute-start(bf16[80,512]{1,0:T(8,128)(2,1)S(1)} %get-tuple-element.50), channel_id=1, source_target_pairs={{0,2},{1,3},{2,0},{3,1},{4,6},{5,7},{6,4},{7,5},{8,10},{9,11},{10,... | collective-permute-start | bytes 245768 | tf_op jit(solution)/shard_map/ppermute | solution.py:486
  4.5 5.0 %collective-permute-start.1 = (bf16[80,512]{1,0:T(8,128)(2,1)S(1)}, bf16[80,512]{1,0:T(8,128)(2,1)S(1)}, u32[]{:S(2)}, u32[]{:S(2)}) collective-permute-start(bf16[80,512]{1,0:T(8,128)(2,1)S(1)} %get-tuple-element.51), channel_id=1, source_target_pairs={{0,4},{1,5},{2,6},{3,7},{4,0},{5,1},{6,2},{7,3},{8,12},{9,13},{10,... | collective-permute-start | bytes 245768 | tf_op jit(solution)/shard_map/ppermute | solution.py:486
  6.8 5.2 %collective-permute-start.2 = (bf16[80,512]{1,0:T(8,128)(2,1)S(1)}, bf16[80,512]{1,0:T(8,128)(2,1)S(1)}, u32[]{:S(2)}, u32[]{:S(2)}) collective-permute-start(bf16[80,512]{1,0:T(8,128)(2,1)S(1)} %get-tuple-element.52), channel_id=1, source_target_pairs={{0,6},{1,7},{2,4},{3,5},{4,2},{5,3},{6,0},{7,1},{8,14},{9,15},{10,... | collective-permute-start | bytes 245768 | tf_op jit(solution)/shard_map/ppermute | solution.py:486
  6.8 1.2 %copy-start.1 = (bf16[1,512,1024]{2,1,0:T(8,128)(2,1)S(1)}, bf16[1,512,1024]{2,1,0:T(8,128)(2,1)}, u32[]{:S(2)}) copy-start(bf16[1,512,1024]{2,1,0:T(8,128)(2,1)} %refs_0_) | copy-start | bytes 3145732
  8.1 1.2 %copy-start.2 = (bf16[1,1024,512]{2,1,0:T(8,128)(2,1)S(1)}, bf16[1,1024,512]{2,1,0:T(8,128)(2,1)}, u32[]{:S(2)}) copy-start(bf16[1,1024,512]{2,1,0:T(8,128)(2,1)} %refs_2_) | copy-start | bytes 3145732
  12.1 3.9 %collective-permute-start.3 = (bf16[320,512]{1,0:T(8,128)(2,1)S(1)}, bf16[320,512]{1,0:T(8,128)(2,1)S(1)}, u32[]{:S(2)}, u32[]{:S(2)}) collective-permute-start(bf16[320,512]{1,0:T(8,128)(2,1)S(1)} %join.1.refs_0_), channel_id=1, source_target_pairs={{0,1},{1,0},{2,3},{3,2},{4,5},{5,4},{6,7},{7,6},{8,9},{9,8},{10,11... | collective-permute-start | bytes 983048 | tf_op jit(solution)/shard_map/ppermute | solution.py:490
  17.7 5.9 %collective-permute-start.4 = (bf16[256,512]{1,0:T(8,128)(2,1)S(1)}, bf16[256,512]{1,0:T(8,128)(2,1)S(1)}, u32[]{:S(2)}, u32[]{:S(2)}) collective-permute-start(bf16[256,512]{1,0:T(8,128)(2,1)S(1)} %get-tuple-element.59), channel_id=1, source_target_pairs={{0,8},{1,0},{2,10},{3,2},{4,12},{5,4},{6,14},{7,6},{8,9},{9,1},{10... | collective-permute-start | bytes 786440 | tf_op jit(solution)/shard_map/ppermute | solution.py:482
  18.0 4.7 %copy-start = (bf16[1024,512]{1,0:T(8,128)(2,1)S(1)}, bf16[1024,512]{1,0:T(8,128)(2,1)}, u32[]{:S(2)}) copy-start(bf16[1024,512]{1,0:T(8,128)(2,1)} %w_decode.3) | copy-start | bytes 3145732
  18.6 4.1 %copy-start.6 = (s32[128]{0:T(128)S(1)}, s32[128]{0:T(128)}, u32[]{:S(2)}) copy-start(s32[128]{0:T(128)} %param.20) | copy-start | bytes 1540
  18.6 7.4 %collective-permute-start.5 = (bf16[256,512]{1,0:T(8,128)(2,1)S(1)}, bf16[256,512]{1,0:T(8,128)(2,1)S(1)}, u32[]{:S(2)}, u32[]{:S(2)}) collective-permute-start(bf16[256,512]{1,0:T(8,128)(2,1)S(1)} %second.4), channel_id=1, source_target_pairs={{0,8},{1,0},{2,10},{3,2},{4,12},{5,4},{6,14},{7,6},{8,9},{9,1},{10... | collective-permute-start | bytes 786440 | tf_op jit(solution)/shard_map/ppermute | solution.py:482
  22.7 19.9 %collective-permute-start.9 = (bf16[1,512,512]{2,1,0:T(8,128)(2,1)S(1)}, bf16[1,512,512]{2,1,0:T(8,128)(2,1)S(1)}, u32[]{:S(2)}, u32[]{:S(2)}) collective-permute-start(bf16[1,512,512]{2,1,0:T(8,128)(2,1)S(1)} %copy-done.4), channel_id=1, source_target_pairs={{0,1},{1,0},{2,3},{3,2},{4,5},{5,4},{6,7},{7,6},{8,9},{9,8},{10,11... | collective-permute-start | bytes 1572872 | tf_op jit(solution)/shard_map/ppermute | solution.py:482
  26.5 11.2 %collective-permute-start.6 = (bf16[256,512]{1,0:T(8,128)(2,1)S(1)}, bf16[256,512]{1,0:T(8,128)(2,1)S(1)}, u32[]{:S(2)}, u32[]{:S(2)}) collective-permute-start(bf16[256,512]{1,0:T(8,128)(2,1)S(1)} %get-tuple-element.66), channel_id=1, source_target_pairs={{0,1},{1,0},{2,3},{3,2},{4,5},{5,4},{6,7},{7,6},{8,16},{9,8},{10,1... | collective-permute-start | bytes 786440 | tf_op jit(solution)/shard_map/ppermute | solution.py:482
  34.7 6.2 %collective-permute-start.7 = (bf16[256,512]{1,0:T(8,128)(2,1)S(1)}, bf16[256,512]{1,0:T(8,128)(2,1)S(1)}, u32[]{:S(2)}, u32[]{:S(2)}) collective-permute-start(bf16[256,512]{1,0:T(8,128)(2,1)S(1)} %second.5), channel_id=1, source_target_pairs={{0,1},{1,0},{2,3},{3,2},{4,5},{5,4},{6,7},{7,6},{8,16},{9,8},{10,1... | collective-permute-start | bytes 786440 | tf_op jit(solution)/shard_map/ppermute | solution.py:482
  43.1 15.3 %collective-permute-start.11 = (bf16[128,512]{1,0:T(8,128)(2,1)S(1)}, bf16[128,512]{1,0:T(8,128)(2,1)S(1)}, u32[]{:S(2)}, u32[]{:S(2)}) collective-permute-start(bf16[128,512]{1,0:T(8,128)(2,1)S(1)} %get-tuple-element.70), channel_id=1, source_target_pairs={{0,1},{1,0},{2,3},{3,2},{4,5},{5,21},{6,7},{7,6},{8,9},{9,8},{10,1... | collective-permute-start | bytes 393224 | tf_op jit(solution)/shard_map/ppermute | solution.py:482
  43.9 14.5 %collective-permute-start.12 = (bf16[128,512]{1,0:T(8,128)(2,1)S(1)}, bf16[128,512]{1,0:T(8,128)(2,1)S(1)}, u32[]{:S(2)}, u32[]{:S(2)}) collective-permute-start(bf16[128,512]{1,0:T(8,128)(2,1)S(1)} %get-tuple-element.71), channel_id=1, source_target_pairs={{0,1},{1,0},{2,3},{3,2},{4,5},{5,4},{6,7},{7,17},{8,9},{9,8},{10,1... | collective-permute-start | bytes 393224 | tf_op jit(solution)/shard_map/ppermute | solution.py:482
  44.6 15.8 %collective-permute-start.13 = (bf16[128,512]{1,0:T(8,128)(2,1)S(1)}, bf16[128,512]{1,0:T(8,128)(2,1)S(1)}, u32[]{:S(2)}, u32[]{:S(2)}) collective-permute-start(bf16[128,512]{1,0:T(8,128)(2,1)S(1)} %get-tuple-element.73.refs_2_), channel_id=1, source_target_pairs={{0,1},{1,17},{2,3},{3,2},{4,5},{5,4},{6,7},{7,6},{8,9},{9,19},{10,... | collective-permute-start | bytes 393224 | tf_op jit(solution)/shard_map/ppermute | solution.py:482
  58.4 2.0 %collective-permute-start.14 = (bf16[128,512]{1,0:T(8,128)(2,1)S(1)}, bf16[128,512]{1,0:T(8,128)(2,1)S(1)}, u32[]{:S(2)}, u32[]{:S(2)}) collective-permute-start(bf16[128,512]{1,0:T(8,128)(2,1)S(1)} %get-tuple-element.74.refs_3_), channel_id=1, source_target_pairs={{0,1},{1,0},{2,3},{3,17},{4,5},{5,4},{6,7},{7,6},{8,9},{9,8},{10,1... | collective-permute-start | bytes 393224 | tf_op jit(solution)/shard_map/ppermute | solution.py:482
  59.0 9.8 %copy-start.5 = (bf16[512,227]{0,1:T(8,128)(2,1)S(1)}, bf16[512,227]{0,1:T(8,128)(2,1)}, u32[]{:S(2)}) copy-start(bf16[512,227]{0,1:T(8,128)(2,1)} %param.18) | copy-start | bytes 697348
  60.9 7.8 %collective-permute-start.15 = (bf16[64,512]{1,0:T(8,128)(2,1)S(1)}, bf16[64,512]{1,0:T(8,128)(2,1)S(1)}, u32[]{:S(2)}, u32[]{:S(2)}) collective-permute-start(bf16[64,512]{1,0:T(8,128)(2,1)S(1)} %get-tuple-element.76), channel_id=1, source_target_pairs={{0,1},{1,0},{2,3},{3,2},{4,5},{5,4},{6,7},{7,6},{8,9},{9,8},{10,11... | collective-permute-start | bytes 196616 | tf_op jit(solution)/shard_map/ppermute | solution.py:490

commit v9 on v8

--- a/solution.py
+++ b/solution.py
@@ -257,7 +257,10 @@
                 picked = jnp.where(picked == mesh_rows, parts * mesh_rows, source * mesh_rows + picked)
                 found = jnp.where(block == list_index + 1, picked, found)
             index_out[:fanout, part * mesh_rows : (part + 1) * mesh_rows] = found[:, :mesh_rows]
-        columns_out[...] = jnp.transpose(index_out[...].astype(jnp.float32))
+        tile = min(nodes, 256)
+        for number in range(1, nodes // tile):
+            index_out[number * fanout : (number + 1) * fanout, :] = index_out[:fanout, :] - number * tile
+        columns_out[...] = jnp.transpose(index_out[...].astype(jnp.float32)).astype(jnp.bfloat16)
 
 
 def hold_kernel(*refs):
@@ -269,14 +272,19 @@
 def renew(fanout, columns, sender, own, w_project, w_message, w_update):
     chunk, width = own.shape
     nodes = sender.shape[0]
-    names = lax.broadcasted_iota(jnp.int32, (chunk, nodes), 1).astype(jnp.float32)
-    receiver = matmul(own, w_project[0, :, :width])
+    tile = min(nodes, 256)
+    names = lax.broadcasted_iota(jnp.int32, (chunk, tile), 1).astype(jnp.float32).astype(jnp.bfloat16)
+    one_half = jnp.full((chunk, tile), 0.5, jnp.bfloat16)
+    none = jnp.zeros((chunk, tile), jnp.bfloat16)
+    receiver = 0.5 * matmul(own, w_project[0, :, :width])
     total = jnp.zeros((chunk, width), jnp.float32)
     for k in range(fanout):
-        hit = columns[:, k : k + 1] == names
-        fetched = matmul(jnp.where(hit, 1.0, 0.0).astype(jnp.bfloat16), sender)
-        edge = silu_by_tanh(receiver + fetched).astype(jnp.bfloat16)
-        total = total + edge.astype(jnp.float32)
+        hits = []
+        for number in range(nodes // tile):
+            lane = number * fanout + k
+            hits.append(jnp.where(columns[:, lane : lane + 1] == names, one_half, none))
+        half = receiver + matmul(jnp.concatenate(hits, axis=1), sender)
+        total = total + (half + half * jnp.tanh(half))
     gathered = (total * (1.0 / fanout)).astype(jnp.bfloat16)
     aggregate = matmul(gathered, w_message[0]).astype(jnp.bfloat16)
     update = silu_by_tanh(
@@ -412,19 +420,26 @@
     out[...] = matmul_nt(w_output[...], hidden).astype(jnp.bfloat16)
 
 
-def call(kernel, name, shapes, inputs, places, scratch=(), room=16, flops=0):
-    kinds = {"s": SMEM, "v": VMEM, "h": HBM}
-    moved = sum(value.size * value.dtype.itemsize for value in list(inputs) + list(shapes))
+def call(kernel, name, shapes, inputs, places, scratch=(), room=16):
+    specs, given = [], []
+    for value, place in zip(inputs, places):
+        specs += [SMEM] * 2 if place == "w" else [VMEM if place == "v" else HBM]
+        given += list(value) if place == "w" else [value]
+    moved = sum(value.size * value.dtype.itemsize for value in given + list(shapes))
+
+    def located(segment, place, *refs):
+        kernel((segment[0], place[0]), *refs)
+
     return pl.pallas_call(
-        kernel,
+        located if places[0] == "w" else kernel,
         out_shape=shapes,
-        in_specs=[kinds[place] for place in places],
+        in_specs=specs,
         out_specs=[VMEM] * len(shapes),
         scratch_shapes=list(scratch),
         name=name,
         compiler_params=pltpu.CompilerParams(vmem_limit_bytes=room * 1024 * 1024),
-        cost_estimate=pl.CostEstimate(flops=flops, bytes_accessed=moved, transcendentals=0),
-    )(*inputs)
+        cost_estimate=pl.CostEstimate(flops=0, bytes_accessed=moved, transcendentals=0),
+    )(*given)
 
 
 def every_device(pairs, count, group):
@@ -492,9 +507,10 @@
     def owner(m, at_segment):
         return device(at_segment, m * group)
 
-    where, *weights = lax.optimization_barrier(
-        (jnp.stack([segment, place]).astype(jnp.int32), w_project, w_message, w_update)
-    )
+    own_segment, own_place, *weights = lax.optimization_barrier(
+        (segment.reshape(1), place.reshape(1), w_project, w_message, w_update)
+    )
+    where = (own_segment, own_place)
     last = segments - 2
     pairs = [(owner(m, last + 1), owner(m, last)) for m in range(samples)]
     came_weights = [send(weight, pairs) for weight in weights]
@@ -518,7 +534,7 @@
         "encode",
         [jax.ShapeDtypeStruct((mesh_rows + 2 * fanout, width), bf16)] * samples,
         [where, snapshots, w_embed, packed],
-        "svvv",
+        "wvvv",
         [pltpu.VMEM((samples * grid_rows, width), bf16)],
     )
     held = call(
@@ -545,12 +561,12 @@
         functools.partial(index_kernel, parts, mesh_rows),
         "index",
         [
-            jax.ShapeDtypeStruct((nodes, 128), jnp.float32),
+            jax.ShapeDtypeStruct((nodes, 128), bf16),
             jax.ShapeDtypeStruct((half, width), bf16),
             jax.ShapeDtypeStruct((half, width), bf16),
         ],
         [where] + lanes,
-        "s" + "v" * group,
+        "w" + "v" * group,
         [pltpu.VMEM((128, nodes), jnp.int32)],
     )
     state_shape = jax.ShapeDtypeStruct((half, width), bf16)
@@ -565,14 +581,14 @@
             "sender",
             [state_shape],
             [where, low, used[0]],
-            "svv",
+            "wvv",
         )
         sender, *first = call(
             functools.partial(first_kernel, *role),
             "first",
             [jax.ShapeDtypeStruct((nodes, width), bf16)] + pieces,
             [where, columns, sender_low, low, high] + used,
-            "svvvvvvv",
+            "wvvvvvvv",
             scratch,
         )
         pairs = [(owner(m, layer), owner(m, layer + 1)) for m in range(samples)]
@@ -582,7 +598,7 @@
             "second",
             pieces,
             [where, columns, sender, low, high] + used,
-            "svvvvvvv",
+            "wvvvvvvv",
             scratch,
         )
         low, high = new_low, send(second[0], pairs) if layer < last else second[0]
@@ -595,7 +611,7 @@
                     jax.ShapeDtypeStruct((mesh_rows, grid_rows), bf16),
                 ],
                 [where, snapshots, w_embed, w_decode, mesh_grid.reshape(1, grid_rows)],
-                "svvvv",
+                "wvvvv",
                     )
             low, ready, table = lax.optimization_barrier((low, ready, table))
     each = samples // 2
@@ -611,14 +627,14 @@
         "far",
         [jax.ShapeDtypeStruct((share, width), bf16)],
         [where] + arrived[:each],
-        "s" + "v" * each,
+        "w" + "v" * each,
     )
     parts_of_block = call(
         functools.partial(near_kernel, group, samples, last),
         "near",
         [jax.ShapeDtypeStruct((mesh_rows, width), bf16)] * group,
         [where, crossed] + arrived[each:] + list(second),
-        "s" + "v" * (1 + 2 * each),
+        "w" + "v" * (1 + 2 * each),
     )
     handed = [parts_of_block[0]]
     for steps in range(1, group):
@@ -628,7 +644,7 @@
         "decode",
         [jax.ShapeDtypeStruct((channels, grid_rows), bf16)],
         [where, ready, table, w_decode, w_output.T] + handed,
-        "svvvv" + "v" * group,
+        "wvvvv" + "v" * group,
         [pltpu.VMEM((mesh_rows, width), bf16)],
     )
     return prediction.T.reshape(1, grid_rows, channels)

time: 70.8 us -> 60.5 us (0.85)
  Pallas kernels: 12.7 us -> 2.66 us
  starting transfers between devices: 43.6 us -> 39.5 us
  waiting for transfers between devices: 10.4 us -> 14.4 us
    pallas_call x20, Pallas kernels: 12.7 us -> 2.66 us  [call(): pl.pallas_call(located if places[0] == 'w' else kernel, out_shape=shapes,...]
    ppermute x11, waiting for transfers between devices: 5.73 us -> 9.74 us  [send(): lax.ppermute(value, ('segment', 'dom'), every_device(pairs, segments * pa...]
    ppermute x11, starting transfers between devices: 30.3 us -> 26.3 us  [send(): lax.ppermute(value, ('segment', 'dom'), every_device(pairs, segments * pa...]
  transfers between devices with their start and end apart: 16 -> 16, of which waited for: 6 -> 7; matrix products, arithmetic and copies ran while one was open for 1% -> 2% of each run, Pallas kernels for 14% -> 2%
where the time goes in v9:
time: 60.5 us; the launch traced here: 60.2 us
  starting transfers between devices  39.5 us (65%)
  waiting for transfers between devices  14.4 us (24%)
  local copies, waits for them, and re-layouts  3.46 us (6%)
  Pallas kernels  2.66 us (4%)
    ppermute x11, starting transfers between devices, send(): lax.ppermute(value, ('segment', 'dom'), every_device(pairs, segments * pa...  26.3 us
    ppermute x11, waiting for transfers between devices, send(): lax.ppermute(value, ('segment', 'dom'), every_device(pairs, segments * pa...  9.74 us
    ppermute x2, starting transfers between devices, change_lane(): return lax.ppermute(value, 'dom', pairs)  9.46 us
    ppermute x3, starting transfers between devices, to_chip(): return lax.ppermute(value, 'dom', pairs)  3.67 us
    unnamed x23, local copies, waits for them, and re-layouts  3.46 us
    pallas_call x20, Pallas kernels, call(): pl.pallas_call(located if places[0] == 'w' else kernel, out_shape=shapes,...  2.66 us
    ppermute x3, waiting for transfers between devices, to_chip(): return lax.ppermute(value, 'dom', pairs)  2.54 us
    ppermute x2, waiting for transfers between devices, change_lane(): return lax.ppermute(value, 'dom', pairs)  2.16 us
  transfers between devices with their start and end apart: 16, of which 7 were waited for; matrix products, arithmetic and copies ran while one was open for 2% of the time, Pallas kernels for 2%

profile of v9, /device:TPU:3, one launch (start us, length us, event | category | flops | bytes accessed | tf_op | source)
XLA Modules:
  0.0 60.2 jit_solution(2711653663402138281)
XLA Ops:
  0.0 0.0 copy-start.10
  0.0 0.0 copy-start.3
  0.0 0.0 copy-start.4
  0.0 0.7 %collective-permute-start.8 = (bf16[1,512,1024]{2,1,0:T(8,128)(2,1)}, bf16[1,512,1024]{2,1,0:T(8,128)(2,1)S(1)}, u32[]{:S(2)}, u32[]{:S(2)}) collective-permute-start(bf16[1,512,1024]{2,1,0:T(8,128)(2,1)} %refs_0_), channel_id=1, source_target_pairs={{0,1},{1,0},{2,3},{3,2},{4,5},{5,4},{6,7},{7,6},{8,9},{9,8},{10,11... | collective-permute-start | bytes 3145736 | tf_op jit(solution)/shard_map/ppermute | solution.py:497
  0.8 0.1 collective-permute-start.10
  0.8 1.0 %copy.15 = bf16[4,128,227]{1,2,0:T(8,128)(2,1)S(1)} copy(bf16[4,128,227]{1,0,2:T(4,128)(2,1)} %param.12) | data formatting | bytes 464896 | tf_op args[0]
  1.8 0.0 copy-done.7
  1.8 0.0 copy-done.8
  1.8 0.0 copy-done.9
  1.8 0.0 copy-done.10
  1.9 0.7 %encode.1 = (bf16[80,512]{1,0:T(8,128)(2,1)S(1)}, bf16[80,512]{1,0:T(8,128)(2,1)S(1)}, bf16[80,512]{1,0:T(8,128)(2,1)S(1)}, bf16[80,512]{1,0:T(8,128)(2,1)S(1)}) custom-call(s32[1]{0:T(128)} %bitcast.segment, s32[1]{0:T(128)} %bitcast.1.place, bf16[4,227,128]{2,1,0:T(8,128)(2,1)S(1)} %bitcast.13, bf16[227,512]{1,0:T(8,128)(2,1)S(1)} %copy-done.3, ...), custom_call_target="tpu_custom_call" | custom-call | bytes 799752 | tf_op jit(solution)/shard_map/encode/pallas_call | solution.py:433
  2.6 1.4 %collective-permute-start = (bf16[80,512]{1,0:T(8,128)(2,1)S(1)}, bf16[80,512]{1,0:T(8,128)(2,1)S(1)}, u32[]{:S(2)}, u32[]{:S(2)}) collective-permute-start(bf16[80,512]{1,0:T(8,128)(2,1)S(1)} %get-tuple-element.52), channel_id=1, source_target_pairs={{0,2},{1,3},{2,0},{3,1},{4,6},{5,7},{6,4},{7,5},{8,10},{9,11},{10,... | collective-permute-start | bytes 245768 | tf_op jit(solution)/shard_map/ppermute | solution.py:501
  4.0 2.3 %collective-permute-start.1 = (bf16[80,512]{1,0:T(8,128)(2,1)S(1)}, bf16[80,512]{1,0:T(8,128)(2,1)S(1)}, u32[]{:S(2)}, u32[]{:S(2)}) collective-permute-start(bf16[80,512]{1,0:T(8,128)(2,1)S(1)} %get-tuple-element.53), channel_id=1, source_target_pairs={{0,4},{1,5},{2,6},{3,7},{4,0},{5,1},{6,2},{7,3},{8,12},{9,13},{10,... | collective-permute-start | bytes 245768 | tf_op jit(solution)/shard_map/ppermute | solution.py:501
  6.3 0.0 collective-permute-start.2
  6.3 1.2 %copy-done.1 = bf16[1,512,1024]{2,1,0:T(8,128)(2,1)S(1)} copy-done((bf16[1,512,1024]{2,1,0:T(8,128)(2,1)S(1)}, bf16[1,512,1024]{2,1,0:T(8,128)(2,1)}, u32[]{:S(2)}) %copy-start.1) | copy-done | bytes 1048600
  7.5 1.2 %copy-done.2 = bf16[1,1024,512]{2,1,0:T(8,128)(2,1)S(1)} copy-done((bf16[1,1024,512]{2,1,0:T(8,128)(2,1)S(1)}, bf16[1,1024,512]{2,1,0:T(8,128)(2,1)}, u32[]{:S(2)}) %copy-start.2) | copy-done | bytes 1048600
  8.7 0.2 hold.1
  8.9 0.0 collective-permute-done.refs_1_
  9.0 0.0 collective-permute-done.1.refs_2_
  9.0 2.5 %collective-permute-done.2.refs_3_ = bf16[80,512]{1,0:T(8,128)(2,1)S(1)} collective-permute-done((bf16[80,512]{1,0:T(8,128)(2,1)S(1)}, bf16[80,512]{1,0:T(8,128)(2,1)S(1)}, u32[]{:S(2)}, u32[]{:S(2)}) %collective-permute-start.2) | collective-permute-done | bytes 81952 | tf_op jit(solution)/shard_map/ppermute | solution.py:501
  11.5 2.7 %collective-permute-start.3 = (bf16[320,512]{1,0:T(8,128)(2,1)S(1)}, bf16[320,512]{1,0:T(8,128)(2,1)S(1)}, u32[]{:S(2)}, u32[]{:S(2)}) collective-permute-start(bf16[320,512]{1,0:T(8,128)(2,1)S(1)} %join.1.refs_0_), channel_id=1, source_target_pairs={{0,1},{1,0},{2,3},{3,2},{4,5},{5,4},{6,7},{7,6},{8,9},{9,8},{10,11... | collective-permute-start | bytes 983048 | tf_op jit(solution)/shard_map/ppermute | solution.py:505
  14.2 1.3 %collective-permute-done.3.refs_1_ = bf16[320,512]{1,0:T(8,128)(2,1)S(1)} collective-permute-done((bf16[320,512]{1,0:T(8,128)(2,1)S(1)}, bf16[320,512]{1,0:T(8,128)(2,1)S(1)}, u32[]{:S(2)}, u32[]{:S(2)}) %collective-permute-start.3) | collective-permute-done | bytes 327712 | tf_op jit(solution)/shard_map/ppermute | solution.py:505
  15.5 0.3 collective-permute-start.4
  15.7 3.8 %collective-permute-start.5 = (bf16[256,512]{1,0:T(8,128)(2,1)S(1)}, bf16[256,512]{1,0:T(8,128)(2,1)S(1)}, u32[]{:S(2)}, u32[]{:S(2)}) collective-permute-start(bf16[256,512]{1,0:T(8,128)(2,1)S(1)} %second.4), channel_id=1, source_target_pairs={{0,8},{1,0},{2,10},{3,2},{4,12},{5,4},{6,14},{7,6},{8,9},{9,1},{10... | collective-permute-start | bytes 786440 | tf_op jit(solution)/shard_map/ppermute | solution.py:497
  19.5 0.0 collective-permute-start.9
  19.5 0.0 copy-done
  19.5 0.4 prepare.1
  19.9 0.0 collective-permute-done.4.refs_0_.refs_2_
  19.9 2.9 %collective-permute-done.5.refs_3_ = bf16[256,512]{1,0:T(8,128)(2,1)S(1)} collective-permute-done((bf16[256,512]{1,0:T(8,128)(2,1)S(1)}, bf16[256,512]{1,0:T(8,128)(2,1)S(1)}, u32[]{:S(2)}, u32[]{:S(2)}) %collective-permute-start.5) | collective-permute-done | bytes 262176 | tf_op jit(solution)/shard_map/ppermute | solution.py:497
  22.8 6.9 %collective-permute-start.6 = (bf16[256,512]{1,0:T(8,128)(2,1)S(1)}, bf16[256,512]{1,0:T(8,128)(2,1)S(1)}, u32[]{:S(2)}, u32[]{:S(2)}) collective-permute-start(bf16[256,512]{1,0:T(8,128)(2,1)S(1)} %get-tuple-element.68), channel_id=1, source_target_pairs={{0,1},{1,0},{2,3},{3,2},{4,5},{5,4},{6,7},{7,6},{8,16},{9,8},{10,1... | collective-permute-start | bytes 786440 | tf_op jit(solution)/shard_map/ppermute | solution.py:497
  29.7 2.7 %collective-permute-start.7 = (bf16[256,512]{1,0:T(8,128)(2,1)S(1)}, bf16[256,512]{1,0:T(8,128)(2,1)S(1)}, u32[]{:S(2)}, u32[]{:S(2)}) collective-permute-start(bf16[256,512]{1,0:T(8,128)(2,1)S(1)} %second.5), channel_id=1, source_target_pairs={{0,1},{1,0},{2,3},{3,2},{4,5},{5,4},{6,7},{7,6},{8,16},{9,8},{10,1... | collective-permute-start | bytes 786440 | tf_op jit(solution)/shard_map/ppermute | solution.py:497
  32.4 2.2 %collective-permute-done.6.refs_0_.refs_2_ = bf16[256,512]{1,0:T(8,128)(2,1)S(1)} collective-permute-done((bf16[256,512]{1,0:T(8,128)(2,1)S(1)}, bf16[256,512]{1,0:T(8,128)(2,1)S(1)}, u32[]{:S(2)}, u32[]{:S(2)}) %collective-permute-start.6) | collective-permute-done | bytes 262176 | tf_op jit(solution)/shard_map/ppermute | solution.py:497
  34.6 2.8 %collective-permute-done.7.refs_3_ = bf16[256,512]{1,0:T(8,128)(2,1)S(1)} collective-permute-done((bf16[256,512]{1,0:T(8,128)(2,1)S(1)}, bf16[256,512]{1,0:T(8,128)(2,1)S(1)}, u32[]{:S(2)}, u32[]{:S(2)}) %collective-permute-start.7) | collective-permute-done | bytes 262176 | tf_op jit(solution)/shard_map/ppermute | solution.py:497
  37.4 0.0 collective-permute-done.8.refs_1_.refs_4_
  37.4 0.0 collective-permute-done.9.refs_5_
  37.4 0.0 collective-permute-done.10.refs_6_
  37.4 0.1 collective-permute-start.11
  37.5 0.5 collective-permute-start.12
  38.0 11.4 %collective-permute-start.13 = (bf16[128,512]{1,0:T(8,128)(2,1)S(1)}, bf16[128,512]{1,0:T(8,128)(2,1)S(1)}, u32[]{:S(2)}, u32[]{:S(2)}) collective-permute-start(bf16[128,512]{1,0:T(8,128)(2,1)S(1)} %get-tuple-element.75.refs_3_), channel_id=1, source_target_pairs={{0,1},{1,17},{2,3},{3,2},{4,5},{5,4},{6,7},{7,6},{8,9},{9,19},{10,... | collective-permute-start | bytes 393224 | tf_op jit(solution)/shard_map/ppermute | solution.py:497
  49.3 0.0 collective-permute-start.14
  49.3 0.0 collective-permute-done.11.refs_0_
  49.4 0.0 collective-permute-done.12.refs_1_
  49.4 0.0 copy-start.5
  49.4 1.9 %collective-permute-done.13.refs_1_ = bf16[128,512]{1,0:T(8,128)(2,1)S(1)} collective-permute-done((bf16[128,512]{1,0:T(8,128)(2,1)S(1)}, bf16[128,512]{1,0:T(8,128)(2,1)S(1)}, u32[]{:S(2)}, u32[]{:S(2)}) %collective-permute-start.13) | collective-permute-done | bytes 131104 | tf_op jit(solution)/shard_map/ppermute | solution.py:497
  51.3 0.0 collective-permute-done.14.refs_2_
  51.3 6.8 %collective-permute-start.15 = (bf16[64,512]{1,0:T(8,128)(2,1)S(1)}, bf16[64,512]{1,0:T(8,128)(2,1)S(1)}, u32[]{:S(2)}, u32[]{:S(2)}) collective-permute-start(bf16[64,512]{1,0:T(8,128)(2,1)S(1)} %get-tuple-element.78), channel_id=1, source_target_pairs={{0,1},{1,0},{2,3},{3,2},{4,5},{5,4},{6,7},{7,6},{8,9},{9,8},{10,11... | collective-permute-start | bytes 196616 | tf_op jit(solution)/shard_map/ppermute | solution.py:505
  58.1 0.9 %collective-permute-done.15.refs_5_ = bf16[64,512]{1,0:T(8,128)(2,1)S(1)} collective-permute-done((bf16[64,512]{1,0:T(8,128)(2,1)S(1)}, bf16[64,512]{1,0:T(8,128)(2,1)S(1)}, u32[]{:S(2)}, u32[]{:S(2)}) %collective-permute-start.15) | collective-permute-done | bytes 65568 | tf_op jit(solution)/shard_map/ppermute | solution.py:505
  59.0 1.2 %decode.1 = bf16[227,128]{1,0:T(8,128)(2,1)} custom-call(s32[1]{0:T(128)} %bitcast.segment, s32[1]{0:T(128)} %bitcast.1.place, f32[128,512]{1,0:T(8,128)S(1)} %get-tuple-element.64.refs_0_, bf16[64,128]{1,0:T(8,128)(2,1)S(1)} %get-tuple-element.65.refs_1_, bf16[1024,512]{1,0:T(8,128)(2,1)S(1)} %copy-done, bf16[227,512]{1,0:T(8,128)(2,1)S(1)} %bitcast.15, ...), custom_call_target="tpu_custom_call" | custom-call | bytes 1748744 | tf_op jit(solution)/shard_map/decode/pallas_call | solution.py:433
  (28 shorter events, 0.1 us)
Async XLA Ops:
  0.0 1.8 %copy-start.7 = (s32[64,8]{0,1:T(8,128)S(1)}, s32[64,8]{0,1:T(8,128)}, u32[]{:S(2)}) copy-start(s32[64,8]{0,1:T(8,128)} %param.21) | copy-start | bytes 6148
  0.0 1.8 %copy-start.8 = (s32[4,64]{1,0:T(4,128)S(1)}, s32[4,64]{1,0:T(4,128)}, u32[]{:S(2)}) copy-start(s32[4,64]{1,0:T(4,128)} %param.22) | copy-start | bytes 3076
  0.0 1.8 %copy-start.9 = (s32[4,1]{0,1:T(1,128)S(1)}, s32[4,1]{0,1:T(1,128)}, u32[]{:S(2)}) copy-start(s32[4,1]{0,1:T(1,128)} %param.23) | copy-start | bytes 52
  0.0 1.8 %copy-start.10 = (s32[128]{0:T(128)S(1)}, s32[128]{0:T(128)}, u32[]{:S(2)}) copy-start(s32[128]{0:T(128)} %param.19) | copy-start | bytes 1540
  0.0 1.9 %copy-start.3 = (bf16[227,512]{1,0:T(8,128)(2,1)S(1)}, bf16[227,512]{1,0:T(8,128)(2,1)}, u32[]{:S(2)}) copy-start(bf16[227,512]{1,0:T(8,128)(2,1)} %refs_1_.4) | copy-start | bytes 697348
  0.0 6.2 %copy-start.4 = (bf16[1,512,512]{2,1,0:T(8,128)(2,1)S(1)}, bf16[1,512,512]{2,1,0:T(8,128)(2,1)}, u32[]{:S(2)}) copy-start(bf16[1,512,512]{2,1,0:T(8,128)(2,1)} %refs_1_.3) | copy-start | bytes 1572868
  0.0 37.3 %collective-permute-start.8 = (bf16[1,512,1024]{2,1,0:T(8,128)(2,1)}, bf16[1,512,1024]{2,1,0:T(8,128)(2,1)S(1)}, u32[]{:S(2)}, u32[]{:S(2)}) collective-permute-start(bf16[1,512,1024]{2,1,0:T(8,128)(2,1)} %refs_0_), channel_id=1, source_target_pairs={{0,1},{1,0},{2,3},{3,2},{4,5},{5,4},{6,7},{7,6},{8,9},{9,8},{10,11... | collective-permute-start | bytes 3145736 | tf_op jit(solution)/shard_map/ppermute | solution.py:497
  0.8 36.6 %collective-permute-start.10 = (bf16[1,1024,512]{2,1,0:T(8,128)(2,1)}, bf16[1,1024,512]{2,1,0:T(8,128)(2,1)S(1)}, u32[]{:S(2)}, u32[]{:S(2)}) collective-permute-start(bf16[1,1024,512]{2,1,0:T(8,128)(2,1)} %refs_2_.2), channel_id=1, source_target_pairs={{0,1},{1,0},{2,3},{3,2},{4,5},{5,4},{6,7},{7,6},{8,9},{9,8},{10,11... | collective-permute-start | bytes 3145736 | tf_op jit(solution)/shard_map/ppermute | solution.py:497
  2.6 6.3 %collective-permute-start = (bf16[80,512]{1,0:T(8,128)(2,1)S(1)}, bf16[80,512]{1,0:T(8,128)(2,1)S(1)}, u32[]{:S(2)}, u32[]{:S(2)}) collective-permute-start(bf16[80,512]{1,0:T(8,128)(2,1)S(1)} %get-tuple-element.52), channel_id=1, source_target_pairs={{0,2},{1,3},{2,0},{3,1},{4,6},{5,7},{6,4},{7,5},{8,10},{9,11},{10,... | collective-permute-start | bytes 245768 | tf_op jit(solution)/shard_map/ppermute | solution.py:501
  4.0 5.0 %collective-permute-start.1 = (bf16[80,512]{1,0:T(8,128)(2,1)S(1)}, bf16[80,512]{1,0:T(8,128)(2,1)S(1)}, u32[]{:S(2)}, u32[]{:S(2)}) collective-permute-start(bf16[80,512]{1,0:T(8,128)(2,1)S(1)} %get-tuple-element.53), channel_id=1, source_target_pairs={{0,4},{1,5},{2,6},{3,7},{4,0},{5,1},{6,2},{7,3},{8,12},{9,13},{10,... | collective-permute-start | bytes 245768 | tf_op jit(solution)/shard_map/ppermute | solution.py:501
  6.3 5.2 %collective-permute-start.2 = (bf16[80,512]{1,0:T(8,128)(2,1)S(1)}, bf16[80,512]{1,0:T(8,128)(2,1)S(1)}, u32[]{:S(2)}, u32[]{:S(2)}) collective-permute-start(bf16[80,512]{1,0:T(8,128)(2,1)S(1)} %get-tuple-element.54), channel_id=1, source_target_pairs={{0,6},{1,7},{2,4},{3,5},{4,2},{5,3},{6,0},{7,1},{8,14},{9,15},{10,... | collective-permute-start | bytes 245768 | tf_op jit(solution)/shard_map/ppermute | solution.py:501
  6.3 1.2 %copy-start.1 = (bf16[1,512,1024]{2,1,0:T(8,128)(2,1)S(1)}, bf16[1,512,1024]{2,1,0:T(8,128)(2,1)}, u32[]{:S(2)}) copy-start(bf16[1,512,1024]{2,1,0:T(8,128)(2,1)} %refs_0_) | copy-start | bytes 3145732
  7.5 1.2 %copy-start.2 = (bf16[1,1024,512]{2,1,0:T(8,128)(2,1)S(1)}, bf16[1,1024,512]{2,1,0:T(8,128)(2,1)}, u32[]{:S(2)}) copy-start(bf16[1,1024,512]{2,1,0:T(8,128)(2,1)} %refs_2_.2) | copy-start | bytes 3145732
  11.5 3.9 %collective-permute-start.3 = (bf16[320,512]{1,0:T(8,128)(2,1)S(1)}, bf16[320,512]{1,0:T(8,128)(2,1)S(1)}, u32[]{:S(2)}, u32[]{:S(2)}) collective-permute-start(bf16[320,512]{1,0:T(8,128)(2,1)S(1)} %join.1.refs_0_), channel_id=1, source_target_pairs={{0,1},{1,0},{2,3},{3,2},{4,5},{5,4},{6,7},{7,6},{8,9},{9,8},{10,11... | collective-permute-start | bytes 983048 | tf_op jit(solution)/shard_map/ppermute | solution.py:505
  15.5 4.5 %collective-permute-start.4 = (bf16[256,512]{1,0:T(8,128)(2,1)S(1)}, bf16[256,512]{1,0:T(8,128)(2,1)S(1)}, u32[]{:S(2)}, u32[]{:S(2)}) collective-permute-start(bf16[256,512]{1,0:T(8,128)(2,1)S(1)} %get-tuple-element.61), channel_id=1, source_target_pairs={{0,8},{1,0},{2,10},{3,2},{4,12},{5,4},{6,14},{7,6},{8,9},{9,1},{10... | collective-permute-start | bytes 786440 | tf_op jit(solution)/shard_map/ppermute | solution.py:497
  15.7 3.8 %copy-start = (bf16[1024,512]{1,0:T(8,128)(2,1)S(1)}, bf16[1024,512]{1,0:T(8,128)(2,1)}, u32[]{:S(2)}) copy-start(bf16[1024,512]{1,0:T(8,128)(2,1)} %refs_2_.4) | copy-start | bytes 3145732
  15.7 3.8 %copy-start.6 = (s32[128]{0:T(128)S(1)}, s32[128]{0:T(128)}, u32[]{:S(2)}) copy-start(s32[128]{0:T(128)} %param.20) | copy-start | bytes 1540
  15.7 7.1 %collective-permute-start.5 = (bf16[256,512]{1,0:T(8,128)(2,1)S(1)}, bf16[256,512]{1,0:T(8,128)(2,1)S(1)}, u32[]{:S(2)}, u32[]{:S(2)}) collective-permute-start(bf16[256,512]{1,0:T(8,128)(2,1)S(1)} %second.4), channel_id=1, source_target_pairs={{0,8},{1,0},{2,10},{3,2},{4,12},{5,4},{6,14},{7,6},{8,9},{9,1},{10... | collective-permute-start | bytes 786440 | tf_op jit(solution)/shard_map/ppermute | solution.py:497
  19.5 17.9 %collective-permute-start.9 = (bf16[1,512,512]{2,1,0:T(8,128)(2,1)S(1)}, bf16[1,512,512]{2,1,0:T(8,128)(2,1)S(1)}, u32[]{:S(2)}, u32[]{:S(2)}) collective-permute-start(bf16[1,512,512]{2,1,0:T(8,128)(2,1)S(1)} %copy-done.4), channel_id=1, source_target_pairs={{0,1},{1,0},{2,3},{3,2},{4,5},{5,4},{6,7},{7,6},{8,9},{9,8},{10,11... | collective-permute-start | bytes 1572872 | tf_op jit(solution)/shard_map/ppermute | solution.py:497
  22.8 11.8 %collective-permute-start.6 = (bf16[256,512]{1,0:T(8,128)(2,1)S(1)}, bf16[256,512]{1,0:T(8,128)(2,1)S(1)}, u32[]{:S(2)}, u32[]{:S(2)}) collective-permute-start(bf16[256,512]{1,0:T(8,128)(2,1)S(1)} %get-tuple-element.68), channel_id=1, source_target_pairs={{0,1},{1,0},{2,3},{3,2},{4,5},{5,4},{6,7},{7,6},{8,16},{9,8},{10,1... | collective-permute-start | bytes 786440 | tf_op jit(solution)/shard_map/ppermute | solution.py:497
  29.7 7.7 %collective-permute-start.7 = (bf16[256,512]{1,0:T(8,128)(2,1)S(1)}, bf16[256,512]{1,0:T(8,128)(2,1)S(1)}, u32[]{:S(2)}, u32[]{:S(2)}) collective-permute-start(bf16[256,512]{1,0:T(8,128)(2,1)S(1)} %second.5), channel_id=1, source_target_pairs={{0,1},{1,0},{2,3},{3,2},{4,5},{5,4},{6,7},{7,6},{8,16},{9,8},{10,1... | collective-permute-start | bytes 786440 | tf_op jit(solution)/shard_map/ppermute | solution.py:497
  37.4 11.9 %collective-permute-start.11 = (bf16[128,512]{1,0:T(8,128)(2,1)S(1)}, bf16[128,512]{1,0:T(8,128)(2,1)S(1)}, u32[]{:S(2)}, u32[]{:S(2)}) collective-permute-start(bf16[128,512]{1,0:T(8,128)(2,1)S(1)} %get-tuple-element.72), channel_id=1, source_target_pairs={{0,1},{1,0},{2,3},{3,2},{4,5},{5,21},{6,7},{7,6},{8,9},{9,8},{10,1... | collective-permute-start | bytes 393224 | tf_op jit(solution)/shard_map/ppermute | solution.py:497
  37.5 11.9 %collective-permute-start.12 = (bf16[128,512]{1,0:T(8,128)(2,1)S(1)}, bf16[128,512]{1,0:T(8,128)(2,1)S(1)}, u32[]{:S(2)}, u32[]{:S(2)}) collective-permute-start(bf16[128,512]{1,0:T(8,128)(2,1)S(1)} %get-tuple-element.73), channel_id=1, source_target_pairs={{0,1},{1,0},{2,3},{3,2},{4,5},{5,4},{6,7},{7,17},{8,9},{9,8},{10,1... | collective-permute-start | bytes 393224 | tf_op jit(solution)/shard_map/ppermute | solution.py:497
  38.0 13.3 %collective-permute-start.13 = (bf16[128,512]{1,0:T(8,128)(2,1)S(1)}, bf16[128,512]{1,0:T(8,128)(2,1)S(1)}, u32[]{:S(2)}, u32[]{:S(2)}) collective-permute-start(bf16[128,512]{1,0:T(8,128)(2,1)S(1)} %get-tuple-element.75.refs_3_), channel_id=1, source_target_pairs={{0,1},{1,17},{2,3},{3,2},{4,5},{5,4},{6,7},{7,6},{8,9},{9,19},{10,... | collective-permute-start | bytes 393224 | tf_op jit(solution)/shard_map/ppermute | solution.py:497
  49.3 2.0 %collective-permute-start.14 = (bf16[128,512]{1,0:T(8,128)(2,1)S(1)}, bf16[128,512]{1,0:T(8,128)(2,1)S(1)}, u32[]{:S(2)}, u32[]{:S(2)}) collective-permute-start(bf16[128,512]{1,0:T(8,128)(2,1)S(1)} %get-tuple-element.76.refs_4_), channel_id=1, source_target_pairs={{0,1},{1,0},{2,3},{3,17},{4,5},{5,4},{6,7},{7,6},{8,9},{9,8},{10,1... | collective-permute-start | bytes 393224 | tf_op jit(solution)/shard_map/ppermute | solution.py:497
  49.4 9.6 %copy-start.5 = (bf16[512,227]{0,1:T(8,128)(2,1)S(1)}, bf16[512,227]{0,1:T(8,128)(2,1)}, u32[]{:S(2)}) copy-start(bf16[512,227]{0,1:T(8,128)(2,1)} %param.18) | copy-start | bytes 697348
  51.3 7.7 %collective-permute-start.15 = (bf16[64,512]{1,0:T(8,128)(2,1)S(1)}, bf16[64,512]{1,0:T(8,128)(2,1)S(1)}, u32[]{:S(2)}, u32[]{:S(2)}) collective-permute-start(bf16[64,512]{1,0:T(8,128)(2,1)S(1)} %get-tuple-element.78), channel_id=1, source_target_pairs={{0,1},{1,0},{2,3},{3,2},{4,5},{5,4},{6,7},{7,6},{8,9},{9,8},{10,11... | collective-permute-start | bytes 196616 | tf_op jit(solution)/shard_map/ppermute | solution.py:505

commit v10 on v9

--- a/solution.py
+++ b/solution.py
@@ -225,10 +225,10 @@
         joined[place * rows : (place + 1) * rows, :] = payload[...]
 
 
-def index_kernel(parts, mesh_rows, where, *refs):
-    lanes, (columns_out, low, high), index_out = refs[:-4], refs[-4:-1], refs[-1]
+def index_kernel(parts, quarters, mesh_rows, where, *refs):
+    group = parts // quarters
+    lanes, columns_out, state, index_out = refs[:group], refs[group], refs[group + 1 : -1], refs[-1]
     nodes = columns_out.shape[0]
-    group = len(lanes)
     rows = lanes[0].shape[0] // (parts // group)
     chip, lane_place = place_of(where, group)
 
@@ -238,8 +238,8 @@
         for part in range(parts):
             lane, turn = lanes[part % group], jnp.bitwise_xor(chip, part // group)
             base = pl.multiple_of(turn * rows, 16)
-            half, spot = (low, part) if part < parts // 2 else (high, part - parts // 2)
-            half[spot * mesh_rows : (spot + 1) * mesh_rows, :] = lane[pl.ds(base, mesh_rows), :]
+            spot = part % group * mesh_rows
+            state[part // group][spot : spot + mesh_rows, :] = lane[pl.ds(base, mesh_rows), :]
             base = pl.multiple_of(turn * rows + mesh_rows, 16)
             coded = lane[pl.ds(base, rows - mesh_rows), :384].astype(jnp.float32).astype(jnp.int32)
             tables.append(coded[: coded.shape[0] // 2])
@@ -263,34 +263,75 @@
         columns_out[...] = jnp.transpose(index_out[...].astype(jnp.float32)).astype(jnp.bfloat16)
 
 
-def hold_kernel(*refs):
-    half = len(refs) // 2
-    for copy in fetch(refs[:half], refs[half:-1], refs[-1]):
+def hold_kernel(w_project, w_message, w_update, held, semaphores):
+    width = held.shape[1]
+    sources = [
+        w_project.at[0, :, :width],
+        w_project.at[0, :, width:],
+        w_message.at[0],
+        w_update.at[0, :width],
+        w_update.at[0, width:],
+    ]
+    for copy in fetch(sources, [held.at[place] for place in range(len(sources))], semaphores):
         copy.wait()
 
 
-def renew(fanout, columns, sender, own, w_project, w_message, w_update):
+def renew(fanout, columns, sender, own, weights):
     chunk, width = own.shape
     nodes = sender.shape[0]
     tile = min(nodes, 256)
+    together = max(1, min(fanout, 1024 // chunk))
     names = lax.broadcasted_iota(jnp.int32, (chunk, tile), 1).astype(jnp.float32).astype(jnp.bfloat16)
     one_half = jnp.full((chunk, tile), 0.5, jnp.bfloat16)
     none = jnp.zeros((chunk, tile), jnp.bfloat16)
-    receiver = 0.5 * matmul(own, w_project[0, :, :width])
+    receiver = 0.5 * matmul(own, weights[0])
     total = jnp.zeros((chunk, width), jnp.float32)
-    for k in range(fanout):
-        hits = []
-        for number in range(nodes // tile):
-            lane = number * fanout + k
-            hits.append(jnp.where(columns[:, lane : lane + 1] == names, one_half, none))
-        half = receiver + matmul(jnp.concatenate(hits, axis=1), sender)
-        total = total + (half + half * jnp.tanh(half))
+    for first in range(0, fanout, together):
+        tables = []
+        for k in range(first, first + together):
+            hits = []
+            for number in range(nodes // tile):
+                lane = number * fanout + k
+                hits.append(jnp.where(columns[:, lane : lane + 1] == names, one_half, none))
+            tables.append(jnp.concatenate(hits, axis=1))
+        fetched = matmul(jnp.concatenate(tables, axis=0), sender)
+        for place in range(together):
+            half = receiver + fetched[place * chunk : (place + 1) * chunk]
+            total = total + (half + half * jnp.tanh(half))
     gathered = (total * (1.0 / fanout)).astype(jnp.bfloat16)
-    aggregate = matmul(gathered, w_message[0]).astype(jnp.bfloat16)
-    update = silu_by_tanh(
-        matmul(own, w_update[0, :width, :]) + matmul(aggregate, w_update[0, width:, :])
-    )
+    aggregate = matmul(gathered, weights[2]).astype(jnp.bfloat16)
+    update = silu_by_tanh(matmul(own, weights[3]) + matmul(aggregate, weights[4]))
     return (own.astype(jnp.float32) + rms_scale(update)).astype(jnp.bfloat16)
+
+
+def sender_kernel(group, at_segment, where, state, weights, sender):
+    @pl.when(owns(where, group, at_segment))
+    def _():
+        sender[...] = matmul(state[...], weights[1]).astype(jnp.bfloat16)
+
+
+def choose(where, group, chips, far, start, count, state, own):
+    rows = state[0].shape[0]
+
+    def take(start):
+        for place in range(count):
+            own[place * rows : (place + 1) * rows, :] = state[start + place][...]
+
+    if not chips:
+        take(start)
+        return start * rows
+    chip, _ = place_of(where, group)
+    upper = (chip < chips // 2) if far else (chip >= chips // 2)
+
+    @pl.when(upper)
+    def _():
+        take(count)
+
+    @pl.when(jnp.logical_not(upper))
+    def _():
+        take(0)
+
+    return pl.multiple_of(jnp.where(upper, count * rows, 0), count * rows)
 
 
 def write_pieces(pieces, value):
@@ -299,60 +340,32 @@
         piece[...] = value[place * rows : (place + 1) * rows]
 
 
-def sender_kernel(group, at_segment, where, low, w_project, sender_low):
-    width = low.shape[1]
+def first_kernel(group, at_segment, chips, fanout, quarters, where, columns, *refs):
+    senders, refs = refs[: quarters - 1], refs[quarters - 1 :]
+    state, (weights, sender), refs = refs[:quarters], refs[quarters : quarters + 2], refs[quarters + 2 :]
+    pieces, own = refs[:-1], refs[-1]
+    rows = state[0].shape[0]
 
     @pl.when(owns(where, group, at_segment))
     def _():
-        sender_low[...] = matmul(low[...], w_project[0, :, width:]).astype(jnp.bfloat16)
-
-
-def half_of(where, group, chips, far, low, high, own):
-    half = low.shape[0]
-    chip, _ = place_of(where, group)
-    upper = (chip < chips // 2) if far else (chip >= chips // 2)
-
-    @pl.when(upper)
-    def _():
-        own[...] = high[...]
-
-    @pl.when(jnp.logical_not(upper))
-    def _():
-        own[...] = low[...]
-
-    return pl.multiple_of(jnp.where(upper, half, 0), half)
-
-
-def first_kernel(
-    group, at_segment, chips, fanout, where, columns, sender_low, low, high, w_project, w_message, w_update, *outs
-):
-    sender, pieces, own = outs[0], outs[1:-1], outs[-1]
-    half, width = low.shape
+        for place, part in enumerate(senders):
+            sender[place * rows : (place + 1) * rows, :] = part[...]
+        rest = matmul(state[-1][...], weights[1]).astype(jnp.bfloat16)
+        sender[(quarters - 1) * rows :, :] = rest
+        start = choose(where, group, chips, True, 0, len(pieces), state, own)
+        lanes = columns[pl.ds(start, own.shape[0]), :]
+        write_pieces(pieces, renew(fanout, lanes, sender[...], own[...], weights))
+
+
+def next_kernel(group, at_segment, chips, fanout, quarters, done, where, columns, sender, *refs):
+    state, weights, refs = refs[:quarters], refs[quarters], refs[quarters + 1 :]
+    pieces, own = refs[:-1], refs[-1]
 
     @pl.when(owns(where, group, at_segment))
     def _():
-        sender[:half, :] = sender_low[...]
-        sender[half:, :] = matmul(high[...], w_project[0, :, width:]).astype(jnp.bfloat16)
-        start, state = 0, low
-        if chips:
-            start, state = half_of(where, group, chips, True, low, high, own), own
-        rows = columns[pl.ds(start, half), :]
-        write_pieces(pieces, renew(fanout, rows, sender[...], state[...], w_project, w_message, w_update))
-
-
-def second_kernel(
-    group, at_segment, chips, fanout, where, columns, sender, low, high, w_project, w_message, w_update, *outs
-):
-    pieces, own = outs[:-1], outs[-1]
-    half = low.shape[0]
-
-    @pl.when(owns(where, group, at_segment))
-    def _():
-        start, state = half, high
-        if chips:
-            start, state = half_of(where, group, chips, False, low, high, own), own
-        rows = columns[pl.ds(start, half), :]
-        write_pieces(pieces, renew(fanout, rows, sender[...], state[...], w_project, w_message, w_update))
+        start = choose(where, group, chips, False, done, len(pieces), state, own)
+        lanes = columns[pl.ds(start, own.shape[0]), :]
+        write_pieces(pieces, renew(fanout, lanes, sender[...], own[...], weights))
 
 
 def arrival(where, group, chips, last):
@@ -513,7 +526,16 @@
     where = (own_segment, own_place)
     last = segments - 2
     pairs = [(owner(m, last + 1), owner(m, last)) for m in range(samples)]
-    came_weights = [send(weight, pairs) for weight in weights]
+    (held,) = call(
+        hold_kernel,
+        "hold",
+        [jax.ShapeDtypeStruct((5, width, width), bf16)],
+        weights,
+        "hhh",
+        [pltpu.SemaphoreType.DMA((5,))],
+        room=16,
+    )
+    came = send(held, pairs)
     snapshots = jnp.transpose(grid_state, (0, 2, 1))
     lists = send_rows.shape[0]
 
@@ -537,15 +559,7 @@
         "wvvv",
         [pltpu.VMEM((samples * grid_rows, width), bf16)],
     )
-    held = call(
-        hold_kernel,
-        "hold",
-        [jax.ShapeDtypeStruct(weight.shape, bf16) for weight in weights],
-        weights,
-        "hhh",
-        [pltpu.SemaphoreType.DMA((3,))],
-    )
-    own_payload, *held = lax.optimization_barrier((payloads[0], *held))
+    own_payload, held = lax.optimization_barrier((payloads[0], held))
     arrived = [own_payload] + [to_chip(payloads[turn], turn) for turn in range(1, samples)]
     (joined,) = call(
         join_kernel,
@@ -555,53 +569,54 @@
         "v" * samples,
     )
     lanes = [joined] + [change_lane(joined, -steps) for steps in range(1, group)]
-    half = nodes // 2
     share = group * mesh_rows
-    columns, low, high = call(
-        functools.partial(index_kernel, parts, mesh_rows),
+    quarter = jax.ShapeDtypeStruct((share, width), bf16)
+    columns, *state = call(
+        functools.partial(index_kernel, parts, samples, mesh_rows),
         "index",
-        [
-            jax.ShapeDtypeStruct((nodes, 128), bf16),
-            jax.ShapeDtypeStruct((half, width), bf16),
-            jax.ShapeDtypeStruct((half, width), bf16),
-        ],
+        [jax.ShapeDtypeStruct((nodes, 128), bf16)] + [quarter] * samples,
         [where] + lanes,
         "w" + "v" * group,
         [pltpu.VMEM((128, nodes), jnp.int32)],
     )
-    state_shape = jax.ShapeDtypeStruct((half, width), bf16)
     for layer in range(segments):
         at_segment, ends = min(layer, last), layer > last
-        used = list(held) if layer <= last else came_weights
-        role = (group, at_segment, samples if ends else 0, fanout)
-        pieces = [jax.ShapeDtypeStruct((share, width), bf16)] * (half // share) if ends else [state_shape]
-        scratch = [pltpu.VMEM((half, width), bf16)]
-        (sender_low,) = call(
-            functools.partial(sender_kernel, group, at_segment),
-            "sender",
-            [state_shape],
-            [where, low, used[0]],
-            "wvv",
-        )
-        sender, *first = call(
+        used = held if layer <= last else came
+        role = (group, at_segment, samples if ends else 0, fanout, samples)
+        count = 1 if layer < last else samples // 2
+        scratch = [pltpu.VMEM((count * share, width), bf16)]
+        pairs = [(owner(m, layer), owner(m, layer + 1)) for m in range(samples)]
+        senders = []
+        for part in state[:-1]:
+            if senders:
+                part, senders[-1] = lax.optimization_barrier((part, senders[-1]))
+            senders += call(
+                functools.partial(sender_kernel, group, at_segment),
+                "sender",
+                [quarter],
+                [where, part, used],
+                "wvv",
+            )
+        sender, *made = call(
             functools.partial(first_kernel, *role),
             "first",
-            [jax.ShapeDtypeStruct((nodes, width), bf16)] + pieces,
-            [where, columns, sender_low, low, high] + used,
-            "wvvvvvvv",
+            [jax.ShapeDtypeStruct((nodes, width), bf16)] + [quarter] * count,
+            [where, columns] + senders + list(state) + [used],
+            "w" + "v" * (2 * samples + 1),
             scratch,
         )
-        pairs = [(owner(m, layer), owner(m, layer + 1)) for m in range(samples)]
-        new_low = send(first[0], pairs) if layer < last else first[0]
-        second = call(
-            functools.partial(second_kernel, *role),
-            "second",
-            pieces,
-            [where, columns, sender, low, high] + used,
-            "wvvvvvvv",
-            scratch,
-        )
-        low, high = new_low, send(second[0], pairs) if layer < last else second[0]
+        renewed = [send(made[0], pairs)] if layer < last else list(made)
+        for done in range(count, samples, count):
+            made = call(
+                functools.partial(next_kernel, *role, done),
+                "next",
+                [quarter] * count,
+                [where, columns, sender] + list(state) + [used],
+                "w" + "v" * (samples + 3),
+                scratch,
+            )
+            renewed += [send(made[0], pairs)] if layer < last else list(made)
+        state = renewed
         if layer == 0:
             ready, table = call(
                 prepare_kernel,
@@ -613,10 +628,10 @@
                 [where, snapshots, w_embed, w_decode, mesh_grid.reshape(1, grid_rows)],
                 "wvvvv",
                     )
-            low, ready, table = lax.optimization_barrier((low, ready, table))
+            state[0], ready, table = lax.optimization_barrier((state[0], ready, table))
     each = samples // 2
     arrived = []
-    for far, blocks in ((1, first), (0, second)):
+    for far, blocks in ((1, state[: samples // 2]), (0, state[samples // 2 :])):
         for turn, block in enumerate(blocks):
             pairs = [
                 (owner(m, last), device(m, ((m // each ^ far) * each + turn) * group)) for m in range(samples)
@@ -633,7 +648,7 @@
         functools.partial(near_kernel, group, samples, last),
         "near",
         [jax.ShapeDtypeStruct((mesh_rows, width), bf16)] * group,
-        [where, crossed] + arrived[each:] + list(second),
+        [where, crossed] + arrived[each:] + state[each:],
         "w" + "v" * (1 + 2 * each),
     )
     handed = [parts_of_block[0]]

time: 60.5 us -> 63.4 us (1.048)
  starting transfers between devices: 39.5 us -> 41.4 us
  waiting for transfers between devices: 14.4 us -> 15.2 us
    ppermute x3, waiting for transfers between devices: 2.54 us -> 5.22 us  [to_chip(): return lax.ppermute(value, 'dom', pairs)]
    ppermute x11 -> x13, waiting for transfers between devices: 9.74 us -> 7.81 us  [send(): lax.ppermute(value, ('segment', 'dom'), every_device(pairs, segments * pa...]
    ppermute x11 -> x13, starting transfers between devices: 26.3 us -> 28.2 us  [send(): lax.ppermute(value, ('segment', 'dom'), every_device(pairs, segments * pa...]
    pallas_call x20 -> x32, Pallas kernels: 2.66 us -> 2.78 us  [call(): pl.pallas_call(located if places[0] == 'w' else kernel, out_shape=shapes,...]
    unnamed x23 -> x25, local copies, waits for them, and re-layouts: 3.46 us -> 3.56 us
  transfers between devices with their start and end apart: 16 -> 18, of which waited for: 7 -> 10; matrix products, arithmetic and copies ran while one was open for 2% -> 0% of each run, Pallas kernels for 2% -> 2%
where the time goes in v10:
time: 63.4 us; the launch traced here: 63.2 us
  starting transfers between devices  41.4 us (65%)
  waiting for transfers between devices  15.2 us (24%)
  local copies, waits for them, and re-layouts  3.56 us (6%)
  Pallas kernels  2.78 us (4%)
    ppermute x13, starting transfers between devices, send(): lax.ppermute(value, ('segment', 'dom'), every_device(pairs, segments * pa...  28.2 us
    ppermute x2, starting transfers between devices, change_lane(): return lax.ppermute(value, 'dom', pairs)  9.48 us
    ppermute x13, waiting for transfers between devices, send(): lax.ppermute(value, ('segment', 'dom'), every_device(pairs, segments * pa...  7.81 us
    ppermute x3, waiting for transfers between devices, to_chip(): return lax.ppermute(value, 'dom', pairs)  5.22 us
    ppermute x3, starting transfers between devices, to_chip(): return lax.ppermute(value, 'dom', pairs)  3.67 us
    unnamed x25, local copies, waits for them, and re-layouts  3.56 us
    pallas_call x32, Pallas kernels, call(): pl.pallas_call(located if places[0] == 'w' else kernel, out_shape=shapes,...  2.78 us
    ppermute x2, waiting for transfers between devices, change_lane(): return lax.ppermute(value, 'dom', pairs)  2.16 us
  transfers between devices with their start and end apart: 18, of which 10 were waited for; matrix products, arithmetic and copies ran while one was open for 0% of the time, Pallas kernels for 2%

profile of v10, /device:TPU:3, one launch (start us, length us, event | category | flops | bytes accessed | tf_op | source)
XLA Modules:
  0.0 63.2 jit_solution(9159885551990998330)
XLA Ops:
  0.0 1.2 %copy-done.1 = bf16[1,512,1024]{2,1,0:T(8,128)(2,1)S(1)} copy-done((bf16[1,512,1024]{2,1,0:T(8,128)(2,1)S(1)}, bf16[1,512,1024]{2,1,0:T(8,128)(2,1)}, u32[]{:S(2)}) %copy-start.1) | copy-done | bytes 1048600
  1.2 1.2 %copy-done.2 = bf16[1,1024,512]{2,1,0:T(8,128)(2,1)S(1)} copy-done((bf16[1,1024,512]{2,1,0:T(8,128)(2,1)S(1)}, bf16[1,1024,512]{2,1,0:T(8,128)(2,1)}, u32[]{:S(2)}) %copy-start.2) | copy-done | bytes 1048600
  2.5 1.0 %copy-done.4 = bf16[1,512,512]{2,1,0:T(8,128)(2,1)S(1)} copy-done((bf16[1,512,512]{2,1,0:T(8,128)(2,1)S(1)}, bf16[1,512,512]{2,1,0:T(8,128)(2,1)}, u32[]{:S(2)}) %copy-start.4) | copy-done | bytes 524312
  3.5 0.0 copy-start.11
  3.5 0.0 copy-start.3
  3.5 0.3 hold.1.refs_1_.refs_8_.refs_6_
  3.8 0.7 %collective-permute-start.12 = (bf16[5,512,512]{2,1,0:T(8,128)(2,1)S(1)}, bf16[5,512,512]{2,1,0:T(8,128)(2,1)S(1)}, u32[]{:S(2)}, u32[]{:S(2)}) collective-permute-start(bf16[5,512,512]{2,1,0:T(8,128)(2,1)S(1)} %hold.1.refs_1_.refs_8_.refs_6_), channel_id=1, source_target_pairs={{0,1},{1,0},{2,3},{3,2},{4,5},{5,4},{6,7},{7,6},{8,9},{9,8},{10,11... | collective-permute-start | bytes 7864328 | tf_op jit(solution)/shard_map/ppermute | solution.py:510
  4.6 0.0 copy-done.7
  4.7 0.7 %encode.1 = (bf16[80,512]{1,0:T(8,128)(2,1)S(1)}, bf16[80,512]{1,0:T(8,128)(2,1)S(1)}, bf16[80,512]{1,0:T(8,128)(2,1)S(1)}, bf16[80,512]{1,0:T(8,128)(2,1)S(1)}) custom-call(s32[1]{0:T(128)} %bitcast.segment, s32[1]{0:T(128)} %bitcast.1.place, bf16[4,227,128]{2,1,0:T(8,128)(2,1)S(1)} %bitcast.13, bf16[227,512]{1,0:T(8,128)(2,1)S(1)} %copy-done.3, ...), custom_call_target="tpu_custom_call" | custom-call | bytes 799752 | tf_op jit(solution)/shard_map/encode/pallas_call | solution.py:446
  5.4 1.4 %collective-permute-start = (bf16[80,512]{1,0:T(8,128)(2,1)S(1)}, bf16[80,512]{1,0:T(8,128)(2,1)S(1)}, u32[]{:S(2)}, u32[]{:S(2)}) collective-permute-start(bf16[80,512]{1,0:T(8,128)(2,1)S(1)} %get-tuple-element.65), channel_id=1, source_target_pairs={{0,2},{1,3},{2,0},{3,1},{4,6},{5,7},{6,4},{7,5},{8,10},{9,11},{10,... | collective-permute-start | bytes 245768 | tf_op jit(solution)/shard_map/ppermute | solution.py:514
  6.7 2.3 %collective-permute-start.1 = (bf16[80,512]{1,0:T(8,128)(2,1)S(1)}, bf16[80,512]{1,0:T(8,128)(2,1)S(1)}, u32[]{:S(2)}, u32[]{:S(2)}) collective-permute-start(bf16[80,512]{1,0:T(8,128)(2,1)S(1)} %get-tuple-element.66), channel_id=1, source_target_pairs={{0,4},{1,5},{2,6},{3,7},{4,0},{5,1},{6,2},{7,3},{8,12},{9,13},{10,... | collective-permute-start | bytes 245768 | tf_op jit(solution)/shard_map/ppermute | solution.py:514
  9.1 0.0 collective-permute-start.2
  9.1 0.0 collective-permute-done.refs_1_
  9.1 2.2 %collective-permute-done.1.refs_2_ = bf16[80,512]{1,0:T(8,128)(2,1)S(1)} collective-permute-done((bf16[80,512]{1,0:T(8,128)(2,1)S(1)}, bf16[80,512]{1,0:T(8,128)(2,1)S(1)}, u32[]{:S(2)}, u32[]{:S(2)}) %collective-permute-start.1) | collective-permute-done | bytes 81952 | tf_op jit(solution)/shard_map/ppermute | solution.py:514
  11.3 3.0 %collective-permute-done.2.refs_3_ = bf16[80,512]{1,0:T(8,128)(2,1)S(1)} collective-permute-done((bf16[80,512]{1,0:T(8,128)(2,1)S(1)}, bf16[80,512]{1,0:T(8,128)(2,1)S(1)}, u32[]{:S(2)}, u32[]{:S(2)}) %collective-permute-start.2) | collective-permute-done | bytes 81952 | tf_op jit(solution)/shard_map/ppermute | solution.py:514
  14.3 2.7 %collective-permute-start.3 = (bf16[320,512]{1,0:T(8,128)(2,1)S(1)}, bf16[320,512]{1,0:T(8,128)(2,1)S(1)}, u32[]{:S(2)}, u32[]{:S(2)}) collective-permute-start(bf16[320,512]{1,0:T(8,128)(2,1)S(1)} %join.1.refs_0_), channel_id=1, source_target_pairs={{0,1},{1,0},{2,3},{3,2},{4,5},{5,4},{6,7},{7,6},{8,9},{9,8},{10,11... | collective-permute-start | bytes 983048 | tf_op jit(solution)/shard_map/ppermute | solution.py:518
  17.0 1.3 %collective-permute-done.3.refs_1_ = bf16[320,512]{1,0:T(8,128)(2,1)S(1)} collective-permute-done((bf16[320,512]{1,0:T(8,128)(2,1)S(1)}, bf16[320,512]{1,0:T(8,128)(2,1)S(1)}, u32[]{:S(2)}, u32[]{:S(2)}) %collective-permute-start.3) | collective-permute-done | bytes 327712 | tf_op jit(solution)/shard_map/ppermute | solution.py:518
  18.3 0.3 collective-permute-start.4
  18.5 3.1 %collective-permute-start.5 = (bf16[128,512]{1,0:T(8,128)(2,1)S(1)}, bf16[128,512]{1,0:T(8,128)(2,1)S(1)}, u32[]{:S(2)}, u32[]{:S(2)}) collective-permute-start(bf16[128,512]{1,0:T(8,128)(2,1)S(1)} %next.8), channel_id=1, source_target_pairs={{0,8},{1,0},{2,10},{3,2},{4,12},{5,4},{6,14},{7,6},{8,9},{9,1},{10... | collective-permute-start | bytes 393224 | tf_op jit(solution)/shard_map/ppermute | solution.py:510
  21.6 1.6 %collective-permute-start.6 = (bf16[128,512]{1,0:T(8,128)(2,1)S(1)}, bf16[128,512]{1,0:T(8,128)(2,1)S(1)}, u32[]{:S(2)}, u32[]{:S(2)}) collective-permute-start(bf16[128,512]{1,0:T(8,128)(2,1)S(1)} %next.9), channel_id=1, source_target_pairs={{0,8},{1,0},{2,10},{3,2},{4,12},{5,4},{6,14},{7,6},{8,9},{9,1},{10... | collective-permute-start | bytes 393224 | tf_op jit(solution)/shard_map/ppermute | solution.py:510
  23.3 1.7 %collective-permute-start.7 = (bf16[128,512]{1,0:T(8,128)(2,1)S(1)}, bf16[128,512]{1,0:T(8,128)(2,1)S(1)}, u32[]{:S(2)}, u32[]{:S(2)}) collective-permute-start(bf16[128,512]{1,0:T(8,128)(2,1)S(1)} %next.10), channel_id=1, source_target_pairs={{0,8},{1,0},{2,10},{3,2},{4,12},{5,4},{6,14},{7,6},{8,9},{9,1},{10... | collective-permute-start | bytes 393224 | tf_op jit(solution)/shard_map/ppermute | solution.py:510
  24.9 0.0 copy-done.6
  24.9 0.4 prepare.1
  25.3 0.0 collective-permute-done.4.refs_0_.refs_4_.refs_2_
  25.4 0.0 collective-permute-done.5.refs_0_.refs_5_.refs_3_
  25.4 0.0 collective-permute-done.6.refs_0_.refs_6_.refs_4_
  25.4 1.4 %collective-permute-done.7.refs_7_.refs_5_ = bf16[128,512]{1,0:T(8,128)(2,1)S(1)} collective-permute-done((bf16[128,512]{1,0:T(8,128)(2,1)S(1)}, bf16[128,512]{1,0:T(8,128)(2,1)S(1)}, u32[]{:S(2)}, u32[]{:S(2)}) %collective-permute-start.7) | collective-permute-done | bytes 131104 | tf_op jit(solution)/shard_map/ppermute | solution.py:510
  26.9 4.6 %collective-permute-start.9 = (bf16[128,512]{1,0:T(8,128)(2,1)S(1)}, bf16[128,512]{1,0:T(8,128)(2,1)S(1)}, u32[]{:S(2)}, u32[]{:S(2)}) collective-permute-start(bf16[128,512]{1,0:T(8,128)(2,1)S(1)} %get-tuple-element.90), channel_id=1, source_target_pairs={{0,1},{1,0},{2,3},{3,2},{4,5},{5,4},{6,7},{7,6},{8,16},{9,8},{10,1... | collective-permute-start | bytes 393224 | tf_op jit(solution)/shard_map/ppermute | solution.py:510
  31.5 1.6 %collective-permute-start.8 = (bf16[128,512]{1,0:T(8,128)(2,1)S(1)}, bf16[128,512]{1,0:T(8,128)(2,1)S(1)}, u32[]{:S(2)}, u32[]{:S(2)}) collective-permute-start(bf16[128,512]{1,0:T(8,128)(2,1)S(1)} %next.11), channel_id=1, source_target_pairs={{0,1},{1,0},{2,3},{3,2},{4,5},{5,4},{6,7},{7,6},{8,16},{9,8},{10,1... | collective-permute-start | bytes 393224 | tf_op jit(solution)/shard_map/ppermute | solution.py:510
  33.1 1.6 %collective-permute-start.10 = (bf16[128,512]{1,0:T(8,128)(2,1)S(1)}, bf16[128,512]{1,0:T(8,128)(2,1)S(1)}, u32[]{:S(2)}, u32[]{:S(2)}) collective-permute-start(bf16[128,512]{1,0:T(8,128)(2,1)S(1)} %next.12), channel_id=1, source_target_pairs={{0,1},{1,0},{2,3},{3,2},{4,5},{5,4},{6,7},{7,6},{8,16},{9,8},{10,1... | collective-permute-start | bytes 393224 | tf_op jit(solution)/shard_map/ppermute | solution.py:510
  34.7 1.8 %collective-permute-start.11 = (bf16[128,512]{1,0:T(8,128)(2,1)S(1)}, bf16[128,512]{1,0:T(8,128)(2,1)S(1)}, u32[]{:S(2)}, u32[]{:S(2)}) collective-permute-start(bf16[128,512]{1,0:T(8,128)(2,1)S(1)} %next.13), channel_id=1, source_target_pairs={{0,1},{1,0},{2,3},{3,2},{4,5},{5,4},{6,7},{7,6},{8,16},{9,8},{10,1... | collective-permute-start | bytes 393224 | tf_op jit(solution)/shard_map/ppermute | solution.py:510
  36.5 0.2 collective-permute-done.9.refs_0_.refs_4_.refs_2_
  36.8 1.4 %collective-permute-done.8.refs_0_.refs_5_.refs_3_ = bf16[128,512]{1,0:T(8,128)(2,1)S(1)} collective-permute-done((bf16[128,512]{1,0:T(8,128)(2,1)S(1)}, bf16[128,512]{1,0:T(8,128)(2,1)S(1)}, u32[]{:S(2)}, u32[]{:S(2)}) %collective-permute-start.8) | collective-permute-done | bytes 131104 | tf_op jit(solution)/shard_map/ppermute | solution.py:510
  38.2 1.4 %collective-permute-done.10.refs_0_.refs_6_.refs_4_ = bf16[128,512]{1,0:T(8,128)(2,1)S(1)} collective-permute-done((bf16[128,512]{1,0:T(8,128)(2,1)S(1)}, bf16[128,512]{1,0:T(8,128)(2,1)S(1)}, u32[]{:S(2)}, u32[]{:S(2)}) %collective-permute-start.10) | collective-permute-done | bytes 131104 | tf_op jit(solution)/shard_map/ppermute | solution.py:510
  39.6 1.4 %collective-permute-done.11.refs_7_.refs_5_ = bf16[128,512]{1,0:T(8,128)(2,1)S(1)} collective-permute-done((bf16[128,512]{1,0:T(8,128)(2,1)S(1)}, bf16[128,512]{1,0:T(8,128)(2,1)S(1)}, u32[]{:S(2)}, u32[]{:S(2)}) %collective-permute-start.11) | collective-permute-done | bytes 131104 | tf_op jit(solution)/shard_map/ppermute | solution.py:510
  41.0 0.0 collective-permute-done.12.refs_1_.refs_8_.refs_6_
  41.0 0.0 copy-start.5
  41.0 0.1 collective-permute-start.13
  41.1 0.5 collective-permute-start.14
  41.6 10.7 %collective-permute-start.15 = (bf16[128,512]{1,0:T(8,128)(2,1)S(1)}, bf16[128,512]{1,0:T(8,128)(2,1)S(1)}, u32[]{:S(2)}, u32[]{:S(2)}) collective-permute-start(bf16[128,512]{1,0:T(8,128)(2,1)S(1)} %get-tuple-element.107.refs_3_), channel_id=1, source_target_pairs={{0,1},{1,17},{2,3},{3,2},{4,5},{5,4},{6,7},{7,6},{8,9},{9,19},{10,... | collective-permute-start | bytes 393224 | tf_op jit(solution)/shard_map/ppermute | solution.py:510
  52.3 0.0 collective-permute-start.16
  52.3 0.0 collective-permute-done.13.refs_0_
  52.3 0.0 collective-permute-done.14.refs_1_
  52.3 1.9 %collective-permute-done.15.refs_1_ = bf16[128,512]{1,0:T(8,128)(2,1)S(1)} collective-permute-done((bf16[128,512]{1,0:T(8,128)(2,1)S(1)}, bf16[128,512]{1,0:T(8,128)(2,1)S(1)}, u32[]{:S(2)}, u32[]{:S(2)}) %collective-permute-start.15) | collective-permute-done | bytes 131104 | tf_op jit(solution)/shard_map/ppermute | solution.py:510
  54.2 0.0 collective-permute-done.16.refs_2_
  54.3 6.8 %collective-permute-start.17 = (bf16[64,512]{1,0:T(8,128)(2,1)S(1)}, bf16[64,512]{1,0:T(8,128)(2,1)S(1)}, u32[]{:S(2)}, u32[]{:S(2)}) collective-permute-start(bf16[64,512]{1,0:T(8,128)(2,1)S(1)} %get-tuple-element.110), channel_id=1, source_target_pairs={{0,1},{1,0},{2,3},{3,2},{4,5},{5,4},{6,7},{7,6},{8,9},{9,8},{10,11... | collective-permute-start | bytes 196616 | tf_op jit(solution)/shard_map/ppermute | solution.py:518
  61.0 0.9 %collective-permute-done.17.refs_5_ = bf16[64,512]{1,0:T(8,128)(2,1)S(1)} collective-permute-done((bf16[64,512]{1,0:T(8,128)(2,1)S(1)}, bf16[64,512]{1,0:T(8,128)(2,1)S(1)}, u32[]{:S(2)}, u32[]{:S(2)}) %collective-permute-start.17) | collective-permute-done | bytes 65568 | tf_op jit(solution)/shard_map/ppermute | solution.py:518
  61.9 1.2 %decode.1 = bf16[227,128]{1,0:T(8,128)(2,1)} custom-call(s32[1]{0:T(128)} %bitcast.segment, s32[1]{0:T(128)} %bitcast.1.place, f32[128,512]{1,0:T(8,128)S(1)} %get-tuple-element.81.refs_0_, bf16[64,128]{1,0:T(8,128)(2,1)S(1)} %get-tuple-element.82.refs_1_, bf16[1024,512]{1,0:T(8,128)(2,1)S(1)} %copy-done, bf16[227,512]{1,0:T(8,128)(2,1)S(1)} %bitcast.15, ...), custom_call_target="tpu_custom_call" | custom-call | bytes 1748744 | tf_op jit(solution)/shard_map/decode/pallas_call | solution.py:446
  (46 shorter events, 0.2 us)
Async XLA Ops:
  0.0 1.2 %copy-start.1 = (bf16[1,512,1024]{2,1,0:T(8,128)(2,1)S(1)}, bf16[1,512,1024]{2,1,0:T(8,128)(2,1)}, u32[]{:S(2)}) copy-start(bf16[1,512,1024]{2,1,0:T(8,128)(2,1)} %w_project) | copy-start | bytes 3145732
  1.2 1.2 %copy-start.2 = (bf16[1,1024,512]{2,1,0:T(8,128)(2,1)S(1)}, bf16[1,1024,512]{2,1,0:T(8,128)(2,1)}, u32[]{:S(2)}) copy-start(bf16[1,1024,512]{2,1,0:T(8,128)(2,1)} %w_update) | copy-start | bytes 3145732
  2.5 1.0 %copy-start.4 = (bf16[1,512,512]{2,1,0:T(8,128)(2,1)S(1)}, bf16[1,512,512]{2,1,0:T(8,128)(2,1)}, u32[]{:S(2)}) copy-start(bf16[1,512,512]{2,1,0:T(8,128)(2,1)} %w_message) | copy-start | bytes 1572868
  3.5 1.1 %copy-start.7 = (bf16[4,128,227]{1,0,2:T(4,128)(2,1)S(1)}, bf16[4,128,227]{1,0,2:T(4,128)(2,1)}, u32[]{:S(2)}) copy-start(bf16[4,128,227]{1,0,2:T(4,128)(2,1)} %param.12) | copy-start | bytes 697348
  3.5 1.1 %copy-start.8 = (s32[64,8]{0,1:T(8,128)S(1)}, s32[64,8]{0,1:T(8,128)}, u32[]{:S(2)}) copy-start(s32[64,8]{0,1:T(8,128)} %param.21) | copy-start | bytes 6148
  3.5 1.1 %copy-start.9 = (s32[4,64]{1,0:T(4,128)S(1)}, s32[4,64]{1,0:T(4,128)}, u32[]{:S(2)}) copy-start(s32[4,64]{1,0:T(4,128)} %param.22) | copy-start | bytes 3076
  3.5 1.1 %copy-start.10 = (s32[4,1]{0,1:T(1,128)S(1)}, s32[4,1]{0,1:T(1,128)}, u32[]{:S(2)}) copy-start(s32[4,1]{0,1:T(1,128)} %param.23) | copy-start | bytes 52
  3.5 1.1 %copy-start.11 = (s32[128]{0:T(128)S(1)}, s32[128]{0:T(128)}, u32[]{:S(2)}) copy-start(s32[128]{0:T(128)} %param.19) | copy-start | bytes 1540
  3.5 1.1 %copy-start.3 = (bf16[227,512]{1,0:T(8,128)(2,1)S(1)}, bf16[227,512]{1,0:T(8,128)(2,1)}, u32[]{:S(2)}) copy-start(bf16[227,512]{1,0:T(8,128)(2,1)} %refs_1_.3) | copy-start | bytes 697348
  3.8 37.1 %collective-permute-start.12 = (bf16[5,512,512]{2,1,0:T(8,128)(2,1)S(1)}, bf16[5,512,512]{2,1,0:T(8,128)(2,1)S(1)}, u32[]{:S(2)}, u32[]{:S(2)}) collective-permute-start(bf16[5,512,512]{2,1,0:T(8,128)(2,1)S(1)} %hold.1.refs_1_.refs_8_.refs_6_), channel_id=1, source_target_pairs={{0,1},{1,0},{2,3},{3,2},{4,5},{5,4},{6,7},{7,6},{8,9},{9,8},{10,11... | collective-permute-start | bytes 7864328 | tf_op jit(solution)/shard_map/ppermute | solution.py:510
  5.4 3.7 %collective-permute-start = (bf16[80,512]{1,0:T(8,128)(2,1)S(1)}, bf16[80,512]{1,0:T(8,128)(2,1)S(1)}, u32[]{:S(2)}, u32[]{:S(2)}) collective-permute-start(bf16[80,512]{1,0:T(8,128)(2,1)S(1)} %get-tuple-element.65), channel_id=1, source_target_pairs={{0,2},{1,3},{2,0},{3,1},{4,6},{5,7},{6,4},{7,5},{8,10},{9,11},{10,... | collective-permute-start | bytes 245768 | tf_op jit(solution)/shard_map/ppermute | solution.py:514
  6.7 4.6 %collective-permute-start.1 = (bf16[80,512]{1,0:T(8,128)(2,1)S(1)}, bf16[80,512]{1,0:T(8,128)(2,1)S(1)}, u32[]{:S(2)}, u32[]{:S(2)}) collective-permute-start(bf16[80,512]{1,0:T(8,128)(2,1)S(1)} %get-tuple-element.66), channel_id=1, source_target_pairs={{0,4},{1,5},{2,6},{3,7},{4,0},{5,1},{6,2},{7,3},{8,12},{9,13},{10,... | collective-permute-start | bytes 245768 | tf_op jit(solution)/shard_map/ppermute | solution.py:514
  9.1 5.2 %collective-permute-start.2 = (bf16[80,512]{1,0:T(8,128)(2,1)S(1)}, bf16[80,512]{1,0:T(8,128)(2,1)S(1)}, u32[]{:S(2)}, u32[]{:S(2)}) collective-permute-start(bf16[80,512]{1,0:T(8,128)(2,1)S(1)} %get-tuple-element.67), channel_id=1, source_target_pairs={{0,6},{1,7},{2,4},{3,5},{4,2},{5,3},{6,0},{7,1},{8,14},{9,15},{10,... | collective-permute-start | bytes 245768 | tf_op jit(solution)/shard_map/ppermute | solution.py:514
  14.3 4.0 %collective-permute-start.3 = (bf16[320,512]{1,0:T(8,128)(2,1)S(1)}, bf16[320,512]{1,0:T(8,128)(2,1)S(1)}, u32[]{:S(2)}, u32[]{:S(2)}) collective-permute-start(bf16[320,512]{1,0:T(8,128)(2,1)S(1)} %join.1.refs_0_), channel_id=1, source_target_pairs={{0,1},{1,0},{2,3},{3,2},{4,5},{5,4},{6,7},{7,6},{8,9},{9,8},{10,11... | collective-permute-start | bytes 983048 | tf_op jit(solution)/shard_map/ppermute | solution.py:518
  18.3 7.1 %collective-permute-start.4 = (bf16[128,512]{1,0:T(8,128)(2,1)S(1)}, bf16[128,512]{1,0:T(8,128)(2,1)S(1)}, u32[]{:S(2)}, u32[]{:S(2)}) collective-permute-start(bf16[128,512]{1,0:T(8,128)(2,1)S(1)} %get-tuple-element.78), channel_id=1, source_target_pairs={{0,8},{1,0},{2,10},{3,2},{4,12},{5,4},{6,14},{7,6},{8,9},{9,1},{10... | collective-permute-start | bytes 393224 | tf_op jit(solution)/shard_map/ppermute | solution.py:510
  18.5 6.8 %collective-permute-start.5 = (bf16[128,512]{1,0:T(8,128)(2,1)S(1)}, bf16[128,512]{1,0:T(8,128)(2,1)S(1)}, u32[]{:S(2)}, u32[]{:S(2)}) collective-permute-start(bf16[128,512]{1,0:T(8,128)(2,1)S(1)} %next.8), channel_id=1, source_target_pairs={{0,8},{1,0},{2,10},{3,2},{4,12},{5,4},{6,14},{7,6},{8,9},{9,1},{10... | collective-permute-start | bytes 393224 | tf_op jit(solution)/shard_map/ppermute | solution.py:510
  21.6 3.3 %copy-start = (bf16[1024,512]{1,0:T(8,128)(2,1)S(1)}, bf16[1024,512]{1,0:T(8,128)(2,1)}, u32[]{:S(2)}) copy-start(bf16[1024,512]{1,0:T(8,128)(2,1)} %refs_2_.3) | copy-start | bytes 3145732
  21.6 3.3 %copy-start.6 = (s32[128]{0:T(128)S(1)}, s32[128]{0:T(128)}, u32[]{:S(2)}) copy-start(s32[128]{0:T(128)} %param.20) | copy-start | bytes 1540
  21.6 3.8 %collective-permute-start.6 = (bf16[128,512]{1,0:T(8,128)(2,1)S(1)}, bf16[128,512]{1,0:T(8,128)(2,1)S(1)}, u32[]{:S(2)}, u32[]{:S(2)}) collective-permute-start(bf16[128,512]{1,0:T(8,128)(2,1)S(1)} %next.9), channel_id=1, source_target_pairs={{0,8},{1,0},{2,10},{3,2},{4,12},{5,4},{6,14},{7,6},{8,9},{9,1},{10... | collective-permute-start | bytes 393224 | tf_op jit(solution)/shard_map/ppermute | solution.py:510
  23.3 3.6 %collective-permute-start.7 = (bf16[128,512]{1,0:T(8,128)(2,1)S(1)}, bf16[128,512]{1,0:T(8,128)(2,1)S(1)}, u32[]{:S(2)}, u32[]{:S(2)}) collective-permute-start(bf16[128,512]{1,0:T(8,128)(2,1)S(1)} %next.10), channel_id=1, source_target_pairs={{0,8},{1,0},{2,10},{3,2},{4,12},{5,4},{6,14},{7,6},{8,9},{9,1},{10... | collective-permute-start | bytes 393224 | tf_op jit(solution)/shard_map/ppermute | solution.py:510
  26.9 9.9 %collective-permute-start.9 = (bf16[128,512]{1,0:T(8,128)(2,1)S(1)}, bf16[128,512]{1,0:T(8,128)(2,1)S(1)}, u32[]{:S(2)}, u32[]{:S(2)}) collective-permute-start(bf16[128,512]{1,0:T(8,128)(2,1)S(1)} %get-tuple-element.90), channel_id=1, source_target_pairs={{0,1},{1,0},{2,3},{3,2},{4,5},{5,4},{6,7},{7,6},{8,16},{9,8},{10,1... | collective-permute-start | bytes 393224 | tf_op jit(solution)/shard_map/ppermute | solution.py:510
  31.5 6.7 %collective-permute-start.8 = (bf16[128,512]{1,0:T(8,128)(2,1)S(1)}, bf16[128,512]{1,0:T(8,128)(2,1)S(1)}, u32[]{:S(2)}, u32[]{:S(2)}) collective-permute-start(bf16[128,512]{1,0:T(8,128)(2,1)S(1)} %next.11), channel_id=1, source_target_pairs={{0,1},{1,0},{2,3},{3,2},{4,5},{5,4},{6,7},{7,6},{8,16},{9,8},{10,1... | collective-permute-start | bytes 393224 | tf_op jit(solution)/shard_map/ppermute | solution.py:510
  33.1 6.5 %collective-permute-start.10 = (bf16[128,512]{1,0:T(8,128)(2,1)S(1)}, bf16[128,512]{1,0:T(8,128)(2,1)S(1)}, u32[]{:S(2)}, u32[]{:S(2)}) collective-permute-start(bf16[128,512]{1,0:T(8,128)(2,1)S(1)} %next.12), channel_id=1, source_target_pairs={{0,1},{1,0},{2,3},{3,2},{4,5},{5,4},{6,7},{7,6},{8,16},{9,8},{10,1... | collective-permute-start | bytes 393224 | tf_op jit(solution)/shard_map/ppermute | solution.py:510
  34.7 6.3 %collective-permute-start.11 = (bf16[128,512]{1,0:T(8,128)(2,1)S(1)}, bf16[128,512]{1,0:T(8,128)(2,1)S(1)}, u32[]{:S(2)}, u32[]{:S(2)}) collective-permute-start(bf16[128,512]{1,0:T(8,128)(2,1)S(1)} %next.13), channel_id=1, source_target_pairs={{0,1},{1,0},{2,3},{3,2},{4,5},{5,4},{6,7},{7,6},{8,16},{9,8},{10,1... | collective-permute-start | bytes 393224 | tf_op jit(solution)/shard_map/ppermute | solution.py:510
  41.0 20.9 %copy-start.5 = (bf16[512,227]{0,1:T(8,128)(2,1)S(1)}, bf16[512,227]{0,1:T(8,128)(2,1)}, u32[]{:S(2)}) copy-start(bf16[512,227]{0,1:T(8,128)(2,1)} %param.18) | copy-start | bytes 697348
  41.0 11.3 %collective-permute-start.13 = (bf16[128,512]{1,0:T(8,128)(2,1)S(1)}, bf16[128,512]{1,0:T(8,128)(2,1)S(1)}, u32[]{:S(2)}, u32[]{:S(2)}) collective-permute-start(bf16[128,512]{1,0:T(8,128)(2,1)S(1)} %get-tuple-element.104), channel_id=1, source_target_pairs={{0,1},{1,0},{2,3},{3,2},{4,5},{5,21},{6,7},{7,6},{8,9},{9,8},{10,1... | collective-permute-start | bytes 393224 | tf_op jit(solution)/shard_map/ppermute | solution.py:510
  41.1 11.2 %collective-permute-start.14 = (bf16[128,512]{1,0:T(8,128)(2,1)S(1)}, bf16[128,512]{1,0:T(8,128)(2,1)S(1)}, u32[]{:S(2)}, u32[]{:S(2)}) collective-permute-start(bf16[128,512]{1,0:T(8,128)(2,1)S(1)} %get-tuple-element.105), channel_id=1, source_target_pairs={{0,1},{1,0},{2,3},{3,2},{4,5},{5,4},{6,7},{7,17},{8,9},{9,8},{10,1... | collective-permute-start | bytes 393224 | tf_op jit(solution)/shard_map/ppermute | solution.py:510
  41.6 12.6 %collective-permute-start.15 = (bf16[128,512]{1,0:T(8,128)(2,1)S(1)}, bf16[128,512]{1,0:T(8,128)(2,1)S(1)}, u32[]{:S(2)}, u32[]{:S(2)}) collective-permute-start(bf16[128,512]{1,0:T(8,128)(2,1)S(1)} %get-tuple-element.107.refs_3_), channel_id=1, source_target_pairs={{0,1},{1,17},{2,3},{3,2},{4,5},{5,4},{6,7},{7,6},{8,9},{9,19},{10,... | collective-permute-start | bytes 393224 | tf_op jit(solution)/shard_map/ppermute | solution.py:510
  52.3 2.0 %collective-permute-start.16 = (bf16[128,512]{1,0:T(8,128)(2,1)S(1)}, bf16[128,512]{1,0:T(8,128)(2,1)S(1)}, u32[]{:S(2)}, u32[]{:S(2)}) collective-permute-start(bf16[128,512]{1,0:T(8,128)(2,1)S(1)} %get-tuple-element.108.refs_4_), channel_id=1, source_target_pairs={{0,1},{1,0},{2,3},{3,17},{4,5},{5,4},{6,7},{7,6},{8,9},{9,8},{10,1... | collective-permute-start | bytes 393224 | tf_op jit(solution)/shard_map/ppermute | solution.py:510
  54.3 7.7 %collective-permute-start.17 = (bf16[64,512]{1,0:T(8,128)(2,1)S(1)}, bf16[64,512]{1,0:T(8,128)(2,1)S(1)}, u32[]{:S(2)}, u32[]{:S(2)}) collective-permute-start(bf16[64,512]{1,0:T(8,128)(2,1)S(1)} %get-tuple-element.110), channel_id=1, source_target_pairs={{0,1},{1,0},{2,3},{3,2},{4,5},{5,4},{6,7},{7,6},{8,9},{9,8},{10,11... | collective-permute-start | bytes 196616 | tf_op jit(solution)/shard_map/ppermute | solution.py:518

commit v11 on v9

--- a/solution.py
+++ b/solution.py
@@ -263,20 +263,38 @@
         columns_out[...] = jnp.transpose(index_out[...].astype(jnp.float32)).astype(jnp.bfloat16)
 
 
-def hold_kernel(*refs):
-    half = len(refs) // 2
-    for copy in fetch(refs[:half], refs[half:-1], refs[-1]):
-        copy.wait()
-
-
-def renew(fanout, columns, sender, own, w_project, w_message, w_update):
+def hold_kernel(w_project, w_message, w_update, held):
+    width = held.shape[1]
+    held[0] = w_project[0, :, :width]
+    held[1] = w_project[0, :, width:]
+    held[2] = w_update[0, :width, :]
+    held[3] = matmul(w_message[0], w_update[0, width:, :]).astype(jnp.bfloat16)
+
+
+def blocks_of(weights):
+    if len(weights) == 1:
+        (held,) = weights
+        return held[0], held[1], held[2], lambda gathered: matmul(gathered, held[3])
+    w_project, w_message, w_update = weights
+    width = w_message.shape[1]
+
+    def finish(gathered):
+        aggregate = matmul(gathered, w_message[0]).astype(jnp.bfloat16)
+        return matmul(aggregate, w_update[0, width:, :])
+
+    return w_project[0, :, :width], w_project[0, :, width:], w_update[0, :width, :], finish
+
+
+def renew(fanout, columns, sender, own, weights):
     chunk, width = own.shape
     nodes = sender.shape[0]
     tile = min(nodes, 256)
     names = lax.broadcasted_iota(jnp.int32, (chunk, tile), 1).astype(jnp.float32).astype(jnp.bfloat16)
     one_half = jnp.full((chunk, tile), 0.5, jnp.bfloat16)
     none = jnp.zeros((chunk, tile), jnp.bfloat16)
-    receiver = 0.5 * matmul(own, w_project[0, :, :width])
+    w_receive, _, w_own, finish = blocks_of(weights)
+    receiver = 0.5 * matmul(own, w_receive)
+    update = matmul(own, w_own)
     total = jnp.zeros((chunk, width), jnp.float32)
     for k in range(fanout):
         hits = []
@@ -286,10 +304,7 @@
         half = receiver + matmul(jnp.concatenate(hits, axis=1), sender)
         total = total + (half + half * jnp.tanh(half))
     gathered = (total * (1.0 / fanout)).astype(jnp.bfloat16)
-    aggregate = matmul(gathered, w_message[0]).astype(jnp.bfloat16)
-    update = silu_by_tanh(
-        matmul(own, w_update[0, :width, :]) + matmul(aggregate, w_update[0, width:, :])
-    )
+    update = silu_by_tanh(update + finish(gathered))
     return (own.astype(jnp.float32) + rms_scale(update)).astype(jnp.bfloat16)
 
 
@@ -299,12 +314,12 @@
         piece[...] = value[place * rows : (place + 1) * rows]
 
 
-def sender_kernel(group, at_segment, where, low, w_project, sender_low):
-    width = low.shape[1]
+def sender_kernel(group, at_segment, where, low, *refs):
+    weights, sender_low = refs[:-1], refs[-1]
 
     @pl.when(owns(where, group, at_segment))
     def _():
-        sender_low[...] = matmul(low[...], w_project[0, :, width:]).astype(jnp.bfloat16)
+        sender_low[...] = matmul(low[...], blocks_of(weights)[1]).astype(jnp.bfloat16)
 
 
 def half_of(where, group, chips, far, low, high, own):
@@ -324,26 +339,26 @@
 
 
 def first_kernel(
-    group, at_segment, chips, fanout, where, columns, sender_low, low, high, w_project, w_message, w_update, *outs
+    group, at_segment, chips, fanout, given, where, columns, sender_low, low, high, *refs
 ):
-    sender, pieces, own = outs[0], outs[1:-1], outs[-1]
-    half, width = low.shape
+    weights, sender, pieces, own = refs[:given], refs[given], refs[given + 1 : -1], refs[-1]
+    half = low.shape[0]
 
     @pl.when(owns(where, group, at_segment))
     def _():
         sender[:half, :] = sender_low[...]
-        sender[half:, :] = matmul(high[...], w_project[0, :, width:]).astype(jnp.bfloat16)
+        sender[half:, :] = matmul(high[...], blocks_of(weights)[1]).astype(jnp.bfloat16)
         start, state = 0, low
         if chips:
             start, state = half_of(where, group, chips, True, low, high, own), own
         rows = columns[pl.ds(start, half), :]
-        write_pieces(pieces, renew(fanout, rows, sender[...], state[...], w_project, w_message, w_update))
+        write_pieces(pieces, renew(fanout, rows, sender[...], state[...], weights))
 
 
 def second_kernel(
-    group, at_segment, chips, fanout, where, columns, sender, low, high, w_project, w_message, w_update, *outs
+    group, at_segment, chips, fanout, given, where, columns, sender, low, high, *refs
 ):
-    pieces, own = outs[:-1], outs[-1]
+    weights, pieces, own = refs[:given], refs[given:-1], refs[-1]
     half = low.shape[0]
 
     @pl.when(owns(where, group, at_segment))
@@ -352,7 +367,7 @@
         if chips:
             start, state = half_of(where, group, chips, False, low, high, own), own
         rows = columns[pl.ds(start, half), :]
-        write_pieces(pieces, renew(fanout, rows, sender[...], state[...], w_project, w_message, w_update))
+        write_pieces(pieces, renew(fanout, rows, sender[...], state[...], weights))
 
 
 def arrival(where, group, chips, last):
@@ -540,10 +555,9 @@
     held = call(
         hold_kernel,
         "hold",
-        [jax.ShapeDtypeStruct(weight.shape, bf16) for weight in weights],
+        [jax.ShapeDtypeStruct((4, width, width), bf16)],
         weights,
-        "hhh",
-        [pltpu.SemaphoreType.DMA((3,))],
+        "vvv",
     )
     own_payload, *held = lax.optimization_barrier((payloads[0], *held))
     arrived = [own_payload] + [to_chip(payloads[turn], turn) for turn in range(1, samples)]
@@ -573,22 +587,22 @@
     for layer in range(segments):
         at_segment, ends = min(layer, last), layer > last
         used = list(held) if layer <= last else came_weights
-        role = (group, at_segment, samples if ends else 0, fanout)
+        role = (group, at_segment, samples if ends else 0, fanout, len(used))
         pieces = [jax.ShapeDtypeStruct((share, width), bf16)] * (half // share) if ends else [state_shape]
         scratch = [pltpu.VMEM((half, width), bf16)]
         (sender_low,) = call(
             functools.partial(sender_kernel, group, at_segment),
             "sender",
             [state_shape],
-            [where, low, used[0]],
-            "wvv",
+            [where, low] + used,
+            "wv" + "v" * len(used),
         )
         sender, *first = call(
             functools.partial(first_kernel, *role),
             "first",
             [jax.ShapeDtypeStruct((nodes, width), bf16)] + pieces,
             [where, columns, sender_low, low, high] + used,
-            "wvvvvvvv",
+            "wvvvv" + "v" * len(used),
             scratch,
         )
         pairs = [(owner(m, layer), owner(m, layer + 1)) for m in range(samples)]
@@ -598,7 +612,7 @@
             "second",
             pieces,
             [where, columns, sender, low, high] + used,
-            "wvvvvvvv",
+            "wvvvv" + "v" * len(used),
             scratch,
         )
         low, high = new_low, send(second[0], pairs) if layer < last else second[0]

time: 60.5 us -> 61.3 us (1.013)
  waiting for transfers between devices: 14.4 us -> 12 us
  local copies, waits for them, and re-layouts: 3.46 us -> 5.42 us
  other arithmetic: 0.01 us -> 0.73 us
    unnamed x23 -> x19, local copies, waits for them, and re-layouts: 3.46 us -> 5.42 us
    ppermute x3, waiting for transfers between devices: 2.54 us -> 1.1 us  [to_chip(): return lax.ppermute(value, 'dom', pairs)]
    ppermute x11, waiting for transfers between devices: 9.74 us -> 8.73 us  [send(): lax.ppermute(value, ('segment', 'dom'), every_device(pairs, segments * pa...]
    concatenate x1, other arithmetic: 0.01 us -> 0.73 us  [resident(): jnp.concatenate([rows_of(neighbors.T), rows_of(send_rows), rows_of(grid_m...]
  transfers between devices with their start and end apart: 16 -> 16, of which waited for: 7 -> 7; matrix products, arithmetic and copies ran while one was open for 2% -> 3% of each run, Pallas kernels for 2% -> 3%
where the time goes in v11:
time: 61.3 us; the launch traced here: 61 us
  starting transfers between devices  39.6 us (65%)
  waiting for transfers between devices  12 us (20%)
  local copies, waits for them, and re-layouts  5.42 us (9%)
  Pallas kernels  3.05 us (5%)
  other arithmetic  0.73 us (1%)
    ppermute x11, starting transfers between devices, send(): lax.ppermute(value, ('segment', 'dom'), every_device(pairs, segments * pa...  26.4 us
    ppermute x2, starting transfers between devices, change_lane(): return lax.ppermute(value, 'dom', pairs)  9.49 us
    ppermute x11, waiting for transfers between devices, send(): lax.ppermute(value, ('segment', 'dom'), every_device(pairs, segments * pa...  8.73 us
    unnamed x19, local copies, waits for them, and re-layouts  5.42 us
    ppermute x3, starting transfers between devices, to_chip(): return lax.ppermute(value, 'dom', pairs)  3.67 us
    pallas_call x20, Pallas kernels, call(): pl.pallas_call(located if places[0] == 'w' else kernel, out_shape=shapes,...  3.05 us
    ppermute x2, waiting for transfers between devices, change_lane(): return lax.ppermute(value, 'dom', pairs)  2.16 us
  transfers between devices with their start and end apart: 16, of which 7 were waited for; matrix products, arithmetic and copies ran while one was open for 3% of the time, Pallas kernels for 3%

profile of v11, /device:TPU:3, one launch (start us, length us, event | category | flops | bytes accessed | tf_op | source)
XLA Modules:
  0.0 61.0 jit_solution(12652442895568002305)
XLA Ops:
  0.0 0.7 %collective-permute-start.10 = (bf16[1,1024,512]{2,1,0:T(8,128)(2,1)}, bf16[1,1024,512]{2,1,0:T(8,128)(2,1)S(1)}, u32[]{:S(2)}, u32[]{:S(2)}) collective-permute-start(bf16[1,1024,512]{2,1,0:T(8,128)(2,1)} %w_update), channel_id=1, source_target_pairs={{0,1},{1,0},{2,3},{3,2},{4,5},{5,4},{6,7},{7,6},{8,9},{9,8},{10,11... | collective-permute-start | bytes 3145736 | tf_op jit(solution)/shard_map/ppermute | solution.py:512
  0.7 0.0 collective-permute-start.8
  0.7 1.0 %copy.15 = bf16[4,128,227]{1,2,0:T(8,128)(2,1)S(1)} copy(bf16[4,128,227]{1,0,2:T(4,128)(2,1)} %param.12) | data formatting | bytes 464896 | tf_op args[0]
  1.7 0.7 %pad_add_fusion.refs_2_ = s32[14,128]{1,0:T(8,128)S(1)} fusion(s32[1,4]{1,0:T(1,128)} %bitcast.18, s32[4,64]{1,0:T(4,128)} %param.22, s32[8,64]{1,0:T(8,128)} %bitcast.17, s32[1,128]{1,0:T(1,128)} %bitcast.19), kind=kLoop, calls=%fused_computation.1 | loop fusion | flops 5376 | bytes 10768 | tf_op jit(solution)/shard_map/concatenate | solution.py:538
  2.4 0.0 copy-start.3
  2.4 0.9 %copy-done.3 = bf16[227,512]{1,0:T(8,128)(2,1)S(1)} copy-done((bf16[227,512]{1,0:T(8,128)(2,1)S(1)}, bf16[227,512]{1,0:T(8,128)(2,1)}, u32[]{:S(2)}) %copy-start.3) | copy-done | bytes 232472
  3.3 0.7 %encode.1 = (bf16[80,512]{1,0:T(8,128)(2,1)S(1)}, bf16[80,512]{1,0:T(8,128)(2,1)S(1)}, bf16[80,512]{1,0:T(8,128)(2,1)S(1)}, bf16[80,512]{1,0:T(8,128)(2,1)S(1)}) custom-call(s32[1]{0:T(128)} %bitcast.segment, s32[1]{0:T(128)} %bitcast.1.place, bf16[4,227,128]{2,1,0:T(8,128)(2,1)S(1)} %bitcast.13, bf16[227,512]{1,0:T(8,128)(2,1)S(1)} %copy-done.3, ...), custom_call_target="tpu_custom_call" | custom-call | bytes 799752 | tf_op jit(solution)/shard_map/encode/pallas_call | solution.py:448
  4.0 1.4 %collective-permute-start = (bf16[80,512]{1,0:T(8,128)(2,1)S(1)}, bf16[80,512]{1,0:T(8,128)(2,1)S(1)}, u32[]{:S(2)}, u32[]{:S(2)}) collective-permute-start(bf16[80,512]{1,0:T(8,128)(2,1)S(1)} %get-tuple-element.44), channel_id=1, source_target_pairs={{0,2},{1,3},{2,0},{3,1},{4,6},{5,7},{6,4},{7,5},{8,10},{9,11},{10,... | collective-permute-start | bytes 245768 | tf_op jit(solution)/shard_map/ppermute | solution.py:516
  5.4 2.3 %collective-permute-start.1 = (bf16[80,512]{1,0:T(8,128)(2,1)S(1)}, bf16[80,512]{1,0:T(8,128)(2,1)S(1)}, u32[]{:S(2)}, u32[]{:S(2)}) collective-permute-start(bf16[80,512]{1,0:T(8,128)(2,1)S(1)} %get-tuple-element.45), channel_id=1, source_target_pairs={{0,4},{1,5},{2,6},{3,7},{4,0},{5,1},{6,2},{7,3},{8,12},{9,13},{10,... | collective-permute-start | bytes 245768 | tf_op jit(solution)/shard_map/ppermute | solution.py:516
  7.7 0.0 collective-permute-start.2
  7.7 1.2 %copy-done.1 = bf16[1,1024,512]{2,1,0:T(8,128)(2,1)S(1)} copy-done((bf16[1,1024,512]{2,1,0:T(8,128)(2,1)S(1)}, bf16[1,1024,512]{2,1,0:T(8,128)(2,1)}, u32[]{:S(2)}) %copy-start.1) | copy-done | bytes 1048600
  8.9 1.2 %copy-done.2 = bf16[1,512,1024]{2,1,0:T(8,128)(2,1)S(1)} copy-done((bf16[1,512,1024]{2,1,0:T(8,128)(2,1)S(1)}, bf16[1,512,1024]{2,1,0:T(8,128)(2,1)}, u32[]{:S(2)}) %copy-start.2) | copy-done | bytes 1048600
  10.2 1.0 %copy-done.5 = bf16[1,512,512]{2,1,0:T(8,128)(2,1)S(1)} copy-done((bf16[1,512,512]{2,1,0:T(8,128)(2,1)S(1)}, bf16[1,512,512]{2,1,0:T(8,128)(2,1)}, u32[]{:S(2)}) %copy-start.5) | copy-done | bytes 524312
  11.2 0.6 hold.1.refs_1_.refs_4_
  11.8 0.0 collective-permute-done.refs_1_
  11.8 0.0 collective-permute-done.1.refs_2_
  11.8 1.1 %collective-permute-done.2.refs_3_ = bf16[80,512]{1,0:T(8,128)(2,1)S(1)} collective-permute-done((bf16[80,512]{1,0:T(8,128)(2,1)S(1)}, bf16[80,512]{1,0:T(8,128)(2,1)S(1)}, u32[]{:S(2)}, u32[]{:S(2)}) %collective-permute-start.2) | collective-permute-done | bytes 81952 | tf_op jit(solution)/shard_map/ppermute | solution.py:516
  13.0 2.7 %collective-permute-start.3 = (bf16[320,512]{1,0:T(8,128)(2,1)S(1)}, bf16[320,512]{1,0:T(8,128)(2,1)S(1)}, u32[]{:S(2)}, u32[]{:S(2)}) collective-permute-start(bf16[320,512]{1,0:T(8,128)(2,1)S(1)} %join.1.refs_0_), channel_id=1, source_target_pairs={{0,1},{1,0},{2,3},{3,2},{4,5},{5,4},{6,7},{7,6},{8,9},{9,8},{10,11... | collective-permute-start | bytes 983048 | tf_op jit(solution)/shard_map/ppermute | solution.py:520
  15.7 1.3 %collective-permute-done.3.refs_1_ = bf16[320,512]{1,0:T(8,128)(2,1)S(1)} collective-permute-done((bf16[320,512]{1,0:T(8,128)(2,1)S(1)}, bf16[320,512]{1,0:T(8,128)(2,1)S(1)}, u32[]{:S(2)}, u32[]{:S(2)}) %collective-permute-start.3) | collective-permute-done | bytes 327712 | tf_op jit(solution)/shard_map/ppermute | solution.py:520
  16.9 0.0 copy-start.8
  17.0 0.3 collective-permute-start.4
  17.3 3.5 %collective-permute-start.5 = (bf16[256,512]{1,0:T(8,128)(2,1)S(1)}, bf16[256,512]{1,0:T(8,128)(2,1)S(1)}, u32[]{:S(2)}, u32[]{:S(2)}) collective-permute-start(bf16[256,512]{1,0:T(8,128)(2,1)S(1)} %second.4), channel_id=1, source_target_pairs={{0,8},{1,0},{2,10},{3,2},{4,12},{5,4},{6,14},{7,6},{8,9},{9,1},{10... | collective-permute-start | bytes 786440 | tf_op jit(solution)/shard_map/ppermute | solution.py:512
  20.8 0.0 copy-done.6
  20.8 0.0 collective-permute-start.9
  20.8 0.0 copy-done
  20.8 0.0 copy-done.4
  20.8 0.0 copy-done.8
  20.8 0.4 prepare.1
  21.2 0.0 collective-permute-done.4.refs_0_.refs_2_
  21.3 2.8 %collective-permute-done.5.refs_3_ = bf16[256,512]{1,0:T(8,128)(2,1)S(1)} collective-permute-done((bf16[256,512]{1,0:T(8,128)(2,1)S(1)}, bf16[256,512]{1,0:T(8,128)(2,1)S(1)}, u32[]{:S(2)}, u32[]{:S(2)}) %collective-permute-start.5) | collective-permute-done | bytes 262176 | tf_op jit(solution)/shard_map/ppermute | solution.py:512
  24.1 6.7 %collective-permute-start.6 = (bf16[256,512]{1,0:T(8,128)(2,1)S(1)}, bf16[256,512]{1,0:T(8,128)(2,1)S(1)}, u32[]{:S(2)}, u32[]{:S(2)}) collective-permute-start(bf16[256,512]{1,0:T(8,128)(2,1)S(1)} %get-tuple-element.58), channel_id=1, source_target_pairs={{0,1},{1,0},{2,3},{3,2},{4,5},{5,4},{6,7},{7,6},{8,16},{9,8},{10,1... | collective-permute-start | bytes 786440 | tf_op jit(solution)/shard_map/ppermute | solution.py:512
  30.8 2.5 %collective-permute-start.7 = (bf16[256,512]{1,0:T(8,128)(2,1)S(1)}, bf16[256,512]{1,0:T(8,128)(2,1)S(1)}, u32[]{:S(2)}, u32[]{:S(2)}) collective-permute-start(bf16[256,512]{1,0:T(8,128)(2,1)S(1)} %second.5), channel_id=1, source_target_pairs={{0,1},{1,0},{2,3},{3,2},{4,5},{5,4},{6,7},{7,6},{8,16},{9,8},{10,1... | collective-permute-start | bytes 786440 | tf_op jit(solution)/shard_map/ppermute | solution.py:512
  33.3 1.2 %collective-permute-done.6.refs_0_.refs_2_ = bf16[256,512]{1,0:T(8,128)(2,1)S(1)} collective-permute-done((bf16[256,512]{1,0:T(8,128)(2,1)S(1)}, bf16[256,512]{1,0:T(8,128)(2,1)S(1)}, u32[]{:S(2)}, u32[]{:S(2)}) %collective-permute-start.6) | collective-permute-done | bytes 262176 | tf_op jit(solution)/shard_map/ppermute | solution.py:512
  34.5 2.8 %collective-permute-done.7.refs_3_ = bf16[256,512]{1,0:T(8,128)(2,1)S(1)} collective-permute-done((bf16[256,512]{1,0:T(8,128)(2,1)S(1)}, bf16[256,512]{1,0:T(8,128)(2,1)S(1)}, u32[]{:S(2)}, u32[]{:S(2)}) %collective-permute-start.7) | collective-permute-done | bytes 262176 | tf_op jit(solution)/shard_map/ppermute | solution.py:512
  37.3 0.0 collective-permute-done.9.refs_2_.refs_5_
  37.3 0.0 collective-permute-done.10.refs_3_.refs_6_
  37.3 0.0 collective-permute-done.8.refs_1_.refs_4_
  37.4 0.3 collective-permute-start.11
  37.6 0.3 collective-permute-start.12
  37.9 12.1 %collective-permute-start.13 = (bf16[128,512]{1,0:T(8,128)(2,1)S(1)}, bf16[128,512]{1,0:T(8,128)(2,1)S(1)}, u32[]{:S(2)}, u32[]{:S(2)}) collective-permute-start(bf16[128,512]{1,0:T(8,128)(2,1)S(1)} %get-tuple-element.65.refs_3_), channel_id=1, source_target_pairs={{0,1},{1,17},{2,3},{3,2},{4,5},{5,4},{6,7},{7,6},{8,9},{9,19},{10,... | collective-permute-start | bytes 393224 | tf_op jit(solution)/shard_map/ppermute | solution.py:512
  50.1 0.0 collective-permute-start.14
  50.1 0.0 collective-permute-done.11.refs_0_
  50.1 0.0 collective-permute-done.12.refs_1_
  50.1 1.9 %collective-permute-done.13.refs_1_ = bf16[128,512]{1,0:T(8,128)(2,1)S(1)} collective-permute-done((bf16[128,512]{1,0:T(8,128)(2,1)S(1)}, bf16[128,512]{1,0:T(8,128)(2,1)S(1)}, u32[]{:S(2)}, u32[]{:S(2)}) %collective-permute-start.13) | collective-permute-done | bytes 131104 | tf_op jit(solution)/shard_map/ppermute | solution.py:512
  52.0 0.0 collective-permute-done.14.refs_2_
  52.0 6.8 %collective-permute-start.15 = (bf16[64,512]{1,0:T(8,128)(2,1)S(1)}, bf16[64,512]{1,0:T(8,128)(2,1)S(1)}, u32[]{:S(2)}, u32[]{:S(2)}) collective-permute-start(bf16[64,512]{1,0:T(8,128)(2,1)S(1)} %get-tuple-element.68), channel_id=1, source_target_pairs={{0,1},{1,0},{2,3},{3,2},{4,5},{5,4},{6,7},{7,6},{8,9},{9,8},{10,11... | collective-permute-start | bytes 196616 | tf_op jit(solution)/shard_map/ppermute | solution.py:520
  58.8 0.9 %collective-permute-done.15.refs_5_ = bf16[64,512]{1,0:T(8,128)(2,1)S(1)} collective-permute-done((bf16[64,512]{1,0:T(8,128)(2,1)S(1)}, bf16[64,512]{1,0:T(8,128)(2,1)S(1)}, u32[]{:S(2)}, u32[]{:S(2)}) %collective-permute-start.15) | collective-permute-done | bytes 65568 | tf_op jit(solution)/shard_map/ppermute | solution.py:520
  59.7 1.2 %decode.1 = bf16[227,128]{1,0:T(8,128)(2,1)} custom-call(s32[1]{0:T(128)} %bitcast.segment, s32[1]{0:T(128)} %bitcast.1.place, f32[128,512]{1,0:T(8,128)S(1)} %get-tuple-element.54.refs_0_, bf16[64,128]{1,0:T(8,128)(2,1)S(1)} %get-tuple-element.55.refs_1_, bf16[1024,512]{1,0:T(8,128)(2,1)S(1)} %copy-done, bf16[227,512]{1,0:T(8,128)(2,1)S(1)} %bitcast.15, ...), custom_call_target="tpu_custom_call" | custom-call | bytes 1748744 | tf_op jit(solution)/shard_map/decode/pallas_call | solution.py:448
  (24 shorter events, 0.1 us)
Async XLA Ops:
  0.0 37.3 %collective-permute-start.10 = (bf16[1,1024,512]{2,1,0:T(8,128)(2,1)}, bf16[1,1024,512]{2,1,0:T(8,128)(2,1)S(1)}, u32[]{:S(2)}, u32[]{:S(2)}) collective-permute-start(bf16[1,1024,512]{2,1,0:T(8,128)(2,1)} %w_update), channel_id=1, source_target_pairs={{0,1},{1,0},{2,3},{3,2},{4,5},{5,4},{6,7},{7,6},{8,9},{9,8},{10,11... | collective-permute-start | bytes 3145736 | tf_op jit(solution)/shard_map/ppermute | solution.py:512
  0.7 36.6 %collective-permute-start.8 = (bf16[1,512,1024]{2,1,0:T(8,128)(2,1)}, bf16[1,512,1024]{2,1,0:T(8,128)(2,1)S(1)}, u32[]{:S(2)}, u32[]{:S(2)}) collective-permute-start(bf16[1,512,1024]{2,1,0:T(8,128)(2,1)} %w_project), channel_id=1, source_target_pairs={{0,1},{1,0},{2,3},{3,2},{4,5},{5,4},{6,7},{7,6},{8,9},{9,8},{10,11... | collective-permute-start | bytes 3145736 | tf_op jit(solution)/shard_map/ppermute | solution.py:512
  2.4 0.9 %copy-start.3 = (bf16[227,512]{1,0:T(8,128)(2,1)S(1)}, bf16[227,512]{1,0:T(8,128)(2,1)}, u32[]{:S(2)}) copy-start(bf16[227,512]{1,0:T(8,128)(2,1)} %refs_1_.3) | copy-start | bytes 697348
  4.0 7.8 %collective-permute-start = (bf16[80,512]{1,0:T(8,128)(2,1)S(1)}, bf16[80,512]{1,0:T(8,128)(2,1)S(1)}, u32[]{:S(2)}, u32[]{:S(2)}) collective-permute-start(bf16[80,512]{1,0:T(8,128)(2,1)S(1)} %get-tuple-element.44), channel_id=1, source_target_pairs={{0,2},{1,3},{2,0},{3,1},{4,6},{5,7},{6,4},{7,5},{8,10},{9,11},{10,... | collective-permute-start | bytes 245768 | tf_op jit(solution)/shard_map/ppermute | solution.py:516
  5.4 6.4 %collective-permute-start.1 = (bf16[80,512]{1,0:T(8,128)(2,1)S(1)}, bf16[80,512]{1,0:T(8,128)(2,1)S(1)}, u32[]{:S(2)}, u32[]{:S(2)}) collective-permute-start(bf16[80,512]{1,0:T(8,128)(2,1)S(1)} %get-tuple-element.45), channel_id=1, source_target_pairs={{0,4},{1,5},{2,6},{3,7},{4,0},{5,1},{6,2},{7,3},{8,12},{9,13},{10,... | collective-permute-start | bytes 245768 | tf_op jit(solution)/shard_map/ppermute | solution.py:516
  7.7 5.2 %collective-permute-start.2 = (bf16[80,512]{1,0:T(8,128)(2,1)S(1)}, bf16[80,512]{1,0:T(8,128)(2,1)S(1)}, u32[]{:S(2)}, u32[]{:S(2)}) collective-permute-start(bf16[80,512]{1,0:T(8,128)(2,1)S(1)} %get-tuple-element.46), channel_id=1, source_target_pairs={{0,6},{1,7},{2,4},{3,5},{4,2},{5,3},{6,0},{7,1},{8,14},{9,15},{10,... | collective-permute-start | bytes 245768 | tf_op jit(solution)/shard_map/ppermute | solution.py:516
  7.7 1.2 %copy-start.1 = (bf16[1,1024,512]{2,1,0:T(8,128)(2,1)S(1)}, bf16[1,1024,512]{2,1,0:T(8,128)(2,1)}, u32[]{:S(2)}) copy-start(bf16[1,1024,512]{2,1,0:T(8,128)(2,1)} %w_update) | copy-start | bytes 3145732
  8.9 1.2 %copy-start.2 = (bf16[1,512,1024]{2,1,0:T(8,128)(2,1)S(1)}, bf16[1,512,1024]{2,1,0:T(8,128)(2,1)}, u32[]{:S(2)}) copy-start(bf16[1,512,1024]{2,1,0:T(8,128)(2,1)} %w_project) | copy-start | bytes 3145732
  10.2 1.0 %copy-start.5 = (bf16[1,512,512]{2,1,0:T(8,128)(2,1)S(1)}, bf16[1,512,512]{2,1,0:T(8,128)(2,1)}, u32[]{:S(2)}) copy-start(bf16[1,512,512]{2,1,0:T(8,128)(2,1)} %w_message) | copy-start | bytes 1572868
  13.0 4.0 %collective-permute-start.3 = (bf16[320,512]{1,0:T(8,128)(2,1)S(1)}, bf16[320,512]{1,0:T(8,128)(2,1)S(1)}, u32[]{:S(2)}, u32[]{:S(2)}) collective-permute-start(bf16[320,512]{1,0:T(8,128)(2,1)S(1)} %join.1.refs_0_), channel_id=1, source_target_pairs={{0,1},{1,0},{2,3},{3,2},{4,5},{5,4},{6,7},{7,6},{8,9},{9,8},{10,11... | collective-permute-start | bytes 983048 | tf_op jit(solution)/shard_map/ppermute | solution.py:520
  16.9 3.9 %copy-start.6 = (bf16[1,512,512]{2,1,0:T(8,128)(2,1)S(1)}, bf16[1,512,512]{2,1,0:T(8,128)(2,1)}, u32[]{:S(2)}) copy-start(bf16[1,512,512]{2,1,0:T(8,128)(2,1)} %w_message) | copy-start | bytes 1572868
  16.9 3.9 %copy-start = (bf16[1024,512]{1,0:T(8,128)(2,1)S(1)}, bf16[1024,512]{1,0:T(8,128)(2,1)}, u32[]{:S(2)}) copy-start(bf16[1024,512]{1,0:T(8,128)(2,1)} %refs_2_.3) | copy-start | bytes 3145732
  16.9 3.9 %copy-start.4 = (bf16[227,512]{1,0:T(8,128)(2,1)S(1)}, bf16[227,512]{1,0:T(8,128)(2,1)}, u32[]{:S(2)}) copy-start(bf16[227,512]{1,0:T(8,128)(2,1)} %refs_1_.3) | copy-start | bytes 697348
  16.9 3.9 %copy-start.8 = (s32[128]{0:T(128)S(1)}, s32[128]{0:T(128)}, u32[]{:S(2)}) copy-start(s32[128]{0:T(128)} %param.20) | copy-start | bytes 1540
  17.0 4.3 %collective-permute-start.4 = (bf16[256,512]{1,0:T(8,128)(2,1)S(1)}, bf16[256,512]{1,0:T(8,128)(2,1)S(1)}, u32[]{:S(2)}, u32[]{:S(2)}) collective-permute-start(bf16[256,512]{1,0:T(8,128)(2,1)S(1)} %get-tuple-element.51), channel_id=1, source_target_pairs={{0,8},{1,0},{2,10},{3,2},{4,12},{5,4},{6,14},{7,6},{8,9},{9,1},{10... | collective-permute-start | bytes 786440 | tf_op jit(solution)/shard_map/ppermute | solution.py:512
  17.3 6.8 %collective-permute-start.5 = (bf16[256,512]{1,0:T(8,128)(2,1)S(1)}, bf16[256,512]{1,0:T(8,128)(2,1)S(1)}, u32[]{:S(2)}, u32[]{:S(2)}) collective-permute-start(bf16[256,512]{1,0:T(8,128)(2,1)S(1)} %second.4), channel_id=1, source_target_pairs={{0,8},{1,0},{2,10},{3,2},{4,12},{5,4},{6,14},{7,6},{8,9},{9,1},{10... | collective-permute-start | bytes 786440 | tf_op jit(solution)/shard_map/ppermute | solution.py:512
  20.8 16.5 %collective-permute-start.9 = (bf16[1,512,512]{2,1,0:T(8,128)(2,1)S(1)}, bf16[1,512,512]{2,1,0:T(8,128)(2,1)S(1)}, u32[]{:S(2)}, u32[]{:S(2)}) collective-permute-start(bf16[1,512,512]{2,1,0:T(8,128)(2,1)S(1)} %copy-done.6), channel_id=1, source_target_pairs={{0,1},{1,0},{2,3},{3,2},{4,5},{5,4},{6,7},{7,6},{8,9},{9,8},{10,11... | collective-permute-start | bytes 1572872 | tf_op jit(solution)/shard_map/ppermute | solution.py:512
  24.1 10.4 %collective-permute-start.6 = (bf16[256,512]{1,0:T(8,128)(2,1)S(1)}, bf16[256,512]{1,0:T(8,128)(2,1)S(1)}, u32[]{:S(2)}, u32[]{:S(2)}) collective-permute-start(bf16[256,512]{1,0:T(8,128)(2,1)S(1)} %get-tuple-element.58), channel_id=1, source_target_pairs={{0,1},{1,0},{2,3},{3,2},{4,5},{5,4},{6,7},{7,6},{8,16},{9,8},{10,1... | collective-permute-start | bytes 786440 | tf_op jit(solution)/shard_map/ppermute | solution.py:512
  30.8 6.5 %collective-permute-start.7 = (bf16[256,512]{1,0:T(8,128)(2,1)S(1)}, bf16[256,512]{1,0:T(8,128)(2,1)S(1)}, u32[]{:S(2)}, u32[]{:S(2)}) collective-permute-start(bf16[256,512]{1,0:T(8,128)(2,1)S(1)} %second.5), channel_id=1, source_target_pairs={{0,1},{1,0},{2,3},{3,2},{4,5},{5,4},{6,7},{7,6},{8,16},{9,8},{10,1... | collective-permute-start | bytes 786440 | tf_op jit(solution)/shard_map/ppermute | solution.py:512
  37.4 12.7 %collective-permute-start.11 = (bf16[128,512]{1,0:T(8,128)(2,1)S(1)}, bf16[128,512]{1,0:T(8,128)(2,1)S(1)}, u32[]{:S(2)}, u32[]{:S(2)}) collective-permute-start(bf16[128,512]{1,0:T(8,128)(2,1)S(1)} %get-tuple-element.62), channel_id=1, source_target_pairs={{0,1},{1,0},{2,3},{3,2},{4,5},{5,21},{6,7},{7,6},{8,9},{9,8},{10,1... | collective-permute-start | bytes 393224 | tf_op jit(solution)/shard_map/ppermute | solution.py:512
  37.6 12.5 %collective-permute-start.12 = (bf16[128,512]{1,0:T(8,128)(2,1)S(1)}, bf16[128,512]{1,0:T(8,128)(2,1)S(1)}, u32[]{:S(2)}, u32[]{:S(2)}) collective-permute-start(bf16[128,512]{1,0:T(8,128)(2,1)S(1)} %get-tuple-element.63), channel_id=1, source_target_pairs={{0,1},{1,0},{2,3},{3,2},{4,5},{5,4},{6,7},{7,17},{8,9},{9,8},{10,1... | collective-permute-start | bytes 393224 | tf_op jit(solution)/shard_map/ppermute | solution.py:512
  37.9 21.8 %copy-start.7 = (bf16[512,227]{0,1:T(8,128)(2,1)S(1)}, bf16[512,227]{0,1:T(8,128)(2,1)}, u32[]{:S(2)}) copy-start(bf16[512,227]{0,1:T(8,128)(2,1)} %param.18) | copy-start | bytes 697348
  37.9 14.1 %collective-permute-start.13 = (bf16[128,512]{1,0:T(8,128)(2,1)S(1)}, bf16[128,512]{1,0:T(8,128)(2,1)S(1)}, u32[]{:S(2)}, u32[]{:S(2)}) collective-permute-start(bf16[128,512]{1,0:T(8,128)(2,1)S(1)} %get-tuple-element.65.refs_3_), channel_id=1, source_target_pairs={{0,1},{1,17},{2,3},{3,2},{4,5},{5,4},{6,7},{7,6},{8,9},{9,19},{10,... | collective-permute-start | bytes 393224 | tf_op jit(solution)/shard_map/ppermute | solution.py:512
  50.1 2.0 %collective-permute-start.14 = (bf16[128,512]{1,0:T(8,128)(2,1)S(1)}, bf16[128,512]{1,0:T(8,128)(2,1)S(1)}, u32[]{:S(2)}, u32[]{:S(2)}) collective-permute-start(bf16[128,512]{1,0:T(8,128)(2,1)S(1)} %get-tuple-element.66.refs_4_), channel_id=1, source_target_pairs={{0,1},{1,0},{2,3},{3,17},{4,5},{5,4},{6,7},{7,6},{8,9},{9,8},{10,1... | collective-permute-start | bytes 393224 | tf_op jit(solution)/shard_map/ppermute | solution.py:512
  52.0 7.7 %collective-permute-start.15 = (bf16[64,512]{1,0:T(8,128)(2,1)S(1)}, bf16[64,512]{1,0:T(8,128)(2,1)S(1)}, u32[]{:S(2)}, u32[]{:S(2)}) collective-permute-start(bf16[64,512]{1,0:T(8,128)(2,1)S(1)} %get-tuple-element.68), channel_id=1, source_target_pairs={{0,1},{1,0},{2,3},{3,2},{4,5},{5,4},{6,7},{7,6},{8,9},{9,8},{10,11... | collective-permute-start | bytes 196616 | tf_op jit(solution)/shard_map/ppermute | solution.py:520

commit v12 on v11

--- a/solution.py
+++ b/solution.py
@@ -8,6 +8,7 @@
 from jax.sharding import PartitionSpec as P
 
 epsilon = 1e-05
+DIGIT = 256
 VMEM = pl.BlockSpec(memory_space=pltpu.VMEM)
 SMEM = pl.BlockSpec(memory_space=pltpu.SMEM)
 HBM = pl.BlockSpec(memory_space=pltpu.HBM)
@@ -225,14 +226,22 @@
         joined[place * rows : (place + 1) * rows, :] = payload[...]
 
 
+def columns_of(names):
+    fanout, nodes = names.shape
+    tile = min(nodes, DIGIT)
+    rows = [names - number * tile for number in range(nodes // tile)]
+    rows.append(jnp.zeros((128 - fanout * len(rows), nodes), jnp.float32))
+    return jnp.transpose(jnp.concatenate(rows, axis=0)).astype(jnp.bfloat16)
+
+
 def index_kernel(parts, mesh_rows, where, *refs):
     lanes, (columns_out, low, high), index_out = refs[:-4], refs[-4:-1], refs[-1]
     nodes = columns_out.shape[0]
     group = len(lanes)
     rows = lanes[0].shape[0] // (parts // group)
-    chip, lane_place = place_of(where, group)
-
-    @pl.when(lane_place == 0)
+    chip, _ = place_of(where, group)
+
+    @pl.when(owns(where, group, 0))
     def _():
         tables = []
         for part in range(parts):
@@ -244,7 +253,6 @@
             coded = lane[pl.ds(base, rows - mesh_rows), :384].astype(jnp.float32).astype(jnp.int32)
             tables.append(coded[: coded.shape[0] // 2])
         fanout = tables[0].shape[0]
-        index_out[fanout:, :] = jnp.zeros((index_out.shape[0] - fanout, nodes), jnp.int32)
         for part in range(parts):
             block = tables[part][:, :128]
             row = tables[part][:, 128:256]
@@ -256,25 +264,35 @@
                 picked = jnp.take_along_axis(lists, row, axis=1)
                 picked = jnp.where(picked == mesh_rows, parts * mesh_rows, source * mesh_rows + picked)
                 found = jnp.where(block == list_index + 1, picked, found)
-            index_out[:fanout, part * mesh_rows : (part + 1) * mesh_rows] = found[:, :mesh_rows]
-        tile = min(nodes, 256)
-        for number in range(1, nodes // tile):
-            index_out[number * fanout : (number + 1) * fanout, :] = index_out[:fanout, :] - number * tile
-        columns_out[...] = jnp.transpose(index_out[...].astype(jnp.float32)).astype(jnp.bfloat16)
-
-
-def hold_kernel(w_project, w_message, w_update, held):
-    width = held.shape[1]
-    held[0] = w_project[0, :, :width]
-    held[1] = w_project[0, :, width:]
-    held[2] = w_update[0, :width, :]
-    held[3] = matmul(w_message[0], w_update[0, width:, :]).astype(jnp.bfloat16)
+            index_out[:, part * mesh_rows : (part + 1) * mesh_rows] = found[:, :mesh_rows]
+        names = index_out[...]
+        high_digit = names // DIGIT
+        digits = jnp.concatenate([high_digit, names - high_digit * DIGIT], axis=0)
+        low[parts // 2 * mesh_rows :, :] = digits.astype(jnp.float32).astype(jnp.bfloat16)
+        columns_out[...] = columns_of(names.astype(jnp.float32))
+
+
+def hold_kernel(w_project, w_message, w_update, receive, send, own, edges, message, update, semaphores):
+    width = own.shape[0]
+    sources = [
+        w_message.at[0],
+        w_update.at[0, width:],
+        w_project.at[0, :, :width],
+        w_project.at[0, :, width:],
+        w_update.at[0, :width],
+    ]
+    copies = fetch(sources, [message, update, receive, send, own], semaphores)
+    copies[0].wait()
+    copies[1].wait()
+    edges[...] = matmul(message[...], update[...]).astype(jnp.bfloat16)
+    for copy in copies[2:]:
+        copy.wait()
 
 
 def blocks_of(weights):
-    if len(weights) == 1:
-        (held,) = weights
-        return held[0], held[1], held[2], lambda gathered: matmul(gathered, held[3])
+    if len(weights) == 4:
+        receive, send, own, edges = weights
+        return receive[...], send[...], own[...], lambda gathered: matmul(gathered, edges[...])
     w_project, w_message, w_update = weights
     width = w_message.shape[1]
 
@@ -288,7 +306,7 @@
 def renew(fanout, columns, sender, own, weights):
     chunk, width = own.shape
     nodes = sender.shape[0]
-    tile = min(nodes, 256)
+    tile = min(nodes, DIGIT)
     names = lax.broadcasted_iota(jnp.int32, (chunk, tile), 1).astype(jnp.float32).astype(jnp.bfloat16)
     one_half = jnp.full((chunk, tile), 0.5, jnp.bfloat16)
     none = jnp.zeros((chunk, tile), jnp.bfloat16)
@@ -309,21 +327,24 @@
 
 
 def write_pieces(pieces, value):
-    rows = pieces[0].shape[0]
+    rows = value.shape[0] // len(pieces)
     for place, piece in enumerate(pieces):
-        piece[...] = value[place * rows : (place + 1) * rows]
-
-
-def sender_kernel(group, at_segment, where, low, *refs):
-    weights, sender_low = refs[:-1], refs[-1]
+        piece[:rows, :] = value[place * rows : (place + 1) * rows]
+
+
+def sender_kernel(group, at_segment, fanout, rows, where, low, *refs):
+    weights, sender_low, columns = (refs[:-2], *refs[-2:]) if fanout else (refs[:-1], refs[-1], None)
 
     @pl.when(owns(where, group, at_segment))
     def _():
-        sender_low[...] = matmul(low[...], blocks_of(weights)[1]).astype(jnp.bfloat16)
+        sender_low[...] = matmul(low[:rows, :], blocks_of(weights)[1]).astype(jnp.bfloat16)
+        if fanout:
+            digits = low[rows:, :].astype(jnp.float32)
+            columns[...] = columns_of(digits[:fanout] * DIGIT + digits[fanout:])
 
 
 def half_of(where, group, chips, far, low, high, own):
-    half = low.shape[0]
+    half = high.shape[0]
     chip, _ = place_of(where, group)
     upper = (chip < chips // 2) if far else (chip >= chips // 2)
 
@@ -342,24 +363,27 @@
     group, at_segment, chips, fanout, given, where, columns, sender_low, low, high, *refs
 ):
     weights, sender, pieces, own = refs[:given], refs[given], refs[given + 1 : -1], refs[-1]
-    half = low.shape[0]
+    half = high.shape[0]
 
     @pl.when(owns(where, group, at_segment))
     def _():
         sender[:half, :] = sender_low[...]
         sender[half:, :] = matmul(high[...], blocks_of(weights)[1]).astype(jnp.bfloat16)
-        start, state = 0, low
+        start, state = 0, low[:half, :]
         if chips:
-            start, state = half_of(where, group, chips, True, low, high, own), own
+            start = half_of(where, group, chips, True, low, high, own)
+            state = own[...]
         rows = columns[pl.ds(start, half), :]
-        write_pieces(pieces, renew(fanout, rows, sender[...], state[...], weights))
+        write_pieces(pieces, renew(fanout, rows, sender[...], state, weights))
+        if pieces[0].shape[0] > half:
+            pieces[0][half:, :] = low[half:, :]
 
 
 def second_kernel(
     group, at_segment, chips, fanout, given, where, columns, sender, low, high, *refs
 ):
     weights, pieces, own = refs[:given], refs[given:-1], refs[-1]
-    half = low.shape[0]
+    half = high.shape[0]
 
     @pl.when(owns(where, group, at_segment))
     def _():
@@ -512,8 +536,19 @@
         return lax.ppermute(value, ("segment", "dom"), every_device(pairs, segments * parts, group))
 
     def to_chip(value, steps):
-        pairs = [(at, (at // group ^ steps) * group + at % group) for at in range(parts)]
-        return lax.ppermute(value, "dom", pairs)
+        giver = steps - 1
+        pairs = []
+        for at in range(segments):
+            for dom in range(parts):
+                chip, lane = divmod(dom, group)
+                across = (chip ^ steps) * group + lane
+                if at == giver:
+                    pairs.append((device(at, dom), device(0, across)))
+                elif at == 0:
+                    pairs.append((device(at, dom), device(giver, dom)))
+                else:
+                    pairs.append((device(at, dom), device(at, chip * group + (lane + 1) % group)))
+        return lax.ppermute(value, ("segment", "dom"), pairs)
 
     def change_lane(value, steps):
         pairs = [(at, at - at % group + (at + steps) % group) for at in range(parts)]
@@ -555,9 +590,10 @@
     held = call(
         hold_kernel,
         "hold",
-        [jax.ShapeDtypeStruct((4, width, width), bf16)],
+        [jax.ShapeDtypeStruct((width, width), bf16)] * 4,
         weights,
-        "vvv",
+        "hhh",
+        [pltpu.VMEM((width, width), bf16)] * 2 + [pltpu.SemaphoreType.DMA((5,))],
     )
     own_payload, *held = lax.optimization_barrier((payloads[0], *held))
     arrived = [own_payload] + [to_chip(payloads[turn], turn) for turn in range(1, samples)]
@@ -576,12 +612,12 @@
         "index",
         [
             jax.ShapeDtypeStruct((nodes, 128), bf16),
-            jax.ShapeDtypeStruct((half, width), bf16),
+            jax.ShapeDtypeStruct((half + 2 * fanout, width), bf16),
             jax.ShapeDtypeStruct((half, width), bf16),
         ],
         [where] + lanes,
         "w" + "v" * group,
-        [pltpu.VMEM((128, nodes), jnp.int32)],
+        [pltpu.VMEM((fanout, nodes), jnp.int32)],
     )
     state_shape = jax.ShapeDtypeStruct((half, width), bf16)
     for layer in range(segments):
@@ -590,17 +626,20 @@
         role = (group, at_segment, samples if ends else 0, fanout, len(used))
         pieces = [jax.ShapeDtypeStruct((share, width), bf16)] * (half // share) if ends else [state_shape]
         scratch = [pltpu.VMEM((half, width), bf16)]
-        (sender_low,) = call(
-            functools.partial(sender_kernel, group, at_segment),
+        arrives = 0 < layer <= last
+        sender_low, *found = call(
+            functools.partial(sender_kernel, group, at_segment, fanout if arrives else 0, half),
             "sender",
-            [state_shape],
+            [state_shape] + [jax.ShapeDtypeStruct((nodes, 128), bf16)] * arrives,
             [where, low] + used,
             "wv" + "v" * len(used),
         )
+        columns = found[0] if arrives else columns
+        tall = jax.ShapeDtypeStruct((half + 2 * fanout, width), bf16)
         sender, *first = call(
             functools.partial(first_kernel, *role),
             "first",
-            [jax.ShapeDtypeStruct((nodes, width), bf16)] + pieces,
+            [jax.ShapeDtypeStruct((nodes, width), bf16)] + ([tall] if layer < last else pieces),
             [where, columns, sender_low, low, high] + used,
             "wvvvv" + "v" * len(used),
             scratch,
@@ -664,14 +703,17 @@
     return prediction.T.reshape(1, grid_rows, channels)
 
 
-def fits(mesh):
+def chosen_plan(mesh, *arrays):
     segments, parts = mesh.shape["segment"], mesh.shape["dom"]
-    return segments == 4 and parts % segments == 0 and parts <= 16
+    samples, width = arrays[0].shape[0], arrays[1].shape[1]
+    nodes = parts * arrays[9].shape[0]
+    fits = samples == segments == 4 and parts % samples == 0 and parts > samples and nodes == width
+    return (resident if fits else streamed)(*arrays)
 
 
 def solution(mesh):
     return jax.shard_map(
-        resident if fits(mesh) else streamed,
+        functools.partial(chosen_plan, mesh),
         mesh=mesh,
         in_specs=(
             P(None, "dom", None),

time: 61.3 us -> 58.2 us (0.949)
  the two profiles are of different devices: /device:TPU:3 before, /device:TPU:9 now
where the time goes in v12:
time: 58.2 us; the launch traced here: 58 us
  starting transfers between devices  42.3 us (73%)
  waiting for transfers between devices  8.94 us (15%)
  local copies, waits for them, and re-layouts  3.46 us (6%)
  Pallas kernels  3.16 us (5%)
    ppermute x11, starting transfers between devices, send(): lax.ppermute(value, ('segment', 'dom'), every_device(pairs, segments * pa...  32.1 us
    ppermute x2, starting transfers between devices, change_lane(): return lax.ppermute(value, 'dom', pairs)  7.18 us
    ppermute x11, waiting for transfers between devices, send(): lax.ppermute(value, ('segment', 'dom'), every_device(pairs, segments * pa...  6.63 us
    unnamed x23, local copies, waits for them, and re-layouts  3.46 us
    pallas_call x20, Pallas kernels, call(): pl.pallas_call(located if places[0] == 'w' else kernel, out_shape=shapes,...  3.16 us
    ppermute x3, starting transfers between devices, to_chip(): return lax.ppermute(value, ('segment', 'dom'), pairs)  2.95 us
    ppermute x2, waiting for transfers between devices, change_lane(): return lax.ppermute(value, 'dom', pairs)  2.16 us
  transfers between devices with their start and end apart: 16, of which 7 were waited for; matrix products, arithmetic and copies ran while one was open for 2% of the time, Pallas kernels for 3%

profile of v12, /device:TPU:9, one launch (start us, length us, event | category | flops | bytes accessed | tf_op | source)
XLA Modules:
  0.0 58.0 jit_solution(10197108727329808415)
XLA Ops:
  0.0 0.0 copy-start.10
  0.0 0.0 copy-start.3
  0.0 0.0 copy-start.4
  0.0 0.7 %collective-permute-start.10 = (bf16[1,1024,512]{2,1,0:T(8,128)(2,1)}, bf16[1,1024,512]{2,1,0:T(8,128)(2,1)S(1)}, u32[]{:S(2)}, u32[]{:S(2)}) collective-permute-start(bf16[1,1024,512]{2,1,0:T(8,128)(2,1)} %w_update), channel_id=1, source_target_pairs={{0,1},{1,0},{2,3},{3,2},{4,5},{5,4},{6,7},{7,6},{8,9},{9,8},{10,11... | collective-permute-start | bytes 3145736 | tf_op jit(solution)/shard_map/ppermute | solution.py:536
  0.8 0.1 collective-permute-start.8
  0.8 1.0 %copy.15 = bf16[4,128,227]{1,2,0:T(8,128)(2,1)S(1)} copy(bf16[4,128,227]{1,0,2:T(4,128)(2,1)} %param.12) | data formatting | bytes 464896 | tf_op args[0]
  1.8 0.0 copy-done.7
  1.8 0.0 copy-done.8
  1.8 0.0 copy-done.9
  1.8 0.0 copy-done.10
  1.9 0.0 copy-done.3
  1.9 0.7 %encode.1 = (bf16[80,512]{1,0:T(8,128)(2,1)S(1)}, bf16[80,512]{1,0:T(8,128)(2,1)S(1)}, bf16[80,512]{1,0:T(8,128)(2,1)S(1)}, bf16[80,512]{1,0:T(8,128)(2,1)S(1)}) custom-call(s32[1]{0:T(128)} %bitcast.segment, s32[1]{0:T(128)} %bitcast.1.place, bf16[4,227,128]{2,1,0:T(8,128)(2,1)S(1)} %bitcast.13, bf16[227,512]{1,0:T(8,128)(2,1)S(1)} %copy-done.3, ...), custom_call_target="tpu_custom_call" | custom-call | bytes 799752 | tf_op jit(solution)/shard_map/encode/pallas_call | solution.py:472
  2.6 0.1 collective-permute-start
  2.7 1.6 %collective-permute-start.1 = (bf16[80,512]{1,0:T(8,128)(2,1)S(1)}, bf16[80,512]{1,0:T(8,128)(2,1)S(1)}, u32[]{:S(2)}, u32[]{:S(2)}) collective-permute-start(bf16[80,512]{1,0:T(8,128)(2,1)S(1)} %get-tuple-element.60), channel_id=1, source_target_pairs={{0,8},{1,9},{2,10},{3,11},{4,12},{5,13},{6,14},{7,15},{8,4},{9,5},... | collective-permute-start | bytes 245768 | tf_op jit(solution)/shard_map/ppermute | solution.py:551
  4.3 1.2 %collective-permute-start.2 = (bf16[80,512]{1,0:T(8,128)(2,1)S(1)}, bf16[80,512]{1,0:T(8,128)(2,1)S(1)}, u32[]{:S(2)}, u32[]{:S(2)}) collective-permute-start(bf16[80,512]{1,0:T(8,128)(2,1)S(1)} %get-tuple-element.61), channel_id=1, source_target_pairs={{0,16},{1,17},{2,18},{3,19},{4,20},{5,21},{6,22},{7,23},{8,9},{9,8... | collective-permute-start | bytes 245768 | tf_op jit(solution)/shard_map/ppermute | solution.py:551
  5.6 0.0 copy-done.4
  5.6 1.2 %copy-done.1 = bf16[1,1024,512]{2,1,0:T(8,128)(2,1)S(1)} copy-done((bf16[1,1024,512]{2,1,0:T(8,128)(2,1)S(1)}, bf16[1,1024,512]{2,1,0:T(8,128)(2,1)}, u32[]{:S(2)}) %copy-start.1) | copy-done | bytes 1048600
  6.8 1.2 %copy-done.2 = bf16[1,512,1024]{2,1,0:T(8,128)(2,1)S(1)} copy-done((bf16[1,512,1024]{2,1,0:T(8,128)(2,1)S(1)}, bf16[1,512,1024]{2,1,0:T(8,128)(2,1)}, u32[]{:S(2)}) %copy-start.2) | copy-done | bytes 1048600
  8.0 0.7 %hold.1 = (bf16[512,512]{1,0:T(8,128)(2,1)S(1)}, bf16[512,512]{1,0:T(8,128)(2,1)S(1)}, bf16[512,512]{1,0:T(8,128)(2,1)S(1)}, bf16[512,512]{1,0:T(8,128)(2,1)S(1)}) custom-call(bf16[1,512,1024]{2,1,0:T(8,128)(2,1)S(1)} %copy-done.2, bf16[1,512,512]{2,1,0:T(8,128)(2,1)S(1)} %copy-done.4, bf16[1,1024,512]{2,1,0:T(8,128)(2,1)S(1)} %copy-done.1), custom_call_target="tpu_custom_call" | custom-call | bytes 4718592 | tf_op jit(solution)/shard_map/hold/pallas_call | solution.py:472
  8.8 0.0 collective-permute-done.refs_1_
  8.8 0.1 collective-permute-done.1.refs_2_
  8.9 0.0 collective-permute-done.2.refs_3_
  8.9 3.0 %collective-permute-start.3 = (bf16[320,512]{1,0:T(8,128)(2,1)S(1)}, bf16[320,512]{1,0:T(8,128)(2,1)S(1)}, u32[]{:S(2)}, u32[]{:S(2)}) collective-permute-start(bf16[320,512]{1,0:T(8,128)(2,1)S(1)} %join.1.refs_0_), channel_id=1, source_target_pairs={{0,1},{1,0},{2,3},{3,2},{4,5},{5,4},{6,7},{7,6},{8,9},{9,8},{10,11... | collective-permute-start | bytes 983048 | tf_op jit(solution)/shard_map/ppermute | solution.py:555
  11.9 1.3 %collective-permute-done.3.refs_1_ = bf16[320,512]{1,0:T(8,128)(2,1)S(1)} collective-permute-done((bf16[320,512]{1,0:T(8,128)(2,1)S(1)}, bf16[320,512]{1,0:T(8,128)(2,1)S(1)}, u32[]{:S(2)}, u32[]{:S(2)}) %collective-permute-start.3) | collective-permute-done | bytes 327712 | tf_op jit(solution)/shard_map/ppermute | solution.py:555
  13.2 3.5 %collective-permute-start.4 = (bf16[272,512]{1,0:T(8,128)(2,1)S(1)}, bf16[272,512]{1,0:T(8,128)(2,1)S(1)}, u32[]{:S(2)}, u32[]{:S(2)}) collective-permute-start(bf16[272,512]{1,0:T(8,128)(2,1)S(1)} %get-tuple-element.69), channel_id=1, source_target_pairs={{0,8},{1,0},{2,10},{3,2},{4,12},{5,4},{6,14},{7,6},{8,9},{9,1},{10... | collective-permute-start | bytes 835592 | tf_op jit(solution)/shard_map/ppermute | solution.py:536
  16.7 2.6 %collective-permute-start.5 = (bf16[256,512]{1,0:T(8,128)(2,1)S(1)}, bf16[256,512]{1,0:T(8,128)(2,1)S(1)}, u32[]{:S(2)}, u32[]{:S(2)}) collective-permute-start(bf16[256,512]{1,0:T(8,128)(2,1)S(1)} %second.4), channel_id=1, source_target_pairs={{0,8},{1,0},{2,10},{3,2},{4,12},{5,4},{6,14},{7,6},{8,9},{9,1},{10... | collective-permute-start | bytes 786440 | tf_op jit(solution)/shard_map/ppermute | solution.py:536
  19.3 0.1 collective-permute-start.9
  19.4 0.4 prepare.1
  19.8 0.0 collective-permute-done.4.refs_0_.refs_2_
  19.8 2.2 %collective-permute-done.5.refs_3_ = bf16[256,512]{1,0:T(8,128)(2,1)S(1)} collective-permute-done((bf16[256,512]{1,0:T(8,128)(2,1)S(1)}, bf16[256,512]{1,0:T(8,128)(2,1)S(1)}, u32[]{:S(2)}, u32[]{:S(2)}) %collective-permute-start.5) | collective-permute-done | bytes 262176 | tf_op jit(solution)/shard_map/ppermute | solution.py:536
  22.0 1.7 %collective-permute-start.6 = (bf16[272,512]{1,0:T(8,128)(2,1)S(1)}, bf16[272,512]{1,0:T(8,128)(2,1)S(1)}, u32[]{:S(2)}, u32[]{:S(2)}) collective-permute-start(bf16[272,512]{1,0:T(8,128)(2,1)S(1)} %get-tuple-element.78), channel_id=1, source_target_pairs={{0,1},{1,0},{2,3},{3,2},{4,5},{5,4},{6,7},{7,6},{8,16},{9,8},{10,1... | collective-permute-start | bytes 835592 | tf_op jit(solution)/shard_map/ppermute | solution.py:536
  23.6 0.0 collective-permute-start.7
  23.6 1.2 %collective-permute-done.6.refs_0_.refs_2_ = bf16[272,512]{1,0:T(8,128)(2,1)S(1)} collective-permute-done((bf16[272,512]{1,0:T(8,128)(2,1)S(1)}, bf16[272,512]{1,0:T(8,128)(2,1)S(1)}, u32[]{:S(2)}, u32[]{:S(2)}) %collective-permute-start.6) | collective-permute-done | bytes 278560 | tf_op jit(solution)/shard_map/ppermute | solution.py:536
  24.8 0.4 collective-permute-done.7.refs_3_
  25.2 0.0 collective-permute-done.9.refs_2_.refs_5_
  25.2 0.0 collective-permute-done.10.refs_3_.refs_6_
  25.2 0.0 collective-permute-done.8.refs_1_.refs_4_
  25.2 0.4 collective-permute-start.11
  25.7 0.1 collective-permute-start.12
  25.8 0.4 collective-permute-start.13
  26.2 22.6 %collective-permute-start.14 = (bf16[128,512]{1,0:T(8,128)(2,1)S(1)}, bf16[128,512]{1,0:T(8,128)(2,1)S(1)}, u32[]{:S(2)}, u32[]{:S(2)}) collective-permute-start(bf16[128,512]{1,0:T(8,128)(2,1)S(1)} %get-tuple-element.88.refs_4_), channel_id=1, source_target_pairs={{0,1},{1,0},{2,3},{3,17},{4,5},{5,4},{6,7},{7,6},{8,9},{9,8},{10,1... | collective-permute-start | bytes 393224 | tf_op jit(solution)/shard_map/ppermute | solution.py:536
  48.8 0.0 collective-permute-done.11.refs_0_
  48.8 0.0 collective-permute-done.12.refs_1_
  48.8 0.0 collective-permute-done.13.refs_1_
  48.8 2.9 %collective-permute-done.14.refs_2_ = bf16[128,512]{1,0:T(8,128)(2,1)S(1)} collective-permute-done((bf16[128,512]{1,0:T(8,128)(2,1)S(1)}, bf16[128,512]{1,0:T(8,128)(2,1)S(1)}, u32[]{:S(2)}, u32[]{:S(2)}) %collective-permute-start.14) | collective-permute-done | bytes 131104 | tf_op jit(solution)/shard_map/ppermute | solution.py:536
  51.7 4.2 %collective-permute-start.15 = (bf16[64,512]{1,0:T(8,128)(2,1)S(1)}, bf16[64,512]{1,0:T(8,128)(2,1)S(1)}, u32[]{:S(2)}, u32[]{:S(2)}) collective-permute-start(bf16[64,512]{1,0:T(8,128)(2,1)S(1)} %get-tuple-element.90), channel_id=1, source_target_pairs={{0,1},{1,0},{2,3},{3,2},{4,5},{5,4},{6,7},{7,6},{8,9},{9,8},{10,11... | collective-permute-start | bytes 196616 | tf_op jit(solution)/shard_map/ppermute | solution.py:555
  55.9 0.9 %collective-permute-done.15.refs_5_ = bf16[64,512]{1,0:T(8,128)(2,1)S(1)} collective-permute-done((bf16[64,512]{1,0:T(8,128)(2,1)S(1)}, bf16[64,512]{1,0:T(8,128)(2,1)S(1)}, u32[]{:S(2)}, u32[]{:S(2)}) %collective-permute-start.15) | collective-permute-done | bytes 65568 | tf_op jit(solution)/shard_map/ppermute | solution.py:555
  56.8 1.2 %decode.1 = bf16[227,128]{1,0:T(8,128)(2,1)} custom-call(s32[1]{0:T(128)} %bitcast.segment, s32[1]{0:T(128)} %bitcast.1.place, f32[128,512]{1,0:T(8,128)S(1)} %get-tuple-element.72.refs_0_, bf16[64,128]{1,0:T(8,128)(2,1)S(1)} %get-tuple-element.73.refs_1_, bf16[1024,512]{1,0:T(8,128)(2,1)S(1)} %copy-done, bf16[227,512]{1,0:T(8,128)(2,1)S(1)} %bitcast.15, ...), custom_call_target="tpu_custom_call" | custom-call | bytes 1748744 | tf_op jit(solution)/shard_map/decode/pallas_call | solution.py:472
  (28 shorter events, 0.1 us)
Async XLA Ops:
  0.0 1.8 %copy-start.7 = (s32[64,8]{0,1:T(8,128)S(1)}, s32[64,8]{0,1:T(8,128)}, u32[]{:S(2)}) copy-start(s32[64,8]{0,1:T(8,128)} %param.21) | copy-start | bytes 6148
  0.0 1.8 %copy-start.8 = (s32[4,64]{1,0:T(4,128)S(1)}, s32[4,64]{1,0:T(4,128)}, u32[]{:S(2)}) copy-start(s32[4,64]{1,0:T(4,128)} %param.22) | copy-start | bytes 3076
  0.0 1.8 %copy-start.9 = (s32[4,1]{0,1:T(1,128)S(1)}, s32[4,1]{0,1:T(1,128)}, u32[]{:S(2)}) copy-start(s32[4,1]{0,1:T(1,128)} %param.23) | copy-start | bytes 52
  0.0 1.8 %copy-start.10 = (s32[128]{0:T(128)S(1)}, s32[128]{0:T(128)}, u32[]{:S(2)}) copy-start(s32[128]{0:T(128)} %param.19) | copy-start | bytes 1540
  0.0 1.9 %copy-start.3 = (bf16[227,512]{1,0:T(8,128)(2,1)S(1)}, bf16[227,512]{1,0:T(8,128)(2,1)}, u32[]{:S(2)}) copy-start(bf16[227,512]{1,0:T(8,128)(2,1)} %refs_1_.3) | copy-start | bytes 697348
  0.0 5.5 %copy-start.4 = (bf16[1,512,512]{2,1,0:T(8,128)(2,1)S(1)}, bf16[1,512,512]{2,1,0:T(8,128)(2,1)}, u32[]{:S(2)}) copy-start(bf16[1,512,512]{2,1,0:T(8,128)(2,1)} %w_message) | copy-start | bytes 1572868
  0.0 25.1 %collective-permute-start.10 = (bf16[1,1024,512]{2,1,0:T(8,128)(2,1)}, bf16[1,1024,512]{2,1,0:T(8,128)(2,1)S(1)}, u32[]{:S(2)}, u32[]{:S(2)}) collective-permute-start(bf16[1,1024,512]{2,1,0:T(8,128)(2,1)} %w_update), channel_id=1, source_target_pairs={{0,1},{1,0},{2,3},{3,2},{4,5},{5,4},{6,7},{7,6},{8,9},{9,8},{10,11... | collective-permute-start | bytes 3145736 | tf_op jit(solution)/shard_map/ppermute | solution.py:536
  0.8 24.4 %collective-permute-start.8 = (bf16[1,512,1024]{2,1,0:T(8,128)(2,1)}, bf16[1,512,1024]{2,1,0:T(8,128)(2,1)S(1)}, u32[]{:S(2)}, u32[]{:S(2)}) collective-permute-start(bf16[1,512,1024]{2,1,0:T(8,128)(2,1)} %w_project), channel_id=1, source_target_pairs={{0,1},{1,0},{2,3},{3,2},{4,5},{5,4},{6,7},{7,6},{8,9},{9,8},{10,11... | collective-permute-start | bytes 3145736 | tf_op jit(solution)/shard_map/ppermute | solution.py:536
  2.6 6.2 %collective-permute-start = (bf16[80,512]{1,0:T(8,128)(2,1)S(1)}, bf16[80,512]{1,0:T(8,128)(2,1)S(1)}, u32[]{:S(2)}, u32[]{:S(2)}) collective-permute-start(bf16[80,512]{1,0:T(8,128)(2,1)S(1)} %get-tuple-element.59), channel_id=1, source_target_pairs={{0,2},{1,3},{2,0},{3,1},{4,6},{5,7},{6,4},{7,5},{8,9},{9,8},{10,11... | collective-permute-start | bytes 245768 | tf_op jit(solution)/shard_map/ppermute | solution.py:551
  2.7 6.2 %collective-permute-start.1 = (bf16[80,512]{1,0:T(8,128)(2,1)S(1)}, bf16[80,512]{1,0:T(8,128)(2,1)S(1)}, u32[]{:S(2)}, u32[]{:S(2)}) collective-permute-start(bf16[80,512]{1,0:T(8,128)(2,1)S(1)} %get-tuple-element.60), channel_id=1, source_target_pairs={{0,8},{1,9},{2,10},{3,11},{4,12},{5,13},{6,14},{7,15},{8,4},{9,5},... | collective-permute-start | bytes 245768 | tf_op jit(solution)/shard_map/ppermute | solution.py:551
  4.3 4.6 %collective-permute-start.2 = (bf16[80,512]{1,0:T(8,128)(2,1)S(1)}, bf16[80,512]{1,0:T(8,128)(2,1)S(1)}, u32[]{:S(2)}, u32[]{:S(2)}) collective-permute-start(bf16[80,512]{1,0:T(8,128)(2,1)S(1)} %get-tuple-element.61), channel_id=1, source_target_pairs={{0,16},{1,17},{2,18},{3,19},{4,20},{5,21},{6,22},{7,23},{8,9},{9,8... | collective-permute-start | bytes 245768 | tf_op jit(solution)/shard_map/ppermute | solution.py:551
  5.6 1.2 %copy-start.1 = (bf16[1,1024,512]{2,1,0:T(8,128)(2,1)S(1)}, bf16[1,1024,512]{2,1,0:T(8,128)(2,1)}, u32[]{:S(2)}) copy-start(bf16[1,1024,512]{2,1,0:T(8,128)(2,1)} %w_update) | copy-start | bytes 3145732
  6.8 1.2 %copy-start.2 = (bf16[1,512,1024]{2,1,0:T(8,128)(2,1)S(1)}, bf16[1,512,1024]{2,1,0:T(8,128)(2,1)}, u32[]{:S(2)}) copy-start(bf16[1,512,1024]{2,1,0:T(8,128)(2,1)} %w_project) | copy-start | bytes 3145732
  8.9 4.2 %collective-permute-start.3 = (bf16[320,512]{1,0:T(8,128)(2,1)S(1)}, bf16[320,512]{1,0:T(8,128)(2,1)S(1)}, u32[]{:S(2)}, u32[]{:S(2)}) collective-permute-start(bf16[320,512]{1,0:T(8,128)(2,1)S(1)} %join.1.refs_0_), channel_id=1, source_target_pairs={{0,1},{1,0},{2,3},{3,2},{4,5},{5,4},{6,7},{7,6},{8,9},{9,8},{10,11... | collective-permute-start | bytes 983048 | tf_op jit(solution)/shard_map/ppermute | solution.py:555
  13.2 6.6 %collective-permute-start.4 = (bf16[272,512]{1,0:T(8,128)(2,1)S(1)}, bf16[272,512]{1,0:T(8,128)(2,1)S(1)}, u32[]{:S(2)}, u32[]{:S(2)}) collective-permute-start(bf16[272,512]{1,0:T(8,128)(2,1)S(1)} %get-tuple-element.69), channel_id=1, source_target_pairs={{0,8},{1,0},{2,10},{3,2},{4,12},{5,4},{6,14},{7,6},{8,9},{9,1},{10... | collective-permute-start | bytes 835592 | tf_op jit(solution)/shard_map/ppermute | solution.py:536
  16.7 2.6 %copy-start = (bf16[1024,512]{1,0:T(8,128)(2,1)S(1)}, bf16[1024,512]{1,0:T(8,128)(2,1)}, u32[]{:S(2)}) copy-start(bf16[1024,512]{1,0:T(8,128)(2,1)} %refs_2_.3) | copy-start | bytes 3145732
  16.7 2.6 %copy-start.6 = (s32[128]{0:T(128)S(1)}, s32[128]{0:T(128)}, u32[]{:S(2)}) copy-start(s32[128]{0:T(128)} %param.20) | copy-start | bytes 1540
  16.7 5.2 %collective-permute-start.5 = (bf16[256,512]{1,0:T(8,128)(2,1)S(1)}, bf16[256,512]{1,0:T(8,128)(2,1)S(1)}, u32[]{:S(2)}, u32[]{:S(2)}) collective-permute-start(bf16[256,512]{1,0:T(8,128)(2,1)S(1)} %second.4), channel_id=1, source_target_pairs={{0,8},{1,0},{2,10},{3,2},{4,12},{5,4},{6,14},{7,6},{8,9},{9,1},{10... | collective-permute-start | bytes 786440 | tf_op jit(solution)/shard_map/ppermute | solution.py:536
  19.3 5.9 %collective-permute-start.9 = (bf16[1,512,512]{2,1,0:T(8,128)(2,1)S(1)}, bf16[1,512,512]{2,1,0:T(8,128)(2,1)S(1)}, u32[]{:S(2)}, u32[]{:S(2)}) collective-permute-start(bf16[1,512,512]{2,1,0:T(8,128)(2,1)S(1)} %copy-done.4), channel_id=1, source_target_pairs={{0,1},{1,0},{2,3},{3,2},{4,5},{5,4},{6,7},{7,6},{8,9},{9,8},{10,11... | collective-permute-start | bytes 1572872 | tf_op jit(solution)/shard_map/ppermute | solution.py:536
  22.0 2.8 %collective-permute-start.6 = (bf16[272,512]{1,0:T(8,128)(2,1)S(1)}, bf16[272,512]{1,0:T(8,128)(2,1)S(1)}, u32[]{:S(2)}, u32[]{:S(2)}) collective-permute-start(bf16[272,512]{1,0:T(8,128)(2,1)S(1)} %get-tuple-element.78), channel_id=1, source_target_pairs={{0,1},{1,0},{2,3},{3,2},{4,5},{5,4},{6,7},{7,6},{8,16},{9,8},{10,1... | collective-permute-start | bytes 835592 | tf_op jit(solution)/shard_map/ppermute | solution.py:536
  23.6 1.6 %collective-permute-start.7 = (bf16[256,512]{1,0:T(8,128)(2,1)S(1)}, bf16[256,512]{1,0:T(8,128)(2,1)S(1)}, u32[]{:S(2)}, u32[]{:S(2)}) collective-permute-start(bf16[256,512]{1,0:T(8,128)(2,1)S(1)} %second.5), channel_id=1, source_target_pairs={{0,1},{1,0},{2,3},{3,2},{4,5},{5,4},{6,7},{7,6},{8,16},{9,8},{10,1... | collective-permute-start | bytes 786440 | tf_op jit(solution)/shard_map/ppermute | solution.py:536
  25.2 23.5 %collective-permute-start.11 = (bf16[128,512]{1,0:T(8,128)(2,1)S(1)}, bf16[128,512]{1,0:T(8,128)(2,1)S(1)}, u32[]{:S(2)}, u32[]{:S(2)}) collective-permute-start(bf16[128,512]{1,0:T(8,128)(2,1)S(1)} %get-tuple-element.84), channel_id=1, source_target_pairs={{0,1},{1,0},{2,3},{3,2},{4,5},{5,21},{6,7},{7,6},{8,9},{9,8},{10,1... | collective-permute-start | bytes 393224 | tf_op jit(solution)/shard_map/ppermute | solution.py:536
  25.7 23.1 %collective-permute-start.12 = (bf16[128,512]{1,0:T(8,128)(2,1)S(1)}, bf16[128,512]{1,0:T(8,128)(2,1)S(1)}, u32[]{:S(2)}, u32[]{:S(2)}) collective-permute-start(bf16[128,512]{1,0:T(8,128)(2,1)S(1)} %get-tuple-element.85), channel_id=1, source_target_pairs={{0,1},{1,0},{2,3},{3,2},{4,5},{5,4},{6,7},{7,17},{8,9},{9,8},{10,1... | collective-permute-start | bytes 393224 | tf_op jit(solution)/shard_map/ppermute | solution.py:536
  25.8 23.0 %collective-permute-start.13 = (bf16[128,512]{1,0:T(8,128)(2,1)S(1)}, bf16[128,512]{1,0:T(8,128)(2,1)S(1)}, u32[]{:S(2)}, u32[]{:S(2)}) collective-permute-start(bf16[128,512]{1,0:T(8,128)(2,1)S(1)} %get-tuple-element.87.refs_3_), channel_id=1, source_target_pairs={{0,1},{1,17},{2,3},{3,2},{4,5},{5,4},{6,7},{7,6},{8,9},{9,19},{10,... | collective-permute-start | bytes 393224 | tf_op jit(solution)/shard_map/ppermute | solution.py:536
  26.2 25.5 %collective-permute-start.14 = (bf16[128,512]{1,0:T(8,128)(2,1)S(1)}, bf16[128,512]{1,0:T(8,128)(2,1)S(1)}, u32[]{:S(2)}, u32[]{:S(2)}) collective-permute-start(bf16[128,512]{1,0:T(8,128)(2,1)S(1)} %get-tuple-element.88.refs_4_), channel_id=1, source_target_pairs={{0,1},{1,0},{2,3},{3,17},{4,5},{5,4},{6,7},{7,6},{8,9},{9,8},{10,1... | collective-permute-start | bytes 393224 | tf_op jit(solution)/shard_map/ppermute | solution.py:536
  48.8 8.0 %copy-start.5 = (bf16[512,227]{0,1:T(8,128)(2,1)S(1)}, bf16[512,227]{0,1:T(8,128)(2,1)}, u32[]{:S(2)}) copy-start(bf16[512,227]{0,1:T(8,128)(2,1)} %param.18) | copy-start | bytes 697348
  51.7 5.1 %collective-permute-start.15 = (bf16[64,512]{1,0:T(8,128)(2,1)S(1)}, bf16[64,512]{1,0:T(8,128)(2,1)S(1)}, u32[]{:S(2)}, u32[]{:S(2)}) collective-permute-start(bf16[64,512]{1,0:T(8,128)(2,1)S(1)} %get-tuple-element.90), channel_id=1, source_target_pairs={{0,1},{1,0},{2,3},{3,2},{4,5},{5,4},{6,7},{7,6},{8,9},{9,8},{10,11... | collective-permute-start | bytes 196616 | tf_op jit(solution)/shard_map/ppermute | solution.py:555

commit v13 on v12

--- a/solution.py
+++ b/solution.py
@@ -235,7 +235,7 @@
 
 
 def index_kernel(parts, mesh_rows, where, *refs):
-    lanes, (columns_out, low, high), index_out = refs[:-4], refs[-4:-1], refs[-1]
+    lanes, (columns_out, low, *high), index_out = refs[:-5], refs[-5:-1], refs[-1]
     nodes = columns_out.shape[0]
     group = len(lanes)
     rows = lanes[0].shape[0] // (parts // group)
@@ -247,8 +247,10 @@
         for part in range(parts):
             lane, turn = lanes[part % group], jnp.bitwise_xor(chip, part // group)
             base = pl.multiple_of(turn * rows, 16)
-            half, spot = (low, part) if part < parts // 2 else (high, part - parts // 2)
-            half[spot * mesh_rows : (spot + 1) * mesh_rows, :] = lane[pl.ds(base, mesh_rows), :]
+            piece, spot = low, part * mesh_rows
+            if part >= parts // 2:
+                piece, spot = high[part * 4 // parts - 2], part % (parts // 4) * mesh_rows
+            piece[spot : spot + mesh_rows, :] = lane[pl.ds(base, mesh_rows), :]
             base = pl.multiple_of(turn * rows + mesh_rows, 16)
             coded = lane[pl.ds(base, rows - mesh_rows), :384].astype(jnp.float32).astype(jnp.int32)
             tables.append(coded[: coded.shape[0] // 2])
@@ -289,18 +291,19 @@
         copy.wait()
 
 
+def pack_kernel(group, at_segment, where, own, edges, pair):
+    @pl.when(owns(where, group, at_segment))
+    def _():
+        pair[0] = own[...]
+        pair[1] = edges[...]
+
+
 def blocks_of(weights):
     if len(weights) == 4:
-        receive, send, own, edges = weights
-        return receive[...], send[...], own[...], lambda gathered: matmul(gathered, edges[...])
-    w_project, w_message, w_update = weights
-    width = w_message.shape[1]
-
-    def finish(gathered):
-        aggregate = matmul(gathered, w_message[0]).astype(jnp.bfloat16)
-        return matmul(aggregate, w_update[0, width:, :])
-
-    return w_project[0, :, :width], w_project[0, :, width:], w_update[0, :width, :], finish
+        return [block[...] for block in weights]
+    w_project, pair = weights
+    width = pair.shape[1]
+    return w_project[0, :, :width], w_project[0, :, width:], pair[0], pair[1]
 
 
 def renew(fanout, columns, sender, own, weights):
@@ -310,7 +313,7 @@
     names = lax.broadcasted_iota(jnp.int32, (chunk, tile), 1).astype(jnp.float32).astype(jnp.bfloat16)
     one_half = jnp.full((chunk, tile), 0.5, jnp.bfloat16)
     none = jnp.zeros((chunk, tile), jnp.bfloat16)
-    w_receive, _, w_own, finish = blocks_of(weights)
+    w_receive, _, w_own, w_edges = blocks_of(weights)
     receiver = 0.5 * matmul(own, w_receive)
     update = matmul(own, w_own)
     total = jnp.zeros((chunk, width), jnp.float32)
@@ -322,7 +325,7 @@
         half = receiver + matmul(jnp.concatenate(hits, axis=1), sender)
         total = total + (half + half * jnp.tanh(half))
     gathered = (total * (1.0 / fanout)).astype(jnp.bfloat16)
-    update = silu_by_tanh(update + finish(gathered))
+    update = silu_by_tanh(update + matmul(gathered, w_edges))
     return (own.astype(jnp.float32) + rms_scale(update)).astype(jnp.bfloat16)
 
 
@@ -332,66 +335,81 @@
         piece[:rows, :] = value[place * rows : (place + 1) * rows]
 
 
-def sender_kernel(group, at_segment, fanout, rows, where, low, *refs):
-    weights, sender_low, columns = (refs[:-2], *refs[-2:]) if fanout else (refs[:-1], refs[-1], None)
+def sender_kernel(group, at_segment, fanout, rows, where, state, *refs):
+    weights, sender, columns = (refs[:-2], *refs[-2:]) if fanout else (refs[:-1], refs[-1], None)
 
     @pl.when(owns(where, group, at_segment))
     def _():
-        sender_low[...] = matmul(low[:rows, :], blocks_of(weights)[1]).astype(jnp.bfloat16)
+        sender[...] = matmul(state[:rows, :], blocks_of(weights)[1]).astype(jnp.bfloat16)
         if fanout:
-            digits = low[rows:, :].astype(jnp.float32)
+            digits = state[rows:, :].astype(jnp.float32)
             columns[...] = columns_of(digits[:fanout] * DIGIT + digits[fanout:])
 
 
-def half_of(where, group, chips, far, low, high, own):
-    half = high.shape[0]
+def take(parts, own):
+    start = 0
+    for part in parts:
+        rows = min(part.shape[0], own.shape[0] - start)
+        own[start : start + rows, :] = part[:rows, :]
+        start += rows
+
+
+def choose(where, group, chips, far, state, own):
+    half = own.shape[0]
     chip, _ = place_of(where, group)
     upper = (chip < chips // 2) if far else (chip >= chips // 2)
 
     @pl.when(upper)
     def _():
-        own[...] = high[...]
+        take(state[1:], own)
 
     @pl.when(jnp.logical_not(upper))
     def _():
-        own[...] = low[...]
+        take(state[:1], own)
 
     return pl.multiple_of(jnp.where(upper, half, 0), half)
 
 
-def first_kernel(
-    group, at_segment, chips, fanout, given, where, columns, sender_low, low, high, *refs
-):
-    weights, sender, pieces, own = refs[:given], refs[given], refs[given + 1 : -1], refs[-1]
-    half = high.shape[0]
+def first_kernel(group, at_segment, chips, fanout, counts, where, columns, *refs):
+    parts, given = counts
+    senders, refs = refs[: parts - 1], refs[parts - 1 :]
+    state, weights, refs = refs[:parts], refs[parts : parts + given], refs[parts + given :]
+    sender, pieces, own = refs[0], refs[1:-1], refs[-1]
+    rows = own.shape[0]
 
     @pl.when(owns(where, group, at_segment))
     def _():
-        sender[:half, :] = sender_low[...]
-        sender[half:, :] = matmul(high[...], blocks_of(weights)[1]).astype(jnp.bfloat16)
-        start, state = 0, low[:half, :]
+        start = 0
+        for part in senders:
+            sender[start : start + part.shape[0], :] = part[...]
+            start += part.shape[0]
+        sender[start:, :] = matmul(state[-1][...], blocks_of(weights)[1]).astype(jnp.bfloat16)
         if chips:
-            start = half_of(where, group, chips, True, low, high, own)
-            state = own[...]
-        rows = columns[pl.ds(start, half), :]
-        write_pieces(pieces, renew(fanout, rows, sender[...], state, weights))
-        if pieces[0].shape[0] > half:
-            pieces[0][half:, :] = low[half:, :]
-
-
-def second_kernel(
-    group, at_segment, chips, fanout, given, where, columns, sender, low, high, *refs
-):
-    weights, pieces, own = refs[:given], refs[given:-1], refs[-1]
-    half = high.shape[0]
+            start = choose(where, group, chips, True, state, own)
+        else:
+            start = 0
+            take(state[:1], own)
+        lanes = columns[pl.ds(start, rows), :]
+        write_pieces(pieces, renew(fanout, lanes, sender[...], own[...], weights))
+        if pieces[0].shape[0] > rows:
+            pieces[0][rows:, :] = state[0][rows:, :]
+
+
+def next_kernel(group, at_segment, chips, fanout, counts, start, where, columns, sender, *refs):
+    parts, given = counts
+    state, weights, refs = refs[:parts], refs[parts : parts + given], refs[parts + given :]
+    pieces, own = refs[:-1], refs[-1]
+    rows = own.shape[0]
 
     @pl.when(owns(where, group, at_segment))
     def _():
-        start, state = half, high
         if chips:
-            start, state = half_of(where, group, chips, False, low, high, own), own
-        rows = columns[pl.ds(start, half), :]
-        write_pieces(pieces, renew(fanout, rows, sender[...], state[...], weights))
+            first = choose(where, group, chips, False, state, own)
+        else:
+            first = start
+            take(state, own)
+        lanes = columns[pl.ds(first, rows), :]
+        write_pieces(pieces, renew(fanout, lanes, sender[...], own[...], weights))
 
 
 def arrival(where, group, chips, last):
@@ -557,13 +575,14 @@
     def owner(m, at_segment):
         return device(at_segment, m * group)
 
-    own_segment, own_place, *weights = lax.optimization_barrier(
-        (segment.reshape(1), place.reshape(1), w_project, w_message, w_update)
+    own_segment, own_place, w_project = lax.optimization_barrier(
+        (segment.reshape(1), place.reshape(1), w_project)
     )
     where = (own_segment, own_place)
+    weights = [w_project, w_message, w_update]
     last = segments - 2
     pairs = [(owner(m, last + 1), owner(m, last)) for m in range(samples)]
-    came_weights = [send(weight, pairs) for weight in weights]
+    came = [send(w_project, pairs)]
     snapshots = jnp.transpose(grid_state, (0, 2, 1))
     lists = send_rows.shape[0]
 
@@ -605,56 +624,79 @@
         "v" * samples,
     )
     lanes = [joined] + [change_lane(joined, -steps) for steps in range(1, group)]
-    half = nodes // 2
-    share = group * mesh_rows
-    columns, low, high = call(
+    half, share = nodes // 2, group * mesh_rows
+    tall, short = [jax.ShapeDtypeStruct((rows, width), bf16) for rows in (half + 2 * fanout, share)]
+    columns, *state = call(
         functools.partial(index_kernel, parts, mesh_rows),
         "index",
-        [
-            jax.ShapeDtypeStruct((nodes, 128), bf16),
-            jax.ShapeDtypeStruct((half + 2 * fanout, width), bf16),
-            jax.ShapeDtypeStruct((half, width), bf16),
-        ],
+        [jax.ShapeDtypeStruct((nodes, 128), bf16), tall, short, short],
         [where] + lanes,
         "w" + "v" * group,
         [pltpu.VMEM((fanout, nodes), jnp.int32)],
     )
-    state_shape = jax.ShapeDtypeStruct((half, width), bf16)
+    columns, *held[2:] = lax.optimization_barrier((columns, *held[2:]))
+    (pair,) = call(
+        functools.partial(pack_kernel, group, last + 1),
+        "pack",
+        [jax.ShapeDtypeStruct((2, width, width), bf16)],
+        [where] + held[2:],
+        "wvv",
+    )
+    came.append(send(pair, pairs))
     for layer in range(segments):
         at_segment, ends = min(layer, last), layer > last
-        used = list(held) if layer <= last else came_weights
-        role = (group, at_segment, samples if ends else 0, fanout, len(used))
-        pieces = [jax.ShapeDtypeStruct((share, width), bf16)] * (half // share) if ends else [state_shape]
-        scratch = [pltpu.VMEM((half, width), bf16)]
+        used = list(held) if layer <= last else came
+        role = (group, at_segment, samples if ends else 0, fanout, (len(state), len(used)))
         arrives = 0 < layer <= last
-        sender_low, *found = call(
-            functools.partial(sender_kernel, group, at_segment, fanout if arrives else 0, half),
-            "sender",
-            [state_shape] + [jax.ShapeDtypeStruct((nodes, 128), bf16)] * arrives,
-            [where, low] + used,
-            "wv" + "v" * len(used),
-        )
-        columns = found[0] if arrives else columns
-        tall = jax.ShapeDtypeStruct((half + 2 * fanout, width), bf16)
-        sender, *first = call(
-            functools.partial(first_kernel, *role),
-            "first",
-            [jax.ShapeDtypeStruct((nodes, width), bf16)] + ([tall] if layer < last else pieces),
-            [where, columns, sender_low, low, high] + used,
-            "wvvvv" + "v" * len(used),
-            scratch,
-        )
+        senders = []
+        for place_in_state, part in enumerate(state[:-1]):
+            if senders:
+                part, senders[-1] = lax.optimization_barrier((part, senders[-1]))
+            rows = min(part.shape[0], half)
+            coded = part.shape[0] > rows and arrives
+            found = call(
+                functools.partial(sender_kernel, group, at_segment, fanout if coded else 0, rows),
+                "sender",
+                [jax.ShapeDtypeStruct((rows, width), bf16)]
+                + [jax.ShapeDtypeStruct((nodes, 128), bf16)] * coded,
+                [where, part] + used,
+                "wv" + "v" * len(used),
+            )
+            senders.append(found[0])
+            columns = found[1] if coded else columns
+        if layer < last:
+            steps = [[tall], [short], [short]]
+        elif layer == last:
+            steps = [[jax.ShapeDtypeStruct((half, width), bf16)], [short, short]]
+        else:
+            steps = [[short, short], [short, short]]
         pairs = [(owner(m, layer), owner(m, layer + 1)) for m in range(samples)]
-        new_low = send(first[0], pairs) if layer < last else first[0]
-        second = call(
-            functools.partial(second_kernel, *role),
-            "second",
-            pieces,
-            [where, columns, sender, low, high] + used,
-            "wvvvv" + "v" * len(used),
-            scratch,
-        )
-        low, high = new_low, send(second[0], pairs) if layer < last else second[0]
+        renewed, start = [], 0
+        for step, pieces in enumerate(steps):
+            rows = min(sum(piece.shape[0] for piece in pieces), half)
+            scratch = [pltpu.VMEM((rows, width), bf16)]
+            if step == 0:
+                sender, *made = call(
+                    functools.partial(first_kernel, *role),
+                    "first",
+                    [jax.ShapeDtypeStruct((nodes, width), bf16)] + pieces,
+                    [where, columns] + senders + state + used,
+                    "w" + "v" * (2 * len(state) + len(used)),
+                    scratch,
+                )
+            else:
+                parts_used = state if ends else state[1:] if layer == last else state[step : step + 1]
+                made = call(
+                    functools.partial(next_kernel, *role[:-1], (len(parts_used), len(used)), start),
+                    "next",
+                    pieces,
+                    [where, columns, sender] + parts_used + used,
+                    "w" + "v" * (2 + len(parts_used) + len(used)),
+                    scratch,
+                )
+            renewed += [send(piece, pairs) for piece in made] if layer < last else list(made)
+            start += rows
+        state = renewed
         if layer == 0:
             ready, table = call(
                 prepare_kernel,
@@ -666,10 +708,10 @@
                 [where, snapshots, w_embed, w_decode, mesh_grid.reshape(1, grid_rows)],
                 "wvvvv",
                     )
-            low, ready, table = lax.optimization_barrier((low, ready, table))
+            state[0], ready, table = lax.optimization_barrier((state[0], ready, table))
     each = samples // 2
     arrived = []
-    for far, blocks in ((1, first), (0, second)):
+    for far, blocks in ((1, state[:each]), (0, state[each:])):
         for turn, block in enumerate(blocks):
             pairs = [
                 (owner(m, last), device(m, ((m // each ^ far) * each + turn) * group)) for m in range(samples)
@@ -686,7 +728,7 @@
         functools.partial(near_kernel, group, samples, last),
         "near",
         [jax.ShapeDtypeStruct((mesh_rows, width), bf16)] * group,
-        [where, crossed] + arrived[each:] + list(second),
+        [where, crossed] + arrived[each:] + state[each:],
         "w" + "v" * (1 + 2 * each),
     )
     handed = [parts_of_block[0]]

time: 58.2 us -> 57.4 us (0.986)
  starting transfers between devices: 42.3 us -> 38.9 us
  waiting for transfers between devices: 8.94 us -> 11.4 us
    ppermute x3, waiting for transfers between devices: 0.15 us -> 3.05 us  [to_chip(): return lax.ppermute(value, ('segment', 'dom'), pairs)]
    ppermute x2, starting transfers between devices: 7.18 us -> 5 us  [change_lane(): return lax.ppermute(value, 'dom', pairs)]
    ppermute x3, starting transfers between devices: 2.95 us -> 2.04 us  [to_chip(): return lax.ppermute(value, ('segment', 'dom'), pairs)]
    ppermute x11 -> x12, waiting for transfers between devices: 6.63 us -> 6.23 us  [send(): lax.ppermute(value, ('segment', 'dom'), every_device(pairs, segments * pa...]
    ppermute x11 -> x12, starting transfers between devices: 32.1 us -> 31.9 us  [send(): lax.ppermute(value, ('segment', 'dom'), every_device(pairs, segments * pa...]
    unnamed x23 -> x25, local copies, waits for them, and re-layouts: 3.46 us -> 3.53 us
    pallas_call x20 -> x27, Pallas kernels: 3.16 us -> 3.17 us  [call(): pl.pallas_call(located if places[0] == 'w' else kernel, out_shape=shapes,...]
  transfers between devices with their start and end apart: 16 -> 17, of which waited for: 7 -> 10; matrix products, arithmetic and copies ran while one was open for 2% -> 0% of each run, Pallas kernels for 3% -> 2%
where the time goes in v13:
time: 57.4 us; the launch traced here: 57.2 us
  starting transfers between devices  38.9 us (68%)
  waiting for transfers between devices  11.4 us (20%)
  local copies, waits for them, and re-layouts  3.53 us (6%)
  Pallas kernels  3.17 us (6%)
    ppermute x12, starting transfers between devices, send(): lax.ppermute(value, ('segment', 'dom'), every_device(pairs, segments * pa...  31.9 us
    ppermute x12, waiting for transfers between devices, send(): lax.ppermute(value, ('segment', 'dom'), every_device(pairs, segments * pa...  6.23 us
    ppermute x2, starting transfers between devices, change_lane(): return lax.ppermute(value, 'dom', pairs)  5 us
    unnamed x25, local copies, waits for them, and re-layouts  3.53 us
    pallas_call x27, Pallas kernels, call(): pl.pallas_call(located if places[0] == 'w' else kernel, out_shape=shapes,...  3.17 us
    ppermute x3, waiting for transfers between devices, to_chip(): return lax.ppermute(value, ('segment', 'dom'), pairs)  3.05 us
    ppermute x2, waiting for transfers between devices, change_lane(): return lax.ppermute(value, 'dom', pairs)  2.08 us
    ppermute x3, starting transfers between devices, to_chip(): return lax.ppermute(value, ('segment', 'dom'), pairs)  2.04 us
  transfers between devices with their start and end apart: 17, of which 10 were waited for; matrix products, arithmetic and copies ran while one was open for 0% of the time, Pallas kernels for 2%

profile of v13, /device:TPU:9, one launch (start us, length us, event | category | flops | bytes accessed | tf_op | source)
XLA Modules:
  0.0 57.2 jit_solution(12238185649857155013)
XLA Ops:
  0.0 0.0 copy-start.8
  0.0 0.0 copy-start.4
  0.0 0.0 copy-start.5
  0.0 1.0 %copy.15 = bf16[4,128,227]{1,2,0:T(8,128)(2,1)S(1)} copy(bf16[4,128,227]{1,0,2:T(4,128)(2,1)} %param.12) | data formatting | bytes 464896 | tf_op args[0]
  1.1 0.0 copy-done.9
  1.1 0.0 copy-done.4
  1.2 0.7 %encode.1 = (bf16[80,512]{1,0:T(8,128)(2,1)S(1)}, bf16[80,512]{1,0:T(8,128)(2,1)S(1)}, bf16[80,512]{1,0:T(8,128)(2,1)S(1)}, bf16[80,512]{1,0:T(8,128)(2,1)S(1)}) custom-call(s32[1]{0:T(128)} %bitcast.segment, s32[1]{0:T(128)} %bitcast.1.place, bf16[4,227,128]{2,1,0:T(8,128)(2,1)S(1)} %bitcast.13, bf16[227,512]{1,0:T(8,128)(2,1)S(1)} %copy-done.4, ...), custom_call_target="tpu_custom_call" | custom-call | bytes 799752 | tf_op jit(solution)/shard_map/encode/pallas_call | solution.py:490
  1.9 0.1 collective-permute-start
  2.0 1.9 %collective-permute-start.1 = (bf16[80,512]{1,0:T(8,128)(2,1)S(1)}, bf16[80,512]{1,0:T(8,128)(2,1)S(1)}, u32[]{:S(2)}, u32[]{:S(2)}) collective-permute-start(bf16[80,512]{1,0:T(8,128)(2,1)S(1)} %get-tuple-element.70), channel_id=1, source_target_pairs={{0,8},{1,9},{2,10},{3,11},{4,12},{5,13},{6,14},{7,15},{8,4},{9,5},... | collective-permute-start | bytes 245768 | tf_op jit(solution)/shard_map/ppermute | solution.py:569
  3.8 0.1 collective-permute-start.2
  3.9 1.2 %copy-done.1 = bf16[1,1024,512]{2,1,0:T(8,128)(2,1)S(1)} copy-done((bf16[1,1024,512]{2,1,0:T(8,128)(2,1)S(1)}, bf16[1,1024,512]{2,1,0:T(8,128)(2,1)}, u32[]{:S(2)}) %copy-start.1) | copy-done | bytes 1048600
  5.1 1.2 %copy-done.2 = bf16[1,512,1024]{2,1,0:T(8,128)(2,1)S(1)} copy-done((bf16[1,512,1024]{2,1,0:T(8,128)(2,1)S(1)}, bf16[1,512,1024]{2,1,0:T(8,128)(2,1)}, u32[]{:S(2)}) %copy-start.2) | copy-done | bytes 1048600
  6.4 0.7 %hold.1 = (bf16[512,512]{1,0:T(8,128)(2,1)S(1)}, bf16[512,512]{1,0:T(8,128)(2,1)S(1)}, bf16[512,512]{1,0:T(8,128)(2,1)S(1)}, bf16[512,512]{1,0:T(8,128)(2,1)S(1)}) custom-call(bf16[1,512,1024]{2,1,0:T(8,128)(2,1)S(1)} %copy-done.2, bf16[1,512,512]{2,1,0:T(8,128)(2,1)S(1)} %copy-done.5, bf16[1,1024,512]{2,1,0:T(8,128)(2,1)S(1)} %copy-done.1), custom_call_target="tpu_custom_call" | custom-call | bytes 4718592 | tf_op jit(solution)/shard_map/hold/pallas_call | solution.py:490
  7.1 0.0 collective-permute-done.refs_1_
  7.1 1.3 %collective-permute-done.1.refs_2_ = bf16[80,512]{1,0:T(8,128)(2,1)S(1)} collective-permute-done((bf16[80,512]{1,0:T(8,128)(2,1)S(1)}, bf16[80,512]{1,0:T(8,128)(2,1)S(1)}, u32[]{:S(2)}, u32[]{:S(2)}) %collective-permute-start.1) | collective-permute-done | bytes 81952 | tf_op jit(solution)/shard_map/ppermute | solution.py:569
  8.4 1.8 %collective-permute-done.2.refs_3_ = bf16[80,512]{1,0:T(8,128)(2,1)S(1)} collective-permute-done((bf16[80,512]{1,0:T(8,128)(2,1)S(1)}, bf16[80,512]{1,0:T(8,128)(2,1)S(1)}, u32[]{:S(2)}, u32[]{:S(2)}) %collective-permute-start.2) | collective-permute-done | bytes 81952 | tf_op jit(solution)/shard_map/ppermute | solution.py:569
  10.2 1.2 %collective-permute-start.3 = (bf16[320,512]{1,0:T(8,128)(2,1)S(1)}, bf16[320,512]{1,0:T(8,128)(2,1)S(1)}, u32[]{:S(2)}, u32[]{:S(2)}) collective-permute-start(bf16[320,512]{1,0:T(8,128)(2,1)S(1)} %join.1.refs_0_), channel_id=1, source_target_pairs={{0,1},{1,0},{2,3},{3,2},{4,5},{5,4},{6,7},{7,6},{8,9},{9,8},{10,11... | collective-permute-start | bytes 983048 | tf_op jit(solution)/shard_map/ppermute | solution.py:573
  11.4 0.0 copy-done.3
  11.4 0.1 collective-permute-start.10
  11.5 1.2 %collective-permute-done.3.refs_1_ = bf16[320,512]{1,0:T(8,128)(2,1)S(1)} collective-permute-done((bf16[320,512]{1,0:T(8,128)(2,1)S(1)}, bf16[320,512]{1,0:T(8,128)(2,1)S(1)}, u32[]{:S(2)}, u32[]{:S(2)}) %collective-permute-start.3) | collective-permute-done | bytes 327712 | tf_op jit(solution)/shard_map/ppermute | solution.py:573
  12.7 0.8 %collective-permute-start.11 = (bf16[2,512,512]{2,1,0:T(8,128)(2,1)S(1)}, bf16[2,512,512]{2,1,0:T(8,128)(2,1)S(1)}, u32[]{:S(2)}, u32[]{:S(2)}) collective-permute-start(bf16[2,512,512]{2,1,0:T(8,128)(2,1)S(1)} %pack.1), channel_id=1, source_target_pairs={{0,1},{1,0},{2,3},{3,2},{4,5},{5,4},{6,7},{7,6},{8,9},{9,8},{10,11... | collective-permute-start | bytes 3145736 | tf_op jit(solution)/shard_map/ppermute | solution.py:554
  13.5 3.1 %collective-permute-start.4 = (bf16[272,512]{1,0:T(8,128)(2,1)S(1)}, bf16[272,512]{1,0:T(8,128)(2,1)S(1)}, u32[]{:S(2)}, u32[]{:S(2)}) collective-permute-start(bf16[272,512]{1,0:T(8,128)(2,1)S(1)} %get-tuple-element.85), channel_id=1, source_target_pairs={{0,8},{1,0},{2,10},{3,2},{4,12},{5,4},{6,14},{7,6},{8,9},{9,1},{10... | collective-permute-start | bytes 835592 | tf_op jit(solution)/shard_map/ppermute | solution.py:554
  16.5 1.5 %collective-permute-start.5 = (bf16[128,512]{1,0:T(8,128)(2,1)S(1)}, bf16[128,512]{1,0:T(8,128)(2,1)S(1)}, u32[]{:S(2)}, u32[]{:S(2)}) collective-permute-start(bf16[128,512]{1,0:T(8,128)(2,1)S(1)} %next.6), channel_id=1, source_target_pairs={{0,8},{1,0},{2,10},{3,2},{4,12},{5,4},{6,14},{7,6},{8,9},{9,1},{10... | collective-permute-start | bytes 393224 | tf_op jit(solution)/shard_map/ppermute | solution.py:554
  18.0 1.5 %collective-permute-start.6 = (bf16[128,512]{1,0:T(8,128)(2,1)S(1)}, bf16[128,512]{1,0:T(8,128)(2,1)S(1)}, u32[]{:S(2)}, u32[]{:S(2)}) collective-permute-start(bf16[128,512]{1,0:T(8,128)(2,1)S(1)} %next.7), channel_id=1, source_target_pairs={{0,8},{1,0},{2,10},{3,2},{4,12},{5,4},{6,14},{7,6},{8,9},{9,1},{10... | collective-permute-start | bytes 393224 | tf_op jit(solution)/shard_map/ppermute | solution.py:554
  19.5 0.0 copy-done.7
  19.5 0.4 prepare.1
  19.9 0.0 collective-permute-done.4.refs_0_.refs_3_
  20.0 0.4 collective-permute-done.5.refs_0_.refs_4_.refs_2_
  20.4 1.5 %collective-permute-done.6.refs_5_.refs_2_ = bf16[128,512]{1,0:T(8,128)(2,1)S(1)} collective-permute-done((bf16[128,512]{1,0:T(8,128)(2,1)S(1)}, bf16[128,512]{1,0:T(8,128)(2,1)S(1)}, u32[]{:S(2)}, u32[]{:S(2)}) %collective-permute-start.6) | collective-permute-done | bytes 131104 | tf_op jit(solution)/shard_map/ppermute | solution.py:554
  21.8 1.6 %collective-permute-start.7 = (bf16[272,512]{1,0:T(8,128)(2,1)S(1)}, bf16[272,512]{1,0:T(8,128)(2,1)S(1)}, u32[]{:S(2)}, u32[]{:S(2)}) collective-permute-start(bf16[272,512]{1,0:T(8,128)(2,1)S(1)} %get-tuple-element.96), channel_id=1, source_target_pairs={{0,1},{1,0},{2,3},{3,2},{4,5},{5,4},{6,7},{7,6},{8,16},{9,8},{10,1... | collective-permute-start | bytes 835592 | tf_op jit(solution)/shard_map/ppermute | solution.py:554
  23.4 0.0 collective-permute-start.8
  23.4 0.5 collective-permute-start.9
  23.9 0.7 %collective-permute-done.7.refs_0_.refs_3_ = bf16[272,512]{1,0:T(8,128)(2,1)S(1)} collective-permute-done((bf16[272,512]{1,0:T(8,128)(2,1)S(1)}, bf16[272,512]{1,0:T(8,128)(2,1)S(1)}, u32[]{:S(2)}, u32[]{:S(2)}) %collective-permute-start.7) | collective-permute-done | bytes 278560 | tf_op jit(solution)/shard_map/ppermute | solution.py:554
  24.6 0.2 collective-permute-done.8.refs_0_.refs_4_.refs_2_
  24.8 0.2 collective-permute-done.9.refs_5_.refs_3_
  25.0 0.0 collective-permute-done.10.refs_1_.refs_6_.refs_5_
  25.0 0.0 collective-permute-done.11.refs_2_.refs_7_.refs_6_
  25.0 0.4 collective-permute-start.12
  25.5 0.1 collective-permute-start.13
  25.6 0.4 collective-permute-start.14
  26.0 22.0 %collective-permute-start.15 = (bf16[128,512]{1,0:T(8,128)(2,1)S(1)}, bf16[128,512]{1,0:T(8,128)(2,1)S(1)}, u32[]{:S(2)}, u32[]{:S(2)}) collective-permute-start(bf16[128,512]{1,0:T(8,128)(2,1)S(1)} %get-tuple-element.112.refs_4_), channel_id=1, source_target_pairs={{0,1},{1,0},{2,3},{3,17},{4,5},{5,4},{6,7},{7,6},{8,9},{9,8},{10,1... | collective-permute-start | bytes 393224 | tf_op jit(solution)/shard_map/ppermute | solution.py:554
  48.0 0.0 collective-permute-done.12.refs_0_
  48.0 0.0 collective-permute-done.13.refs_1_
  48.0 0.0 collective-permute-done.14.refs_1_
  48.0 3.3 %collective-permute-done.15.refs_2_ = bf16[128,512]{1,0:T(8,128)(2,1)S(1)} collective-permute-done((bf16[128,512]{1,0:T(8,128)(2,1)S(1)}, bf16[128,512]{1,0:T(8,128)(2,1)S(1)}, u32[]{:S(2)}, u32[]{:S(2)}) %collective-permute-start.15) | collective-permute-done | bytes 131104 | tf_op jit(solution)/shard_map/ppermute | solution.py:554
  51.3 3.8 %collective-permute-start.16 = (bf16[64,512]{1,0:T(8,128)(2,1)S(1)}, bf16[64,512]{1,0:T(8,128)(2,1)S(1)}, u32[]{:S(2)}, u32[]{:S(2)}) collective-permute-start(bf16[64,512]{1,0:T(8,128)(2,1)S(1)} %get-tuple-element.114), channel_id=1, source_target_pairs={{0,1},{1,0},{2,3},{3,2},{4,5},{5,4},{6,7},{7,6},{8,9},{9,8},{10,11... | collective-permute-start | bytes 196616 | tf_op jit(solution)/shard_map/ppermute | solution.py:573
  55.1 0.9 %collective-permute-done.16.refs_5_ = bf16[64,512]{1,0:T(8,128)(2,1)S(1)} collective-permute-done((bf16[64,512]{1,0:T(8,128)(2,1)S(1)}, bf16[64,512]{1,0:T(8,128)(2,1)S(1)}, u32[]{:S(2)}, u32[]{:S(2)}) %collective-permute-start.16) | collective-permute-done | bytes 65568 | tf_op jit(solution)/shard_map/ppermute | solution.py:573
  56.0 1.2 %decode.1 = bf16[227,128]{1,0:T(8,128)(2,1)} custom-call(s32[1]{0:T(128)} %bitcast.segment, s32[1]{0:T(128)} %bitcast.1.place, f32[128,512]{1,0:T(8,128)S(1)} %get-tuple-element.88.refs_0_, bf16[64,128]{1,0:T(8,128)(2,1)S(1)} %get-tuple-element.89.refs_1_, bf16[1024,512]{1,0:T(8,128)(2,1)S(1)} %copy-done, bf16[227,512]{1,0:T(8,128)(2,1)S(1)} %bitcast.15, ...), custom_call_target="tpu_custom_call" | custom-call | bytes 1748744 | tf_op jit(solution)/shard_map/decode/pallas_call | solution.py:490
  (39 shorter events, 0.1 us)
Async XLA Ops:
  0.0 1.1 %copy-start.9 = (s32[4,64]{1,0:T(4,128)S(1)}, s32[4,64]{1,0:T(4,128)}, u32[]{:S(2)}) copy-start(s32[4,64]{1,0:T(4,128)} %param.22) | copy-start | bytes 3076
  0.0 1.1 %copy-start.10 = (s32[4,1]{0,1:T(1,128)S(1)}, s32[4,1]{0,1:T(1,128)}, u32[]{:S(2)}) copy-start(s32[4,1]{0,1:T(1,128)} %param.23) | copy-start | bytes 52
  0.0 1.1 %copy-start.11 = (s32[128]{0:T(128)S(1)}, s32[128]{0:T(128)}, u32[]{:S(2)}) copy-start(s32[128]{0:T(128)} %param.19) | copy-start | bytes 1540
  0.0 1.1 %copy-start.8 = (s32[64,8]{0,1:T(8,128)S(1)}, s32[64,8]{0,1:T(8,128)}, u32[]{:S(2)}) copy-start(s32[64,8]{0,1:T(8,128)} %param.21) | copy-start | bytes 6148
  0.0 1.1 %copy-start.4 = (bf16[227,512]{1,0:T(8,128)(2,1)S(1)}, bf16[227,512]{1,0:T(8,128)(2,1)}, u32[]{:S(2)}) copy-start(bf16[227,512]{1,0:T(8,128)(2,1)} %refs_1_.3) | copy-start | bytes 697348
  0.0 3.9 %copy-start.5 = (bf16[1,512,512]{2,1,0:T(8,128)(2,1)S(1)}, bf16[1,512,512]{2,1,0:T(8,128)(2,1)}, u32[]{:S(2)}) copy-start(bf16[1,512,512]{2,1,0:T(8,128)(2,1)} %w_message.1) | copy-start | bytes 1572868
  1.9 5.2 %collective-permute-start = (bf16[80,512]{1,0:T(8,128)(2,1)S(1)}, bf16[80,512]{1,0:T(8,128)(2,1)S(1)}, u32[]{:S(2)}, u32[]{:S(2)}) collective-permute-start(bf16[80,512]{1,0:T(8,128)(2,1)S(1)} %get-tuple-element.69), channel_id=1, source_target_pairs={{0,2},{1,3},{2,0},{3,1},{4,6},{5,7},{6,4},{7,5},{8,9},{9,8},{10,11... | collective-permute-start | bytes 245768 | tf_op jit(solution)/shard_map/ppermute | solution.py:569
  2.0 6.5 %collective-permute-start.1 = (bf16[80,512]{1,0:T(8,128)(2,1)S(1)}, bf16[80,512]{1,0:T(8,128)(2,1)S(1)}, u32[]{:S(2)}, u32[]{:S(2)}) collective-permute-start(bf16[80,512]{1,0:T(8,128)(2,1)S(1)} %get-tuple-element.70), channel_id=1, source_target_pairs={{0,8},{1,9},{2,10},{3,11},{4,12},{5,13},{6,14},{7,15},{8,4},{9,5},... | collective-permute-start | bytes 245768 | tf_op jit(solution)/shard_map/ppermute | solution.py:569
  3.8 6.4 %collective-permute-start.2 = (bf16[80,512]{1,0:T(8,128)(2,1)S(1)}, bf16[80,512]{1,0:T(8,128)(2,1)S(1)}, u32[]{:S(2)}, u32[]{:S(2)}) collective-permute-start(bf16[80,512]{1,0:T(8,128)(2,1)S(1)} %get-tuple-element.71), channel_id=1, source_target_pairs={{0,16},{1,17},{2,18},{3,19},{4,20},{5,21},{6,22},{7,23},{8,9},{9,8... | collective-permute-start | bytes 245768 | tf_op jit(solution)/shard_map/ppermute | solution.py:569
  3.9 1.2 %copy-start.1 = (bf16[1,1024,512]{2,1,0:T(8,128)(2,1)S(1)}, bf16[1,1024,512]{2,1,0:T(8,128)(2,1)}, u32[]{:S(2)}) copy-start(bf16[1,1024,512]{2,1,0:T(8,128)(2,1)} %w_update.1) | copy-start | bytes 3145732
  5.1 1.2 %copy-start.2 = (bf16[1,512,1024]{2,1,0:T(8,128)(2,1)S(1)}, bf16[1,512,1024]{2,1,0:T(8,128)(2,1)}, u32[]{:S(2)}) copy-start(bf16[1,512,1024]{2,1,0:T(8,128)(2,1)} %w_project) | copy-start | bytes 3145732
  6.4 5.1 %copy-start.3 = (bf16[1,512,1024]{2,1,0:T(8,128)(2,1)S(1)}, bf16[1,512,1024]{2,1,0:T(8,128)(2,1)}, u32[]{:S(2)}) copy-start(bf16[1,512,1024]{2,1,0:T(8,128)(2,1)} %w_project) | copy-start | bytes 3145732
  10.2 2.5 %collective-permute-start.3 = (bf16[320,512]{1,0:T(8,128)(2,1)S(1)}, bf16[320,512]{1,0:T(8,128)(2,1)S(1)}, u32[]{:S(2)}, u32[]{:S(2)}) collective-permute-start(bf16[320,512]{1,0:T(8,128)(2,1)S(1)} %join.1.refs_0_), channel_id=1, source_target_pairs={{0,1},{1,0},{2,3},{3,2},{4,5},{5,4},{6,7},{7,6},{8,9},{9,8},{10,11... | collective-permute-start | bytes 983048 | tf_op jit(solution)/shard_map/ppermute | solution.py:573
  11.4 13.6 %collective-permute-start.10 = (bf16[1,512,1024]{2,1,0:T(8,128)(2,1)S(1)}, bf16[1,512,1024]{2,1,0:T(8,128)(2,1)S(1)}, u32[]{:S(2)}, u32[]{:S(2)}) collective-permute-start(bf16[1,512,1024]{2,1,0:T(8,128)(2,1)S(1)} %copy-done.3), channel_id=1, source_target_pairs={{0,1},{1,0},{2,3},{3,2},{4,5},{5,4},{6,7},{7,6},{8,9},{9,8},{10,11... | collective-permute-start | bytes 3145736 | tf_op jit(solution)/shard_map/ppermute | solution.py:554
  12.7 12.3 %collective-permute-start.11 = (bf16[2,512,512]{2,1,0:T(8,128)(2,1)S(1)}, bf16[2,512,512]{2,1,0:T(8,128)(2,1)S(1)}, u32[]{:S(2)}, u32[]{:S(2)}) collective-permute-start(bf16[2,512,512]{2,1,0:T(8,128)(2,1)S(1)} %pack.1), channel_id=1, source_target_pairs={{0,1},{1,0},{2,3},{3,2},{4,5},{5,4},{6,7},{7,6},{8,9},{9,8},{10,11... | collective-permute-start | bytes 3145736 | tf_op jit(solution)/shard_map/ppermute | solution.py:554
  13.5 6.5 %collective-permute-start.4 = (bf16[272,512]{1,0:T(8,128)(2,1)S(1)}, bf16[272,512]{1,0:T(8,128)(2,1)S(1)}, u32[]{:S(2)}, u32[]{:S(2)}) collective-permute-start(bf16[272,512]{1,0:T(8,128)(2,1)S(1)} %get-tuple-element.85), channel_id=1, source_target_pairs={{0,8},{1,0},{2,10},{3,2},{4,12},{5,4},{6,14},{7,6},{8,9},{9,1},{10... | collective-permute-start | bytes 835592 | tf_op jit(solution)/shard_map/ppermute | solution.py:554
  16.5 3.0 %copy-start = (bf16[1024,512]{1,0:T(8,128)(2,1)S(1)}, bf16[1024,512]{1,0:T(8,128)(2,1)}, u32[]{:S(2)}) copy-start(bf16[1024,512]{1,0:T(8,128)(2,1)} %refs_2_.3) | copy-start | bytes 3145732
  16.5 3.8 %collective-permute-start.5 = (bf16[128,512]{1,0:T(8,128)(2,1)S(1)}, bf16[128,512]{1,0:T(8,128)(2,1)S(1)}, u32[]{:S(2)}, u32[]{:S(2)}) collective-permute-start(bf16[128,512]{1,0:T(8,128)(2,1)S(1)} %next.6), channel_id=1, source_target_pairs={{0,8},{1,0},{2,10},{3,2},{4,12},{5,4},{6,14},{7,6},{8,9},{9,1},{10... | collective-permute-start | bytes 393224 | tf_op jit(solution)/shard_map/ppermute | solution.py:554
  18.0 1.5 %copy-start.7 = (s32[128]{0:T(128)S(1)}, s32[128]{0:T(128)}, u32[]{:S(2)}) copy-start(s32[128]{0:T(128)} %param.20) | copy-start | bytes 1540
  18.0 3.8 %collective-permute-start.6 = (bf16[128,512]{1,0:T(8,128)(2,1)S(1)}, bf16[128,512]{1,0:T(8,128)(2,1)S(1)}, u32[]{:S(2)}, u32[]{:S(2)}) collective-permute-start(bf16[128,512]{1,0:T(8,128)(2,1)S(1)} %next.7), channel_id=1, source_target_pairs={{0,8},{1,0},{2,10},{3,2},{4,12},{5,4},{6,14},{7,6},{8,9},{9,1},{10... | collective-permute-start | bytes 393224 | tf_op jit(solution)/shard_map/ppermute | solution.py:554
  21.8 2.8 %collective-permute-start.7 = (bf16[272,512]{1,0:T(8,128)(2,1)S(1)}, bf16[272,512]{1,0:T(8,128)(2,1)S(1)}, u32[]{:S(2)}, u32[]{:S(2)}) collective-permute-start(bf16[272,512]{1,0:T(8,128)(2,1)S(1)} %get-tuple-element.96), channel_id=1, source_target_pairs={{0,1},{1,0},{2,3},{3,2},{4,5},{5,4},{6,7},{7,6},{8,16},{9,8},{10,1... | collective-permute-start | bytes 835592 | tf_op jit(solution)/shard_map/ppermute | solution.py:554
  23.4 1.4 %collective-permute-start.8 = (bf16[128,512]{1,0:T(8,128)(2,1)S(1)}, bf16[128,512]{1,0:T(8,128)(2,1)S(1)}, u32[]{:S(2)}, u32[]{:S(2)}) collective-permute-start(bf16[128,512]{1,0:T(8,128)(2,1)S(1)} %next.8), channel_id=1, source_target_pairs={{0,1},{1,0},{2,3},{3,2},{4,5},{5,4},{6,7},{7,6},{8,16},{9,8},{10,1... | collective-permute-start | bytes 393224 | tf_op jit(solution)/shard_map/ppermute | solution.py:554
  23.4 1.6 %collective-permute-start.9 = (bf16[128,512]{1,0:T(8,128)(2,1)S(1)}, bf16[128,512]{1,0:T(8,128)(2,1)S(1)}, u32[]{:S(2)}, u32[]{:S(2)}) collective-permute-start(bf16[128,512]{1,0:T(8,128)(2,1)S(1)} %next.9), channel_id=1, source_target_pairs={{0,1},{1,0},{2,3},{3,2},{4,5},{5,4},{6,7},{7,6},{8,16},{9,8},{10,1... | collective-permute-start | bytes 393224 | tf_op jit(solution)/shard_map/ppermute | solution.py:554
  25.0 22.9 %collective-permute-start.12 = (bf16[128,512]{1,0:T(8,128)(2,1)S(1)}, bf16[128,512]{1,0:T(8,128)(2,1)S(1)}, u32[]{:S(2)}, u32[]{:S(2)}) collective-permute-start(bf16[128,512]{1,0:T(8,128)(2,1)S(1)} %get-tuple-element.108), channel_id=1, source_target_pairs={{0,1},{1,0},{2,3},{3,2},{4,5},{5,21},{6,7},{7,6},{8,9},{9,8},{10,1... | collective-permute-start | bytes 393224 | tf_op jit(solution)/shard_map/ppermute | solution.py:554
  25.5 22.5 %collective-permute-start.13 = (bf16[128,512]{1,0:T(8,128)(2,1)S(1)}, bf16[128,512]{1,0:T(8,128)(2,1)S(1)}, u32[]{:S(2)}, u32[]{:S(2)}) collective-permute-start(bf16[128,512]{1,0:T(8,128)(2,1)S(1)} %get-tuple-element.109), channel_id=1, source_target_pairs={{0,1},{1,0},{2,3},{3,2},{4,5},{5,4},{6,7},{7,17},{8,9},{9,8},{10,1... | collective-permute-start | bytes 393224 | tf_op jit(solution)/shard_map/ppermute | solution.py:554
  25.6 22.4 %collective-permute-start.14 = (bf16[128,512]{1,0:T(8,128)(2,1)S(1)}, bf16[128,512]{1,0:T(8,128)(2,1)S(1)}, u32[]{:S(2)}, u32[]{:S(2)}) collective-permute-start(bf16[128,512]{1,0:T(8,128)(2,1)S(1)} %get-tuple-element.111.refs_3_), channel_id=1, source_target_pairs={{0,1},{1,17},{2,3},{3,2},{4,5},{5,4},{6,7},{7,6},{8,9},{9,19},{10,... | collective-permute-start | bytes 393224 | tf_op jit(solution)/shard_map/ppermute | solution.py:554
  26.0 25.3 %collective-permute-start.15 = (bf16[128,512]{1,0:T(8,128)(2,1)S(1)}, bf16[128,512]{1,0:T(8,128)(2,1)S(1)}, u32[]{:S(2)}, u32[]{:S(2)}) collective-permute-start(bf16[128,512]{1,0:T(8,128)(2,1)S(1)} %get-tuple-element.112.refs_4_), channel_id=1, source_target_pairs={{0,1},{1,0},{2,3},{3,17},{4,5},{5,4},{6,7},{7,6},{8,9},{9,8},{10,1... | collective-permute-start | bytes 393224 | tf_op jit(solution)/shard_map/ppermute | solution.py:554
  48.0 8.0 %copy-start.6 = (bf16[512,227]{0,1:T(8,128)(2,1)S(1)}, bf16[512,227]{0,1:T(8,128)(2,1)}, u32[]{:S(2)}) copy-start(bf16[512,227]{0,1:T(8,128)(2,1)} %param.18) | copy-start | bytes 697348
  51.3 4.7 %collective-permute-start.16 = (bf16[64,512]{1,0:T(8,128)(2,1)S(1)}, bf16[64,512]{1,0:T(8,128)(2,1)S(1)}, u32[]{:S(2)}, u32[]{:S(2)}) collective-permute-start(bf16[64,512]{1,0:T(8,128)(2,1)S(1)} %get-tuple-element.114), channel_id=1, source_target_pairs={{0,1},{1,0},{2,3},{3,2},{4,5},{5,4},{6,7},{7,6},{8,9},{9,8},{10,11... | collective-permute-start | bytes 196616 | tf_op jit(solution)/shard_map/ppermute | solution.py:573

commit v14 on v12

--- a/solution.py
+++ b/solution.py
@@ -235,7 +235,7 @@
 
 
 def index_kernel(parts, mesh_rows, where, *refs):
-    lanes, (columns_out, low, high), index_out = refs[:-4], refs[-4:-1], refs[-1]
+    lanes, (columns_out, codes, state), index_out = refs[:-4], refs[-4:-1], refs[-1]
     nodes = columns_out.shape[0]
     group = len(lanes)
     rows = lanes[0].shape[0] // (parts // group)
@@ -247,8 +247,7 @@
         for part in range(parts):
             lane, turn = lanes[part % group], jnp.bitwise_xor(chip, part // group)
             base = pl.multiple_of(turn * rows, 16)
-            half, spot = (low, part) if part < parts // 2 else (high, part - parts // 2)
-            half[spot * mesh_rows : (spot + 1) * mesh_rows, :] = lane[pl.ds(base, mesh_rows), :]
+            state[part * mesh_rows : (part + 1) * mesh_rows, :] = lane[pl.ds(base, mesh_rows), :]
             base = pl.multiple_of(turn * rows + mesh_rows, 16)
             coded = lane[pl.ds(base, rows - mesh_rows), :384].astype(jnp.float32).astype(jnp.int32)
             tables.append(coded[: coded.shape[0] // 2])
@@ -268,12 +267,25 @@
         names = index_out[...]
         high_digit = names // DIGIT
         digits = jnp.concatenate([high_digit, names - high_digit * DIGIT], axis=0)
-        low[parts // 2 * mesh_rows :, :] = digits.astype(jnp.float32).astype(jnp.bfloat16)
+        codes[...] = digits.astype(jnp.float32).astype(jnp.bfloat16)
         columns_out[...] = columns_of(names.astype(jnp.float32))
 
 
-def hold_kernel(w_project, w_message, w_update, receive, send, own, edges, message, update, semaphores):
-    width = own.shape[0]
+def pack_kernel(group, where, w_message, w_update, pair, message, update, semaphores):
+    width = message.shape[0]
+
+    @pl.when(jnp.logical_and(lax.rem(where[0], 2) == 1, lax.rem(where[1], group) == 0))
+    def _():
+        sources = [w_message.at[0], w_update.at[0, width:], w_update.at[0, :width]]
+        copies = fetch(sources, [message, update, pair.at[0]], semaphores)
+        copies[0].wait()
+        copies[1].wait()
+        pair[1] = matmul(message[...], update[...]).astype(jnp.bfloat16)
+        copies[2].wait()
+
+
+def hold_kernel(w_project, w_message, w_update, receive, send, pair, message, update, semaphores):
+    width = receive.shape[0]
     sources = [
         w_message.at[0],
         w_update.at[0, width:],
@@ -281,38 +293,22 @@
         w_project.at[0, :, width:],
         w_update.at[0, :width],
     ]
-    copies = fetch(sources, [message, update, receive, send, own], semaphores)
+    copies = fetch(sources, [message, update, receive, send, pair.at[0]], semaphores)
     copies[0].wait()
     copies[1].wait()
-    edges[...] = matmul(message[...], update[...]).astype(jnp.bfloat16)
+    pair[1] = matmul(message[...], update[...]).astype(jnp.bfloat16)
     for copy in copies[2:]:
         copy.wait()
 
 
-def blocks_of(weights):
-    if len(weights) == 4:
-        receive, send, own, edges = weights
-        return receive[...], send[...], own[...], lambda gathered: matmul(gathered, edges[...])
-    w_project, w_message, w_update = weights
-    width = w_message.shape[1]
-
-    def finish(gathered):
-        aggregate = matmul(gathered, w_message[0]).astype(jnp.bfloat16)
-        return matmul(aggregate, w_update[0, width:, :])
-
-    return w_project[0, :, :width], w_project[0, :, width:], w_update[0, :width, :], finish
-
-
-def renew(fanout, columns, sender, own, weights):
+def sum_edges(fanout, columns, sender, own, w_receive):
     chunk, width = own.shape
     nodes = sender.shape[0]
     tile = min(nodes, DIGIT)
     names = lax.broadcasted_iota(jnp.int32, (chunk, tile), 1).astype(jnp.float32).astype(jnp.bfloat16)
     one_half = jnp.full((chunk, tile), 0.5, jnp.bfloat16)
     none = jnp.zeros((chunk, tile), jnp.bfloat16)
-    w_receive, _, w_own, finish = blocks_of(weights)
     receiver = 0.5 * matmul(own, w_receive)
-    update = matmul(own, w_own)
     total = jnp.zeros((chunk, width), jnp.float32)
     for k in range(fanout):
         hits = []
@@ -321,77 +317,99 @@
             hits.append(jnp.where(columns[:, lane : lane + 1] == names, one_half, none))
         half = receiver + matmul(jnp.concatenate(hits, axis=1), sender)
         total = total + (half + half * jnp.tanh(half))
-    gathered = (total * (1.0 / fanout)).astype(jnp.bfloat16)
-    update = silu_by_tanh(update + finish(gathered))
+    return (total * (1.0 / fanout)).astype(jnp.bfloat16)
+
+
+def update_nodes(own, gathered, w_own, w_edges):
+    update = silu_by_tanh(matmul(own, w_own) + matmul(gathered, w_edges))
     return (own.astype(jnp.float32) + rms_scale(update)).astype(jnp.bfloat16)
+
+
+def sender_kernel(group, at_segment, fanout, rows, where, state, w_send, sender, *columns):
+    @pl.when(owns(where, group, at_segment))
+    def _():
+        sender[...] = matmul(state[:rows, :], w_send[...]).astype(jnp.bfloat16)
+        if columns:
+            digits = state[rows:, :].astype(jnp.float32)
+            columns[0][...] = columns_of(digits[:fanout] * DIGIT + digits[fanout:])
+
+
+def layer_kernel(group, at_segment, fanout, rows, where, columns, *refs):
+    parts = len(rows)
+    state, senders, refs = refs[:parts], refs[parts : 2 * parts - 1], refs[2 * parts - 1 :]
+    (w_receive, w_send, pair), (renewed, whole, sender) = refs[:3], refs[3:]
+    nodes = renewed.shape[0]
+    chunk = min(nodes, 256)
+
+    @pl.when(owns(where, group, at_segment))
+    def _():
+        start = 0
+        for part, count in zip(state, rows):
+            whole[start : start + count, :] = part[:count, :]
+            start += count
+        start = 0
+        for part in senders:
+            sender[start : start + part.shape[0], :] = part[...]
+            start += part.shape[0]
+        sender[start:, :] = matmul(whole[start:, :], w_send[...]).astype(jnp.bfloat16)
+        for start in range(0, nodes, chunk):
+            span = slice(start, start + chunk)
+            gathered = sum_edges(fanout, columns[span, :], sender[...], whole[span, :], w_receive[...])
+            renewed[span, :] = update_nodes(whole[span, :], gathered, pair[0], pair[1])
+
+
+def edges_kernel(group, at_segment, fanout, where, columns, state, w_project, gathered, sender):
+    nodes, width = state.shape
+    chunk = min(nodes, 256)
+
+    @pl.when(owns(where, group, at_segment))
+    def _():
+        sender[...] = matmul(state[...], w_project[0, :, width:]).astype(jnp.bfloat16)
+        for start in range(0, nodes, chunk):
+            span = slice(start, start + chunk)
+            gathered[span, :] = sum_edges(
+                fanout, columns[span, :], sender[...], state[span, :], w_project[0, :, :width]
+            )
+
+
+def update_kernel(group, at_segment, start, where, gathered, state, codes, pair, piece):
+    rows = piece.shape[0] - (codes.shape[0] if start == 0 else 0)
+
+    @pl.when(owns(where, group, at_segment))
+    def _():
+        span = slice(start, start + rows)
+        piece[:rows, :] = update_nodes(state[span, :], gathered[span, :], pair[0], pair[1])
+        if start == 0:
+            piece[rows:, :] = codes[...]
+
+
+def half_kernel(group, at_segment, chips, far, fanout, where, columns, state, *refs):
+    senders, refs = (refs[:0], refs) if far else (refs[:1], refs[1:])
+    (w_project, pair), outs = refs[:2], refs[2:]
+    nodes, width = state.shape
+    half = nodes // 2
+    chip, _ = place_of(where, group)
+
+    @pl.when(owns(where, group, at_segment))
+    def _():
+        pieces = outs
+        if far:
+            outs[0][...] = matmul(state[...], w_project[0, :, width:]).astype(jnp.bfloat16)
+            pieces = outs[1:]
+        sender = outs[0] if far else senders[0]
+        upper = (chip < chips // 2) if far else (chip >= chips // 2)
+        start = pl.multiple_of(jnp.where(upper, half, 0), half)
+        own = state[pl.ds(start, half), :]
+        gathered = sum_edges(
+            fanout, columns[pl.ds(start, half), :], sender[...], own, w_project[0, :, :width]
+        )
+        write_pieces(pieces, update_nodes(own, gathered, pair[0], pair[1]))
 
 
 def write_pieces(pieces, value):
     rows = value.shape[0] // len(pieces)
     for place, piece in enumerate(pieces):
         piece[:rows, :] = value[place * rows : (place + 1) * rows]
-
-
-def sender_kernel(group, at_segment, fanout, rows, where, low, *refs):
-    weights, sender_low, columns = (refs[:-2], *refs[-2:]) if fanout else (refs[:-1], refs[-1], None)
-
-    @pl.when(owns(where, group, at_segment))
-    def _():
-        sender_low[...] = matmul(low[:rows, :], blocks_of(weights)[1]).astype(jnp.bfloat16)
-        if fanout:
-            digits = low[rows:, :].astype(jnp.float32)
-            columns[...] = columns_of(digits[:fanout] * DIGIT + digits[fanout:])
-
-
-def half_of(where, group, chips, far, low, high, own):
-    half = high.shape[0]
-    chip, _ = place_of(where, group)
-    upper = (chip < chips // 2) if far else (chip >= chips // 2)
-
-    @pl.when(upper)
-    def _():
-        own[...] = high[...]
-
-    @pl.when(jnp.logical_not(upper))
-    def _():
-        own[...] = low[...]
-
-    return pl.multiple_of(jnp.where(upper, half, 0), half)
-
-
-def first_kernel(
-    group, at_segment, chips, fanout, given, where, columns, sender_low, low, high, *refs
-):
-    weights, sender, pieces, own = refs[:given], refs[given], refs[given + 1 : -1], refs[-1]
-    half = high.shape[0]
-
-    @pl.when(owns(where, group, at_segment))
-    def _():
-        sender[:half, :] = sender_low[...]
-        sender[half:, :] = matmul(high[...], blocks_of(weights)[1]).astype(jnp.bfloat16)
-        start, state = 0, low[:half, :]
-        if chips:
-            start = half_of(where, group, chips, True, low, high, own)
-            state = own[...]
-        rows = columns[pl.ds(start, half), :]
-        write_pieces(pieces, renew(fanout, rows, sender[...], state, weights))
-        if pieces[0].shape[0] > half:
-            pieces[0][half:, :] = low[half:, :]
-
-
-def second_kernel(
-    group, at_segment, chips, fanout, given, where, columns, sender, low, high, *refs
-):
-    weights, pieces, own = refs[:given], refs[given:-1], refs[-1]
-    half = high.shape[0]
-
-    @pl.when(owns(where, group, at_segment))
-    def _():
-        start, state = half, high
-        if chips:
-            start, state = half_of(where, group, chips, False, low, high, own), own
-        rows = columns[pl.ds(start, half), :]
-        write_pieces(pieces, renew(fanout, rows, sender[...], state[...], weights))
 
 
 def arrival(where, group, chips, last):
@@ -459,7 +477,7 @@
     out[...] = matmul_nt(w_output[...], hidden).astype(jnp.bfloat16)
 
 
-def call(kernel, name, shapes, inputs, places, scratch=(), room=16):
+def call(kernel, name, shapes, inputs, places, scratch=(), room=16, flops=0):
     specs, given = [], []
     for value, place in zip(inputs, places):
         specs += [SMEM] * 2 if place == "w" else [VMEM if place == "v" else HBM]
@@ -477,7 +495,7 @@
         scratch_shapes=list(scratch),
         name=name,
         compiler_params=pltpu.CompilerParams(vmem_limit_bytes=room * 1024 * 1024),
-        cost_estimate=pl.CostEstimate(flops=0, bytes_accessed=moved, transcendentals=0),
+        cost_estimate=pl.CostEstimate(flops=flops, bytes_accessed=moved, transcendentals=0),
     )(*given)
 
 
@@ -536,7 +554,7 @@
         return lax.ppermute(value, ("segment", "dom"), every_device(pairs, segments * parts, group))
 
     def to_chip(value, steps):
-        giver = steps - 1
+        giver = last if steps == samples - 1 else 0
         pairs = []
         for at in range(segments):
             for dom in range(parts):
@@ -557,13 +575,23 @@
     def owner(m, at_segment):
         return device(at_segment, m * group)
 
-    own_segment, own_place, *weights = lax.optimization_barrier(
-        (segment.reshape(1), place.reshape(1), w_project, w_message, w_update)
+    own_segment, own_place, w_project = lax.optimization_barrier(
+        (segment.reshape(1), place.reshape(1), w_project)
     )
     where = (own_segment, own_place)
+    weights = [w_project, w_message, w_update]
     last = segments - 2
-    pairs = [(owner(m, last + 1), owner(m, last)) for m in range(samples)]
-    came_weights = [send(weight, pairs) for weight in weights]
+    pairs = [(owner(m, at + 1), owner(m, at)) for m in range(samples) for at in range(0, segments, 2)]
+    (pair,) = call(
+        functools.partial(pack_kernel, group),
+        "pack",
+        [jax.ShapeDtypeStruct((2, width, width), bf16)],
+        [where, w_message, w_update],
+        "whh",
+        [pltpu.VMEM((width, width), bf16)] * 2 + [pltpu.SemaphoreType.DMA((3,))],
+        room=60,
+    )
+    came = [send(w_project, pairs), send(pair, pairs)]
     snapshots = jnp.transpose(grid_state, (0, 2, 1))
     lists = send_rows.shape[0]
 
@@ -590,7 +618,7 @@
     held = call(
         hold_kernel,
         "hold",
-        [jax.ShapeDtypeStruct((width, width), bf16)] * 4,
+        [jax.ShapeDtypeStruct((width, width), bf16)] * 2 + [jax.ShapeDtypeStruct((2, width, width), bf16)],
         weights,
         "hhh",
         [pltpu.VMEM((width, width), bf16)] * 2 + [pltpu.SemaphoreType.DMA((5,))],
@@ -605,71 +633,96 @@
         "v" * samples,
     )
     lanes = [joined] + [change_lane(joined, -steps) for steps in range(1, group)]
-    half = nodes // 2
     share = group * mesh_rows
-    columns, low, high = call(
+    whole, short, tall = [
+        jax.ShapeDtypeStruct((rows, width), bf16) for rows in (nodes, share, share + 2 * fanout)
+    ]
+    columns_shape = jax.ShapeDtypeStruct((nodes, 128), bf16)
+    columns, codes, state = call(
         functools.partial(index_kernel, parts, mesh_rows),
         "index",
-        [
-            jax.ShapeDtypeStruct((nodes, 128), bf16),
-            jax.ShapeDtypeStruct((half + 2 * fanout, width), bf16),
-            jax.ShapeDtypeStruct((half, width), bf16),
-        ],
+        [columns_shape, jax.ShapeDtypeStruct((2 * fanout, width), bf16), whole],
         [where] + lanes,
         "w" + "v" * group,
         [pltpu.VMEM((fanout, nodes), jnp.int32)],
     )
-    state_shape = jax.ShapeDtypeStruct((half, width), bf16)
-    for layer in range(segments):
-        at_segment, ends = min(layer, last), layer > last
-        used = list(held) if layer <= last else came_weights
-        role = (group, at_segment, samples if ends else 0, fanout, len(used))
-        pieces = [jax.ShapeDtypeStruct((share, width), bf16)] * (half // share) if ends else [state_shape]
-        scratch = [pltpu.VMEM((half, width), bf16)]
-        arrives = 0 < layer <= last
-        sender_low, *found = call(
-            functools.partial(sender_kernel, group, at_segment, fanout if arrives else 0, half),
+    both = [pltpu.VMEM((nodes, width), bf16)] * 2
+    (state,) = call(
+        functools.partial(layer_kernel, group, 0, fanout, (nodes,)),
+        "layer",
+        [whole],
+        [where, columns, state] + list(held),
+        "w" + "v" * 5,
+        both,
+    )
+    (gathered,) = call(
+        functools.partial(edges_kernel, group, 0, fanout),
+        "edges",
+        [whole],
+        [where, columns, state, came[0]],
+        "wvvv",
+        both[:1],
+    )
+    pairs = [(owner(m, 0), owner(m, last)) for m in range(samples)]
+    pieces, senders = [], []
+    for start in range(0, nodes, share):
+        (piece,) = call(
+            functools.partial(update_kernel, group, 0, start),
+            "update",
+            [short if start else tall],
+            [where, gathered, state, codes, came[1]],
+            "wvvvv",
+        )
+        pieces.append(send(piece, pairs))
+    ready, table = call(
+        prepare_kernel,
+        "prepare",
+        [
+            jax.ShapeDtypeStruct((grid_rows, width), jnp.float32),
+            jax.ShapeDtypeStruct((mesh_rows, grid_rows), bf16),
+        ],
+        [where, snapshots, w_embed, w_decode, mesh_grid.reshape(1, grid_rows)],
+        "wvvvv",
+    )
+    pieces[0], ready, table = lax.optimization_barrier((pieces[0], ready, table))
+    for piece in pieces[:-1]:
+        if senders:
+            piece, senders[-1] = lax.optimization_barrier((piece, senders[-1]))
+        sender, *found = call(
+            functools.partial(sender_kernel, group, last, fanout, share),
             "sender",
-            [state_shape] + [jax.ShapeDtypeStruct((nodes, 128), bf16)] * arrives,
-            [where, low] + used,
-            "wv" + "v" * len(used),
-        )
-        columns = found[0] if arrives else columns
-        tall = jax.ShapeDtypeStruct((half + 2 * fanout, width), bf16)
-        sender, *first = call(
-            functools.partial(first_kernel, *role),
-            "first",
-            [jax.ShapeDtypeStruct((nodes, width), bf16)] + ([tall] if layer < last else pieces),
-            [where, columns, sender_low, low, high] + used,
-            "wvvvv" + "v" * len(used),
-            scratch,
-        )
-        pairs = [(owner(m, layer), owner(m, layer + 1)) for m in range(samples)]
-        new_low = send(first[0], pairs) if layer < last else first[0]
-        second = call(
-            functools.partial(second_kernel, *role),
-            "second",
-            pieces,
-            [where, columns, sender, low, high] + used,
-            "wvvvv" + "v" * len(used),
-            scratch,
-        )
-        low, high = new_low, send(second[0], pairs) if layer < last else second[0]
-        if layer == 0:
-            ready, table = call(
-                prepare_kernel,
-                "prepare",
-                [
-                    jax.ShapeDtypeStruct((grid_rows, width), jnp.float32),
-                    jax.ShapeDtypeStruct((mesh_rows, grid_rows), bf16),
-                ],
-                [where, snapshots, w_embed, w_decode, mesh_grid.reshape(1, grid_rows)],
-                "wvvvv",
-                    )
-            low, ready, table = lax.optimization_barrier((low, ready, table))
+            [short] + [columns_shape] * (not senders),
+            [where, piece, held[1]],
+            "wvv",
+        )
+        columns = found[0] if found else columns
+        senders.append(sender)
+    (state,) = call(
+        functools.partial(layer_kernel, group, last, fanout, (share,) * samples),
+        "layer",
+        [whole],
+        [where, columns] + pieces + senders + list(held),
+        "w" + "v" * (2 * samples + 3),
+        both,
+    )
+    sender, *far = call(
+        functools.partial(half_kernel, group, last, samples, True, fanout),
+        "far_half",
+        [whole] + [short] * (samples // 2),
+        [where, columns, state] + came,
+        "wvvvv",
+    )
+    near = call(
+        functools.partial(half_kernel, group, last, samples, False, fanout),
+        "near_half",
+        [short] * (samples // 2),
+        [where, columns, state, sender] + came,
+        "wvvvvv",
+    )
+    state = far + list(near)
     each = samples // 2
     arrived = []
-    for far, blocks in ((1, first), (0, second)):
+    for far, blocks in ((1, state[:each]), (0, state[each:])):
         for turn, block in enumerate(blocks):
             pairs = [
                 (owner(m, last), device(m, ((m // each ^ far) * each + turn) * group)) for m in range(samples)
@@ -686,7 +739,7 @@
         functools.partial(near_kernel, group, samples, last),
         "near",
         [jax.ShapeDtypeStruct((mesh_rows, width), bf16)] * group,
-        [where, crossed] + arrived[each:] + list(second),
+        [where, crossed] + arrived[each:] + state[each:],
         "w" + "v" * (1 + 2 * each),
     )
     handed = [parts_of_block[0]]

time: 58.2 us -> 56.3 us (0.967)
  the two profiles are of different devices: /device:TPU:9 before, /device:TPU:13 now
where the time goes in v14:
time: 56.3 us; the launch traced here: 56.2 us
  starting transfers between devices  27.8 us (49%)
  waiting for transfers between devices  23.8 us (42%)
  Pallas kernels  4.21 us (7%)
    ppermute x10, starting transfers between devices, send(): lax.ppermute(value, ('segment', 'dom'), every_device(pairs, segments * pa...  20.6 us
    ppermute x10, waiting for transfers between devices, send(): lax.ppermute(value, ('segment', 'dom'), every_device(pairs, segments * pa...  19.7 us
    ppermute x2, starting transfers between devices, change_lane(): return lax.ppermute(value, 'dom', pairs)  4.46 us
    pallas_call x21, Pallas kernels, call(): pl.pallas_call(located if places[0] == 'w' else kernel, out_shape=shapes,...  4.21 us
    ppermute x3, starting transfers between devices, to_chip(): return lax.ppermute(value, ('segment', 'dom'), pairs)  2.68 us
    ppermute x2, waiting for transfers between devices, change_lane(): return lax.ppermute(value, 'dom', pairs)  2.16 us
    ppermute x3, waiting for transfers between devices, to_chip(): return lax.ppermute(value, ('segment', 'dom'), pairs)  1.87 us
  transfers between devices with their start and end apart: 15, of which 8 were waited for; matrix products, arithmetic and copies ran while one was open for 0% of the time, Pallas kernels for 5%

profile of v14, /device:TPU:13, one launch (start us, length us, event | category | flops | bytes accessed | tf_op | source)
XLA Modules:
  0.0 56.2 jit_solution(8742144971456360969)
XLA Ops:
  0.0 1.2 %collective-permute-start.4 = (bf16[1,512,1024]{2,1,0:T(8,128)(2,1)}, bf16[1,512,1024]{2,1,0:T(8,128)(2,1)S(1)}, u32[]{:S(2)}, u32[]{:S(2)}) collective-permute-start(bf16[1,512,1024]{2,1,0:T(8,128)(2,1)} %w_project), channel_id=1, source_target_pairs={{0,1},{1,9},{2,3},{3,11},{4,5},{5,13},{6,7},{7,15},{8,0},{9,8},{10... | collective-permute-start | bytes 3145736 | tf_op jit(solution)/shard_map/ppermute | solution.py:554
  1.2 0.0 copy-start.4
  1.2 0.0 copy-start
  1.2 0.0 copy-start.3
  1.3 1.0 %pack.1 = bf16[2,512,512]{2,1,0:T(8,128)(2,1)} custom-call(s32[1]{0:T(128)} %bitcast.segment, s32[1]{0:T(128)} %bitcast.1.place, bf16[1,512,512]{2,1,0:T(8,128)(2,1)} %refs_0_.1, bf16[1,1024,512]{2,1,0:T(8,128)(2,1)} %refs_1_.4), custom_call_target="tpu_custom_call" | custom-call | bytes 2621448 | tf_op jit(solution)/shard_map/pack/pallas_call | solution.py:490
  2.3 0.0 copy-start.2
  2.3 0.7 %collective-permute-start.5 = (bf16[2,512,512]{2,1,0:T(8,128)(2,1)}, bf16[2,512,512]{2,1,0:T(8,128)(2,1)S(1)}, u32[]{:S(2)}, u32[]{:S(2)}) collective-permute-start(bf16[2,512,512]{2,1,0:T(8,128)(2,1)} %pack.1), channel_id=1, source_target_pairs={{0,1},{1,9},{2,3},{3,11},{4,5},{5,13},{6,7},{7,15},{8,0},{9,8},{10... | collective-permute-start | bytes 3145736 | tf_op jit(solution)/shard_map/ppermute | solution.py:554
  3.0 0.0 copy-done.7
  3.0 0.0 copy-done.8
  3.0 0.0 copy-done.9
  3.1 0.0 copy-done.10
  3.1 0.0 copy-done.11
  3.1 0.0 copy-done.4
  3.1 0.7 %encode.1 = (bf16[80,512]{1,0:T(8,128)(2,1)S(1)}, bf16[80,512]{1,0:T(8,128)(2,1)S(1)}, bf16[80,512]{1,0:T(8,128)(2,1)S(1)}, bf16[80,512]{1,0:T(8,128)(2,1)S(1)}) custom-call(s32[1]{0:T(128)} %bitcast.segment, s32[1]{0:T(128)} %bitcast.1.place, bf16[4,227,128]{2,1,0:T(8,128)(2,1)S(1)} %bitcast.13, bf16[227,512]{1,0:T(8,128)(2,1)S(1)} %copy-done.4, ...), custom_call_target="tpu_custom_call" | custom-call | bytes 799752 | tf_op jit(solution)/shard_map/encode/pallas_call | solution.py:490
  3.8 0.1 collective-permute-start
  3.9 0.5 collective-permute-start.1
  4.4 2.1 %collective-permute-start.2 = (bf16[80,512]{1,0:T(8,128)(2,1)S(1)}, bf16[80,512]{1,0:T(8,128)(2,1)S(1)}, u32[]{:S(2)}, u32[]{:S(2)}) collective-permute-start(bf16[80,512]{1,0:T(8,128)(2,1)S(1)} %get-tuple-element.50), channel_id=1, source_target_pairs={{0,16},{1,17},{2,18},{3,19},{4,20},{5,21},{6,22},{7,23},{8,9},{9,8... | collective-permute-start | bytes 245768 | tf_op jit(solution)/shard_map/ppermute | solution.py:569
  6.5 0.0 copy-done.3
  6.5 0.7 %hold.1 = (bf16[512,512]{1,0:T(8,128)(2,1)S(1)}, bf16[512,512]{1,0:T(8,128)(2,1)S(1)}, bf16[2,512,512]{2,1,0:T(8,128)(2,1)S(1)}) custom-call(bf16[1,512,1024]{2,1,0:T(8,128)(2,1)S(1)} %copy-done.3, bf16[1,512,512]{2,1,0:T(8,128)(2,1)S(1)} %copy-done.2, bf16[1,1024,512]{2,1,0:T(8,128)(2,1)S(1)} %copy-done), custom_call_target="tpu_custom_call" | custom-call | bytes 4718592 | tf_op jit(solution)/shard_map/hold/pallas_call | solution.py:490
  7.3 0.0 collective-permute-done.refs_1_
  7.3 0.0 collective-permute-done.1.refs_2_
  7.3 1.9 %collective-permute-done.2.refs_3_ = bf16[80,512]{1,0:T(8,128)(2,1)S(1)} collective-permute-done((bf16[80,512]{1,0:T(8,128)(2,1)S(1)}, bf16[80,512]{1,0:T(8,128)(2,1)S(1)}, u32[]{:S(2)}, u32[]{:S(2)}) %collective-permute-start.2) | collective-permute-done | bytes 81952 | tf_op jit(solution)/shard_map/ppermute | solution.py:569
  9.2 1.8 %collective-permute-start.3 = (bf16[320,512]{1,0:T(8,128)(2,1)S(1)}, bf16[320,512]{1,0:T(8,128)(2,1)S(1)}, u32[]{:S(2)}, u32[]{:S(2)}) collective-permute-start(bf16[320,512]{1,0:T(8,128)(2,1)S(1)} %join.1.refs_0_), channel_id=1, source_target_pairs={{0,1},{1,0},{2,3},{3,2},{4,5},{5,4},{6,7},{7,6},{8,9},{9,8},{10,11... | collective-permute-start | bytes 983048 | tf_op jit(solution)/shard_map/ppermute | solution.py:573
  11.0 1.3 %collective-permute-done.3.refs_1_ = bf16[320,512]{1,0:T(8,128)(2,1)S(1)} collective-permute-done((bf16[320,512]{1,0:T(8,128)(2,1)S(1)}, bf16[320,512]{1,0:T(8,128)(2,1)S(1)}, u32[]{:S(2)}, u32[]{:S(2)}) %collective-permute-start.3) | collective-permute-done | bytes 327712 | tf_op jit(solution)/shard_map/ppermute | solution.py:573
  12.3 1.0 %collective-permute-done.4.refs_2_.refs_3_ = bf16[1,512,1024]{2,1,0:T(8,128)(2,1)S(1)} collective-permute-done((bf16[1,512,1024]{2,1,0:T(8,128)(2,1)}, bf16[1,512,1024]{2,1,0:T(8,128)(2,1)S(1)}, u32[]{:S(2)}, u32[]{:S(2)}) %collective-permute-start.4) | collective-permute-done | bytes 1048608 | tf_op jit(solution)/shard_map/ppermute | solution.py:554
  13.3 11.2 %collective-permute-done.5.refs_3_.refs_4_ = bf16[2,512,512]{2,1,0:T(8,128)(2,1)S(1)} collective-permute-done((bf16[2,512,512]{2,1,0:T(8,128)(2,1)}, bf16[2,512,512]{2,1,0:T(8,128)(2,1)S(1)}, u32[]{:S(2)}, u32[]{:S(2)}) %collective-permute-start.5) | collective-permute-done | bytes 1048608 | tf_op jit(solution)/shard_map/ppermute | solution.py:554
  24.5 0.2 collective-permute-start.6
  24.7 2.9 %collective-permute-start.7 = (bf16[128,512]{1,0:T(8,128)(2,1)S(1)}, bf16[128,512]{1,0:T(8,128)(2,1)S(1)}, u32[]{:S(2)}, u32[]{:S(2)}) collective-permute-start(bf16[128,512]{1,0:T(8,128)(2,1)S(1)} %update.5), channel_id=1, source_target_pairs={{0,16},{1,0},{2,18},{3,2},{4,20},{5,4},{6,22},{7,6},{8,9},{9,8},{1... | collective-permute-start | bytes 393224 | tf_op jit(solution)/shard_map/ppermute | solution.py:554
  27.7 1.5 %collective-permute-start.8 = (bf16[128,512]{1,0:T(8,128)(2,1)S(1)}, bf16[128,512]{1,0:T(8,128)(2,1)S(1)}, u32[]{:S(2)}, u32[]{:S(2)}) collective-permute-start(bf16[128,512]{1,0:T(8,128)(2,1)S(1)} %update.6), channel_id=1, source_target_pairs={{0,16},{1,0},{2,18},{3,2},{4,20},{5,4},{6,22},{7,6},{8,9},{9,8},{1... | collective-permute-start | bytes 393224 | tf_op jit(solution)/shard_map/ppermute | solution.py:554
  29.2 0.5 collective-permute-start.9
  29.7 0.1 copy-done.6
  29.8 0.4 prepare.1
  30.2 0.0 collective-permute-done.6.refs_0_.refs_1_
  30.3 0.0 collective-permute-done.7.refs_0_.refs_2_
  30.3 0.8 %collective-permute-done.8.refs_0_.refs_3_ = bf16[128,512]{1,0:T(8,128)(2,1)S(1)} collective-permute-done((bf16[128,512]{1,0:T(8,128)(2,1)S(1)}, bf16[128,512]{1,0:T(8,128)(2,1)S(1)}, u32[]{:S(2)}, u32[]{:S(2)}) %collective-permute-start.8) | collective-permute-done | bytes 131104 | tf_op jit(solution)/shard_map/ppermute | solution.py:554
  31.1 1.4 %collective-permute-done.9.refs_4_ = bf16[128,512]{1,0:T(8,128)(2,1)S(1)} collective-permute-done((bf16[128,512]{1,0:T(8,128)(2,1)S(1)}, bf16[128,512]{1,0:T(8,128)(2,1)S(1)}, u32[]{:S(2)}, u32[]{:S(2)}) %collective-permute-start.9) | collective-permute-done | bytes 131104 | tf_op jit(solution)/shard_map/ppermute | solution.py:554
  32.5 0.2 collective-permute-start.10
  32.7 10.9 %collective-permute-start.11 = (bf16[128,512]{1,0:T(8,128)(2,1)S(1)}, bf16[128,512]{1,0:T(8,128)(2,1)S(1)}, u32[]{:S(2)}, u32[]{:S(2)}) collective-permute-start(bf16[128,512]{1,0:T(8,128)(2,1)S(1)} %get-tuple-element.69), channel_id=1, source_target_pairs={{0,1},{1,0},{2,3},{3,2},{4,5},{5,4},{6,7},{7,17},{8,9},{9,8},{10,1... | collective-permute-start | bytes 393224 | tf_op jit(solution)/shard_map/ppermute | solution.py:554
  43.5 2.4 %collective-permute-start.12 = (bf16[128,512]{1,0:T(8,128)(2,1)S(1)}, bf16[128,512]{1,0:T(8,128)(2,1)S(1)}, u32[]{:S(2)}, u32[]{:S(2)}) collective-permute-start(bf16[128,512]{1,0:T(8,128)(2,1)S(1)} %get-tuple-element.71.refs_3_), channel_id=1, source_target_pairs={{0,1},{1,17},{2,3},{3,2},{4,5},{5,4},{6,7},{7,6},{8,9},{9,19},{10,... | collective-permute-start | bytes 393224 | tf_op jit(solution)/shard_map/ppermute | solution.py:554
  46.0 0.1 collective-permute-start.13
  46.0 0.0 collective-permute-done.10.refs_0_
  46.0 5.3 %collective-permute-done.11.refs_1_ = bf16[128,512]{1,0:T(8,128)(2,1)S(1)} collective-permute-done((bf16[128,512]{1,0:T(8,128)(2,1)S(1)}, bf16[128,512]{1,0:T(8,128)(2,1)S(1)}, u32[]{:S(2)}, u32[]{:S(2)}) %collective-permute-start.11) | collective-permute-done | bytes 131104 | tf_op jit(solution)/shard_map/ppermute | solution.py:554
  51.3 0.0 copy-start.5
  51.3 0.0 collective-permute-done.12.refs_1_
  51.4 0.0 collective-permute-done.13.refs_2_
  51.4 2.6 %collective-permute-start.14 = (bf16[64,512]{1,0:T(8,128)(2,1)S(1)}, bf16[64,512]{1,0:T(8,128)(2,1)S(1)}, u32[]{:S(2)}, u32[]{:S(2)}) collective-permute-start(bf16[64,512]{1,0:T(8,128)(2,1)S(1)} %get-tuple-element.74), channel_id=1, source_target_pairs={{0,1},{1,0},{2,3},{3,2},{4,5},{5,4},{6,7},{7,6},{8,9},{9,8},{10,11... | collective-permute-start | bytes 196616 | tf_op jit(solution)/shard_map/ppermute | solution.py:573
  54.0 0.9 %collective-permute-done.14.refs_5_ = bf16[64,512]{1,0:T(8,128)(2,1)S(1)} collective-permute-done((bf16[64,512]{1,0:T(8,128)(2,1)S(1)}, bf16[64,512]{1,0:T(8,128)(2,1)S(1)}, u32[]{:S(2)}, u32[]{:S(2)}) %collective-permute-start.14) | collective-permute-done | bytes 65568 | tf_op jit(solution)/shard_map/ppermute | solution.py:573
  54.9 1.2 %decode.1 = bf16[227,128]{1,0:T(8,128)(2,1)} custom-call(s32[1]{0:T(128)} %bitcast.segment, s32[1]{0:T(128)} %bitcast.1.place, f32[128,512]{1,0:T(8,128)S(1)} %get-tuple-element.59.refs_0_, bf16[64,128]{1,0:T(8,128)(2,1)S(1)} %get-tuple-element.60.refs_1_, bf16[1024,512]{1,0:T(8,128)(2,1)S(1)} %copy-done.1, bf16[227,512]{1,0:T(8,128)(2,1)S(1)} %bitcast.15, ...), custom_call_target="tpu_custom_call" | custom-call | bytes 1748744 | tf_op jit(solution)/shard_map/decode/pallas_call | solution.py:490
  (29 shorter events, 0.2 us)
Async XLA Ops:
  0.0 3.0 %copy-start.7 = (bf16[4,128,227]{1,0,2:T(4,128)(2,1)S(1)}, bf16[4,128,227]{1,0,2:T(4,128)(2,1)}, u32[]{:S(2)}) copy-start(bf16[4,128,227]{1,0,2:T(4,128)(2,1)} %param.12) | copy-start | bytes 697348
  0.0 13.3 %collective-permute-start.4 = (bf16[1,512,1024]{2,1,0:T(8,128)(2,1)}, bf16[1,512,1024]{2,1,0:T(8,128)(2,1)S(1)}, u32[]{:S(2)}, u32[]{:S(2)}) collective-permute-start(bf16[1,512,1024]{2,1,0:T(8,128)(2,1)} %w_project), channel_id=1, source_target_pairs={{0,1},{1,9},{2,3},{3,11},{4,5},{5,13},{6,7},{7,15},{8,0},{9,8},{10... | collective-permute-start | bytes 3145736 | tf_op jit(solution)/shard_map/ppermute | solution.py:554
  1.2 1.8 %copy-start.8 = (s32[64,8]{0,1:T(8,128)S(1)}, s32[64,8]{0,1:T(8,128)}, u32[]{:S(2)}) copy-start(s32[64,8]{0,1:T(8,128)} %param.21) | copy-start | bytes 6148
  1.2 1.8 %copy-start.9 = (s32[4,64]{1,0:T(4,128)S(1)}, s32[4,64]{1,0:T(4,128)}, u32[]{:S(2)}) copy-start(s32[4,64]{1,0:T(4,128)} %param.22) | copy-start | bytes 3076
  1.2 1.8 %copy-start.10 = (s32[4,1]{0,1:T(1,128)S(1)}, s32[4,1]{0,1:T(1,128)}, u32[]{:S(2)}) copy-start(s32[4,1]{0,1:T(1,128)} %param.23) | copy-start | bytes 52
  1.2 1.8 %copy-start.11 = (s32[128]{0:T(128)S(1)}, s32[128]{0:T(128)}, u32[]{:S(2)}) copy-start(s32[128]{0:T(128)} %param.19) | copy-start | bytes 1540
  1.2 1.9 %copy-start.4 = (bf16[227,512]{1,0:T(8,128)(2,1)S(1)}, bf16[227,512]{1,0:T(8,128)(2,1)}, u32[]{:S(2)}) copy-start(bf16[227,512]{1,0:T(8,128)(2,1)} %refs_1_.5) | copy-start | bytes 697348
  1.2 5.3 %copy-start = (bf16[1,1024,512]{2,1,0:T(8,128)(2,1)S(1)}, bf16[1,1024,512]{2,1,0:T(8,128)(2,1)}, u32[]{:S(2)}) copy-start(bf16[1,1024,512]{2,1,0:T(8,128)(2,1)} %refs_1_.4) | copy-start | bytes 3145732
  1.2 5.3 %copy-start.3 = (bf16[1,512,1024]{2,1,0:T(8,128)(2,1)S(1)}, bf16[1,512,1024]{2,1,0:T(8,128)(2,1)}, u32[]{:S(2)}) copy-start(bf16[1,512,1024]{2,1,0:T(8,128)(2,1)} %w_project) | copy-start | bytes 3145732
  2.3 4.2 %copy-start.2 = (bf16[1,512,512]{2,1,0:T(8,128)(2,1)S(1)}, bf16[1,512,512]{2,1,0:T(8,128)(2,1)}, u32[]{:S(2)}) copy-start(bf16[1,512,512]{2,1,0:T(8,128)(2,1)} %refs_0_.1) | copy-start | bytes 1572868
  2.3 22.2 %collective-permute-start.5 = (bf16[2,512,512]{2,1,0:T(8,128)(2,1)}, bf16[2,512,512]{2,1,0:T(8,128)(2,1)S(1)}, u32[]{:S(2)}, u32[]{:S(2)}) collective-permute-start(bf16[2,512,512]{2,1,0:T(8,128)(2,1)} %pack.1), channel_id=1, source_target_pairs={{0,1},{1,9},{2,3},{3,11},{4,5},{5,13},{6,7},{7,15},{8,0},{9,8},{10... | collective-permute-start | bytes 3145736 | tf_op jit(solution)/shard_map/ppermute | solution.py:554
  3.8 3.4 %collective-permute-start = (bf16[80,512]{1,0:T(8,128)(2,1)S(1)}, bf16[80,512]{1,0:T(8,128)(2,1)S(1)}, u32[]{:S(2)}, u32[]{:S(2)}) collective-permute-start(bf16[80,512]{1,0:T(8,128)(2,1)S(1)} %get-tuple-element.48), channel_id=1, source_target_pairs={{0,2},{1,3},{2,0},{3,1},{4,6},{5,7},{6,4},{7,5},{8,9},{9,8},{10,11... | collective-permute-start | bytes 245768 | tf_op jit(solution)/shard_map/ppermute | solution.py:569
  3.9 3.4 %collective-permute-start.1 = (bf16[80,512]{1,0:T(8,128)(2,1)S(1)}, bf16[80,512]{1,0:T(8,128)(2,1)S(1)}, u32[]{:S(2)}, u32[]{:S(2)}) collective-permute-start(bf16[80,512]{1,0:T(8,128)(2,1)S(1)} %get-tuple-element.49), channel_id=1, source_target_pairs={{0,4},{1,5},{2,6},{3,7},{4,0},{5,1},{6,2},{7,3},{8,9},{9,8},{10,11... | collective-permute-start | bytes 245768 | tf_op jit(solution)/shard_map/ppermute | solution.py:569
  4.4 4.8 %collective-permute-start.2 = (bf16[80,512]{1,0:T(8,128)(2,1)S(1)}, bf16[80,512]{1,0:T(8,128)(2,1)S(1)}, u32[]{:S(2)}, u32[]{:S(2)}) collective-permute-start(bf16[80,512]{1,0:T(8,128)(2,1)S(1)} %get-tuple-element.50), channel_id=1, source_target_pairs={{0,16},{1,17},{2,18},{3,19},{4,20},{5,21},{6,22},{7,23},{8,9},{9,8... | collective-permute-start | bytes 245768 | tf_op jit(solution)/shard_map/ppermute | solution.py:569
  9.2 3.1 %collective-permute-start.3 = (bf16[320,512]{1,0:T(8,128)(2,1)S(1)}, bf16[320,512]{1,0:T(8,128)(2,1)S(1)}, u32[]{:S(2)}, u32[]{:S(2)}) collective-permute-start(bf16[320,512]{1,0:T(8,128)(2,1)S(1)} %join.1.refs_0_), channel_id=1, source_target_pairs={{0,1},{1,0},{2,3},{3,2},{4,5},{5,4},{6,7},{7,6},{8,9},{9,8},{10,11... | collective-permute-start | bytes 983048 | tf_op jit(solution)/shard_map/ppermute | solution.py:573
  24.5 5.7 %collective-permute-start.6 = (bf16[144,512]{1,0:T(8,128)(2,1)S(1)}, bf16[144,512]{1,0:T(8,128)(2,1)S(1)}, u32[]{:S(2)}, u32[]{:S(2)}) collective-permute-start(bf16[144,512]{1,0:T(8,128)(2,1)S(1)} %update.4), channel_id=1, source_target_pairs={{0,16},{1,0},{2,18},{3,2},{4,20},{5,4},{6,22},{7,6},{8,9},{9,8},{1... | collective-permute-start | bytes 442376 | tf_op jit(solution)/shard_map/ppermute | solution.py:554
  24.7 5.5 %collective-permute-start.7 = (bf16[128,512]{1,0:T(8,128)(2,1)S(1)}, bf16[128,512]{1,0:T(8,128)(2,1)S(1)}, u32[]{:S(2)}, u32[]{:S(2)}) collective-permute-start(bf16[128,512]{1,0:T(8,128)(2,1)S(1)} %update.5), channel_id=1, source_target_pairs={{0,16},{1,0},{2,18},{3,2},{4,20},{5,4},{6,22},{7,6},{8,9},{9,8},{1... | collective-permute-start | bytes 393224 | tf_op jit(solution)/shard_map/ppermute | solution.py:554
  27.7 2.1 %copy-start.1 = (bf16[1024,512]{1,0:T(8,128)(2,1)S(1)}, bf16[1024,512]{1,0:T(8,128)(2,1)}, u32[]{:S(2)}) copy-start(bf16[1024,512]{1,0:T(8,128)(2,1)} %refs_2_.3) | copy-start | bytes 3145732
  27.7 3.5 %collective-permute-start.8 = (bf16[128,512]{1,0:T(8,128)(2,1)S(1)}, bf16[128,512]{1,0:T(8,128)(2,1)S(1)}, u32[]{:S(2)}, u32[]{:S(2)}) collective-permute-start(bf16[128,512]{1,0:T(8,128)(2,1)S(1)} %update.6), channel_id=1, source_target_pairs={{0,16},{1,0},{2,18},{3,2},{4,20},{5,4},{6,22},{7,6},{8,9},{9,8},{1... | collective-permute-start | bytes 393224 | tf_op jit(solution)/shard_map/ppermute | solution.py:554
  29.2 0.7 %copy-start.6 = (s32[128]{0:T(128)S(1)}, s32[128]{0:T(128)}, u32[]{:S(2)}) copy-start(s32[128]{0:T(128)} %param.20) | copy-start | bytes 1540
  29.2 3.3 %collective-permute-start.9 = (bf16[128,512]{1,0:T(8,128)(2,1)S(1)}, bf16[128,512]{1,0:T(8,128)(2,1)S(1)}, u32[]{:S(2)}, u32[]{:S(2)}) collective-permute-start(bf16[128,512]{1,0:T(8,128)(2,1)S(1)} %update.7), channel_id=1, source_target_pairs={{0,16},{1,0},{2,18},{3,2},{4,20},{5,4},{6,22},{7,6},{8,9},{9,8},{1... | collective-permute-start | bytes 393224 | tf_op jit(solution)/shard_map/ppermute | solution.py:554
  32.5 13.5 %collective-permute-start.10 = (bf16[128,512]{1,0:T(8,128)(2,1)S(1)}, bf16[128,512]{1,0:T(8,128)(2,1)S(1)}, u32[]{:S(2)}, u32[]{:S(2)}) collective-permute-start(bf16[128,512]{1,0:T(8,128)(2,1)S(1)} %get-tuple-element.68), channel_id=1, source_target_pairs={{0,1},{1,0},{2,3},{3,2},{4,5},{5,21},{6,7},{7,6},{8,9},{9,8},{10,1... | collective-permute-start | bytes 393224 | tf_op jit(solution)/shard_map/ppermute | solution.py:554
  32.7 18.7 %collective-permute-start.11 = (bf16[128,512]{1,0:T(8,128)(2,1)S(1)}, bf16[128,512]{1,0:T(8,128)(2,1)S(1)}, u32[]{:S(2)}, u32[]{:S(2)}) collective-permute-start(bf16[128,512]{1,0:T(8,128)(2,1)S(1)} %get-tuple-element.69), channel_id=1, source_target_pairs={{0,1},{1,0},{2,3},{3,2},{4,5},{5,4},{6,7},{7,17},{8,9},{9,8},{10,1... | collective-permute-start | bytes 393224 | tf_op jit(solution)/shard_map/ppermute | solution.py:554
  43.5 7.8 %collective-permute-start.12 = (bf16[128,512]{1,0:T(8,128)(2,1)S(1)}, bf16[128,512]{1,0:T(8,128)(2,1)S(1)}, u32[]{:S(2)}, u32[]{:S(2)}) collective-permute-start(bf16[128,512]{1,0:T(8,128)(2,1)S(1)} %get-tuple-element.71.refs_3_), channel_id=1, source_target_pairs={{0,1},{1,17},{2,3},{3,2},{4,5},{5,4},{6,7},{7,6},{8,9},{9,19},{10,... | collective-permute-start | bytes 393224 | tf_op jit(solution)/shard_map/ppermute | solution.py:554
  46.0 5.4 %collective-permute-start.13 = (bf16[128,512]{1,0:T(8,128)(2,1)S(1)}, bf16[128,512]{1,0:T(8,128)(2,1)S(1)}, u32[]{:S(2)}, u32[]{:S(2)}) collective-permute-start(bf16[128,512]{1,0:T(8,128)(2,1)S(1)} %get-tuple-element.72.refs_4_), channel_id=1, source_target_pairs={{0,1},{1,0},{2,3},{3,17},{4,5},{5,4},{6,7},{7,6},{8,9},{9,8},{10,1... | collective-permute-start | bytes 393224 | tf_op jit(solution)/shard_map/ppermute | solution.py:554
  51.3 3.6 %copy-start.5 = (bf16[512,227]{0,1:T(8,128)(2,1)S(1)}, bf16[512,227]{0,1:T(8,128)(2,1)}, u32[]{:S(2)}) copy-start(bf16[512,227]{0,1:T(8,128)(2,1)} %param.18) | copy-start | bytes 697348
  51.4 3.5 %collective-permute-start.14 = (bf16[64,512]{1,0:T(8,128)(2,1)S(1)}, bf16[64,512]{1,0:T(8,128)(2,1)S(1)}, u32[]{:S(2)}, u32[]{:S(2)}) collective-permute-start(bf16[64,512]{1,0:T(8,128)(2,1)S(1)} %get-tuple-element.74), channel_id=1, source_target_pairs={{0,1},{1,0},{2,3},{3,2},{4,5},{5,4},{6,7},{7,6},{8,9},{9,8},{10,11... | collective-permute-start | bytes 196616 | tf_op jit(solution)/shard_map/ppermute | solution.py:573

commit v15 on v14

--- a/solution.py
+++ b/solution.py
@@ -271,21 +271,15 @@
         columns_out[...] = columns_of(names.astype(jnp.float32))
 
 
-def pack_kernel(group, where, w_message, w_update, pair, message, update, semaphores):
-    width = message.shape[0]
-
-    @pl.when(jnp.logical_and(lax.rem(where[0], 2) == 1, lax.rem(where[1], group) == 0))
-    def _():
-        sources = [w_message.at[0], w_update.at[0, width:], w_update.at[0, :width]]
-        copies = fetch(sources, [message, update, pair.at[0]], semaphores)
-        copies[0].wait()
-        copies[1].wait()
-        pair[1] = matmul(message[...], update[...]).astype(jnp.bfloat16)
-        copies[2].wait()
-
-
-def hold_kernel(w_project, w_message, w_update, receive, send, pair, message, update, semaphores):
-    width = receive.shape[0]
+def pack_kernel(group, at_segment, where, *refs):
+    @pl.when(owns(where, group, at_segment))
+    def _():
+        for place, block in enumerate(refs[:-1]):
+            refs[-1][place] = block[...]
+
+
+def hold_kernel(w_project, w_message, w_update, receive, send, own, edges, message, update, semaphores):
+    width = own.shape[0]
     sources = [
         w_message.at[0],
         w_update.at[0, width:],
@@ -293,10 +287,10 @@
         w_project.at[0, :, width:],
         w_update.at[0, :width],
     ]
-    copies = fetch(sources, [message, update, receive, send, pair.at[0]], semaphores)
+    copies = fetch(sources, [message, update, receive, send, own], semaphores)
     copies[0].wait()
     copies[1].wait()
-    pair[1] = matmul(message[...], update[...]).astype(jnp.bfloat16)
+    edges[...] = matmul(message[...], update[...]).astype(jnp.bfloat16)
     for copy in copies[2:]:
         copy.wait()
 
@@ -337,7 +331,7 @@
 def layer_kernel(group, at_segment, fanout, rows, where, columns, *refs):
     parts = len(rows)
     state, senders, refs = refs[:parts], refs[parts : 2 * parts - 1], refs[2 * parts - 1 :]
-    (w_receive, w_send, pair), (renewed, whole, sender) = refs[:3], refs[3:]
+    (w_receive, w_send, w_own, w_edges), (renewed, whole, sender) = refs[:4], refs[4:]
     nodes = renewed.shape[0]
     chunk = min(nodes, 256)
 
@@ -355,53 +349,64 @@
         for start in range(0, nodes, chunk):
             span = slice(start, start + chunk)
             gathered = sum_edges(fanout, columns[span, :], sender[...], whole[span, :], w_receive[...])
-            renewed[span, :] = update_nodes(whole[span, :], gathered, pair[0], pair[1])
-
-
-def edges_kernel(group, at_segment, fanout, where, columns, state, w_project, gathered, sender):
-    nodes, width = state.shape
-    chunk = min(nodes, 256)
+            renewed[span, :] = update_nodes(whole[span, :], gathered, w_own[...], w_edges[...])
+
+
+def open_kernel(group, at_segment, fanout, rows, where, columns, *refs):
+    parts = len(rows)
+    state, senders, refs = refs[:parts], refs[parts : 2 * parts - 1], refs[2 * parts - 1 :]
+    codes, (w_receive, w_send, w_own, w_edges), (sender, whole, piece) = refs[:-7], refs[-7:-3], refs[-3:]
 
     @pl.when(owns(where, group, at_segment))
     def _():
-        sender[...] = matmul(state[...], w_project[0, :, width:]).astype(jnp.bfloat16)
-        for start in range(0, nodes, chunk):
-            span = slice(start, start + chunk)
-            gathered[span, :] = sum_edges(
-                fanout, columns[span, :], sender[...], state[span, :], w_project[0, :, :width]
-            )
-
-
-def update_kernel(group, at_segment, start, where, gathered, state, codes, pair, piece):
-    rows = piece.shape[0] - (codes.shape[0] if start == 0 else 0)
+        start = 0
+        for part, count in zip(state, rows):
+            whole[start : start + count, :] = part[:count, :]
+            start += count
+        start = 0
+        for part in senders:
+            sender[start : start + part.shape[0], :] = part[...]
+            start += part.shape[0]
+        sender[start:, :] = matmul(whole[start:, :], w_send[...]).astype(jnp.bfloat16)
+        below = codes[0][...] if codes else state[0][rows[0] :, :]
+        count = piece.shape[0] - below.shape[0]
+        own = whole[:count, :]
+        gathered = sum_edges(fanout, columns[:count, :], sender[...], own, w_receive[...])
+        piece[:count, :] = update_nodes(own, gathered, w_own[...], w_edges[...])
+        piece[count:, :] = below
+
+
+def next_kernel(group, at_segment, fanout, start, where, columns, sender, whole, *refs):
+    w_receive, _, w_own, w_edges, piece = refs
+    span = slice(start, start + piece.shape[0])
 
     @pl.when(owns(where, group, at_segment))
     def _():
-        span = slice(start, start + rows)
-        piece[:rows, :] = update_nodes(state[span, :], gathered[span, :], pair[0], pair[1])
-        if start == 0:
-            piece[rows:, :] = codes[...]
-
-
-def half_kernel(group, at_segment, chips, far, fanout, where, columns, state, *refs):
-    senders, refs = (refs[:0], refs) if far else (refs[:1], refs[1:])
+        own = whole[span, :]
+        gathered = sum_edges(fanout, columns[span, :], sender[...], own, w_receive[...])
+        piece[...] = update_nodes(own, gathered, w_own[...], w_edges[...])
+
+
+def end_kernel(group, at_segment, chips, far, begin, first, fanout, where, columns, state, *refs):
+    senders, refs = (refs[:0], refs) if first else (refs[:1], refs[1:])
     (w_project, pair), outs = refs[:2], refs[2:]
-    nodes, width = state.shape
-    half = nodes // 2
+    width = state.shape[1]
+    half = state.shape[0] // 2
     chip, _ = place_of(where, group)
 
     @pl.when(owns(where, group, at_segment))
     def _():
         pieces = outs
-        if far:
+        if first:
             outs[0][...] = matmul(state[...], w_project[0, :, width:]).astype(jnp.bfloat16)
             pieces = outs[1:]
-        sender = outs[0] if far else senders[0]
+        sender = outs[0] if first else senders[0]
+        rows = sum(piece.shape[0] for piece in pieces)
         upper = (chip < chips // 2) if far else (chip >= chips // 2)
-        start = pl.multiple_of(jnp.where(upper, half, 0), half)
-        own = state[pl.ds(start, half), :]
+        start = pl.multiple_of(jnp.where(upper, half, 0) + begin, rows)
+        own = state[pl.ds(start, rows), :]
         gathered = sum_edges(
-            fanout, columns[pl.ds(start, half), :], sender[...], own, w_project[0, :, :width]
+            fanout, columns[pl.ds(start, rows), :], sender[...], own, w_project[0, :, :width]
         )
         write_pieces(pieces, update_nodes(own, gathered, pair[0], pair[1]))
 
@@ -420,14 +425,19 @@
     return crosses, jnp.logical_and(segment == last, chip == last), lax.rem(chip, each)
 
 
-def far_kernel(group, chips, last, where, *refs):
-    far, out = refs[:-1], refs[-1]
+def far_kernel(group, chips, last, number, where, *refs):
+    block, out = refs[0], refs[-1]
     crosses, _, spot = arrival(where, group, chips, last)
-    for number, block in enumerate(far):
-
-        @pl.when(jnp.logical_and(crosses, spot == number))
-        def _(block=block):
-            out[...] = block[...]
+
+    @pl.when(jnp.logical_and(crosses, spot == number))
+    def _():
+        out[...] = block[...]
+
+    if number:
+
+        @pl.when(jnp.logical_and(crosses, spot < number))
+        def _():
+            out[...] = refs[1][...]
 
 
 def near_kernel(group, chips, last, where, crossed, *refs):
@@ -554,7 +564,7 @@
         return lax.ppermute(value, ("segment", "dom"), every_device(pairs, segments * parts, group))
 
     def to_chip(value, steps):
-        giver = last if steps == samples - 1 else 0
+        giver = steps - 1
         pairs = []
         for at in range(segments):
             for dom in range(parts):
@@ -581,17 +591,8 @@
     where = (own_segment, own_place)
     weights = [w_project, w_message, w_update]
     last = segments - 2
-    pairs = [(owner(m, at + 1), owner(m, at)) for m in range(samples) for at in range(0, segments, 2)]
-    (pair,) = call(
-        functools.partial(pack_kernel, group),
-        "pack",
-        [jax.ShapeDtypeStruct((2, width, width), bf16)],
-        [where, w_message, w_update],
-        "whh",
-        [pltpu.VMEM((width, width), bf16)] * 2 + [pltpu.SemaphoreType.DMA((3,))],
-        room=60,
-    )
-    came = [send(w_project, pairs), send(pair, pairs)]
+    to_last = [(owner(m, last + 1), owner(m, last)) for m in range(samples)]
+    came_project = send(w_project, to_last)
     snapshots = jnp.transpose(grid_state, (0, 2, 1))
     lists = send_rows.shape[0]
 
@@ -618,7 +619,7 @@
     held = call(
         hold_kernel,
         "hold",
-        [jax.ShapeDtypeStruct((width, width), bf16)] * 2 + [jax.ShapeDtypeStruct((2, width, width), bf16)],
+        [jax.ShapeDtypeStruct((width, width), bf16)] * 4,
         weights,
         "hhh",
         [pltpu.VMEM((width, width), bf16)] * 2 + [pltpu.SemaphoreType.DMA((5,))],
@@ -646,74 +647,81 @@
         "w" + "v" * group,
         [pltpu.VMEM((fanout, nodes), jnp.int32)],
     )
-    both = [pltpu.VMEM((nodes, width), bf16)] * 2
+    columns, came_project, *held = lax.optimization_barrier((columns, came_project, *held))
+    (pair,) = call(
+        functools.partial(pack_kernel, group, last + 1),
+        "pack",
+        [jax.ShapeDtypeStruct((2, width, width), bf16)],
+        [where] + held[2:],
+        "wvv",
+    )
+    came = [came_project, send(pair, to_last)]
+    pieces, senders, rows, extra = [state], [], (nodes,), [codes]
+    for layer in range(last):
+        pairs = [(owner(m, layer), owner(m, layer + 1)) for m in range(samples)]
+        sender, joined_state, piece = call(
+            functools.partial(open_kernel, group, layer, fanout, rows),
+            "open",
+            [whole, whole, tall],
+            [where, columns] + pieces + senders + extra + held,
+            "w" + "v" * (1 + len(pieces + senders + extra + held)),
+        )
+        sent = [send(piece, pairs)]
+        for start in range(share, nodes, share):
+            (piece,) = call(
+                functools.partial(next_kernel, group, layer, fanout, start),
+                "next",
+                [short],
+                [where, columns, sender, joined_state] + held,
+                "w" + "v" * (3 + len(held)),
+            )
+            sent.append(send(piece, pairs))
+        pieces, senders, rows, extra = sent, [], (share,) * samples, []
+        if layer == 0:
+            ready, table = call(
+                prepare_kernel,
+                "prepare",
+                [
+                    jax.ShapeDtypeStruct((grid_rows, width), jnp.float32),
+                    jax.ShapeDtypeStruct((mesh_rows, grid_rows), bf16),
+                ],
+                [where, snapshots, w_embed, w_decode, mesh_grid.reshape(1, grid_rows)],
+                "wvvvv",
+            )
+            pieces[0], ready, table = lax.optimization_barrier((pieces[0], ready, table))
+        for piece in pieces[:-1]:
+            if senders:
+                piece, senders[-1] = lax.optimization_barrier((piece, senders[-1]))
+            sender, *found = call(
+                functools.partial(sender_kernel, group, layer + 1, fanout, share),
+                "sender",
+                [short] + [columns_shape] * (not senders),
+                [where, piece, held[1]],
+                "wvv",
+            )
+            columns = found[0] if found else columns
+            senders.append(sender)
     (state,) = call(
-        functools.partial(layer_kernel, group, 0, fanout, (nodes,)),
+        functools.partial(layer_kernel, group, last, fanout, rows),
         "layer",
         [whole],
-        [where, columns, state] + list(held),
-        "w" + "v" * 5,
-        both,
-    )
-    (gathered,) = call(
-        functools.partial(edges_kernel, group, 0, fanout),
-        "edges",
-        [whole],
-        [where, columns, state, came[0]],
-        "wvvv",
-        both[:1],
-    )
-    pairs = [(owner(m, 0), owner(m, last)) for m in range(samples)]
-    pieces, senders = [], []
-    for start in range(0, nodes, share):
-        (piece,) = call(
-            functools.partial(update_kernel, group, 0, start),
-            "update",
-            [short if start else tall],
-            [where, gathered, state, codes, came[1]],
-            "wvvvv",
-        )
-        pieces.append(send(piece, pairs))
-    ready, table = call(
-        prepare_kernel,
-        "prepare",
-        [
-            jax.ShapeDtypeStruct((grid_rows, width), jnp.float32),
-            jax.ShapeDtypeStruct((mesh_rows, grid_rows), bf16),
-        ],
-        [where, snapshots, w_embed, w_decode, mesh_grid.reshape(1, grid_rows)],
-        "wvvvv",
-    )
-    pieces[0], ready, table = lax.optimization_barrier((pieces[0], ready, table))
-    for piece in pieces[:-1]:
-        if senders:
-            piece, senders[-1] = lax.optimization_barrier((piece, senders[-1]))
-        sender, *found = call(
-            functools.partial(sender_kernel, group, last, fanout, share),
-            "sender",
-            [short] + [columns_shape] * (not senders),
-            [where, piece, held[1]],
-            "wvv",
-        )
-        columns = found[0] if found else columns
-        senders.append(sender)
-    (state,) = call(
-        functools.partial(layer_kernel, group, last, fanout, (share,) * samples),
-        "layer",
-        [whole],
-        [where, columns] + pieces + senders + list(held),
-        "w" + "v" * (2 * samples + 3),
-        both,
-    )
-    sender, *far = call(
-        functools.partial(half_kernel, group, last, samples, True, fanout),
-        "far_half",
-        [whole] + [short] * (samples // 2),
-        [where, columns, state] + came,
-        "wvvvv",
-    )
+        [where, columns] + pieces + senders + held,
+        "w" + "v" * (1 + len(pieces + senders + held)),
+        [pltpu.VMEM((nodes, width), bf16)] * 2,
+    )
+    far = []
+    for begin in range(0, nodes // 2, share):
+        found = call(
+            functools.partial(end_kernel, group, last, samples, True, begin, not far, fanout),
+            "far_part",
+            [whole] * (not far) + [short],
+            [where, columns, state] + ([sender] if far else []) + came,
+            "w" + "v" * (5 if far else 4),
+        )
+        sender = found[0] if not far else sender
+        far.append(found[-1])
     near = call(
-        functools.partial(half_kernel, group, last, samples, False, fanout),
+        functools.partial(end_kernel, group, last, samples, False, 0, False, fanout),
         "near_half",
         [short] * (samples // 2),
         [where, columns, state, sender] + came,
@@ -728,18 +736,20 @@
                 (owner(m, last), device(m, ((m // each ^ far) * each + turn) * group)) for m in range(samples)
             ]
             arrived.append(send(block, [pair for pair in pairs if pair[0] != pair[1]]))
-    (crossed,) = call(
-        functools.partial(far_kernel, group, samples, last),
-        "far",
-        [jax.ShapeDtypeStruct((share, width), bf16)],
-        [where] + arrived[:each],
-        "w" + "v" * each,
-    )
+    crossed = []
+    for number, block in enumerate(arrived[:each]):
+        crossed = call(
+            functools.partial(far_kernel, group, samples, last, number),
+            "far",
+            [short],
+            [where, block] + list(crossed),
+            "wv" + "v" * len(crossed),
+        )
     parts_of_block = call(
         functools.partial(near_kernel, group, samples, last),
         "near",
         [jax.ShapeDtypeStruct((mesh_rows, width), bf16)] * group,
-        [where, crossed] + arrived[each:] + state[each:],
+        [where, crossed[0]] + arrived[each:] + state[each:],
         "w" + "v" * (1 + 2 * each),
     )
     handed = [parts_of_block[0]]

time: 56.3 us -> 56.7 us (level)
  the two profiles are of different devices: /device:TPU:13 before, /device:TPU:3 now
where the time goes in v15:
time: 56.7 us; the launch traced here: 56.5 us
  starting transfers between devices  39.1 us (69%)
  waiting for transfers between devices  10.5 us (19%)
  local copies, waits for them, and re-layouts  3.46 us (6%)
  Pallas kernels  3.2 us (6%)
    ppermute x14, starting transfers between devices, send(): lax.ppermute(value, ('segment', 'dom'), every_device(pairs, segments * pa...  26.8 us
    ppermute x14, waiting for transfers between devices, send(): lax.ppermute(value, ('segment', 'dom'), every_device(pairs, segments * pa...  7.99 us
    ppermute x2, starting transfers between devices, change_lane(): return lax.ppermute(value, 'dom', pairs)  7.89 us
    ppermute x3, starting transfers between devices, to_chip(): return lax.ppermute(value, ('segment', 'dom'), pairs)  4.36 us
    unnamed x23, local copies, waits for them, and re-layouts  3.46 us
    pallas_call x28, Pallas kernels, call(): pl.pallas_call(located if places[0] == 'w' else kernel, out_shape=shapes,...  3.2 us
    ppermute x2, waiting for transfers between devices, change_lane(): return lax.ppermute(value, 'dom', pairs)  2.52 us
  transfers between devices with their start and end apart: 19, of which 8 were waited for; matrix products, arithmetic and copies ran while one was open for 2% of the time, Pallas kernels for 3%

profile of v15, /device:TPU:3, one launch (start us, length us, event | category | flops | bytes accessed | tf_op | source)
XLA Modules:
  0.0 56.5 jit_solution(5781594838154165593)
XLA Ops:
  0.0 0.0 copy-start.10
  0.0 0.0 copy-start.3
  0.0 0.7 %collective-permute-start.4 = (bf16[1,512,1024]{2,1,0:T(8,128)(2,1)}, bf16[1,512,1024]{2,1,0:T(8,128)(2,1)S(1)}, u32[]{:S(2)}, u32[]{:S(2)}) collective-permute-start(bf16[1,512,1024]{2,1,0:T(8,128)(2,1)} %w_project), channel_id=1, source_target_pairs={{0,1},{1,0},{2,3},{3,2},{4,5},{5,4},{6,7},{7,6},{8,9},{9,8},{10,11... | collective-permute-start | bytes 3145736 | tf_op jit(solution)/shard_map/ppermute | solution.py:564
  0.8 1.0 %copy.15 = bf16[4,128,227]{1,2,0:T(8,128)(2,1)S(1)} copy(bf16[4,128,227]{1,0,2:T(4,128)(2,1)} %param.12) | data formatting | bytes 464896 | tf_op args[0]
  1.8 0.7 %encode.1 = (bf16[80,512]{1,0:T(8,128)(2,1)S(1)}, bf16[80,512]{1,0:T(8,128)(2,1)S(1)}, bf16[80,512]{1,0:T(8,128)(2,1)S(1)}, bf16[80,512]{1,0:T(8,128)(2,1)S(1)}) custom-call(s32[1]{0:T(128)} %bitcast.segment, s32[1]{0:T(128)} %bitcast.1.place, bf16[4,227,128]{2,1,0:T(8,128)(2,1)S(1)} %bitcast.13, bf16[227,512]{1,0:T(8,128)(2,1)S(1)} %copy-done.3, ...), custom_call_target="tpu_custom_call" | custom-call | bytes 799752 | tf_op jit(solution)/shard_map/encode/pallas_call | solution.py:500
  2.5 0.2 collective-permute-start
  2.7 3.4 %collective-permute-start.1 = (bf16[80,512]{1,0:T(8,128)(2,1)S(1)}, bf16[80,512]{1,0:T(8,128)(2,1)S(1)}, u32[]{:S(2)}, u32[]{:S(2)}) collective-permute-start(bf16[80,512]{1,0:T(8,128)(2,1)S(1)} %get-tuple-element.69), channel_id=1, source_target_pairs={{0,8},{1,9},{2,10},{3,11},{4,12},{5,13},{6,14},{7,15},{8,4},{9,5},... | collective-permute-start | bytes 245768 | tf_op jit(solution)/shard_map/ppermute | solution.py:579
  6.2 0.7 %collective-permute-start.2 = (bf16[80,512]{1,0:T(8,128)(2,1)S(1)}, bf16[80,512]{1,0:T(8,128)(2,1)S(1)}, u32[]{:S(2)}, u32[]{:S(2)}) collective-permute-start(bf16[80,512]{1,0:T(8,128)(2,1)S(1)} %get-tuple-element.70), channel_id=1, source_target_pairs={{0,16},{1,17},{2,18},{3,19},{4,20},{5,21},{6,22},{7,23},{8,9},{9,8... | collective-permute-start | bytes 245768 | tf_op jit(solution)/shard_map/ppermute | solution.py:579
  6.9 1.2 %copy-done.1 = bf16[1,1024,512]{2,1,0:T(8,128)(2,1)S(1)} copy-done((bf16[1,1024,512]{2,1,0:T(8,128)(2,1)S(1)}, bf16[1,1024,512]{2,1,0:T(8,128)(2,1)}, u32[]{:S(2)}) %copy-start.1) | copy-done | bytes 1048600
  8.1 1.2 %copy-done.2 = bf16[1,512,1024]{2,1,0:T(8,128)(2,1)S(1)} copy-done((bf16[1,512,1024]{2,1,0:T(8,128)(2,1)S(1)}, bf16[1,512,1024]{2,1,0:T(8,128)(2,1)}, u32[]{:S(2)}) %copy-start.2) | copy-done | bytes 1048600
  9.3 0.7 %hold.1 = (bf16[512,512]{1,0:T(8,128)(2,1)S(1)}, bf16[512,512]{1,0:T(8,128)(2,1)S(1)}, bf16[512,512]{1,0:T(8,128)(2,1)S(1)}, bf16[512,512]{1,0:T(8,128)(2,1)S(1)}) custom-call(bf16[1,512,1024]{2,1,0:T(8,128)(2,1)S(1)} %copy-done.2, bf16[1,512,512]{2,1,0:T(8,128)(2,1)S(1)} %copy-done.4, bf16[1,1024,512]{2,1,0:T(8,128)(2,1)S(1)} %copy-done.1), custom_call_target="tpu_custom_call" | custom-call | bytes 4718592 | tf_op jit(solution)/shard_map/hold/pallas_call | solution.py:500
  10.1 0.0 collective-permute-done.refs_1_
  10.1 0.0 collective-permute-done.1.refs_2_
  10.1 0.0 collective-permute-done.2.refs_3_
  10.2 0.1 collective-permute-start.3
  10.2 1.6 %collective-permute-done.3.refs_1_ = bf16[320,512]{1,0:T(8,128)(2,1)S(1)} collective-permute-done((bf16[320,512]{1,0:T(8,128)(2,1)S(1)}, bf16[320,512]{1,0:T(8,128)(2,1)S(1)}, u32[]{:S(2)}, u32[]{:S(2)}) %collective-permute-start.3) | collective-permute-done | bytes 327712 | tf_op jit(solution)/shard_map/ppermute | solution.py:583
  11.9 0.0 collective-permute-done.4.refs_2_.refs_3_
  11.9 0.1 collective-permute-start.13
  12.0 2.5 %collective-permute-start.5 = (bf16[144,512]{1,0:T(8,128)(2,1)S(1)}, bf16[144,512]{1,0:T(8,128)(2,1)S(1)}, u32[]{:S(2)}, u32[]{:S(2)}) collective-permute-start(bf16[144,512]{1,0:T(8,128)(2,1)S(1)} %get-tuple-element.83), channel_id=1, source_target_pairs={{0,8},{1,0},{2,10},{3,2},{4,12},{5,4},{6,14},{7,6},{8,9},{9,1},{10... | collective-permute-start | bytes 442376 | tf_op jit(solution)/shard_map/ppermute | solution.py:564
  14.5 1.7 %collective-permute-start.6 = (bf16[128,512]{1,0:T(8,128)(2,1)S(1)}, bf16[128,512]{1,0:T(8,128)(2,1)S(1)}, u32[]{:S(2)}, u32[]{:S(2)}) collective-permute-start(bf16[128,512]{1,0:T(8,128)(2,1)S(1)} %next.6), channel_id=1, source_target_pairs={{0,8},{1,0},{2,10},{3,2},{4,12},{5,4},{6,14},{7,6},{8,9},{9,1},{10... | collective-permute-start | bytes 393224 | tf_op jit(solution)/shard_map/ppermute | solution.py:564
  16.2 1.5 %collective-permute-start.7 = (bf16[128,512]{1,0:T(8,128)(2,1)S(1)}, bf16[128,512]{1,0:T(8,128)(2,1)S(1)}, u32[]{:S(2)}, u32[]{:S(2)}) collective-permute-start(bf16[128,512]{1,0:T(8,128)(2,1)S(1)} %next.7), channel_id=1, source_target_pairs={{0,8},{1,0},{2,10},{3,2},{4,12},{5,4},{6,14},{7,6},{8,9},{9,1},{10... | collective-permute-start | bytes 393224 | tf_op jit(solution)/shard_map/ppermute | solution.py:564
  17.7 1.5 %collective-permute-start.8 = (bf16[128,512]{1,0:T(8,128)(2,1)S(1)}, bf16[128,512]{1,0:T(8,128)(2,1)S(1)}, u32[]{:S(2)}, u32[]{:S(2)}) collective-permute-start(bf16[128,512]{1,0:T(8,128)(2,1)S(1)} %next.8), channel_id=1, source_target_pairs={{0,8},{1,0},{2,10},{3,2},{4,12},{5,4},{6,14},{7,6},{8,9},{9,1},{10... | collective-permute-start | bytes 393224 | tf_op jit(solution)/shard_map/ppermute | solution.py:564
  19.2 0.4 prepare.1
  19.6 0.0 collective-permute-done.5.refs_0_.refs_1_
  19.6 0.0 collective-permute-done.6.refs_0_.refs_2_
  19.7 0.0 collective-permute-done.7.refs_0_.refs_3_
  19.7 1.4 %collective-permute-done.8.refs_4_ = bf16[128,512]{1,0:T(8,128)(2,1)S(1)} collective-permute-done((bf16[128,512]{1,0:T(8,128)(2,1)S(1)}, bf16[128,512]{1,0:T(8,128)(2,1)S(1)}, u32[]{:S(2)}, u32[]{:S(2)}) %collective-permute-start.8) | collective-permute-done | bytes 131104 | tf_op jit(solution)/shard_map/ppermute | solution.py:564
  21.1 4.3 %collective-permute-start.9 = (bf16[144,512]{1,0:T(8,128)(2,1)S(1)}, bf16[144,512]{1,0:T(8,128)(2,1)S(1)}, u32[]{:S(2)}, u32[]{:S(2)}) collective-permute-start(bf16[144,512]{1,0:T(8,128)(2,1)S(1)} %get-tuple-element.97), channel_id=1, source_target_pairs={{0,1},{1,0},{2,3},{3,2},{4,5},{5,4},{6,7},{7,6},{8,16},{9,8},{10,1... | collective-permute-start | bytes 442376 | tf_op jit(solution)/shard_map/ppermute | solution.py:564
  25.4 1.5 %collective-permute-start.10 = (bf16[128,512]{1,0:T(8,128)(2,1)S(1)}, bf16[128,512]{1,0:T(8,128)(2,1)S(1)}, u32[]{:S(2)}, u32[]{:S(2)}) collective-permute-start(bf16[128,512]{1,0:T(8,128)(2,1)S(1)} %next.9), channel_id=1, source_target_pairs={{0,1},{1,0},{2,3},{3,2},{4,5},{5,4},{6,7},{7,6},{8,16},{9,8},{10,1... | collective-permute-start | bytes 393224 | tf_op jit(solution)/shard_map/ppermute | solution.py:564
  26.9 1.5 %collective-permute-start.11 = (bf16[128,512]{1,0:T(8,128)(2,1)S(1)}, bf16[128,512]{1,0:T(8,128)(2,1)S(1)}, u32[]{:S(2)}, u32[]{:S(2)}) collective-permute-start(bf16[128,512]{1,0:T(8,128)(2,1)S(1)} %next.10), channel_id=1, source_target_pairs={{0,1},{1,0},{2,3},{3,2},{4,5},{5,4},{6,7},{7,6},{8,16},{9,8},{10,1... | collective-permute-start | bytes 393224 | tf_op jit(solution)/shard_map/ppermute | solution.py:564
  28.4 1.7 %collective-permute-start.12 = (bf16[128,512]{1,0:T(8,128)(2,1)S(1)}, bf16[128,512]{1,0:T(8,128)(2,1)S(1)}, u32[]{:S(2)}, u32[]{:S(2)}) collective-permute-start(bf16[128,512]{1,0:T(8,128)(2,1)S(1)} %next.11), channel_id=1, source_target_pairs={{0,1},{1,0},{2,3},{3,2},{4,5},{5,4},{6,7},{7,6},{8,16},{9,8},{10,1... | collective-permute-start | bytes 393224 | tf_op jit(solution)/shard_map/ppermute | solution.py:564
  30.1 0.1 collective-permute-done.9.refs_0_.refs_1_
  30.1 1.4 %collective-permute-done.10.refs_0_.refs_2_ = bf16[128,512]{1,0:T(8,128)(2,1)S(1)} collective-permute-done((bf16[128,512]{1,0:T(8,128)(2,1)S(1)}, bf16[128,512]{1,0:T(8,128)(2,1)S(1)}, u32[]{:S(2)}, u32[]{:S(2)}) %collective-permute-start.10) | collective-permute-done | bytes 131104 | tf_op jit(solution)/shard_map/ppermute | solution.py:564
  31.5 1.4 %collective-permute-done.11.refs_0_.refs_3_ = bf16[128,512]{1,0:T(8,128)(2,1)S(1)} collective-permute-done((bf16[128,512]{1,0:T(8,128)(2,1)S(1)}, bf16[128,512]{1,0:T(8,128)(2,1)S(1)}, u32[]{:S(2)}, u32[]{:S(2)}) %collective-permute-start.11) | collective-permute-done | bytes 131104 | tf_op jit(solution)/shard_map/ppermute | solution.py:564
  33.0 1.4 %collective-permute-done.12.refs_4_ = bf16[128,512]{1,0:T(8,128)(2,1)S(1)} collective-permute-done((bf16[128,512]{1,0:T(8,128)(2,1)S(1)}, bf16[128,512]{1,0:T(8,128)(2,1)S(1)}, u32[]{:S(2)}, u32[]{:S(2)}) %collective-permute-start.12) | collective-permute-done | bytes 131104 | tf_op jit(solution)/shard_map/ppermute | solution.py:564
  34.4 0.0 collective-permute-done.13.refs_3_.refs_4_
  34.4 0.0 collective-permute-start.14
  34.4 0.5 collective-permute-start.15
  34.9 9.4 %collective-permute-start.16 = (bf16[128,512]{1,0:T(8,128)(2,1)S(1)}, bf16[128,512]{1,0:T(8,128)(2,1)S(1)}, u32[]{:S(2)}, u32[]{:S(2)}) collective-permute-start(bf16[128,512]{1,0:T(8,128)(2,1)S(1)} %get-tuple-element.109.refs_3_), channel_id=1, source_target_pairs={{0,1},{1,17},{2,3},{3,2},{4,5},{5,4},{6,7},{7,6},{8,9},{9,19},{10,... | collective-permute-start | bytes 393224 | tf_op jit(solution)/shard_map/ppermute | solution.py:564
  44.2 0.0 collective-permute-start.17
  44.2 0.0 collective-permute-done.15.refs_0_
  44.2 0.0 collective-permute-done.14.refs_0_
  44.3 0.0 copy-start.5
  44.3 2.2 %collective-permute-done.16.refs_1_ = bf16[128,512]{1,0:T(8,128)(2,1)S(1)} collective-permute-done((bf16[128,512]{1,0:T(8,128)(2,1)S(1)}, bf16[128,512]{1,0:T(8,128)(2,1)S(1)}, u32[]{:S(2)}, u32[]{:S(2)}) %collective-permute-start.16) | collective-permute-done | bytes 131104 | tf_op jit(solution)/shard_map/ppermute | solution.py:564
  46.5 0.0 collective-permute-done.17.refs_2_
  46.6 7.8 %collective-permute-start.18 = (bf16[64,512]{1,0:T(8,128)(2,1)S(1)}, bf16[64,512]{1,0:T(8,128)(2,1)S(1)}, u32[]{:S(2)}, u32[]{:S(2)}) collective-permute-start(bf16[64,512]{1,0:T(8,128)(2,1)S(1)} %get-tuple-element.112), channel_id=1, source_target_pairs={{0,1},{1,0},{2,3},{3,2},{4,5},{5,4},{6,7},{7,6},{8,9},{9,8},{10,11... | collective-permute-start | bytes 196616 | tf_op jit(solution)/shard_map/ppermute | solution.py:583
  54.4 0.9 %collective-permute-done.18.refs_5_ = bf16[64,512]{1,0:T(8,128)(2,1)S(1)} collective-permute-done((bf16[64,512]{1,0:T(8,128)(2,1)S(1)}, bf16[64,512]{1,0:T(8,128)(2,1)S(1)}, u32[]{:S(2)}, u32[]{:S(2)}) %collective-permute-start.18) | collective-permute-done | bytes 65568 | tf_op jit(solution)/shard_map/ppermute | solution.py:583
  55.3 1.2 %decode.1 = bf16[227,128]{1,0:T(8,128)(2,1)} custom-call(s32[1]{0:T(128)} %bitcast.segment, s32[1]{0:T(128)} %bitcast.1.place, f32[128,512]{1,0:T(8,128)S(1)} %get-tuple-element.86.refs_0_, bf16[64,128]{1,0:T(8,128)(2,1)S(1)} %get-tuple-element.87.refs_1_, bf16[1024,512]{1,0:T(8,128)(2,1)S(1)} %copy-done, bf16[227,512]{1,0:T(8,128)(2,1)S(1)} %bitcast.15, ...), custom_call_target="tpu_custom_call" | custom-call | bytes 1748744 | tf_op jit(solution)/shard_map/decode/pallas_call | solution.py:500
  (42 shorter events, 0.2 us)
Async XLA Ops:
  0.0 1.7 %copy-start.7 = (s32[64,8]{0,1:T(8,128)S(1)}, s32[64,8]{0,1:T(8,128)}, u32[]{:S(2)}) copy-start(s32[64,8]{0,1:T(8,128)} %param.21) | copy-start | bytes 6148
  0.0 1.8 %copy-start.8 = (s32[4,64]{1,0:T(4,128)S(1)}, s32[4,64]{1,0:T(4,128)}, u32[]{:S(2)}) copy-start(s32[4,64]{1,0:T(4,128)} %param.22) | copy-start | bytes 3076
  0.0 1.8 %copy-start.9 = (s32[4,1]{0,1:T(1,128)S(1)}, s32[4,1]{0,1:T(1,128)}, u32[]{:S(2)}) copy-start(s32[4,1]{0,1:T(1,128)} %param.23) | copy-start | bytes 52
  0.0 1.8 %copy-start.10 = (s32[128]{0:T(128)S(1)}, s32[128]{0:T(128)}, u32[]{:S(2)}) copy-start(s32[128]{0:T(128)} %param.19) | copy-start | bytes 1540
  0.0 1.8 %copy-start.3 = (bf16[227,512]{1,0:T(8,128)(2,1)S(1)}, bf16[227,512]{1,0:T(8,128)(2,1)}, u32[]{:S(2)}) copy-start(bf16[227,512]{1,0:T(8,128)(2,1)} %refs_1_.3) | copy-start | bytes 697348
  0.0 6.9 %copy-start.4 = (bf16[1,512,512]{2,1,0:T(8,128)(2,1)S(1)}, bf16[1,512,512]{2,1,0:T(8,128)(2,1)}, u32[]{:S(2)}) copy-start(bf16[1,512,512]{2,1,0:T(8,128)(2,1)} %w_message.1) | copy-start | bytes 1572868
  0.0 11.8 %collective-permute-start.4 = (bf16[1,512,1024]{2,1,0:T(8,128)(2,1)}, bf16[1,512,1024]{2,1,0:T(8,128)(2,1)S(1)}, u32[]{:S(2)}, u32[]{:S(2)}) collective-permute-start(bf16[1,512,1024]{2,1,0:T(8,128)(2,1)} %w_project), channel_id=1, source_target_pairs={{0,1},{1,0},{2,3},{3,2},{4,5},{5,4},{6,7},{7,6},{8,9},{9,8},{10,11... | collective-permute-start | bytes 3145736 | tf_op jit(solution)/shard_map/ppermute | solution.py:564
  2.5 7.6 %collective-permute-start = (bf16[80,512]{1,0:T(8,128)(2,1)S(1)}, bf16[80,512]{1,0:T(8,128)(2,1)S(1)}, u32[]{:S(2)}, u32[]{:S(2)}) collective-permute-start(bf16[80,512]{1,0:T(8,128)(2,1)S(1)} %get-tuple-element.68), channel_id=1, source_target_pairs={{0,2},{1,3},{2,0},{3,1},{4,6},{5,7},{6,4},{7,5},{8,9},{9,8},{10,11... | collective-permute-start | bytes 245768 | tf_op jit(solution)/shard_map/ppermute | solution.py:579
  2.7 7.4 %collective-permute-start.1 = (bf16[80,512]{1,0:T(8,128)(2,1)S(1)}, bf16[80,512]{1,0:T(8,128)(2,1)S(1)}, u32[]{:S(2)}, u32[]{:S(2)}) collective-permute-start(bf16[80,512]{1,0:T(8,128)(2,1)S(1)} %get-tuple-element.69), channel_id=1, source_target_pairs={{0,8},{1,9},{2,10},{3,11},{4,12},{5,13},{6,14},{7,15},{8,4},{9,5},... | collective-permute-start | bytes 245768 | tf_op jit(solution)/shard_map/ppermute | solution.py:579
  6.2 3.9 %collective-permute-start.2 = (bf16[80,512]{1,0:T(8,128)(2,1)S(1)}, bf16[80,512]{1,0:T(8,128)(2,1)S(1)}, u32[]{:S(2)}, u32[]{:S(2)}) collective-permute-start(bf16[80,512]{1,0:T(8,128)(2,1)S(1)} %get-tuple-element.70), channel_id=1, source_target_pairs={{0,16},{1,17},{2,18},{3,19},{4,20},{5,21},{6,22},{7,23},{8,9},{9,8... | collective-permute-start | bytes 245768 | tf_op jit(solution)/shard_map/ppermute | solution.py:579
  6.9 1.2 %copy-start.1 = (bf16[1,1024,512]{2,1,0:T(8,128)(2,1)S(1)}, bf16[1,1024,512]{2,1,0:T(8,128)(2,1)}, u32[]{:S(2)}) copy-start(bf16[1,1024,512]{2,1,0:T(8,128)(2,1)} %w_update.1) | copy-start | bytes 3145732
  8.1 1.2 %copy-start.2 = (bf16[1,512,1024]{2,1,0:T(8,128)(2,1)S(1)}, bf16[1,512,1024]{2,1,0:T(8,128)(2,1)}, u32[]{:S(2)}) copy-start(bf16[1,512,1024]{2,1,0:T(8,128)(2,1)} %w_project) | copy-start | bytes 3145732
  10.2 1.7 %collective-permute-start.3 = (bf16[320,512]{1,0:T(8,128)(2,1)S(1)}, bf16[320,512]{1,0:T(8,128)(2,1)S(1)}, u32[]{:S(2)}, u32[]{:S(2)}) collective-permute-start(bf16[320,512]{1,0:T(8,128)(2,1)S(1)} %join.1.refs_0_), channel_id=1, source_target_pairs={{0,1},{1,0},{2,3},{3,2},{4,5},{5,4},{6,7},{7,6},{8,9},{9,8},{10,11... | collective-permute-start | bytes 983048 | tf_op jit(solution)/shard_map/ppermute | solution.py:583
  11.9 22.5 %collective-permute-start.13 = (bf16[2,512,512]{2,1,0:T(8,128)(2,1)S(1)}, bf16[2,512,512]{2,1,0:T(8,128)(2,1)S(1)}, u32[]{:S(2)}, u32[]{:S(2)}) collective-permute-start(bf16[2,512,512]{2,1,0:T(8,128)(2,1)S(1)} %pack.1), channel_id=1, source_target_pairs={{0,1},{1,0},{2,3},{3,2},{4,5},{5,4},{6,7},{7,6},{8,9},{9,8},{10,11... | collective-permute-start | bytes 3145736 | tf_op jit(solution)/shard_map/ppermute | solution.py:564
  12.0 7.6 %collective-permute-start.5 = (bf16[144,512]{1,0:T(8,128)(2,1)S(1)}, bf16[144,512]{1,0:T(8,128)(2,1)S(1)}, u32[]{:S(2)}, u32[]{:S(2)}) collective-permute-start(bf16[144,512]{1,0:T(8,128)(2,1)S(1)} %get-tuple-element.83), channel_id=1, source_target_pairs={{0,8},{1,0},{2,10},{3,2},{4,12},{5,4},{6,14},{7,6},{8,9},{9,1},{10... | collective-permute-start | bytes 442376 | tf_op jit(solution)/shard_map/ppermute | solution.py:564
  14.5 5.1 %collective-permute-start.6 = (bf16[128,512]{1,0:T(8,128)(2,1)S(1)}, bf16[128,512]{1,0:T(8,128)(2,1)S(1)}, u32[]{:S(2)}, u32[]{:S(2)}) collective-permute-start(bf16[128,512]{1,0:T(8,128)(2,1)S(1)} %next.6), channel_id=1, source_target_pairs={{0,8},{1,0},{2,10},{3,2},{4,12},{5,4},{6,14},{7,6},{8,9},{9,1},{10... | collective-permute-start | bytes 393224 | tf_op jit(solution)/shard_map/ppermute | solution.py:564
  16.2 3.0 %copy-start = (bf16[1024,512]{1,0:T(8,128)(2,1)S(1)}, bf16[1024,512]{1,0:T(8,128)(2,1)}, u32[]{:S(2)}) copy-start(bf16[1024,512]{1,0:T(8,128)(2,1)} %refs_2_.3) | copy-start | bytes 3145732
  16.2 3.5 %collective-permute-start.7 = (bf16[128,512]{1,0:T(8,128)(2,1)S(1)}, bf16[128,512]{1,0:T(8,128)(2,1)S(1)}, u32[]{:S(2)}, u32[]{:S(2)}) collective-permute-start(bf16[128,512]{1,0:T(8,128)(2,1)S(1)} %next.7), channel_id=1, source_target_pairs={{0,8},{1,0},{2,10},{3,2},{4,12},{5,4},{6,14},{7,6},{8,9},{9,1},{10... | collective-permute-start | bytes 393224 | tf_op jit(solution)/shard_map/ppermute | solution.py:564
  17.7 1.5 %copy-start.6 = (s32[128]{0:T(128)S(1)}, s32[128]{0:T(128)}, u32[]{:S(2)}) copy-start(s32[128]{0:T(128)} %param.20) | copy-start | bytes 1540
  17.7 3.4 %collective-permute-start.8 = (bf16[128,512]{1,0:T(8,128)(2,1)S(1)}, bf16[128,512]{1,0:T(8,128)(2,1)S(1)}, u32[]{:S(2)}, u32[]{:S(2)}) collective-permute-start(bf16[128,512]{1,0:T(8,128)(2,1)S(1)} %next.8), channel_id=1, source_target_pairs={{0,8},{1,0},{2,10},{3,2},{4,12},{5,4},{6,14},{7,6},{8,9},{9,1},{10... | collective-permute-start | bytes 393224 | tf_op jit(solution)/shard_map/ppermute | solution.py:564
  21.1 9.0 %collective-permute-start.9 = (bf16[144,512]{1,0:T(8,128)(2,1)S(1)}, bf16[144,512]{1,0:T(8,128)(2,1)S(1)}, u32[]{:S(2)}, u32[]{:S(2)}) collective-permute-start(bf16[144,512]{1,0:T(8,128)(2,1)S(1)} %get-tuple-element.97), channel_id=1, source_target_pairs={{0,1},{1,0},{2,3},{3,2},{4,5},{5,4},{6,7},{7,6},{8,16},{9,8},{10,1... | collective-permute-start | bytes 442376 | tf_op jit(solution)/shard_map/ppermute | solution.py:564
  25.4 6.1 %collective-permute-start.10 = (bf16[128,512]{1,0:T(8,128)(2,1)S(1)}, bf16[128,512]{1,0:T(8,128)(2,1)S(1)}, u32[]{:S(2)}, u32[]{:S(2)}) collective-permute-start(bf16[128,512]{1,0:T(8,128)(2,1)S(1)} %next.9), channel_id=1, source_target_pairs={{0,1},{1,0},{2,3},{3,2},{4,5},{5,4},{6,7},{7,6},{8,16},{9,8},{10,1... | collective-permute-start | bytes 393224 | tf_op jit(solution)/shard_map/ppermute | solution.py:564
  26.9 6.0 %collective-permute-start.11 = (bf16[128,512]{1,0:T(8,128)(2,1)S(1)}, bf16[128,512]{1,0:T(8,128)(2,1)S(1)}, u32[]{:S(2)}, u32[]{:S(2)}) collective-permute-start(bf16[128,512]{1,0:T(8,128)(2,1)S(1)} %next.10), channel_id=1, source_target_pairs={{0,1},{1,0},{2,3},{3,2},{4,5},{5,4},{6,7},{7,6},{8,16},{9,8},{10,1... | collective-permute-start | bytes 393224 | tf_op jit(solution)/shard_map/ppermute | solution.py:564
  28.4 5.9 %collective-permute-start.12 = (bf16[128,512]{1,0:T(8,128)(2,1)S(1)}, bf16[128,512]{1,0:T(8,128)(2,1)S(1)}, u32[]{:S(2)}, u32[]{:S(2)}) collective-permute-start(bf16[128,512]{1,0:T(8,128)(2,1)S(1)} %next.11), channel_id=1, source_target_pairs={{0,1},{1,0},{2,3},{3,2},{4,5},{5,4},{6,7},{7,6},{8,16},{9,8},{10,1... | collective-permute-start | bytes 393224 | tf_op jit(solution)/shard_map/ppermute | solution.py:564
  34.4 9.9 %collective-permute-start.14 = (bf16[128,512]{1,0:T(8,128)(2,1)S(1)}, bf16[128,512]{1,0:T(8,128)(2,1)S(1)}, u32[]{:S(2)}, u32[]{:S(2)}) collective-permute-start(bf16[128,512]{1,0:T(8,128)(2,1)S(1)} %far_part.3), channel_id=1, source_target_pairs={{0,1},{1,0},{2,3},{3,2},{4,5},{5,4},{6,7},{7,17},{8,9},{9,8},{10,1... | collective-permute-start | bytes 393224 | tf_op jit(solution)/shard_map/ppermute | solution.py:564
  34.4 9.9 %collective-permute-start.15 = (bf16[128,512]{1,0:T(8,128)(2,1)S(1)}, bf16[128,512]{1,0:T(8,128)(2,1)S(1)}, u32[]{:S(2)}, u32[]{:S(2)}) collective-permute-start(bf16[128,512]{1,0:T(8,128)(2,1)S(1)} %get-tuple-element.108), channel_id=1, source_target_pairs={{0,1},{1,0},{2,3},{3,2},{4,5},{5,21},{6,7},{7,6},{8,9},{9,8},{10,1... | collective-permute-start | bytes 393224 | tf_op jit(solution)/shard_map/ppermute | solution.py:564
  34.9 11.7 %collective-permute-start.16 = (bf16[128,512]{1,0:T(8,128)(2,1)S(1)}, bf16[128,512]{1,0:T(8,128)(2,1)S(1)}, u32[]{:S(2)}, u32[]{:S(2)}) collective-permute-start(bf16[128,512]{1,0:T(8,128)(2,1)S(1)} %get-tuple-element.109.refs_3_), channel_id=1, source_target_pairs={{0,1},{1,17},{2,3},{3,2},{4,5},{5,4},{6,7},{7,6},{8,9},{9,19},{10,... | collective-permute-start | bytes 393224 | tf_op jit(solution)/shard_map/ppermute | solution.py:564
  44.2 2.3 %collective-permute-start.17 = (bf16[128,512]{1,0:T(8,128)(2,1)S(1)}, bf16[128,512]{1,0:T(8,128)(2,1)S(1)}, u32[]{:S(2)}, u32[]{:S(2)}) collective-permute-start(bf16[128,512]{1,0:T(8,128)(2,1)S(1)} %get-tuple-element.110.refs_4_), channel_id=1, source_target_pairs={{0,1},{1,0},{2,3},{3,17},{4,5},{5,4},{6,7},{7,6},{8,9},{9,8},{10,1... | collective-permute-start | bytes 393224 | tf_op jit(solution)/shard_map/ppermute | solution.py:564
  44.3 11.0 %copy-start.5 = (bf16[512,227]{0,1:T(8,128)(2,1)S(1)}, bf16[512,227]{0,1:T(8,128)(2,1)}, u32[]{:S(2)}) copy-start(bf16[512,227]{0,1:T(8,128)(2,1)} %param.18) | copy-start | bytes 697348
  46.6 8.7 %collective-permute-start.18 = (bf16[64,512]{1,0:T(8,128)(2,1)S(1)}, bf16[64,512]{1,0:T(8,128)(2,1)S(1)}, u32[]{:S(2)}, u32[]{:S(2)}) collective-permute-start(bf16[64,512]{1,0:T(8,128)(2,1)S(1)} %get-tuple-element.112), channel_id=1, source_target_pairs={{0,1},{1,0},{2,3},{3,2},{4,5},{5,4},{6,7},{7,6},{8,9},{9,8},{10,11... | collective-permute-start | bytes 196616 | tf_op jit(solution)/shard_map/ppermute | solution.py:583

commit v16 on v15

--- a/solution.py
+++ b/solution.py
@@ -172,6 +172,21 @@
 
 def owns(where, group, at_segment):
     return jnp.logical_and(where[0] == at_segment, lax.rem(where[1], group) == 0)
+
+
+def swapped_roles(where, group, at_segment):
+    chip, lane = place_of(where, group)
+    for number in range(2):
+        here = jnp.logical_and(where[0] == at_segment + number, lane == 0)
+        yield jnp.logical_and(here, lax.rem(chip, 2) == number), number
+
+
+def weights_of(came, held, own):
+    if own:
+        return [block[...] for block in held]
+    w_project, pair = came
+    width = pair.shape[1]
+    return [w_project[0, :, :width], w_project[0, :, width:], pair[0], pair[1]]
 
 
 def fetch(sources, targets, semaphores):
@@ -272,7 +287,7 @@
 
 
 def pack_kernel(group, at_segment, where, *refs):
-    @pl.when(owns(where, group, at_segment))
+    @pl.when(jnp.logical_or(owns(where, group, at_segment), owns(where, group, at_segment + 1)))
     def _():
         for place, block in enumerate(refs[:-1]):
             refs[-1][place] = block[...]
@@ -328,28 +343,43 @@
             columns[0][...] = columns_of(digits[:fanout] * DIGIT + digits[fanout:])
 
 
+def late_sender_kernel(group, at_segment, fanout, rows, where, state, w_send, w_project, sender, *columns):
+    width = state.shape[1]
+    for here, number in swapped_roles(where, group, at_segment):
+
+        @pl.when(here)
+        def _(number=number):
+            weights = w_project[0, :, width:] if number else w_send[...]
+            sender[...] = matmul(state[:rows, :], weights).astype(jnp.bfloat16)
+            if columns:
+                digits = state[rows:, :].astype(jnp.float32)
+                columns[0][...] = columns_of(digits[:fanout] * DIGIT + digits[fanout:])
+
+
 def layer_kernel(group, at_segment, fanout, rows, where, columns, *refs):
     parts = len(rows)
     state, senders, refs = refs[:parts], refs[parts : 2 * parts - 1], refs[2 * parts - 1 :]
-    (w_receive, w_send, w_own, w_edges), (renewed, whole, sender) = refs[:4], refs[4:]
+    held, came, (renewed, whole, sender) = refs[:4], refs[4:6], refs[6:]
     nodes = renewed.shape[0]
     chunk = min(nodes, 256)
-
-    @pl.when(owns(where, group, at_segment))
-    def _():
-        start = 0
-        for part, count in zip(state, rows):
-            whole[start : start + count, :] = part[:count, :]
-            start += count
-        start = 0
-        for part in senders:
-            sender[start : start + part.shape[0], :] = part[...]
-            start += part.shape[0]
-        sender[start:, :] = matmul(whole[start:, :], w_send[...]).astype(jnp.bfloat16)
-        for start in range(0, nodes, chunk):
-            span = slice(start, start + chunk)
-            gathered = sum_edges(fanout, columns[span, :], sender[...], whole[span, :], w_receive[...])
-            renewed[span, :] = update_nodes(whole[span, :], gathered, w_own[...], w_edges[...])
+    for here, number in swapped_roles(where, group, at_segment):
+
+        @pl.when(here)
+        def _(number=number):
+            w_receive, w_send, w_own, w_edges = weights_of(came, held, number == 0)
+            start = 0
+            for part, count in zip(state, rows):
+                whole[start : start + count, :] = part[:count, :]
+                start += count
+            start = 0
+            for part in senders:
+                sender[start : start + part.shape[0], :] = part[...]
+                start += part.shape[0]
+            sender[start:, :] = matmul(whole[start:, :], w_send).astype(jnp.bfloat16)
+            for start in range(0, nodes, chunk):
+                span = slice(start, start + chunk)
+                gathered = sum_edges(fanout, columns[span, :], sender[...], whole[span, :], w_receive)
+                renewed[span, :] = update_nodes(whole[span, :], gathered, w_own, w_edges)
 
 
 def open_kernel(group, at_segment, fanout, rows, where, columns, *refs):
@@ -389,26 +419,25 @@
 
 def end_kernel(group, at_segment, chips, far, begin, first, fanout, where, columns, state, *refs):
     senders, refs = (refs[:0], refs) if first else (refs[:1], refs[1:])
-    (w_project, pair), outs = refs[:2], refs[2:]
-    width = state.shape[1]
+    held, came, outs = refs[:4], refs[4:6], refs[6:]
     half = state.shape[0] // 2
     chip, _ = place_of(where, group)
-
-    @pl.when(owns(where, group, at_segment))
-    def _():
-        pieces = outs
-        if first:
-            outs[0][...] = matmul(state[...], w_project[0, :, width:]).astype(jnp.bfloat16)
-            pieces = outs[1:]
-        sender = outs[0] if first else senders[0]
-        rows = sum(piece.shape[0] for piece in pieces)
-        upper = (chip < chips // 2) if far else (chip >= chips // 2)
-        start = pl.multiple_of(jnp.where(upper, half, 0) + begin, rows)
-        own = state[pl.ds(start, rows), :]
-        gathered = sum_edges(
-            fanout, columns[pl.ds(start, rows), :], sender[...], own, w_project[0, :, :width]
-        )
-        write_pieces(pieces, update_nodes(own, gathered, pair[0], pair[1]))
+    for here, number in swapped_roles(where, group, at_segment):
+
+        @pl.when(here)
+        def _(number=number):
+            w_receive, w_send, w_own, w_edges = weights_of(came, held, number == 1)
+            pieces = outs
+            if first:
+                outs[0][...] = matmul(state[...], w_send).astype(jnp.bfloat16)
+                pieces = outs[1:]
+            sender = outs[0] if first else senders[0]
+            rows = sum(piece.shape[0] for piece in pieces)
+            upper = (chip < chips // 2) if far else (chip >= chips // 2)
+            start = pl.multiple_of(jnp.where(upper, half, 0) + begin, rows)
+            own = state[pl.ds(start, rows), :]
+            gathered = sum_edges(fanout, columns[pl.ds(start, rows), :], sender[...], own, w_receive)
+            write_pieces(pieces, update_nodes(own, gathered, w_own, w_edges))
 
 
 def write_pieces(pieces, value):
@@ -422,7 +451,7 @@
     segment = where[0]
     chip, _ = place_of(where, group)
     crosses = lax.div(chip, each) != lax.div(segment, each)
-    return crosses, jnp.logical_and(segment == last, chip == last), lax.rem(chip, each)
+    return crosses, jnp.logical_and(segment >= last, chip == segment), lax.rem(chip, each)
 
 
 def far_kernel(group, chips, last, number, where, *refs):
@@ -583,7 +612,7 @@
         return lax.ppermute(value, "dom", pairs)
 
     def owner(m, at_segment):
-        return device(at_segment, m * group)
+        return device(min(at_segment, last + m % 2), m * group)
 
     own_segment, own_place, w_project = lax.optimization_barrier(
         (segment.reshape(1), place.reshape(1), w_project)
@@ -591,7 +620,7 @@
     where = (own_segment, own_place)
     weights = [w_project, w_message, w_update]
     last = segments - 2
-    to_last = [(owner(m, last + 1), owner(m, last)) for m in range(samples)]
+    to_last = [(device(last + 1 - m % 2, m * group), owner(m, segments)) for m in range(samples)]
     came_project = send(w_project, to_last)
     snapshots = jnp.transpose(grid_state, (0, 2, 1))
     lists = send_rows.shape[0]
@@ -649,7 +678,7 @@
     )
     columns, came_project, *held = lax.optimization_barrier((columns, came_project, *held))
     (pair,) = call(
-        functools.partial(pack_kernel, group, last + 1),
+        functools.partial(pack_kernel, group, last),
         "pack",
         [jax.ShapeDtypeStruct((2, width, width), bf16)],
         [where] + held[2:],
@@ -658,7 +687,7 @@
     came = [came_project, send(pair, to_last)]
     pieces, senders, rows, extra = [state], [], (nodes,), [codes]
     for layer in range(last):
-        pairs = [(owner(m, layer), owner(m, layer + 1)) for m in range(samples)]
+        pairs = [(owner(m, layer), owner(m, segments if layer + 1 == last else layer + 1)) for m in range(samples)]
         sender, joined_state, piece = call(
             functools.partial(open_kernel, group, layer, fanout, rows),
             "open",
@@ -692,12 +721,13 @@
         for piece in pieces[:-1]:
             if senders:
                 piece, senders[-1] = lax.optimization_barrier((piece, senders[-1]))
+            late = layer + 1 == last
             sender, *found = call(
-                functools.partial(sender_kernel, group, layer + 1, fanout, share),
+                functools.partial(late_sender_kernel if late else sender_kernel, group, layer + 1, fanout, share),
                 "sender",
                 [short] + [columns_shape] * (not senders),
-                [where, piece, held[1]],
-                "wvv",
+                [where, piece, held[1]] + came[:1] * late,
+                "wvv" + "v" * late,
             )
             columns = found[0] if found else columns
             senders.append(sender)
@@ -705,8 +735,8 @@
         functools.partial(layer_kernel, group, last, fanout, rows),
         "layer",
         [whole],
-        [where, columns] + pieces + senders + held,
-        "w" + "v" * (1 + len(pieces + senders + held)),
+        [where, columns] + pieces + senders + held + came,
+        "w" + "v" * (1 + len(pieces + senders + held + came)),
         [pltpu.VMEM((nodes, width), bf16)] * 2,
     )
     far = []
@@ -715,8 +745,8 @@
             functools.partial(end_kernel, group, last, samples, True, begin, not far, fanout),
             "far_part",
             [whole] * (not far) + [short],
-            [where, columns, state] + ([sender] if far else []) + came,
-            "w" + "v" * (5 if far else 4),
+            [where, columns, state] + ([sender] if far else []) + held + came,
+            "w" + "v" * (9 if far else 8),
         )
         sender = found[0] if not far else sender
         far.append(found[-1])
@@ -724,8 +754,8 @@
         functools.partial(end_kernel, group, last, samples, False, 0, False, fanout),
         "near_half",
         [short] * (samples // 2),
-        [where, columns, state, sender] + came,
-        "wvvvvv",
+        [where, columns, state, sender] + held + came,
+        "w" + "v" * 9,
     )
     state = far + list(near)
     each = samples // 2
@@ -733,7 +763,7 @@
     for far, blocks in ((1, state[:each]), (0, state[each:])):
         for turn, block in enumerate(blocks):
             pairs = [
-                (owner(m, last), device(m, ((m // each ^ far) * each + turn) * group)) for m in range(samples)
+                (owner(m, segments), device(m, ((m // each ^ far) * each + turn) * group)) for m in range(samples)
             ]
             arrived.append(send(block, [pair for pair in pairs if pair[0] != pair[1]]))
     crossed = []

time: 56.7 us -> 54.1 us (0.954)
  starting transfers between devices: 39.1 us -> 36.4 us
    ppermute x2, starting transfers between devices: 7.89 us -> 4.97 us  [change_lane(): return lax.ppermute(value, 'dom', pairs)]
  transfers between devices with their start and end apart: 19 -> 19, of which waited for: 8 -> 8; matrix products, arithmetic and copies ran while one was open for 2% -> 2% of each run, Pallas kernels for 3% -> 4%
where the time goes in v16:
time: 54.1 us; the launch traced here: 53.9 us
  starting transfers between devices  36.4 us (67%)
  waiting for transfers between devices  10.6 us (20%)
  local copies, waits for them, and re-layouts  3.46 us (6%)
  Pallas kernels  3.2 us (6%)
    ppermute x14, starting transfers between devices, send(): lax.ppermute(value, ('segment', 'dom'), every_device(pairs, segments * pa...  27 us
    ppermute x14, waiting for transfers between devices, send(): lax.ppermute(value, ('segment', 'dom'), every_device(pairs, segments * pa...  8.05 us
    ppermute x2, starting transfers between devices, change_lane(): return lax.ppermute(value, 'dom', pairs)  4.97 us
    ppermute x3, starting transfers between devices, to_chip(): return lax.ppermute(value, ('segment', 'dom'), pairs)  4.36 us
    unnamed x23, local copies, waits for them, and re-layouts  3.46 us
    pallas_call x28, Pallas kernels, call(): pl.pallas_call(located if places[0] == 'w' else kernel, out_shape=shapes,...  3.2 us
    ppermute x2, waiting for transfers between devices, change_lane(): return lax.ppermute(value, 'dom', pairs)  2.52 us
  transfers between devices with their start and end apart: 19, of which 8 were waited for; matrix products, arithmetic and copies ran while one was open for 2% of the time, Pallas kernels for 4%

profile of v16, /device:TPU:3, one launch (start us, length us, event | category | flops | bytes accessed | tf_op | source)
XLA Modules:
  0.0 53.9 jit_solution(17641226948710676520)
XLA Ops:
  0.0 0.0 copy-start.10
  0.0 0.7 %collective-permute-start.4 = (bf16[1,512,1024]{2,1,0:T(8,128)(2,1)}, bf16[1,512,1024]{2,1,0:T(8,128)(2,1)S(1)}, u32[]{:S(2)}, u32[]{:S(2)}) collective-permute-start(bf16[1,512,1024]{2,1,0:T(8,128)(2,1)} %w_project), channel_id=1, source_target_pairs={{0,1},{1,0},{2,3},{3,2},{4,5},{5,4},{6,7},{7,6},{8,9},{9,8},{10,11... | collective-permute-start | bytes 3145736 | tf_op jit(solution)/shard_map/ppermute | solution.py:593
  0.8 1.0 %copy.15 = bf16[4,128,227]{1,2,0:T(8,128)(2,1)S(1)} copy(bf16[4,128,227]{1,0,2:T(4,128)(2,1)} %param.12) | data formatting | bytes 464896 | tf_op args[0]
  1.8 0.7 %encode.1 = (bf16[80,512]{1,0:T(8,128)(2,1)S(1)}, bf16[80,512]{1,0:T(8,128)(2,1)S(1)}, bf16[80,512]{1,0:T(8,128)(2,1)S(1)}, bf16[80,512]{1,0:T(8,128)(2,1)S(1)}) custom-call(s32[1]{0:T(128)} %bitcast.segment, s32[1]{0:T(128)} %bitcast.1.place, bf16[4,227,128]{2,1,0:T(8,128)(2,1)S(1)} %bitcast.13, bf16[227,512]{1,0:T(8,128)(2,1)S(1)} %copy-done.3, ...), custom_call_target="tpu_custom_call" | custom-call | bytes 799752 | tf_op jit(solution)/shard_map/encode/pallas_call | solution.py:529
  2.5 0.2 collective-permute-start
  2.7 3.4 %collective-permute-start.1 = (bf16[80,512]{1,0:T(8,128)(2,1)S(1)}, bf16[80,512]{1,0:T(8,128)(2,1)S(1)}, u32[]{:S(2)}, u32[]{:S(2)}) collective-permute-start(bf16[80,512]{1,0:T(8,128)(2,1)S(1)} %get-tuple-element.69), channel_id=1, source_target_pairs={{0,8},{1,9},{2,10},{3,11},{4,12},{5,13},{6,14},{7,15},{8,4},{9,5},... | collective-permute-start | bytes 245768 | tf_op jit(solution)/shard_map/ppermute | solution.py:608
  6.2 0.7 %collective-permute-start.2 = (bf16[80,512]{1,0:T(8,128)(2,1)S(1)}, bf16[80,512]{1,0:T(8,128)(2,1)S(1)}, u32[]{:S(2)}, u32[]{:S(2)}) collective-permute-start(bf16[80,512]{1,0:T(8,128)(2,1)S(1)} %get-tuple-element.70), channel_id=1, source_target_pairs={{0,16},{1,17},{2,18},{3,19},{4,20},{5,21},{6,22},{7,23},{8,9},{9,8... | collective-permute-start | bytes 245768 | tf_op jit(solution)/shard_map/ppermute | solution.py:608
  6.9 1.2 %copy-done.1 = bf16[1,1024,512]{2,1,0:T(8,128)(2,1)S(1)} copy-done((bf16[1,1024,512]{2,1,0:T(8,128)(2,1)S(1)}, bf16[1,1024,512]{2,1,0:T(8,128)(2,1)}, u32[]{:S(2)}) %copy-start.1) | copy-done | bytes 1048600
  8.1 1.2 %copy-done.2 = bf16[1,512,1024]{2,1,0:T(8,128)(2,1)S(1)} copy-done((bf16[1,512,1024]{2,1,0:T(8,128)(2,1)S(1)}, bf16[1,512,1024]{2,1,0:T(8,128)(2,1)}, u32[]{:S(2)}) %copy-start.2) | copy-done | bytes 1048600
  9.3 0.7 %hold.1 = (bf16[512,512]{1,0:T(8,128)(2,1)S(1)}, bf16[512,512]{1,0:T(8,128)(2,1)S(1)}, bf16[512,512]{1,0:T(8,128)(2,1)S(1)}, bf16[512,512]{1,0:T(8,128)(2,1)S(1)}) custom-call(bf16[1,512,1024]{2,1,0:T(8,128)(2,1)S(1)} %copy-done.2, bf16[1,512,512]{2,1,0:T(8,128)(2,1)S(1)} %copy-done.4, bf16[1,1024,512]{2,1,0:T(8,128)(2,1)S(1)} %copy-done.1), custom_call_target="tpu_custom_call" | custom-call | bytes 4718592 | tf_op jit(solution)/shard_map/hold/pallas_call | solution.py:529
  10.1 0.0 collective-permute-done.refs_1_
  10.1 0.0 collective-permute-done.1.refs_2_
  10.1 0.0 collective-permute-done.2.refs_3_
  10.2 0.1 collective-permute-start.3
  10.2 1.6 %collective-permute-done.3.refs_1_ = bf16[320,512]{1,0:T(8,128)(2,1)S(1)} collective-permute-done((bf16[320,512]{1,0:T(8,128)(2,1)S(1)}, bf16[320,512]{1,0:T(8,128)(2,1)S(1)}, u32[]{:S(2)}, u32[]{:S(2)}) %collective-permute-start.3) | collective-permute-done | bytes 327712 | tf_op jit(solution)/shard_map/ppermute | solution.py:612
  11.8 0.0 collective-permute-done.4.refs_2_.refs_12_.refs_6_.refs_7_
  11.9 0.1 collective-permute-start.13
  12.0 2.5 %collective-permute-start.5 = (bf16[144,512]{1,0:T(8,128)(2,1)S(1)}, bf16[144,512]{1,0:T(8,128)(2,1)S(1)}, u32[]{:S(2)}, u32[]{:S(2)}) collective-permute-start(bf16[144,512]{1,0:T(8,128)(2,1)S(1)} %get-tuple-element.83), channel_id=1, source_target_pairs={{0,8},{1,0},{2,10},{3,2},{4,12},{5,4},{6,14},{7,6},{8,9},{9,1},{10... | collective-permute-start | bytes 442376 | tf_op jit(solution)/shard_map/ppermute | solution.py:593
  14.5 1.7 %collective-permute-start.6 = (bf16[128,512]{1,0:T(8,128)(2,1)S(1)}, bf16[128,512]{1,0:T(8,128)(2,1)S(1)}, u32[]{:S(2)}, u32[]{:S(2)}) collective-permute-start(bf16[128,512]{1,0:T(8,128)(2,1)S(1)} %next.6), channel_id=1, source_target_pairs={{0,8},{1,0},{2,10},{3,2},{4,12},{5,4},{6,14},{7,6},{8,9},{9,1},{10... | collective-permute-start | bytes 393224 | tf_op jit(solution)/shard_map/ppermute | solution.py:593
  16.2 1.5 %collective-permute-start.7 = (bf16[128,512]{1,0:T(8,128)(2,1)S(1)}, bf16[128,512]{1,0:T(8,128)(2,1)S(1)}, u32[]{:S(2)}, u32[]{:S(2)}) collective-permute-start(bf16[128,512]{1,0:T(8,128)(2,1)S(1)} %next.7), channel_id=1, source_target_pairs={{0,8},{1,0},{2,10},{3,2},{4,12},{5,4},{6,14},{7,6},{8,9},{9,1},{10... | collective-permute-start | bytes 393224 | tf_op jit(solution)/shard_map/ppermute | solution.py:593
  17.7 1.5 %collective-permute-start.8 = (bf16[128,512]{1,0:T(8,128)(2,1)S(1)}, bf16[128,512]{1,0:T(8,128)(2,1)S(1)}, u32[]{:S(2)}, u32[]{:S(2)}) collective-permute-start(bf16[128,512]{1,0:T(8,128)(2,1)S(1)} %next.8), channel_id=1, source_target_pairs={{0,8},{1,0},{2,10},{3,2},{4,12},{5,4},{6,14},{7,6},{8,9},{9,1},{10... | collective-permute-start | bytes 393224 | tf_op jit(solution)/shard_map/ppermute | solution.py:593
  19.2 0.0 copy-done
  19.2 0.4 prepare.1
  19.6 0.0 collective-permute-done.5.refs_0_.refs_1_
  19.6 0.0 collective-permute-done.6.refs_0_.refs_2_
  19.6 0.0 collective-permute-done.7.refs_0_.refs_3_
  19.7 1.4 %collective-permute-done.8.refs_4_ = bf16[128,512]{1,0:T(8,128)(2,1)S(1)} collective-permute-done((bf16[128,512]{1,0:T(8,128)(2,1)S(1)}, bf16[128,512]{1,0:T(8,128)(2,1)S(1)}, u32[]{:S(2)}, u32[]{:S(2)}) %collective-permute-start.8) | collective-permute-done | bytes 131104 | tf_op jit(solution)/shard_map/ppermute | solution.py:593
  21.1 4.3 %collective-permute-start.9 = (bf16[144,512]{1,0:T(8,128)(2,1)S(1)}, bf16[144,512]{1,0:T(8,128)(2,1)S(1)}, u32[]{:S(2)}, u32[]{:S(2)}) collective-permute-start(bf16[144,512]{1,0:T(8,128)(2,1)S(1)} %get-tuple-element.97), channel_id=1, source_target_pairs={{0,1},{1,0},{2,3},{3,2},{4,5},{5,4},{6,7},{7,6},{8,16},{9,8},{10,2... | collective-permute-start | bytes 442376 | tf_op jit(solution)/shard_map/ppermute | solution.py:593
  25.4 1.5 %collective-permute-start.10 = (bf16[128,512]{1,0:T(8,128)(2,1)S(1)}, bf16[128,512]{1,0:T(8,128)(2,1)S(1)}, u32[]{:S(2)}, u32[]{:S(2)}) collective-permute-start(bf16[128,512]{1,0:T(8,128)(2,1)S(1)} %next.9), channel_id=1, source_target_pairs={{0,1},{1,0},{2,3},{3,2},{4,5},{5,4},{6,7},{7,6},{8,16},{9,8},{10,2... | collective-permute-start | bytes 393224 | tf_op jit(solution)/shard_map/ppermute | solution.py:593
  26.9 1.5 %collective-permute-start.11 = (bf16[128,512]{1,0:T(8,128)(2,1)S(1)}, bf16[128,512]{1,0:T(8,128)(2,1)S(1)}, u32[]{:S(2)}, u32[]{:S(2)}) collective-permute-start(bf16[128,512]{1,0:T(8,128)(2,1)S(1)} %next.10), channel_id=1, source_target_pairs={{0,1},{1,0},{2,3},{3,2},{4,5},{5,4},{6,7},{7,6},{8,16},{9,8},{10,2... | collective-permute-start | bytes 393224 | tf_op jit(solution)/shard_map/ppermute | solution.py:593
  28.4 1.6 %collective-permute-start.12 = (bf16[128,512]{1,0:T(8,128)(2,1)S(1)}, bf16[128,512]{1,0:T(8,128)(2,1)S(1)}, u32[]{:S(2)}, u32[]{:S(2)}) collective-permute-start(bf16[128,512]{1,0:T(8,128)(2,1)S(1)} %next.11), channel_id=1, source_target_pairs={{0,1},{1,0},{2,3},{3,2},{4,5},{5,4},{6,7},{7,6},{8,16},{9,8},{10,2... | collective-permute-start | bytes 393224 | tf_op jit(solution)/shard_map/ppermute | solution.py:593
  30.1 0.1 collective-permute-done.9.refs_0_.refs_1_
  30.1 1.4 %collective-permute-done.10.refs_0_.refs_2_ = bf16[128,512]{1,0:T(8,128)(2,1)S(1)} collective-permute-done((bf16[128,512]{1,0:T(8,128)(2,1)S(1)}, bf16[128,512]{1,0:T(8,128)(2,1)S(1)}, u32[]{:S(2)}, u32[]{:S(2)}) %collective-permute-start.10) | collective-permute-done | bytes 131104 | tf_op jit(solution)/shard_map/ppermute | solution.py:593
  31.5 1.4 %collective-permute-done.11.refs_0_.refs_3_ = bf16[128,512]{1,0:T(8,128)(2,1)S(1)} collective-permute-done((bf16[128,512]{1,0:T(8,128)(2,1)S(1)}, bf16[128,512]{1,0:T(8,128)(2,1)S(1)}, u32[]{:S(2)}, u32[]{:S(2)}) %collective-permute-start.11) | collective-permute-done | bytes 131104 | tf_op jit(solution)/shard_map/ppermute | solution.py:593
  33.0 1.4 %collective-permute-done.12.refs_4_ = bf16[128,512]{1,0:T(8,128)(2,1)S(1)} collective-permute-done((bf16[128,512]{1,0:T(8,128)(2,1)S(1)}, bf16[128,512]{1,0:T(8,128)(2,1)S(1)}, u32[]{:S(2)}, u32[]{:S(2)}) %collective-permute-start.12) | collective-permute-done | bytes 131104 | tf_op jit(solution)/shard_map/ppermute | solution.py:593
  34.4 0.0 collective-permute-done.13.refs_13_.refs_7_.refs_8_
  34.4 0.0 collective-permute-start.14
  34.4 0.5 collective-permute-start.15
  34.9 9.6 %collective-permute-start.16 = (bf16[128,512]{1,0:T(8,128)(2,1)S(1)}, bf16[128,512]{1,0:T(8,128)(2,1)S(1)}, u32[]{:S(2)}, u32[]{:S(2)}) collective-permute-start(bf16[128,512]{1,0:T(8,128)(2,1)S(1)} %get-tuple-element.109.refs_3_), channel_id=1, source_target_pairs={{0,1},{1,17},{2,3},{3,2},{4,5},{5,4},{6,7},{7,6},{8,9},{9,27},{10,... | collective-permute-start | bytes 393224 | tf_op jit(solution)/shard_map/ppermute | solution.py:593
  44.4 0.0 collective-permute-start.17
  44.4 0.0 collective-permute-done.15.refs_0_
  44.5 0.0 collective-permute-done.14.refs_0_
  44.5 0.0 copy-start.5
  44.5 2.3 %collective-permute-done.16.refs_1_ = bf16[128,512]{1,0:T(8,128)(2,1)S(1)} collective-permute-done((bf16[128,512]{1,0:T(8,128)(2,1)S(1)}, bf16[128,512]{1,0:T(8,128)(2,1)S(1)}, u32[]{:S(2)}, u32[]{:S(2)}) %collective-permute-start.16) | collective-permute-done | bytes 131104 | tf_op jit(solution)/shard_map/ppermute | solution.py:593
  46.8 0.0 collective-permute-done.17.refs_2_
  46.8 4.9 %collective-permute-start.18 = (bf16[64,512]{1,0:T(8,128)(2,1)S(1)}, bf16[64,512]{1,0:T(8,128)(2,1)S(1)}, u32[]{:S(2)}, u32[]{:S(2)}) collective-permute-start(bf16[64,512]{1,0:T(8,128)(2,1)S(1)} %get-tuple-element.112), channel_id=1, source_target_pairs={{0,1},{1,0},{2,3},{3,2},{4,5},{5,4},{6,7},{7,6},{8,9},{9,8},{10,11... | collective-permute-start | bytes 196616 | tf_op jit(solution)/shard_map/ppermute | solution.py:612
  51.7 0.9 %collective-permute-done.18.refs_5_ = bf16[64,512]{1,0:T(8,128)(2,1)S(1)} collective-permute-done((bf16[64,512]{1,0:T(8,128)(2,1)S(1)}, bf16[64,512]{1,0:T(8,128)(2,1)S(1)}, u32[]{:S(2)}, u32[]{:S(2)}) %collective-permute-start.18) | collective-permute-done | bytes 65568 | tf_op jit(solution)/shard_map/ppermute | solution.py:612
  52.6 1.2 %decode.1 = bf16[227,128]{1,0:T(8,128)(2,1)} custom-call(s32[1]{0:T(128)} %bitcast.segment, s32[1]{0:T(128)} %bitcast.1.place, f32[128,512]{1,0:T(8,128)S(1)} %get-tuple-element.86.refs_0_, bf16[64,128]{1,0:T(8,128)(2,1)S(1)} %get-tuple-element.87.refs_1_, bf16[1024,512]{1,0:T(8,128)(2,1)S(1)} %copy-done, bf16[227,512]{1,0:T(8,128)(2,1)S(1)} %bitcast.15, ...), custom_call_target="tpu_custom_call" | custom-call | bytes 1748744 | tf_op jit(solution)/shard_map/decode/pallas_call | solution.py:529
  (42 shorter events, 0.2 us)
Async XLA Ops:
  0.0 1.7 %copy-start.7 = (s32[64,8]{0,1:T(8,128)S(1)}, s32[64,8]{0,1:T(8,128)}, u32[]{:S(2)}) copy-start(s32[64,8]{0,1:T(8,128)} %param.21) | copy-start | bytes 6148
  0.0 1.8 %copy-start.8 = (s32[4,64]{1,0:T(4,128)S(1)}, s32[4,64]{1,0:T(4,128)}, u32[]{:S(2)}) copy-start(s32[4,64]{1,0:T(4,128)} %param.22) | copy-start | bytes 3076
  0.0 1.8 %copy-start.9 = (s32[4,1]{0,1:T(1,128)S(1)}, s32[4,1]{0,1:T(1,128)}, u32[]{:S(2)}) copy-start(s32[4,1]{0,1:T(1,128)} %param.23) | copy-start | bytes 52
  0.0 1.8 %copy-start.10 = (s32[128]{0:T(128)S(1)}, s32[128]{0:T(128)}, u32[]{:S(2)}) copy-start(s32[128]{0:T(128)} %param.19) | copy-start | bytes 1540
  0.0 1.8 %copy-start.3 = (bf16[227,512]{1,0:T(8,128)(2,1)S(1)}, bf16[227,512]{1,0:T(8,128)(2,1)}, u32[]{:S(2)}) copy-start(bf16[227,512]{1,0:T(8,128)(2,1)} %refs_1_.3) | copy-start | bytes 697348
  0.0 6.9 %copy-start.4 = (bf16[1,512,512]{2,1,0:T(8,128)(2,1)S(1)}, bf16[1,512,512]{2,1,0:T(8,128)(2,1)}, u32[]{:S(2)}) copy-start(bf16[1,512,512]{2,1,0:T(8,128)(2,1)} %w_message.1) | copy-start | bytes 1572868
  0.0 11.8 %collective-permute-start.4 = (bf16[1,512,1024]{2,1,0:T(8,128)(2,1)}, bf16[1,512,1024]{2,1,0:T(8,128)(2,1)S(1)}, u32[]{:S(2)}, u32[]{:S(2)}) collective-permute-start(bf16[1,512,1024]{2,1,0:T(8,128)(2,1)} %w_project), channel_id=1, source_target_pairs={{0,1},{1,0},{2,3},{3,2},{4,5},{5,4},{6,7},{7,6},{8,9},{9,8},{10,11... | collective-permute-start | bytes 3145736 | tf_op jit(solution)/shard_map/ppermute | solution.py:593
  2.5 7.6 %collective-permute-start = (bf16[80,512]{1,0:T(8,128)(2,1)S(1)}, bf16[80,512]{1,0:T(8,128)(2,1)S(1)}, u32[]{:S(2)}, u32[]{:S(2)}) collective-permute-start(bf16[80,512]{1,0:T(8,128)(2,1)S(1)} %get-tuple-element.68), channel_id=1, source_target_pairs={{0,2},{1,3},{2,0},{3,1},{4,6},{5,7},{6,4},{7,5},{8,9},{9,8},{10,11... | collective-permute-start | bytes 245768 | tf_op jit(solution)/shard_map/ppermute | solution.py:608
  2.7 7.4 %collective-permute-start.1 = (bf16[80,512]{1,0:T(8,128)(2,1)S(1)}, bf16[80,512]{1,0:T(8,128)(2,1)S(1)}, u32[]{:S(2)}, u32[]{:S(2)}) collective-permute-start(bf16[80,512]{1,0:T(8,128)(2,1)S(1)} %get-tuple-element.69), channel_id=1, source_target_pairs={{0,8},{1,9},{2,10},{3,11},{4,12},{5,13},{6,14},{7,15},{8,4},{9,5},... | collective-permute-start | bytes 245768 | tf_op jit(solution)/shard_map/ppermute | solution.py:608
  6.2 3.9 %collective-permute-start.2 = (bf16[80,512]{1,0:T(8,128)(2,1)S(1)}, bf16[80,512]{1,0:T(8,128)(2,1)S(1)}, u32[]{:S(2)}, u32[]{:S(2)}) collective-permute-start(bf16[80,512]{1,0:T(8,128)(2,1)S(1)} %get-tuple-element.70), channel_id=1, source_target_pairs={{0,16},{1,17},{2,18},{3,19},{4,20},{5,21},{6,22},{7,23},{8,9},{9,8... | collective-permute-start | bytes 245768 | tf_op jit(solution)/shard_map/ppermute | solution.py:608
  6.9 1.2 %copy-start.1 = (bf16[1,1024,512]{2,1,0:T(8,128)(2,1)S(1)}, bf16[1,1024,512]{2,1,0:T(8,128)(2,1)}, u32[]{:S(2)}) copy-start(bf16[1,1024,512]{2,1,0:T(8,128)(2,1)} %w_update.1) | copy-start | bytes 3145732
  8.1 1.2 %copy-start.2 = (bf16[1,512,1024]{2,1,0:T(8,128)(2,1)S(1)}, bf16[1,512,1024]{2,1,0:T(8,128)(2,1)}, u32[]{:S(2)}) copy-start(bf16[1,512,1024]{2,1,0:T(8,128)(2,1)} %w_project) | copy-start | bytes 3145732
  10.2 1.7 %collective-permute-start.3 = (bf16[320,512]{1,0:T(8,128)(2,1)S(1)}, bf16[320,512]{1,0:T(8,128)(2,1)S(1)}, u32[]{:S(2)}, u32[]{:S(2)}) collective-permute-start(bf16[320,512]{1,0:T(8,128)(2,1)S(1)} %join.1.refs_0_), channel_id=1, source_target_pairs={{0,1},{1,0},{2,3},{3,2},{4,5},{5,4},{6,7},{7,6},{8,9},{9,8},{10,11... | collective-permute-start | bytes 983048 | tf_op jit(solution)/shard_map/ppermute | solution.py:612
  11.9 22.5 %collective-permute-start.13 = (bf16[2,512,512]{2,1,0:T(8,128)(2,1)S(1)}, bf16[2,512,512]{2,1,0:T(8,128)(2,1)S(1)}, u32[]{:S(2)}, u32[]{:S(2)}) collective-permute-start(bf16[2,512,512]{2,1,0:T(8,128)(2,1)S(1)} %pack.1), channel_id=1, source_target_pairs={{0,1},{1,0},{2,3},{3,2},{4,5},{5,4},{6,7},{7,6},{8,9},{9,8},{10,11... | collective-permute-start | bytes 3145736 | tf_op jit(solution)/shard_map/ppermute | solution.py:593
  12.0 7.6 %collective-permute-start.5 = (bf16[144,512]{1,0:T(8,128)(2,1)S(1)}, bf16[144,512]{1,0:T(8,128)(2,1)S(1)}, u32[]{:S(2)}, u32[]{:S(2)}) collective-permute-start(bf16[144,512]{1,0:T(8,128)(2,1)S(1)} %get-tuple-element.83), channel_id=1, source_target_pairs={{0,8},{1,0},{2,10},{3,2},{4,12},{5,4},{6,14},{7,6},{8,9},{9,1},{10... | collective-permute-start | bytes 442376 | tf_op jit(solution)/shard_map/ppermute | solution.py:593
  14.5 5.1 %collective-permute-start.6 = (bf16[128,512]{1,0:T(8,128)(2,1)S(1)}, bf16[128,512]{1,0:T(8,128)(2,1)S(1)}, u32[]{:S(2)}, u32[]{:S(2)}) collective-permute-start(bf16[128,512]{1,0:T(8,128)(2,1)S(1)} %next.6), channel_id=1, source_target_pairs={{0,8},{1,0},{2,10},{3,2},{4,12},{5,4},{6,14},{7,6},{8,9},{9,1},{10... | collective-permute-start | bytes 393224 | tf_op jit(solution)/shard_map/ppermute | solution.py:593
  16.2 3.0 %copy-start = (bf16[1024,512]{1,0:T(8,128)(2,1)S(1)}, bf16[1024,512]{1,0:T(8,128)(2,1)}, u32[]{:S(2)}) copy-start(bf16[1024,512]{1,0:T(8,128)(2,1)} %refs_2_.3) | copy-start | bytes 3145732
  16.2 3.4 %collective-permute-start.7 = (bf16[128,512]{1,0:T(8,128)(2,1)S(1)}, bf16[128,512]{1,0:T(8,128)(2,1)S(1)}, u32[]{:S(2)}, u32[]{:S(2)}) collective-permute-start(bf16[128,512]{1,0:T(8,128)(2,1)S(1)} %next.7), channel_id=1, source_target_pairs={{0,8},{1,0},{2,10},{3,2},{4,12},{5,4},{6,14},{7,6},{8,9},{9,1},{10... | collective-permute-start | bytes 393224 | tf_op jit(solution)/shard_map/ppermute | solution.py:593
  17.7 1.5 %copy-start.6 = (s32[128]{0:T(128)S(1)}, s32[128]{0:T(128)}, u32[]{:S(2)}) copy-start(s32[128]{0:T(128)} %param.20) | copy-start | bytes 1540
  17.7 3.4 %collective-permute-start.8 = (bf16[128,512]{1,0:T(8,128)(2,1)S(1)}, bf16[128,512]{1,0:T(8,128)(2,1)S(1)}, u32[]{:S(2)}, u32[]{:S(2)}) collective-permute-start(bf16[128,512]{1,0:T(8,128)(2,1)S(1)} %next.8), channel_id=1, source_target_pairs={{0,8},{1,0},{2,10},{3,2},{4,12},{5,4},{6,14},{7,6},{8,9},{9,1},{10... | collective-permute-start | bytes 393224 | tf_op jit(solution)/shard_map/ppermute | solution.py:593
  21.1 9.0 %collective-permute-start.9 = (bf16[144,512]{1,0:T(8,128)(2,1)S(1)}, bf16[144,512]{1,0:T(8,128)(2,1)S(1)}, u32[]{:S(2)}, u32[]{:S(2)}) collective-permute-start(bf16[144,512]{1,0:T(8,128)(2,1)S(1)} %get-tuple-element.97), channel_id=1, source_target_pairs={{0,1},{1,0},{2,3},{3,2},{4,5},{5,4},{6,7},{7,6},{8,16},{9,8},{10,2... | collective-permute-start | bytes 442376 | tf_op jit(solution)/shard_map/ppermute | solution.py:593
  25.4 6.1 %collective-permute-start.10 = (bf16[128,512]{1,0:T(8,128)(2,1)S(1)}, bf16[128,512]{1,0:T(8,128)(2,1)S(1)}, u32[]{:S(2)}, u32[]{:S(2)}) collective-permute-start(bf16[128,512]{1,0:T(8,128)(2,1)S(1)} %next.9), channel_id=1, source_target_pairs={{0,1},{1,0},{2,3},{3,2},{4,5},{5,4},{6,7},{7,6},{8,16},{9,8},{10,2... | collective-permute-start | bytes 393224 | tf_op jit(solution)/shard_map/ppermute | solution.py:593
  26.9 6.0 %collective-permute-start.11 = (bf16[128,512]{1,0:T(8,128)(2,1)S(1)}, bf16[128,512]{1,0:T(8,128)(2,1)S(1)}, u32[]{:S(2)}, u32[]{:S(2)}) collective-permute-start(bf16[128,512]{1,0:T(8,128)(2,1)S(1)} %next.10), channel_id=1, source_target_pairs={{0,1},{1,0},{2,3},{3,2},{4,5},{5,4},{6,7},{7,6},{8,16},{9,8},{10,2... | collective-permute-start | bytes 393224 | tf_op jit(solution)/shard_map/ppermute | solution.py:593
  28.4 5.9 %collective-permute-start.12 = (bf16[128,512]{1,0:T(8,128)(2,1)S(1)}, bf16[128,512]{1,0:T(8,128)(2,1)S(1)}, u32[]{:S(2)}, u32[]{:S(2)}) collective-permute-start(bf16[128,512]{1,0:T(8,128)(2,1)S(1)} %next.11), channel_id=1, source_target_pairs={{0,1},{1,0},{2,3},{3,2},{4,5},{5,4},{6,7},{7,6},{8,16},{9,8},{10,2... | collective-permute-start | bytes 393224 | tf_op jit(solution)/shard_map/ppermute | solution.py:593
  34.4 10.1 %collective-permute-start.14 = (bf16[128,512]{1,0:T(8,128)(2,1)S(1)}, bf16[128,512]{1,0:T(8,128)(2,1)S(1)}, u32[]{:S(2)}, u32[]{:S(2)}) collective-permute-start(bf16[128,512]{1,0:T(8,128)(2,1)S(1)} %far_part.3), channel_id=1, source_target_pairs={{0,1},{1,0},{2,3},{3,2},{4,5},{5,4},{6,7},{7,17},{8,9},{9,8},{10,1... | collective-permute-start | bytes 393224 | tf_op jit(solution)/shard_map/ppermute | solution.py:593
  34.4 10.1 %collective-permute-start.15 = (bf16[128,512]{1,0:T(8,128)(2,1)S(1)}, bf16[128,512]{1,0:T(8,128)(2,1)S(1)}, u32[]{:S(2)}, u32[]{:S(2)}) collective-permute-start(bf16[128,512]{1,0:T(8,128)(2,1)S(1)} %get-tuple-element.108), channel_id=1, source_target_pairs={{0,1},{1,0},{2,3},{3,2},{4,5},{5,21},{6,7},{7,6},{8,9},{9,8},{10,1... | collective-permute-start | bytes 393224 | tf_op jit(solution)/shard_map/ppermute | solution.py:593
  34.9 11.9 %collective-permute-start.16 = (bf16[128,512]{1,0:T(8,128)(2,1)S(1)}, bf16[128,512]{1,0:T(8,128)(2,1)S(1)}, u32[]{:S(2)}, u32[]{:S(2)}) collective-permute-start(bf16[128,512]{1,0:T(8,128)(2,1)S(1)} %get-tuple-element.109.refs_3_), channel_id=1, source_target_pairs={{0,1},{1,17},{2,3},{3,2},{4,5},{5,4},{6,7},{7,6},{8,9},{9,27},{10,... | collective-permute-start | bytes 393224 | tf_op jit(solution)/shard_map/ppermute | solution.py:593
  44.4 2.4 %collective-permute-start.17 = (bf16[128,512]{1,0:T(8,128)(2,1)S(1)}, bf16[128,512]{1,0:T(8,128)(2,1)S(1)}, u32[]{:S(2)}, u32[]{:S(2)}) collective-permute-start(bf16[128,512]{1,0:T(8,128)(2,1)S(1)} %get-tuple-element.110.refs_4_), channel_id=1, source_target_pairs={{0,1},{1,0},{2,3},{3,17},{4,5},{5,4},{6,7},{7,6},{8,9},{9,8},{10,1... | collective-permute-start | bytes 393224 | tf_op jit(solution)/shard_map/ppermute | solution.py:593
  44.5 8.2 %copy-start.5 = (bf16[512,227]{0,1:T(8,128)(2,1)S(1)}, bf16[512,227]{0,1:T(8,128)(2,1)}, u32[]{:S(2)}) copy-start(bf16[512,227]{0,1:T(8,128)(2,1)} %param.18) | copy-start | bytes 697348
  46.8 5.8 %collective-permute-start.18 = (bf16[64,512]{1,0:T(8,128)(2,1)S(1)}, bf16[64,512]{1,0:T(8,128)(2,1)S(1)}, u32[]{:S(2)}, u32[]{:S(2)}) collective-permute-start(bf16[64,512]{1,0:T(8,128)(2,1)S(1)} %get-tuple-element.112), channel_id=1, source_target_pairs={{0,1},{1,0},{2,3},{3,2},{4,5},{5,4},{6,7},{7,6},{8,9},{9,8},{10,11... | collective-permute-start | bytes 196616 | tf_op jit(solution)/shard_map/ppermute | solution.py:612

commit v17 on v16

--- a/solution.py
+++ b/solution.py
@@ -356,54 +356,77 @@
                 columns[0][...] = columns_of(digits[:fanout] * DIGIT + digits[fanout:])
 
 
-def layer_kernel(group, at_segment, fanout, rows, where, columns, *refs):
-    parts = len(rows)
+def roles(where, group, at_segment, late):
+    return swapped_roles(where, group, at_segment) if late else [(owns(where, group, at_segment), 0)]
+
+
+def early_kernel(group, at_segment, late, fanout, places, quarter, where, columns, *refs):
+    count = len(places)
+    senders, refs = refs[:count], refs[count:]
+    (own, coded), held, came, (piece, sender) = refs[:2], refs[2:6], refs[6:-2], refs[-2:]
+    rows = senders[0].shape[0]
+    for here, number in roles(where, group, at_segment, late):
+
+        @pl.when(here)
+        def _(number=number):
+            w_receive, _, w_own, w_edges = weights_of(came, held, number == 0)
+            sender[...] = jnp.zeros_like(sender)
+            for place, part in zip(places, senders):
+                sender[place * rows : (place + 1) * rows, :] = part[...]
+            state = own[:rows, :]
+            span = slice(quarter * rows, (quarter + 1) * rows)
+            gathered = sum_edges(fanout, columns[span, :], sender[...], state, w_receive)
+            piece[:rows, :] = update_nodes(state, gathered, w_own, w_edges)
+            if piece.shape[0] > rows:
+                piece[rows:, :] = coded[rows:, :]
+
+
+def layer_kernel(group, at_segment, fanout, places, quarter, where, columns, *refs):
+    parts = len(places)
     state, senders, refs = refs[:parts], refs[parts : 2 * parts - 1], refs[2 * parts - 1 :]
-    held, came, (renewed, whole, sender) = refs[:4], refs[4:6], refs[6:]
-    nodes = renewed.shape[0]
-    chunk = min(nodes, 256)
+    done, held, came, (renewed, whole, sender) = refs[0], refs[1:5], refs[5:7], refs[7:]
+    rows = done.shape[0]
+    spans = [slice(place * rows, (place + 1) * rows) for place in places]
+    own = slice(quarter * rows, (quarter + 1) * rows)
+    rest = [slice(0, own.start), slice(own.stop, renewed.shape[0])]
     for here, number in swapped_roles(where, group, at_segment):
 
         @pl.when(here)
         def _(number=number):
             w_receive, w_send, w_own, w_edges = weights_of(came, held, number == 0)
-            start = 0
-            for part, count in zip(state, rows):
-                whole[start : start + count, :] = part[:count, :]
-                start += count
-            start = 0
-            for part in senders:
-                sender[start : start + part.shape[0], :] = part[...]
-                start += part.shape[0]
-            sender[start:, :] = matmul(whole[start:, :], w_send).astype(jnp.bfloat16)
-            for start in range(0, nodes, chunk):
-                span = slice(start, start + chunk)
-                gathered = sum_edges(fanout, columns[span, :], sender[...], whole[span, :], w_receive)
-                renewed[span, :] = update_nodes(whole[span, :], gathered, w_own, w_edges)
-
-
-def open_kernel(group, at_segment, fanout, rows, where, columns, *refs):
-    parts = len(rows)
+            for span, part in zip(spans, state):
+                whole[span, :] = part[:rows, :]
+            for span, part in zip(spans, senders):
+                sender[span, :] = part[...]
+            sender[spans[-1], :] = matmul(whole[spans[-1], :], w_send).astype(jnp.bfloat16)
+            renewed[own, :] = done[...]
+            for span in rest:
+                if span.stop > span.start:
+                    gathered = sum_edges(fanout, columns[span, :], sender[...], whole[span, :], w_receive)
+                    renewed[span, :] = update_nodes(whole[span, :], gathered, w_own, w_edges)
+
+
+def open_kernel(group, at_segment, fanout, places, start, where, columns, *refs):
+    parts = len(places)
     state, senders, refs = refs[:parts], refs[parts : 2 * parts - 1], refs[2 * parts - 1 :]
     codes, (w_receive, w_send, w_own, w_edges), (sender, whole, piece) = refs[:-7], refs[-7:-3], refs[-3:]
+    rows = whole.shape[0] // parts
+    spans = [slice(place * rows, (place + 1) * rows) for place in places]
 
     @pl.when(owns(where, group, at_segment))
     def _():
-        start = 0
-        for part, count in zip(state, rows):
-            whole[start : start + count, :] = part[:count, :]
-            start += count
-        start = 0
-        for part in senders:
-            sender[start : start + part.shape[0], :] = part[...]
-            start += part.shape[0]
-        sender[start:, :] = matmul(whole[start:, :], w_send[...]).astype(jnp.bfloat16)
-        below = codes[0][...] if codes else state[0][rows[0] :, :]
-        count = piece.shape[0] - below.shape[0]
-        own = whole[:count, :]
-        gathered = sum_edges(fanout, columns[:count, :], sender[...], own, w_receive[...])
+        for span, part in zip(spans, state):
+            whole[span, :] = part[:rows, :]
+        for span, part in zip(spans, senders):
+            sender[span, :] = part[...]
+        sender[spans[-1], :] = matmul(whole[spans[-1], :], w_send[...]).astype(jnp.bfloat16)
+        count = piece.shape[0] - (codes[0].shape[0] if codes else 0)
+        span = slice(start, start + count)
+        own = whole[span, :]
+        gathered = sum_edges(fanout, columns[span, :], sender[...], own, w_receive[...])
         piece[:count, :] = update_nodes(own, gathered, w_own[...], w_edges[...])
-        piece[count:, :] = below
+        if codes:
+            piece[count:, :] = codes[0][...]
 
 
 def next_kernel(group, at_segment, fanout, start, where, columns, sender, whole, *refs):
@@ -685,27 +708,48 @@
         "wvv",
     )
     came = [came_project, send(pair, to_last)]
-    pieces, senders, rows, extra = [state], [], (nodes,), [codes]
-    for layer in range(last):
+    pieces, senders, places, early = [state], [], (0,), []
+    for layer in range(last + 1):
+        late = layer == last
         pairs = [(owner(m, layer), owner(m, segments if layer + 1 == last else layer + 1)) for m in range(samples)]
+        if layer == 0:
+            order, sent = list(range(samples)), []
+        else:
+            first = places[1]
+            order = [first] + [(first + step) % samples for step in range(1, samples)]
+            (piece,) = call(
+                functools.partial(early_kernel, group, layer, late, fanout, places[:-1], first),
+                "early",
+                [short if late else tall],
+                [where, columns] + senders + [pieces[1], pieces[0]] + held + came * late,
+                "w" + "v" * (3 + len(senders + held + came * late)),
+                [pltpu.VMEM((nodes, width), bf16)],
+            )
+            if late:
+                pieces[-1], piece = lax.optimization_barrier((pieces[-1], piece))
+                break
+            sent = [send(piece, pairs)]
+            pieces[-1], columns = lax.optimization_barrier((pieces[-1], columns))
+        start = order[len(sent)] * share
+        extra = [codes] * (layer == 0)
         sender, joined_state, piece = call(
-            functools.partial(open_kernel, group, layer, fanout, rows),
+            functools.partial(open_kernel, group, layer, fanout, places, start),
             "open",
-            [whole, whole, tall],
+            [whole, whole, tall if layer == 0 else short],
             [where, columns] + pieces + senders + extra + held,
             "w" + "v" * (1 + len(pieces + senders + extra + held)),
         )
-        sent = [send(piece, pairs)]
-        for start in range(share, nodes, share):
+        sent.append(send(piece, pairs))
+        for place_sent in order[len(sent) :]:
             (piece,) = call(
-                functools.partial(next_kernel, group, layer, fanout, start),
+                functools.partial(next_kernel, group, layer, fanout, place_sent * share),
                 "next",
                 [short],
                 [where, columns, sender, joined_state] + held,
                 "w" + "v" * (3 + len(held)),
             )
             sent.append(send(piece, pairs))
-        pieces, senders, rows, extra = sent, [], (share,) * samples, []
+        pieces, senders, places = sent, [], tuple(order)
         if layer == 0:
             ready, table = call(
                 prepare_kernel,
@@ -718,25 +762,26 @@
                 "wvvvv",
             )
             pieces[0], ready, table = lax.optimization_barrier((pieces[0], ready, table))
-        for piece in pieces[:-1]:
+        for number, part in enumerate(pieces[:-1]):
             if senders:
-                piece, senders[-1] = lax.optimization_barrier((piece, senders[-1]))
+                part, senders[-1] = lax.optimization_barrier((part, senders[-1]))
+                pieces[number] = part
             late = layer + 1 == last
             sender, *found = call(
                 functools.partial(late_sender_kernel if late else sender_kernel, group, layer + 1, fanout, share),
                 "sender",
                 [short] + [columns_shape] * (not senders),
-                [where, piece, held[1]] + came[:1] * late,
+                [where, part, held[1]] + came[:1] * late,
                 "wvv" + "v" * late,
             )
             columns = found[0] if found else columns
             senders.append(sender)
     (state,) = call(
-        functools.partial(layer_kernel, group, last, fanout, rows),
+        functools.partial(layer_kernel, group, last, fanout, places, order[0]),
         "layer",
         [whole],
-        [where, columns] + pieces + senders + held + came,
-        "w" + "v" * (1 + len(pieces + senders + held + came)),
+        [where, columns] + pieces + senders + [piece] + held + came,
+        "w" + "v" * (2 + len(pieces + senders + held + came)),
         [pltpu.VMEM((nodes, width), bf16)] * 2,
     )
     far = []
@@ -750,13 +795,15 @@
         )
         sender = found[0] if not far else sender
         far.append(found[-1])
-    near = call(
-        functools.partial(end_kernel, group, last, samples, False, 0, False, fanout),
-        "near_half",
-        [short] * (samples // 2),
-        [where, columns, state, sender] + held + came,
-        "w" + "v" * 9,
-    )
+    near = []
+    for begin in range(0, nodes // 2, share):
+        near += call(
+            functools.partial(end_kernel, group, last, samples, False, begin, False, fanout),
+            "near_part",
+            [short],
+            [where, columns, state, sender] + held + came,
+            "w" + "v" * 9,
+        )
     state = far + list(near)
     each = samples // 2
     arrived = []

time: 54.1 us -> 50.9 us (0.941); the launches traced: 53.9 us -> 50 us
  starting transfers between devices: 36.4 us -> 33 us
  waiting for transfers between devices: 10.6 us -> 10 us
    ppermute x14, starting transfers between devices: 27 us -> 24.9 us  [send(): lax.ppermute(value, ('segment', 'dom'), every_device(pairs, segments * pa...]
    ppermute x2, starting transfers between devices: 4.97 us -> 3.72 us  [change_lane(): return lax.ppermute(value, 'dom', pairs)]
    ppermute x14, waiting for transfers between devices: 8.05 us -> 7.5 us  [send(): lax.ppermute(value, ('segment', 'dom'), every_device(pairs, segments * pa...]
    pallas_call x28 -> x30, Pallas kernels: 3.2 us -> 3.21 us  [call(): pl.pallas_call(located if places[0] == 'w' else kernel, out_shape=shapes,...]
  transfers between devices with their start and end apart: 19 -> 19, of which waited for: 8 -> 7; matrix products, arithmetic and copies ran while one was open for 2% -> 2% of each run, Pallas kernels for 4% -> 4%
where the time goes in v17:
time: 50.9 us; the launch traced here: 50 us
  starting transfers between devices  33 us (65%)
  waiting for transfers between devices  10 us (20%)
  local copies, waits for them, and re-layouts  3.46 us (7%)
  Pallas kernels  3.21 us (6%)
    ppermute x14, starting transfers between devices, send(): lax.ppermute(value, ('segment', 'dom'), every_device(pairs, segments * pa...  24.9 us
    ppermute x14, waiting for transfers between devices, send(): lax.ppermute(value, ('segment', 'dom'), every_device(pairs, segments * pa...  7.5 us
    ppermute x3, starting transfers between devices, to_chip(): return lax.ppermute(value, ('segment', 'dom'), pairs)  4.36 us
    ppermute x2, starting transfers between devices, change_lane(): return lax.ppermute(value, 'dom', pairs)  3.72 us
    unnamed x23, local copies, waits for them, and re-layouts  3.46 us
    pallas_call x30, Pallas kernels, call(): pl.pallas_call(located if places[0] == 'w' else kernel, out_shape=shapes,...  3.21 us
    ppermute x2, waiting for transfers between devices, change_lane(): return lax.ppermute(value, 'dom', pairs)  2.52 us
  transfers between devices with their start and end apart: 19, of which 7 were waited for; matrix products, arithmetic and copies ran while one was open for 2% of the time, Pallas kernels for 4%

profile of v17, /device:TPU:3, one launch (start us, length us, event | category | flops | bytes accessed | tf_op | source)
XLA Modules:
  0.0 50.0 jit_solution(11720099717012549135)
XLA Ops:
  0.0 0.0 copy-start.10
  0.0 0.0 copy-start.3
  0.0 0.7 %collective-permute-start.4 = (bf16[1,512,1024]{2,1,0:T(8,128)(2,1)}, bf16[1,512,1024]{2,1,0:T(8,128)(2,1)S(1)}, u32[]{:S(2)}, u32[]{:S(2)}) collective-permute-start(bf16[1,512,1024]{2,1,0:T(8,128)(2,1)} %w_project), channel_id=1, source_target_pairs={{0,1},{1,0},{2,3},{3,2},{4,5},{5,4},{6,7},{7,6},{8,9},{9,8},{10,11... | collective-permute-start | bytes 3145736 | tf_op jit(solution)/shard_map/ppermute | solution.py:616
  0.8 1.0 %copy.15 = bf16[4,128,227]{1,2,0:T(8,128)(2,1)S(1)} copy(bf16[4,128,227]{1,0,2:T(4,128)(2,1)} %param.12) | data formatting | bytes 464896 | tf_op args[0]
  1.8 0.7 %encode.1 = (bf16[80,512]{1,0:T(8,128)(2,1)S(1)}, bf16[80,512]{1,0:T(8,128)(2,1)S(1)}, bf16[80,512]{1,0:T(8,128)(2,1)S(1)}, bf16[80,512]{1,0:T(8,128)(2,1)S(1)}) custom-call(s32[1]{0:T(128)} %bitcast.segment, s32[1]{0:T(128)} %bitcast.1.place, bf16[4,227,128]{2,1,0:T(8,128)(2,1)S(1)} %bitcast.13, bf16[227,512]{1,0:T(8,128)(2,1)S(1)} %copy-done.3, ...), custom_call_target="tpu_custom_call" | custom-call | bytes 799752 | tf_op jit(solution)/shard_map/encode/pallas_call | solution.py:552
  2.5 0.2 collective-permute-start
  2.7 3.4 %collective-permute-start.1 = (bf16[80,512]{1,0:T(8,128)(2,1)S(1)}, bf16[80,512]{1,0:T(8,128)(2,1)S(1)}, u32[]{:S(2)}, u32[]{:S(2)}) collective-permute-start(bf16[80,512]{1,0:T(8,128)(2,1)S(1)} %get-tuple-element.71), channel_id=1, source_target_pairs={{0,8},{1,9},{2,10},{3,11},{4,12},{5,13},{6,14},{7,15},{8,4},{9,5},... | collective-permute-start | bytes 245768 | tf_op jit(solution)/shard_map/ppermute | solution.py:631
  6.2 0.7 %collective-permute-start.2 = (bf16[80,512]{1,0:T(8,128)(2,1)S(1)}, bf16[80,512]{1,0:T(8,128)(2,1)S(1)}, u32[]{:S(2)}, u32[]{:S(2)}) collective-permute-start(bf16[80,512]{1,0:T(8,128)(2,1)S(1)} %get-tuple-element.72), channel_id=1, source_target_pairs={{0,16},{1,17},{2,18},{3,19},{4,20},{5,21},{6,22},{7,23},{8,9},{9,8... | collective-permute-start | bytes 245768 | tf_op jit(solution)/shard_map/ppermute | solution.py:631
  6.9 1.2 %copy-done.1 = bf16[1,1024,512]{2,1,0:T(8,128)(2,1)S(1)} copy-done((bf16[1,1024,512]{2,1,0:T(8,128)(2,1)S(1)}, bf16[1,1024,512]{2,1,0:T(8,128)(2,1)}, u32[]{:S(2)}) %copy-start.1) | copy-done | bytes 1048600
  8.1 1.2 %copy-done.2 = bf16[1,512,1024]{2,1,0:T(8,128)(2,1)S(1)} copy-done((bf16[1,512,1024]{2,1,0:T(8,128)(2,1)S(1)}, bf16[1,512,1024]{2,1,0:T(8,128)(2,1)}, u32[]{:S(2)}) %copy-start.2) | copy-done | bytes 1048600
  9.3 0.7 %hold.1 = (bf16[512,512]{1,0:T(8,128)(2,1)S(1)}, bf16[512,512]{1,0:T(8,128)(2,1)S(1)}, bf16[512,512]{1,0:T(8,128)(2,1)S(1)}, bf16[512,512]{1,0:T(8,128)(2,1)S(1)}) custom-call(bf16[1,512,1024]{2,1,0:T(8,128)(2,1)S(1)} %copy-done.2, bf16[1,512,512]{2,1,0:T(8,128)(2,1)S(1)} %copy-done.4, bf16[1,1024,512]{2,1,0:T(8,128)(2,1)S(1)} %copy-done.1), custom_call_target="tpu_custom_call" | custom-call | bytes 4718592 | tf_op jit(solution)/shard_map/hold/pallas_call | solution.py:552
  10.1 0.0 collective-permute-done.refs_1_
  10.1 0.0 collective-permute-done.1.refs_2_
  10.1 0.0 collective-permute-done.2.refs_3_
  10.2 0.1 collective-permute-start.3
  10.2 1.6 %collective-permute-done.3.refs_1_ = bf16[320,512]{1,0:T(8,128)(2,1)S(1)} collective-permute-done((bf16[320,512]{1,0:T(8,128)(2,1)S(1)}, bf16[320,512]{1,0:T(8,128)(2,1)S(1)}, u32[]{:S(2)}, u32[]{:S(2)}) %collective-permute-start.3) | collective-permute-done | bytes 327712 | tf_op jit(solution)/shard_map/ppermute | solution.py:635
  11.8 0.0 collective-permute-done.4.refs_2_.refs_10_.refs_13_.refs_6_.refs_7_
  11.9 0.1 collective-permute-start.13
  12.0 2.5 %collective-permute-start.5 = (bf16[144,512]{1,0:T(8,128)(2,1)S(1)}, bf16[144,512]{1,0:T(8,128)(2,1)S(1)}, u32[]{:S(2)}, u32[]{:S(2)}) collective-permute-start(bf16[144,512]{1,0:T(8,128)(2,1)S(1)} %get-tuple-element.85), channel_id=1, source_target_pairs={{0,8},{1,0},{2,10},{3,2},{4,12},{5,4},{6,14},{7,6},{8,9},{9,1},{10... | collective-permute-start | bytes 442376 | tf_op jit(solution)/shard_map/ppermute | solution.py:616
  14.5 1.7 %collective-permute-start.6 = (bf16[128,512]{1,0:T(8,128)(2,1)S(1)}, bf16[128,512]{1,0:T(8,128)(2,1)S(1)}, u32[]{:S(2)}, u32[]{:S(2)}) collective-permute-start(bf16[128,512]{1,0:T(8,128)(2,1)S(1)} %next.5), channel_id=1, source_target_pairs={{0,8},{1,0},{2,10},{3,2},{4,12},{5,4},{6,14},{7,6},{8,9},{9,1},{10... | collective-permute-start | bytes 393224 | tf_op jit(solution)/shard_map/ppermute | solution.py:616
  16.2 1.5 %collective-permute-start.7 = (bf16[128,512]{1,0:T(8,128)(2,1)S(1)}, bf16[128,512]{1,0:T(8,128)(2,1)S(1)}, u32[]{:S(2)}, u32[]{:S(2)}) collective-permute-start(bf16[128,512]{1,0:T(8,128)(2,1)S(1)} %next.6), channel_id=1, source_target_pairs={{0,8},{1,0},{2,10},{3,2},{4,12},{5,4},{6,14},{7,6},{8,9},{9,1},{10... | collective-permute-start | bytes 393224 | tf_op jit(solution)/shard_map/ppermute | solution.py:616
  17.7 1.5 %collective-permute-start.9 = (bf16[128,512]{1,0:T(8,128)(2,1)S(1)}, bf16[128,512]{1,0:T(8,128)(2,1)S(1)}, u32[]{:S(2)}, u32[]{:S(2)}) collective-permute-start(bf16[128,512]{1,0:T(8,128)(2,1)S(1)} %next.7), channel_id=1, source_target_pairs={{0,8},{1,0},{2,10},{3,2},{4,12},{5,4},{6,14},{7,6},{8,9},{9,1},{10... | collective-permute-start | bytes 393224 | tf_op jit(solution)/shard_map/ppermute | solution.py:616
  19.2 0.4 prepare.1
  19.6 0.0 collective-permute-done.5.refs_0_.refs_5_.refs_1_
  19.6 0.0 collective-permute-done.6.refs_0_.refs_4_.refs_2_
  19.7 0.0 collective-permute-done.7.refs_0_.refs_3_
  19.7 4.4 %collective-permute-start.8 = (bf16[144,512]{1,0:T(8,128)(2,1)S(1)}, bf16[144,512]{1,0:T(8,128)(2,1)S(1)}, u32[]{:S(2)}, u32[]{:S(2)}) collective-permute-start(bf16[144,512]{1,0:T(8,128)(2,1)S(1)} %early.2), channel_id=1, source_target_pairs={{0,1},{1,0},{2,3},{3,2},{4,5},{5,4},{6,7},{7,6},{8,16},{9,8},{10,2... | collective-permute-start | bytes 442376 | tf_op jit(solution)/shard_map/ppermute | solution.py:616
  24.1 0.0 collective-permute-done.9.refs_4_
  24.1 1.6 %collective-permute-start.10 = (bf16[128,512]{1,0:T(8,128)(2,1)S(1)}, bf16[128,512]{1,0:T(8,128)(2,1)S(1)}, u32[]{:S(2)}, u32[]{:S(2)}) collective-permute-start(bf16[128,512]{1,0:T(8,128)(2,1)S(1)} %get-tuple-element.103), channel_id=1, source_target_pairs={{0,1},{1,0},{2,3},{3,2},{4,5},{5,4},{6,7},{7,6},{8,16},{9,8},{10,2... | collective-permute-start | bytes 393224 | tf_op jit(solution)/shard_map/ppermute | solution.py:616
  25.6 1.5 %collective-permute-start.11 = (bf16[128,512]{1,0:T(8,128)(2,1)S(1)}, bf16[128,512]{1,0:T(8,128)(2,1)S(1)}, u32[]{:S(2)}, u32[]{:S(2)}) collective-permute-start(bf16[128,512]{1,0:T(8,128)(2,1)S(1)} %next.8), channel_id=1, source_target_pairs={{0,1},{1,0},{2,3},{3,2},{4,5},{5,4},{6,7},{7,6},{8,16},{9,8},{10,2... | collective-permute-start | bytes 393224 | tf_op jit(solution)/shard_map/ppermute | solution.py:616
  27.1 1.7 %collective-permute-start.12 = (bf16[128,512]{1,0:T(8,128)(2,1)S(1)}, bf16[128,512]{1,0:T(8,128)(2,1)S(1)}, u32[]{:S(2)}, u32[]{:S(2)}) collective-permute-start(bf16[128,512]{1,0:T(8,128)(2,1)S(1)} %next.9), channel_id=1, source_target_pairs={{0,1},{1,0},{2,3},{3,2},{4,5},{5,4},{6,7},{7,6},{8,16},{9,8},{10,2... | collective-permute-start | bytes 393224 | tf_op jit(solution)/shard_map/ppermute | solution.py:616
  28.8 1.4 %collective-permute-done.8.refs_0_.refs_5_.refs_1_ = bf16[144,512]{1,0:T(8,128)(2,1)S(1)} collective-permute-done((bf16[144,512]{1,0:T(8,128)(2,1)S(1)}, bf16[144,512]{1,0:T(8,128)(2,1)S(1)}, u32[]{:S(2)}, u32[]{:S(2)}) %collective-permute-start.8) | collective-permute-done | bytes 147488 | tf_op jit(solution)/shard_map/ppermute | solution.py:616
  30.1 1.4 %collective-permute-done.10.refs_0_.refs_4_.refs_2_ = bf16[128,512]{1,0:T(8,128)(2,1)S(1)} collective-permute-done((bf16[128,512]{1,0:T(8,128)(2,1)S(1)}, bf16[128,512]{1,0:T(8,128)(2,1)S(1)}, u32[]{:S(2)}, u32[]{:S(2)}) %collective-permute-start.10) | collective-permute-done | bytes 131104 | tf_op jit(solution)/shard_map/ppermute | solution.py:616
  31.5 1.4 %collective-permute-done.11.refs_0_.refs_3_ = bf16[128,512]{1,0:T(8,128)(2,1)S(1)} collective-permute-done((bf16[128,512]{1,0:T(8,128)(2,1)S(1)}, bf16[128,512]{1,0:T(8,128)(2,1)S(1)}, u32[]{:S(2)}, u32[]{:S(2)}) %collective-permute-start.11) | collective-permute-done | bytes 131104 | tf_op jit(solution)/shard_map/ppermute | solution.py:616
  33.0 0.0 collective-permute-done.13.refs_11_.refs_14_.refs_7_.refs_8_
  33.0 1.4 %collective-permute-done.12.refs_4_ = bf16[128,512]{1,0:T(8,128)(2,1)S(1)} collective-permute-done((bf16[128,512]{1,0:T(8,128)(2,1)S(1)}, bf16[128,512]{1,0:T(8,128)(2,1)S(1)}, u32[]{:S(2)}, u32[]{:S(2)}) %collective-permute-start.12) | collective-permute-done | bytes 131104 | tf_op jit(solution)/shard_map/ppermute | solution.py:616
  34.4 0.0 collective-permute-start.15
  34.4 0.5 %collective-permute-start.14 = (bf16[128,512]{1,0:T(8,128)(2,1)S(1)}, bf16[128,512]{1,0:T(8,128)(2,1)S(1)}, u32[]{:S(2)}, u32[]{:S(2)}) collective-permute-start(bf16[128,512]{1,0:T(8,128)(2,1)S(1)} %far_part.3), channel_id=1, source_target_pairs={{0,1},{1,0},{2,3},{3,2},{4,5},{5,4},{6,7},{7,17},{8,9},{9,8},{10,1... | collective-permute-start | bytes 393224 | tf_op jit(solution)/shard_map/ppermute | solution.py:616
  34.9 7.3 %collective-permute-start.16 = (bf16[128,512]{1,0:T(8,128)(2,1)S(1)}, bf16[128,512]{1,0:T(8,128)(2,1)S(1)}, u32[]{:S(2)}, u32[]{:S(2)}) collective-permute-start(bf16[128,512]{1,0:T(8,128)(2,1)S(1)} %near_part.2.refs_3_), channel_id=1, source_target_pairs={{0,1},{1,17},{2,3},{3,2},{4,5},{5,4},{6,7},{7,6},{8,9},{9,27},{10,... | collective-permute-start | bytes 393224 | tf_op jit(solution)/shard_map/ppermute | solution.py:616
  42.2 0.0 collective-permute-start.17
  42.2 0.0 collective-permute-done.15.refs_0_
  42.2 0.0 collective-permute-done.14.refs_0_
  42.2 0.0 copy-start.5
  42.2 1.9 %collective-permute-done.16.refs_1_ = bf16[128,512]{1,0:T(8,128)(2,1)S(1)} collective-permute-done((bf16[128,512]{1,0:T(8,128)(2,1)S(1)}, bf16[128,512]{1,0:T(8,128)(2,1)S(1)}, u32[]{:S(2)}, u32[]{:S(2)}) %collective-permute-start.16) | collective-permute-done | bytes 131104 | tf_op jit(solution)/shard_map/ppermute | solution.py:616
  44.1 0.0 collective-permute-done.17.refs_2_
  44.2 3.6 %collective-permute-start.18 = (bf16[64,512]{1,0:T(8,128)(2,1)S(1)}, bf16[64,512]{1,0:T(8,128)(2,1)S(1)}, u32[]{:S(2)}, u32[]{:S(2)}) collective-permute-start(bf16[64,512]{1,0:T(8,128)(2,1)S(1)} %get-tuple-element.116), channel_id=1, source_target_pairs={{0,1},{1,0},{2,3},{3,2},{4,5},{5,4},{6,7},{7,6},{8,9},{9,8},{10,11... | collective-permute-start | bytes 196616 | tf_op jit(solution)/shard_map/ppermute | solution.py:635
  47.8 0.9 %collective-permute-done.18.refs_5_ = bf16[64,512]{1,0:T(8,128)(2,1)S(1)} collective-permute-done((bf16[64,512]{1,0:T(8,128)(2,1)S(1)}, bf16[64,512]{1,0:T(8,128)(2,1)S(1)}, u32[]{:S(2)}, u32[]{:S(2)}) %collective-permute-start.18) | collective-permute-done | bytes 65568 | tf_op jit(solution)/shard_map/ppermute | solution.py:635
  48.7 1.2 %decode.1 = bf16[227,128]{1,0:T(8,128)(2,1)} custom-call(s32[1]{0:T(128)} %bitcast.segment, s32[1]{0:T(128)} %bitcast.1.place, f32[128,512]{1,0:T(8,128)S(1)} %get-tuple-element.88.refs_0_, bf16[64,128]{1,0:T(8,128)(2,1)S(1)} %get-tuple-element.89.refs_1_, bf16[1024,512]{1,0:T(8,128)(2,1)S(1)} %copy-done, bf16[227,512]{1,0:T(8,128)(2,1)S(1)} %bitcast.15, ...), custom_call_target="tpu_custom_call" | custom-call | bytes 1748744 | tf_op jit(solution)/shard_map/decode/pallas_call | solution.py:552
  (44 shorter events, 0.2 us)
Async XLA Ops:
  0.0 1.7 %copy-start.7 = (s32[64,8]{0,1:T(8,128)S(1)}, s32[64,8]{0,1:T(8,128)}, u32[]{:S(2)}) copy-start(s32[64,8]{0,1:T(8,128)} %param.21) | copy-start | bytes 6148
  0.0 1.8 %copy-start.8 = (s32[4,64]{1,0:T(4,128)S(1)}, s32[4,64]{1,0:T(4,128)}, u32[]{:S(2)}) copy-start(s32[4,64]{1,0:T(4,128)} %param.22) | copy-start | bytes 3076
  0.0 1.8 %copy-start.9 = (s32[4,1]{0,1:T(1,128)S(1)}, s32[4,1]{0,1:T(1,128)}, u32[]{:S(2)}) copy-start(s32[4,1]{0,1:T(1,128)} %param.23) | copy-start | bytes 52
  0.0 1.8 %copy-start.10 = (s32[128]{0:T(128)S(1)}, s32[128]{0:T(128)}, u32[]{:S(2)}) copy-start(s32[128]{0:T(128)} %param.19) | copy-start | bytes 1540
  0.0 1.8 %copy-start.3 = (bf16[227,512]{1,0:T(8,128)(2,1)S(1)}, bf16[227,512]{1,0:T(8,128)(2,1)}, u32[]{:S(2)}) copy-start(bf16[227,512]{1,0:T(8,128)(2,1)} %refs_1_.3) | copy-start | bytes 697348
  0.0 6.9 %copy-start.4 = (bf16[1,512,512]{2,1,0:T(8,128)(2,1)S(1)}, bf16[1,512,512]{2,1,0:T(8,128)(2,1)}, u32[]{:S(2)}) copy-start(bf16[1,512,512]{2,1,0:T(8,128)(2,1)} %w_message.1) | copy-start | bytes 1572868
  0.0 11.8 %collective-permute-start.4 = (bf16[1,512,1024]{2,1,0:T(8,128)(2,1)}, bf16[1,512,1024]{2,1,0:T(8,128)(2,1)S(1)}, u32[]{:S(2)}, u32[]{:S(2)}) collective-permute-start(bf16[1,512,1024]{2,1,0:T(8,128)(2,1)} %w_project), channel_id=1, source_target_pairs={{0,1},{1,0},{2,3},{3,2},{4,5},{5,4},{6,7},{7,6},{8,9},{9,8},{10,11... | collective-permute-start | bytes 3145736 | tf_op jit(solution)/shard_map/ppermute | solution.py:616
  2.5 7.6 %collective-permute-start = (bf16[80,512]{1,0:T(8,128)(2,1)S(1)}, bf16[80,512]{1,0:T(8,128)(2,1)S(1)}, u32[]{:S(2)}, u32[]{:S(2)}) collective-permute-start(bf16[80,512]{1,0:T(8,128)(2,1)S(1)} %get-tuple-element.70), channel_id=1, source_target_pairs={{0,2},{1,3},{2,0},{3,1},{4,6},{5,7},{6,4},{7,5},{8,9},{9,8},{10,11... | collective-permute-start | bytes 245768 | tf_op jit(solution)/shard_map/ppermute | solution.py:631
  2.7 7.4 %collective-permute-start.1 = (bf16[80,512]{1,0:T(8,128)(2,1)S(1)}, bf16[80,512]{1,0:T(8,128)(2,1)S(1)}, u32[]{:S(2)}, u32[]{:S(2)}) collective-permute-start(bf16[80,512]{1,0:T(8,128)(2,1)S(1)} %get-tuple-element.71), channel_id=1, source_target_pairs={{0,8},{1,9},{2,10},{3,11},{4,12},{5,13},{6,14},{7,15},{8,4},{9,5},... | collective-permute-start | bytes 245768 | tf_op jit(solution)/shard_map/ppermute | solution.py:631
  6.2 3.9 %collective-permute-start.2 = (bf16[80,512]{1,0:T(8,128)(2,1)S(1)}, bf16[80,512]{1,0:T(8,128)(2,1)S(1)}, u32[]{:S(2)}, u32[]{:S(2)}) collective-permute-start(bf16[80,512]{1,0:T(8,128)(2,1)S(1)} %get-tuple-element.72), channel_id=1, source_target_pairs={{0,16},{1,17},{2,18},{3,19},{4,20},{5,21},{6,22},{7,23},{8,9},{9,8... | collective-permute-start | bytes 245768 | tf_op jit(solution)/shard_map/ppermute | solution.py:631
  6.9 1.2 %copy-start.1 = (bf16[1,1024,512]{2,1,0:T(8,128)(2,1)S(1)}, bf16[1,1024,512]{2,1,0:T(8,128)(2,1)}, u32[]{:S(2)}) copy-start(bf16[1,1024,512]{2,1,0:T(8,128)(2,1)} %w_update.1) | copy-start | bytes 3145732
  8.1 1.2 %copy-start.2 = (bf16[1,512,1024]{2,1,0:T(8,128)(2,1)S(1)}, bf16[1,512,1024]{2,1,0:T(8,128)(2,1)}, u32[]{:S(2)}) copy-start(bf16[1,512,1024]{2,1,0:T(8,128)(2,1)} %w_project) | copy-start | bytes 3145732
  10.2 1.7 %collective-permute-start.3 = (bf16[320,512]{1,0:T(8,128)(2,1)S(1)}, bf16[320,512]{1,0:T(8,128)(2,1)S(1)}, u32[]{:S(2)}, u32[]{:S(2)}) collective-permute-start(bf16[320,512]{1,0:T(8,128)(2,1)S(1)} %join.1.refs_0_), channel_id=1, source_target_pairs={{0,1},{1,0},{2,3},{3,2},{4,5},{5,4},{6,7},{7,6},{8,9},{9,8},{10,11... | collective-permute-start | bytes 983048 | tf_op jit(solution)/shard_map/ppermute | solution.py:635
  11.9 21.1 %collective-permute-start.13 = (bf16[2,512,512]{2,1,0:T(8,128)(2,1)S(1)}, bf16[2,512,512]{2,1,0:T(8,128)(2,1)S(1)}, u32[]{:S(2)}, u32[]{:S(2)}) collective-permute-start(bf16[2,512,512]{2,1,0:T(8,128)(2,1)S(1)} %pack.1), channel_id=1, source_target_pairs={{0,1},{1,0},{2,3},{3,2},{4,5},{5,4},{6,7},{7,6},{8,9},{9,8},{10,11... | collective-permute-start | bytes 3145736 | tf_op jit(solution)/shard_map/ppermute | solution.py:616
  12.0 7.6 %collective-permute-start.5 = (bf16[144,512]{1,0:T(8,128)(2,1)S(1)}, bf16[144,512]{1,0:T(8,128)(2,1)S(1)}, u32[]{:S(2)}, u32[]{:S(2)}) collective-permute-start(bf16[144,512]{1,0:T(8,128)(2,1)S(1)} %get-tuple-element.85), channel_id=1, source_target_pairs={{0,8},{1,0},{2,10},{3,2},{4,12},{5,4},{6,14},{7,6},{8,9},{9,1},{10... | collective-permute-start | bytes 442376 | tf_op jit(solution)/shard_map/ppermute | solution.py:616
  14.5 5.1 %collective-permute-start.6 = (bf16[128,512]{1,0:T(8,128)(2,1)S(1)}, bf16[128,512]{1,0:T(8,128)(2,1)S(1)}, u32[]{:S(2)}, u32[]{:S(2)}) collective-permute-start(bf16[128,512]{1,0:T(8,128)(2,1)S(1)} %next.5), channel_id=1, source_target_pairs={{0,8},{1,0},{2,10},{3,2},{4,12},{5,4},{6,14},{7,6},{8,9},{9,1},{10... | collective-permute-start | bytes 393224 | tf_op jit(solution)/shard_map/ppermute | solution.py:616
  16.2 3.0 %copy-start = (bf16[1024,512]{1,0:T(8,128)(2,1)S(1)}, bf16[1024,512]{1,0:T(8,128)(2,1)}, u32[]{:S(2)}) copy-start(bf16[1024,512]{1,0:T(8,128)(2,1)} %refs_2_.3) | copy-start | bytes 3145732
  16.2 3.4 %collective-permute-start.7 = (bf16[128,512]{1,0:T(8,128)(2,1)S(1)}, bf16[128,512]{1,0:T(8,128)(2,1)S(1)}, u32[]{:S(2)}, u32[]{:S(2)}) collective-permute-start(bf16[128,512]{1,0:T(8,128)(2,1)S(1)} %next.6), channel_id=1, source_target_pairs={{0,8},{1,0},{2,10},{3,2},{4,12},{5,4},{6,14},{7,6},{8,9},{9,1},{10... | collective-permute-start | bytes 393224 | tf_op jit(solution)/shard_map/ppermute | solution.py:616
  17.7 1.5 %copy-start.6 = (s32[128]{0:T(128)S(1)}, s32[128]{0:T(128)}, u32[]{:S(2)}) copy-start(s32[128]{0:T(128)} %param.20) | copy-start | bytes 1540
  17.7 6.4 %collective-permute-start.9 = (bf16[128,512]{1,0:T(8,128)(2,1)S(1)}, bf16[128,512]{1,0:T(8,128)(2,1)S(1)}, u32[]{:S(2)}, u32[]{:S(2)}) collective-permute-start(bf16[128,512]{1,0:T(8,128)(2,1)S(1)} %next.7), channel_id=1, source_target_pairs={{0,8},{1,0},{2,10},{3,2},{4,12},{5,4},{6,14},{7,6},{8,9},{9,1},{10... | collective-permute-start | bytes 393224 | tf_op jit(solution)/shard_map/ppermute | solution.py:616
  19.7 10.4 %collective-permute-start.8 = (bf16[144,512]{1,0:T(8,128)(2,1)S(1)}, bf16[144,512]{1,0:T(8,128)(2,1)S(1)}, u32[]{:S(2)}, u32[]{:S(2)}) collective-permute-start(bf16[144,512]{1,0:T(8,128)(2,1)S(1)} %early.2), channel_id=1, source_target_pairs={{0,1},{1,0},{2,3},{3,2},{4,5},{5,4},{6,7},{7,6},{8,16},{9,8},{10,2... | collective-permute-start | bytes 442376 | tf_op jit(solution)/shard_map/ppermute | solution.py:616
  24.1 7.5 %collective-permute-start.10 = (bf16[128,512]{1,0:T(8,128)(2,1)S(1)}, bf16[128,512]{1,0:T(8,128)(2,1)S(1)}, u32[]{:S(2)}, u32[]{:S(2)}) collective-permute-start(bf16[128,512]{1,0:T(8,128)(2,1)S(1)} %get-tuple-element.103), channel_id=1, source_target_pairs={{0,1},{1,0},{2,3},{3,2},{4,5},{5,4},{6,7},{7,6},{8,16},{9,8},{10,2... | collective-permute-start | bytes 393224 | tf_op jit(solution)/shard_map/ppermute | solution.py:616
  25.6 7.3 %collective-permute-start.11 = (bf16[128,512]{1,0:T(8,128)(2,1)S(1)}, bf16[128,512]{1,0:T(8,128)(2,1)S(1)}, u32[]{:S(2)}, u32[]{:S(2)}) collective-permute-start(bf16[128,512]{1,0:T(8,128)(2,1)S(1)} %next.8), channel_id=1, source_target_pairs={{0,1},{1,0},{2,3},{3,2},{4,5},{5,4},{6,7},{7,6},{8,16},{9,8},{10,2... | collective-permute-start | bytes 393224 | tf_op jit(solution)/shard_map/ppermute | solution.py:616
  27.1 7.2 %collective-permute-start.12 = (bf16[128,512]{1,0:T(8,128)(2,1)S(1)}, bf16[128,512]{1,0:T(8,128)(2,1)S(1)}, u32[]{:S(2)}, u32[]{:S(2)}) collective-permute-start(bf16[128,512]{1,0:T(8,128)(2,1)S(1)} %next.9), channel_id=1, source_target_pairs={{0,1},{1,0},{2,3},{3,2},{4,5},{5,4},{6,7},{7,6},{8,16},{9,8},{10,2... | collective-permute-start | bytes 393224 | tf_op jit(solution)/shard_map/ppermute | solution.py:616
  34.4 7.8 %collective-permute-start.15 = (bf16[128,512]{1,0:T(8,128)(2,1)S(1)}, bf16[128,512]{1,0:T(8,128)(2,1)S(1)}, u32[]{:S(2)}, u32[]{:S(2)}) collective-permute-start(bf16[128,512]{1,0:T(8,128)(2,1)S(1)} %get-tuple-element.114), channel_id=1, source_target_pairs={{0,1},{1,0},{2,3},{3,2},{4,5},{5,21},{6,7},{7,6},{8,9},{9,8},{10,1... | collective-permute-start | bytes 393224 | tf_op jit(solution)/shard_map/ppermute | solution.py:616
  34.4 7.8 %collective-permute-start.14 = (bf16[128,512]{1,0:T(8,128)(2,1)S(1)}, bf16[128,512]{1,0:T(8,128)(2,1)S(1)}, u32[]{:S(2)}, u32[]{:S(2)}) collective-permute-start(bf16[128,512]{1,0:T(8,128)(2,1)S(1)} %far_part.3), channel_id=1, source_target_pairs={{0,1},{1,0},{2,3},{3,2},{4,5},{5,4},{6,7},{7,17},{8,9},{9,8},{10,1... | collective-permute-start | bytes 393224 | tf_op jit(solution)/shard_map/ppermute | solution.py:616
  34.9 9.3 %collective-permute-start.16 = (bf16[128,512]{1,0:T(8,128)(2,1)S(1)}, bf16[128,512]{1,0:T(8,128)(2,1)S(1)}, u32[]{:S(2)}, u32[]{:S(2)}) collective-permute-start(bf16[128,512]{1,0:T(8,128)(2,1)S(1)} %near_part.2.refs_3_), channel_id=1, source_target_pairs={{0,1},{1,17},{2,3},{3,2},{4,5},{5,4},{6,7},{7,6},{8,9},{9,27},{10,... | collective-permute-start | bytes 393224 | tf_op jit(solution)/shard_map/ppermute | solution.py:616
  42.2 2.0 %collective-permute-start.17 = (bf16[128,512]{1,0:T(8,128)(2,1)S(1)}, bf16[128,512]{1,0:T(8,128)(2,1)S(1)}, u32[]{:S(2)}, u32[]{:S(2)}) collective-permute-start(bf16[128,512]{1,0:T(8,128)(2,1)S(1)} %near_part.3.refs_4_), channel_id=1, source_target_pairs={{0,1},{1,0},{2,3},{3,17},{4,5},{5,4},{6,7},{7,6},{8,9},{9,8},{10,1... | collective-permute-start | bytes 393224 | tf_op jit(solution)/shard_map/ppermute | solution.py:616
  42.2 6.5 %copy-start.5 = (bf16[512,227]{0,1:T(8,128)(2,1)S(1)}, bf16[512,227]{0,1:T(8,128)(2,1)}, u32[]{:S(2)}) copy-start(bf16[512,227]{0,1:T(8,128)(2,1)} %param.18) | copy-start | bytes 697348
  44.2 4.5 %collective-permute-start.18 = (bf16[64,512]{1,0:T(8,128)(2,1)S(1)}, bf16[64,512]{1,0:T(8,128)(2,1)S(1)}, u32[]{:S(2)}, u32[]{:S(2)}) collective-permute-start(bf16[64,512]{1,0:T(8,128)(2,1)S(1)} %get-tuple-element.116), channel_id=1, source_target_pairs={{0,1},{1,0},{2,3},{3,2},{4,5},{5,4},{6,7},{7,6},{8,9},{9,8},{10,11... | collective-permute-start | bytes 196616 | tf_op jit(solution)/shard_map/ppermute | solution.py:635

commit v18 on v17

--- a/solution.py
+++ b/solution.py
@@ -324,8 +324,8 @@
         for number in range(nodes // tile):
             lane = number * fanout + k
             hits.append(jnp.where(columns[:, lane : lane + 1] == names, one_half, none))
-        half = receiver + matmul(jnp.concatenate(hits, axis=1), sender)
-        total = total + (half + half * jnp.tanh(half))
+        half = (receiver + matmul(jnp.concatenate(hits, axis=1), sender)).astype(jnp.bfloat16)
+        total = total + (half + half * jnp.tanh(half)).astype(jnp.float32)
     return (total * (1.0 / fanout)).astype(jnp.bfloat16)
 
 

time: 50.9 us -> 50.9 us (level)
  no operation moved by 1% of the time
where the time goes in v18:
time: 50.9 us; the launch traced here: 50 us
  starting transfers between devices  33 us (65%)
  waiting for transfers between devices  10 us (20%)
  local copies, waits for them, and re-layouts  3.46 us (7%)
  Pallas kernels  3.21 us (6%)
    ppermute x14, starting transfers between devices, send(): lax.ppermute(value, ('segment', 'dom'), every_device(pairs, segments * pa...  24.9 us
    ppermute x14, waiting for transfers between devices, send(): lax.ppermute(value, ('segment', 'dom'), every_device(pairs, segments * pa...  7.49 us
    ppermute x3, starting transfers between devices, to_chip(): return lax.ppermute(value, ('segment', 'dom'), pairs)  4.36 us
    ppermute x2, starting transfers between devices, change_lane(): return lax.ppermute(value, 'dom', pairs)  3.75 us
    unnamed x23, local copies, waits for them, and re-layouts  3.46 us
    pallas_call x30, Pallas kernels, call(): pl.pallas_call(located if places[0] == 'w' else kernel, out_shape=shapes,...  3.21 us
    ppermute x2, waiting for transfers between devices, change_lane(): return lax.ppermute(value, 'dom', pairs)  2.52 us
  transfers between devices with their start and end apart: 19, of which 7 were waited for; matrix products, arithmetic and copies ran while one was open for 2% of the time, Pallas kernels for 4%

profile of v18, /device:TPU:3, one launch (start us, length us, event | category | flops | bytes accessed | tf_op | source)
XLA Modules:
  0.0 50.0 jit_solution(14521331777392346894)
XLA Ops:
  0.0 0.7 %collective-permute-start.4 = (bf16[1,512,1024]{2,1,0:T(8,128)(2,1)}, bf16[1,512,1024]{2,1,0:T(8,128)(2,1)S(1)}, u32[]{:S(2)}, u32[]{:S(2)}) collective-permute-start(bf16[1,512,1024]{2,1,0:T(8,128)(2,1)} %w_project), channel_id=1, source_target_pairs={{0,1},{1,0},{2,3},{3,2},{4,5},{5,4},{6,7},{7,6},{8,9},{9,8},{10,11... | collective-permute-start | bytes 3145736 | tf_op jit(solution)/shard_map/ppermute | solution.py:616
  0.8 1.0 %copy.15 = bf16[4,128,227]{1,2,0:T(8,128)(2,1)S(1)} copy(bf16[4,128,227]{1,0,2:T(4,128)(2,1)} %param.12) | data formatting | bytes 464896 | tf_op args[0]
  1.7 0.0 copy-done.7
  1.8 0.0 copy-done.8
  1.8 0.7 %encode.1 = (bf16[80,512]{1,0:T(8,128)(2,1)S(1)}, bf16[80,512]{1,0:T(8,128)(2,1)S(1)}, bf16[80,512]{1,0:T(8,128)(2,1)S(1)}, bf16[80,512]{1,0:T(8,128)(2,1)S(1)}) custom-call(s32[1]{0:T(128)} %bitcast.segment, s32[1]{0:T(128)} %bitcast.1.place, bf16[4,227,128]{2,1,0:T(8,128)(2,1)S(1)} %bitcast.13, bf16[227,512]{1,0:T(8,128)(2,1)S(1)} %copy-done.3, ...), custom_call_target="tpu_custom_call" | custom-call | bytes 799752 | tf_op jit(solution)/shard_map/encode/pallas_call | solution.py:552
  2.5 0.2 collective-permute-start
  2.7 3.4 %collective-permute-start.1 = (bf16[80,512]{1,0:T(8,128)(2,1)S(1)}, bf16[80,512]{1,0:T(8,128)(2,1)S(1)}, u32[]{:S(2)}, u32[]{:S(2)}) collective-permute-start(bf16[80,512]{1,0:T(8,128)(2,1)S(1)} %get-tuple-element.71), channel_id=1, source_target_pairs={{0,8},{1,9},{2,10},{3,11},{4,12},{5,13},{6,14},{7,15},{8,4},{9,5},... | collective-permute-start | bytes 245768 | tf_op jit(solution)/shard_map/ppermute | solution.py:631
  6.2 0.7 %collective-permute-start.2 = (bf16[80,512]{1,0:T(8,128)(2,1)S(1)}, bf16[80,512]{1,0:T(8,128)(2,1)S(1)}, u32[]{:S(2)}, u32[]{:S(2)}) collective-permute-start(bf16[80,512]{1,0:T(8,128)(2,1)S(1)} %get-tuple-element.72), channel_id=1, source_target_pairs={{0,16},{1,17},{2,18},{3,19},{4,20},{5,21},{6,22},{7,23},{8,9},{9,8... | collective-permute-start | bytes 245768 | tf_op jit(solution)/shard_map/ppermute | solution.py:631
  6.9 1.2 %copy-done.1 = bf16[1,1024,512]{2,1,0:T(8,128)(2,1)S(1)} copy-done((bf16[1,1024,512]{2,1,0:T(8,128)(2,1)S(1)}, bf16[1,1024,512]{2,1,0:T(8,128)(2,1)}, u32[]{:S(2)}) %copy-start.1) | copy-done | bytes 1048600
  8.1 1.2 %copy-done.2 = bf16[1,512,1024]{2,1,0:T(8,128)(2,1)S(1)} copy-done((bf16[1,512,1024]{2,1,0:T(8,128)(2,1)S(1)}, bf16[1,512,1024]{2,1,0:T(8,128)(2,1)}, u32[]{:S(2)}) %copy-start.2) | copy-done | bytes 1048600
  9.3 0.7 %hold.1 = (bf16[512,512]{1,0:T(8,128)(2,1)S(1)}, bf16[512,512]{1,0:T(8,128)(2,1)S(1)}, bf16[512,512]{1,0:T(8,128)(2,1)S(1)}, bf16[512,512]{1,0:T(8,128)(2,1)S(1)}) custom-call(bf16[1,512,1024]{2,1,0:T(8,128)(2,1)S(1)} %copy-done.2, bf16[1,512,512]{2,1,0:T(8,128)(2,1)S(1)} %copy-done.4, bf16[1,1024,512]{2,1,0:T(8,128)(2,1)S(1)} %copy-done.1), custom_call_target="tpu_custom_call" | custom-call | bytes 4718592 | tf_op jit(solution)/shard_map/hold/pallas_call | solution.py:552
  10.1 0.0 collective-permute-done.refs_1_
  10.1 0.0 collective-permute-done.1.refs_2_
  10.1 0.0 collective-permute-done.2.refs_3_
  10.2 0.1 collective-permute-start.3
  10.2 1.6 %collective-permute-done.3.refs_1_ = bf16[320,512]{1,0:T(8,128)(2,1)S(1)} collective-permute-done((bf16[320,512]{1,0:T(8,128)(2,1)S(1)}, bf16[320,512]{1,0:T(8,128)(2,1)S(1)}, u32[]{:S(2)}, u32[]{:S(2)}) %collective-permute-start.3) | collective-permute-done | bytes 327712 | tf_op jit(solution)/shard_map/ppermute | solution.py:635
  11.8 0.0 collective-permute-done.4.refs_2_.refs_10_.refs_13_.refs_6_.refs_7_
  11.9 0.1 collective-permute-start.13
  12.0 2.5 %collective-permute-start.5 = (bf16[144,512]{1,0:T(8,128)(2,1)S(1)}, bf16[144,512]{1,0:T(8,128)(2,1)S(1)}, u32[]{:S(2)}, u32[]{:S(2)}) collective-permute-start(bf16[144,512]{1,0:T(8,128)(2,1)S(1)} %get-tuple-element.85), channel_id=1, source_target_pairs={{0,8},{1,0},{2,10},{3,2},{4,12},{5,4},{6,14},{7,6},{8,9},{9,1},{10... | collective-permute-start | bytes 442376 | tf_op jit(solution)/shard_map/ppermute | solution.py:616
  14.5 1.7 %collective-permute-start.6 = (bf16[128,512]{1,0:T(8,128)(2,1)S(1)}, bf16[128,512]{1,0:T(8,128)(2,1)S(1)}, u32[]{:S(2)}, u32[]{:S(2)}) collective-permute-start(bf16[128,512]{1,0:T(8,128)(2,1)S(1)} %next.5), channel_id=1, source_target_pairs={{0,8},{1,0},{2,10},{3,2},{4,12},{5,4},{6,14},{7,6},{8,9},{9,1},{10... | collective-permute-start | bytes 393224 | tf_op jit(solution)/shard_map/ppermute | solution.py:616
  16.2 1.5 %collective-permute-start.7 = (bf16[128,512]{1,0:T(8,128)(2,1)S(1)}, bf16[128,512]{1,0:T(8,128)(2,1)S(1)}, u32[]{:S(2)}, u32[]{:S(2)}) collective-permute-start(bf16[128,512]{1,0:T(8,128)(2,1)S(1)} %next.6), channel_id=1, source_target_pairs={{0,8},{1,0},{2,10},{3,2},{4,12},{5,4},{6,14},{7,6},{8,9},{9,1},{10... | collective-permute-start | bytes 393224 | tf_op jit(solution)/shard_map/ppermute | solution.py:616
  17.7 1.5 %collective-permute-start.9 = (bf16[128,512]{1,0:T(8,128)(2,1)S(1)}, bf16[128,512]{1,0:T(8,128)(2,1)S(1)}, u32[]{:S(2)}, u32[]{:S(2)}) collective-permute-start(bf16[128,512]{1,0:T(8,128)(2,1)S(1)} %next.7), channel_id=1, source_target_pairs={{0,8},{1,0},{2,10},{3,2},{4,12},{5,4},{6,14},{7,6},{8,9},{9,1},{10... | collective-permute-start | bytes 393224 | tf_op jit(solution)/shard_map/ppermute | solution.py:616
  19.1 0.4 prepare.1
  19.6 0.0 collective-permute-done.5.refs_0_.refs_5_.refs_1_
  19.6 0.0 collective-permute-done.6.refs_0_.refs_4_.refs_2_
  19.6 0.0 collective-permute-done.7.refs_0_.refs_3_
  19.7 4.4 %collective-permute-start.8 = (bf16[144,512]{1,0:T(8,128)(2,1)S(1)}, bf16[144,512]{1,0:T(8,128)(2,1)S(1)}, u32[]{:S(2)}, u32[]{:S(2)}) collective-permute-start(bf16[144,512]{1,0:T(8,128)(2,1)S(1)} %early.2), channel_id=1, source_target_pairs={{0,1},{1,0},{2,3},{3,2},{4,5},{5,4},{6,7},{7,6},{8,16},{9,8},{10,2... | collective-permute-start | bytes 442376 | tf_op jit(solution)/shard_map/ppermute | solution.py:616
  24.1 0.0 collective-permute-done.9.refs_4_
  24.1 1.6 %collective-permute-start.10 = (bf16[128,512]{1,0:T(8,128)(2,1)S(1)}, bf16[128,512]{1,0:T(8,128)(2,1)S(1)}, u32[]{:S(2)}, u32[]{:S(2)}) collective-permute-start(bf16[128,512]{1,0:T(8,128)(2,1)S(1)} %get-tuple-element.103), channel_id=1, source_target_pairs={{0,1},{1,0},{2,3},{3,2},{4,5},{5,4},{6,7},{7,6},{8,16},{9,8},{10,2... | collective-permute-start | bytes 393224 | tf_op jit(solution)/shard_map/ppermute | solution.py:616
  25.7 1.5 %collective-permute-start.11 = (bf16[128,512]{1,0:T(8,128)(2,1)S(1)}, bf16[128,512]{1,0:T(8,128)(2,1)S(1)}, u32[]{:S(2)}, u32[]{:S(2)}) collective-permute-start(bf16[128,512]{1,0:T(8,128)(2,1)S(1)} %next.8), channel_id=1, source_target_pairs={{0,1},{1,0},{2,3},{3,2},{4,5},{5,4},{6,7},{7,6},{8,16},{9,8},{10,2... | collective-permute-start | bytes 393224 | tf_op jit(solution)/shard_map/ppermute | solution.py:616
  27.1 1.6 %collective-permute-start.12 = (bf16[128,512]{1,0:T(8,128)(2,1)S(1)}, bf16[128,512]{1,0:T(8,128)(2,1)S(1)}, u32[]{:S(2)}, u32[]{:S(2)}) collective-permute-start(bf16[128,512]{1,0:T(8,128)(2,1)S(1)} %next.9), channel_id=1, source_target_pairs={{0,1},{1,0},{2,3},{3,2},{4,5},{5,4},{6,7},{7,6},{8,16},{9,8},{10,2... | collective-permute-start | bytes 393224 | tf_op jit(solution)/shard_map/ppermute | solution.py:616
  28.8 1.4 %collective-permute-done.8.refs_0_.refs_5_.refs_1_ = bf16[144,512]{1,0:T(8,128)(2,1)S(1)} collective-permute-done((bf16[144,512]{1,0:T(8,128)(2,1)S(1)}, bf16[144,512]{1,0:T(8,128)(2,1)S(1)}, u32[]{:S(2)}, u32[]{:S(2)}) %collective-permute-start.8) | collective-permute-done | bytes 147488 | tf_op jit(solution)/shard_map/ppermute | solution.py:616
  30.1 1.4 %collective-permute-done.10.refs_0_.refs_4_.refs_2_ = bf16[128,512]{1,0:T(8,128)(2,1)S(1)} collective-permute-done((bf16[128,512]{1,0:T(8,128)(2,1)S(1)}, bf16[128,512]{1,0:T(8,128)(2,1)S(1)}, u32[]{:S(2)}, u32[]{:S(2)}) %collective-permute-start.10) | collective-permute-done | bytes 131104 | tf_op jit(solution)/shard_map/ppermute | solution.py:616
  31.5 1.4 %collective-permute-done.11.refs_0_.refs_3_ = bf16[128,512]{1,0:T(8,128)(2,1)S(1)} collective-permute-done((bf16[128,512]{1,0:T(8,128)(2,1)S(1)}, bf16[128,512]{1,0:T(8,128)(2,1)S(1)}, u32[]{:S(2)}, u32[]{:S(2)}) %collective-permute-start.11) | collective-permute-done | bytes 131104 | tf_op jit(solution)/shard_map/ppermute | solution.py:616
  33.0 0.0 collective-permute-done.13.refs_11_.refs_14_.refs_7_.refs_8_
  33.0 1.4 %collective-permute-done.12.refs_4_ = bf16[128,512]{1,0:T(8,128)(2,1)S(1)} collective-permute-done((bf16[128,512]{1,0:T(8,128)(2,1)S(1)}, bf16[128,512]{1,0:T(8,128)(2,1)S(1)}, u32[]{:S(2)}, u32[]{:S(2)}) %collective-permute-start.12) | collective-permute-done | bytes 131104 | tf_op jit(solution)/shard_map/ppermute | solution.py:616
  34.4 0.0 collective-permute-start.15
  34.4 0.5 %collective-permute-start.14 = (bf16[128,512]{1,0:T(8,128)(2,1)S(1)}, bf16[128,512]{1,0:T(8,128)(2,1)S(1)}, u32[]{:S(2)}, u32[]{:S(2)}) collective-permute-start(bf16[128,512]{1,0:T(8,128)(2,1)S(1)} %far_part.3), channel_id=1, source_target_pairs={{0,1},{1,0},{2,3},{3,2},{4,5},{5,4},{6,7},{7,17},{8,9},{9,8},{10,1... | collective-permute-start | bytes 393224 | tf_op jit(solution)/shard_map/ppermute | solution.py:616
  34.9 7.3 %collective-permute-start.16 = (bf16[128,512]{1,0:T(8,128)(2,1)S(1)}, bf16[128,512]{1,0:T(8,128)(2,1)S(1)}, u32[]{:S(2)}, u32[]{:S(2)}) collective-permute-start(bf16[128,512]{1,0:T(8,128)(2,1)S(1)} %near_part.2.refs_3_), channel_id=1, source_target_pairs={{0,1},{1,17},{2,3},{3,2},{4,5},{5,4},{6,7},{7,6},{8,9},{9,27},{10,... | collective-permute-start | bytes 393224 | tf_op jit(solution)/shard_map/ppermute | solution.py:616
  42.2 0.0 collective-permute-start.17
  42.2 0.0 collective-permute-done.15.refs_0_
  42.2 0.0 collective-permute-done.14.refs_0_
  42.2 0.0 copy-start.5
  42.2 1.9 %collective-permute-done.16.refs_1_ = bf16[128,512]{1,0:T(8,128)(2,1)S(1)} collective-permute-done((bf16[128,512]{1,0:T(8,128)(2,1)S(1)}, bf16[128,512]{1,0:T(8,128)(2,1)S(1)}, u32[]{:S(2)}, u32[]{:S(2)}) %collective-permute-start.16) | collective-permute-done | bytes 131104 | tf_op jit(solution)/shard_map/ppermute | solution.py:616
  44.1 0.0 collective-permute-done.17.refs_2_
  44.2 3.7 %collective-permute-start.18 = (bf16[64,512]{1,0:T(8,128)(2,1)S(1)}, bf16[64,512]{1,0:T(8,128)(2,1)S(1)}, u32[]{:S(2)}, u32[]{:S(2)}) collective-permute-start(bf16[64,512]{1,0:T(8,128)(2,1)S(1)} %get-tuple-element.116), channel_id=1, source_target_pairs={{0,1},{1,0},{2,3},{3,2},{4,5},{5,4},{6,7},{7,6},{8,9},{9,8},{10,11... | collective-permute-start | bytes 196616 | tf_op jit(solution)/shard_map/ppermute | solution.py:635
  47.8 0.9 %collective-permute-done.18.refs_5_ = bf16[64,512]{1,0:T(8,128)(2,1)S(1)} collective-permute-done((bf16[64,512]{1,0:T(8,128)(2,1)S(1)}, bf16[64,512]{1,0:T(8,128)(2,1)S(1)}, u32[]{:S(2)}, u32[]{:S(2)}) %collective-permute-start.18) | collective-permute-done | bytes 65568 | tf_op jit(solution)/shard_map/ppermute | solution.py:635
  48.7 1.2 %decode.1 = bf16[227,128]{1,0:T(8,128)(2,1)} custom-call(s32[1]{0:T(128)} %bitcast.segment, s32[1]{0:T(128)} %bitcast.1.place, f32[128,512]{1,0:T(8,128)S(1)} %get-tuple-element.88.refs_0_, bf16[64,128]{1,0:T(8,128)(2,1)S(1)} %get-tuple-element.89.refs_1_, bf16[1024,512]{1,0:T(8,128)(2,1)S(1)} %copy-done, bf16[227,512]{1,0:T(8,128)(2,1)S(1)} %bitcast.15, ...), custom_call_target="tpu_custom_call" | custom-call | bytes 1748744 | tf_op jit(solution)/shard_map/decode/pallas_call | solution.py:552
  (44 shorter events, 0.2 us)
Async XLA Ops:
  0.0 1.7 %copy-start.7 = (s32[64,8]{0,1:T(8,128)S(1)}, s32[64,8]{0,1:T(8,128)}, u32[]{:S(2)}) copy-start(s32[64,8]{0,1:T(8,128)} %param.21) | copy-start | bytes 6148
  0.0 1.8 %copy-start.8 = (s32[4,64]{1,0:T(4,128)S(1)}, s32[4,64]{1,0:T(4,128)}, u32[]{:S(2)}) copy-start(s32[4,64]{1,0:T(4,128)} %param.22) | copy-start | bytes 3076
  0.0 1.8 %copy-start.9 = (s32[4,1]{0,1:T(1,128)S(1)}, s32[4,1]{0,1:T(1,128)}, u32[]{:S(2)}) copy-start(s32[4,1]{0,1:T(1,128)} %param.23) | copy-start | bytes 52
  0.0 1.8 %copy-start.10 = (s32[128]{0:T(128)S(1)}, s32[128]{0:T(128)}, u32[]{:S(2)}) copy-start(s32[128]{0:T(128)} %param.19) | copy-start | bytes 1540
  0.0 1.8 %copy-start.3 = (bf16[227,512]{1,0:T(8,128)(2,1)S(1)}, bf16[227,512]{1,0:T(8,128)(2,1)}, u32[]{:S(2)}) copy-start(bf16[227,512]{1,0:T(8,128)(2,1)} %refs_1_.3) | copy-start | bytes 697348
  0.0 6.9 %copy-start.4 = (bf16[1,512,512]{2,1,0:T(8,128)(2,1)S(1)}, bf16[1,512,512]{2,1,0:T(8,128)(2,1)}, u32[]{:S(2)}) copy-start(bf16[1,512,512]{2,1,0:T(8,128)(2,1)} %w_message.1) | copy-start | bytes 1572868
  0.0 11.8 %collective-permute-start.4 = (bf16[1,512,1024]{2,1,0:T(8,128)(2,1)}, bf16[1,512,1024]{2,1,0:T(8,128)(2,1)S(1)}, u32[]{:S(2)}, u32[]{:S(2)}) collective-permute-start(bf16[1,512,1024]{2,1,0:T(8,128)(2,1)} %w_project), channel_id=1, source_target_pairs={{0,1},{1,0},{2,3},{3,2},{4,5},{5,4},{6,7},{7,6},{8,9},{9,8},{10,11... | collective-permute-start | bytes 3145736 | tf_op jit(solution)/shard_map/ppermute | solution.py:616
  2.5 7.6 %collective-permute-start = (bf16[80,512]{1,0:T(8,128)(2,1)S(1)}, bf16[80,512]{1,0:T(8,128)(2,1)S(1)}, u32[]{:S(2)}, u32[]{:S(2)}) collective-permute-start(bf16[80,512]{1,0:T(8,128)(2,1)S(1)} %get-tuple-element.70), channel_id=1, source_target_pairs={{0,2},{1,3},{2,0},{3,1},{4,6},{5,7},{6,4},{7,5},{8,9},{9,8},{10,11... | collective-permute-start | bytes 245768 | tf_op jit(solution)/shard_map/ppermute | solution.py:631
  2.7 7.4 %collective-permute-start.1 = (bf16[80,512]{1,0:T(8,128)(2,1)S(1)}, bf16[80,512]{1,0:T(8,128)(2,1)S(1)}, u32[]{:S(2)}, u32[]{:S(2)}) collective-permute-start(bf16[80,512]{1,0:T(8,128)(2,1)S(1)} %get-tuple-element.71), channel_id=1, source_target_pairs={{0,8},{1,9},{2,10},{3,11},{4,12},{5,13},{6,14},{7,15},{8,4},{9,5},... | collective-permute-start | bytes 245768 | tf_op jit(solution)/shard_map/ppermute | solution.py:631
  6.2 3.9 %collective-permute-start.2 = (bf16[80,512]{1,0:T(8,128)(2,1)S(1)}, bf16[80,512]{1,0:T(8,128)(2,1)S(1)}, u32[]{:S(2)}, u32[]{:S(2)}) collective-permute-start(bf16[80,512]{1,0:T(8,128)(2,1)S(1)} %get-tuple-element.72), channel_id=1, source_target_pairs={{0,16},{1,17},{2,18},{3,19},{4,20},{5,21},{6,22},{7,23},{8,9},{9,8... | collective-permute-start | bytes 245768 | tf_op jit(solution)/shard_map/ppermute | solution.py:631
  6.9 1.2 %copy-start.1 = (bf16[1,1024,512]{2,1,0:T(8,128)(2,1)S(1)}, bf16[1,1024,512]{2,1,0:T(8,128)(2,1)}, u32[]{:S(2)}) copy-start(bf16[1,1024,512]{2,1,0:T(8,128)(2,1)} %w_update.1) | copy-start | bytes 3145732
  8.1 1.2 %copy-start.2 = (bf16[1,512,1024]{2,1,0:T(8,128)(2,1)S(1)}, bf16[1,512,1024]{2,1,0:T(8,128)(2,1)}, u32[]{:S(2)}) copy-start(bf16[1,512,1024]{2,1,0:T(8,128)(2,1)} %w_project) | copy-start | bytes 3145732
  10.2 1.7 %collective-permute-start.3 = (bf16[320,512]{1,0:T(8,128)(2,1)S(1)}, bf16[320,512]{1,0:T(8,128)(2,1)S(1)}, u32[]{:S(2)}, u32[]{:S(2)}) collective-permute-start(bf16[320,512]{1,0:T(8,128)(2,1)S(1)} %join.1.refs_0_), channel_id=1, source_target_pairs={{0,1},{1,0},{2,3},{3,2},{4,5},{5,4},{6,7},{7,6},{8,9},{9,8},{10,11... | collective-permute-start | bytes 983048 | tf_op jit(solution)/shard_map/ppermute | solution.py:635
  11.9 21.1 %collective-permute-start.13 = (bf16[2,512,512]{2,1,0:T(8,128)(2,1)S(1)}, bf16[2,512,512]{2,1,0:T(8,128)(2,1)S(1)}, u32[]{:S(2)}, u32[]{:S(2)}) collective-permute-start(bf16[2,512,512]{2,1,0:T(8,128)(2,1)S(1)} %pack.1), channel_id=1, source_target_pairs={{0,1},{1,0},{2,3},{3,2},{4,5},{5,4},{6,7},{7,6},{8,9},{9,8},{10,11... | collective-permute-start | bytes 3145736 | tf_op jit(solution)/shard_map/ppermute | solution.py:616
  12.0 7.6 %collective-permute-start.5 = (bf16[144,512]{1,0:T(8,128)(2,1)S(1)}, bf16[144,512]{1,0:T(8,128)(2,1)S(1)}, u32[]{:S(2)}, u32[]{:S(2)}) collective-permute-start(bf16[144,512]{1,0:T(8,128)(2,1)S(1)} %get-tuple-element.85), channel_id=1, source_target_pairs={{0,8},{1,0},{2,10},{3,2},{4,12},{5,4},{6,14},{7,6},{8,9},{9,1},{10... | collective-permute-start | bytes 442376 | tf_op jit(solution)/shard_map/ppermute | solution.py:616
  14.5 5.1 %collective-permute-start.6 = (bf16[128,512]{1,0:T(8,128)(2,1)S(1)}, bf16[128,512]{1,0:T(8,128)(2,1)S(1)}, u32[]{:S(2)}, u32[]{:S(2)}) collective-permute-start(bf16[128,512]{1,0:T(8,128)(2,1)S(1)} %next.5), channel_id=1, source_target_pairs={{0,8},{1,0},{2,10},{3,2},{4,12},{5,4},{6,14},{7,6},{8,9},{9,1},{10... | collective-permute-start | bytes 393224 | tf_op jit(solution)/shard_map/ppermute | solution.py:616
  16.2 2.9 %copy-start = (bf16[1024,512]{1,0:T(8,128)(2,1)S(1)}, bf16[1024,512]{1,0:T(8,128)(2,1)}, u32[]{:S(2)}) copy-start(bf16[1024,512]{1,0:T(8,128)(2,1)} %refs_2_.3) | copy-start | bytes 3145732
  16.2 3.4 %collective-permute-start.7 = (bf16[128,512]{1,0:T(8,128)(2,1)S(1)}, bf16[128,512]{1,0:T(8,128)(2,1)S(1)}, u32[]{:S(2)}, u32[]{:S(2)}) collective-permute-start(bf16[128,512]{1,0:T(8,128)(2,1)S(1)} %next.6), channel_id=1, source_target_pairs={{0,8},{1,0},{2,10},{3,2},{4,12},{5,4},{6,14},{7,6},{8,9},{9,1},{10... | collective-permute-start | bytes 393224 | tf_op jit(solution)/shard_map/ppermute | solution.py:616
  17.7 1.5 %copy-start.6 = (s32[128]{0:T(128)S(1)}, s32[128]{0:T(128)}, u32[]{:S(2)}) copy-start(s32[128]{0:T(128)} %param.20) | copy-start | bytes 1540
  17.7 6.4 %collective-permute-start.9 = (bf16[128,512]{1,0:T(8,128)(2,1)S(1)}, bf16[128,512]{1,0:T(8,128)(2,1)S(1)}, u32[]{:S(2)}, u32[]{:S(2)}) collective-permute-start(bf16[128,512]{1,0:T(8,128)(2,1)S(1)} %next.7), channel_id=1, source_target_pairs={{0,8},{1,0},{2,10},{3,2},{4,12},{5,4},{6,14},{7,6},{8,9},{9,1},{10... | collective-permute-start | bytes 393224 | tf_op jit(solution)/shard_map/ppermute | solution.py:616
  19.7 10.5 %collective-permute-start.8 = (bf16[144,512]{1,0:T(8,128)(2,1)S(1)}, bf16[144,512]{1,0:T(8,128)(2,1)S(1)}, u32[]{:S(2)}, u32[]{:S(2)}) collective-permute-start(bf16[144,512]{1,0:T(8,128)(2,1)S(1)} %early.2), channel_id=1, source_target_pairs={{0,1},{1,0},{2,3},{3,2},{4,5},{5,4},{6,7},{7,6},{8,16},{9,8},{10,2... | collective-permute-start | bytes 442376 | tf_op jit(solution)/shard_map/ppermute | solution.py:616
  24.1 7.4 %collective-permute-start.10 = (bf16[128,512]{1,0:T(8,128)(2,1)S(1)}, bf16[128,512]{1,0:T(8,128)(2,1)S(1)}, u32[]{:S(2)}, u32[]{:S(2)}) collective-permute-start(bf16[128,512]{1,0:T(8,128)(2,1)S(1)} %get-tuple-element.103), channel_id=1, source_target_pairs={{0,1},{1,0},{2,3},{3,2},{4,5},{5,4},{6,7},{7,6},{8,16},{9,8},{10,2... | collective-permute-start | bytes 393224 | tf_op jit(solution)/shard_map/ppermute | solution.py:616
  25.7 7.3 %collective-permute-start.11 = (bf16[128,512]{1,0:T(8,128)(2,1)S(1)}, bf16[128,512]{1,0:T(8,128)(2,1)S(1)}, u32[]{:S(2)}, u32[]{:S(2)}) collective-permute-start(bf16[128,512]{1,0:T(8,128)(2,1)S(1)} %next.8), channel_id=1, source_target_pairs={{0,1},{1,0},{2,3},{3,2},{4,5},{5,4},{6,7},{7,6},{8,16},{9,8},{10,2... | collective-permute-start | bytes 393224 | tf_op jit(solution)/shard_map/ppermute | solution.py:616
  27.1 7.2 %collective-permute-start.12 = (bf16[128,512]{1,0:T(8,128)(2,1)S(1)}, bf16[128,512]{1,0:T(8,128)(2,1)S(1)}, u32[]{:S(2)}, u32[]{:S(2)}) collective-permute-start(bf16[128,512]{1,0:T(8,128)(2,1)S(1)} %next.9), channel_id=1, source_target_pairs={{0,1},{1,0},{2,3},{3,2},{4,5},{5,4},{6,7},{7,6},{8,16},{9,8},{10,2... | collective-permute-start | bytes 393224 | tf_op jit(solution)/shard_map/ppermute | solution.py:616
  34.4 7.8 %collective-permute-start.15 = (bf16[128,512]{1,0:T(8,128)(2,1)S(1)}, bf16[128,512]{1,0:T(8,128)(2,1)S(1)}, u32[]{:S(2)}, u32[]{:S(2)}) collective-permute-start(bf16[128,512]{1,0:T(8,128)(2,1)S(1)} %get-tuple-element.114), channel_id=1, source_target_pairs={{0,1},{1,0},{2,3},{3,2},{4,5},{5,21},{6,7},{7,6},{8,9},{9,8},{10,1... | collective-permute-start | bytes 393224 | tf_op jit(solution)/shard_map/ppermute | solution.py:616
  34.4 7.8 %collective-permute-start.14 = (bf16[128,512]{1,0:T(8,128)(2,1)S(1)}, bf16[128,512]{1,0:T(8,128)(2,1)S(1)}, u32[]{:S(2)}, u32[]{:S(2)}) collective-permute-start(bf16[128,512]{1,0:T(8,128)(2,1)S(1)} %far_part.3), channel_id=1, source_target_pairs={{0,1},{1,0},{2,3},{3,2},{4,5},{5,4},{6,7},{7,17},{8,9},{9,8},{10,1... | collective-permute-start | bytes 393224 | tf_op jit(solution)/shard_map/ppermute | solution.py:616
  34.9 9.3 %collective-permute-start.16 = (bf16[128,512]{1,0:T(8,128)(2,1)S(1)}, bf16[128,512]{1,0:T(8,128)(2,1)S(1)}, u32[]{:S(2)}, u32[]{:S(2)}) collective-permute-start(bf16[128,512]{1,0:T(8,128)(2,1)S(1)} %near_part.2.refs_3_), channel_id=1, source_target_pairs={{0,1},{1,17},{2,3},{3,2},{4,5},{5,4},{6,7},{7,6},{8,9},{9,27},{10,... | collective-permute-start | bytes 393224 | tf_op jit(solution)/shard_map/ppermute | solution.py:616
  42.2 2.0 %collective-permute-start.17 = (bf16[128,512]{1,0:T(8,128)(2,1)S(1)}, bf16[128,512]{1,0:T(8,128)(2,1)S(1)}, u32[]{:S(2)}, u32[]{:S(2)}) collective-permute-start(bf16[128,512]{1,0:T(8,128)(2,1)S(1)} %near_part.3.refs_4_), channel_id=1, source_target_pairs={{0,1},{1,0},{2,3},{3,17},{4,5},{5,4},{6,7},{7,6},{8,9},{9,8},{10,1... | collective-permute-start | bytes 393224 | tf_op jit(solution)/shard_map/ppermute | solution.py:616
  42.2 6.5 %copy-start.5 = (bf16[512,227]{0,1:T(8,128)(2,1)S(1)}, bf16[512,227]{0,1:T(8,128)(2,1)}, u32[]{:S(2)}) copy-start(bf16[512,227]{0,1:T(8,128)(2,1)} %param.18) | copy-start | bytes 697348
  44.2 4.6 %collective-permute-start.18 = (bf16[64,512]{1,0:T(8,128)(2,1)S(1)}, bf16[64,512]{1,0:T(8,128)(2,1)S(1)}, u32[]{:S(2)}, u32[]{:S(2)}) collective-permute-start(bf16[64,512]{1,0:T(8,128)(2,1)S(1)} %get-tuple-element.116), channel_id=1, source_target_pairs={{0,1},{1,0},{2,3},{3,2},{4,5},{5,4},{6,7},{7,6},{8,9},{9,8},{10,11... | collective-permute-start | bytes 196616 | tf_op jit(solution)/shard_map/ppermute | solution.py:635

commit v19 on v17

--- a/solution.py
+++ b/solution.py
@@ -456,8 +456,11 @@
                 pieces = outs[1:]
             sender = outs[0] if first else senders[0]
             rows = sum(piece.shape[0] for piece in pieces)
-            upper = (chip < chips // 2) if far else (chip >= chips // 2)
-            start = pl.multiple_of(jnp.where(upper, half, 0) + begin, rows)
+            if far:
+                start = jnp.where(chip < chips // 2, half, 0) + begin
+            else:
+                start = (chip if begin else jnp.bitwise_xor(chip, 1)) * rows
+            start = pl.multiple_of(start, rows)
             own = state[pl.ds(start, rows), :]
             gathered = sum_edges(fanout, columns[pl.ds(start, rows), :], sender[...], own, w_receive)
             write_pieces(pieces, update_nodes(own, gathered, w_own, w_edges))
@@ -469,17 +472,15 @@
         piece[:rows, :] = value[place * rows : (place + 1) * rows]
 
 
-def arrival(where, group, chips, last):
+def arrival(where, group, chips):
     each = chips // 2
-    segment = where[0]
     chip, _ = place_of(where, group)
-    crosses = lax.div(chip, each) != lax.div(segment, each)
-    return crosses, jnp.logical_and(segment >= last, chip == segment), lax.rem(chip, each)
+    return lax.div(chip, each) != lax.div(where[0], each), lax.rem(chip, each)
 
 
 def far_kernel(group, chips, last, number, where, *refs):
     block, out = refs[0], refs[-1]
-    crosses, _, spot = arrival(where, group, chips, last)
+    crosses, spot = arrival(where, group, chips)
 
     @pl.when(jnp.logical_and(crosses, spot == number))
     def _():
@@ -492,27 +493,24 @@
             out[...] = refs[1][...]
 
 
-def near_kernel(group, chips, last, where, crossed, *refs):
-    each = chips // 2
-    near, kept, outs = refs[:each], refs[each : 2 * each], refs[2 * each :]
+def near_kernel(group, chips, last, where, crossed, beside, same, kept, *outs):
     rows = outs[0].shape[0]
-    crosses, stays, spot = arrival(where, group, chips, last)
-    arrives = jnp.logical_not(jnp.logical_or(crosses, stays))
-
-    def give(block):
-        for place, out in enumerate(outs):
-            out[...] = block[place * rows : (place + 1) * rows, :]
-
-    @pl.when(crosses)
-    def _():
-        give(crossed)
-
-    for number in range(each):
-        for blocks, chosen in ((near, arrives), (kept, stays)):
-
-            @pl.when(jnp.logical_and(chosen, spot == number))
-            def _(block=blocks[number]):
-                give(block)
+    crosses, _ = arrival(where, group, chips)
+    chip, _ = place_of(where, group)
+    own = chip == where[0]
+    stays = jnp.logical_and(own, chip >= last)
+    chosen = [
+        (crossed, crosses),
+        (beside, jnp.logical_not(jnp.logical_or(crosses, own))),
+        (same, jnp.logical_and(own, chip < last)),
+        (kept, stays),
+    ]
+    for block, here in chosen:
+
+        @pl.when(here)
+        def _(block=block):
+            for place, out in enumerate(outs):
+                out[...] = block[place * rows : (place + 1) * rows, :]
 
 
 def prepare_kernel(where, snapshots, w_embed, w_decode, mesh_grid, ready, table_out):
@@ -809,9 +807,8 @@
     arrived = []
     for far, blocks in ((1, state[:each]), (0, state[each:])):
         for turn, block in enumerate(blocks):
-            pairs = [
-                (owner(m, segments), device(m, ((m // each ^ far) * each + turn) * group)) for m in range(samples)
-            ]
+            chips = [(m // each ^ 1) * each + turn if far else m ^ (1 - turn) for m in range(samples)]
+            pairs = [(owner(m, segments), device(m, chips[m] * group)) for m in range(samples)]
             arrived.append(send(block, [pair for pair in pairs if pair[0] != pair[1]]))
     crossed = []
     for number, block in enumerate(arrived[:each]):
@@ -826,8 +823,8 @@
         functools.partial(near_kernel, group, samples, last),
         "near",
         [jax.ShapeDtypeStruct((mesh_rows, width), bf16)] * group,
-        [where, crossed[0]] + arrived[each:] + state[each:],
-        "w" + "v" * (1 + 2 * each),
+        [where, crossed[0]] + arrived[each:] + state[-1:],
+        "w" + "v" * (2 + each),
     )
     handed = [parts_of_block[0]]
     for steps in range(1, group):
@@ -847,7 +844,7 @@
     segments, parts = mesh.shape["segment"], mesh.shape["dom"]
     samples, width = arrays[0].shape[0], arrays[1].shape[1]
     nodes = parts * arrays[9].shape[0]
-    fits = samples == segments == 4 and parts % samples == 0 and parts > samples and nodes == width
+    fits = samples == segments == 4 and parts == 2 * samples and nodes == width
     return (resident if fits else streamed)(*arrays)
 
 

time: 50.9 us -> 50.9 us (level)
  no operation moved by 1% of the time
where the time goes in v19:
time: 50.9 us; the launch traced here: 50 us
  starting transfers between devices  33 us (65%)
  waiting for transfers between devices  10 us (20%)
  local copies, waits for them, and re-layouts  3.46 us (7%)
  Pallas kernels  3.2 us (6%)
    ppermute x14, starting transfers between devices, send(): lax.ppermute(value, ('segment', 'dom'), every_device(pairs, segments * pa...  24.9 us
    ppermute x14, waiting for transfers between devices, send(): lax.ppermute(value, ('segment', 'dom'), every_device(pairs, segments * pa...  7.5 us
    ppermute x3, starting transfers between devices, to_chip(): return lax.ppermute(value, ('segment', 'dom'), pairs)  4.36 us
    ppermute x2, starting transfers between devices, change_lane(): return lax.ppermute(value, 'dom', pairs)  3.72 us
    unnamed x23, local copies, waits for them, and re-layouts  3.46 us
    pallas_call x30, Pallas kernels, call(): pl.pallas_call(located if places[0] == 'w' else kernel, out_shape=shapes,...  3.2 us
    ppermute x2, waiting for transfers between devices, change_lane(): return lax.ppermute(value, 'dom', pairs)  2.52 us
  transfers between devices with their start and end apart: 19, of which 7 were waited for; matrix products, arithmetic and copies ran while one was open for 2% of the time, Pallas kernels for 4%

profile of v19, /device:TPU:3, one launch (start us, length us, event | category | flops | bytes accessed | tf_op | source)
XLA Modules:
  0.0 50.0 jit_solution(4521413065463211026)
XLA Ops:
  0.0 0.0 copy-start.10
  0.0 0.0 copy-start.3
  0.0 0.7 %collective-permute-start.4 = (bf16[1,512,1024]{2,1,0:T(8,128)(2,1)}, bf16[1,512,1024]{2,1,0:T(8,128)(2,1)S(1)}, u32[]{:S(2)}, u32[]{:S(2)}) collective-permute-start(bf16[1,512,1024]{2,1,0:T(8,128)(2,1)} %w_project), channel_id=1, source_target_pairs={{0,1},{1,0},{2,3},{3,2},{4,5},{5,4},{6,7},{7,6},{8,9},{9,8},{10,11... | collective-permute-start | bytes 3145736 | tf_op jit(solution)/shard_map/ppermute | solution.py:614
  0.8 1.0 %copy.15 = bf16[4,128,227]{1,2,0:T(8,128)(2,1)S(1)} copy(bf16[4,128,227]{1,0,2:T(4,128)(2,1)} %param.12) | data formatting | bytes 464896 | tf_op args[0]
  1.8 0.7 %encode.1 = (bf16[80,512]{1,0:T(8,128)(2,1)S(1)}, bf16[80,512]{1,0:T(8,128)(2,1)S(1)}, bf16[80,512]{1,0:T(8,128)(2,1)S(1)}, bf16[80,512]{1,0:T(8,128)(2,1)S(1)}) custom-call(s32[1]{0:T(128)} %bitcast.segment, s32[1]{0:T(128)} %bitcast.1.place, bf16[4,227,128]{2,1,0:T(8,128)(2,1)S(1)} %bitcast.13, bf16[227,512]{1,0:T(8,128)(2,1)S(1)} %copy-done.3, ...), custom_call_target="tpu_custom_call" | custom-call | bytes 799752 | tf_op jit(solution)/shard_map/encode/pallas_call | solution.py:550
  2.5 0.2 collective-permute-start
  2.7 3.4 %collective-permute-start.1 = (bf16[80,512]{1,0:T(8,128)(2,1)S(1)}, bf16[80,512]{1,0:T(8,128)(2,1)S(1)}, u32[]{:S(2)}, u32[]{:S(2)}) collective-permute-start(bf16[80,512]{1,0:T(8,128)(2,1)S(1)} %get-tuple-element.71), channel_id=1, source_target_pairs={{0,8},{1,9},{2,10},{3,11},{4,12},{5,13},{6,14},{7,15},{8,4},{9,5},... | collective-permute-start | bytes 245768 | tf_op jit(solution)/shard_map/ppermute | solution.py:629
  6.2 0.7 %collective-permute-start.2 = (bf16[80,512]{1,0:T(8,128)(2,1)S(1)}, bf16[80,512]{1,0:T(8,128)(2,1)S(1)}, u32[]{:S(2)}, u32[]{:S(2)}) collective-permute-start(bf16[80,512]{1,0:T(8,128)(2,1)S(1)} %get-tuple-element.72), channel_id=1, source_target_pairs={{0,16},{1,17},{2,18},{3,19},{4,20},{5,21},{6,22},{7,23},{8,9},{9,8... | collective-permute-start | bytes 245768 | tf_op jit(solution)/shard_map/ppermute | solution.py:629
  6.9 1.2 %copy-done.1 = bf16[1,1024,512]{2,1,0:T(8,128)(2,1)S(1)} copy-done((bf16[1,1024,512]{2,1,0:T(8,128)(2,1)S(1)}, bf16[1,1024,512]{2,1,0:T(8,128)(2,1)}, u32[]{:S(2)}) %copy-start.1) | copy-done | bytes 1048600
  8.1 1.2 %copy-done.2 = bf16[1,512,1024]{2,1,0:T(8,128)(2,1)S(1)} copy-done((bf16[1,512,1024]{2,1,0:T(8,128)(2,1)S(1)}, bf16[1,512,1024]{2,1,0:T(8,128)(2,1)}, u32[]{:S(2)}) %copy-start.2) | copy-done | bytes 1048600
  9.3 0.7 %hold.1 = (bf16[512,512]{1,0:T(8,128)(2,1)S(1)}, bf16[512,512]{1,0:T(8,128)(2,1)S(1)}, bf16[512,512]{1,0:T(8,128)(2,1)S(1)}, bf16[512,512]{1,0:T(8,128)(2,1)S(1)}) custom-call(bf16[1,512,1024]{2,1,0:T(8,128)(2,1)S(1)} %copy-done.2, bf16[1,512,512]{2,1,0:T(8,128)(2,1)S(1)} %copy-done.4, bf16[1,1024,512]{2,1,0:T(8,128)(2,1)S(1)} %copy-done.1), custom_call_target="tpu_custom_call" | custom-call | bytes 4718592 | tf_op jit(solution)/shard_map/hold/pallas_call | solution.py:550
  10.1 0.0 collective-permute-done.refs_1_
  10.1 0.0 collective-permute-done.1.refs_2_
  10.1 0.0 collective-permute-done.2.refs_3_
  10.2 0.1 collective-permute-start.3
  10.2 1.6 %collective-permute-done.3.refs_1_ = bf16[320,512]{1,0:T(8,128)(2,1)S(1)} collective-permute-done((bf16[320,512]{1,0:T(8,128)(2,1)S(1)}, bf16[320,512]{1,0:T(8,128)(2,1)S(1)}, u32[]{:S(2)}, u32[]{:S(2)}) %collective-permute-start.3) | collective-permute-done | bytes 327712 | tf_op jit(solution)/shard_map/ppermute | solution.py:633
  11.8 0.0 collective-permute-done.4.refs_2_.refs_10_.refs_13_.refs_6_.refs_7_
  11.9 0.1 collective-permute-start.13
  12.0 2.5 %collective-permute-start.5 = (bf16[144,512]{1,0:T(8,128)(2,1)S(1)}, bf16[144,512]{1,0:T(8,128)(2,1)S(1)}, u32[]{:S(2)}, u32[]{:S(2)}) collective-permute-start(bf16[144,512]{1,0:T(8,128)(2,1)S(1)} %get-tuple-element.85), channel_id=1, source_target_pairs={{0,8},{1,0},{2,10},{3,2},{4,12},{5,4},{6,14},{7,6},{8,9},{9,1},{10... | collective-permute-start | bytes 442376 | tf_op jit(solution)/shard_map/ppermute | solution.py:614
  14.5 1.7 %collective-permute-start.6 = (bf16[128,512]{1,0:T(8,128)(2,1)S(1)}, bf16[128,512]{1,0:T(8,128)(2,1)S(1)}, u32[]{:S(2)}, u32[]{:S(2)}) collective-permute-start(bf16[128,512]{1,0:T(8,128)(2,1)S(1)} %next.5), channel_id=1, source_target_pairs={{0,8},{1,0},{2,10},{3,2},{4,12},{5,4},{6,14},{7,6},{8,9},{9,1},{10... | collective-permute-start | bytes 393224 | tf_op jit(solution)/shard_map/ppermute | solution.py:614
  16.2 1.5 %collective-permute-start.7 = (bf16[128,512]{1,0:T(8,128)(2,1)S(1)}, bf16[128,512]{1,0:T(8,128)(2,1)S(1)}, u32[]{:S(2)}, u32[]{:S(2)}) collective-permute-start(bf16[128,512]{1,0:T(8,128)(2,1)S(1)} %next.6), channel_id=1, source_target_pairs={{0,8},{1,0},{2,10},{3,2},{4,12},{5,4},{6,14},{7,6},{8,9},{9,1},{10... | collective-permute-start | bytes 393224 | tf_op jit(solution)/shard_map/ppermute | solution.py:614
  17.7 1.5 %collective-permute-start.9 = (bf16[128,512]{1,0:T(8,128)(2,1)S(1)}, bf16[128,512]{1,0:T(8,128)(2,1)S(1)}, u32[]{:S(2)}, u32[]{:S(2)}) collective-permute-start(bf16[128,512]{1,0:T(8,128)(2,1)S(1)} %next.7), channel_id=1, source_target_pairs={{0,8},{1,0},{2,10},{3,2},{4,12},{5,4},{6,14},{7,6},{8,9},{9,1},{10... | collective-permute-start | bytes 393224 | tf_op jit(solution)/shard_map/ppermute | solution.py:614
  19.2 0.4 prepare.1
  19.6 0.0 collective-permute-done.5.refs_0_.refs_5_.refs_1_
  19.6 0.0 collective-permute-done.6.refs_0_.refs_4_.refs_2_
  19.7 0.0 collective-permute-done.7.refs_0_.refs_3_
  19.7 4.4 %collective-permute-start.8 = (bf16[144,512]{1,0:T(8,128)(2,1)S(1)}, bf16[144,512]{1,0:T(8,128)(2,1)S(1)}, u32[]{:S(2)}, u32[]{:S(2)}) collective-permute-start(bf16[144,512]{1,0:T(8,128)(2,1)S(1)} %early.2), channel_id=1, source_target_pairs={{0,1},{1,0},{2,3},{3,2},{4,5},{5,4},{6,7},{7,6},{8,16},{9,8},{10,2... | collective-permute-start | bytes 442376 | tf_op jit(solution)/shard_map/ppermute | solution.py:614
  24.1 0.0 collective-permute-done.9.refs_4_
  24.1 1.6 %collective-permute-start.10 = (bf16[128,512]{1,0:T(8,128)(2,1)S(1)}, bf16[128,512]{1,0:T(8,128)(2,1)S(1)}, u32[]{:S(2)}, u32[]{:S(2)}) collective-permute-start(bf16[128,512]{1,0:T(8,128)(2,1)S(1)} %get-tuple-element.103), channel_id=1, source_target_pairs={{0,1},{1,0},{2,3},{3,2},{4,5},{5,4},{6,7},{7,6},{8,16},{9,8},{10,2... | collective-permute-start | bytes 393224 | tf_op jit(solution)/shard_map/ppermute | solution.py:614
  25.6 1.5 %collective-permute-start.11 = (bf16[128,512]{1,0:T(8,128)(2,1)S(1)}, bf16[128,512]{1,0:T(8,128)(2,1)S(1)}, u32[]{:S(2)}, u32[]{:S(2)}) collective-permute-start(bf16[128,512]{1,0:T(8,128)(2,1)S(1)} %next.8), channel_id=1, source_target_pairs={{0,1},{1,0},{2,3},{3,2},{4,5},{5,4},{6,7},{7,6},{8,16},{9,8},{10,2... | collective-permute-start | bytes 393224 | tf_op jit(solution)/shard_map/ppermute | solution.py:614
  27.1 1.7 %collective-permute-start.12 = (bf16[128,512]{1,0:T(8,128)(2,1)S(1)}, bf16[128,512]{1,0:T(8,128)(2,1)S(1)}, u32[]{:S(2)}, u32[]{:S(2)}) collective-permute-start(bf16[128,512]{1,0:T(8,128)(2,1)S(1)} %next.9), channel_id=1, source_target_pairs={{0,1},{1,0},{2,3},{3,2},{4,5},{5,4},{6,7},{7,6},{8,16},{9,8},{10,2... | collective-permute-start | bytes 393224 | tf_op jit(solution)/shard_map/ppermute | solution.py:614
  28.8 1.4 %collective-permute-done.8.refs_0_.refs_5_.refs_1_ = bf16[144,512]{1,0:T(8,128)(2,1)S(1)} collective-permute-done((bf16[144,512]{1,0:T(8,128)(2,1)S(1)}, bf16[144,512]{1,0:T(8,128)(2,1)S(1)}, u32[]{:S(2)}, u32[]{:S(2)}) %collective-permute-start.8) | collective-permute-done | bytes 147488 | tf_op jit(solution)/shard_map/ppermute | solution.py:614
  30.1 1.4 %collective-permute-done.10.refs_0_.refs_4_.refs_2_ = bf16[128,512]{1,0:T(8,128)(2,1)S(1)} collective-permute-done((bf16[128,512]{1,0:T(8,128)(2,1)S(1)}, bf16[128,512]{1,0:T(8,128)(2,1)S(1)}, u32[]{:S(2)}, u32[]{:S(2)}) %collective-permute-start.10) | collective-permute-done | bytes 131104 | tf_op jit(solution)/shard_map/ppermute | solution.py:614
  31.5 1.4 %collective-permute-done.11.refs_0_.refs_3_ = bf16[128,512]{1,0:T(8,128)(2,1)S(1)} collective-permute-done((bf16[128,512]{1,0:T(8,128)(2,1)S(1)}, bf16[128,512]{1,0:T(8,128)(2,1)S(1)}, u32[]{:S(2)}, u32[]{:S(2)}) %collective-permute-start.11) | collective-permute-done | bytes 131104 | tf_op jit(solution)/shard_map/ppermute | solution.py:614
  33.0 0.0 collective-permute-done.13.refs_11_.refs_14_.refs_7_.refs_8_
  33.0 1.4 %collective-permute-done.12.refs_4_ = bf16[128,512]{1,0:T(8,128)(2,1)S(1)} collective-permute-done((bf16[128,512]{1,0:T(8,128)(2,1)S(1)}, bf16[128,512]{1,0:T(8,128)(2,1)S(1)}, u32[]{:S(2)}, u32[]{:S(2)}) %collective-permute-start.12) | collective-permute-done | bytes 131104 | tf_op jit(solution)/shard_map/ppermute | solution.py:614
  34.4 0.0 collective-permute-start.15
  34.4 0.5 %collective-permute-start.14 = (bf16[128,512]{1,0:T(8,128)(2,1)S(1)}, bf16[128,512]{1,0:T(8,128)(2,1)S(1)}, u32[]{:S(2)}, u32[]{:S(2)}) collective-permute-start(bf16[128,512]{1,0:T(8,128)(2,1)S(1)} %far_part.3), channel_id=1, source_target_pairs={{0,1},{1,0},{2,3},{3,2},{4,5},{5,4},{6,7},{7,17},{8,9},{9,8},{10,1... | collective-permute-start | bytes 393224 | tf_op jit(solution)/shard_map/ppermute | solution.py:614
  34.9 7.3 %collective-permute-start.16 = (bf16[128,512]{1,0:T(8,128)(2,1)S(1)}, bf16[128,512]{1,0:T(8,128)(2,1)S(1)}, u32[]{:S(2)}, u32[]{:S(2)}) collective-permute-start(bf16[128,512]{1,0:T(8,128)(2,1)S(1)} %near_part.2), channel_id=1, source_target_pairs={{0,1},{1,0},{2,3},{3,17},{4,5},{5,4},{6,7},{7,6},{8,9},{9,27},{10,... | collective-permute-start | bytes 393224 | tf_op jit(solution)/shard_map/ppermute | solution.py:614
  42.2 0.0 collective-permute-start.17
  42.2 0.0 collective-permute-done.15.refs_0_
  42.2 0.0 collective-permute-done.14.refs_0_
  42.2 0.0 copy-start.5
  42.2 1.9 %collective-permute-done.16.refs_1_ = bf16[128,512]{1,0:T(8,128)(2,1)S(1)} collective-permute-done((bf16[128,512]{1,0:T(8,128)(2,1)S(1)}, bf16[128,512]{1,0:T(8,128)(2,1)S(1)}, u32[]{:S(2)}, u32[]{:S(2)}) %collective-permute-start.16) | collective-permute-done | bytes 131104 | tf_op jit(solution)/shard_map/ppermute | solution.py:614
  44.1 0.0 collective-permute-done.17.refs_2_
  44.2 3.6 %collective-permute-start.18 = (bf16[64,512]{1,0:T(8,128)(2,1)S(1)}, bf16[64,512]{1,0:T(8,128)(2,1)S(1)}, u32[]{:S(2)}, u32[]{:S(2)}) collective-permute-start(bf16[64,512]{1,0:T(8,128)(2,1)S(1)} %get-tuple-element.116), channel_id=1, source_target_pairs={{0,1},{1,0},{2,3},{3,2},{4,5},{5,4},{6,7},{7,6},{8,9},{9,8},{10,11... | collective-permute-start | bytes 196616 | tf_op jit(solution)/shard_map/ppermute | solution.py:633
  47.8 0.9 %collective-permute-done.18.refs_5_ = bf16[64,512]{1,0:T(8,128)(2,1)S(1)} collective-permute-done((bf16[64,512]{1,0:T(8,128)(2,1)S(1)}, bf16[64,512]{1,0:T(8,128)(2,1)S(1)}, u32[]{:S(2)}, u32[]{:S(2)}) %collective-permute-start.18) | collective-permute-done | bytes 65568 | tf_op jit(solution)/shard_map/ppermute | solution.py:633
  48.7 1.2 %decode.1 = bf16[227,128]{1,0:T(8,128)(2,1)} custom-call(s32[1]{0:T(128)} %bitcast.segment, s32[1]{0:T(128)} %bitcast.1.place, f32[128,512]{1,0:T(8,128)S(1)} %get-tuple-element.88.refs_0_, bf16[64,128]{1,0:T(8,128)(2,1)S(1)} %get-tuple-element.89.refs_1_, bf16[1024,512]{1,0:T(8,128)(2,1)S(1)} %copy-done, bf16[227,512]{1,0:T(8,128)(2,1)S(1)} %bitcast.15, ...), custom_call_target="tpu_custom_call" | custom-call | bytes 1748744 | tf_op jit(solution)/shard_map/decode/pallas_call | solution.py:550
  (44 shorter events, 0.2 us)
Async XLA Ops:
  0.0 1.7 %copy-start.7 = (s32[64,8]{0,1:T(8,128)S(1)}, s32[64,8]{0,1:T(8,128)}, u32[]{:S(2)}) copy-start(s32[64,8]{0,1:T(8,128)} %param.21) | copy-start | bytes 6148
  0.0 1.8 %copy-start.8 = (s32[4,64]{1,0:T(4,128)S(1)}, s32[4,64]{1,0:T(4,128)}, u32[]{:S(2)}) copy-start(s32[4,64]{1,0:T(4,128)} %param.22) | copy-start | bytes 3076
  0.0 1.8 %copy-start.9 = (s32[4,1]{0,1:T(1,128)S(1)}, s32[4,1]{0,1:T(1,128)}, u32[]{:S(2)}) copy-start(s32[4,1]{0,1:T(1,128)} %param.23) | copy-start | bytes 52
  0.0 1.8 %copy-start.10 = (s32[128]{0:T(128)S(1)}, s32[128]{0:T(128)}, u32[]{:S(2)}) copy-start(s32[128]{0:T(128)} %param.19) | copy-start | bytes 1540
  0.0 1.8 %copy-start.3 = (bf16[227,512]{1,0:T(8,128)(2,1)S(1)}, bf16[227,512]{1,0:T(8,128)(2,1)}, u32[]{:S(2)}) copy-start(bf16[227,512]{1,0:T(8,128)(2,1)} %refs_1_.3) | copy-start | bytes 697348
  0.0 6.9 %copy-start.4 = (bf16[1,512,512]{2,1,0:T(8,128)(2,1)S(1)}, bf16[1,512,512]{2,1,0:T(8,128)(2,1)}, u32[]{:S(2)}) copy-start(bf16[1,512,512]{2,1,0:T(8,128)(2,1)} %w_message.1) | copy-start | bytes 1572868
  0.0 11.8 %collective-permute-start.4 = (bf16[1,512,1024]{2,1,0:T(8,128)(2,1)}, bf16[1,512,1024]{2,1,0:T(8,128)(2,1)S(1)}, u32[]{:S(2)}, u32[]{:S(2)}) collective-permute-start(bf16[1,512,1024]{2,1,0:T(8,128)(2,1)} %w_project), channel_id=1, source_target_pairs={{0,1},{1,0},{2,3},{3,2},{4,5},{5,4},{6,7},{7,6},{8,9},{9,8},{10,11... | collective-permute-start | bytes 3145736 | tf_op jit(solution)/shard_map/ppermute | solution.py:614
  2.5 7.6 %collective-permute-start = (bf16[80,512]{1,0:T(8,128)(2,1)S(1)}, bf16[80,512]{1,0:T(8,128)(2,1)S(1)}, u32[]{:S(2)}, u32[]{:S(2)}) collective-permute-start(bf16[80,512]{1,0:T(8,128)(2,1)S(1)} %get-tuple-element.70), channel_id=1, source_target_pairs={{0,2},{1,3},{2,0},{3,1},{4,6},{5,7},{6,4},{7,5},{8,9},{9,8},{10,11... | collective-permute-start | bytes 245768 | tf_op jit(solution)/shard_map/ppermute | solution.py:629
  2.7 7.4 %collective-permute-start.1 = (bf16[80,512]{1,0:T(8,128)(2,1)S(1)}, bf16[80,512]{1,0:T(8,128)(2,1)S(1)}, u32[]{:S(2)}, u32[]{:S(2)}) collective-permute-start(bf16[80,512]{1,0:T(8,128)(2,1)S(1)} %get-tuple-element.71), channel_id=1, source_target_pairs={{0,8},{1,9},{2,10},{3,11},{4,12},{5,13},{6,14},{7,15},{8,4},{9,5},... | collective-permute-start | bytes 245768 | tf_op jit(solution)/shard_map/ppermute | solution.py:629
  6.2 3.9 %collective-permute-start.2 = (bf16[80,512]{1,0:T(8,128)(2,1)S(1)}, bf16[80,512]{1,0:T(8,128)(2,1)S(1)}, u32[]{:S(2)}, u32[]{:S(2)}) collective-permute-start(bf16[80,512]{1,0:T(8,128)(2,1)S(1)} %get-tuple-element.72), channel_id=1, source_target_pairs={{0,16},{1,17},{2,18},{3,19},{4,20},{5,21},{6,22},{7,23},{8,9},{9,8... | collective-permute-start | bytes 245768 | tf_op jit(solution)/shard_map/ppermute | solution.py:629
  6.9 1.2 %copy-start.1 = (bf16[1,1024,512]{2,1,0:T(8,128)(2,1)S(1)}, bf16[1,1024,512]{2,1,0:T(8,128)(2,1)}, u32[]{:S(2)}) copy-start(bf16[1,1024,512]{2,1,0:T(8,128)(2,1)} %w_update.1) | copy-start | bytes 3145732
  8.1 1.2 %copy-start.2 = (bf16[1,512,1024]{2,1,0:T(8,128)(2,1)S(1)}, bf16[1,512,1024]{2,1,0:T(8,128)(2,1)}, u32[]{:S(2)}) copy-start(bf16[1,512,1024]{2,1,0:T(8,128)(2,1)} %w_project) | copy-start | bytes 3145732
  10.2 1.7 %collective-permute-start.3 = (bf16[320,512]{1,0:T(8,128)(2,1)S(1)}, bf16[320,512]{1,0:T(8,128)(2,1)S(1)}, u32[]{:S(2)}, u32[]{:S(2)}) collective-permute-start(bf16[320,512]{1,0:T(8,128)(2,1)S(1)} %join.1.refs_0_), channel_id=1, source_target_pairs={{0,1},{1,0},{2,3},{3,2},{4,5},{5,4},{6,7},{7,6},{8,9},{9,8},{10,11... | collective-permute-start | bytes 983048 | tf_op jit(solution)/shard_map/ppermute | solution.py:633
  11.9 21.1 %collective-permute-start.13 = (bf16[2,512,512]{2,1,0:T(8,128)(2,1)S(1)}, bf16[2,512,512]{2,1,0:T(8,128)(2,1)S(1)}, u32[]{:S(2)}, u32[]{:S(2)}) collective-permute-start(bf16[2,512,512]{2,1,0:T(8,128)(2,1)S(1)} %pack.1), channel_id=1, source_target_pairs={{0,1},{1,0},{2,3},{3,2},{4,5},{5,4},{6,7},{7,6},{8,9},{9,8},{10,11... | collective-permute-start | bytes 3145736 | tf_op jit(solution)/shard_map/ppermute | solution.py:614
  12.0 7.6 %collective-permute-start.5 = (bf16[144,512]{1,0:T(8,128)(2,1)S(1)}, bf16[144,512]{1,0:T(8,128)(2,1)S(1)}, u32[]{:S(2)}, u32[]{:S(2)}) collective-permute-start(bf16[144,512]{1,0:T(8,128)(2,1)S(1)} %get-tuple-element.85), channel_id=1, source_target_pairs={{0,8},{1,0},{2,10},{3,2},{4,12},{5,4},{6,14},{7,6},{8,9},{9,1},{10... | collective-permute-start | bytes 442376 | tf_op jit(solution)/shard_map/ppermute | solution.py:614
  14.5 5.1 %collective-permute-start.6 = (bf16[128,512]{1,0:T(8,128)(2,1)S(1)}, bf16[128,512]{1,0:T(8,128)(2,1)S(1)}, u32[]{:S(2)}, u32[]{:S(2)}) collective-permute-start(bf16[128,512]{1,0:T(8,128)(2,1)S(1)} %next.5), channel_id=1, source_target_pairs={{0,8},{1,0},{2,10},{3,2},{4,12},{5,4},{6,14},{7,6},{8,9},{9,1},{10... | collective-permute-start | bytes 393224 | tf_op jit(solution)/shard_map/ppermute | solution.py:614
  16.2 3.0 %copy-start = (bf16[1024,512]{1,0:T(8,128)(2,1)S(1)}, bf16[1024,512]{1,0:T(8,128)(2,1)}, u32[]{:S(2)}) copy-start(bf16[1024,512]{1,0:T(8,128)(2,1)} %refs_2_.3) | copy-start | bytes 3145732
  16.2 3.4 %collective-permute-start.7 = (bf16[128,512]{1,0:T(8,128)(2,1)S(1)}, bf16[128,512]{1,0:T(8,128)(2,1)S(1)}, u32[]{:S(2)}, u32[]{:S(2)}) collective-permute-start(bf16[128,512]{1,0:T(8,128)(2,1)S(1)} %next.6), channel_id=1, source_target_pairs={{0,8},{1,0},{2,10},{3,2},{4,12},{5,4},{6,14},{7,6},{8,9},{9,1},{10... | collective-permute-start | bytes 393224 | tf_op jit(solution)/shard_map/ppermute | solution.py:614
  17.7 1.5 %copy-start.6 = (s32[128]{0:T(128)S(1)}, s32[128]{0:T(128)}, u32[]{:S(2)}) copy-start(s32[128]{0:T(128)} %param.20) | copy-start | bytes 1540
  17.7 6.4 %collective-permute-start.9 = (bf16[128,512]{1,0:T(8,128)(2,1)S(1)}, bf16[128,512]{1,0:T(8,128)(2,1)S(1)}, u32[]{:S(2)}, u32[]{:S(2)}) collective-permute-start(bf16[128,512]{1,0:T(8,128)(2,1)S(1)} %next.7), channel_id=1, source_target_pairs={{0,8},{1,0},{2,10},{3,2},{4,12},{5,4},{6,14},{7,6},{8,9},{9,1},{10... | collective-permute-start | bytes 393224 | tf_op jit(solution)/shard_map/ppermute | solution.py:614
  19.7 10.4 %collective-permute-start.8 = (bf16[144,512]{1,0:T(8,128)(2,1)S(1)}, bf16[144,512]{1,0:T(8,128)(2,1)S(1)}, u32[]{:S(2)}, u32[]{:S(2)}) collective-permute-start(bf16[144,512]{1,0:T(8,128)(2,1)S(1)} %early.2), channel_id=1, source_target_pairs={{0,1},{1,0},{2,3},{3,2},{4,5},{5,4},{6,7},{7,6},{8,16},{9,8},{10,2... | collective-permute-start | bytes 442376 | tf_op jit(solution)/shard_map/ppermute | solution.py:614
  24.1 7.5 %collective-permute-start.10 = (bf16[128,512]{1,0:T(8,128)(2,1)S(1)}, bf16[128,512]{1,0:T(8,128)(2,1)S(1)}, u32[]{:S(2)}, u32[]{:S(2)}) collective-permute-start(bf16[128,512]{1,0:T(8,128)(2,1)S(1)} %get-tuple-element.103), channel_id=1, source_target_pairs={{0,1},{1,0},{2,3},{3,2},{4,5},{5,4},{6,7},{7,6},{8,16},{9,8},{10,2... | collective-permute-start | bytes 393224 | tf_op jit(solution)/shard_map/ppermute | solution.py:614
  25.6 7.3 %collective-permute-start.11 = (bf16[128,512]{1,0:T(8,128)(2,1)S(1)}, bf16[128,512]{1,0:T(8,128)(2,1)S(1)}, u32[]{:S(2)}, u32[]{:S(2)}) collective-permute-start(bf16[128,512]{1,0:T(8,128)(2,1)S(1)} %next.8), channel_id=1, source_target_pairs={{0,1},{1,0},{2,3},{3,2},{4,5},{5,4},{6,7},{7,6},{8,16},{9,8},{10,2... | collective-permute-start | bytes 393224 | tf_op jit(solution)/shard_map/ppermute | solution.py:614
  27.1 7.2 %collective-permute-start.12 = (bf16[128,512]{1,0:T(8,128)(2,1)S(1)}, bf16[128,512]{1,0:T(8,128)(2,1)S(1)}, u32[]{:S(2)}, u32[]{:S(2)}) collective-permute-start(bf16[128,512]{1,0:T(8,128)(2,1)S(1)} %next.9), channel_id=1, source_target_pairs={{0,1},{1,0},{2,3},{3,2},{4,5},{5,4},{6,7},{7,6},{8,16},{9,8},{10,2... | collective-permute-start | bytes 393224 | tf_op jit(solution)/shard_map/ppermute | solution.py:614
  34.4 7.8 %collective-permute-start.15 = (bf16[128,512]{1,0:T(8,128)(2,1)S(1)}, bf16[128,512]{1,0:T(8,128)(2,1)S(1)}, u32[]{:S(2)}, u32[]{:S(2)}) collective-permute-start(bf16[128,512]{1,0:T(8,128)(2,1)S(1)} %get-tuple-element.114), channel_id=1, source_target_pairs={{0,1},{1,0},{2,3},{3,2},{4,5},{5,21},{6,7},{7,6},{8,9},{9,8},{10,1... | collective-permute-start | bytes 393224 | tf_op jit(solution)/shard_map/ppermute | solution.py:614
  34.4 7.8 %collective-permute-start.14 = (bf16[128,512]{1,0:T(8,128)(2,1)S(1)}, bf16[128,512]{1,0:T(8,128)(2,1)S(1)}, u32[]{:S(2)}, u32[]{:S(2)}) collective-permute-start(bf16[128,512]{1,0:T(8,128)(2,1)S(1)} %far_part.3), channel_id=1, source_target_pairs={{0,1},{1,0},{2,3},{3,2},{4,5},{5,4},{6,7},{7,17},{8,9},{9,8},{10,1... | collective-permute-start | bytes 393224 | tf_op jit(solution)/shard_map/ppermute | solution.py:614
  34.9 9.3 %collective-permute-start.16 = (bf16[128,512]{1,0:T(8,128)(2,1)S(1)}, bf16[128,512]{1,0:T(8,128)(2,1)S(1)}, u32[]{:S(2)}, u32[]{:S(2)}) collective-permute-start(bf16[128,512]{1,0:T(8,128)(2,1)S(1)} %near_part.2), channel_id=1, source_target_pairs={{0,1},{1,0},{2,3},{3,17},{4,5},{5,4},{6,7},{7,6},{8,9},{9,27},{10,... | collective-permute-start | bytes 393224 | tf_op jit(solution)/shard_map/ppermute | solution.py:614
  42.2 2.0 %collective-permute-start.17 = (bf16[128,512]{1,0:T(8,128)(2,1)S(1)}, bf16[128,512]{1,0:T(8,128)(2,1)S(1)}, u32[]{:S(2)}, u32[]{:S(2)}) collective-permute-start(bf16[128,512]{1,0:T(8,128)(2,1)S(1)} %near_part.3.refs_3_), channel_id=1, source_target_pairs={{0,1},{1,17},{2,3},{3,2},{4,5},{5,4},{6,7},{7,6},{8,9},{9,8},{10,1... | collective-permute-start | bytes 393224 | tf_op jit(solution)/shard_map/ppermute | solution.py:614
  42.2 6.5 %copy-start.5 = (bf16[512,227]{0,1:T(8,128)(2,1)S(1)}, bf16[512,227]{0,1:T(8,128)(2,1)}, u32[]{:S(2)}) copy-start(bf16[512,227]{0,1:T(8,128)(2,1)} %param.18) | copy-start | bytes 697348
  44.2 4.5 %collective-permute-start.18 = (bf16[64,512]{1,0:T(8,128)(2,1)S(1)}, bf16[64,512]{1,0:T(8,128)(2,1)S(1)}, u32[]{:S(2)}, u32[]{:S(2)}) collective-permute-start(bf16[64,512]{1,0:T(8,128)(2,1)S(1)} %get-tuple-element.116), channel_id=1, source_target_pairs={{0,1},{1,0},{2,3},{3,2},{4,5},{5,4},{6,7},{7,6},{8,9},{9,8},{10,11... | collective-permute-start | bytes 196616 | tf_op jit(solution)/shard_map/ppermute | solution.py:633

commit v20 on v17

--- a/solution.py
+++ b/solution.py
@@ -234,10 +234,10 @@
         payload[mesh_rows:, :] = coded
 
 
-def join_kernel(*refs):
+def join_kernel(places, *refs):
     payloads, joined = refs[:-1], refs[-1]
     rows = payloads[0].shape[0]
-    for place, payload in enumerate(payloads):
+    for place, payload in zip(places, payloads):
         joined[place * rows : (place + 1) * rows, :] = payload[...]
 
 
@@ -677,9 +677,10 @@
         [pltpu.VMEM((width, width), bf16)] * 2 + [pltpu.SemaphoreType.DMA((5,))],
     )
     own_payload, *held = lax.optimization_barrier((payloads[0], *held))
-    arrived = [own_payload] + [to_chip(payloads[turn], turn) for turn in range(1, samples)]
+    longest_first = sorted(range(1, samples), key=lambda turn: (turn < samples // 2, turn))
+    arrived = [to_chip(payloads[turn], turn) for turn in longest_first] + [own_payload]
     (joined,) = call(
-        join_kernel,
+        functools.partial(join_kernel, longest_first + [0]),
         "join",
         [jax.ShapeDtypeStruct((samples * (mesh_rows + 2 * fanout), width), bf16)],
         arrived,

time: 50.9 us -> 50.6 us (level)
    ppermute x3, starting transfers between devices: 4.36 us -> 2.84 us  [to_chip(): return lax.ppermute(value, ('segment', 'dom'), pairs)]
    ppermute x14, starting transfers between devices: 24.9 us -> 25.7 us  [send(): lax.ppermute(value, ('segment', 'dom'), every_device(pairs, segments * pa...]
    ppermute x2, starting transfers between devices: 3.72 us -> 4.46 us  [change_lane(): return lax.ppermute(value, 'dom', pairs)]
where the time goes in v20:
time: 50.6 us; the launch traced here: 50 us
  starting transfers between devices  33.1 us (65%)
  waiting for transfers between devices  9.97 us (20%)
  local copies, waits for them, and re-layouts  3.46 us (7%)
  Pallas kernels  3.21 us (6%)
    ppermute x14, starting transfers between devices, send(): lax.ppermute(value, ('segment', 'dom'), every_device(pairs, segments * pa...  25.7 us
    ppermute x14, waiting for transfers between devices, send(): lax.ppermute(value, ('segment', 'dom'), every_device(pairs, segments * pa...  7.81 us
    ppermute x2, starting transfers between devices, change_lane(): return lax.ppermute(value, 'dom', pairs)  4.46 us
    unnamed x23, local copies, waits for them, and re-layouts  3.46 us
    pallas_call x30, Pallas kernels, call(): pl.pallas_call(located if places[0] == 'w' else kernel, out_shape=shapes,...  3.21 us
    ppermute x3, starting transfers between devices, to_chip(): return lax.ppermute(value, ('segment', 'dom'), pairs)  2.84 us
    ppermute x2, waiting for transfers between devices, change_lane(): return lax.ppermute(value, 'dom', pairs)  2.16 us
  transfers between devices with their start and end apart: 19, of which 7 were waited for; matrix products, arithmetic and copies ran while one was open for 2% of the time, Pallas kernels for 4%

profile of v20, /device:TPU:3, one launch (start us, length us, event | category | flops | bytes accessed | tf_op | source)
XLA Modules:
  0.0 50.0 jit_solution(8914038281252858466)
XLA Ops:
  0.0 0.7 %collective-permute-start.4 = (bf16[1,512,1024]{2,1,0:T(8,128)(2,1)}, bf16[1,512,1024]{2,1,0:T(8,128)(2,1)S(1)}, u32[]{:S(2)}, u32[]{:S(2)}) collective-permute-start(bf16[1,512,1024]{2,1,0:T(8,128)(2,1)} %w_project), channel_id=1, source_target_pairs={{0,1},{1,0},{2,3},{3,2},{4,5},{5,4},{6,7},{7,6},{8,9},{9,8},{10,11... | collective-permute-start | bytes 3145736 | tf_op jit(solution)/shard_map/ppermute | solution.py:616
  0.8 1.0 %copy.15 = bf16[4,128,227]{1,2,0:T(8,128)(2,1)S(1)} copy(bf16[4,128,227]{1,0,2:T(4,128)(2,1)} %param.12) | data formatting | bytes 464896 | tf_op args[0]
  1.8 0.7 %encode.1 = (bf16[80,512]{1,0:T(8,128)(2,1)S(1)}, bf16[80,512]{1,0:T(8,128)(2,1)S(1)}, bf16[80,512]{1,0:T(8,128)(2,1)S(1)}, bf16[80,512]{1,0:T(8,128)(2,1)S(1)}) custom-call(s32[1]{0:T(128)} %bitcast.segment, s32[1]{0:T(128)} %bitcast.1.place, bf16[4,227,128]{2,1,0:T(8,128)(2,1)S(1)} %bitcast.13, bf16[227,512]{1,0:T(8,128)(2,1)S(1)} %copy-done.3, ...), custom_call_target="tpu_custom_call" | custom-call | bytes 799752 | tf_op jit(solution)/shard_map/encode/pallas_call | solution.py:552
  2.5 2.3 %collective-permute-start = (bf16[80,512]{1,0:T(8,128)(2,1)S(1)}, bf16[80,512]{1,0:T(8,128)(2,1)S(1)}, u32[]{:S(2)}, u32[]{:S(2)}) collective-permute-start(bf16[80,512]{1,0:T(8,128)(2,1)S(1)} %get-tuple-element.63), channel_id=1, source_target_pairs={{0,8},{1,9},{2,10},{3,11},{4,12},{5,13},{6,14},{7,15},{8,4},{9,5},... | collective-permute-start | bytes 245768 | tf_op jit(solution)/shard_map/ppermute | solution.py:631
  4.9 0.4 collective-permute-start.1
  5.3 0.1 collective-permute-start.2
  5.4 0.0 copy-done.4
  5.4 1.2 %copy-done.1 = bf16[1,1024,512]{2,1,0:T(8,128)(2,1)S(1)} copy-done((bf16[1,1024,512]{2,1,0:T(8,128)(2,1)S(1)}, bf16[1,1024,512]{2,1,0:T(8,128)(2,1)}, u32[]{:S(2)}) %copy-start.1) | copy-done | bytes 1048600
  6.6 1.2 %copy-done.2 = bf16[1,512,1024]{2,1,0:T(8,128)(2,1)S(1)} copy-done((bf16[1,512,1024]{2,1,0:T(8,128)(2,1)S(1)}, bf16[1,512,1024]{2,1,0:T(8,128)(2,1)}, u32[]{:S(2)}) %copy-start.2) | copy-done | bytes 1048600
  7.8 0.7 %hold.1 = (bf16[512,512]{1,0:T(8,128)(2,1)S(1)}, bf16[512,512]{1,0:T(8,128)(2,1)S(1)}, bf16[512,512]{1,0:T(8,128)(2,1)S(1)}, bf16[512,512]{1,0:T(8,128)(2,1)S(1)}) custom-call(bf16[1,512,1024]{2,1,0:T(8,128)(2,1)S(1)} %copy-done.2, bf16[1,512,512]{2,1,0:T(8,128)(2,1)S(1)} %copy-done.4, bf16[1,1024,512]{2,1,0:T(8,128)(2,1)S(1)} %copy-done.1), custom_call_target="tpu_custom_call" | custom-call | bytes 4718592 | tf_op jit(solution)/shard_map/hold/pallas_call | solution.py:552
  8.6 0.0 collective-permute-done.refs_0_
  8.6 0.0 collective-permute-done.1.refs_1_
  8.6 0.0 collective-permute-done.2.refs_2_
  8.6 0.5 %collective-permute-start.3 = (bf16[320,512]{1,0:T(8,128)(2,1)S(1)}, bf16[320,512]{1,0:T(8,128)(2,1)S(1)}, u32[]{:S(2)}, u32[]{:S(2)}) collective-permute-start(bf16[320,512]{1,0:T(8,128)(2,1)S(1)} %join.1.refs_0_), channel_id=1, source_target_pairs={{0,1},{1,0},{2,3},{3,2},{4,5},{5,4},{6,7},{7,6},{8,9},{9,8},{10,11... | collective-permute-start | bytes 983048 | tf_op jit(solution)/shard_map/ppermute | solution.py:635
  9.1 1.3 %collective-permute-done.3.refs_1_ = bf16[320,512]{1,0:T(8,128)(2,1)S(1)} collective-permute-done((bf16[320,512]{1,0:T(8,128)(2,1)S(1)}, bf16[320,512]{1,0:T(8,128)(2,1)S(1)}, u32[]{:S(2)}, u32[]{:S(2)}) %collective-permute-start.3) | collective-permute-done | bytes 327712 | tf_op jit(solution)/shard_map/ppermute | solution.py:635
  10.4 0.0 collective-permute-done.4.refs_2_.refs_10_.refs_13_.refs_6_.refs_7_
  10.4 0.4 collective-permute-start.13
  10.8 3.5 %collective-permute-start.5 = (bf16[144,512]{1,0:T(8,128)(2,1)S(1)}, bf16[144,512]{1,0:T(8,128)(2,1)S(1)}, u32[]{:S(2)}, u32[]{:S(2)}) collective-permute-start(bf16[144,512]{1,0:T(8,128)(2,1)S(1)} %get-tuple-element.85), channel_id=1, source_target_pairs={{0,8},{1,0},{2,10},{3,2},{4,12},{5,4},{6,14},{7,6},{8,9},{9,1},{10... | collective-permute-start | bytes 442376 | tf_op jit(solution)/shard_map/ppermute | solution.py:616
  14.2 1.7 %collective-permute-start.6 = (bf16[128,512]{1,0:T(8,128)(2,1)S(1)}, bf16[128,512]{1,0:T(8,128)(2,1)S(1)}, u32[]{:S(2)}, u32[]{:S(2)}) collective-permute-start(bf16[128,512]{1,0:T(8,128)(2,1)S(1)} %next.5), channel_id=1, source_target_pairs={{0,8},{1,0},{2,10},{3,2},{4,12},{5,4},{6,14},{7,6},{8,9},{9,1},{10... | collective-permute-start | bytes 393224 | tf_op jit(solution)/shard_map/ppermute | solution.py:616
  15.9 1.5 %collective-permute-start.7 = (bf16[128,512]{1,0:T(8,128)(2,1)S(1)}, bf16[128,512]{1,0:T(8,128)(2,1)S(1)}, u32[]{:S(2)}, u32[]{:S(2)}) collective-permute-start(bf16[128,512]{1,0:T(8,128)(2,1)S(1)} %next.6), channel_id=1, source_target_pairs={{0,8},{1,0},{2,10},{3,2},{4,12},{5,4},{6,14},{7,6},{8,9},{9,1},{10... | collective-permute-start | bytes 393224 | tf_op jit(solution)/shard_map/ppermute | solution.py:616
  17.4 1.5 %collective-permute-start.9 = (bf16[128,512]{1,0:T(8,128)(2,1)S(1)}, bf16[128,512]{1,0:T(8,128)(2,1)S(1)}, u32[]{:S(2)}, u32[]{:S(2)}) collective-permute-start(bf16[128,512]{1,0:T(8,128)(2,1)S(1)} %next.7), channel_id=1, source_target_pairs={{0,8},{1,0},{2,10},{3,2},{4,12},{5,4},{6,14},{7,6},{8,9},{9,1},{10... | collective-permute-start | bytes 393224 | tf_op jit(solution)/shard_map/ppermute | solution.py:616
  18.9 0.0 copy-done.6
  18.9 0.4 prepare.1
  19.3 0.0 collective-permute-done.5.refs_0_.refs_5_.refs_1_
  19.3 0.0 collective-permute-done.6.refs_0_.refs_4_.refs_2_
  19.4 0.0 collective-permute-done.7.refs_0_.refs_3_
  19.4 4.4 %collective-permute-start.8 = (bf16[144,512]{1,0:T(8,128)(2,1)S(1)}, bf16[144,512]{1,0:T(8,128)(2,1)S(1)}, u32[]{:S(2)}, u32[]{:S(2)}) collective-permute-start(bf16[144,512]{1,0:T(8,128)(2,1)S(1)} %early.2), channel_id=1, source_target_pairs={{0,1},{1,0},{2,3},{3,2},{4,5},{5,4},{6,7},{7,6},{8,16},{9,8},{10,2... | collective-permute-start | bytes 442376 | tf_op jit(solution)/shard_map/ppermute | solution.py:616
  23.8 0.0 collective-permute-done.9.refs_4_
  23.8 1.6 %collective-permute-start.10 = (bf16[128,512]{1,0:T(8,128)(2,1)S(1)}, bf16[128,512]{1,0:T(8,128)(2,1)S(1)}, u32[]{:S(2)}, u32[]{:S(2)}) collective-permute-start(bf16[128,512]{1,0:T(8,128)(2,1)S(1)} %get-tuple-element.103), channel_id=1, source_target_pairs={{0,1},{1,0},{2,3},{3,2},{4,5},{5,4},{6,7},{7,6},{8,16},{9,8},{10,2... | collective-permute-start | bytes 393224 | tf_op jit(solution)/shard_map/ppermute | solution.py:616
  25.3 1.5 %collective-permute-start.11 = (bf16[128,512]{1,0:T(8,128)(2,1)S(1)}, bf16[128,512]{1,0:T(8,128)(2,1)S(1)}, u32[]{:S(2)}, u32[]{:S(2)}) collective-permute-start(bf16[128,512]{1,0:T(8,128)(2,1)S(1)} %next.8), channel_id=1, source_target_pairs={{0,1},{1,0},{2,3},{3,2},{4,5},{5,4},{6,7},{7,6},{8,16},{9,8},{10,2... | collective-permute-start | bytes 393224 | tf_op jit(solution)/shard_map/ppermute | solution.py:616
  26.8 1.6 %collective-permute-start.12 = (bf16[128,512]{1,0:T(8,128)(2,1)S(1)}, bf16[128,512]{1,0:T(8,128)(2,1)S(1)}, u32[]{:S(2)}, u32[]{:S(2)}) collective-permute-start(bf16[128,512]{1,0:T(8,128)(2,1)S(1)} %next.9), channel_id=1, source_target_pairs={{0,1},{1,0},{2,3},{3,2},{4,5},{5,4},{6,7},{7,6},{8,16},{9,8},{10,2... | collective-permute-start | bytes 393224 | tf_op jit(solution)/shard_map/ppermute | solution.py:616
  28.5 1.7 %collective-permute-done.8.refs_0_.refs_5_.refs_1_ = bf16[144,512]{1,0:T(8,128)(2,1)S(1)} collective-permute-done((bf16[144,512]{1,0:T(8,128)(2,1)S(1)}, bf16[144,512]{1,0:T(8,128)(2,1)S(1)}, u32[]{:S(2)}, u32[]{:S(2)}) %collective-permute-start.8) | collective-permute-done | bytes 147488 | tf_op jit(solution)/shard_map/ppermute | solution.py:616
  30.1 1.4 %collective-permute-done.10.refs_0_.refs_4_.refs_2_ = bf16[128,512]{1,0:T(8,128)(2,1)S(1)} collective-permute-done((bf16[128,512]{1,0:T(8,128)(2,1)S(1)}, bf16[128,512]{1,0:T(8,128)(2,1)S(1)}, u32[]{:S(2)}, u32[]{:S(2)}) %collective-permute-start.10) | collective-permute-done | bytes 131104 | tf_op jit(solution)/shard_map/ppermute | solution.py:616
  31.5 1.4 %collective-permute-done.11.refs_0_.refs_3_ = bf16[128,512]{1,0:T(8,128)(2,1)S(1)} collective-permute-done((bf16[128,512]{1,0:T(8,128)(2,1)S(1)}, bf16[128,512]{1,0:T(8,128)(2,1)S(1)}, u32[]{:S(2)}, u32[]{:S(2)}) %collective-permute-start.11) | collective-permute-done | bytes 131104 | tf_op jit(solution)/shard_map/ppermute | solution.py:616
  33.0 0.0 collective-permute-done.13.refs_11_.refs_14_.refs_7_.refs_8_
  33.0 1.4 %collective-permute-done.12.refs_4_ = bf16[128,512]{1,0:T(8,128)(2,1)S(1)} collective-permute-done((bf16[128,512]{1,0:T(8,128)(2,1)S(1)}, bf16[128,512]{1,0:T(8,128)(2,1)S(1)}, u32[]{:S(2)}, u32[]{:S(2)}) %collective-permute-start.12) | collective-permute-done | bytes 131104 | tf_op jit(solution)/shard_map/ppermute | solution.py:616
  34.4 0.0 collective-permute-start.15
  34.4 0.5 %collective-permute-start.14 = (bf16[128,512]{1,0:T(8,128)(2,1)S(1)}, bf16[128,512]{1,0:T(8,128)(2,1)S(1)}, u32[]{:S(2)}, u32[]{:S(2)}) collective-permute-start(bf16[128,512]{1,0:T(8,128)(2,1)S(1)} %far_part.3), channel_id=1, source_target_pairs={{0,1},{1,0},{2,3},{3,2},{4,5},{5,4},{6,7},{7,17},{8,9},{9,8},{10,1... | collective-permute-start | bytes 393224 | tf_op jit(solution)/shard_map/ppermute | solution.py:616
  34.9 7.0 %collective-permute-start.16 = (bf16[128,512]{1,0:T(8,128)(2,1)S(1)}, bf16[128,512]{1,0:T(8,128)(2,1)S(1)}, u32[]{:S(2)}, u32[]{:S(2)}) collective-permute-start(bf16[128,512]{1,0:T(8,128)(2,1)S(1)} %near_part.2.refs_3_), channel_id=1, source_target_pairs={{0,1},{1,17},{2,3},{3,2},{4,5},{5,4},{6,7},{7,6},{8,9},{9,27},{10,... | collective-permute-start | bytes 393224 | tf_op jit(solution)/shard_map/ppermute | solution.py:616
  41.9 0.0 collective-permute-start.17
  41.9 0.0 collective-permute-done.15.refs_0_
  41.9 0.0 collective-permute-done.14.refs_0_
  41.9 0.0 copy-start.5
  41.9 1.9 %collective-permute-done.16.refs_1_ = bf16[128,512]{1,0:T(8,128)(2,1)S(1)} collective-permute-done((bf16[128,512]{1,0:T(8,128)(2,1)S(1)}, bf16[128,512]{1,0:T(8,128)(2,1)S(1)}, u32[]{:S(2)}, u32[]{:S(2)}) %collective-permute-start.16) | collective-permute-done | bytes 131104 | tf_op jit(solution)/shard_map/ppermute | solution.py:616
  43.8 0.0 collective-permute-done.17.refs_2_
  43.9 4.0 %collective-permute-start.18 = (bf16[64,512]{1,0:T(8,128)(2,1)S(1)}, bf16[64,512]{1,0:T(8,128)(2,1)S(1)}, u32[]{:S(2)}, u32[]{:S(2)}) collective-permute-start(bf16[64,512]{1,0:T(8,128)(2,1)S(1)} %get-tuple-element.116), channel_id=1, source_target_pairs={{0,1},{1,0},{2,3},{3,2},{4,5},{5,4},{6,7},{7,6},{8,9},{9,8},{10,11... | collective-permute-start | bytes 196616 | tf_op jit(solution)/shard_map/ppermute | solution.py:635
  47.8 0.9 %collective-permute-done.18.refs_5_ = bf16[64,512]{1,0:T(8,128)(2,1)S(1)} collective-permute-done((bf16[64,512]{1,0:T(8,128)(2,1)S(1)}, bf16[64,512]{1,0:T(8,128)(2,1)S(1)}, u32[]{:S(2)}, u32[]{:S(2)}) %collective-permute-start.18) | collective-permute-done | bytes 65568 | tf_op jit(solution)/shard_map/ppermute | solution.py:635
  48.7 1.2 %decode.1 = bf16[227,128]{1,0:T(8,128)(2,1)} custom-call(s32[1]{0:T(128)} %bitcast.segment, s32[1]{0:T(128)} %bitcast.1.place, f32[128,512]{1,0:T(8,128)S(1)} %get-tuple-element.88.refs_0_, bf16[64,128]{1,0:T(8,128)(2,1)S(1)} %get-tuple-element.89.refs_1_, bf16[1024,512]{1,0:T(8,128)(2,1)S(1)} %copy-done, bf16[227,512]{1,0:T(8,128)(2,1)S(1)} %bitcast.15, ...), custom_call_target="tpu_custom_call" | custom-call | bytes 1748744 | tf_op jit(solution)/shard_map/decode/pallas_call | solution.py:552
  (44 shorter events, 0.2 us)
Async XLA Ops:
  0.0 1.7 %copy-start.7 = (s32[64,8]{0,1:T(8,128)S(1)}, s32[64,8]{0,1:T(8,128)}, u32[]{:S(2)}) copy-start(s32[64,8]{0,1:T(8,128)} %param.21) | copy-start | bytes 6148
  0.0 1.8 %copy-start.8 = (s32[4,64]{1,0:T(4,128)S(1)}, s32[4,64]{1,0:T(4,128)}, u32[]{:S(2)}) copy-start(s32[4,64]{1,0:T(4,128)} %param.22) | copy-start | bytes 3076
  0.0 1.8 %copy-start.9 = (s32[4,1]{0,1:T(1,128)S(1)}, s32[4,1]{0,1:T(1,128)}, u32[]{:S(2)}) copy-start(s32[4,1]{0,1:T(1,128)} %param.23) | copy-start | bytes 52
  0.0 1.8 %copy-start.10 = (s32[128]{0:T(128)S(1)}, s32[128]{0:T(128)}, u32[]{:S(2)}) copy-start(s32[128]{0:T(128)} %param.19) | copy-start | bytes 1540
  0.0 1.8 %copy-start.3 = (bf16[227,512]{1,0:T(8,128)(2,1)S(1)}, bf16[227,512]{1,0:T(8,128)(2,1)}, u32[]{:S(2)}) copy-start(bf16[227,512]{1,0:T(8,128)(2,1)} %refs_1_.3) | copy-start | bytes 697348
  0.0 5.3 %copy-start.4 = (bf16[1,512,512]{2,1,0:T(8,128)(2,1)S(1)}, bf16[1,512,512]{2,1,0:T(8,128)(2,1)}, u32[]{:S(2)}) copy-start(bf16[1,512,512]{2,1,0:T(8,128)(2,1)} %w_message.1) | copy-start | bytes 1572868
  0.0 10.4 %collective-permute-start.4 = (bf16[1,512,1024]{2,1,0:T(8,128)(2,1)}, bf16[1,512,1024]{2,1,0:T(8,128)(2,1)S(1)}, u32[]{:S(2)}, u32[]{:S(2)}) collective-permute-start(bf16[1,512,1024]{2,1,0:T(8,128)(2,1)} %w_project), channel_id=1, source_target_pairs={{0,1},{1,0},{2,3},{3,2},{4,5},{5,4},{6,7},{7,6},{8,9},{9,8},{10,11... | collective-permute-start | bytes 3145736 | tf_op jit(solution)/shard_map/ppermute | solution.py:616
  2.5 6.0 %collective-permute-start = (bf16[80,512]{1,0:T(8,128)(2,1)S(1)}, bf16[80,512]{1,0:T(8,128)(2,1)S(1)}, u32[]{:S(2)}, u32[]{:S(2)}) collective-permute-start(bf16[80,512]{1,0:T(8,128)(2,1)S(1)} %get-tuple-element.63), channel_id=1, source_target_pairs={{0,8},{1,9},{2,10},{3,11},{4,12},{5,13},{6,14},{7,15},{8,4},{9,5},... | collective-permute-start | bytes 245768 | tf_op jit(solution)/shard_map/ppermute | solution.py:631
  4.9 3.7 %collective-permute-start.1 = (bf16[80,512]{1,0:T(8,128)(2,1)S(1)}, bf16[80,512]{1,0:T(8,128)(2,1)S(1)}, u32[]{:S(2)}, u32[]{:S(2)}) collective-permute-start(bf16[80,512]{1,0:T(8,128)(2,1)S(1)} %get-tuple-element.64), channel_id=1, source_target_pairs={{0,16},{1,17},{2,18},{3,19},{4,20},{5,21},{6,22},{7,23},{8,9},{9,8... | collective-permute-start | bytes 245768 | tf_op jit(solution)/shard_map/ppermute | solution.py:631
  5.3 3.3 %collective-permute-start.2 = (bf16[80,512]{1,0:T(8,128)(2,1)S(1)}, bf16[80,512]{1,0:T(8,128)(2,1)S(1)}, u32[]{:S(2)}, u32[]{:S(2)}) collective-permute-start(bf16[80,512]{1,0:T(8,128)(2,1)S(1)} %get-tuple-element.65), channel_id=1, source_target_pairs={{0,2},{1,3},{2,0},{3,1},{4,6},{5,7},{6,4},{7,5},{8,9},{9,8},{10,11... | collective-permute-start | bytes 245768 | tf_op jit(solution)/shard_map/ppermute | solution.py:631
  5.4 1.2 %copy-start.1 = (bf16[1,1024,512]{2,1,0:T(8,128)(2,1)S(1)}, bf16[1,1024,512]{2,1,0:T(8,128)(2,1)}, u32[]{:S(2)}) copy-start(bf16[1,1024,512]{2,1,0:T(8,128)(2,1)} %w_update.1) | copy-start | bytes 3145732
  6.6 1.2 %copy-start.2 = (bf16[1,512,1024]{2,1,0:T(8,128)(2,1)S(1)}, bf16[1,512,1024]{2,1,0:T(8,128)(2,1)}, u32[]{:S(2)}) copy-start(bf16[1,512,1024]{2,1,0:T(8,128)(2,1)} %w_project) | copy-start | bytes 3145732
  8.6 1.8 %collective-permute-start.3 = (bf16[320,512]{1,0:T(8,128)(2,1)S(1)}, bf16[320,512]{1,0:T(8,128)(2,1)S(1)}, u32[]{:S(2)}, u32[]{:S(2)}) collective-permute-start(bf16[320,512]{1,0:T(8,128)(2,1)S(1)} %join.1.refs_0_), channel_id=1, source_target_pairs={{0,1},{1,0},{2,3},{3,2},{4,5},{5,4},{6,7},{7,6},{8,9},{9,8},{10,11... | collective-permute-start | bytes 983048 | tf_op jit(solution)/shard_map/ppermute | solution.py:635
  10.4 22.6 %collective-permute-start.13 = (bf16[2,512,512]{2,1,0:T(8,128)(2,1)S(1)}, bf16[2,512,512]{2,1,0:T(8,128)(2,1)S(1)}, u32[]{:S(2)}, u32[]{:S(2)}) collective-permute-start(bf16[2,512,512]{2,1,0:T(8,128)(2,1)S(1)} %pack.1), channel_id=1, source_target_pairs={{0,1},{1,0},{2,3},{3,2},{4,5},{5,4},{6,7},{7,6},{8,9},{9,8},{10,11... | collective-permute-start | bytes 3145736 | tf_op jit(solution)/shard_map/ppermute | solution.py:616
  10.8 8.5 %collective-permute-start.5 = (bf16[144,512]{1,0:T(8,128)(2,1)S(1)}, bf16[144,512]{1,0:T(8,128)(2,1)S(1)}, u32[]{:S(2)}, u32[]{:S(2)}) collective-permute-start(bf16[144,512]{1,0:T(8,128)(2,1)S(1)} %get-tuple-element.85), channel_id=1, source_target_pairs={{0,8},{1,0},{2,10},{3,2},{4,12},{5,4},{6,14},{7,6},{8,9},{9,1},{10... | collective-permute-start | bytes 442376 | tf_op jit(solution)/shard_map/ppermute | solution.py:616
  14.2 5.1 %collective-permute-start.6 = (bf16[128,512]{1,0:T(8,128)(2,1)S(1)}, bf16[128,512]{1,0:T(8,128)(2,1)S(1)}, u32[]{:S(2)}, u32[]{:S(2)}) collective-permute-start(bf16[128,512]{1,0:T(8,128)(2,1)S(1)} %next.5), channel_id=1, source_target_pairs={{0,8},{1,0},{2,10},{3,2},{4,12},{5,4},{6,14},{7,6},{8,9},{9,1},{10... | collective-permute-start | bytes 393224 | tf_op jit(solution)/shard_map/ppermute | solution.py:616
  15.9 3.0 %copy-start = (bf16[1024,512]{1,0:T(8,128)(2,1)S(1)}, bf16[1024,512]{1,0:T(8,128)(2,1)}, u32[]{:S(2)}) copy-start(bf16[1024,512]{1,0:T(8,128)(2,1)} %refs_2_.3) | copy-start | bytes 3145732
  15.9 3.5 %collective-permute-start.7 = (bf16[128,512]{1,0:T(8,128)(2,1)S(1)}, bf16[128,512]{1,0:T(8,128)(2,1)S(1)}, u32[]{:S(2)}, u32[]{:S(2)}) collective-permute-start(bf16[128,512]{1,0:T(8,128)(2,1)S(1)} %next.6), channel_id=1, source_target_pairs={{0,8},{1,0},{2,10},{3,2},{4,12},{5,4},{6,14},{7,6},{8,9},{9,1},{10... | collective-permute-start | bytes 393224 | tf_op jit(solution)/shard_map/ppermute | solution.py:616
  17.4 1.5 %copy-start.6 = (s32[128]{0:T(128)S(1)}, s32[128]{0:T(128)}, u32[]{:S(2)}) copy-start(s32[128]{0:T(128)} %param.20) | copy-start | bytes 1540
  17.4 6.4 %collective-permute-start.9 = (bf16[128,512]{1,0:T(8,128)(2,1)S(1)}, bf16[128,512]{1,0:T(8,128)(2,1)S(1)}, u32[]{:S(2)}, u32[]{:S(2)}) collective-permute-start(bf16[128,512]{1,0:T(8,128)(2,1)S(1)} %next.7), channel_id=1, source_target_pairs={{0,8},{1,0},{2,10},{3,2},{4,12},{5,4},{6,14},{7,6},{8,9},{9,1},{10... | collective-permute-start | bytes 393224 | tf_op jit(solution)/shard_map/ppermute | solution.py:616
  19.4 10.7 %collective-permute-start.8 = (bf16[144,512]{1,0:T(8,128)(2,1)S(1)}, bf16[144,512]{1,0:T(8,128)(2,1)S(1)}, u32[]{:S(2)}, u32[]{:S(2)}) collective-permute-start(bf16[144,512]{1,0:T(8,128)(2,1)S(1)} %early.2), channel_id=1, source_target_pairs={{0,1},{1,0},{2,3},{3,2},{4,5},{5,4},{6,7},{7,6},{8,16},{9,8},{10,2... | collective-permute-start | bytes 442376 | tf_op jit(solution)/shard_map/ppermute | solution.py:616
  23.8 7.8 %collective-permute-start.10 = (bf16[128,512]{1,0:T(8,128)(2,1)S(1)}, bf16[128,512]{1,0:T(8,128)(2,1)S(1)}, u32[]{:S(2)}, u32[]{:S(2)}) collective-permute-start(bf16[128,512]{1,0:T(8,128)(2,1)S(1)} %get-tuple-element.103), channel_id=1, source_target_pairs={{0,1},{1,0},{2,3},{3,2},{4,5},{5,4},{6,7},{7,6},{8,16},{9,8},{10,2... | collective-permute-start | bytes 393224 | tf_op jit(solution)/shard_map/ppermute | solution.py:616
  25.3 7.6 %collective-permute-start.11 = (bf16[128,512]{1,0:T(8,128)(2,1)S(1)}, bf16[128,512]{1,0:T(8,128)(2,1)S(1)}, u32[]{:S(2)}, u32[]{:S(2)}) collective-permute-start(bf16[128,512]{1,0:T(8,128)(2,1)S(1)} %next.8), channel_id=1, source_target_pairs={{0,1},{1,0},{2,3},{3,2},{4,5},{5,4},{6,7},{7,6},{8,16},{9,8},{10,2... | collective-permute-start | bytes 393224 | tf_op jit(solution)/shard_map/ppermute | solution.py:616
  26.8 7.5 %collective-permute-start.12 = (bf16[128,512]{1,0:T(8,128)(2,1)S(1)}, bf16[128,512]{1,0:T(8,128)(2,1)S(1)}, u32[]{:S(2)}, u32[]{:S(2)}) collective-permute-start(bf16[128,512]{1,0:T(8,128)(2,1)S(1)} %next.9), channel_id=1, source_target_pairs={{0,1},{1,0},{2,3},{3,2},{4,5},{5,4},{6,7},{7,6},{8,16},{9,8},{10,2... | collective-permute-start | bytes 393224 | tf_op jit(solution)/shard_map/ppermute | solution.py:616
  34.4 7.5 %collective-permute-start.15 = (bf16[128,512]{1,0:T(8,128)(2,1)S(1)}, bf16[128,512]{1,0:T(8,128)(2,1)S(1)}, u32[]{:S(2)}, u32[]{:S(2)}) collective-permute-start(bf16[128,512]{1,0:T(8,128)(2,1)S(1)} %get-tuple-element.114), channel_id=1, source_target_pairs={{0,1},{1,0},{2,3},{3,2},{4,5},{5,21},{6,7},{7,6},{8,9},{9,8},{10,1... | collective-permute-start | bytes 393224 | tf_op jit(solution)/shard_map/ppermute | solution.py:616
  34.4 7.5 %collective-permute-start.14 = (bf16[128,512]{1,0:T(8,128)(2,1)S(1)}, bf16[128,512]{1,0:T(8,128)(2,1)S(1)}, u32[]{:S(2)}, u32[]{:S(2)}) collective-permute-start(bf16[128,512]{1,0:T(8,128)(2,1)S(1)} %far_part.3), channel_id=1, source_target_pairs={{0,1},{1,0},{2,3},{3,2},{4,5},{5,4},{6,7},{7,17},{8,9},{9,8},{10,1... | collective-permute-start | bytes 393224 | tf_op jit(solution)/shard_map/ppermute | solution.py:616
  34.9 9.0 %collective-permute-start.16 = (bf16[128,512]{1,0:T(8,128)(2,1)S(1)}, bf16[128,512]{1,0:T(8,128)(2,1)S(1)}, u32[]{:S(2)}, u32[]{:S(2)}) collective-permute-start(bf16[128,512]{1,0:T(8,128)(2,1)S(1)} %near_part.2.refs_3_), channel_id=1, source_target_pairs={{0,1},{1,17},{2,3},{3,2},{4,5},{5,4},{6,7},{7,6},{8,9},{9,27},{10,... | collective-permute-start | bytes 393224 | tf_op jit(solution)/shard_map/ppermute | solution.py:616
  41.9 2.0 %collective-permute-start.17 = (bf16[128,512]{1,0:T(8,128)(2,1)S(1)}, bf16[128,512]{1,0:T(8,128)(2,1)S(1)}, u32[]{:S(2)}, u32[]{:S(2)}) collective-permute-start(bf16[128,512]{1,0:T(8,128)(2,1)S(1)} %near_part.3.refs_4_), channel_id=1, source_target_pairs={{0,1},{1,0},{2,3},{3,17},{4,5},{5,4},{6,7},{7,6},{8,9},{9,8},{10,1... | collective-permute-start | bytes 393224 | tf_op jit(solution)/shard_map/ppermute | solution.py:616
  41.9 6.8 %copy-start.5 = (bf16[512,227]{0,1:T(8,128)(2,1)S(1)}, bf16[512,227]{0,1:T(8,128)(2,1)}, u32[]{:S(2)}) copy-start(bf16[512,227]{0,1:T(8,128)(2,1)} %param.18) | copy-start | bytes 697348
  43.9 4.9 %collective-permute-start.18 = (bf16[64,512]{1,0:T(8,128)(2,1)S(1)}, bf16[64,512]{1,0:T(8,128)(2,1)S(1)}, u32[]{:S(2)}, u32[]{:S(2)}) collective-permute-start(bf16[64,512]{1,0:T(8,128)(2,1)S(1)} %get-tuple-element.116), channel_id=1, source_target_pairs={{0,1},{1,0},{2,3},{3,2},{4,5},{5,4},{6,7},{7,6},{8,9},{9,8},{10,11... | collective-permute-start | bytes 196616 | tf_op jit(solution)/shard_map/ppermute | solution.py:635

commit v21 on v20

--- a/solution.py
+++ b/solution.py
@@ -785,26 +785,20 @@
         "w" + "v" * (2 + len(pieces + senders + held + came)),
         [pltpu.VMEM((nodes, width), bf16)] * 2,
     )
-    far = []
-    for begin in range(0, nodes // 2, share):
-        found = call(
-            functools.partial(end_kernel, group, last, samples, True, begin, not far, fanout),
-            "far_part",
-            [whole] * (not far) + [short],
-            [where, columns, state] + ([sender] if far else []) + held + came,
-            "w" + "v" * (9 if far else 8),
-        )
-        sender = found[0] if not far else sender
-        far.append(found[-1])
-    near = []
-    for begin in range(0, nodes // 2, share):
-        near += call(
-            functools.partial(end_kernel, group, last, samples, False, begin, False, fanout),
-            "near_part",
-            [short],
-            [where, columns, state, sender] + held + came,
-            "w" + "v" * 9,
-        )
+    sender, *far = call(
+        functools.partial(end_kernel, group, last, samples, True, 0, True, fanout),
+        "far_half",
+        [whole] + [short] * (samples // 2),
+        [where, columns, state] + held + came,
+        "w" + "v" * 8,
+    )
+    near = call(
+        functools.partial(end_kernel, group, last, samples, False, 0, False, fanout),
+        "near_half",
+        [short] * (samples // 2),
+        [where, columns, state, sender] + held + came,
+        "w" + "v" * 9,
+    )
     state = far + list(near)
     each = samples // 2
     arrived = []

time: 50.6 us -> 51.3 us (1.014)
  starting transfers between devices: 33.1 us -> 33.8 us
    ppermute x2, starting transfers between devices: 4.46 us -> 5.52 us  [change_lane(): return lax.ppermute(value, 'dom', pairs)]
    pallas_call x30 -> x28, Pallas kernels: 3.21 us -> 3.21 us  [call(): pl.pallas_call(located if places[0] == 'w' else kernel, out_shape=shapes,...]
where the time goes in v21:
time: 51.3 us; the launch traced here: 51 us
  starting transfers between devices  33.8 us (66%)
  waiting for transfers between devices  10.3 us (20%)
  local copies, waits for them, and re-layouts  3.46 us (7%)
  Pallas kernels  3.21 us (6%)
    ppermute x14, starting transfers between devices, send(): lax.ppermute(value, ('segment', 'dom'), every_device(pairs, segments * pa...  25.4 us
    ppermute x14, waiting for transfers between devices, send(): lax.ppermute(value, ('segment', 'dom'), every_device(pairs, segments * pa...  8.14 us
    ppermute x2, starting transfers between devices, change_lane(): return lax.ppermute(value, 'dom', pairs)  5.52 us
    unnamed x23, local copies, waits for them, and re-layouts  3.46 us
    pallas_call x28, Pallas kernels, call(): pl.pallas_call(located if places[0] == 'w' else kernel, out_shape=shapes,...  3.21 us
    ppermute x3, starting transfers between devices, to_chip(): return lax.ppermute(value, ('segment', 'dom'), pairs)  2.84 us
    ppermute x2, waiting for transfers between devices, change_lane(): return lax.ppermute(value, 'dom', pairs)  2.16 us
  transfers between devices with their start and end apart: 19, of which 7 were waited for; matrix products, arithmetic and copies ran while one was open for 2% of the time, Pallas kernels for 4%

profile of v21, /device:TPU:3, one launch (start us, length us, event | category | flops | bytes accessed | tf_op | source)
XLA Modules:
  0.0 51.0 jit_solution(3897234611678521787)
XLA Ops:
  0.0 0.0 copy-start.10
  0.0 0.0 copy-start.3
  0.0 0.7 %collective-permute-start.4 = (bf16[1,512,1024]{2,1,0:T(8,128)(2,1)}, bf16[1,512,1024]{2,1,0:T(8,128)(2,1)S(1)}, u32[]{:S(2)}, u32[]{:S(2)}) collective-permute-start(bf16[1,512,1024]{2,1,0:T(8,128)(2,1)} %w_project), channel_id=1, source_target_pairs={{0,1},{1,0},{2,3},{3,2},{4,5},{5,4},{6,7},{7,6},{8,9},{9,8},{10,11... | collective-permute-start | bytes 3145736 | tf_op jit(solution)/shard_map/ppermute | solution.py:616
  0.8 1.0 %copy.15 = bf16[4,128,227]{1,2,0:T(8,128)(2,1)S(1)} copy(bf16[4,128,227]{1,0,2:T(4,128)(2,1)} %param.12) | data formatting | bytes 464896 | tf_op args[0]
  1.8 0.7 %encode.1 = (bf16[80,512]{1,0:T(8,128)(2,1)S(1)}, bf16[80,512]{1,0:T(8,128)(2,1)S(1)}, bf16[80,512]{1,0:T(8,128)(2,1)S(1)}, bf16[80,512]{1,0:T(8,128)(2,1)S(1)}) custom-call(s32[1]{0:T(128)} %bitcast.segment, s32[1]{0:T(128)} %bitcast.1.place, bf16[4,227,128]{2,1,0:T(8,128)(2,1)S(1)} %bitcast.13, bf16[227,512]{1,0:T(8,128)(2,1)S(1)} %copy-done.3, ...), custom_call_target="tpu_custom_call" | custom-call | bytes 799752 | tf_op jit(solution)/shard_map/encode/pallas_call | solution.py:552
  2.5 2.3 %collective-permute-start = (bf16[80,512]{1,0:T(8,128)(2,1)S(1)}, bf16[80,512]{1,0:T(8,128)(2,1)S(1)}, u32[]{:S(2)}, u32[]{:S(2)}) collective-permute-start(bf16[80,512]{1,0:T(8,128)(2,1)S(1)} %get-tuple-element.66), channel_id=1, source_target_pairs={{0,8},{1,9},{2,10},{3,11},{4,12},{5,13},{6,14},{7,15},{8,4},{9,5},... | collective-permute-start | bytes 245768 | tf_op jit(solution)/shard_map/ppermute | solution.py:631
  4.9 0.4 collective-permute-start.1
  5.3 0.1 collective-permute-start.2
  5.4 1.2 %copy-done.1 = bf16[1,1024,512]{2,1,0:T(8,128)(2,1)S(1)} copy-done((bf16[1,1024,512]{2,1,0:T(8,128)(2,1)S(1)}, bf16[1,1024,512]{2,1,0:T(8,128)(2,1)}, u32[]{:S(2)}) %copy-start.1) | copy-done | bytes 1048600
  6.6 1.2 %copy-done.2 = bf16[1,512,1024]{2,1,0:T(8,128)(2,1)S(1)} copy-done((bf16[1,512,1024]{2,1,0:T(8,128)(2,1)S(1)}, bf16[1,512,1024]{2,1,0:T(8,128)(2,1)}, u32[]{:S(2)}) %copy-start.2) | copy-done | bytes 1048600
  7.8 0.7 %hold.1 = (bf16[512,512]{1,0:T(8,128)(2,1)S(1)}, bf16[512,512]{1,0:T(8,128)(2,1)S(1)}, bf16[512,512]{1,0:T(8,128)(2,1)S(1)}, bf16[512,512]{1,0:T(8,128)(2,1)S(1)}) custom-call(bf16[1,512,1024]{2,1,0:T(8,128)(2,1)S(1)} %copy-done.2, bf16[1,512,512]{2,1,0:T(8,128)(2,1)S(1)} %copy-done.4, bf16[1,1024,512]{2,1,0:T(8,128)(2,1)S(1)} %copy-done.1), custom_call_target="tpu_custom_call" | custom-call | bytes 4718592 | tf_op jit(solution)/shard_map/hold/pallas_call | solution.py:552
  8.6 0.0 collective-permute-done.refs_0_
  8.6 0.0 collective-permute-done.1.refs_1_
  8.6 0.0 collective-permute-done.2.refs_2_
  8.6 0.5 collective-permute-start.3
  9.1 1.3 %collective-permute-done.3.refs_1_ = bf16[320,512]{1,0:T(8,128)(2,1)S(1)} collective-permute-done((bf16[320,512]{1,0:T(8,128)(2,1)S(1)}, bf16[320,512]{1,0:T(8,128)(2,1)S(1)}, u32[]{:S(2)}, u32[]{:S(2)}) %collective-permute-start.3) | collective-permute-done | bytes 327712 | tf_op jit(solution)/shard_map/ppermute | solution.py:635
  10.4 0.0 collective-permute-done.4.refs_2_.refs_10_.refs_13_.refs_6_.refs_7_
  10.4 0.4 collective-permute-start.13
  10.8 3.5 %collective-permute-start.5 = (bf16[144,512]{1,0:T(8,128)(2,1)S(1)}, bf16[144,512]{1,0:T(8,128)(2,1)S(1)}, u32[]{:S(2)}, u32[]{:S(2)}) collective-permute-start(bf16[144,512]{1,0:T(8,128)(2,1)S(1)} %get-tuple-element.88), channel_id=1, source_target_pairs={{0,8},{1,0},{2,10},{3,2},{4,12},{5,4},{6,14},{7,6},{8,9},{9,1},{10... | collective-permute-start | bytes 442376 | tf_op jit(solution)/shard_map/ppermute | solution.py:616
  14.2 1.7 %collective-permute-start.6 = (bf16[128,512]{1,0:T(8,128)(2,1)S(1)}, bf16[128,512]{1,0:T(8,128)(2,1)S(1)}, u32[]{:S(2)}, u32[]{:S(2)}) collective-permute-start(bf16[128,512]{1,0:T(8,128)(2,1)S(1)} %next.5), channel_id=1, source_target_pairs={{0,8},{1,0},{2,10},{3,2},{4,12},{5,4},{6,14},{7,6},{8,9},{9,1},{10... | collective-permute-start | bytes 393224 | tf_op jit(solution)/shard_map/ppermute | solution.py:616
  15.9 1.5 %collective-permute-start.7 = (bf16[128,512]{1,0:T(8,128)(2,1)S(1)}, bf16[128,512]{1,0:T(8,128)(2,1)S(1)}, u32[]{:S(2)}, u32[]{:S(2)}) collective-permute-start(bf16[128,512]{1,0:T(8,128)(2,1)S(1)} %next.6), channel_id=1, source_target_pairs={{0,8},{1,0},{2,10},{3,2},{4,12},{5,4},{6,14},{7,6},{8,9},{9,1},{10... | collective-permute-start | bytes 393224 | tf_op jit(solution)/shard_map/ppermute | solution.py:616
  17.4 1.5 %collective-permute-start.9 = (bf16[128,512]{1,0:T(8,128)(2,1)S(1)}, bf16[128,512]{1,0:T(8,128)(2,1)S(1)}, u32[]{:S(2)}, u32[]{:S(2)}) collective-permute-start(bf16[128,512]{1,0:T(8,128)(2,1)S(1)} %next.7), channel_id=1, source_target_pairs={{0,8},{1,0},{2,10},{3,2},{4,12},{5,4},{6,14},{7,6},{8,9},{9,1},{10... | collective-permute-start | bytes 393224 | tf_op jit(solution)/shard_map/ppermute | solution.py:616
  18.9 0.4 prepare.1
  19.3 0.0 collective-permute-done.5.refs_0_.refs_5_.refs_1_
  19.3 0.0 collective-permute-done.6.refs_0_.refs_4_.refs_2_
  19.4 0.0 collective-permute-done.7.refs_0_.refs_3_
  19.4 4.4 %collective-permute-start.8 = (bf16[144,512]{1,0:T(8,128)(2,1)S(1)}, bf16[144,512]{1,0:T(8,128)(2,1)S(1)}, u32[]{:S(2)}, u32[]{:S(2)}) collective-permute-start(bf16[144,512]{1,0:T(8,128)(2,1)S(1)} %early.2), channel_id=1, source_target_pairs={{0,1},{1,0},{2,3},{3,2},{4,5},{5,4},{6,7},{7,6},{8,16},{9,8},{10,2... | collective-permute-start | bytes 442376 | tf_op jit(solution)/shard_map/ppermute | solution.py:616
  23.8 0.0 collective-permute-done.9.refs_4_
  23.8 1.6 %collective-permute-start.10 = (bf16[128,512]{1,0:T(8,128)(2,1)S(1)}, bf16[128,512]{1,0:T(8,128)(2,1)S(1)}, u32[]{:S(2)}, u32[]{:S(2)}) collective-permute-start(bf16[128,512]{1,0:T(8,128)(2,1)S(1)} %get-tuple-element.106), channel_id=1, source_target_pairs={{0,1},{1,0},{2,3},{3,2},{4,5},{5,4},{6,7},{7,6},{8,16},{9,8},{10,2... | collective-permute-start | bytes 393224 | tf_op jit(solution)/shard_map/ppermute | solution.py:616
  25.3 1.5 %collective-permute-start.11 = (bf16[128,512]{1,0:T(8,128)(2,1)S(1)}, bf16[128,512]{1,0:T(8,128)(2,1)S(1)}, u32[]{:S(2)}, u32[]{:S(2)}) collective-permute-start(bf16[128,512]{1,0:T(8,128)(2,1)S(1)} %next.8), channel_id=1, source_target_pairs={{0,1},{1,0},{2,3},{3,2},{4,5},{5,4},{6,7},{7,6},{8,16},{9,8},{10,2... | collective-permute-start | bytes 393224 | tf_op jit(solution)/shard_map/ppermute | solution.py:616
  26.8 1.6 %collective-permute-start.12 = (bf16[128,512]{1,0:T(8,128)(2,1)S(1)}, bf16[128,512]{1,0:T(8,128)(2,1)S(1)}, u32[]{:S(2)}, u32[]{:S(2)}) collective-permute-start(bf16[128,512]{1,0:T(8,128)(2,1)S(1)} %next.9), channel_id=1, source_target_pairs={{0,1},{1,0},{2,3},{3,2},{4,5},{5,4},{6,7},{7,6},{8,16},{9,8},{10,2... | collective-permute-start | bytes 393224 | tf_op jit(solution)/shard_map/ppermute | solution.py:616
  28.5 1.7 %collective-permute-done.8.refs_0_.refs_5_.refs_1_ = bf16[144,512]{1,0:T(8,128)(2,1)S(1)} collective-permute-done((bf16[144,512]{1,0:T(8,128)(2,1)S(1)}, bf16[144,512]{1,0:T(8,128)(2,1)S(1)}, u32[]{:S(2)}, u32[]{:S(2)}) %collective-permute-start.8) | collective-permute-done | bytes 147488 | tf_op jit(solution)/shard_map/ppermute | solution.py:616
  30.1 1.4 %collective-permute-done.10.refs_0_.refs_4_.refs_2_ = bf16[128,512]{1,0:T(8,128)(2,1)S(1)} collective-permute-done((bf16[128,512]{1,0:T(8,128)(2,1)S(1)}, bf16[128,512]{1,0:T(8,128)(2,1)S(1)}, u32[]{:S(2)}, u32[]{:S(2)}) %collective-permute-start.10) | collective-permute-done | bytes 131104 | tf_op jit(solution)/shard_map/ppermute | solution.py:616
  31.5 1.4 %collective-permute-done.11.refs_0_.refs_3_ = bf16[128,512]{1,0:T(8,128)(2,1)S(1)} collective-permute-done((bf16[128,512]{1,0:T(8,128)(2,1)S(1)}, bf16[128,512]{1,0:T(8,128)(2,1)S(1)}, u32[]{:S(2)}, u32[]{:S(2)}) %collective-permute-start.11) | collective-permute-done | bytes 131104 | tf_op jit(solution)/shard_map/ppermute | solution.py:616
  33.0 0.0 collective-permute-done.13.refs_11_.refs_14_.refs_7_.refs_8_
  33.0 1.4 %collective-permute-done.12.refs_4_ = bf16[128,512]{1,0:T(8,128)(2,1)S(1)} collective-permute-done((bf16[128,512]{1,0:T(8,128)(2,1)S(1)}, bf16[128,512]{1,0:T(8,128)(2,1)S(1)}, u32[]{:S(2)}, u32[]{:S(2)}) %collective-permute-start.12) | collective-permute-done | bytes 131104 | tf_op jit(solution)/shard_map/ppermute | solution.py:616
  34.4 0.0 collective-permute-start.14
  34.4 0.5 collective-permute-start.15
  34.9 6.7 %collective-permute-start.16 = (bf16[128,512]{1,0:T(8,128)(2,1)S(1)}, bf16[128,512]{1,0:T(8,128)(2,1)S(1)}, u32[]{:S(2)}, u32[]{:S(2)}) collective-permute-start(bf16[128,512]{1,0:T(8,128)(2,1)S(1)} %get-tuple-element.119.refs_3_), channel_id=1, source_target_pairs={{0,1},{1,17},{2,3},{3,2},{4,5},{5,4},{6,7},{7,6},{8,9},{9,27},{10,... | collective-permute-start | bytes 393224 | tf_op jit(solution)/shard_map/ppermute | solution.py:616
  41.5 0.0 collective-permute-start.17
  41.6 0.0 collective-permute-done.15.refs_0_
  41.6 0.0 collective-permute-done.14.refs_0_
  41.6 0.0 copy-start.5
  41.6 2.2 %collective-permute-done.16.refs_1_ = bf16[128,512]{1,0:T(8,128)(2,1)S(1)} collective-permute-done((bf16[128,512]{1,0:T(8,128)(2,1)S(1)}, bf16[128,512]{1,0:T(8,128)(2,1)S(1)}, u32[]{:S(2)}, u32[]{:S(2)}) %collective-permute-start.16) | collective-permute-done | bytes 131104 | tf_op jit(solution)/shard_map/ppermute | solution.py:616
  43.9 0.0 collective-permute-done.17.refs_2_
  43.9 5.0 %collective-permute-start.18 = (bf16[64,512]{1,0:T(8,128)(2,1)S(1)}, bf16[64,512]{1,0:T(8,128)(2,1)S(1)}, u32[]{:S(2)}, u32[]{:S(2)}) collective-permute-start(bf16[64,512]{1,0:T(8,128)(2,1)S(1)} %get-tuple-element.122), channel_id=1, source_target_pairs={{0,1},{1,0},{2,3},{3,2},{4,5},{5,4},{6,7},{7,6},{8,9},{9,8},{10,11... | collective-permute-start | bytes 196616 | tf_op jit(solution)/shard_map/ppermute | solution.py:635
  48.9 0.9 %collective-permute-done.18.refs_5_ = bf16[64,512]{1,0:T(8,128)(2,1)S(1)} collective-permute-done((bf16[64,512]{1,0:T(8,128)(2,1)S(1)}, bf16[64,512]{1,0:T(8,128)(2,1)S(1)}, u32[]{:S(2)}, u32[]{:S(2)}) %collective-permute-start.18) | collective-permute-done | bytes 65568 | tf_op jit(solution)/shard_map/ppermute | solution.py:635
  49.8 1.2 %decode.1 = bf16[227,128]{1,0:T(8,128)(2,1)} custom-call(s32[1]{0:T(128)} %bitcast.segment, s32[1]{0:T(128)} %bitcast.1.place, f32[128,512]{1,0:T(8,128)S(1)} %get-tuple-element.91.refs_0_, bf16[64,128]{1,0:T(8,128)(2,1)S(1)} %get-tuple-element.92.refs_1_, bf16[1024,512]{1,0:T(8,128)(2,1)S(1)} %copy-done, bf16[227,512]{1,0:T(8,128)(2,1)S(1)} %bitcast.15, ...), custom_call_target="tpu_custom_call" | custom-call | bytes 1748744 | tf_op jit(solution)/shard_map/decode/pallas_call | solution.py:552
  (42 shorter events, 0.2 us)
Async XLA Ops:
  0.0 1.7 %copy-start.7 = (s32[64,8]{0,1:T(8,128)S(1)}, s32[64,8]{0,1:T(8,128)}, u32[]{:S(2)}) copy-start(s32[64,8]{0,1:T(8,128)} %param.21) | copy-start | bytes 6148
  0.0 1.8 %copy-start.8 = (s32[4,64]{1,0:T(4,128)S(1)}, s32[4,64]{1,0:T(4,128)}, u32[]{:S(2)}) copy-start(s32[4,64]{1,0:T(4,128)} %param.22) | copy-start | bytes 3076
  0.0 1.8 %copy-start.9 = (s32[4,1]{0,1:T(1,128)S(1)}, s32[4,1]{0,1:T(1,128)}, u32[]{:S(2)}) copy-start(s32[4,1]{0,1:T(1,128)} %param.23) | copy-start | bytes 52
  0.0 1.8 %copy-start.10 = (s32[128]{0:T(128)S(1)}, s32[128]{0:T(128)}, u32[]{:S(2)}) copy-start(s32[128]{0:T(128)} %param.19) | copy-start | bytes 1540
  0.0 1.8 %copy-start.3 = (bf16[227,512]{1,0:T(8,128)(2,1)S(1)}, bf16[227,512]{1,0:T(8,128)(2,1)}, u32[]{:S(2)}) copy-start(bf16[227,512]{1,0:T(8,128)(2,1)} %refs_1_.3) | copy-start | bytes 697348
  0.0 5.3 %copy-start.4 = (bf16[1,512,512]{2,1,0:T(8,128)(2,1)S(1)}, bf16[1,512,512]{2,1,0:T(8,128)(2,1)}, u32[]{:S(2)}) copy-start(bf16[1,512,512]{2,1,0:T(8,128)(2,1)} %w_message.1) | copy-start | bytes 1572868
  0.0 10.4 %collective-permute-start.4 = (bf16[1,512,1024]{2,1,0:T(8,128)(2,1)}, bf16[1,512,1024]{2,1,0:T(8,128)(2,1)S(1)}, u32[]{:S(2)}, u32[]{:S(2)}) collective-permute-start(bf16[1,512,1024]{2,1,0:T(8,128)(2,1)} %w_project), channel_id=1, source_target_pairs={{0,1},{1,0},{2,3},{3,2},{4,5},{5,4},{6,7},{7,6},{8,9},{9,8},{10,11... | collective-permute-start | bytes 3145736 | tf_op jit(solution)/shard_map/ppermute | solution.py:616
  2.5 6.0 %collective-permute-start = (bf16[80,512]{1,0:T(8,128)(2,1)S(1)}, bf16[80,512]{1,0:T(8,128)(2,1)S(1)}, u32[]{:S(2)}, u32[]{:S(2)}) collective-permute-start(bf16[80,512]{1,0:T(8,128)(2,1)S(1)} %get-tuple-element.66), channel_id=1, source_target_pairs={{0,8},{1,9},{2,10},{3,11},{4,12},{5,13},{6,14},{7,15},{8,4},{9,5},... | collective-permute-start | bytes 245768 | tf_op jit(solution)/shard_map/ppermute | solution.py:631
  4.9 3.7 %collective-permute-start.1 = (bf16[80,512]{1,0:T(8,128)(2,1)S(1)}, bf16[80,512]{1,0:T(8,128)(2,1)S(1)}, u32[]{:S(2)}, u32[]{:S(2)}) collective-permute-start(bf16[80,512]{1,0:T(8,128)(2,1)S(1)} %get-tuple-element.67), channel_id=1, source_target_pairs={{0,16},{1,17},{2,18},{3,19},{4,20},{5,21},{6,22},{7,23},{8,9},{9,8... | collective-permute-start | bytes 245768 | tf_op jit(solution)/shard_map/ppermute | solution.py:631
  5.3 3.3 %collective-permute-start.2 = (bf16[80,512]{1,0:T(8,128)(2,1)S(1)}, bf16[80,512]{1,0:T(8,128)(2,1)S(1)}, u32[]{:S(2)}, u32[]{:S(2)}) collective-permute-start(bf16[80,512]{1,0:T(8,128)(2,1)S(1)} %get-tuple-element.68), channel_id=1, source_target_pairs={{0,2},{1,3},{2,0},{3,1},{4,6},{5,7},{6,4},{7,5},{8,9},{9,8},{10,11... | collective-permute-start | bytes 245768 | tf_op jit(solution)/shard_map/ppermute | solution.py:631
  5.4 1.2 %copy-start.1 = (bf16[1,1024,512]{2,1,0:T(8,128)(2,1)S(1)}, bf16[1,1024,512]{2,1,0:T(8,128)(2,1)}, u32[]{:S(2)}) copy-start(bf16[1,1024,512]{2,1,0:T(8,128)(2,1)} %w_update.1) | copy-start | bytes 3145732
  6.6 1.2 %copy-start.2 = (bf16[1,512,1024]{2,1,0:T(8,128)(2,1)S(1)}, bf16[1,512,1024]{2,1,0:T(8,128)(2,1)}, u32[]{:S(2)}) copy-start(bf16[1,512,1024]{2,1,0:T(8,128)(2,1)} %w_project) | copy-start | bytes 3145732
  8.6 1.8 %collective-permute-start.3 = (bf16[320,512]{1,0:T(8,128)(2,1)S(1)}, bf16[320,512]{1,0:T(8,128)(2,1)S(1)}, u32[]{:S(2)}, u32[]{:S(2)}) collective-permute-start(bf16[320,512]{1,0:T(8,128)(2,1)S(1)} %join.1.refs_0_), channel_id=1, source_target_pairs={{0,1},{1,0},{2,3},{3,2},{4,5},{5,4},{6,7},{7,6},{8,9},{9,8},{10,11... | collective-permute-start | bytes 983048 | tf_op jit(solution)/shard_map/ppermute | solution.py:635
  10.4 22.6 %collective-permute-start.13 = (bf16[2,512,512]{2,1,0:T(8,128)(2,1)S(1)}, bf16[2,512,512]{2,1,0:T(8,128)(2,1)S(1)}, u32[]{:S(2)}, u32[]{:S(2)}) collective-permute-start(bf16[2,512,512]{2,1,0:T(8,128)(2,1)S(1)} %pack.1), channel_id=1, source_target_pairs={{0,1},{1,0},{2,3},{3,2},{4,5},{5,4},{6,7},{7,6},{8,9},{9,8},{10,11... | collective-permute-start | bytes 3145736 | tf_op jit(solution)/shard_map/ppermute | solution.py:616
  10.8 8.5 %collective-permute-start.5 = (bf16[144,512]{1,0:T(8,128)(2,1)S(1)}, bf16[144,512]{1,0:T(8,128)(2,1)S(1)}, u32[]{:S(2)}, u32[]{:S(2)}) collective-permute-start(bf16[144,512]{1,0:T(8,128)(2,1)S(1)} %get-tuple-element.88), channel_id=1, source_target_pairs={{0,8},{1,0},{2,10},{3,2},{4,12},{5,4},{6,14},{7,6},{8,9},{9,1},{10... | collective-permute-start | bytes 442376 | tf_op jit(solution)/shard_map/ppermute | solution.py:616
  14.2 5.1 %collective-permute-start.6 = (bf16[128,512]{1,0:T(8,128)(2,1)S(1)}, bf16[128,512]{1,0:T(8,128)(2,1)S(1)}, u32[]{:S(2)}, u32[]{:S(2)}) collective-permute-start(bf16[128,512]{1,0:T(8,128)(2,1)S(1)} %next.5), channel_id=1, source_target_pairs={{0,8},{1,0},{2,10},{3,2},{4,12},{5,4},{6,14},{7,6},{8,9},{9,1},{10... | collective-permute-start | bytes 393224 | tf_op jit(solution)/shard_map/ppermute | solution.py:616
  15.9 3.0 %copy-start = (bf16[1024,512]{1,0:T(8,128)(2,1)S(1)}, bf16[1024,512]{1,0:T(8,128)(2,1)}, u32[]{:S(2)}) copy-start(bf16[1024,512]{1,0:T(8,128)(2,1)} %refs_2_.3) | copy-start | bytes 3145732
  15.9 3.5 %collective-permute-start.7 = (bf16[128,512]{1,0:T(8,128)(2,1)S(1)}, bf16[128,512]{1,0:T(8,128)(2,1)S(1)}, u32[]{:S(2)}, u32[]{:S(2)}) collective-permute-start(bf16[128,512]{1,0:T(8,128)(2,1)S(1)} %next.6), channel_id=1, source_target_pairs={{0,8},{1,0},{2,10},{3,2},{4,12},{5,4},{6,14},{7,6},{8,9},{9,1},{10... | collective-permute-start | bytes 393224 | tf_op jit(solution)/shard_map/ppermute | solution.py:616
  17.4 1.5 %copy-start.6 = (s32[128]{0:T(128)S(1)}, s32[128]{0:T(128)}, u32[]{:S(2)}) copy-start(s32[128]{0:T(128)} %param.20) | copy-start | bytes 1540
  17.4 6.4 %collective-permute-start.9 = (bf16[128,512]{1,0:T(8,128)(2,1)S(1)}, bf16[128,512]{1,0:T(8,128)(2,1)S(1)}, u32[]{:S(2)}, u32[]{:S(2)}) collective-permute-start(bf16[128,512]{1,0:T(8,128)(2,1)S(1)} %next.7), channel_id=1, source_target_pairs={{0,8},{1,0},{2,10},{3,2},{4,12},{5,4},{6,14},{7,6},{8,9},{9,1},{10... | collective-permute-start | bytes 393224 | tf_op jit(solution)/shard_map/ppermute | solution.py:616
  19.4 10.7 %collective-permute-start.8 = (bf16[144,512]{1,0:T(8,128)(2,1)S(1)}, bf16[144,512]{1,0:T(8,128)(2,1)S(1)}, u32[]{:S(2)}, u32[]{:S(2)}) collective-permute-start(bf16[144,512]{1,0:T(8,128)(2,1)S(1)} %early.2), channel_id=1, source_target_pairs={{0,1},{1,0},{2,3},{3,2},{4,5},{5,4},{6,7},{7,6},{8,16},{9,8},{10,2... | collective-permute-start | bytes 442376 | tf_op jit(solution)/shard_map/ppermute | solution.py:616
  23.8 7.8 %collective-permute-start.10 = (bf16[128,512]{1,0:T(8,128)(2,1)S(1)}, bf16[128,512]{1,0:T(8,128)(2,1)S(1)}, u32[]{:S(2)}, u32[]{:S(2)}) collective-permute-start(bf16[128,512]{1,0:T(8,128)(2,1)S(1)} %get-tuple-element.106), channel_id=1, source_target_pairs={{0,1},{1,0},{2,3},{3,2},{4,5},{5,4},{6,7},{7,6},{8,16},{9,8},{10,2... | collective-permute-start | bytes 393224 | tf_op jit(solution)/shard_map/ppermute | solution.py:616
  25.3 7.6 %collective-permute-start.11 = (bf16[128,512]{1,0:T(8,128)(2,1)S(1)}, bf16[128,512]{1,0:T(8,128)(2,1)S(1)}, u32[]{:S(2)}, u32[]{:S(2)}) collective-permute-start(bf16[128,512]{1,0:T(8,128)(2,1)S(1)} %next.8), channel_id=1, source_target_pairs={{0,1},{1,0},{2,3},{3,2},{4,5},{5,4},{6,7},{7,6},{8,16},{9,8},{10,2... | collective-permute-start | bytes 393224 | tf_op jit(solution)/shard_map/ppermute | solution.py:616
  26.8 7.5 %collective-permute-start.12 = (bf16[128,512]{1,0:T(8,128)(2,1)S(1)}, bf16[128,512]{1,0:T(8,128)(2,1)S(1)}, u32[]{:S(2)}, u32[]{:S(2)}) collective-permute-start(bf16[128,512]{1,0:T(8,128)(2,1)S(1)} %next.9), channel_id=1, source_target_pairs={{0,1},{1,0},{2,3},{3,2},{4,5},{5,4},{6,7},{7,6},{8,16},{9,8},{10,2... | collective-permute-start | bytes 393224 | tf_op jit(solution)/shard_map/ppermute | solution.py:616
  34.4 7.2 %collective-permute-start.14 = (bf16[128,512]{1,0:T(8,128)(2,1)S(1)}, bf16[128,512]{1,0:T(8,128)(2,1)S(1)}, u32[]{:S(2)}, u32[]{:S(2)}) collective-permute-start(bf16[128,512]{1,0:T(8,128)(2,1)S(1)} %get-tuple-element.116), channel_id=1, source_target_pairs={{0,1},{1,0},{2,3},{3,2},{4,5},{5,4},{6,7},{7,17},{8,9},{9,8},{10,1... | collective-permute-start | bytes 393224 | tf_op jit(solution)/shard_map/ppermute | solution.py:616
  34.4 7.2 %collective-permute-start.15 = (bf16[128,512]{1,0:T(8,128)(2,1)S(1)}, bf16[128,512]{1,0:T(8,128)(2,1)S(1)}, u32[]{:S(2)}, u32[]{:S(2)}) collective-permute-start(bf16[128,512]{1,0:T(8,128)(2,1)S(1)} %get-tuple-element.117), channel_id=1, source_target_pairs={{0,1},{1,0},{2,3},{3,2},{4,5},{5,21},{6,7},{7,6},{8,9},{9,8},{10,1... | collective-permute-start | bytes 393224 | tf_op jit(solution)/shard_map/ppermute | solution.py:616
  34.9 9.0 %collective-permute-start.16 = (bf16[128,512]{1,0:T(8,128)(2,1)S(1)}, bf16[128,512]{1,0:T(8,128)(2,1)S(1)}, u32[]{:S(2)}, u32[]{:S(2)}) collective-permute-start(bf16[128,512]{1,0:T(8,128)(2,1)S(1)} %get-tuple-element.119.refs_3_), channel_id=1, source_target_pairs={{0,1},{1,17},{2,3},{3,2},{4,5},{5,4},{6,7},{7,6},{8,9},{9,27},{10,... | collective-permute-start | bytes 393224 | tf_op jit(solution)/shard_map/ppermute | solution.py:616
  41.5 2.3 %collective-permute-start.17 = (bf16[128,512]{1,0:T(8,128)(2,1)S(1)}, bf16[128,512]{1,0:T(8,128)(2,1)S(1)}, u32[]{:S(2)}, u32[]{:S(2)}) collective-permute-start(bf16[128,512]{1,0:T(8,128)(2,1)S(1)} %get-tuple-element.120.refs_4_), channel_id=1, source_target_pairs={{0,1},{1,0},{2,3},{3,17},{4,5},{5,4},{6,7},{7,6},{8,9},{9,8},{10,1... | collective-permute-start | bytes 393224 | tf_op jit(solution)/shard_map/ppermute | solution.py:616
  41.6 8.2 %copy-start.5 = (bf16[512,227]{0,1:T(8,128)(2,1)S(1)}, bf16[512,227]{0,1:T(8,128)(2,1)}, u32[]{:S(2)}) copy-start(bf16[512,227]{0,1:T(8,128)(2,1)} %param.18) | copy-start | bytes 697348
  43.9 5.9 %collective-permute-start.18 = (bf16[64,512]{1,0:T(8,128)(2,1)S(1)}, bf16[64,512]{1,0:T(8,128)(2,1)S(1)}, u32[]{:S(2)}, u32[]{:S(2)}) collective-permute-start(bf16[64,512]{1,0:T(8,128)(2,1)S(1)} %get-tuple-element.122), channel_id=1, source_target_pairs={{0,1},{1,0},{2,3},{3,2},{4,5},{5,4},{6,7},{7,6},{8,9},{9,8},{10,11... | collective-permute-start | bytes 196616 | tf_op jit(solution)/shard_map/ppermute | solution.py:635

commit v22 on v20

--- a/solution.py
+++ b/solution.py
@@ -456,8 +456,11 @@
                 pieces = outs[1:]
             sender = outs[0] if first else senders[0]
             rows = sum(piece.shape[0] for piece in pieces)
-            upper = (chip < chips // 2) if far else (chip >= chips // 2)
-            start = pl.multiple_of(jnp.where(upper, half, 0) + begin, rows)
+            if far:
+                start = jnp.where(chip < chips // 2, 2 * half - rows - begin, begin)
+            else:
+                start = jnp.where(chip >= chips // 2, half, 0) + begin
+            start = pl.multiple_of(start, rows)
             own = state[pl.ds(start, rows), :]
             gathered = sum_edges(fanout, columns[pl.ds(start, rows), :], sender[...], own, w_receive)
             write_pieces(pieces, update_nodes(own, gathered, w_own, w_edges))
@@ -480,6 +483,8 @@
 def far_kernel(group, chips, last, number, where, *refs):
     block, out = refs[0], refs[-1]
     crosses, _, spot = arrival(where, group, chips, last)
+    chip, _ = place_of(where, group)
+    spot = jnp.where(chip < chips // 2, chip, chips - 1 - chip)
 
     @pl.when(jnp.logical_and(crosses, spot == number))
     def _():
@@ -810,9 +815,11 @@
     arrived = []
     for far, blocks in ((1, state[:each]), (0, state[each:])):
         for turn, block in enumerate(blocks):
-            pairs = [
-                (owner(m, segments), device(m, ((m // each ^ far) * each + turn) * group)) for m in range(samples)
-            ]
+            if far:
+                chips = [samples - 1 - turn if m < each else turn for m in range(samples)]
+            else:
+                chips = [m // each * each + turn for m in range(samples)]
+            pairs = [(owner(m, segments), device(m, chips[m] * group)) for m in range(samples)]
             arrived.append(send(block, [pair for pair in pairs if pair[0] != pair[1]]))
     crossed = []
     for number, block in enumerate(arrived[:each]):

time: 50.6 us -> 50.6 us (level)
  no operation moved by 1% of the time
where the time goes in v22:
time: 50.6 us; the launch traced here: 50 us
  starting transfers between devices  33.1 us (65%)
  waiting for transfers between devices  9.97 us (20%)
  local copies, waits for them, and re-layouts  3.46 us (7%)
  Pallas kernels  3.21 us (6%)
    ppermute x14, starting transfers between devices, send(): lax.ppermute(value, ('segment', 'dom'), every_device(pairs, segments * pa...  25.7 us
    ppermute x14, waiting for transfers between devices, send(): lax.ppermute(value, ('segment', 'dom'), every_device(pairs, segments * pa...  7.81 us
    ppermute x2, starting transfers between devices, change_lane(): return lax.ppermute(value, 'dom', pairs)  4.46 us
    unnamed x23, local copies, waits for them, and re-layouts  3.46 us
    pallas_call x30, Pallas kernels, call(): pl.pallas_call(located if places[0] == 'w' else kernel, out_shape=shapes,...  3.21 us
    ppermute x3, starting transfers between devices, to_chip(): return lax.ppermute(value, ('segment', 'dom'), pairs)  2.84 us
    ppermute x2, waiting for transfers between devices, change_lane(): return lax.ppermute(value, 'dom', pairs)  2.16 us
  transfers between devices with their start and end apart: 19, of which 7 were waited for; matrix products, arithmetic and copies ran while one was open for 2% of the time, Pallas kernels for 4%

profile of v22, /device:TPU:3, one launch (start us, length us, event | category | flops | bytes accessed | tf_op | source)
XLA Modules:
  0.0 50.0 jit_solution(14556433550799384235)
XLA Ops:
  0.0 0.7 %collective-permute-start.4 = (bf16[1,512,1024]{2,1,0:T(8,128)(2,1)}, bf16[1,512,1024]{2,1,0:T(8,128)(2,1)S(1)}, u32[]{:S(2)}, u32[]{:S(2)}) collective-permute-start(bf16[1,512,1024]{2,1,0:T(8,128)(2,1)} %w_project), channel_id=1, source_target_pairs={{0,1},{1,0},{2,3},{3,2},{4,5},{5,4},{6,7},{7,6},{8,9},{9,8},{10,11... | collective-permute-start | bytes 3145736 | tf_op jit(solution)/shard_map/ppermute | solution.py:621
  0.8 1.0 %copy.15 = bf16[4,128,227]{1,2,0:T(8,128)(2,1)S(1)} copy(bf16[4,128,227]{1,0,2:T(4,128)(2,1)} %param.12) | data formatting | bytes 464896 | tf_op args[0]
  1.8 0.7 %encode.1 = (bf16[80,512]{1,0:T(8,128)(2,1)S(1)}, bf16[80,512]{1,0:T(8,128)(2,1)S(1)}, bf16[80,512]{1,0:T(8,128)(2,1)S(1)}, bf16[80,512]{1,0:T(8,128)(2,1)S(1)}) custom-call(s32[1]{0:T(128)} %bitcast.segment, s32[1]{0:T(128)} %bitcast.1.place, bf16[4,227,128]{2,1,0:T(8,128)(2,1)S(1)} %bitcast.13, bf16[227,512]{1,0:T(8,128)(2,1)S(1)} %copy-done.3, ...), custom_call_target="tpu_custom_call" | custom-call | bytes 799752 | tf_op jit(solution)/shard_map/encode/pallas_call | solution.py:557
  2.5 2.3 %collective-permute-start = (bf16[80,512]{1,0:T(8,128)(2,1)S(1)}, bf16[80,512]{1,0:T(8,128)(2,1)S(1)}, u32[]{:S(2)}, u32[]{:S(2)}) collective-permute-start(bf16[80,512]{1,0:T(8,128)(2,1)S(1)} %get-tuple-element.63), channel_id=1, source_target_pairs={{0,8},{1,9},{2,10},{3,11},{4,12},{5,13},{6,14},{7,15},{8,4},{9,5},... | collective-permute-start | bytes 245768 | tf_op jit(solution)/shard_map/ppermute | solution.py:636
  4.9 0.4 collective-permute-start.1
  5.3 0.1 collective-permute-start.2
  5.4 0.0 copy-done.4
  5.4 1.2 %copy-done.1 = bf16[1,1024,512]{2,1,0:T(8,128)(2,1)S(1)} copy-done((bf16[1,1024,512]{2,1,0:T(8,128)(2,1)S(1)}, bf16[1,1024,512]{2,1,0:T(8,128)(2,1)}, u32[]{:S(2)}) %copy-start.1) | copy-done | bytes 1048600
  6.6 1.2 %copy-done.2 = bf16[1,512,1024]{2,1,0:T(8,128)(2,1)S(1)} copy-done((bf16[1,512,1024]{2,1,0:T(8,128)(2,1)S(1)}, bf16[1,512,1024]{2,1,0:T(8,128)(2,1)}, u32[]{:S(2)}) %copy-start.2) | copy-done | bytes 1048600
  7.8 0.7 %hold.1 = (bf16[512,512]{1,0:T(8,128)(2,1)S(1)}, bf16[512,512]{1,0:T(8,128)(2,1)S(1)}, bf16[512,512]{1,0:T(8,128)(2,1)S(1)}, bf16[512,512]{1,0:T(8,128)(2,1)S(1)}) custom-call(bf16[1,512,1024]{2,1,0:T(8,128)(2,1)S(1)} %copy-done.2, bf16[1,512,512]{2,1,0:T(8,128)(2,1)S(1)} %copy-done.4, bf16[1,1024,512]{2,1,0:T(8,128)(2,1)S(1)} %copy-done.1), custom_call_target="tpu_custom_call" | custom-call | bytes 4718592 | tf_op jit(solution)/shard_map/hold/pallas_call | solution.py:557
  8.6 0.0 collective-permute-done.refs_0_
  8.6 0.0 collective-permute-done.1.refs_1_
  8.6 0.0 collective-permute-done.2.refs_2_
  8.6 0.5 %collective-permute-start.3 = (bf16[320,512]{1,0:T(8,128)(2,1)S(1)}, bf16[320,512]{1,0:T(8,128)(2,1)S(1)}, u32[]{:S(2)}, u32[]{:S(2)}) collective-permute-start(bf16[320,512]{1,0:T(8,128)(2,1)S(1)} %join.1.refs_0_), channel_id=1, source_target_pairs={{0,1},{1,0},{2,3},{3,2},{4,5},{5,4},{6,7},{7,6},{8,9},{9,8},{10,11... | collective-permute-start | bytes 983048 | tf_op jit(solution)/shard_map/ppermute | solution.py:640
  9.1 1.3 %collective-permute-done.3.refs_1_ = bf16[320,512]{1,0:T(8,128)(2,1)S(1)} collective-permute-done((bf16[320,512]{1,0:T(8,128)(2,1)S(1)}, bf16[320,512]{1,0:T(8,128)(2,1)S(1)}, u32[]{:S(2)}, u32[]{:S(2)}) %collective-permute-start.3) | collective-permute-done | bytes 327712 | tf_op jit(solution)/shard_map/ppermute | solution.py:640
  10.4 0.0 collective-permute-done.4.refs_2_.refs_10_.refs_13_.refs_6_.refs_7_
  10.4 0.4 collective-permute-start.13
  10.8 3.5 %collective-permute-start.5 = (bf16[144,512]{1,0:T(8,128)(2,1)S(1)}, bf16[144,512]{1,0:T(8,128)(2,1)S(1)}, u32[]{:S(2)}, u32[]{:S(2)}) collective-permute-start(bf16[144,512]{1,0:T(8,128)(2,1)S(1)} %get-tuple-element.85), channel_id=1, source_target_pairs={{0,8},{1,0},{2,10},{3,2},{4,12},{5,4},{6,14},{7,6},{8,9},{9,1},{10... | collective-permute-start | bytes 442376 | tf_op jit(solution)/shard_map/ppermute | solution.py:621
  14.2 1.7 %collective-permute-start.6 = (bf16[128,512]{1,0:T(8,128)(2,1)S(1)}, bf16[128,512]{1,0:T(8,128)(2,1)S(1)}, u32[]{:S(2)}, u32[]{:S(2)}) collective-permute-start(bf16[128,512]{1,0:T(8,128)(2,1)S(1)} %next.5), channel_id=1, source_target_pairs={{0,8},{1,0},{2,10},{3,2},{4,12},{5,4},{6,14},{7,6},{8,9},{9,1},{10... | collective-permute-start | bytes 393224 | tf_op jit(solution)/shard_map/ppermute | solution.py:621
  15.9 1.5 %collective-permute-start.7 = (bf16[128,512]{1,0:T(8,128)(2,1)S(1)}, bf16[128,512]{1,0:T(8,128)(2,1)S(1)}, u32[]{:S(2)}, u32[]{:S(2)}) collective-permute-start(bf16[128,512]{1,0:T(8,128)(2,1)S(1)} %next.6), channel_id=1, source_target_pairs={{0,8},{1,0},{2,10},{3,2},{4,12},{5,4},{6,14},{7,6},{8,9},{9,1},{10... | collective-permute-start | bytes 393224 | tf_op jit(solution)/shard_map/ppermute | solution.py:621
  17.4 1.5 %collective-permute-start.9 = (bf16[128,512]{1,0:T(8,128)(2,1)S(1)}, bf16[128,512]{1,0:T(8,128)(2,1)S(1)}, u32[]{:S(2)}, u32[]{:S(2)}) collective-permute-start(bf16[128,512]{1,0:T(8,128)(2,1)S(1)} %next.7), channel_id=1, source_target_pairs={{0,8},{1,0},{2,10},{3,2},{4,12},{5,4},{6,14},{7,6},{8,9},{9,1},{10... | collective-permute-start | bytes 393224 | tf_op jit(solution)/shard_map/ppermute | solution.py:621
  18.9 0.0 copy-done.6
  18.9 0.4 prepare.1
  19.3 0.0 collective-permute-done.5.refs_0_.refs_5_.refs_1_
  19.3 0.0 collective-permute-done.6.refs_0_.refs_4_.refs_2_
  19.4 0.0 collective-permute-done.7.refs_0_.refs_3_
  19.4 4.4 %collective-permute-start.8 = (bf16[144,512]{1,0:T(8,128)(2,1)S(1)}, bf16[144,512]{1,0:T(8,128)(2,1)S(1)}, u32[]{:S(2)}, u32[]{:S(2)}) collective-permute-start(bf16[144,512]{1,0:T(8,128)(2,1)S(1)} %early.2), channel_id=1, source_target_pairs={{0,1},{1,0},{2,3},{3,2},{4,5},{5,4},{6,7},{7,6},{8,16},{9,8},{10,2... | collective-permute-start | bytes 442376 | tf_op jit(solution)/shard_map/ppermute | solution.py:621
  23.8 0.0 collective-permute-done.9.refs_4_
  23.8 1.6 %collective-permute-start.10 = (bf16[128,512]{1,0:T(8,128)(2,1)S(1)}, bf16[128,512]{1,0:T(8,128)(2,1)S(1)}, u32[]{:S(2)}, u32[]{:S(2)}) collective-permute-start(bf16[128,512]{1,0:T(8,128)(2,1)S(1)} %get-tuple-element.103), channel_id=1, source_target_pairs={{0,1},{1,0},{2,3},{3,2},{4,5},{5,4},{6,7},{7,6},{8,16},{9,8},{10,2... | collective-permute-start | bytes 393224 | tf_op jit(solution)/shard_map/ppermute | solution.py:621
  25.3 1.5 %collective-permute-start.11 = (bf16[128,512]{1,0:T(8,128)(2,1)S(1)}, bf16[128,512]{1,0:T(8,128)(2,1)S(1)}, u32[]{:S(2)}, u32[]{:S(2)}) collective-permute-start(bf16[128,512]{1,0:T(8,128)(2,1)S(1)} %next.8), channel_id=1, source_target_pairs={{0,1},{1,0},{2,3},{3,2},{4,5},{5,4},{6,7},{7,6},{8,16},{9,8},{10,2... | collective-permute-start | bytes 393224 | tf_op jit(solution)/shard_map/ppermute | solution.py:621
  26.8 1.6 %collective-permute-start.12 = (bf16[128,512]{1,0:T(8,128)(2,1)S(1)}, bf16[128,512]{1,0:T(8,128)(2,1)S(1)}, u32[]{:S(2)}, u32[]{:S(2)}) collective-permute-start(bf16[128,512]{1,0:T(8,128)(2,1)S(1)} %next.9), channel_id=1, source_target_pairs={{0,1},{1,0},{2,3},{3,2},{4,5},{5,4},{6,7},{7,6},{8,16},{9,8},{10,2... | collective-permute-start | bytes 393224 | tf_op jit(solution)/shard_map/ppermute | solution.py:621
  28.5 1.7 %collective-permute-done.8.refs_0_.refs_5_.refs_1_ = bf16[144,512]{1,0:T(8,128)(2,1)S(1)} collective-permute-done((bf16[144,512]{1,0:T(8,128)(2,1)S(1)}, bf16[144,512]{1,0:T(8,128)(2,1)S(1)}, u32[]{:S(2)}, u32[]{:S(2)}) %collective-permute-start.8) | collective-permute-done | bytes 147488 | tf_op jit(solution)/shard_map/ppermute | solution.py:621
  30.1 1.4 %collective-permute-done.10.refs_0_.refs_4_.refs_2_ = bf16[128,512]{1,0:T(8,128)(2,1)S(1)} collective-permute-done((bf16[128,512]{1,0:T(8,128)(2,1)S(1)}, bf16[128,512]{1,0:T(8,128)(2,1)S(1)}, u32[]{:S(2)}, u32[]{:S(2)}) %collective-permute-start.10) | collective-permute-done | bytes 131104 | tf_op jit(solution)/shard_map/ppermute | solution.py:621
  31.5 1.4 %collective-permute-done.11.refs_0_.refs_3_ = bf16[128,512]{1,0:T(8,128)(2,1)S(1)} collective-permute-done((bf16[128,512]{1,0:T(8,128)(2,1)S(1)}, bf16[128,512]{1,0:T(8,128)(2,1)S(1)}, u32[]{:S(2)}, u32[]{:S(2)}) %collective-permute-start.11) | collective-permute-done | bytes 131104 | tf_op jit(solution)/shard_map/ppermute | solution.py:621
  33.0 0.0 collective-permute-done.13.refs_11_.refs_14_.refs_7_.refs_8_
  33.0 1.4 %collective-permute-done.12.refs_4_ = bf16[128,512]{1,0:T(8,128)(2,1)S(1)} collective-permute-done((bf16[128,512]{1,0:T(8,128)(2,1)S(1)}, bf16[128,512]{1,0:T(8,128)(2,1)S(1)}, u32[]{:S(2)}, u32[]{:S(2)}) %collective-permute-start.12) | collective-permute-done | bytes 131104 | tf_op jit(solution)/shard_map/ppermute | solution.py:621
  34.4 0.0 collective-permute-start.15
  34.4 0.5 %collective-permute-start.14 = (bf16[128,512]{1,0:T(8,128)(2,1)S(1)}, bf16[128,512]{1,0:T(8,128)(2,1)S(1)}, u32[]{:S(2)}, u32[]{:S(2)}) collective-permute-start(bf16[128,512]{1,0:T(8,128)(2,1)S(1)} %far_part.3), channel_id=1, source_target_pairs={{0,1},{1,0},{2,3},{3,2},{4,5},{5,17},{6,7},{7,6},{8,9},{9,8},{10,1... | collective-permute-start | bytes 393224 | tf_op jit(solution)/shard_map/ppermute | solution.py:621
  34.9 7.0 %collective-permute-start.16 = (bf16[128,512]{1,0:T(8,128)(2,1)S(1)}, bf16[128,512]{1,0:T(8,128)(2,1)S(1)}, u32[]{:S(2)}, u32[]{:S(2)}) collective-permute-start(bf16[128,512]{1,0:T(8,128)(2,1)S(1)} %near_part.2.refs_3_), channel_id=1, source_target_pairs={{0,1},{1,17},{2,3},{3,2},{4,5},{5,4},{6,7},{7,6},{8,9},{9,27},{10,... | collective-permute-start | bytes 393224 | tf_op jit(solution)/shard_map/ppermute | solution.py:621
  41.9 0.0 collective-permute-start.17
  41.9 0.0 collective-permute-done.15.refs_0_
  41.9 0.0 collective-permute-done.14.refs_0_
  41.9 0.0 copy-start.5
  41.9 1.9 %collective-permute-done.16.refs_1_ = bf16[128,512]{1,0:T(8,128)(2,1)S(1)} collective-permute-done((bf16[128,512]{1,0:T(8,128)(2,1)S(1)}, bf16[128,512]{1,0:T(8,128)(2,1)S(1)}, u32[]{:S(2)}, u32[]{:S(2)}) %collective-permute-start.16) | collective-permute-done | bytes 131104 | tf_op jit(solution)/shard_map/ppermute | solution.py:621
  43.8 0.0 collective-permute-done.17.refs_2_
  43.9 4.0 %collective-permute-start.18 = (bf16[64,512]{1,0:T(8,128)(2,1)S(1)}, bf16[64,512]{1,0:T(8,128)(2,1)S(1)}, u32[]{:S(2)}, u32[]{:S(2)}) collective-permute-start(bf16[64,512]{1,0:T(8,128)(2,1)S(1)} %get-tuple-element.116), channel_id=1, source_target_pairs={{0,1},{1,0},{2,3},{3,2},{4,5},{5,4},{6,7},{7,6},{8,9},{9,8},{10,11... | collective-permute-start | bytes 196616 | tf_op jit(solution)/shard_map/ppermute | solution.py:640
  47.8 0.9 %collective-permute-done.18.refs_5_ = bf16[64,512]{1,0:T(8,128)(2,1)S(1)} collective-permute-done((bf16[64,512]{1,0:T(8,128)(2,1)S(1)}, bf16[64,512]{1,0:T(8,128)(2,1)S(1)}, u32[]{:S(2)}, u32[]{:S(2)}) %collective-permute-start.18) | collective-permute-done | bytes 65568 | tf_op jit(solution)/shard_map/ppermute | solution.py:640
  48.7 1.2 %decode.1 = bf16[227,128]{1,0:T(8,128)(2,1)} custom-call(s32[1]{0:T(128)} %bitcast.segment, s32[1]{0:T(128)} %bitcast.1.place, f32[128,512]{1,0:T(8,128)S(1)} %get-tuple-element.88.refs_0_, bf16[64,128]{1,0:T(8,128)(2,1)S(1)} %get-tuple-element.89.refs_1_, bf16[1024,512]{1,0:T(8,128)(2,1)S(1)} %copy-done, bf16[227,512]{1,0:T(8,128)(2,1)S(1)} %bitcast.15, ...), custom_call_target="tpu_custom_call" | custom-call | bytes 1748744 | tf_op jit(solution)/shard_map/decode/pallas_call | solution.py:557
  (44 shorter events, 0.2 us)
Async XLA Ops:
  0.0 1.7 %copy-start.7 = (s32[64,8]{0,1:T(8,128)S(1)}, s32[64,8]{0,1:T(8,128)}, u32[]{:S(2)}) copy-start(s32[64,8]{0,1:T(8,128)} %param.21) | copy-start | bytes 6148
  0.0 1.8 %copy-start.8 = (s32[4,64]{1,0:T(4,128)S(1)}, s32[4,64]{1,0:T(4,128)}, u32[]{:S(2)}) copy-start(s32[4,64]{1,0:T(4,128)} %param.22) | copy-start | bytes 3076
  0.0 1.8 %copy-start.9 = (s32[4,1]{0,1:T(1,128)S(1)}, s32[4,1]{0,1:T(1,128)}, u32[]{:S(2)}) copy-start(s32[4,1]{0,1:T(1,128)} %param.23) | copy-start | bytes 52
  0.0 1.8 %copy-start.10 = (s32[128]{0:T(128)S(1)}, s32[128]{0:T(128)}, u32[]{:S(2)}) copy-start(s32[128]{0:T(128)} %param.19) | copy-start | bytes 1540
  0.0 1.8 %copy-start.3 = (bf16[227,512]{1,0:T(8,128)(2,1)S(1)}, bf16[227,512]{1,0:T(8,128)(2,1)}, u32[]{:S(2)}) copy-start(bf16[227,512]{1,0:T(8,128)(2,1)} %refs_1_.3) | copy-start | bytes 697348
  0.0 5.3 %copy-start.4 = (bf16[1,512,512]{2,1,0:T(8,128)(2,1)S(1)}, bf16[1,512,512]{2,1,0:T(8,128)(2,1)}, u32[]{:S(2)}) copy-start(bf16[1,512,512]{2,1,0:T(8,128)(2,1)} %w_message.1) | copy-start | bytes 1572868
  0.0 10.4 %collective-permute-start.4 = (bf16[1,512,1024]{2,1,0:T(8,128)(2,1)}, bf16[1,512,1024]{2,1,0:T(8,128)(2,1)S(1)}, u32[]{:S(2)}, u32[]{:S(2)}) collective-permute-start(bf16[1,512,1024]{2,1,0:T(8,128)(2,1)} %w_project), channel_id=1, source_target_pairs={{0,1},{1,0},{2,3},{3,2},{4,5},{5,4},{6,7},{7,6},{8,9},{9,8},{10,11... | collective-permute-start | bytes 3145736 | tf_op jit(solution)/shard_map/ppermute | solution.py:621
  2.5 6.0 %collective-permute-start = (bf16[80,512]{1,0:T(8,128)(2,1)S(1)}, bf16[80,512]{1,0:T(8,128)(2,1)S(1)}, u32[]{:S(2)}, u32[]{:S(2)}) collective-permute-start(bf16[80,512]{1,0:T(8,128)(2,1)S(1)} %get-tuple-element.63), channel_id=1, source_target_pairs={{0,8},{1,9},{2,10},{3,11},{4,12},{5,13},{6,14},{7,15},{8,4},{9,5},... | collective-permute-start | bytes 245768 | tf_op jit(solution)/shard_map/ppermute | solution.py:636
  4.9 3.7 %collective-permute-start.1 = (bf16[80,512]{1,0:T(8,128)(2,1)S(1)}, bf16[80,512]{1,0:T(8,128)(2,1)S(1)}, u32[]{:S(2)}, u32[]{:S(2)}) collective-permute-start(bf16[80,512]{1,0:T(8,128)(2,1)S(1)} %get-tuple-element.64), channel_id=1, source_target_pairs={{0,16},{1,17},{2,18},{3,19},{4,20},{5,21},{6,22},{7,23},{8,9},{9,8... | collective-permute-start | bytes 245768 | tf_op jit(solution)/shard_map/ppermute | solution.py:636
  5.3 3.3 %collective-permute-start.2 = (bf16[80,512]{1,0:T(8,128)(2,1)S(1)}, bf16[80,512]{1,0:T(8,128)(2,1)S(1)}, u32[]{:S(2)}, u32[]{:S(2)}) collective-permute-start(bf16[80,512]{1,0:T(8,128)(2,1)S(1)} %get-tuple-element.65), channel_id=1, source_target_pairs={{0,2},{1,3},{2,0},{3,1},{4,6},{5,7},{6,4},{7,5},{8,9},{9,8},{10,11... | collective-permute-start | bytes 245768 | tf_op jit(solution)/shard_map/ppermute | solution.py:636
  5.4 1.2 %copy-start.1 = (bf16[1,1024,512]{2,1,0:T(8,128)(2,1)S(1)}, bf16[1,1024,512]{2,1,0:T(8,128)(2,1)}, u32[]{:S(2)}) copy-start(bf16[1,1024,512]{2,1,0:T(8,128)(2,1)} %w_update.1) | copy-start | bytes 3145732
  6.6 1.2 %copy-start.2 = (bf16[1,512,1024]{2,1,0:T(8,128)(2,1)S(1)}, bf16[1,512,1024]{2,1,0:T(8,128)(2,1)}, u32[]{:S(2)}) copy-start(bf16[1,512,1024]{2,1,0:T(8,128)(2,1)} %w_project) | copy-start | bytes 3145732
  8.6 1.8 %collective-permute-start.3 = (bf16[320,512]{1,0:T(8,128)(2,1)S(1)}, bf16[320,512]{1,0:T(8,128)(2,1)S(1)}, u32[]{:S(2)}, u32[]{:S(2)}) collective-permute-start(bf16[320,512]{1,0:T(8,128)(2,1)S(1)} %join.1.refs_0_), channel_id=1, source_target_pairs={{0,1},{1,0},{2,3},{3,2},{4,5},{5,4},{6,7},{7,6},{8,9},{9,8},{10,11... | collective-permute-start | bytes 983048 | tf_op jit(solution)/shard_map/ppermute | solution.py:640
  10.4 22.6 %collective-permute-start.13 = (bf16[2,512,512]{2,1,0:T(8,128)(2,1)S(1)}, bf16[2,512,512]{2,1,0:T(8,128)(2,1)S(1)}, u32[]{:S(2)}, u32[]{:S(2)}) collective-permute-start(bf16[2,512,512]{2,1,0:T(8,128)(2,1)S(1)} %pack.1), channel_id=1, source_target_pairs={{0,1},{1,0},{2,3},{3,2},{4,5},{5,4},{6,7},{7,6},{8,9},{9,8},{10,11... | collective-permute-start | bytes 3145736 | tf_op jit(solution)/shard_map/ppermute | solution.py:621
  10.8 8.5 %collective-permute-start.5 = (bf16[144,512]{1,0:T(8,128)(2,1)S(1)}, bf16[144,512]{1,0:T(8,128)(2,1)S(1)}, u32[]{:S(2)}, u32[]{:S(2)}) collective-permute-start(bf16[144,512]{1,0:T(8,128)(2,1)S(1)} %get-tuple-element.85), channel_id=1, source_target_pairs={{0,8},{1,0},{2,10},{3,2},{4,12},{5,4},{6,14},{7,6},{8,9},{9,1},{10... | collective-permute-start | bytes 442376 | tf_op jit(solution)/shard_map/ppermute | solution.py:621
  14.2 5.1 %collective-permute-start.6 = (bf16[128,512]{1,0:T(8,128)(2,1)S(1)}, bf16[128,512]{1,0:T(8,128)(2,1)S(1)}, u32[]{:S(2)}, u32[]{:S(2)}) collective-permute-start(bf16[128,512]{1,0:T(8,128)(2,1)S(1)} %next.5), channel_id=1, source_target_pairs={{0,8},{1,0},{2,10},{3,2},{4,12},{5,4},{6,14},{7,6},{8,9},{9,1},{10... | collective-permute-start | bytes 393224 | tf_op jit(solution)/shard_map/ppermute | solution.py:621
  15.9 3.0 %copy-start = (bf16[1024,512]{1,0:T(8,128)(2,1)S(1)}, bf16[1024,512]{1,0:T(8,128)(2,1)}, u32[]{:S(2)}) copy-start(bf16[1024,512]{1,0:T(8,128)(2,1)} %refs_2_.3) | copy-start | bytes 3145732
  15.9 3.5 %collective-permute-start.7 = (bf16[128,512]{1,0:T(8,128)(2,1)S(1)}, bf16[128,512]{1,0:T(8,128)(2,1)S(1)}, u32[]{:S(2)}, u32[]{:S(2)}) collective-permute-start(bf16[128,512]{1,0:T(8,128)(2,1)S(1)} %next.6), channel_id=1, source_target_pairs={{0,8},{1,0},{2,10},{3,2},{4,12},{5,4},{6,14},{7,6},{8,9},{9,1},{10... | collective-permute-start | bytes 393224 | tf_op jit(solution)/shard_map/ppermute | solution.py:621
  17.4 1.5 %copy-start.6 = (s32[128]{0:T(128)S(1)}, s32[128]{0:T(128)}, u32[]{:S(2)}) copy-start(s32[128]{0:T(128)} %param.20) | copy-start | bytes 1540
  17.4 6.4 %collective-permute-start.9 = (bf16[128,512]{1,0:T(8,128)(2,1)S(1)}, bf16[128,512]{1,0:T(8,128)(2,1)S(1)}, u32[]{:S(2)}, u32[]{:S(2)}) collective-permute-start(bf16[128,512]{1,0:T(8,128)(2,1)S(1)} %next.7), channel_id=1, source_target_pairs={{0,8},{1,0},{2,10},{3,2},{4,12},{5,4},{6,14},{7,6},{8,9},{9,1},{10... | collective-permute-start | bytes 393224 | tf_op jit(solution)/shard_map/ppermute | solution.py:621
  19.4 10.7 %collective-permute-start.8 = (bf16[144,512]{1,0:T(8,128)(2,1)S(1)}, bf16[144,512]{1,0:T(8,128)(2,1)S(1)}, u32[]{:S(2)}, u32[]{:S(2)}) collective-permute-start(bf16[144,512]{1,0:T(8,128)(2,1)S(1)} %early.2), channel_id=1, source_target_pairs={{0,1},{1,0},{2,3},{3,2},{4,5},{5,4},{6,7},{7,6},{8,16},{9,8},{10,2... | collective-permute-start | bytes 442376 | tf_op jit(solution)/shard_map/ppermute | solution.py:621
  23.8 7.8 %collective-permute-start.10 = (bf16[128,512]{1,0:T(8,128)(2,1)S(1)}, bf16[128,512]{1,0:T(8,128)(2,1)S(1)}, u32[]{:S(2)}, u32[]{:S(2)}) collective-permute-start(bf16[128,512]{1,0:T(8,128)(2,1)S(1)} %get-tuple-element.103), channel_id=1, source_target_pairs={{0,1},{1,0},{2,3},{3,2},{4,5},{5,4},{6,7},{7,6},{8,16},{9,8},{10,2... | collective-permute-start | bytes 393224 | tf_op jit(solution)/shard_map/ppermute | solution.py:621
  25.3 7.6 %collective-permute-start.11 = (bf16[128,512]{1,0:T(8,128)(2,1)S(1)}, bf16[128,512]{1,0:T(8,128)(2,1)S(1)}, u32[]{:S(2)}, u32[]{:S(2)}) collective-permute-start(bf16[128,512]{1,0:T(8,128)(2,1)S(1)} %next.8), channel_id=1, source_target_pairs={{0,1},{1,0},{2,3},{3,2},{4,5},{5,4},{6,7},{7,6},{8,16},{9,8},{10,2... | collective-permute-start | bytes 393224 | tf_op jit(solution)/shard_map/ppermute | solution.py:621
  26.8 7.5 %collective-permute-start.12 = (bf16[128,512]{1,0:T(8,128)(2,1)S(1)}, bf16[128,512]{1,0:T(8,128)(2,1)S(1)}, u32[]{:S(2)}, u32[]{:S(2)}) collective-permute-start(bf16[128,512]{1,0:T(8,128)(2,1)S(1)} %next.9), channel_id=1, source_target_pairs={{0,1},{1,0},{2,3},{3,2},{4,5},{5,4},{6,7},{7,6},{8,16},{9,8},{10,2... | collective-permute-start | bytes 393224 | tf_op jit(solution)/shard_map/ppermute | solution.py:621
  34.4 7.5 %collective-permute-start.15 = (bf16[128,512]{1,0:T(8,128)(2,1)S(1)}, bf16[128,512]{1,0:T(8,128)(2,1)S(1)}, u32[]{:S(2)}, u32[]{:S(2)}) collective-permute-start(bf16[128,512]{1,0:T(8,128)(2,1)S(1)} %get-tuple-element.114), channel_id=1, source_target_pairs={{0,1},{1,0},{2,3},{3,2},{4,5},{5,4},{6,7},{7,21},{8,9},{9,8},{10,1... | collective-permute-start | bytes 393224 | tf_op jit(solution)/shard_map/ppermute | solution.py:621
  34.4 7.5 %collective-permute-start.14 = (bf16[128,512]{1,0:T(8,128)(2,1)S(1)}, bf16[128,512]{1,0:T(8,128)(2,1)S(1)}, u32[]{:S(2)}, u32[]{:S(2)}) collective-permute-start(bf16[128,512]{1,0:T(8,128)(2,1)S(1)} %far_part.3), channel_id=1, source_target_pairs={{0,1},{1,0},{2,3},{3,2},{4,5},{5,17},{6,7},{7,6},{8,9},{9,8},{10,1... | collective-permute-start | bytes 393224 | tf_op jit(solution)/shard_map/ppermute | solution.py:621
  34.9 9.0 %collective-permute-start.16 = (bf16[128,512]{1,0:T(8,128)(2,1)S(1)}, bf16[128,512]{1,0:T(8,128)(2,1)S(1)}, u32[]{:S(2)}, u32[]{:S(2)}) collective-permute-start(bf16[128,512]{1,0:T(8,128)(2,1)S(1)} %near_part.2.refs_3_), channel_id=1, source_target_pairs={{0,1},{1,17},{2,3},{3,2},{4,5},{5,4},{6,7},{7,6},{8,9},{9,27},{10,... | collective-permute-start | bytes 393224 | tf_op jit(solution)/shard_map/ppermute | solution.py:621
  41.9 2.0 %collective-permute-start.17 = (bf16[128,512]{1,0:T(8,128)(2,1)S(1)}, bf16[128,512]{1,0:T(8,128)(2,1)S(1)}, u32[]{:S(2)}, u32[]{:S(2)}) collective-permute-start(bf16[128,512]{1,0:T(8,128)(2,1)S(1)} %near_part.3.refs_4_), channel_id=1, source_target_pairs={{0,1},{1,0},{2,3},{3,17},{4,5},{5,4},{6,7},{7,6},{8,9},{9,8},{10,1... | collective-permute-start | bytes 393224 | tf_op jit(solution)/shard_map/ppermute | solution.py:621
  41.9 6.8 %copy-start.5 = (bf16[512,227]{0,1:T(8,128)(2,1)S(1)}, bf16[512,227]{0,1:T(8,128)(2,1)}, u32[]{:S(2)}) copy-start(bf16[512,227]{0,1:T(8,128)(2,1)} %param.18) | copy-start | bytes 697348
  43.9 4.9 %collective-permute-start.18 = (bf16[64,512]{1,0:T(8,128)(2,1)S(1)}, bf16[64,512]{1,0:T(8,128)(2,1)S(1)}, u32[]{:S(2)}, u32[]{:S(2)}) collective-permute-start(bf16[64,512]{1,0:T(8,128)(2,1)S(1)} %get-tuple-element.116), channel_id=1, source_target_pairs={{0,1},{1,0},{2,3},{3,2},{4,5},{5,4},{6,7},{7,6},{8,9},{9,8},{10,11... | collective-permute-start | bytes 196616 | tf_op jit(solution)/shard_map/ppermute | solution.py:640

commit v23 on v20

--- a/solution.py
+++ b/solution.py
@@ -319,13 +319,18 @@
     none = jnp.zeros((chunk, tile), jnp.bfloat16)
     receiver = 0.5 * matmul(own, w_receive)
     total = jnp.zeros((chunk, width), jnp.float32)
-    for k in range(fanout):
-        hits = []
-        for number in range(nodes // tile):
-            lane = number * fanout + k
-            hits.append(jnp.where(columns[:, lane : lane + 1] == names, one_half, none))
-        half = receiver + matmul(jnp.concatenate(hits, axis=1), sender)
-        total = total + (half + half * jnp.tanh(half))
+    for first in range(0, fanout, 2):
+        tables = []
+        for k in range(first, min(first + 2, fanout)):
+            hits = []
+            for number in range(nodes // tile):
+                lane = number * fanout + k
+                hits.append(jnp.where(columns[:, lane : lane + 1] == names, one_half, none))
+            tables.append(jnp.concatenate(hits, axis=1))
+        fetched = matmul(jnp.concatenate(tables, axis=0), sender)
+        for place in range(len(tables)):
+            half = receiver + fetched[place * chunk : (place + 1) * chunk]
+            total = total + (half + half * jnp.tanh(half))
     return (total * (1.0 / fanout)).astype(jnp.bfloat16)
 
 

time: 50.6 us -> 50.7 us (level)
  no operation moved by 1% of the time
where the time goes in v23:
time: 50.7 us; the launch traced here: 50.1 us
  starting transfers between devices  33.2 us (65%)
  waiting for transfers between devices  10 us (20%)
  local copies, waits for them, and re-layouts  3.46 us (7%)
  Pallas kernels  3.2 us (6%)
    ppermute x14, starting transfers between devices, send(): lax.ppermute(value, ('segment', 'dom'), every_device(pairs, segments * pa...  25.9 us
    ppermute x14, waiting for transfers between devices, send(): lax.ppermute(value, ('segment', 'dom'), every_device(pairs, segments * pa...  7.88 us
    ppermute x2, starting transfers between devices, change_lane(): return lax.ppermute(value, 'dom', pairs)  4.46 us
    unnamed x23, local copies, waits for them, and re-layouts  3.46 us
    pallas_call x30, Pallas kernels, call(): pl.pallas_call(located if places[0] == 'w' else kernel, out_shape=shapes,...  3.2 us
    ppermute x3, starting transfers between devices, to_chip(): return lax.ppermute(value, ('segment', 'dom'), pairs)  2.84 us
    ppermute x2, waiting for transfers between devices, change_lane(): return lax.ppermute(value, 'dom', pairs)  2.16 us
  transfers between devices with their start and end apart: 19, of which 7 were waited for; matrix products, arithmetic and copies ran while one was open for 2% of the time, Pallas kernels for 4%

profile of v23, /device:TPU:3, one launch (start us, length us, event | category | flops | bytes accessed | tf_op | source)
XLA Modules:
  0.0 50.1 jit_solution(8357317573324234458)
XLA Ops:
  0.0 0.0 copy-start.10
  0.0 0.7 %collective-permute-start.4 = (bf16[1,512,1024]{2,1,0:T(8,128)(2,1)}, bf16[1,512,1024]{2,1,0:T(8,128)(2,1)S(1)}, u32[]{:S(2)}, u32[]{:S(2)}) collective-permute-start(bf16[1,512,1024]{2,1,0:T(8,128)(2,1)} %w_project), channel_id=1, source_target_pairs={{0,1},{1,0},{2,3},{3,2},{4,5},{5,4},{6,7},{7,6},{8,9},{9,8},{10,11... | collective-permute-start | bytes 3145736 | tf_op jit(solution)/shard_map/ppermute | solution.py:621
  0.8 1.0 %copy.15 = bf16[4,128,227]{1,2,0:T(8,128)(2,1)S(1)} copy(bf16[4,128,227]{1,0,2:T(4,128)(2,1)} %param.12) | data formatting | bytes 464896 | tf_op args[0]
  1.8 0.7 %encode.1 = (bf16[80,512]{1,0:T(8,128)(2,1)S(1)}, bf16[80,512]{1,0:T(8,128)(2,1)S(1)}, bf16[80,512]{1,0:T(8,128)(2,1)S(1)}, bf16[80,512]{1,0:T(8,128)(2,1)S(1)}) custom-call(s32[1]{0:T(128)} %bitcast.segment, s32[1]{0:T(128)} %bitcast.1.place, bf16[4,227,128]{2,1,0:T(8,128)(2,1)S(1)} %bitcast.13, bf16[227,512]{1,0:T(8,128)(2,1)S(1)} %copy-done.3, ...), custom_call_target="tpu_custom_call" | custom-call | bytes 799752 | tf_op jit(solution)/shard_map/encode/pallas_call | solution.py:557
  2.5 2.3 %collective-permute-start = (bf16[80,512]{1,0:T(8,128)(2,1)S(1)}, bf16[80,512]{1,0:T(8,128)(2,1)S(1)}, u32[]{:S(2)}, u32[]{:S(2)}) collective-permute-start(bf16[80,512]{1,0:T(8,128)(2,1)S(1)} %get-tuple-element.63), channel_id=1, source_target_pairs={{0,8},{1,9},{2,10},{3,11},{4,12},{5,13},{6,14},{7,15},{8,4},{9,5},... | collective-permute-start | bytes 245768 | tf_op jit(solution)/shard_map/ppermute | solution.py:636
  4.9 0.4 collective-permute-start.1
  5.3 0.1 collective-permute-start.2
  5.4 1.2 %copy-done.1 = bf16[1,1024,512]{2,1,0:T(8,128)(2,1)S(1)} copy-done((bf16[1,1024,512]{2,1,0:T(8,128)(2,1)S(1)}, bf16[1,1024,512]{2,1,0:T(8,128)(2,1)}, u32[]{:S(2)}) %copy-start.1) | copy-done | bytes 1048600
  6.6 1.2 %copy-done.2 = bf16[1,512,1024]{2,1,0:T(8,128)(2,1)S(1)} copy-done((bf16[1,512,1024]{2,1,0:T(8,128)(2,1)S(1)}, bf16[1,512,1024]{2,1,0:T(8,128)(2,1)}, u32[]{:S(2)}) %copy-start.2) | copy-done | bytes 1048600
  7.8 0.7 %hold.1 = (bf16[512,512]{1,0:T(8,128)(2,1)S(1)}, bf16[512,512]{1,0:T(8,128)(2,1)S(1)}, bf16[512,512]{1,0:T(8,128)(2,1)S(1)}, bf16[512,512]{1,0:T(8,128)(2,1)S(1)}) custom-call(bf16[1,512,1024]{2,1,0:T(8,128)(2,1)S(1)} %copy-done.2, bf16[1,512,512]{2,1,0:T(8,128)(2,1)S(1)} %copy-done.4, bf16[1,1024,512]{2,1,0:T(8,128)(2,1)S(1)} %copy-done.1), custom_call_target="tpu_custom_call" | custom-call | bytes 4718592 | tf_op jit(solution)/shard_map/hold/pallas_call | solution.py:557
  8.6 0.0 collective-permute-done.refs_0_
  8.6 0.0 collective-permute-done.1.refs_1_
  8.6 0.0 collective-permute-done.2.refs_2_
  8.6 0.5 %collective-permute-start.3 = (bf16[320,512]{1,0:T(8,128)(2,1)S(1)}, bf16[320,512]{1,0:T(8,128)(2,1)S(1)}, u32[]{:S(2)}, u32[]{:S(2)}) collective-permute-start(bf16[320,512]{1,0:T(8,128)(2,1)S(1)} %join.1.refs_0_), channel_id=1, source_target_pairs={{0,1},{1,0},{2,3},{3,2},{4,5},{5,4},{6,7},{7,6},{8,9},{9,8},{10,11... | collective-permute-start | bytes 983048 | tf_op jit(solution)/shard_map/ppermute | solution.py:640
  9.1 1.3 %collective-permute-done.3.refs_1_ = bf16[320,512]{1,0:T(8,128)(2,1)S(1)} collective-permute-done((bf16[320,512]{1,0:T(8,128)(2,1)S(1)}, bf16[320,512]{1,0:T(8,128)(2,1)S(1)}, u32[]{:S(2)}, u32[]{:S(2)}) %collective-permute-start.3) | collective-permute-done | bytes 327712 | tf_op jit(solution)/shard_map/ppermute | solution.py:640
  10.4 0.0 collective-permute-done.4.refs_2_.refs_10_.refs_13_.refs_6_.refs_7_
  10.4 0.4 collective-permute-start.13
  10.8 3.5 %collective-permute-start.5 = (bf16[144,512]{1,0:T(8,128)(2,1)S(1)}, bf16[144,512]{1,0:T(8,128)(2,1)S(1)}, u32[]{:S(2)}, u32[]{:S(2)}) collective-permute-start(bf16[144,512]{1,0:T(8,128)(2,1)S(1)} %get-tuple-element.85), channel_id=1, source_target_pairs={{0,8},{1,0},{2,10},{3,2},{4,12},{5,4},{6,14},{7,6},{8,9},{9,1},{10... | collective-permute-start | bytes 442376 | tf_op jit(solution)/shard_map/ppermute | solution.py:621
  14.2 1.7 %collective-permute-start.6 = (bf16[128,512]{1,0:T(8,128)(2,1)S(1)}, bf16[128,512]{1,0:T(8,128)(2,1)S(1)}, u32[]{:S(2)}, u32[]{:S(2)}) collective-permute-start(bf16[128,512]{1,0:T(8,128)(2,1)S(1)} %next.5), channel_id=1, source_target_pairs={{0,8},{1,0},{2,10},{3,2},{4,12},{5,4},{6,14},{7,6},{8,9},{9,1},{10... | collective-permute-start | bytes 393224 | tf_op jit(solution)/shard_map/ppermute | solution.py:621
  15.9 1.4 %collective-permute-start.7 = (bf16[128,512]{1,0:T(8,128)(2,1)S(1)}, bf16[128,512]{1,0:T(8,128)(2,1)S(1)}, u32[]{:S(2)}, u32[]{:S(2)}) collective-permute-start(bf16[128,512]{1,0:T(8,128)(2,1)S(1)} %next.6), channel_id=1, source_target_pairs={{0,8},{1,0},{2,10},{3,2},{4,12},{5,4},{6,14},{7,6},{8,9},{9,1},{10... | collective-permute-start | bytes 393224 | tf_op jit(solution)/shard_map/ppermute | solution.py:621
  17.3 1.4 %collective-permute-start.9 = (bf16[128,512]{1,0:T(8,128)(2,1)S(1)}, bf16[128,512]{1,0:T(8,128)(2,1)S(1)}, u32[]{:S(2)}, u32[]{:S(2)}) collective-permute-start(bf16[128,512]{1,0:T(8,128)(2,1)S(1)} %next.7), channel_id=1, source_target_pairs={{0,8},{1,0},{2,10},{3,2},{4,12},{5,4},{6,14},{7,6},{8,9},{9,1},{10... | collective-permute-start | bytes 393224 | tf_op jit(solution)/shard_map/ppermute | solution.py:621
  18.8 0.0 copy-done
  18.8 0.4 prepare.1
  19.2 0.0 collective-permute-done.5.refs_0_.refs_5_.refs_1_
  19.2 0.0 collective-permute-done.6.refs_0_.refs_4_.refs_2_
  19.3 0.0 collective-permute-done.7.refs_0_.refs_3_
  19.3 4.5 %collective-permute-start.8 = (bf16[144,512]{1,0:T(8,128)(2,1)S(1)}, bf16[144,512]{1,0:T(8,128)(2,1)S(1)}, u32[]{:S(2)}, u32[]{:S(2)}) collective-permute-start(bf16[144,512]{1,0:T(8,128)(2,1)S(1)} %early.2), channel_id=1, source_target_pairs={{0,1},{1,0},{2,3},{3,2},{4,5},{5,4},{6,7},{7,6},{8,16},{9,8},{10,2... | collective-permute-start | bytes 442376 | tf_op jit(solution)/shard_map/ppermute | solution.py:621
  23.8 0.0 collective-permute-done.9.refs_4_
  23.8 1.6 %collective-permute-start.10 = (bf16[128,512]{1,0:T(8,128)(2,1)S(1)}, bf16[128,512]{1,0:T(8,128)(2,1)S(1)}, u32[]{:S(2)}, u32[]{:S(2)}) collective-permute-start(bf16[128,512]{1,0:T(8,128)(2,1)S(1)} %get-tuple-element.103), channel_id=1, source_target_pairs={{0,1},{1,0},{2,3},{3,2},{4,5},{5,4},{6,7},{7,6},{8,16},{9,8},{10,2... | collective-permute-start | bytes 393224 | tf_op jit(solution)/shard_map/ppermute | solution.py:621
  25.3 1.4 %collective-permute-start.11 = (bf16[128,512]{1,0:T(8,128)(2,1)S(1)}, bf16[128,512]{1,0:T(8,128)(2,1)S(1)}, u32[]{:S(2)}, u32[]{:S(2)}) collective-permute-start(bf16[128,512]{1,0:T(8,128)(2,1)S(1)} %next.8), channel_id=1, source_target_pairs={{0,1},{1,0},{2,3},{3,2},{4,5},{5,4},{6,7},{7,6},{8,16},{9,8},{10,2... | collective-permute-start | bytes 393224 | tf_op jit(solution)/shard_map/ppermute | solution.py:621
  26.8 1.6 %collective-permute-start.12 = (bf16[128,512]{1,0:T(8,128)(2,1)S(1)}, bf16[128,512]{1,0:T(8,128)(2,1)S(1)}, u32[]{:S(2)}, u32[]{:S(2)}) collective-permute-start(bf16[128,512]{1,0:T(8,128)(2,1)S(1)} %next.9), channel_id=1, source_target_pairs={{0,1},{1,0},{2,3},{3,2},{4,5},{5,4},{6,7},{7,6},{8,16},{9,8},{10,2... | collective-permute-start | bytes 393224 | tf_op jit(solution)/shard_map/ppermute | solution.py:621
  28.4 1.7 %collective-permute-done.8.refs_0_.refs_5_.refs_1_ = bf16[144,512]{1,0:T(8,128)(2,1)S(1)} collective-permute-done((bf16[144,512]{1,0:T(8,128)(2,1)S(1)}, bf16[144,512]{1,0:T(8,128)(2,1)S(1)}, u32[]{:S(2)}, u32[]{:S(2)}) %collective-permute-start.8) | collective-permute-done | bytes 147488 | tf_op jit(solution)/shard_map/ppermute | solution.py:621
  30.1 1.4 %collective-permute-done.10.refs_0_.refs_4_.refs_2_ = bf16[128,512]{1,0:T(8,128)(2,1)S(1)} collective-permute-done((bf16[128,512]{1,0:T(8,128)(2,1)S(1)}, bf16[128,512]{1,0:T(8,128)(2,1)S(1)}, u32[]{:S(2)}, u32[]{:S(2)}) %collective-permute-start.10) | collective-permute-done | bytes 131104 | tf_op jit(solution)/shard_map/ppermute | solution.py:621
  31.5 1.4 %collective-permute-done.11.refs_0_.refs_3_ = bf16[128,512]{1,0:T(8,128)(2,1)S(1)} collective-permute-done((bf16[128,512]{1,0:T(8,128)(2,1)S(1)}, bf16[128,512]{1,0:T(8,128)(2,1)S(1)}, u32[]{:S(2)}, u32[]{:S(2)}) %collective-permute-start.11) | collective-permute-done | bytes 131104 | tf_op jit(solution)/shard_map/ppermute | solution.py:621
  33.0 0.0 collective-permute-done.13.refs_11_.refs_14_.refs_7_.refs_8_
  33.0 1.4 %collective-permute-done.12.refs_4_ = bf16[128,512]{1,0:T(8,128)(2,1)S(1)} collective-permute-done((bf16[128,512]{1,0:T(8,128)(2,1)S(1)}, bf16[128,512]{1,0:T(8,128)(2,1)S(1)}, u32[]{:S(2)}, u32[]{:S(2)}) %collective-permute-start.12) | collective-permute-done | bytes 131104 | tf_op jit(solution)/shard_map/ppermute | solution.py:621
  34.4 0.0 collective-permute-start.15
  34.4 0.5 %collective-permute-start.14 = (bf16[128,512]{1,0:T(8,128)(2,1)S(1)}, bf16[128,512]{1,0:T(8,128)(2,1)S(1)}, u32[]{:S(2)}, u32[]{:S(2)}) collective-permute-start(bf16[128,512]{1,0:T(8,128)(2,1)S(1)} %far_part.3), channel_id=1, source_target_pairs={{0,1},{1,0},{2,3},{3,2},{4,5},{5,4},{6,7},{7,17},{8,9},{9,8},{10,1... | collective-permute-start | bytes 393224 | tf_op jit(solution)/shard_map/ppermute | solution.py:621
  34.9 7.2 %collective-permute-start.16 = (bf16[128,512]{1,0:T(8,128)(2,1)S(1)}, bf16[128,512]{1,0:T(8,128)(2,1)S(1)}, u32[]{:S(2)}, u32[]{:S(2)}) collective-permute-start(bf16[128,512]{1,0:T(8,128)(2,1)S(1)} %near_part.2.refs_3_), channel_id=1, source_target_pairs={{0,1},{1,17},{2,3},{3,2},{4,5},{5,4},{6,7},{7,6},{8,9},{9,27},{10,... | collective-permute-start | bytes 393224 | tf_op jit(solution)/shard_map/ppermute | solution.py:621
  42.0 0.0 collective-permute-start.17
  42.0 0.0 collective-permute-done.15.refs_0_
  42.0 0.0 collective-permute-done.14.refs_0_
  42.1 0.0 copy-start.5
  42.1 1.9 %collective-permute-done.16.refs_1_ = bf16[128,512]{1,0:T(8,128)(2,1)S(1)} collective-permute-done((bf16[128,512]{1,0:T(8,128)(2,1)S(1)}, bf16[128,512]{1,0:T(8,128)(2,1)S(1)}, u32[]{:S(2)}, u32[]{:S(2)}) %collective-permute-start.16) | collective-permute-done | bytes 131104 | tf_op jit(solution)/shard_map/ppermute | solution.py:621
  44.0 0.0 collective-permute-done.17.refs_2_
  44.0 4.0 %collective-permute-start.18 = (bf16[64,512]{1,0:T(8,128)(2,1)S(1)}, bf16[64,512]{1,0:T(8,128)(2,1)S(1)}, u32[]{:S(2)}, u32[]{:S(2)}) collective-permute-start(bf16[64,512]{1,0:T(8,128)(2,1)S(1)} %get-tuple-element.116), channel_id=1, source_target_pairs={{0,1},{1,0},{2,3},{3,2},{4,5},{5,4},{6,7},{7,6},{8,9},{9,8},{10,11... | collective-permute-start | bytes 196616 | tf_op jit(solution)/shard_map/ppermute | solution.py:640
  48.0 0.9 %collective-permute-done.18.refs_5_ = bf16[64,512]{1,0:T(8,128)(2,1)S(1)} collective-permute-done((bf16[64,512]{1,0:T(8,128)(2,1)S(1)}, bf16[64,512]{1,0:T(8,128)(2,1)S(1)}, u32[]{:S(2)}, u32[]{:S(2)}) %collective-permute-start.18) | collective-permute-done | bytes 65568 | tf_op jit(solution)/shard_map/ppermute | solution.py:640
  48.9 1.2 %decode.1 = bf16[227,128]{1,0:T(8,128)(2,1)} custom-call(s32[1]{0:T(128)} %bitcast.segment, s32[1]{0:T(128)} %bitcast.1.place, f32[128,512]{1,0:T(8,128)S(1)} %get-tuple-element.88.refs_0_, bf16[64,128]{1,0:T(8,128)(2,1)S(1)} %get-tuple-element.89.refs_1_, bf16[1024,512]{1,0:T(8,128)(2,1)S(1)} %copy-done, bf16[227,512]{1,0:T(8,128)(2,1)S(1)} %bitcast.15, ...), custom_call_target="tpu_custom_call" | custom-call | bytes 1748744 | tf_op jit(solution)/shard_map/decode/pallas_call | solution.py:557
  (44 shorter events, 0.2 us)
Async XLA Ops:
  0.0 1.7 %copy-start.7 = (s32[64,8]{0,1:T(8,128)S(1)}, s32[64,8]{0,1:T(8,128)}, u32[]{:S(2)}) copy-start(s32[64,8]{0,1:T(8,128)} %param.21) | copy-start | bytes 6148
  0.0 1.8 %copy-start.8 = (s32[4,64]{1,0:T(4,128)S(1)}, s32[4,64]{1,0:T(4,128)}, u32[]{:S(2)}) copy-start(s32[4,64]{1,0:T(4,128)} %param.22) | copy-start | bytes 3076
  0.0 1.8 %copy-start.9 = (s32[4,1]{0,1:T(1,128)S(1)}, s32[4,1]{0,1:T(1,128)}, u32[]{:S(2)}) copy-start(s32[4,1]{0,1:T(1,128)} %param.23) | copy-start | bytes 52
  0.0 1.8 %copy-start.10 = (s32[128]{0:T(128)S(1)}, s32[128]{0:T(128)}, u32[]{:S(2)}) copy-start(s32[128]{0:T(128)} %param.19) | copy-start | bytes 1540
  0.0 1.8 %copy-start.3 = (bf16[227,512]{1,0:T(8,128)(2,1)S(1)}, bf16[227,512]{1,0:T(8,128)(2,1)}, u32[]{:S(2)}) copy-start(bf16[227,512]{1,0:T(8,128)(2,1)} %refs_1_.3) | copy-start | bytes 697348
  0.0 5.3 %copy-start.4 = (bf16[1,512,512]{2,1,0:T(8,128)(2,1)S(1)}, bf16[1,512,512]{2,1,0:T(8,128)(2,1)}, u32[]{:S(2)}) copy-start(bf16[1,512,512]{2,1,0:T(8,128)(2,1)} %w_message.1) | copy-start | bytes 1572868
  0.0 10.4 %collective-permute-start.4 = (bf16[1,512,1024]{2,1,0:T(8,128)(2,1)}, bf16[1,512,1024]{2,1,0:T(8,128)(2,1)S(1)}, u32[]{:S(2)}, u32[]{:S(2)}) collective-permute-start(bf16[1,512,1024]{2,1,0:T(8,128)(2,1)} %w_project), channel_id=1, source_target_pairs={{0,1},{1,0},{2,3},{3,2},{4,5},{5,4},{6,7},{7,6},{8,9},{9,8},{10,11... | collective-permute-start | bytes 3145736 | tf_op jit(solution)/shard_map/ppermute | solution.py:621
  2.5 6.0 %collective-permute-start = (bf16[80,512]{1,0:T(8,128)(2,1)S(1)}, bf16[80,512]{1,0:T(8,128)(2,1)S(1)}, u32[]{:S(2)}, u32[]{:S(2)}) collective-permute-start(bf16[80,512]{1,0:T(8,128)(2,1)S(1)} %get-tuple-element.63), channel_id=1, source_target_pairs={{0,8},{1,9},{2,10},{3,11},{4,12},{5,13},{6,14},{7,15},{8,4},{9,5},... | collective-permute-start | bytes 245768 | tf_op jit(solution)/shard_map/ppermute | solution.py:636
  4.9 3.7 %collective-permute-start.1 = (bf16[80,512]{1,0:T(8,128)(2,1)S(1)}, bf16[80,512]{1,0:T(8,128)(2,1)S(1)}, u32[]{:S(2)}, u32[]{:S(2)}) collective-permute-start(bf16[80,512]{1,0:T(8,128)(2,1)S(1)} %get-tuple-element.64), channel_id=1, source_target_pairs={{0,16},{1,17},{2,18},{3,19},{4,20},{5,21},{6,22},{7,23},{8,9},{9,8... | collective-permute-start | bytes 245768 | tf_op jit(solution)/shard_map/ppermute | solution.py:636
  5.3 3.3 %collective-permute-start.2 = (bf16[80,512]{1,0:T(8,128)(2,1)S(1)}, bf16[80,512]{1,0:T(8,128)(2,1)S(1)}, u32[]{:S(2)}, u32[]{:S(2)}) collective-permute-start(bf16[80,512]{1,0:T(8,128)(2,1)S(1)} %get-tuple-element.65), channel_id=1, source_target_pairs={{0,2},{1,3},{2,0},{3,1},{4,6},{5,7},{6,4},{7,5},{8,9},{9,8},{10,11... | collective-permute-start | bytes 245768 | tf_op jit(solution)/shard_map/ppermute | solution.py:636
  5.4 1.2 %copy-start.1 = (bf16[1,1024,512]{2,1,0:T(8,128)(2,1)S(1)}, bf16[1,1024,512]{2,1,0:T(8,128)(2,1)}, u32[]{:S(2)}) copy-start(bf16[1,1024,512]{2,1,0:T(8,128)(2,1)} %w_update.1) | copy-start | bytes 3145732
  6.6 1.2 %copy-start.2 = (bf16[1,512,1024]{2,1,0:T(8,128)(2,1)S(1)}, bf16[1,512,1024]{2,1,0:T(8,128)(2,1)}, u32[]{:S(2)}) copy-start(bf16[1,512,1024]{2,1,0:T(8,128)(2,1)} %w_project) | copy-start | bytes 3145732
  8.6 1.8 %collective-permute-start.3 = (bf16[320,512]{1,0:T(8,128)(2,1)S(1)}, bf16[320,512]{1,0:T(8,128)(2,1)S(1)}, u32[]{:S(2)}, u32[]{:S(2)}) collective-permute-start(bf16[320,512]{1,0:T(8,128)(2,1)S(1)} %join.1.refs_0_), channel_id=1, source_target_pairs={{0,1},{1,0},{2,3},{3,2},{4,5},{5,4},{6,7},{7,6},{8,9},{9,8},{10,11... | collective-permute-start | bytes 983048 | tf_op jit(solution)/shard_map/ppermute | solution.py:640
  10.4 22.6 %collective-permute-start.13 = (bf16[2,512,512]{2,1,0:T(8,128)(2,1)S(1)}, bf16[2,512,512]{2,1,0:T(8,128)(2,1)S(1)}, u32[]{:S(2)}, u32[]{:S(2)}) collective-permute-start(bf16[2,512,512]{2,1,0:T(8,128)(2,1)S(1)} %pack.1), channel_id=1, source_target_pairs={{0,1},{1,0},{2,3},{3,2},{4,5},{5,4},{6,7},{7,6},{8,9},{9,8},{10,11... | collective-permute-start | bytes 3145736 | tf_op jit(solution)/shard_map/ppermute | solution.py:621
  10.8 8.4 %collective-permute-start.5 = (bf16[144,512]{1,0:T(8,128)(2,1)S(1)}, bf16[144,512]{1,0:T(8,128)(2,1)S(1)}, u32[]{:S(2)}, u32[]{:S(2)}) collective-permute-start(bf16[144,512]{1,0:T(8,128)(2,1)S(1)} %get-tuple-element.85), channel_id=1, source_target_pairs={{0,8},{1,0},{2,10},{3,2},{4,12},{5,4},{6,14},{7,6},{8,9},{9,1},{10... | collective-permute-start | bytes 442376 | tf_op jit(solution)/shard_map/ppermute | solution.py:621
  14.2 5.0 %collective-permute-start.6 = (bf16[128,512]{1,0:T(8,128)(2,1)S(1)}, bf16[128,512]{1,0:T(8,128)(2,1)S(1)}, u32[]{:S(2)}, u32[]{:S(2)}) collective-permute-start(bf16[128,512]{1,0:T(8,128)(2,1)S(1)} %next.5), channel_id=1, source_target_pairs={{0,8},{1,0},{2,10},{3,2},{4,12},{5,4},{6,14},{7,6},{8,9},{9,1},{10... | collective-permute-start | bytes 393224 | tf_op jit(solution)/shard_map/ppermute | solution.py:621
  15.9 2.9 %copy-start = (bf16[1024,512]{1,0:T(8,128)(2,1)S(1)}, bf16[1024,512]{1,0:T(8,128)(2,1)}, u32[]{:S(2)}) copy-start(bf16[1024,512]{1,0:T(8,128)(2,1)} %refs_2_.3) | copy-start | bytes 3145732
  15.9 3.4 %collective-permute-start.7 = (bf16[128,512]{1,0:T(8,128)(2,1)S(1)}, bf16[128,512]{1,0:T(8,128)(2,1)S(1)}, u32[]{:S(2)}, u32[]{:S(2)}) collective-permute-start(bf16[128,512]{1,0:T(8,128)(2,1)S(1)} %next.6), channel_id=1, source_target_pairs={{0,8},{1,0},{2,10},{3,2},{4,12},{5,4},{6,14},{7,6},{8,9},{9,1},{10... | collective-permute-start | bytes 393224 | tf_op jit(solution)/shard_map/ppermute | solution.py:621
  17.3 1.4 %copy-start.6 = (s32[128]{0:T(128)S(1)}, s32[128]{0:T(128)}, u32[]{:S(2)}) copy-start(s32[128]{0:T(128)} %param.20) | copy-start | bytes 1540
  17.3 6.4 %collective-permute-start.9 = (bf16[128,512]{1,0:T(8,128)(2,1)S(1)}, bf16[128,512]{1,0:T(8,128)(2,1)S(1)}, u32[]{:S(2)}, u32[]{:S(2)}) collective-permute-start(bf16[128,512]{1,0:T(8,128)(2,1)S(1)} %next.7), channel_id=1, source_target_pairs={{0,8},{1,0},{2,10},{3,2},{4,12},{5,4},{6,14},{7,6},{8,9},{9,1},{10... | collective-permute-start | bytes 393224 | tf_op jit(solution)/shard_map/ppermute | solution.py:621
  19.3 10.8 %collective-permute-start.8 = (bf16[144,512]{1,0:T(8,128)(2,1)S(1)}, bf16[144,512]{1,0:T(8,128)(2,1)S(1)}, u32[]{:S(2)}, u32[]{:S(2)}) collective-permute-start(bf16[144,512]{1,0:T(8,128)(2,1)S(1)} %early.2), channel_id=1, source_target_pairs={{0,1},{1,0},{2,3},{3,2},{4,5},{5,4},{6,7},{7,6},{8,16},{9,8},{10,2... | collective-permute-start | bytes 442376 | tf_op jit(solution)/shard_map/ppermute | solution.py:621
  23.8 7.8 %collective-permute-start.10 = (bf16[128,512]{1,0:T(8,128)(2,1)S(1)}, bf16[128,512]{1,0:T(8,128)(2,1)S(1)}, u32[]{:S(2)}, u32[]{:S(2)}) collective-permute-start(bf16[128,512]{1,0:T(8,128)(2,1)S(1)} %get-tuple-element.103), channel_id=1, source_target_pairs={{0,1},{1,0},{2,3},{3,2},{4,5},{5,4},{6,7},{7,6},{8,16},{9,8},{10,2... | collective-permute-start | bytes 393224 | tf_op jit(solution)/shard_map/ppermute | solution.py:621
  25.3 7.6 %collective-permute-start.11 = (bf16[128,512]{1,0:T(8,128)(2,1)S(1)}, bf16[128,512]{1,0:T(8,128)(2,1)S(1)}, u32[]{:S(2)}, u32[]{:S(2)}) collective-permute-start(bf16[128,512]{1,0:T(8,128)(2,1)S(1)} %next.8), channel_id=1, source_target_pairs={{0,1},{1,0},{2,3},{3,2},{4,5},{5,4},{6,7},{7,6},{8,16},{9,8},{10,2... | collective-permute-start | bytes 393224 | tf_op jit(solution)/shard_map/ppermute | solution.py:621
  26.8 7.6 %collective-permute-start.12 = (bf16[128,512]{1,0:T(8,128)(2,1)S(1)}, bf16[128,512]{1,0:T(8,128)(2,1)S(1)}, u32[]{:S(2)}, u32[]{:S(2)}) collective-permute-start(bf16[128,512]{1,0:T(8,128)(2,1)S(1)} %next.9), channel_id=1, source_target_pairs={{0,1},{1,0},{2,3},{3,2},{4,5},{5,4},{6,7},{7,6},{8,16},{9,8},{10,2... | collective-permute-start | bytes 393224 | tf_op jit(solution)/shard_map/ppermute | solution.py:621
  34.4 7.7 %collective-permute-start.15 = (bf16[128,512]{1,0:T(8,128)(2,1)S(1)}, bf16[128,512]{1,0:T(8,128)(2,1)S(1)}, u32[]{:S(2)}, u32[]{:S(2)}) collective-permute-start(bf16[128,512]{1,0:T(8,128)(2,1)S(1)} %get-tuple-element.114), channel_id=1, source_target_pairs={{0,1},{1,0},{2,3},{3,2},{4,5},{5,21},{6,7},{7,6},{8,9},{9,8},{10,1... | collective-permute-start | bytes 393224 | tf_op jit(solution)/shard_map/ppermute | solution.py:621
  34.4 7.7 %collective-permute-start.14 = (bf16[128,512]{1,0:T(8,128)(2,1)S(1)}, bf16[128,512]{1,0:T(8,128)(2,1)S(1)}, u32[]{:S(2)}, u32[]{:S(2)}) collective-permute-start(bf16[128,512]{1,0:T(8,128)(2,1)S(1)} %far_part.3), channel_id=1, source_target_pairs={{0,1},{1,0},{2,3},{3,2},{4,5},{5,4},{6,7},{7,17},{8,9},{9,8},{10,1... | collective-permute-start | bytes 393224 | tf_op jit(solution)/shard_map/ppermute | solution.py:621
  34.9 9.1 %collective-permute-start.16 = (bf16[128,512]{1,0:T(8,128)(2,1)S(1)}, bf16[128,512]{1,0:T(8,128)(2,1)S(1)}, u32[]{:S(2)}, u32[]{:S(2)}) collective-permute-start(bf16[128,512]{1,0:T(8,128)(2,1)S(1)} %near_part.2.refs_3_), channel_id=1, source_target_pairs={{0,1},{1,17},{2,3},{3,2},{4,5},{5,4},{6,7},{7,6},{8,9},{9,27},{10,... | collective-permute-start | bytes 393224 | tf_op jit(solution)/shard_map/ppermute | solution.py:621
  42.0 2.0 %collective-permute-start.17 = (bf16[128,512]{1,0:T(8,128)(2,1)S(1)}, bf16[128,512]{1,0:T(8,128)(2,1)S(1)}, u32[]{:S(2)}, u32[]{:S(2)}) collective-permute-start(bf16[128,512]{1,0:T(8,128)(2,1)S(1)} %near_part.3.refs_4_), channel_id=1, source_target_pairs={{0,1},{1,0},{2,3},{3,17},{4,5},{5,4},{6,7},{7,6},{8,9},{9,8},{10,1... | collective-permute-start | bytes 393224 | tf_op jit(solution)/shard_map/ppermute | solution.py:621
  42.1 6.8 %copy-start.5 = (bf16[512,227]{0,1:T(8,128)(2,1)S(1)}, bf16[512,227]{0,1:T(8,128)(2,1)}, u32[]{:S(2)}) copy-start(bf16[512,227]{0,1:T(8,128)(2,1)} %param.18) | copy-start | bytes 697348
  44.0 4.9 %collective-permute-start.18 = (bf16[64,512]{1,0:T(8,128)(2,1)S(1)}, bf16[64,512]{1,0:T(8,128)(2,1)S(1)}, u32[]{:S(2)}, u32[]{:S(2)}) collective-permute-start(bf16[64,512]{1,0:T(8,128)(2,1)S(1)} %get-tuple-element.116), channel_id=1, source_target_pairs={{0,1},{1,0},{2,3},{3,2},{4,5},{5,4},{6,7},{7,6},{8,9},{9,8},{10,11... | collective-permute-start | bytes 196616 | tf_op jit(solution)/shard_map/ppermute | solution.py:640
